TPU v7x, 32 devices: a whole 2x2x4 slice. The times are simulated.
32 devices in a mesh: ctx: 8 (over y, x, core), wt: 4 (over z).
Axes of the slice: x: 2, y: 2, z: 4, core: 2. Of those that a mesh axis runs over, the one named last changes fastest.
Arguments:
- hidden: bfloat16 [4, 2048, 1536], P('wt', 'ctx'), may hold values from -6 to 6
- teacher: bfloat16 [4, 2048, 1536], P('wt', 'ctx'), may hold values from -6 to 6
- valid_mask: int32 [4, 2048], P('wt', 'ctx'), may hold values from 0 to 1, as said below
- routes: int32 [4, 2048, 6], P('wt', 'ctx'), may hold values from 0 to 15, all different within a row; in each aligned block of 256 rows (0 to 255, 256 to 511, ..., all dimensions but the last counted through in order) at most 128 rows name the same one
- route_gates: float32 [4, 2048, 6], P('wt', 'ctx'), may hold values from 0.2 to 0.8
- gain_in: bfloat16 [1536], P('wt'), may hold values from 0.25 to 1.75
- query_key_value_weight: bfloat16 [1536, 2560], P('wt'), may hold values from -0.15625 to 0.15625
- out_weight: bfloat16 [1536, 1536], P('wt'), may hold values from -2.5 to 2.5
- gain_mid: bfloat16 [1536], P('wt'), may hold values from 0.25 to 1.75
- shared_weight: bfloat16 [1536, 3072], P('wt'), may hold values from -0.15625 to 0.15625
- expert_weight: bfloat16 [16, 1536, 1536], P('wt'), may hold values from -0.21875 to 0.21875
Outputs:
- output: bfloat16 [4, 2048, 1536], P('wt', 'ctx')
- loss: float32 [], replicated
- grad_hidden: float32 [4, 2048, 1536], P('wt', 'ctx')
- grad_gain_in: float32 [1536], P('wt')
- grad_qkv: float32 [1536, 2560], P('wt')
- grad_out: float32 [1536, 1536], P('wt')
- grad_gain_mid: float32 [1536], P('wt')
- grad_shared: float32 [1536, 3072], P('wt')
- grad_experts: float32 [16, 1536, 1536], P('wt')
Inputs may be any that keep to these rules, and one draw needn't show every extreme that they name: `valid_mask`: in the last row of every aligned block of 256 rows of a sequence the mask is 1. A token's 6 routes name different experts. In the rows of one device (aligned blocks of 256 rows of a sequence) no expert is named more than 128 times, a bound that some block reaches.
All inputs are finite; a program needn't handle non-finite values.
Results may differ from a plain program's by a relative error of at most 0.023.
Values may be sent and summed in bfloat16 or wider, within the bound.
No kernel may reach another device: no remote copies, remote signals or barrier semaphores. Data moves between devices by JAX's collectives and lax.ppermute only.
A program may use at most 512 MiB of HBM per device.

v0:
```python
import math

import jax
import jax.numpy as jnp
from jax import lax
from jax.sharding import PartitionSpec as P

QUERY_HEADS = 12
KEY_VALUE_HEADS = 4
HEAD_SIZE = 128
F = 512
SF = 1024
EXPERTS = 16
TOP = 6


norm_eps = 1e-05
masked_score = -1e30


def sigmoid_linear(values):
    return values * jax.nn.sigmoid(values)


def silu_slope(values):
    sigma_value = jax.nn.sigmoid(values)
    return sigma_value * (1.0 + values * (1.0 - sigma_value))


def normalize(values):
    inverse = lax.rsqrt(jnp.mean(values * values, axis=-1, keepdims=True) + norm_eps)
    return (values * inverse, inverse)


def norm_back(grad_normed, scaled, inverse, gain_vector):
    grad_scaled = grad_normed * gain_vector
    return inverse * (grad_scaled - scaled * jnp.mean(grad_scaled * scaled, axis=-1, keepdims=True))


def positions(row_ids, token_rows, context_count):
    piece_index = row_ids // token_rows
    within = row_ids % token_rows
    half_rows = token_rows // 2
    mirrored = jnp.where(within < half_rows, piece_index, 2 * context_count - 1 - piece_index)
    return mirrored * half_rows + within % half_rows


def route_tables(local_routes, local_gates, experts, capacity):
    token_rows = local_routes.shape[0]
    flat_routes = local_routes.reshape(-1)
    one_hot = (flat_routes[:, None] == jnp.arange(experts, dtype=jnp.int32)[None, :]).astype(
        jnp.int32
    )
    earlier = jnp.cumsum(one_hot, axis=0) - one_hot
    slot_index = jnp.sum(earlier * one_hot, axis=1)
    token_index = jnp.arange(flat_routes.shape[0], dtype=jnp.int32) // local_routes.shape[1]
    slot_table = (
        jnp.full((experts, capacity), token_rows, jnp.int32)
        .at[flat_routes, slot_index]
        .set(token_index)
    )
    slot_gate = (
        jnp.zeros((experts, capacity), jnp.float32)
        .at[flat_routes, slot_index]
        .set(local_gates.reshape(-1))
    )
    return (slot_table, slot_gate)


def block_scores(query_rows, key_block, key_position, query_place, score_scale):
    scores = (
        jnp.einsum("qhgd,khd->qhgk", query_rows, key_block, preferred_element_type=jnp.float32)
        * score_scale
    )
    allowed = key_position[None, None, None, :] <= query_place[:, None, None, None]
    return jnp.where(allowed, scores, masked_score)


def attend_forward(
    query_rows, blocked_keys, blocked_values, place_blocks, query_place, score_scale
):
    head_shape = query_rows.shape[:3]

    def online_step(running, block_args):
        running_max, running_sum, accumulated = running
        key_block, value_block, key_position = block_args
        scores = block_scores(query_rows, key_block, key_position, query_place, score_scale)
        new_max = jnp.maximum(running_max, jnp.max(scores, axis=-1))
        rescale = jnp.exp(running_max - new_max)
        powers = jnp.exp(scores - new_max[..., None])
        new_sum = running_sum * rescale + jnp.sum(powers, axis=-1)
        weighted = jnp.einsum(
            "qhgk,khd->qhgd",
            powers.astype(jnp.bfloat16),
            value_block,
            preferred_element_type=jnp.float32,
        )
        return ((new_max, new_sum, accumulated * rescale[..., None] + weighted), None)

    initial = (
        jnp.full(head_shape, masked_score, jnp.float32),
        jnp.zeros(head_shape, jnp.float32),
        jnp.zeros(query_rows.shape, jnp.float32),
    )
    row_max, row_sum, accumulated = lax.scan(
        online_step, initial, (blocked_keys, blocked_values, place_blocks)
    )[0]
    log_total = row_max + jnp.log(row_sum)
    return (accumulated / row_sum[..., None], log_total)


def attend_backward(
    query_rows,
    blocked_keys,
    blocked_values,
    place_blocks,
    query_place,
    log_total,
    attention_output_gradient,
    attention_output,
    score_scale,
):
    row_delta = jnp.sum(attention_output_gradient.astype(jnp.float32) * attention_output, axis=-1)

    def block_grads(grad_queries, block_args):
        key_block, value_block, key_position = block_args
        scores = block_scores(query_rows, key_block, key_position, query_place, score_scale)
        probabilities = jnp.exp(scores - log_total[..., None])
        grad_probs = jnp.einsum(
            "qhgd,khd->qhgk",
            attention_output_gradient,
            value_block,
            preferred_element_type=jnp.float32,
        )
        grad_scores = (probabilities * (grad_probs - row_delta[..., None])).astype(jnp.bfloat16)
        grad_queries = grad_queries + jnp.einsum(
            "qhgk,khd->qhgd", grad_scores, key_block, preferred_element_type=jnp.float32
        )
        grad_keys = (
            jnp.einsum(
                "qhgk,qhgd->khd", grad_scores, query_rows, preferred_element_type=jnp.float32
            )
            * score_scale
        )
        grad_values = jnp.einsum(
            "qhgk,qhgd->khd",
            probabilities.astype(jnp.bfloat16),
            attention_output_gradient,
            preferred_element_type=jnp.float32,
        )
        return (grad_queries, (grad_keys, grad_values))

    grad_queries, (grad_keys, grad_values) = lax.scan(
        block_grads,
        jnp.zeros(query_rows.shape, jnp.float32),
        (blocked_keys, blocked_values, place_blocks),
    )
    return (grad_queries * score_scale, grad_keys, grad_values)


def gate_up_grads(grad_act, gate_up, hidden_units):
    gate_part = gate_up[..., :hidden_units]
    up_part = gate_up[..., hidden_units:]
    return jnp.concatenate(
        [grad_act * up_part * silu_slope(gate_part), grad_act * sigmoid_linear(gate_part)], axis=-1
    ).astype(jnp.bfloat16)


def on_device(
    hidden,
    teacher,
    valid_mask,
    routes,
    route_gates,
    gain_in,
    query_key_value_weight,
    out_weight,
    gain_mid,
    shared_weight,
    expert_weight,
):
    token_rows = hidden.shape[1]
    model_width = hidden.shape[2]
    context_count = lax.axis_size("ctx")
    shard_count = lax.axis_size("wt")
    seq_rows = token_rows * context_count
    all_tokens = seq_rows * shard_count
    query_groups = QUERY_HEADS // KEY_VALUE_HEADS
    query_total_width = QUERY_HEADS * HEAD_SIZE
    key_value_width = KEY_VALUE_HEADS * HEAD_SIZE
    score_scale = 1.0 / math.sqrt(HEAD_SIZE)
    key_row_count = min(512, seq_rows)
    number_of_blocks = seq_rows // key_row_count
    capacity = token_rows * TOP // 12
    local_experts = expert_weight.shape[0]
    contract_last = (((1,), (1,)), ((), ()))
    contract_first = (((0,), (0,)), ((), ()))
    full_gain_in, full_qkv, full_out, full_gain_mid, full_shared = (
        lax.all_gather(gain_in, "wt", axis=0, tiled=True),
        lax.all_gather(query_key_value_weight, "wt", axis=0, tiled=True),
        lax.all_gather(out_weight, "wt", axis=0, tiled=True),
        lax.all_gather(gain_mid, "wt", axis=0, tiled=True),
        lax.all_gather(shared_weight, "wt", axis=0, tiled=True),
    )
    gain_in_float = full_gain_in.astype(jnp.float32)
    gain_mid_float = full_gain_mid.astype(jnp.float32)
    inputs = hidden[0].astype(jnp.float32)
    scaled_in, inverse_in = normalize(inputs)
    normed_in = (scaled_in * gain_in_float).astype(jnp.bfloat16)
    projected_rows = jnp.dot(normed_in, full_qkv, preferred_element_type=jnp.float32).astype(
        jnp.bfloat16
    )
    query_rows = projected_rows[:, :query_total_width].reshape(
        token_rows, KEY_VALUE_HEADS, query_groups, HEAD_SIZE
    )
    context_local = projected_rows[:, query_total_width:]
    context_gathered = lax.all_gather(context_local, "ctx", axis=0, tiled=True)
    context_index = lax.axis_index("ctx")
    query_place = positions(
        context_index * token_rows + jnp.arange(token_rows, dtype=jnp.int32),
        token_rows,
        context_count,
    )
    place_blocks = positions(
        jnp.arange(seq_rows, dtype=jnp.int32), token_rows, context_count
    ).reshape(number_of_blocks, key_row_count)
    blocked_keys = context_gathered[:, :key_value_width].reshape(
        number_of_blocks, key_row_count, KEY_VALUE_HEADS, HEAD_SIZE
    )
    blocked_values = context_gathered[:, key_value_width:].reshape(
        number_of_blocks, key_row_count, KEY_VALUE_HEADS, HEAD_SIZE
    )
    attention_output, log_total = attend_forward(
        query_rows, blocked_keys, blocked_values, place_blocks, query_place, score_scale
    )
    mixed_rows = attention_output.reshape(token_rows, query_total_width).astype(jnp.bfloat16)
    middle = inputs + jnp.dot(mixed_rows, full_out, preferred_element_type=jnp.float32)
    scaled_mid, inverse_mid = normalize(middle)
    normed_mid = (scaled_mid * gain_mid_float).astype(jnp.bfloat16)
    shared_gate_up = jnp.dot(
        normed_mid, full_shared[:, : 2 * SF], preferred_element_type=jnp.float32
    )
    shared_act = (sigmoid_linear(shared_gate_up[:, :SF]) * shared_gate_up[:, SF:]).astype(
        jnp.bfloat16
    )
    shared_out = lax.dot_general(
        shared_act, full_shared[:, 2 * SF :], contract_last, preferred_element_type=jnp.float32
    )
    slot_table, slot_gate = route_tables(routes[0], route_gates[0], EXPERTS, capacity)
    padded_rows = jnp.concatenate([normed_mid, jnp.zeros((1, model_width), jnp.bfloat16)], axis=0)
    expert_rows = jnp.take(padded_rows, slot_table, axis=0)
    arrived = lax.all_to_all(expert_rows, "wt", split_axis=0, concat_axis=0, tiled=True)
    slot_count = arrived.shape[1]
    grouped = arrived.reshape(shard_count, local_experts, slot_count, model_width)
    owner_gate_up = jnp.einsum(
        "wesd,edf->wesf", grouped, expert_weight[:, :, : 2 * F], preferred_element_type=jnp.float32
    )
    owner_act = (sigmoid_linear(owner_gate_up[..., :F]) * owner_gate_up[..., F:]).astype(
        jnp.bfloat16
    )
    owner_out = jnp.einsum(
        "wesf,edf->wesd",
        owner_act,
        expert_weight[:, :, 2 * F :],
        preferred_element_type=jnp.float32,
    ).astype(jnp.bfloat16)
    returned = lax.all_to_all(
        owner_out.reshape(shard_count * local_experts, slot_count, model_width),
        "wt",
        split_axis=0,
        concat_axis=0,
        tiled=True,
    )
    expert_out, owner_rows, owner_gate_up, owner_act = (
        returned,
        arrived,
        owner_gate_up.reshape(shard_count * local_experts, slot_count, 2 * F),
        owner_act.reshape(shard_count * local_experts, slot_count, F),
    )
    routed = (
        jnp.zeros((token_rows + 1, model_width), jnp.float32)
        .at[slot_table]
        .add(expert_out.astype(jnp.float32) * slot_gate[..., None])[:token_rows]
    )
    final_state = middle + shared_out + routed
    valid_float = valid_mask[0].astype(jnp.float32)
    deviation = final_state - teacher[0].astype(jnp.float32)
    squared_local = jnp.sum(valid_float[:, None] * deviation * deviation)
    count_local = jnp.sum(valid_float)
    squared_total, valid_count = lax.psum((squared_local, count_local), ("ctx", "wt"))
    loss_value = 0.5 * squared_total / (valid_count * model_width)
    grad_final = all_tokens / valid_count * valid_float[:, None] * deviation
    grad_shared_out = grad_final.astype(jnp.bfloat16)
    grad_shared_act = jnp.dot(
        grad_shared_out, full_shared[:, 2 * SF :], preferred_element_type=jnp.float32
    )
    grad_shared_down = lax.dot_general(
        grad_shared_out, shared_act, contract_first, preferred_element_type=jnp.float32
    )
    grad_shared_gate_up = gate_up_grads(grad_shared_act, shared_gate_up, SF)
    grad_normed_mid = lax.dot_general(
        grad_shared_gate_up,
        full_shared[:, : 2 * SF],
        contract_last,
        preferred_element_type=jnp.float32,
    )
    grad_shared_front = lax.dot_general(
        normed_mid, grad_shared_gate_up, contract_first, preferred_element_type=jnp.float32
    )
    grad_shared_full = jnp.concatenate([grad_shared_front, grad_shared_down], axis=1)
    padded_grads = jnp.concatenate([grad_final, jnp.zeros((1, model_width), jnp.float32)], axis=0)
    grad_expert_out = (jnp.take(padded_grads, slot_table, axis=0) * slot_gate[..., None]).astype(
        jnp.bfloat16
    )
    grad_arrived = lax.all_to_all(grad_expert_out, "wt", split_axis=0, concat_axis=0, tiled=True)
    grad_grouped = grad_arrived.reshape(shard_count, local_experts, capacity, model_width)
    owner_gate_up_grouped = owner_gate_up.reshape(shard_count, local_experts, capacity, 2 * F)
    owner_act_grouped = owner_act.reshape(shard_count, local_experts, capacity, F)
    owner_rows_grouped = owner_rows.reshape(shard_count, local_experts, capacity, model_width)
    grad_owner_act = jnp.einsum(
        "wecd,edf->wecf",
        grad_grouped,
        expert_weight[:, :, 2 * F :],
        preferred_element_type=jnp.float32,
    )
    grad_owner_gate_up = gate_up_grads(grad_owner_act, owner_gate_up_grouped, F)
    grad_owner_rows = jnp.einsum(
        "wecf,edf->wecd",
        grad_owner_gate_up,
        expert_weight[:, :, : 2 * F],
        preferred_element_type=jnp.float32,
    ).astype(jnp.bfloat16)
    front = jnp.einsum(
        "wecd,wecf->edf", owner_rows_grouped, grad_owner_gate_up, preferred_element_type=jnp.float32
    )
    back = jnp.einsum(
        "wecd,wecf->edf", grad_grouped, owner_act_grouped, preferred_element_type=jnp.float32
    )
    expert_grad = jnp.concatenate([front, back], axis=2)
    grad_rows = lax.all_to_all(
        grad_owner_rows.reshape(shard_count * local_experts, capacity, model_width),
        "wt",
        split_axis=0,
        concat_axis=0,
        tiled=True,
    )
    grad_normed_mid = (
        grad_normed_mid
        + jnp.zeros((token_rows + 1, model_width), jnp.float32)
        .at[slot_table]
        .add(grad_rows.astype(jnp.float32))[:token_rows]
    )
    grad_gain_mid_local = jnp.sum(grad_normed_mid * scaled_mid, axis=0)
    grad_middle = grad_final + norm_back(grad_normed_mid, scaled_mid, inverse_mid, gain_mid_float)
    grad_branch = grad_middle.astype(jnp.bfloat16)
    mixed_gradient = lax.dot_general(
        grad_branch, full_out, contract_last, preferred_element_type=jnp.float32
    ).astype(jnp.bfloat16)
    grad_out_local = lax.dot_general(
        mixed_rows, grad_branch, contract_first, preferred_element_type=jnp.float32
    )
    context_recomputed = lax.all_gather(context_local, "ctx", axis=0, tiled=True)
    backward_keys = context_recomputed[:, :key_value_width].reshape(
        number_of_blocks, key_row_count, KEY_VALUE_HEADS, HEAD_SIZE
    )
    backward_values = context_recomputed[:, key_value_width:].reshape(
        number_of_blocks, key_row_count, KEY_VALUE_HEADS, HEAD_SIZE
    )
    attention_output_gradient = mixed_gradient.reshape(
        token_rows, KEY_VALUE_HEADS, query_groups, HEAD_SIZE
    )
    grad_queries, grad_keys, grad_values = attend_backward(
        query_rows,
        backward_keys,
        backward_values,
        place_blocks,
        query_place,
        log_total,
        attention_output_gradient,
        attention_output,
        score_scale,
    )
    grad_context_all = jnp.concatenate(
        [
            grad_keys.reshape(seq_rows, key_value_width),
            grad_values.reshape(seq_rows, key_value_width),
        ],
        axis=1,
    )
    grad_context = lax.psum_scatter(
        grad_context_all.astype(jnp.bfloat16), "ctx", scatter_dimension=0, tiled=True
    ).astype(jnp.float32)
    grad_projected = jnp.concatenate(
        [grad_queries.reshape(token_rows, query_total_width), grad_context], axis=1
    ).astype(jnp.bfloat16)
    grad_normed_in = lax.dot_general(
        grad_projected, full_qkv, contract_last, preferred_element_type=jnp.float32
    )
    grad_qkv_local = lax.dot_general(
        normed_in, grad_projected, contract_first, preferred_element_type=jnp.float32
    )
    grad_gain_in_local = jnp.sum(grad_normed_in * scaled_in, axis=0)
    grad_inputs = grad_middle + norm_back(grad_normed_in, scaled_in, inverse_in, gain_in_float)
    weight_sums = (
        lax.psum_scatter(
            grad_gain_in_local.astype(jnp.bfloat16), "wt", scatter_dimension=0, tiled=True
        ).astype(jnp.float32),
        lax.psum_scatter(
            grad_qkv_local.astype(jnp.bfloat16), "wt", scatter_dimension=0, tiled=True
        ).astype(jnp.float32),
        lax.psum_scatter(
            grad_out_local.astype(jnp.bfloat16), "wt", scatter_dimension=0, tiled=True
        ).astype(jnp.float32),
        lax.psum_scatter(
            grad_gain_mid_local.astype(jnp.bfloat16), "wt", scatter_dimension=0, tiled=True
        ).astype(jnp.float32),
        lax.psum_scatter(
            grad_shared_full.astype(jnp.bfloat16), "wt", scatter_dimension=0, tiled=True
        ).astype(jnp.float32),
    )
    summed = (
        lax.psum(weight_sums[0].astype(jnp.bfloat16), "ctx").astype(jnp.float32),
        lax.psum(weight_sums[1].astype(jnp.bfloat16), "ctx").astype(jnp.float32),
        lax.psum(weight_sums[2].astype(jnp.bfloat16), "ctx").astype(jnp.float32),
        lax.psum(weight_sums[3].astype(jnp.bfloat16), "ctx").astype(jnp.float32),
        lax.psum(weight_sums[4].astype(jnp.bfloat16), "ctx").astype(jnp.float32),
        lax.psum(expert_grad.astype(jnp.bfloat16), "ctx").astype(jnp.float32),
    )
    return (
        final_state.astype(jnp.bfloat16)[None],
        loss_value,
        grad_inputs[None],
        summed[0],
        summed[1],
        summed[2],
        summed[3],
        summed[4],
        summed[5],
    )


def solution(mesh):
    in_specs = (
        P("wt", "ctx", None),
        P("wt", "ctx", None),
        P("wt", "ctx"),
        P("wt", "ctx", None),
        P("wt", "ctx", None),
        P("wt"),
        P("wt", None),
        P("wt", None),
        P("wt"),
        P("wt", None),
        P("wt", None, None),
    )
    out_specs = (
        P("wt", "ctx", None),
        P(),
        P("wt", "ctx", None),
        P("wt"),
        P("wt", None),
        P("wt", None),
        P("wt"),
        P("wt", None),
        P("wt", None, None),
    )
    return jax.shard_map(
        on_device, mesh=mesh, in_specs=in_specs, out_specs=out_specs, check_vma=False
    )
```

profile of v0, /device:TPU:0, one launch (start us, length us, event | category | flops | bytes accessed | tf_op | source)
XLA Modules:
  0.0 2092.9 jit_solution(8230155754010462525)
XLA Ops:
  8.6 13.5 all-gather
  23.6 129.7 %all-gather.7.cloned.1.call-done = bf16[1536,2560]{1,0:T(8,128)(2,1)} async-done(((bf16[384,2560]{1,0:T(8,128)(2,1)}), bf16[1536,2560]{1,0:T(8,128)(2,1)}) %all-gather.7.cloned.1.call-update) | async-done | bytes 7864336 | tf_op jit(solution)/shard_map/all_gather | solution.py:200
  153.4 5.8 convolution_convert_fusion.3
  167.7 6.2 scatter_custom_fusion.2
  175.1 12.0 all-gather.1
  188.5 6.7 all-gather.9.cloned.1.call-done
  207.1 74.3 %while.30 = (s32[]{:T(128)}, f32[256,4,3]{0,2,1:T(4,128)S(1)}, f32[256,4,3]{0,2,1:T(4,128)S(1)}, f32[256,4,3,128]{0,3,2,1:T(8,128)}, s32[4,512]{1,0:T(4,128)}, /...) while((s32[]{:T(128)}, f32[256,4,3]{0,2,1:T(4,128)S(1)}, ...), condition=%wide.region_4.5_spmd.clone, body=%wide.region_1.4_spmd.clone.sunk | while | flops 823943168 | bytes 26829028 | solution.py:105
  219.5 5.9 bitcast_add_fusion.4
  237.8 6.3 bitcast_add_fusion.4
  256.5 6.3 bitcast_add_fusion.4
  275.1 6.3 bitcast_add_fusion.4
  292.0 10.0 gather_fusion
  302.1 6.1 broadcast_select_fusion
  308.2 5.2 all-to-all-start
  314.0 281.2 %all-to-all-done = bf16[16,128,1536]{2,1,0:T(8,128)(2,1)} async-done(((bf16[16,128,1536]{2,1,0:T(8,128)(2,1)}), bf16[16,128,1536]{2,1,0:T(8,128)(2,1)}, u32[]{:S(2)}, u32[]{:S(2)}) %all-to-all-start) | async-done | bytes 6291488 | tf_op jit(solution)/shard_map/all_to_all | solution.py:252
  595.2 11.5 fusion.84
  610.7 9.7 convert_bitcast_fusion.1
  620.4 5.9 copy.75
  626.3 5.4 all-to-all-start.1
  632.0 6.7 scatter_custom_fusion.3
  646.5 120.9 %all-to-all-done.1 = bf16[16,128,1536]{2,1,0:T(8,128)(2,1)} async-done(((bf16[16,128,1536]{2,1,0:T(8,128)(2,1)}), bf16[16,128,1536]{2,1,0:T(8,128)(2,1)}, u32[]{:S(2)}, u32[]{:S(2)}) %all-to-all-start.1) | async-done | bytes 6291488 | tf_op jit(solution)/shard_map/all_to_all | solution.py:267
  767.4 8.6 convert_multiply_fusion
  776.0 21.8 %scatter_custom_fusion = f32[257,1536]{1,0:T(8,128)S(1)} fusion(s32[2048]{0:T(1024)S(1)} %fusion.137, f32[2048,1536]{1,0:T(8,128)} %bitcast.285, f32[]{:T(128)} %constant.168.clone.1), kind=kCustom, calls=%fused_computation.178 | custom fusion | flops 3145728 | bytes 1579520 | tf_op jit(solution)/shard_map/scatter-add | solution.py:283
  802.9 38.0 %all-reduce.4 = (f32[]{:T(128)}, f32[]{:T(128)}) all-reduce(f32[]{:T(128)} %convert_reduce_fusion.2, f32[]{:T(128)} %get-tuple-element.363), channel_id=1, replica_groups=mesh['ctx'=8,'wt'=4] {'ctx','wt'}, use_global_device_ids=true, to_apply=%region_15.16 | all-reduce | flops 2 | bytes 16 | tf_op jit(solution)/shard_map/psum | solution.py:290
  845.2 10.7 gather_fusion.1
  855.9 5.7 multiply_convert_fusion
  861.5 142.0 %all_to_all.20 = bf16[16,128,1536]{2,1,0:T(8,128)(2,1)S(1)} all-to-all(bf16[16,128,1536]{2,1,0:T(8,128)(2,1)S(1)} %multiply_convert_fusion), channel_id=1, replica_groups=mesh['ctx'=8,'wt'=4] {'wt'}, dimensions={0} | all-to-all | bytes 12582912 | tf_op jit(solution)/shard_map/all_to_all | solution.py:315
  1003.6 12.1 fusion.81
  1015.6 12.7 convert_bitcast_fusion
  1028.3 6.0 copy.78
  1034.4 5.4 all-to-all-start.3
  1044.6 132.3 %all-to-all-done.3 = bf16[16,128,1536]{2,1,0:T(8,128)(2,1)} async-done(((bf16[16,128,1536]{2,1,0:T(8,128)(2,1)}), bf16[16,128,1536]{2,1,0:T(8,128)(2,1)}, u32[]{:S(2)}, u32[]{:S(2)}) %all-to-all-start.3) | async-done | bytes 6291488 | tf_op jit(solution)/shard_map/all_to_all | solution.py:340
  1176.9 23.0 %scatter_custom_fusion.1 = f32[257,1536]{1,0:T(8,128)} fusion(s32[2048]{0:T(1024)S(1)} %fusion.137, bf16[2048,1536]{1,0:T(8,128)(2,1)} %bitcast.63, f32[]{:T(128)} %constant.168.clone.1), kind=kCustom, calls=%fused_computation.89 | custom fusion | flops 6291456 | bytes 7870468 | tf_op jit(solution)/shard_map/scatter-add | solution.py:351
  1199.9 6.3 multiply_reduce_fusion
  1216.8 74.4 %while.31 = (s32[]{:T(128)}, f32[256,4,3,128]{0,3,2,1:T(8,128)S(1)}, bf16[4,512,4,128]{3,1,2,0:T(8,128)(2,1)}, bf16[4,512,4,128]{3,1,2,0:T(8,128)(2,1)}, bf16[4,...) while((s32[]{:T(128)}, ...), condition=%wide.region_20.21_spmd.clone, body=%wide.region_19.20_spmd.clone.sunk | while | flops 2030183424 | bytes 110018880 | solution.py:153
  1317.2 33.5 %reduce-scatter.5.cloned.1.call-done = bf16[256,1024]{1,0:T(8,128)(2,1)} async-done(((bf16[2048,1024]{1,0:T(8,128)(2,1)}), bf16[256,1024]{1,0:T(8,128)(2,1)}) %reduce-scatter.5.cloned.1.call-update) | async-done | bytes 524304 | tf_op jit(solution)/shard_map/reduce_scatter | solution.py:390
  1352.0 5.7 convolution_convert_fusion
  1357.9 10.3 bitcast_convert_fusion.1
  1368.3 12.9 bitcast_convert_fusion
  1381.2 20.7 pad_maximum_fusion
  1402.0 112.4 %reduce-scatter.11.cloned.1.call-done = bf16[384,3072]{1,0:T(8,128)(2,1)} async-done(((bf16[1536,3072]{1,0:T(8,128)(2,1)}), bf16[384,3072]{1,0:T(8,128)(2,1)}) %reduce-scatter.11.cloned.1.call-update) | async-done | bytes 2359312 | tf_op jit(solution)/shard_map/reduce_scatter | solution.py:417
  1514.4 89.1 %reduce-scatter.9.cloned.1.call-done = bf16[384,1536]{1,0:T(8,128)(2,1)} async-done(((bf16[1536,1536]{1,0:T(8,128)(2,1)}), bf16[384,1536]{1,0:T(8,128)(2,1)}) %reduce-scatter.9.cloned.1.call-update) | async-done | bytes 1179664 | tf_op jit(solution)/shard_map/reduce_scatter | solution.py:411
  1603.5 139.2 %reduce-scatter.7.cloned.1.call-done = bf16[384,2560]{1,0:T(8,128)(2,1)} async-done(((bf16[1536,2560]{1,0:T(8,128)(2,1)}), bf16[384,2560]{1,0:T(8,128)(2,1)}) %reduce-scatter.7.cloned.1.call-update) | async-done | bytes 1966096 | tf_op jit(solution)/shard_map/reduce_scatter | solution.py:408
  1745.9 7.1 fusion.110
  1753.1 11.1 all-reduce.7
  1764.3 12.9 all-reduce.5
  1781.6 268.2 %all-reduce.10.cloned.1.call-done = (bf16[4,1536,1536]{1,2,0:T(8,128)(2,1)}, bf16[384,2560]{1,0:T(8,128)(2,1)}, bf16[384,1536]{1,0:T(8,128)(2,1)}, bf16[384,3072]{1,0:T(8,128)(2,1)}) async-done(((bf16[4,1536,1536]{1,2,0:T(8,128)(2,1)}, bf16[384,2560]{1,0:T(8,128)(2,1)}, bf16[384,1536]{1,0:T(8,128)(2,1)}, bf16[384,3072]{1,0:T(8,128)(2,1)}), (bf16[4,1536,1536]{1,2,0:T(8,128)(2,1)}, ...) | async-done | bytes 24379408 | tf_op jit(solution)/shard_map/psum | solution.py:427
  2059.1 25.9 %copy.90 = f32[4,1536,1536]{2,1,0:T(8,128)} copy(bf16[4,1536,1536]{1,2,0:T(8,128)(2,1)} %get-tuple-element.343) | data formatting | bytes 56623104
  (338 shorter events, 238.3 us)
Async XLA Ops:
  7.2 146.2 %all-gather.7.cloned.1.call-start = ((), (), s32[]{:S(2)}) async-start(), calls=%async_computation.8 | async-start | bytes 9830400 | tf_op jit(solution)/shard_map/all_gather | solution.py:200
  7.9 187.3 %all-gather.9.cloned.1.call-start = ((), (), s32[]{:S(2)}) async-start(), calls=%async_computation.9 | async-start | bytes 4718592 | tf_op jit(solution)/shard_map/all_gather | solution.py:217
  22.2 136.9 %copy-start.39 = (f32[1536]{0:T(1024)}, f32[1536]{0:T(1024)S(1)}, u32[]{:S(2)}) copy-start(f32[1536]{0:T(1024)S(1)} %reshape.318) | copy-start | bytes 18436
  23.6 135.5 %copy-start.44 = (f32[256]{0:T(256)}, f32[256]{0:T(256)S(1)}, u32[]{:S(2)}) copy-start(f32[256]{0:T(256)S(1)} %add_rsqrt_fusion.1) | copy-start | bytes 3076
  23.6 137.2 %copy-start.47 = (s32[1,256,6]{1,0,2:T(1,128)S(1)}, s32[1,256,6]{1,0,2:T(1,128)}, u32[]{:S(2)}) copy-start(s32[1,256,6]{1,0,2:T(1,128)} %param.18) | copy-start | bytes 18436
  159.2 8.3 copy-start.52
  159.2 8.4 copy-start.51
  159.2 15.9 copy-start.49
  160.1 126.1 %all-gather.11.cloned.1.call-start = ((), (), s32[]{:S(2)}) async-start(), calls=%async_computation.10 | async-start | bytes 5898240 | tf_op jit(solution)/shard_map/all_gather | solution.py:201
  167.7 7.4 copy-start.46
  173.9 13.3 copy-start.37
  219.5 5.9 copy-start.25
  219.5 5.9 copy-start.31
  237.8 6.3 copy-start.25
  237.8 6.3 copy-start.31
  256.5 6.4 copy-start.25
  256.5 6.4 copy-start.31
  275.1 6.3 copy-start.25
  275.1 6.3 copy-start.31
  281.4 9.1 copy-start.2
  281.4 9.1 copy-start.4
  281.5 9.1 copy-start.26
  281.5 9.1 copy-start.32
  291.9 347.5 %copy-start.14 = (bf16[256,1536]{1,0:T(8,128)(2,1)}, bf16[256,1536]{1,0:T(8,128)(2,1)S(1)}, u32[]{:S(2)}) copy-start(bf16[256,1536]{1,0:T(8,128)(2,1)S(1)} %multiply_convert_fusion.3) | copy-start | bytes 2359300
  292.0 10.1 copy-start.43
  308.2 287.0 %all-to-all-start = ((bf16[16,128,1536]{2,1,0:T(8,128)(2,1)}), bf16[16,128,1536]{2,1,0:T(8,128)(2,1)}, u32[]{:S(2)}, u32[]{:S(2)}) async-start(bf16[16,128,1536]{2,1,0:T(8,128)(2,1)} %broadcast_select_fusion), calls=%async_computation | async-start | bytes 12582912 | tf_op jit(solution)/shard_map/all_to_all | solution.py:252
  313.4 325.9 %all-gather.13.cloned.1.call-start = ((), (), s32[]{:S(2)}) async-start(), calls=%async_computation.11 | async-start | bytes 11796480 | tf_op jit(solution)/shard_map/all_gather | solution.py:203
  626.3 13.0 copy-start.38
  626.3 141.1 %all-to-all-start.1 = ((bf16[16,128,1536]{2,1,0:T(8,128)(2,1)}), bf16[16,128,1536]{2,1,0:T(8,128)(2,1)}, u32[]{:S(2)}, u32[]{:S(2)}) async-start(bf16[16,128,1536]{2,1,0:T(8,128)(2,1)} %bitcast.280), calls=%async_computation.1 | async-start | bytes 12582912 | tf_op jit(solution)/shard_map/all_to_all | solution.py:267
  767.4 30.4 %copy-start.8 = (f32[256,1536]{1,0:T(8,128)S(1)}, f32[256,1536]{1,0:T(8,128)}, u32[]{:S(2)}) copy-start(f32[256,1536]{1,0:T(8,128)} %copy-done.7) | copy-start | bytes 4718596
  845.0 361.2 %copy-start.5 = (f32[256,1536]{1,0:T(8,128)}, f32[256,1536]{1,0:T(8,128)S(1)}, u32[]{:S(2)}) copy-start(f32[256,1536]{1,0:T(8,128)S(1)} %get-tuple-element.359) | copy-start | bytes 4718596
  1003.6 12.1 copy-start.17
  1034.4 142.6 %all-to-all-start.3 = ((bf16[16,128,1536]{2,1,0:T(8,128)(2,1)}), bf16[16,128,1536]{2,1,0:T(8,128)(2,1)}, u32[]{:S(2)}, u32[]{:S(2)}) async-start(bf16[16,128,1536]{2,1,0:T(8,128)(2,1)} %bitcast.281), calls=%async_computation.3 | async-start | bytes 12582912 | tf_op jit(solution)/shard_map/all_to_all | solution.py:340
  1039.7 311.0 %reduce-scatter.5.cloned.1.call-start = ((), (), s32[]{:S(2)}) async-start(), calls=%async_computation.12 | async-start | bytes 4718592 | tf_op jit(solution)/shard_map/reduce_scatter | solution.py:390
  1199.9 6.4 copy-start.9
  1225.5 7.1 copy-start.1
  1244.1 7.1 copy-start.1
  1262.6 7.1 copy-start.1
  1281.1 7.1 copy-start.1
  1300.7 213.7 %reduce-scatter.11.cloned.1.call-start = ((), (), s32[]{:S(2)}) async-start(), calls=%async_computation.15 | async-start | bytes 11796480 | tf_op jit(solution)/shard_map/reduce_scatter | solution.py:417
  1310.7 292.8 %reduce-scatter.9.cloned.1.call-start = ((), (), s32[]{:S(2)}) async-start(), calls=%async_computation.14 | async-start | bytes 5898240 | tf_op jit(solution)/shard_map/reduce_scatter | solution.py:411
  1317.0 35.0 %copy-start.11 = (bf16[1,256,1536]{2,1,0:T(8,128)(2,1)S(1)}, bf16[1,256,1536]{2,1,0:T(8,128)(2,1)}, u32[]{:S(2)}) copy-start(bf16[1,256,1536]{2,1,0:T(8,128)(2,1)} %param.15) | copy-start | bytes 2359300
  1317.0 35.1 %copy-start.40 = (f32[1536]{0:T(1024)S(1)}, f32[1536]{0:T(1024)}, u32[]{:S(2)}) copy-start(f32[1536]{0:T(1024)} %copy-done.39) | copy-start | bytes 18436
  1317.0 35.1 %copy-start.45 = (f32[256]{0:T(256)S(1)}, f32[256]{0:T(256)}, u32[]{:S(2)}) copy-start(f32[256]{0:T(256)} %copy-done.44) | copy-start | bytes 3076
  1317.0 425.7 %reduce-scatter.7.cloned.1.call-start = ((), (), s32[]{:S(2)}) async-start(), calls=%async_computation.13 | async-start | bytes 9830400 | tf_op jit(solution)/shard_map/reduce_scatter | solution.py:408
  1352.0 5.7 copy-start.20
  1357.7 692.0 %all-reduce.10.cloned.1.call-start = ((), (), s32[]{:S(2)}) async-start(), calls=%async_computation.16 | async-start | bytes 48758784 | tf_op jit(solution)/shard_map/psum | solution.py:427
  1745.9 32.4 %copy-start.13 = (f32[256,1536]{1,0:T(8,128)S(1)}, f32[256,1536]{1,0:T(8,128)}, u32[]{:S(2)}) copy-start(f32[256,1536]{1,0:T(8,128)} %copy-done.12) | copy-start | bytes 4718596
  (42 other events, 120.0 us)
Sparse Core Ops, SparseCore 0:
  9.6 143.7 all-gather.6
  160.2 34.9 all-gather.8
  196.8 89.4 all-gather.10
  315.5 288.3 all-gather.12
  1300.8 49.9 reduce-scatter.4
  1353.1 161.2 reduce-scatter.10
  1517.4 86.0 reduce-scatter.8
  1605.9 136.7 reduce-scatter.6
  1748.3 301.4 all-reduce.9
where the time goes:
time: 2100 us; the launch traced here: 2090 us
  waiting for transfers between devices  1320 us (63%)
  blocking collectives  230 us (11%)
  matrix products  225 us (11%)
  other arithmetic  149 us (7%)
  local copies, waits for them, and re-layouts  137 us (7%)
    all_to_all x1, waiting for transfers between devices, on_device(): lax.all_to_all(expert_rows, 'wt', split_axis=0, concat_axis=0, tiled=True)  281 us
    psum x1, waiting for transfers between devices, on_device(): lax.psum(expert_grad.astype(jnp.bfloat16), 'ctx').astype(jnp.float32)  268 us
    all_to_all x1, blocking collectives, on_device(): lax.all_to_all(grad_expert_out, 'wt', split_axis=0, concat_axis=0, tiled=...  142 us
    reduce_scatter x1, waiting for transfers between devices, on_device(): lax.psum_scatter(grad_qkv_local.astype(jnp.bfloat16), 'wt', scatter_dimen...  139 us
    all_to_all x1, waiting for transfers between devices, on_device(): lax.all_to_all(grad_owner_rows.reshape(shard_count * local_experts, capac...  132 us
    all_gather x1, waiting for transfers between devices, on_device(): lax.all_gather(query_key_value_weight, 'wt', axis=0, tiled=True)  130 us
    all_to_all x1, waiting for transfers between devices, on_device(): lax.all_to_all(owner_out.reshape(shard_count * local_experts, slot_count,...  121 us
    reduce_scatter x1, waiting for transfers between devices, on_device(): lax.psum_scatter(grad_shared_full.astype(jnp.bfloat16), 'wt', scatter_dim...  112 us
  transfers between devices with their start and end apart: 12, of which 11 were waited for; matrix products, arithmetic and copies ran while one was open for 11% of the time, Pallas kernels for 0%

commit v1 on v0

--- a/solution.py
+++ b/solution.py
@@ -3,6 +3,8 @@
 import jax
 import jax.numpy as jnp
 from jax import lax
+from jax.experimental import pallas as pl
+from jax.experimental.pallas import tpu as pltpu
 from jax.sharding import PartitionSpec as P
 
 QUERY_HEADS = 12
@@ -439,6 +441,614 @@
     )
 
 
+def flip(value, bit):
+    return lax.ppermute(value, "ctx", [(index, index ^ bit) for index in range(8)])
+
+
+def line_swap(value, offset):
+    return lax.ppermute(value, "wt", [(index, index ^ offset) for index in range(4)])
+
+
+def line_middle(value):
+    return lax.ppermute(value, "wt", [(1, 2), (2, 1)])
+
+
+def line_outward(value):
+    return lax.ppermute(value, "wt", [(1, 0), (2, 3)])
+
+
+def line_inward(value):
+    return lax.ppermute(value, "wt", [(0, 1), (3, 2)])
+
+
+def line_gather(value, at_end):
+    near = line_swap(value, 1)
+    middle = line_middle(value)
+    middle_far = line_middle(near)
+    outward = line_outward(middle)
+    outward_far = line_outward(middle_far)
+    return [
+        value,
+        near,
+        jnp.where(at_end, outward, middle_far),
+        jnp.where(at_end, outward_far, middle),
+    ]
+
+
+def line_reduce(parts):
+    far = line_inward(parts[3])
+    carried = parts[2] + far
+    inward = line_inward(carried)
+    crossed = line_middle(carried)
+    near = line_swap(parts[1] + crossed, 1)
+    middle = line_middle(parts[3] + inward)
+    return (
+        parts[0].astype(jnp.float32) + near.astype(jnp.float32) + middle.astype(jnp.float32)
+    )
+
+
+def chips_gather(value):
+    half = value.shape[0] // 2
+    along_x = flip(value, 2)
+    along_y = flip(value, 4)
+    corner = jnp.concatenate([flip(along_x[:half], 4), flip(along_y[half:], 2)], axis=0)
+    return [value, along_x, along_y, corner]
+
+
+def plane_gather(value):
+    chips = jnp.stack(chips_gather(value))
+    return jnp.stack([chips, flip(chips, 1)], axis=1).reshape((8,) + value.shape)
+
+
+def pick(blocks, index):
+    return lax.dynamic_index_in_dim(blocks, index, 0, keepdims=False)
+
+
+def plane_reduce(blocks, context_index):
+    core = context_index & 1
+    x_bit = (context_index >> 1) & 1
+    y_bit = context_index >> 2
+    rows, columns = blocks.shape[1:]
+    by_core = blocks.reshape(4, 2, rows, columns)
+    keep = lax.dynamic_index_in_dim(by_core, core, 1, keepdims=False)
+    give = lax.dynamic_index_in_dim(by_core, 1 - core, 1, keepdims=False)
+    chip_sum = (keep + flip(give, 1)).reshape(2, 2, rows, columns)
+    left = chip_sum[..., : columns // 2]
+    right = chip_sum[..., columns // 2 :]
+    left_x = lax.dynamic_index_in_dim(left, x_bit, 1, keepdims=False) + flip(
+        lax.dynamic_index_in_dim(left, 1 - x_bit, 1, keepdims=False), 2
+    )
+    right_y = pick(right, y_bit) + flip(pick(right, 1 - y_bit), 4)
+    left_done = pick(left_x, y_bit) + flip(pick(left_x, 1 - y_bit), 4)
+    right_done = pick(right_y, x_bit) + flip(pick(right_y, 1 - x_bit), 2)
+    return jnp.concatenate([left_done, right_done], axis=1)
+
+
+def plane_sum_small(value):
+    for bit in (1, 2, 4):
+        value = value + flip(value, bit)
+    return value
+
+
+def gated(gate_up, units):
+    gate_part = gate_up[:, :units]
+    sigma = 1.0 / (1.0 + jnp.exp(-gate_part))
+    return gate_part * sigma * gate_up[:, units:]
+
+
+def gated_back(grad_act, gate_up, units):
+    gate_part = gate_up[:, :units].astype(jnp.float32)
+    up_part = gate_up[:, units:].astype(jnp.float32)
+    sigma = 1.0 / (1.0 + jnp.exp(-gate_part))
+    linear = gate_part * sigma
+    grad_gate = grad_act * up_part * (sigma * (1.0 + gate_part * (1.0 - sigma)))
+    return grad_gate, grad_act * linear, linear * up_part
+
+
+def dot_plain(left, right):
+    return lax.dot_general(
+        left, right, (((1,), (0,)), ((), ())), preferred_element_type=jnp.float32
+    )
+
+
+def dot_last(left, right):
+    return lax.dot_general(
+        left, right, (((1,), (1,)), ((), ())), preferred_element_type=jnp.float32
+    )
+
+
+def dot_first(left, right):
+    return lax.dot_general(
+        left, right, (((0,), (0,)), ((), ())), preferred_element_type=jnp.float32
+    )
+
+
+def experts_forward_kernel(
+    rows_ref, gates_ref, expert_ref, shared_ref, gate_up_ref, shared_gate_up_ref, out_ref, total
+):
+    expert = pl.program_id(0)
+    rows = rows_ref[...]
+
+    @pl.when(expert == 0)
+    def _():
+        units = shared_ref.shape[1] // 3
+        gate_up = dot_plain(rows, shared_ref[:, : 2 * units])
+        shared_gate_up_ref[...] = gate_up.astype(jnp.bfloat16)
+        act = gated(gate_up, units).astype(jnp.bfloat16)
+        total[...] = dot_last(act, shared_ref[:, 2 * units :])
+
+    gate_up = dot_plain(rows, expert_ref[0, :, : 2 * F])
+    gate_up_ref[0] = gate_up.astype(jnp.bfloat16)
+    act = (gated(gate_up, F) * gates_ref[0]).astype(jnp.bfloat16)
+    total[...] += dot_last(act, expert_ref[0, :, 2 * F :])
+
+    @pl.when(expert == pl.num_programs(0) - 1)
+    def _():
+        out_ref[...] = total[...].astype(jnp.bfloat16)
+
+
+def experts_forward(rows, gates, expert_weight, shared_slice):
+    local_experts, width, _ = expert_weight.shape
+    token_rows = rows.shape[0]
+    shared_units = shared_slice.shape[1] // 3
+    return pl.pallas_call(
+        experts_forward_kernel,
+        grid=(local_experts,),
+        in_specs=[
+            pl.BlockSpec((token_rows, width), lambda e: (0, 0)),
+            pl.BlockSpec((1, token_rows, 1), lambda e: (e, 0, 0)),
+            pl.BlockSpec((1, width, 3 * F), lambda e: (e, 0, 0)),
+            pl.BlockSpec((width, 3 * shared_units), lambda e: (0, 0)),
+        ],
+        out_specs=[
+            pl.BlockSpec((1, token_rows, 2 * F), lambda e: (e, 0, 0)),
+            pl.BlockSpec((token_rows, 2 * shared_units), lambda e: (0, 0)),
+            pl.BlockSpec((token_rows, width), lambda e: (0, 0)),
+        ],
+        out_shape=[
+            jax.ShapeDtypeStruct((local_experts, token_rows, 2 * F), jnp.bfloat16),
+            jax.ShapeDtypeStruct((token_rows, 2 * shared_units), jnp.bfloat16),
+            jax.ShapeDtypeStruct((token_rows, width), jnp.bfloat16),
+        ],
+        scratch_shapes=[pltpu.VMEM((token_rows, width), jnp.float32)],
+        compiler_params=pltpu.CompilerParams(vmem_limit_bytes=48 * 1024 * 1024),
+        name="experts_forward",
+    )(rows, gates, expert_weight, shared_slice)
+
+
+def experts_backward_kernel(
+    grad_ref,
+    gates_ref,
+    gate_up_ref,
+    shared_gate_up_ref,
+    expert_ref,
+    shared_ref,
+    grad_gate_up_ref,
+    act_ref,
+    shared_grad_ref,
+    shared_act_ref,
+    grad_rows_ref,
+    total,
+):
+    expert = pl.program_id(0)
+    grad = grad_ref[...]
+
+    @pl.when(expert == 0)
+    def _():
+        units = shared_ref.shape[1] // 3
+        grad_act = dot_plain(grad, shared_ref[:, 2 * units :])
+        grad_gate, grad_up, act = gated_back(grad_act, shared_gate_up_ref[...], units)
+        both = jnp.concatenate([grad_gate, grad_up], axis=1).astype(jnp.bfloat16)
+        shared_grad_ref[...] = both
+        shared_act_ref[...] = act.astype(jnp.bfloat16)
+        total[...] = dot_last(both, shared_ref[:, : 2 * units])
+
+    grad_act = dot_plain(grad, expert_ref[0, :, 2 * F :]) * gates_ref[0]
+    grad_gate, grad_up, act = gated_back(grad_act, gate_up_ref[0], F)
+    both = jnp.concatenate([grad_gate, grad_up], axis=1).astype(jnp.bfloat16)
+    grad_gate_up_ref[0] = both
+    act_ref[0] = (act * gates_ref[0]).astype(jnp.bfloat16)
+    total[...] += dot_last(both, expert_ref[0, :, : 2 * F])
+
+    @pl.when(expert == pl.num_programs(0) - 1)
+    def _():
+        grad_rows_ref[...] = total[...].astype(jnp.bfloat16)
+
+
+def experts_backward(grad, gates, gate_up, shared_gate_up, expert_weight, shared_slice):
+    local_experts, width, _ = expert_weight.shape
+    token_rows = grad.shape[0]
+    shared_units = shared_slice.shape[1] // 3
+    return pl.pallas_call(
+        experts_backward_kernel,
+        grid=(local_experts,),
+        in_specs=[
+            pl.BlockSpec((token_rows, width), lambda e: (0, 0)),
+            pl.BlockSpec((1, token_rows, 1), lambda e: (e, 0, 0)),
+            pl.BlockSpec((1, token_rows, 2 * F), lambda e: (e, 0, 0)),
+            pl.BlockSpec((token_rows, 2 * shared_units), lambda e: (0, 0)),
+            pl.BlockSpec((1, width, 3 * F), lambda e: (e, 0, 0)),
+            pl.BlockSpec((width, 3 * shared_units), lambda e: (0, 0)),
+        ],
+        out_specs=[
+            pl.BlockSpec((1, token_rows, 2 * F), lambda e: (e, 0, 0)),
+            pl.BlockSpec((1, token_rows, F), lambda e: (e, 0, 0)),
+            pl.BlockSpec((token_rows, 2 * shared_units), lambda e: (0, 0)),
+            pl.BlockSpec((token_rows, shared_units), lambda e: (0, 0)),
+            pl.BlockSpec((token_rows, width), lambda e: (0, 0)),
+        ],
+        out_shape=[
+            jax.ShapeDtypeStruct((local_experts, token_rows, 2 * F), jnp.bfloat16),
+            jax.ShapeDtypeStruct((local_experts, token_rows, F), jnp.bfloat16),
+            jax.ShapeDtypeStruct((token_rows, 2 * shared_units), jnp.bfloat16),
+            jax.ShapeDtypeStruct((token_rows, shared_units), jnp.bfloat16),
+            jax.ShapeDtypeStruct((token_rows, width), jnp.bfloat16),
+        ],
+        scratch_shapes=[pltpu.VMEM((token_rows, width), jnp.float32)],
+        compiler_params=pltpu.CompilerParams(vmem_limit_bytes=48 * 1024 * 1024),
+        name="experts_backward",
+    )(grad, gates, gate_up, shared_gate_up, expert_weight, shared_slice)
+
+
+def weight_grad_kernel(count, *refs):
+    rows, grads = refs[:count], refs[count : 2 * count]
+    front, acts = refs[2 * count : 3 * count], refs[3 * count : 4 * count]
+    out_ref = refs[4 * count]
+    split = front[0].shape[-1]
+    out_ref[:, :split] = sum(
+        dot_first(rows[i][...], front[i][0]) for i in range(count)
+    ).astype(jnp.bfloat16)
+    out_ref[:, split:] = sum(
+        dot_first(grads[i][...], acts[i][0]) for i in range(count)
+    ).astype(jnp.bfloat16)
+
+
+def weight_grad(rows, grads, front, acts, expert):
+    count = len(rows)
+    token_rows, width = rows[0].shape
+    tile = 256
+    front_units, act_units = front[0].shape[-1], acts[0].shape[-1]
+    column = pl.BlockSpec((token_rows, tile), lambda i: (0, i))
+    return pl.pallas_call(
+        lambda *refs: weight_grad_kernel(count, *refs),
+        grid=(width // tile,),
+        in_specs=[column] * (2 * count)
+        + [pl.BlockSpec((1, token_rows, front_units), lambda i: (expert, 0, 0))] * count
+        + [pl.BlockSpec((1, token_rows, act_units), lambda i: (expert, 0, 0))] * count,
+        out_specs=pl.BlockSpec((tile, front_units + act_units), lambda i: (i, 0)),
+        out_shape=jax.ShapeDtypeStruct((width, front_units + act_units), jnp.bfloat16),
+        compiler_params=pltpu.CompilerParams(vmem_limit_bytes=48 * 1024 * 1024),
+        name="weight_grad",
+    )(*rows, *grads, *front, *acts)
+
+
+def plane_places(context_index, token_rows, context_count):
+    blocks = (context_index ^ jnp.arange(8, dtype=jnp.int32))[:, None]
+    return positions(
+        blocks * token_rows + jnp.arange(token_rows, dtype=jnp.int32)[None, :],
+        token_rows,
+        context_count,
+    )
+
+
+def attention_scores(query, keys, key_place, query_place, scale):
+    scores = jnp.einsum("qhd,kd->hqk", query, keys, preferred_element_type=jnp.float32) * scale
+    return jnp.where(key_place[None, None, :] <= query_place[None, :, None], scores, masked_score)
+
+
+def heads_forward(query, keys, values, key_place, query_place, scale):
+    scores = attention_scores(query, keys, key_place, query_place, scale)
+    highest = jnp.max(scores, axis=-1, keepdims=True)
+    powers = jnp.exp(scores - highest)
+    total = jnp.sum(powers, axis=-1, keepdims=True)
+    mixed = jnp.einsum(
+        "hqk,kd->qhd", powers.astype(jnp.bfloat16), values, preferred_element_type=jnp.float32
+    ) / jnp.transpose(total, (1, 0, 2))
+    return mixed, (highest + jnp.log(total))[..., 0]
+
+
+def heads_backward(query, keys, values, key_place, query_place, scale, log_total, mixed, grad):
+    scores = attention_scores(query, keys, key_place, query_place, scale)
+    probs = jnp.exp(scores - log_total[..., None])
+    delta = jnp.sum(grad.astype(jnp.float32) * mixed.astype(jnp.float32), axis=-1).T
+    grad_probs = jnp.einsum("qhd,kd->hqk", grad, values, preferred_element_type=jnp.float32)
+    grad_scores = (probs * (grad_probs - delta[..., None])).astype(jnp.bfloat16)
+    grad_query = (
+        jnp.einsum("hqk,kd->qhd", grad_scores, keys, preferred_element_type=jnp.float32) * scale
+    )
+    grad_keys = (
+        jnp.einsum("hqk,qhd->kd", grad_scores, query, preferred_element_type=jnp.float32) * scale
+    )
+    grad_values = jnp.einsum(
+        "hqk,qhd->kd", probs.astype(jnp.bfloat16), grad, preferred_element_type=jnp.float32
+    )
+    return grad_query, grad_keys, grad_values
+
+
+def fast_device(
+    hidden,
+    teacher,
+    valid_mask,
+    routes,
+    route_gates,
+    gain_in,
+    query_key_value_weight,
+    out_weight,
+    gain_mid,
+    shared_weight,
+    expert_weight,
+):
+    token_rows, width = hidden.shape[1:]
+    context_count, shard_count = 8, 4
+    context_index = lax.axis_index("ctx")
+    shard_index = lax.axis_index("wt")
+    core = context_index & 1
+    chip = context_index >> 1
+    at_end = (shard_index == 0) | (shard_index == shard_count - 1)
+    four = jnp.arange(4, dtype=jnp.int32)
+    eight = jnp.arange(8, dtype=jnp.int32)
+    group = QUERY_HEADS // KEY_VALUE_HEADS
+    group_width = group * HEAD_SIZE
+    query_width = QUERY_HEADS * HEAD_SIZE
+    kv_width = KEY_VALUE_HEADS * HEAD_SIZE
+    slice_width = group_width + 2 * HEAD_SIZE
+    scale = 1.0 / math.sqrt(HEAD_SIZE)
+    all_tokens = token_rows * context_count * shard_count
+    shard_rows = query_key_value_weight.shape[0]
+    half_rows = shard_rows // 2
+    local_experts = expert_weight.shape[0]
+    bf16, f32 = jnp.bfloat16, jnp.float32
+
+    states = jnp.concatenate(chips_gather(hidden[0]), axis=0).astype(f32)
+
+    gains = jnp.stack([gain_in, gain_mid])
+    gains = jnp.stack([gains] + [line_swap(gains, i) for i in (1, 2, 3)])
+    gains = jnp.take(gains, shard_index ^ four, axis=0)
+    gain_in_float = gains[:, 0].reshape(width).astype(f32)
+    gain_mid_float = gains[:, 1].reshape(width).astype(f32)
+
+    def own_heads(rows):
+        return jnp.concatenate(
+            [
+                lax.dynamic_slice_in_dim(rows, chip * group_width, group_width, 1),
+                lax.dynamic_slice_in_dim(rows, query_width + chip * HEAD_SIZE, HEAD_SIZE, 1),
+                lax.dynamic_slice_in_dim(
+                    rows, query_width + kv_width + chip * HEAD_SIZE, HEAD_SIZE, 1
+                ),
+            ],
+            axis=1,
+        )
+
+    def both_cores(mine, axis):
+        other = flip(mine, 1)
+        return jnp.where(
+            core == 0, jnp.stack([mine, other], axis=axis), jnp.stack([other, mine], axis=axis)
+        )
+
+    def half_shard(rows):
+        return lax.dynamic_slice_in_dim(rows, core * half_rows, half_rows, 0)
+
+    qkv_half = jnp.stack(line_gather(own_heads(half_shard(query_key_value_weight)), at_end))
+    qkv_slice = jnp.take(both_cores(qkv_half, 1), shard_index ^ four, axis=0).reshape(
+        width, slice_width
+    )
+
+    scaled_in = states * lax.rsqrt(jnp.mean(states * states, axis=-1, keepdims=True) + norm_eps)
+    normed_in = (scaled_in * gain_in_float).astype(bf16)
+    projected = jnp.dot(normed_in, qkv_slice, preferred_element_type=f32).astype(bf16)
+    key_value = projected[:, group_width:].reshape(4, token_rows, 2 * HEAD_SIZE)
+    key_value = jnp.stack([key_value, flip(key_value, 1)], axis=1)
+    keys = key_value[..., :HEAD_SIZE].reshape(8 * token_rows, HEAD_SIZE)
+    values = key_value[..., HEAD_SIZE:].reshape(8 * token_rows, HEAD_SIZE)
+    places = plane_places(context_index, token_rows, context_count)
+    key_place = places.reshape(-1)
+    query_place = places.reshape(4, 2, token_rows)[:, 0].reshape(-1)
+    query = projected[:, :group_width].reshape(4 * token_rows, group, HEAD_SIZE)
+
+    out_half = jnp.stack(line_gather(half_shard(out_weight), at_end))
+    out_rel = jnp.take(both_cores(out_half, 1), shard_index ^ chip ^ four, axis=0).reshape(
+        query_width, width
+    )
+
+    eighth = shard_rows // 8
+    shared_piece = lax.dynamic_slice_in_dim(shared_weight, context_index * eighth, eighth, 0)
+    shared_units = SF // shard_count
+    shared_piece = shared_piece.reshape(eighth, 3, shard_count, shared_units)
+
+    def shared_columns(index):
+        return lax.dynamic_index_in_dim(shared_piece, shard_index ^ index, 2, keepdims=False)
+
+    shared_pieces = jnp.stack(
+        [shared_columns(0)] + [line_swap(shared_columns(i), i) for i in (1, 2, 3)]
+    ).reshape(4 * eighth, 3 * shared_units)
+    shared_all = plane_gather(shared_pieces).reshape(8, 4, eighth, 3 * shared_units)
+    shared_slice = jnp.transpose(
+        jnp.take(jnp.take(shared_all, context_index ^ eight, axis=0), shard_index ^ four, axis=1),
+        (1, 0, 2, 3),
+    ).reshape(width, 3 * shared_units)
+
+    expert_ids = jnp.arange(EXPERTS, dtype=jnp.int32)
+    gate_matrix = jnp.sum(
+        jnp.where(
+            routes[0][None, :, :] == expert_ids[:, None, None], route_gates[0][None, :, :], 0.0
+        ),
+        axis=-1,
+    ).reshape(shard_count, local_experts, token_rows)
+    gates = [pick(gate_matrix, shard_index)] + [
+        line_swap(pick(gate_matrix, shard_index ^ i), i) for i in (1, 2, 3)
+    ]
+    gates = [part[..., None] for part in gates]
+
+    valid_float = valid_mask[0].astype(f32)
+    valid_count = plane_sum_small(jnp.full((8, 128), jnp.sum(valid_float), f32))
+    valid_count = valid_count + line_swap(valid_count, 1)
+    valid_count = (valid_count + line_swap(valid_count, 2))[0, 0]
+
+    mixed_heads, log_total = heads_forward(query, keys, values, key_place, query_place, scale)
+    mixed_heads = mixed_heads.reshape(4, token_rows, group_width).astype(bf16)
+    mixed = jnp.concatenate(
+        [mixed_heads[0]] + [flip(mixed_heads[r], 2 * r) for r in (1, 2, 3)], axis=1
+    )
+    inputs = hidden[0].astype(f32)
+    middle = inputs + jnp.dot(mixed, out_rel, preferred_element_type=f32)
+    scaled_mid, inverse_mid = normalize(middle)
+    normed_mid = (scaled_mid * gain_mid_float).astype(bf16)
+
+    line_rows = line_gather(normed_mid, at_end)
+    forward = [
+        experts_forward(line_rows[i], gates[i], expert_weight, shared_slice) for i in range(4)
+    ]
+    gate_ups, shared_gate_ups, partial_out = zip(*forward)
+    final_state = middle + line_reduce(partial_out)
+
+    deviation = final_state - teacher[0].astype(f32)
+    squared = jnp.sum(valid_float[:, None] * deviation * deviation)
+    squared = plane_sum_small(jnp.full((8, 128), squared, f32))
+    squared = squared + line_swap(squared, 1)
+    squared = (squared + line_swap(squared, 2))[0, 0]
+    loss_value = 0.5 * squared / (valid_count * width)
+    grad_final = all_tokens / valid_count * valid_float[:, None] * deviation
+
+    line_grads = line_gather(grad_final.astype(bf16), at_end)
+    backward = [
+        experts_backward(
+            line_grads[i], gates[i], gate_ups[i], shared_gate_ups[i], expert_weight, shared_slice
+        )
+        for i in range(4)
+    ]
+    grad_gate_ups, acts, shared_grads, shared_acts, partial_rows = zip(*backward)
+    grad_normed_mid = line_reduce(partial_rows)
+
+    grad_experts = []
+    for expert in range(local_experts):
+        own = weight_grad(line_rows, line_grads, grad_gate_ups, acts, expert)
+        reduced = plane_reduce(own.reshape(8, width // 8, 3 * F), context_index)
+        gathered = jnp.take(plane_gather(reduced), context_index ^ eight, axis=0)
+        grad_experts.append(gathered.reshape(width, 3 * F).astype(f32))
+    grad_experts = jnp.stack(grad_experts)
+
+    own = weight_grad(
+        line_rows, line_grads, [v[None] for v in shared_grads], [v[None] for v in shared_acts], 0
+    )
+    own = jnp.transpose(own.reshape(4, 8, eighth, 3 * shared_units), (1, 0, 2, 3))
+    reduced = plane_reduce(own.reshape(8, 4 * eighth, 3 * shared_units), context_index)
+    reduced = reduced.reshape(4, eighth, 3 * shared_units)
+    reduced = jnp.stack(
+        [pick(reduced, shard_index)]
+        + [line_swap(pick(reduced, shard_index ^ i), i) for i in (1, 2, 3)]
+    )
+    gathered = jnp.take(plane_gather(reduced), context_index ^ eight, axis=0)
+    gathered = jnp.take(gathered, shard_index ^ four, axis=1)
+    grad_shared = jnp.transpose(
+        gathered.reshape(8, 4, eighth, 3, shared_units), (0, 2, 3, 1, 4)
+    ).reshape(shard_rows, 3 * SF)
+    grad_shared = grad_shared.astype(f32)
+
+    grad_gain_mid = jnp.sum(grad_normed_mid * scaled_mid, axis=0)
+    grad_middle = grad_final + norm_back(grad_normed_mid, scaled_mid, inverse_mid, gain_mid_float)
+    grad_branch = grad_middle.astype(bf16)
+    grad_mixed = dot_last(grad_branch, out_rel).astype(bf16)
+    grad_mixed = jnp.stack(
+        [grad_mixed[:, :group_width]]
+        + [
+            flip(grad_mixed[:, r * group_width : (r + 1) * group_width], 2 * r)
+            for r in (1, 2, 3)
+        ]
+    )
+
+    grad_out = dot_first(mixed, grad_branch).astype(bf16).reshape(4, 2, half_rows, width)
+    grad_out = lax.dynamic_index_in_dim(grad_out, core, 1, keepdims=False) + flip(
+        lax.dynamic_index_in_dim(grad_out, 1 - core, 1, keepdims=False), 1
+    )
+    grad_out = line_reduce([pick(grad_out, chip ^ shard_index ^ i) for i in range(4)]).astype(bf16)
+    left, right = grad_out[:, : width // 2], grad_out[:, width // 2 :]
+    left = left + flip(left, 2)
+    right = right + flip(right, 4)
+    left = left + flip(left, 4)
+    right = right + flip(right, 2)
+    grad_out = both_cores(jnp.concatenate([left, right], axis=1), 0)
+    grad_out = grad_out.reshape(shard_rows, width).astype(f32)
+
+    grad_query, grad_keys, grad_values = heads_backward(
+        query,
+        keys,
+        values,
+        key_place,
+        query_place,
+        scale,
+        log_total,
+        mixed_heads.reshape(4 * token_rows, group, HEAD_SIZE),
+        grad_mixed.reshape(4 * token_rows, group, HEAD_SIZE),
+    )
+    grad_kv = jnp.concatenate([grad_keys, grad_values], axis=1)
+    grad_kv = grad_kv.reshape(4, 2, token_rows, 2 * HEAD_SIZE)
+    grad_kv = grad_kv[:, 0] + flip(grad_kv[:, 1].astype(bf16), 1).astype(f32)
+    grad_projected = jnp.concatenate(
+        [
+            grad_query.astype(bf16).reshape(4 * token_rows, group_width),
+            grad_kv.astype(bf16).reshape(4 * token_rows, 2 * HEAD_SIZE),
+        ],
+        axis=1,
+    )
+
+    grad_qkv = dot_first(normed_in, grad_projected).astype(bf16)
+    grad_qkv = grad_qkv.reshape(4, 2, half_rows, slice_width)
+    grad_qkv = lax.dynamic_index_in_dim(grad_qkv, core, 1, keepdims=False) + flip(
+        lax.dynamic_index_in_dim(grad_qkv, 1 - core, 1, keepdims=False), 1
+    )
+    grad_qkv = line_reduce([pick(grad_qkv, shard_index ^ i) for i in range(4)]).astype(bf16)
+    grad_qkv = jnp.stack(chips_gather(grad_qkv))
+    grad_qkv = jnp.take(both_cores(grad_qkv, 1), chip ^ four, axis=0).astype(f32)
+    grad_qkv = grad_qkv.reshape(4, shard_rows, slice_width)
+
+    def side_by_side(columns):
+        return jnp.transpose(columns, (1, 0, 2)).reshape(shard_rows, -1)
+
+    grad_qkv = jnp.concatenate(
+        [
+            side_by_side(grad_qkv[..., :group_width]),
+            side_by_side(grad_qkv[..., group_width : group_width + HEAD_SIZE]),
+            side_by_side(grad_qkv[..., group_width + HEAD_SIZE :]),
+        ],
+        axis=1,
+    )
+
+    qkv_rel = both_cores(
+        jnp.stack(
+            chips_gather(lax.dynamic_slice_in_dim(qkv_slice, core * (width // 2), width // 2, 0))
+        ),
+        1,
+    ).reshape(4, width, slice_width)
+    grad_projected = grad_projected.reshape(4, token_rows, slice_width)
+    grad_projected = jnp.concatenate(
+        [grad_projected[0]] + [flip(grad_projected[r], 2 * r) for r in (1, 2, 3)], axis=1
+    )
+    qkv_rel = jnp.transpose(qkv_rel, (1, 0, 2)).reshape(width, 4 * slice_width)
+    grad_normed_in = dot_last(grad_projected, qkv_rel)
+    scaled_own, inverse_own = normalize(inputs)
+    grad_gain_in = jnp.sum(grad_normed_in * scaled_own, axis=0)
+    grad_inputs = grad_middle + norm_back(grad_normed_in, scaled_own, inverse_own, gain_in_float)
+
+    def gain_sum(local):
+        parts = local.reshape(shard_count, shard_rows)
+        mine = pick(parts, shard_index)
+        for i in (1, 2, 3):
+            mine = mine + line_swap(pick(parts, shard_index ^ i), i)
+        return plane_sum_small(mine)
+
+    return (
+        final_state.astype(bf16)[None],
+        loss_value,
+        grad_inputs[None],
+        gain_sum(grad_gain_in),
+        grad_qkv,
+        grad_out,
+        gain_sum(grad_gain_mid),
+        grad_shared,
+        grad_experts,
+    )
+
+
 def solution(mesh):
     in_specs = (
         P("wt", "ctx", None),
@@ -464,6 +1074,7 @@
         P("wt", None),
         P("wt", None, None),
     )
+    plane_of_eight = dict(mesh.shape) == {"ctx": 8, "wt": 4}
     return jax.shard_map(
-        on_device, mesh=mesh, in_specs=in_specs, out_specs=out_specs, check_vma=False
-    )
+        fast_device if plane_of_eight else on_device, mesh=mesh, in_specs=in_specs, out_specs=out_specs, check_vma=False
+    )

time: 2100 us -> 1050 us (0.50)
  waiting for transfers between devices: 1320 us -> 213 us
  blocking collectives: 230 us -> 0 us
  starting transfers between devices: 17.1 us -> 204 us
  matrix products: 225 us -> 82.4 us
  Pallas kernels: 0 us -> 142 us
  local copies, waits for them, and re-layouts: 137 us -> 195 us
  other arithmetic: 149 us -> 192 us
    all_to_all x3 -> x0, waiting for transfers between devices: 534 us -> none  [the longest x1 281 us: on_device(): lax.all_to_all(expert_rows, 'wt', split_axis=0, concat_axis=0, tiled=True)]
    reduce_scatter x4 -> x0, waiting for transfers between devices: 374 us -> none  [the longest x1 139 us: on_device(): lax.psum_scatter(grad_qkv_local.astype(jnp.bfloat16), 'wt', scatter_dimen...]
    psum x1 -> x0, waiting for transfers between devices: 268 us -> none  [on_device(): lax.psum(expert_grad.astype(jnp.bfloat16), 'ctx').astype(jnp.float32)]
    ppermute x0 -> x163, waiting for transfers between devices: none -> 213 us  [the longest x101 97.4 us: flip(): lax.ppermute(value, 'ctx', [(index, index ^ bit) for index in range(8)])]
    ppermute x0 -> x163, starting transfers between devices: none -> 204 us  [the longest x101 80.7 us: flip(): lax.ppermute(value, 'ctx', [(index, index ^ bit) for index in range(8)])]
    dot_general x46 -> x12, matrix products: 225 us -> 82.4 us  [the longest x1 15.8 us: heads_backward(): jnp.einsum('qhd,kd->hqk', grad, values, preferred_element_type=jnp.float32)]
    pallas_call x0 -> x13, Pallas kernels: none -> 142 us  [the longest x4 50.3 us: experts_backward(): pl.pallas_call(experts_backward_kernel, grid=(local_experts,), in_specs=[...]
    all_to_all x1 -> x0, blocking collectives: 142 us -> none  [on_device(): lax.all_to_all(grad_expert_out, 'wt', split_axis=0, concat_axis=0, tiled=...]
  transfers between devices with their start and end apart: 12 -> 163, of which waited for: 11 -> 51; matrix products, arithmetic and copies ran while one was open for 11% -> 41% of each run, Pallas kernels for 0% -> 12%
where the time goes in v1:
time: 1050 us; the launch traced here: 1040 us
  waiting for transfers between devices  213 us (20%)
  starting transfers between devices  204 us (19%)
  local copies, waits for them, and re-layouts  195 us (19%)
  other arithmetic  192 us (18%)
  Pallas kernels  142 us (14%)
  matrix products  82.4 us (8%)
    ppermute x101, waiting for transfers between devices, flip(): lax.ppermute(value, 'ctx', [(index, index ^ bit) for index in range(8)])  97.4 us
    ppermute x101, starting transfers between devices, flip(): lax.ppermute(value, 'ctx', [(index, index ^ bit) for index in range(8)])  80.7 us
    ppermute x30, waiting for transfers between devices, line_swap(): lax.ppermute(value, 'wt', [(index, index ^ offset) for index in range(4)])  73.1 us
    ppermute x30, starting transfers between devices, line_swap(): lax.ppermute(value, 'wt', [(index, index ^ offset) for index in range(4)])  54.9 us
    pallas_call x4, Pallas kernels, experts_backward(): pl.pallas_call(experts_backward_kernel, grid=(local_experts,), in_specs=[...  50.3 us
    pallas_call x5, Pallas kernels, weight_grad(): pl.pallas_call(lambda *refs: weight_grad_kernel(count, *refs), grid=(widt...  45.9 us
    pallas_call x4, Pallas kernels, experts_forward(): pl.pallas_call(experts_forward_kernel, grid=(local_experts,), in_specs=[p...  45.8 us
    another operation x12, other arithmetic, plane_gather(): jnp.stack([chips, flip(chips, 1)], axis=1).reshape((8,) + value.shape)  40.1 us
  transfers between devices with their start and end apart: 163, of which 51 were waited for; matrix products, arithmetic and copies ran while one was open for 41% of the time, Pallas kernels for 12%

profile of v1, /device:TPU:0, one launch (start us, length us, event | category | flops | bytes accessed | tf_op | source)
XLA Modules:
  0.0 1036.0 jit_solution(9676493222576848000)
XLA Ops:
  43.1 10.3 collective-permute-done.9
  72.2 9.3 collective-permute-done.19
  99.6 11.5 %fusion.5 = (f32[3,1024]{1,0:T(4,128)S(1)}, f32[2048,1024,3]{1,0,2:T(8,128)}) fusion(pred[1024,2048]{0,1:T(8,128)(4,1)S(1)} %copy-done.65, bf16[2048,128,1]{1,0,2:T(8,128)(2,1)S(1)} %bitcast.546, bf16[1024,3,128]{0,2,1:T(8,128)(2,1)S(1)} %bitcast.558), kind=kOutput, calls=%fused_computation.22 | convolution fusion | flops 1629484032 | bytes 28585984 | tf_op jit(solution)/shard_map/qhd,kd->hqk/dot_general | solution.py:735
  111.1 11.5 %fusion.2 = f32[3,1024]{1,0:T(4,128)S(1)} fusion(f32[2048,1024,3]{1,0,2:T(8,128)} %get-tuple-element.185, f32[3,1024]{1,0:T(4,128)S(1)} %get-tuple-element.184, pred[1024,2048]{0,1:T(8,128)(4,1)S(1)} %copy-done.65), kind=kLoop, calls=%fused_computation.18 | loop fusion | flops 25162752 | bytes 27287552 | tf_op jit(solution)/shard_map/reduce_sum | solution.py:743
  126.8 12.5 %fusion.30 = bf16[1024,3,128]{0,2,1:T(8,128)(2,1)S(1)} fusion(bf16[2048,128,1]{0,1,2:T(8,128)(2,1)} %reshape.639, f32[2048,1024,3]{1,0,2:T(8,128)} %get-tuple-element.185, f32[3,1024]{1,0:T(4,128)S(1)} %get-tuple-element.184, pred[1024,2048]{0,1:T(8,128)(4,1)} %broadcast_compare_fusion, f32[1024,3]{0,1:T(4,128)S(1)} %bitcast.582), kind=kOutput, calls=%fused_computation.106 | convolution fusion | flops 1636564992 | bytes 28598272 | tf_op jit(solution)/shard_map/hqk,kd->qhd/dot_general | solution.py:744
  144.5 5.6 maximum_select_fusion.1
  150.2 5.4 gather_fusion.1
  168.6 13.1 %collective-permute-done.31.rows_ref.refs_1_ = bf16[256,1536]{1,0:T(8,128)(2,1)S(1)} collective-permute-done((bf16[256,1536]{1,0:T(8,128)(2,1)S(1)}, bf16[256,1536]{1,0:T(8,128)(2,1)S(1)}, u32[]{:S(2)}, u32[]{:S(2)}) %collective-permute-start.31) | collective-permute-done | bytes 786464 | tf_op jit(solution)/shard_map/ppermute | solution.py:449
  210.7 11.5 %collective-permute-done.37 = bf16[256,1536]{1,0:T(8,128)(2,1)} collective-permute-done((bf16[256,1536]{1,0:T(8,128)(2,1)S(1)}, bf16[256,1536]{1,0:T(8,128)(2,1)}, u32[]{:S(2)}, u32[]{:S(2)}) %collective-permute-start.37) | collective-permute-done | bytes 786464 | tf_op jit(solution)/shard_map/ppermute | solution.py:457
  223.4 12.1 %experts_forward.7 = (bf16[4,256,1024]{2,1,0:T(8,128)(2,1)S(1)}, bf16[256,512]{1,0:T(8,128)(2,1)S(1)}, bf16[256,1536]{1,0:T(8,128)(2,1)}) custom-call(bf16[256,1536]{1,0:T(8,128)(2,1)S(1)} %broadcast_select_fusion.11.rows_ref.refs_3_, f32[4,256,1]{2,1,0:T(8,128)S(1)} %copy.136.gates_ref, bf16[4,1536,1536]{2,1,0:T(8,128)(2,1)} %expert_ref.15, ...), custom_call_target="tpu_custom_call" | custom-call | tf_op jit(solution)/shard_map/experts_forward/pallas_call | solution.py:594
  236.8 8.0 collective-permute-start.39
  244.8 14.3 %collective-permute-done.36 = f32[4,256]{1,0:T(4,128)S(1)} collective-permute-done((f32[4,256]{1,0:T(4,128)S(1)}, f32[4,256]{1,0:T(4,128)S(1)}, u32[]{:S(2)}, u32[]{:S(2)}) %collective-permute-start.36) | collective-permute-done | bytes 4128 | tf_op jit(solution)/shard_map/ppermute | solution.py:449
  261.4 11.2 %experts_forward.6 = (bf16[4,256,1024]{2,1,0:T(8,128)(2,1)S(1)}, bf16[256,512]{1,0:T(8,128)(2,1)S(1)}, bf16[256,1536]{1,0:T(8,128)(2,1)S(1)}) custom-call(bf16[256,1536]{1,0:T(8,128)(2,1)S(1)} %broadcast_select_fusion.12.rows_ref.refs_2_, f32[4,256,1]{2,1,0:T(8,128)S(1)} %copy-done.23, bf16[4,1536,1536]{2,1,0:T(8,128)(2,1)} %expert_ref.15, ...), custom_call_target="tpu_custom_call" | custom-call | tf_op jit(solution)/shard_map/experts_forward/pallas_call | solution.py:594
  276.3 6.2 collective-permute-start.42
  284.1 11.4 %collective-permute-done.32 = f32[4,256]{1,0:T(4,128)S(1)} collective-permute-done((f32[4,256]{1,0:T(4,128)S(1)}, f32[4,256]{1,0:T(4,128)S(1)}, u32[]{:S(2)}, u32[]{:S(2)}) %collective-permute-start.32) | collective-permute-done | bytes 4128 | tf_op jit(solution)/shard_map/ppermute | solution.py:449
  297.5 11.2 %experts_forward.5 = (bf16[4,256,1024]{2,1,0:T(8,128)(2,1)S(1)}, bf16[256,512]{1,0:T(8,128)(2,1)S(1)}, bf16[256,1536]{1,0:T(8,128)(2,1)S(1)}) custom-call(bf16[256,1536]{1,0:T(8,128)(2,1)S(1)} %collective-permute-done.31.rows_ref.refs_1_, f32[4,256,1]{2,1,0:T(8,128)S(1)} %copy-done.25, bf16[4,1536,1536]{2,1,0:T(8,128)(2,1)} %expert_ref.15, ...), custom_call_target="tpu_custom_call" | custom-call | tf_op jit(solution)/shard_map/experts_forward/pallas_call | solution.py:594
  339.8 11.3 %experts_forward.4 = (bf16[4,256,1024]{2,1,0:T(8,128)(2,1)S(1)}, bf16[256,512]{1,0:T(8,128)(2,1)S(1)}, bf16[256,1536]{1,0:T(8,128)(2,1)S(1)}) custom-call(bf16[256,1536]{1,0:T(8,128)(2,1)S(1)} %multiply_convert_fusion.1.rows_ref.refs_0_, f32[4,256,1]{2,1,0:T(8,128)S(1)} %copy.133.gates_ref, bf16[4,1536,1536]{2,1,0:T(8,128)(2,1)} %expert_ref.15, ...), custom_call_target="tpu_custom_call" | custom-call | tf_op jit(solution)/shard_map/experts_forward/pallas_call | solution.py:594
  361.0 11.1 %collective-permute-done.54.grad_ref.refs_5_ = bf16[256,1536]{1,0:T(8,128)(2,1)} collective-permute-done((bf16[256,1536]{1,0:T(8,128)(2,1)S(1)}, bf16[256,1536]{1,0:T(8,128)(2,1)}, u32[]{:S(2)}, u32[]{:S(2)}) %collective-permute-start.54) | collective-permute-done | bytes 786464 | tf_op jit(solution)/shard_map/ppermute | solution.py:449
  392.4 12.5 %experts_backward.4 = (bf16[4,256,1024]{2,1,0:T(8,128)(2,1)S(1)}, bf16[4,256,512]{2,1,0:T(8,128)(2,1)S(1)}, bf16[256,512]{1,0:T(8,128)(2,1)S(1)}, bf16[256,256]{1,0:T(8,128)(2,1)S(1)}, bf16[256,1536]{1,0:T(8,128)(2,1)S(1)}) custom-call(bf16[256,1536]{1,0:T(8,128)(2,1)S(1)} %get-tuple-element.91.grad_ref.refs_4_, f32[4,256,1]{2,1,0:T(8,128)S(1)} %copy-done.28, ...), custom_call_target="tpu_custom_call" | custom-call | tf_op jit(solution)/shard_map/experts_backward/pallas_call | solution.py:662
  408.1 12.7 %experts_backward.5 = (bf16[4,256,1024]{2,1,0:T(8,128)(2,1)S(1)}, bf16[4,256,512]{2,1,0:T(8,128)(2,1)S(1)}, bf16[256,512]{1,0:T(8,128)(2,1)S(1)}, bf16[256,256]{1,0:T(8,128)(2,1)S(1)}, bf16[256,1536]{1,0:T(8,128)(2,1)S(1)}) custom-call(bf16[256,1536]{1,0:T(8,128)(2,1)} %collective-permute-done.54.grad_ref.refs_5_, f32[4,256,1]{2,1,0:T(8,128)S(1)} %copy-done.26, ...), custom_call_target="tpu_custom_call" | custom-call | tf_op jit(solution)/shard_map/experts_backward/pallas_call | solution.py:662
  424.1 12.6 %experts_backward.6 = (bf16[4,256,1024]{2,1,0:T(8,128)(2,1)S(1)}, bf16[4,256,512]{2,1,0:T(8,128)(2,1)S(1)}, bf16[256,512]{1,0:T(8,128)(2,1)S(1)}, bf16[256,256]{1,0:T(8,128)(2,1)S(1)}, bf16[256,1536]{1,0:T(8,128)(2,1)S(1)}) custom-call(bf16[256,1536]{1,0:T(8,128)(2,1)S(1)} %broadcast_select_fusion.10.grad_ref.refs_6_, f32[4,256,1]{2,1,0:T(8,128)S(1)} %copy-done.24, ...), custom_call_target="tpu_custom_call" | custom-call | tf_op jit(solution)/shard_map/experts_backward/pallas_call | solution.py:662
  440.5 12.5 %experts_backward.7 = (bf16[4,256,1024]{2,1,0:T(8,128)(2,1)S(1)}, bf16[4,256,512]{2,1,0:T(8,128)(2,1)S(1)}, bf16[256,512]{1,0:T(8,128)(2,1)S(1)}, bf16[256,256]{1,0:T(8,128)(2,1)S(1)}, bf16[256,1536]{1,0:T(8,128)(2,1)S(1)}) custom-call(bf16[256,1536]{1,0:T(8,128)(2,1)S(1)} %broadcast_select_fusion.9.grad_ref.refs_7_, f32[4,256,1]{2,1,0:T(8,128)S(1)} %copy-done.22, ...), custom_call_target="tpu_custom_call" | custom-call | tf_op jit(solution)/shard_map/experts_backward/pallas_call | solution.py:662
  455.3 7.1 weight_grad.5
  476.7 10.2 collective-permute-start.59
  488.0 9.7 weight_grad.6
  503.1 9.6 weight_grad.7
  515.0 7.6 collective-permute-done.111
  541.8 7.8 maximum_select_fusion
  549.6 10.7 %copy.151 = bf16[1536,4,640]{0,2,1:T(8,128)(2,1)} copy(bf16[1536,4,640]{2,0,1:T(8,128)(2,1)} %bitcast.488) | data formatting | bytes 15728640 | tf_op jit(solution)/shard_map/transpose | solution.py:1026
  562.6 9.7 weight_grad.8
  572.3 9.8 weight_grad.9
  584.2 6.4 collective-permute-done.118
  665.7 12.8 %fusion.15 = f32[2048,128]{0,1:T(8,128)} fusion(bf16[1024,3,128]{0,2,1:T(8,128)(2,1)} %reshape.476, f32[2048,1024,3]{1,0,2:T(8,128)} %get-tuple-element.185, f32[3,1024]{1,0:T(4,128)S(1)} %copy-done.150, pred[1024,2048]{0,1:T(8,128)(4,1)S(1)} %copy-done.66), kind=kOutput, calls=%fused_computation.50 | convolution fusion | flops 1635778560 | bytes 29110272 | tf_op jit(solution)/shard_map/hqk,qhd->kd/dot_general | solution.py:762
  678.5 15.8 %fusion.1 = bf16[3,1024,2048]{1,2,0:T(8,128)(2,1)} fusion(f32[2048,1024,3]{1,0,2:T(8,128)} %get-tuple-element.185, f32[3,1024]{1,0:T(4,128)S(1)} %bitcast.586, f32[3,1024]{1,0:T(4,128)S(1)} %copy-done.150, pred[1024,2048]{0,1:T(8,128)(4,1)S(1)} %copy-done.66, bf16[2048,128,1]{1,0,2:T(8,128)(2,1)} %bitcast.565, bf16[1024,3,128]{0,2,1:T(8,128)(2,1)} %reshape.476), kind=kOutput, calls=%fused_computation.14 | convolution fusion | flops 1648361472 | bytes 41181184 | tf_op jit(solution)/shard_map/qhd,kd->hqk/dot_general | solution.py:754
  694.3 9.1 fusion.18
  741.8 5.8 collective-permute-done.156
  816.1 6.6 collective-permute-done.81
  827.9 8.2 reshape.511
  836.1 7.9 copy.158
  844.0 6.7 reshape.510
  868.9 10.7 %collective-permute-done.158 = bf16[192,1536]{1,0:T(8,128)(2,1)S(1)} collective-permute-done((bf16[192,1536]{1,0:T(8,128)(2,1)}, bf16[192,1536]{1,0:T(8,128)(2,1)S(1)}, u32[]{:S(2)}, u32[]{:S(2)}) %collective-permute-start.158) | collective-permute-done | bytes 589856 | tf_op jit(solution)/shard_map/ppermute | solution.py:445
  933.4 7.5 collective-permute-done.97
  956.3 10.6 %collective-permute-start.96 = (bf16[192,1536]{1,0:T(8,128)(2,1)}, bf16[192,1536]{1,0:T(8,128)(2,1)}, u32[]{:S(2)}, u32[]{:S(2)}) collective-permute-start(bf16[192,1536]{1,0:T(8,128)(2,1)} %bitcast_add_fusion.17), channel_id=1, source_target_pairs={{0,1},{1,0},{2,3},{3,2},{4,5},{5,4},{6,7},{7,6},{8,9},{9,8},{10,11... | collective-permute-start | bytes 1769480 | tf_op jit(solution)/shard_map/ppermute | solution.py:449
  971.2 5.6 gather_fusion.8
  981.1 5.5 gather_fusion.9
  1004.4 5.4 gather_fusion.11
  1012.4 7.3 broadcast_select_fusion.3
  1020.1 12.6 %maximum_convert_fusion = f32[4,1536,1536]{2,1,0:T(8,128)} fusion(bf16[1,1536,1536]{2,1,0:T(8,128)(2,1)S(1)} %bitcast.493, bf16[1,1536,1536]{2,1,0:T(8,128)(2,1)S(1)} %bitcast.492, bf16[1,1536,1536]{2,1,0:T(8,128)(2,1)S(1)} %bitcast.491, bf16[1,1536,1536]{2,1,0:T(8,128)(2,1)S(1)} %bitcast.490), kind=kLoop, calls=%fused_computation.21 | loop fusion | flops 37748736 | bytes 56623104 | tf_op jit(solution)/shard_map/stack | solution.py:928
  (985 shorter events, 564.0 us)
Async XLA Ops:
  3.8 31.2 %collective-permute-start.7 = (bf16[192,640]{1,0:T(8,128)(2,1)}, bf16[192,640]{1,0:T(8,128)(2,1)}, u32[]{:S(2)}, u32[]{:S(2)}) collective-permute-start(bf16[192,640]{1,0:T(8,128)(2,1)} %get-tuple-element.169), channel_id=1, source_target_pairs={{0,1},{1,0},{2,3},{3,2},{4,5},{5,4},{6,7},{7,6},{8,9},{9,8},{10,11... | collective-permute-start | bytes 737288 | tf_op jit(solution)/shard_map/ppermute | solution.py:449
  6.8 30.1 %collective-permute-start.8 = (bf16[192,640]{1,0:T(8,128)(2,1)}, bf16[192,640]{1,0:T(8,128)(2,1)}, u32[]{:S(2)}, u32[]{:S(2)}) collective-permute-start(bf16[192,640]{1,0:T(8,128)(2,1)} %get-tuple-element.169), channel_id=1, source_target_pairs={{1,2},{2,1},{5,6},{6,5},{9,10},{10,9},{13,14},{14,13},{17,18},{18,... | collective-permute-start | bytes 737288 | tf_op jit(solution)/shard_map/ppermute | solution.py:453
  36.9 23.0 %collective-permute-start = (bf16[256,1536]{1,0:T(8,128)(2,1)S(1)}, bf16[256,1536]{1,0:T(8,128)(2,1)S(1)}, u32[]{:S(2)}, u32[]{:S(2)}) collective-permute-start(bf16[256,1536]{1,0:T(8,128)(2,1)S(1)} %bitcast.529), channel_id=1, source_target_pairs={{0,8},{4,12},{8,0},{12,4},{16,24},{20,28},{24,16},{28,20},{1,9},{5... | collective-permute-start | bytes 2359304 | tf_op jit(solution)/shard_map/ppermute | solution.py:445
  37.6 22.7 %collective-permute-start.1 = (bf16[256,1536]{1,0:T(8,128)(2,1)S(1)}, bf16[256,1536]{1,0:T(8,128)(2,1)S(1)}, u32[]{:S(2)}, u32[]{:S(2)}) collective-permute-start(bf16[256,1536]{1,0:T(8,128)(2,1)S(1)} %bitcast.530), channel_id=1, source_target_pairs={{0,16},{4,20},{8,24},{12,28},{16,0},{20,4},{24,8},{28,12},{1,17},{... | collective-permute-start | bytes 2359304 | tf_op jit(solution)/shard_map/ppermute | solution.py:445
  55.1 109.7 %collective-permute-start.29 = (bf16[96,768]{1,0:T(8,128)(2,1)}, bf16[96,768]{1,0:T(8,128)(2,1)}, u32[]{:S(2)}, u32[]{:S(2)}) collective-permute-start(bf16[96,768]{1,0:T(8,128)(2,1)} %slice.276), channel_id=1, source_target_pairs={{0,8},{4,12},{8,0},{12,4},{16,24},{20,28},{24,16},{28,20},{1,9},{5... | collective-permute-start | bytes 442376 | tf_op jit(solution)/shard_map/ppermute | solution.py:445
  61.7 103.2 %collective-permute-start.28 = (bf16[96,768]{1,0:T(8,128)(2,1)}, bf16[96,768]{1,0:T(8,128)(2,1)}, u32[]{:S(2)}, u32[]{:S(2)}) collective-permute-start(bf16[96,768]{1,0:T(8,128)(2,1)} %slice.275), channel_id=1, source_target_pairs={{0,16},{4,20},{8,24},{12,28},{16,0},{20,4},{24,8},{28,12},{1,17},{... | collective-permute-start | bytes 442376 | tf_op jit(solution)/shard_map/ppermute | solution.py:445
  70.1 23.1 %collective-permute-start.21 = (bf16[192,1536]{1,0:T(8,128)(2,1)}, bf16[192,1536]{1,0:T(8,128)(2,1)}, u32[]{:S(2)}, u32[]{:S(2)}) collective-permute-start(bf16[192,1536]{1,0:T(8,128)(2,1)} %collective-permute-done.20), channel_id=1, source_target_pairs={{1,0},{2,3},{5,4},{6,7},{9,8},{10,11},{13,12},{14,15},{17,16},{18,... | collective-permute-start | bytes 1769480 | tf_op jit(solution)/shard_map/ppermute | solution.py:457
  97.3 46.3 %collective-permute-start.22 = (bf16[4,192,1536]{2,1,0:T(8,128)(2,1)}, bf16[4,192,1536]{2,1,0:T(8,128)(2,1)}, u32[]{:S(2)}, u32[]{:S(2)}) collective-permute-start(bf16[4,192,1536]{2,1,0:T(8,128)(2,1)} %get-tuple-element.116), channel_id=1, source_target_pairs={{0,4},{4,0},{8,12},{12,8},{16,20},{20,16},{24,28},{28,24},{1,5},{5... | collective-permute-start | bytes 7077896 | tf_op jit(solution)/shard_map/ppermute | solution.py:445
  168.6 23.0 %collective-permute-start.30 = (bf16[4,192,768]{2,1,0:T(8,128)(2,1)}, bf16[4,192,768]{2,1,0:T(8,128)(2,1)}, u32[]{:S(2)}, u32[]{:S(2)}) collective-permute-start(bf16[4,192,768]{2,1,0:T(8,128)(2,1)} %get-tuple-element.129), channel_id=1, source_target_pairs={{0,4},{4,0},{8,12},{12,8},{16,20},{20,16},{24,28},{28,24},{1,5},{5... | collective-permute-start | bytes 3538952 | tf_op jit(solution)/shard_map/ppermute | solution.py:445
  189.9 32.3 %collective-permute-start.37 = (bf16[256,1536]{1,0:T(8,128)(2,1)S(1)}, bf16[256,1536]{1,0:T(8,128)(2,1)}, u32[]{:S(2)}, u32[]{:S(2)}) collective-permute-start(bf16[256,1536]{1,0:T(8,128)(2,1)S(1)} %collective-permute-done.35), channel_id=1, source_target_pairs={{1,0},{2,3},{5,4},{6,7},{9,8},{10,11},{13,12},{14,15},{17,16},{18,... | collective-permute-start | bytes 2359304 | tf_op jit(solution)/shard_map/ppermute | solution.py:457
  209.4 50.8 %collective-permute-start.34 = (bf16[256,1536]{1,0:T(8,128)(2,1)}, bf16[256,1536]{1,0:T(8,128)(2,1)}, u32[]{:S(2)}, u32[]{:S(2)}) collective-permute-start(bf16[256,1536]{1,0:T(8,128)(2,1)} %collective-permute-done.33), channel_id=1, source_target_pairs={{1,0},{2,3},{5,4},{6,7},{9,8},{10,11},{13,12},{14,15},{17,16},{18,... | collective-permute-start | bytes 2359304 | tf_op jit(solution)/shard_map/ppermute | solution.py:457
  236.8 37.2 %collective-permute-start.39 = (bf16[256,1536]{1,0:T(8,128)(2,1)}, bf16[256,1536]{1,0:T(8,128)(2,1)}, u32[]{:S(2)}, u32[]{:S(2)}) collective-permute-start(bf16[256,1536]{1,0:T(8,128)(2,1)} %get-tuple-element.48), channel_id=1, source_target_pairs={{0,1},{3,2},{4,5},{7,6},{8,9},{11,10},{12,13},{15,14},{16,17},{19,... | collective-permute-start | bytes 2359304 | tf_op jit(solution)/shard_map/ppermute | solution.py:461
  276.3 32.5 %collective-permute-start.42 = (bf16[256,1536]{1,0:T(8,128)(2,1)}, bf16[256,1536]{1,0:T(8,128)(2,1)}, u32[]{:S(2)}, u32[]{:S(2)}) collective-permute-start(bf16[256,1536]{1,0:T(8,128)(2,1)} %add.570), channel_id=1, source_target_pairs={{0,1},{3,2},{4,5},{7,6},{8,9},{11,10},{12,13},{15,14},{16,17},{19,... | collective-permute-start | bytes 2359304 | tf_op jit(solution)/shard_map/ppermute | solution.py:461
  282.5 31.1 %collective-permute-start.40 = (bf16[256,1536]{1,0:T(8,128)(2,1)}, bf16[256,1536]{1,0:T(8,128)(2,1)}, u32[]{:S(2)}, u32[]{:S(2)}) collective-permute-start(bf16[256,1536]{1,0:T(8,128)(2,1)} %add.570), channel_id=1, source_target_pairs={{1,2},{2,1},{5,6},{6,5},{9,10},{10,9},{13,14},{14,13},{17,18},{18,... | collective-permute-start | bytes 2359304 | tf_op jit(solution)/shard_map/ppermute | solution.py:453
  312.1 39.8 %collective-permute-start.43 = (bf16[256,1536]{1,0:T(8,128)(2,1)}, bf16[256,1536]{1,0:T(8,128)(2,1)}, u32[]{:S(2)}, u32[]{:S(2)}) collective-permute-start(bf16[256,1536]{1,0:T(8,128)(2,1)} %add.573), channel_id=1, source_target_pairs={{1,2},{2,1},{5,6},{6,5},{9,10},{10,9},{13,14},{14,13},{17,18},{18,... | collective-permute-start | bytes 2359304 | tf_op jit(solution)/shard_map/ppermute | solution.py:453
  315.8 36.0 %collective-permute-start.41 = (bf16[256,1536]{1,0:T(8,128)(2,1)}, bf16[256,1536]{1,0:T(8,128)(2,1)}, u32[]{:S(2)}, u32[]{:S(2)}) collective-permute-start(bf16[256,1536]{1,0:T(8,128)(2,1)} %add.571), channel_id=1, source_target_pairs={{0,1},{1,0},{2,3},{3,2},{4,5},{5,4},{6,7},{7,6},{8,9},{9,8},{10,11... | collective-permute-start | bytes 2359304 | tf_op jit(solution)/shard_map/ppermute | solution.py:449
  373.7 48.4 %collective-permute-start.56 = (bf16[256,1536]{1,0:T(8,128)(2,1)}, bf16[256,1536]{1,0:T(8,128)(2,1)}, u32[]{:S(2)}, u32[]{:S(2)}) collective-permute-start(bf16[256,1536]{1,0:T(8,128)(2,1)} %collective-permute-done.55), channel_id=1, source_target_pairs={{1,0},{2,3},{5,4},{6,7},{9,8},{10,11},{13,12},{14,15},{17,16},{18,... | collective-permute-start | bytes 2359304 | tf_op jit(solution)/shard_map/ppermute | solution.py:457
  383.3 55.7 %collective-permute-start.58 = (bf16[256,1536]{1,0:T(8,128)(2,1)}, bf16[256,1536]{1,0:T(8,128)(2,1)S(1)}, u32[]{:S(2)}, u32[]{:S(2)}) collective-permute-start(bf16[256,1536]{1,0:T(8,128)(2,1)} %collective-permute-done.57), channel_id=1, source_target_pairs={{1,0},{2,3},{5,4},{6,7},{9,8},{10,11},{13,12},{14,15},{17,16},{18,... | collective-permute-start | bytes 2359304 | tf_op jit(solution)/shard_map/ppermute | solution.py:457
  466.8 30.9 %collective-permute-start.110 = (bf16[4,192,768]{2,1,0:T(8,128)(2,1)}, bf16[4,192,768]{2,1,0:T(8,128)(2,1)}, u32[]{:S(2)}, u32[]{:S(2)}) collective-permute-start(bf16[4,192,768]{2,1,0:T(8,128)(2,1)} %dynamic-slice_bitcast_fusion.5), channel_id=1, source_target_pairs={{0,4},{4,0},{8,12},{12,8},{16,20},{20,16},{24,28},{28,24},{1,5},{5... | collective-permute-start | bytes 3538952 | tf_op jit(solution)/shard_map/ppermute | solution.py:445
  470.5 70.5 %collective-permute-start.75 = (bf16[4,768,640]{2,1,0:T(8,128)(2,1)}, bf16[4,768,640]{2,1,0:T(8,128)(2,1)}, u32[]{:S(2)}, u32[]{:S(2)}) collective-permute-start(bf16[4,768,640]{2,1,0:T(8,128)(2,1)} %get-tuple-element.96), channel_id=1, source_target_pairs={{0,4},{4,0},{8,12},{12,8},{16,20},{20,16},{24,28},{28,24},{1,5},{5... | collective-permute-start | bytes 11796488 | tf_op jit(solution)/shard_map/ppermute | solution.py:445
  476.7 53.7 %collective-permute-start.59 = (bf16[256,1536]{1,0:T(8,128)(2,1)}, bf16[256,1536]{1,0:T(8,128)(2,1)S(1)}, u32[]{:S(2)}, u32[]{:S(2)}) collective-permute-start(bf16[256,1536]{1,0:T(8,128)(2,1)} %copy-done.37), channel_id=1, source_target_pairs={{0,1},{3,2},{4,5},{7,6},{8,9},{11,10},{12,13},{15,14},{16,17},{19,... | collective-permute-start | bytes 2359304 | tf_op jit(solution)/shard_map/ppermute | solution.py:461
  503.1 98.2 %collective-permute-start.123 = (bf16[4,192,1536]{2,1,0:T(8,128)(2,1)}, bf16[4,192,1536]{2,1,0:T(8,128)(2,1)}, u32[]{:S(2)}, u32[]{:S(2)}) collective-permute-start(bf16[4,192,1536]{2,1,0:T(8,128)(2,1)} %dynamic-slice_bitcast_fusion.3), channel_id=1, source_target_pairs={{0,4},{4,0},{8,12},{12,8},{16,20},{20,16},{24,28},{28,24},{1,5},{5... | collective-permute-start | bytes 7077896 | tf_op jit(solution)/shard_map/ppermute | solution.py:445
  535.2 72.2 %collective-permute-start.133 = (bf16[4,192,1536]{2,1,0:T(8,128)(2,1)}, bf16[4,192,1536]{2,1,0:T(8,128)(2,1)}, u32[]{:S(2)}, u32[]{:S(2)}) collective-permute-start(bf16[4,192,1536]{2,1,0:T(8,128)(2,1)} %dynamic-slice_bitcast_fusion.2), channel_id=1, source_target_pairs={{0,4},{4,0},{8,12},{12,8},{16,20},{20,16},{24,28},{28,24},{1,5},{5... | collective-permute-start | bytes 7077896 | tf_op jit(solution)/shard_map/ppermute | solution.py:445
  536.1 55.4 %collective-permute-start.62 = (bf16[256,1536]{1,0:T(8,128)(2,1)}, bf16[256,1536]{1,0:T(8,128)(2,1)}, u32[]{:S(2)}, u32[]{:S(2)}) collective-permute-start(bf16[256,1536]{1,0:T(8,128)(2,1)} %add.586), channel_id=1, source_target_pairs={{0,1},{3,2},{4,5},{7,6},{8,9},{11,10},{12,13},{15,14},{16,17},{19,... | collective-permute-start | bytes 2359304 | tf_op jit(solution)/shard_map/ppermute | solution.py:461
  538.7 56.8 %collective-permute-start.60 = (bf16[256,1536]{1,0:T(8,128)(2,1)}, bf16[256,1536]{1,0:T(8,128)(2,1)}, u32[]{:S(2)}, u32[]{:S(2)}) collective-permute-start(bf16[256,1536]{1,0:T(8,128)(2,1)} %add.586), channel_id=1, source_target_pairs={{1,2},{2,1},{5,6},{6,5},{9,10},{10,9},{13,14},{14,13},{17,18},{18,... | collective-permute-start | bytes 2359304 | tf_op jit(solution)/shard_map/ppermute | solution.py:453
  541.0 41.1 %collective-permute-start.119 = (bf16[4,48,768]{2,1,0:T(8,128)(2,1)}, bf16[4,48,768]{2,1,0:T(8,128)(2,1)}, u32[]{:S(2)}, u32[]{:S(2)}) collective-permute-start(bf16[4,48,768]{2,1,0:T(8,128)(2,1)} %get-tuple-element.159), channel_id=1, source_target_pairs={{0,16},{4,20},{8,24},{12,28},{16,0},{20,4},{24,8},{28,12},{1,17},{... | collective-permute-start | bytes 884744 | tf_op jit(solution)/shard_map/ppermute | solution.py:445
  651.6 152.0 %collective-permute-start.122 = (bf16[4,4,48,768]{3,2,1,0:T(8,128)(2,1)}, bf16[4,4,48,768]{3,2,1,0:T(8,128)(2,1)}, u32[]{:S(2)}, u32[]{:S(2)}) collective-permute-start(bf16[4,4,48,768]{3,2,1,0:T(8,128)(2,1)} %get-tuple-element.125), channel_id=1, source_target_pairs={{0,4},{4,0},{8,12},{12,8},{16,20},{20,16},{24,28},{28,24},{1,5},{5... | collective-permute-start | bytes 3538952 | tf_op jit(solution)/shard_map/ppermute | solution.py:445
  652.7 67.8 %collective-permute-start.126 = (bf16[2,192,768]{2,1,0:T(8,128)(2,1)}, bf16[2,192,768]{2,1,0:T(8,128)(2,1)}, u32[]{:S(2)}, u32[]{:S(2)}) collective-permute-start(bf16[2,192,768]{2,1,0:T(8,128)(2,1)} %dynamic-slice_bitcast_fusion.13), channel_id=1, source_target_pairs={{0,16},{4,20},{8,24},{12,28},{16,0},{20,4},{24,8},{28,12},{1,17},{... | collective-permute-start | bytes 1769480 | tf_op jit(solution)/shard_map/ppermute | solution.py:445
  655.0 68.0 %collective-permute-start.124 = (bf16[2,192,768]{2,1,0:T(8,128)(2,1)}, bf16[2,192,768]{2,1,0:T(8,128)(2,1)}, u32[]{:S(2)}, u32[]{:S(2)}) collective-permute-start(bf16[2,192,768]{2,1,0:T(8,128)(2,1)} %dynamic-slice_bitcast_fusion.14), channel_id=1, source_target_pairs={{0,8},{4,12},{8,0},{12,4},{16,24},{20,28},{24,16},{28,20},{1,9},{5... | collective-permute-start | bytes 1769480 | tf_op jit(solution)/shard_map/ppermute | solution.py:445
  656.3 70.0 %collective-permute-start.136 = (bf16[2,192,768]{2,1,0:T(8,128)(2,1)}, bf16[2,192,768]{2,1,0:T(8,128)(2,1)}, u32[]{:S(2)}, u32[]{:S(2)}) collective-permute-start(bf16[2,192,768]{2,1,0:T(8,128)(2,1)} %dynamic-slice_bitcast_fusion.11), channel_id=1, source_target_pairs={{0,16},{4,20},{8,24},{12,28},{16,0},{20,4},{24,8},{28,12},{1,17},{... | collective-permute-start | bytes 1769480 | tf_op jit(solution)/shard_map/ppermute | solution.py:445
  657.2 72.8 %collective-permute-start.134 = (bf16[2,192,768]{2,1,0:T(8,128)(2,1)}, bf16[2,192,768]{2,1,0:T(8,128)(2,1)}, u32[]{:S(2)}, u32[]{:S(2)}) collective-permute-start(bf16[2,192,768]{2,1,0:T(8,128)(2,1)} %dynamic-slice_bitcast_fusion.12), channel_id=1, source_target_pairs={{0,8},{4,12},{8,0},{12,4},{16,24},{20,28},{24,16},{28,20},{1,9},{5... | collective-permute-start | bytes 1769480 | tf_op jit(solution)/shard_map/ppermute | solution.py:445
  739.6 23.0 %collective-permute-start.127 = (bf16[192,768]{1,0:T(8,128)(2,1)}, bf16[192,768]{1,0:T(8,128)(2,1)}, u32[]{:S(2)}, u32[]{:S(2)}) collective-permute-start(bf16[192,768]{1,0:T(8,128)(2,1)} %dynamic-slice_bitcast_fusion.22), channel_id=1, source_target_pairs={{0,8},{4,12},{8,0},{12,4},{16,24},{20,28},{24,16},{28,20},{1,9},{5... | collective-permute-start | bytes 884744 | tf_op jit(solution)/shard_map/ppermute | solution.py:445
  769.6 26.7 %collective-permute-start.155 = (bf16[192,768]{1,0:T(8,128)(2,1)}, bf16[192,768]{1,0:T(8,128)(2,1)S(1)}, u32[]{:S(2)}, u32[]{:S(2)}) collective-permute-start(bf16[192,768]{1,0:T(8,128)(2,1)} %dynamic-slice_bitcast_fusion.17), channel_id=1, source_target_pairs={{0,16},{4,20},{8,24},{12,28},{16,0},{20,4},{24,8},{28,12},{1,17},{... | collective-permute-start | bytes 884744 | tf_op jit(solution)/shard_map/ppermute | solution.py:445
  786.1 94.5 %collective-permute-start.82 = (bf16[4,192,640]{2,1,0:T(8,128)(2,1)}, bf16[4,192,640]{2,1,0:T(8,128)(2,1)}, u32[]{:S(2)}, u32[]{:S(2)}) collective-permute-start(bf16[4,192,640]{2,1,0:T(8,128)(2,1)} %dynamic-slice_bitcast_fusion.6), channel_id=1, source_target_pairs={{0,4},{4,0},{8,12},{12,8},{16,20},{20,16},{24,28},{28,24},{1,5},{5... | collective-permute-start | bytes 2949128 | tf_op jit(solution)/shard_map/ppermute | solution.py:445
  799.7 24.5 %collective-permute-start.129 = (bf16[192,1536]{1,0:T(8,128)(2,1)}, bf16[192,1536]{1,0:T(8,128)(2,1)}, u32[]{:S(2)}, u32[]{:S(2)}) collective-permute-start(bf16[192,1536]{1,0:T(8,128)(2,1)} %get-tuple-element.145), channel_id=1, source_target_pairs={{0,16},{4,20},{8,24},{12,28},{16,0},{20,4},{24,8},{28,12},{1,17},{... | collective-permute-start | bytes 1769480 | tf_op jit(solution)/shard_map/ppermute | solution.py:445
  800.6 50.2 %collective-permute-start.128 = (bf16[192,1536]{1,0:T(8,128)(2,1)}, bf16[192,1536]{1,0:T(8,128)(2,1)}, u32[]{:S(2)}, u32[]{:S(2)}) collective-permute-start(bf16[192,1536]{1,0:T(8,128)(2,1)} %get-tuple-element.145), channel_id=1, source_target_pairs={{0,8},{4,12},{8,0},{12,4},{16,24},{20,28},{24,16},{28,20},{1,9},{5... | collective-permute-start | bytes 1769480 | tf_op jit(solution)/shard_map/ppermute | solution.py:445
  802.5 48.3 %collective-permute-start.139 = (bf16[192,1536]{1,0:T(8,128)(2,1)}, bf16[192,1536]{1,0:T(8,128)(2,1)}, u32[]{:S(2)}, u32[]{:S(2)}) collective-permute-start(bf16[192,1536]{1,0:T(8,128)(2,1)} %get-tuple-element.147), channel_id=1, source_target_pairs={{0,16},{4,20},{8,24},{12,28},{16,0},{20,4},{24,8},{28,12},{1,17},{... | collective-permute-start | bytes 1769480 | tf_op jit(solution)/shard_map/ppermute | solution.py:445
  822.7 29.1 %collective-permute-start.138 = (bf16[192,1536]{1,0:T(8,128)(2,1)}, bf16[192,1536]{1,0:T(8,128)(2,1)}, u32[]{:S(2)}, u32[]{:S(2)}) collective-permute-start(bf16[192,1536]{1,0:T(8,128)(2,1)} %get-tuple-element.147), channel_id=1, source_target_pairs={{0,8},{4,12},{8,0},{12,4},{16,24},{20,28},{24,16},{28,20},{1,9},{5... | collective-permute-start | bytes 1769480 | tf_op jit(solution)/shard_map/ppermute | solution.py:445
  824.1 28.5 %collective-permute-start.149 = (bf16[192,1536]{1,0:T(8,128)(2,1)}, bf16[192,1536]{1,0:T(8,128)(2,1)}, u32[]{:S(2)}, u32[]{:S(2)}) collective-permute-start(bf16[192,1536]{1,0:T(8,128)(2,1)} %get-tuple-element.149), channel_id=1, source_target_pairs={{0,16},{4,20},{8,24},{12,28},{16,0},{20,4},{24,8},{28,12},{1,17},{... | collective-permute-start | bytes 1769480 | tf_op jit(solution)/shard_map/ppermute | solution.py:445
  850.8 52.5 %collective-permute-start.93 = (bf16[4,192,1536]{2,1,0:T(8,128)(2,1)}, bf16[4,192,1536]{2,1,0:T(8,128)(2,1)S(1)}, u32[]{:S(2)}, u32[]{:S(2)}) collective-permute-start(bf16[4,192,1536]{2,1,0:T(8,128)(2,1)} %dynamic-slice_bitcast_fusion.4), channel_id=1, source_target_pairs={{0,4},{4,0},{8,12},{12,8},{16,20},{20,16},{24,28},{28,24},{1,5},{5... | collective-permute-start | bytes 7077896 | tf_op jit(solution)/shard_map/ppermute | solution.py:445
  852.7 27.0 %collective-permute-start.158 = (bf16[192,1536]{1,0:T(8,128)(2,1)}, bf16[192,1536]{1,0:T(8,128)(2,1)S(1)}, u32[]{:S(2)}, u32[]{:S(2)}) collective-permute-start(bf16[192,1536]{1,0:T(8,128)(2,1)} %get-tuple-element.151), channel_id=1, source_target_pairs={{0,8},{4,12},{8,0},{12,4},{16,24},{20,28},{24,16},{28,20},{1,9},{5... | collective-permute-start | bytes 1769480 | tf_op jit(solution)/shard_map/ppermute | solution.py:445
  901.4 22.6 %collective-permute-start.161 = (bf16[96,1536]{1,0:T(8,128)(2,1)S(1)}, bf16[96,1536]{1,0:T(8,128)(2,1)S(1)}, u32[]{:S(2)}, u32[]{:S(2)}) collective-permute-start(bf16[96,1536]{1,0:T(8,128)(2,1)S(1)} %slice.319), channel_id=1, source_target_pairs={{0,8},{4,12},{8,0},{12,4},{16,24},{20,28},{24,16},{28,20},{1,9},{5... | collective-permute-start | bytes 884744 | tf_op jit(solution)/shard_map/ppermute | solution.py:445
  920.2 36.0 %collective-permute-start.132 = (bf16[4,192,1536]{2,1,0:T(8,128)(2,1)}, bf16[4,192,1536]{2,1,0:T(8,128)(2,1)}, u32[]{:S(2)}, u32[]{:S(2)}) collective-permute-start(bf16[4,192,1536]{2,1,0:T(8,128)(2,1)} %get-tuple-element.98), channel_id=1, source_target_pairs={{0,4},{4,0},{8,12},{12,8},{16,20},{20,16},{24,28},{28,24},{1,5},{5... | collective-permute-start | bytes 7077896 | tf_op jit(solution)/shard_map/ppermute | solution.py:445
  921.1 55.7 %collective-permute-start.142 = (bf16[4,192,1536]{2,1,0:T(8,128)(2,1)}, bf16[4,192,1536]{2,1,0:T(8,128)(2,1)}, u32[]{:S(2)}, u32[]{:S(2)}) collective-permute-start(bf16[4,192,1536]{2,1,0:T(8,128)(2,1)} %get-tuple-element.102), channel_id=1, source_target_pairs={{0,4},{4,0},{8,12},{12,8},{16,20},{20,16},{24,28},{28,24},{1,5},{5... | collective-permute-start | bytes 7077896 | tf_op jit(solution)/shard_map/ppermute | solution.py:445
  940.9 45.6 %collective-permute-start.152 = (bf16[4,192,1536]{2,1,0:T(8,128)(2,1)}, bf16[4,192,1536]{2,1,0:T(8,128)(2,1)}, u32[]{:S(2)}, u32[]{:S(2)}) collective-permute-start(bf16[4,192,1536]{2,1,0:T(8,128)(2,1)} %get-tuple-element.106), channel_id=1, source_target_pairs={{0,4},{4,0},{8,12},{12,8},{16,20},{20,16},{24,28},{28,24},{1,5},{5... | collective-permute-start | bytes 7077896 | tf_op jit(solution)/shard_map/ppermute | solution.py:445
  941.0 59.1 %collective-permute-start.162 = (bf16[4,192,1536]{2,1,0:T(8,128)(2,1)}, bf16[4,192,1536]{2,1,0:T(8,128)(2,1)}, u32[]{:S(2)}, u32[]{:S(2)}) collective-permute-start(bf16[4,192,1536]{2,1,0:T(8,128)(2,1)} %get-tuple-element.110), channel_id=1, source_target_pairs={{0,4},{4,0},{8,12},{12,8},{16,20},{20,16},{24,28},{28,24},{1,5},{5... | collective-permute-start | bytes 7077896 | tf_op jit(solution)/shard_map/ppermute | solution.py:445
  942.5 53.6 %collective-permute-start.98 = (bf16[192,1536]{1,0:T(8,128)(2,1)S(1)}, bf16[192,1536]{1,0:T(8,128)(2,1)S(1)}, u32[]{:S(2)}, u32[]{:S(2)}) collective-permute-start(bf16[192,1536]{1,0:T(8,128)(2,1)S(1)} %fusion.129), channel_id=1, source_target_pairs={{1,2},{2,1},{5,6},{6,5},{9,10},{10,9},{13,14},{14,13},{17,18},{18,... | collective-permute-start | bytes 1769480 | tf_op jit(solution)/shard_map/ppermute | solution.py:453
  956.3 39.8 %collective-permute-start.96 = (bf16[192,1536]{1,0:T(8,128)(2,1)}, bf16[192,1536]{1,0:T(8,128)(2,1)}, u32[]{:S(2)}, u32[]{:S(2)}) collective-permute-start(bf16[192,1536]{1,0:T(8,128)(2,1)} %bitcast_add_fusion.17), channel_id=1, source_target_pairs={{0,1},{1,0},{2,3},{3,2},{4,5},{5,4},{6,7},{7,6},{8,9},{9,8},{10,11... | collective-permute-start | bytes 1769480 | tf_op jit(solution)/shard_map/ppermute | solution.py:449
  (299 other events, 3235.1 us)

commit v2 on v0

--- a/solution.py
+++ b/solution.py
@@ -1,8 +1,11 @@
+import functools
 import math
 
 import jax
 import jax.numpy as jnp
 from jax import lax
+from jax.experimental import pallas as pl
+from jax.experimental.pallas import tpu as pltpu
 from jax.sharding import PartitionSpec as P
 
 QUERY_HEADS = 12
@@ -439,6 +442,1137 @@
     )
 
 
+def flip(value, bit):
+    return lax.ppermute(value, "ctx", [(index, index ^ bit) for index in range(8)])
+
+
+def line_swap(value, offset):
+    return lax.ppermute(value, "wt", [(index, index ^ offset) for index in range(4)])
+
+
+def line_middle(value):
+    return lax.ppermute(value, "wt", [(1, 2), (2, 1)])
+
+
+def line_outward(value):
+    return lax.ppermute(value, "wt", [(1, 0), (2, 3)])
+
+
+def line_inward(value):
+    return lax.ppermute(value, "wt", [(0, 1), (3, 2)])
+
+
+def line_gather(value, at_end):
+    near = line_swap(value, 1)
+    middle = line_middle(value)
+    middle_far = line_middle(near)
+    outward = line_outward(middle)
+    outward_far = line_outward(middle_far)
+    return [
+        value,
+        near,
+        jnp.where(at_end, outward, middle_far),
+        jnp.where(at_end, outward_far, middle),
+    ]
+
+
+def line_reduce(parts):
+    far = line_inward(parts[3])
+    carried = parts[2] + far
+    inward = line_inward(carried)
+    crossed = line_middle(carried)
+    near = line_swap(parts[1] + crossed, 1)
+    middle = line_middle(parts[3] + inward)
+    return (
+        parts[0].astype(jnp.float32) + near.astype(jnp.float32) + middle.astype(jnp.float32)
+    )
+
+
+def chips_swap(values):
+    return [values[0]] + [flip(values[r], 2 * r) for r in (1, 2, 3)]
+
+
+def chips_gather(value, x_last):
+    along_x = flip(value, 2)
+    along_y = flip(value, 4)
+    corner = flip(along_y, 2) if x_last else flip(along_x, 4)
+    return [value, along_x, along_y, corner]
+
+
+def core_swap(values):
+    return [flip(value, 1) for value in values]
+
+
+def everywhere_sum(value):
+    for bit in (1, 2, 4):
+        value = value + flip(value, bit)
+    for offset in (1, 2):
+        value = value + line_swap(value, offset)
+    return value
+
+
+def pick(blocks, index):
+    return lax.dynamic_index_in_dim(blocks, index, 0, keepdims=False)
+
+
+def chips_reduce(keep, came):
+    half = keep.shape[1] // 2
+    upper = keep[:, :half] + came[:, :half]
+    lower = keep[:, half:] + came[:, half:]
+    upper_came = flip(upper[1::2], 2)
+    lower_came = flip(lower[2:], 4)
+    upper = upper[0::2] + upper_came
+    lower = lower[:2] + lower_came
+    upper_came = flip(upper[1], 4)
+    lower_came = flip(lower[1], 2)
+    return jnp.concatenate([upper[0] + upper_came, lower[0] + lower_came], axis=0)
+
+
+def dot_plain(left, right):
+    return lax.dot_general(
+        left, right, (((1,), (0,)), ((), ())), preferred_element_type=jnp.float32
+    )
+
+
+def dot_last(left, right):
+    return lax.dot_general(
+        left, right, (((1,), (1,)), ((), ())), preferred_element_type=jnp.float32
+    )
+
+
+def dot_first(left, right):
+    return lax.dot_general(
+        left, right, (((0,), (0,)), ((), ())), preferred_element_type=jnp.float32
+    )
+
+
+def call(kernel, name, meta, arrays, grid, in_specs, out_specs, out_shape, scratch, flops, moved):
+    return pl.pallas_call(
+        kernel,
+        grid_spec=pltpu.PrefetchScalarGridSpec(
+            num_scalar_prefetch=1,
+            grid=grid,
+            in_specs=in_specs,
+            out_specs=out_specs,
+            scratch_shapes=scratch,
+        ),
+        out_shape=out_shape,
+        compiler_params=pltpu.CompilerParams(vmem_limit_bytes=48 * 1024 * 1024),
+        cost_estimate=pl.CostEstimate(
+            flops=int(flops), bytes_accessed=int(moved), transcendentals=0
+        ),
+        name=name,
+    )(meta, *arrays)
+
+
+def whole(array):
+    rank = len(array.shape)
+    return pl.BlockSpec(tuple(array.shape), lambda *_: (0,) * rank)
+
+
+def shape_of(shape, dtype):
+    return jax.ShapeDtypeStruct(shape, dtype)
+
+
+def size_of(arrays):
+    return sum(math.prod(a.shape) * a.dtype.itemsize for a in arrays)
+
+
+def aligned(value, step):
+    return pl.multiple_of(value * step, step)
+
+
+def project_kernel(meta, *refs):
+    blocks, gain_ref = refs[:4], refs[4]
+    mine, other = refs[5:9], refs[9:13]
+    normed_ref, query_ref, pair_ref, weight_ref, held = refs[13:]
+    step = pl.program_id(0)
+    core, shard = meta[0] & 1, meta[1]
+    rows = mine[0].shape[0]
+
+    @pl.when(step == 0)
+    def _():
+        for i in range(4):
+            at = 2 * (shard ^ i)
+            weight_ref[pl.ds(aligned(at + core, rows), rows), :] = mine[i][...]
+            weight_ref[pl.ds(aligned(at + 1 - core, rows), rows), :] = other[i][...]
+
+    for r in range(4):
+
+        @pl.when(step == r)
+        def _():
+            held[...] = blocks[r][...]
+
+    states = held[...].astype(jnp.float32)
+    inverse = lax.rsqrt(jnp.mean(states * states, axis=-1, keepdims=True) + norm_eps)
+    normed = (states * inverse * gain_ref[...]).astype(jnp.bfloat16)
+    normed_ref[0] = normed
+    projected = dot_plain(normed, weight_ref[...]).astype(jnp.bfloat16)
+    query_width = query_ref.shape[-1]
+    query_ref[0] = projected[:, :query_width]
+    pair_ref[0] = projected[:, query_width:]
+
+
+def project(meta, blocks, gain, mine, other, query_width):
+    token_rows, width = blocks[0].shape
+    columns = mine[0].shape[1]
+    arrays = list(blocks) + [gain] + list(mine) + list(other)
+    outs = [
+        shape_of((4, token_rows, width), jnp.bfloat16),
+        shape_of((4, token_rows, query_width), jnp.bfloat16),
+        shape_of((4, token_rows, columns - query_width), jnp.bfloat16),
+        shape_of((width, columns), jnp.bfloat16),
+    ]
+    return call(
+        project_kernel,
+        "project",
+        meta,
+        arrays,
+        (4,),
+        [whole(a) for a in arrays],
+        [
+            pl.BlockSpec((1, token_rows, width), lambda r, m: (r, 0, 0)),
+            pl.BlockSpec((1, token_rows, query_width), lambda r, m: (r, 0, 0)),
+            pl.BlockSpec((1, token_rows, columns - query_width), lambda r, m: (r, 0, 0)),
+            whole(outs[3]),
+        ],
+        outs,
+        [pltpu.VMEM((token_rows, width), jnp.bfloat16)],
+        2 * 4 * token_rows * width * columns,
+        size_of(arrays) + size_of(outs),
+    )
+
+
+def sort_pairs(meta, mine_ref, other_ref, keys, values):
+    half = mine_ref.shape[1] // 2
+    for slot in range(16):
+        block, part = (slot, 0) if slot < 8 else (15 - slot, 1)
+        relative = meta[0] ^ block
+        place = relative >> 1
+        rows = pl.ds(part * half, half)
+        to = pl.ds(slot * half, half)
+
+        @pl.when((relative & 1) == 0)
+        def _():
+            keys[to, :] = mine_ref[place, rows, :HEAD_SIZE]
+            values[to, :] = mine_ref[place, rows, HEAD_SIZE:]
+
+        @pl.when((relative & 1) == 1)
+        def _():
+            keys[to, :] = other_ref[place, rows, :HEAD_SIZE]
+            values[to, :] = other_ref[place, rows, HEAD_SIZE:]
+
+
+def stack_heads(rows):
+    count = rows.shape[1] // HEAD_SIZE
+    return jnp.concatenate(
+        [rows[:, h * HEAD_SIZE : (h + 1) * HEAD_SIZE] for h in range(count)], axis=0
+    )
+
+
+def unstack_heads(rows, count):
+    each = rows.shape[0] // count
+    return jnp.concatenate([rows[h * each : (h + 1) * each] for h in range(count)], axis=1)
+
+
+def step_slot(meta):
+    step = pl.program_id(0)
+    block = meta[0] ^ (2 * (step >> 1))
+    return jnp.where((step & 1) == 0, block, 15 - block)
+
+
+def allowed_pairs(key_block, slot, shape, half):
+    key_place = key_block * shape[0] + lax.broadcasted_iota(jnp.int32, shape, 0)
+    query_place = slot * half + (lax.broadcasted_iota(jnp.int32, shape, 1) & (half - 1))
+    return key_place <= query_place
+
+
+def attend_kernel(scale, span, meta, query_ref, mine_ref, other_ref, *refs):
+    outs, log_ref = refs[:4], refs[4]
+    keys, values, values_turned = refs[5:]
+    step = pl.program_id(0)
+    half, group_width = query_ref.shape[1:]
+    count = group_width // HEAD_SIZE
+
+    @pl.when(step == 0)
+    def _():
+        sort_pairs(meta, mine_ref, other_ref, keys, values)
+        values_turned[...] = values[...].T
+
+    slot = step_slot(meta)
+    query = stack_heads(query_ref[0])
+    last = slot * half // span
+
+    def scores_of(key_block):
+        at = pl.ds(aligned(key_block, span), span)
+        return at, dot_last(keys[at, :], query) * scale
+
+    def add(carry, at, scores):
+        highest, total, mixed = carry
+        new = jnp.maximum(highest, jnp.max(scores, axis=0, keepdims=True))
+        rescale = jnp.exp(highest - new)
+        powers = jnp.exp(scores - new)
+        total = total * rescale + jnp.sum(powers, axis=0, keepdims=True)
+        mixed = mixed * rescale + dot_plain(values_turned[:, at], powers.astype(jnp.bfloat16))
+        return new, total, mixed
+
+    def body(key_block, carry):
+        at, scores = scores_of(key_block)
+        return add(carry, at, scores)
+
+    wide = count * half
+    carry = (
+        jnp.full((1, wide), masked_score, jnp.float32),
+        jnp.zeros((1, wide), jnp.float32),
+        jnp.zeros((HEAD_SIZE, wide), jnp.float32),
+    )
+    carry = lax.fori_loop(0, last, body, carry)
+    at, scores = scores_of(last)
+    scores = jnp.where(allowed_pairs(last, slot, scores.shape, half), scores, masked_score)
+    highest, total, mixed = add(carry, at, scores)
+    log_ref[0] = highest + jnp.log(total)
+    result = unstack_heads((mixed / total).T, count).astype(jnp.bfloat16)
+    for r in range(4):
+        for part in range(2):
+
+            @pl.when(step == 2 * r + part)
+            def _():
+                outs[r][part * half : (part + 1) * half, :] = result
+
+
+def attend(meta, query, mine, other, scale):
+    token_rows, group_width = query.shape[1:]
+    half = token_rows // 2
+    count = group_width // HEAD_SIZE
+    everything = 8 * token_rows
+    span = min(256, everything)
+    arrays = [query, mine, other]
+    outs = [shape_of((token_rows, group_width), jnp.bfloat16)] * 4
+    outs = outs + [shape_of((8, 1, count * half), jnp.float32)]
+    result = call(
+        functools.partial(attend_kernel, scale, span),
+        "attend",
+        meta,
+        arrays,
+        (8,),
+        [
+            pl.BlockSpec((1, half, group_width), lambda i, m: (i // 2, i % 2, 0)),
+            whole(mine),
+            whole(other),
+        ],
+        [whole(a) for a in outs[:4]]
+        + [pl.BlockSpec((1, 1, count * half), lambda i, m: (i, 0, 0))],
+        outs,
+        [
+            pltpu.VMEM((everything, HEAD_SIZE), jnp.bfloat16),
+            pltpu.VMEM((everything, HEAD_SIZE), jnp.bfloat16),
+            pltpu.VMEM((HEAD_SIZE, everything), jnp.bfloat16),
+        ],
+        2 * 2 * 4 * token_rows * everything * group_width,
+        size_of(arrays) + size_of(outs),
+    )
+    return result[:4], result[4]
+
+
+def attend_back_kernel(scale, span, meta, query_ref, mine_ref, other_ref, log_ref, *refs):
+    mixed_refs, grad_refs = refs[:4], refs[4:8]
+    grad_query_ref, grad_mine_ref, grad_other_ref = refs[8:11]
+    keys, values, keys_turned, grad_keys, grad_values, mixed_held, grad_held = refs[11:]
+    step = pl.program_id(0)
+    half, group_width = query_ref.shape[1:]
+    count = group_width // HEAD_SIZE
+
+    @pl.when(step == 0)
+    def _():
+        sort_pairs(meta, mine_ref, other_ref, keys, values)
+        keys_turned[...] = keys[...].T
+        grad_keys[...] = jnp.zeros_like(grad_keys)
+        grad_values[...] = jnp.zeros_like(grad_values)
+
+    for r in range(4):
+        for part in range(2):
+
+            @pl.when(step == 2 * r + part)
+            def _():
+                mixed_held[...] = mixed_refs[r][part * half : (part + 1) * half, :]
+                grad_held[...] = grad_refs[r][part * half : (part + 1) * half, :]
+
+    slot = step_slot(meta)
+    query = stack_heads(query_ref[0])
+    mixed = stack_heads(mixed_held[...]).astype(jnp.float32)
+    grad = stack_heads(grad_held[...])
+    delta = jnp.sum((mixed * grad.astype(jnp.float32)).T, axis=0, keepdims=True)
+    log_total = log_ref[0]
+    last = slot * half // span
+
+    def one(key_block, grad_turned, masked):
+        at = pl.ds(aligned(key_block, span), span)
+        scores = dot_last(keys[at, :], query) * scale
+        probs = jnp.exp(scores - log_total)
+        if masked:
+            probs = jnp.where(allowed_pairs(key_block, slot, probs.shape, half), probs, 0.0)
+        grad_probs = dot_last(values[at, :], grad)
+        grad_scores = (probs * (grad_probs - delta)).astype(jnp.bfloat16)
+        grad_values[at, :] += dot_plain(probs.astype(jnp.bfloat16), grad)
+        grad_keys[at, :] += dot_plain(grad_scores, query)
+        return grad_turned + dot_plain(keys_turned[:, at], grad_scores)
+
+    grad_turned = jnp.zeros((HEAD_SIZE, count * half), jnp.float32)
+    grad_turned = lax.fori_loop(0, last, lambda b, total: one(b, total, False), grad_turned)
+    grad_turned = one(last, grad_turned, True)
+    grad_query_ref[0] = unstack_heads((grad_turned * scale).T, count).astype(jnp.bfloat16)
+
+    @pl.when(step == 7)
+    def _():
+        for slot_at in range(16):
+            block, part = (slot_at, 0) if slot_at < 8 else (15 - slot_at, 1)
+            relative = meta[0] ^ block
+            place = relative >> 1
+            rows = pl.ds(part * half, half)
+            here = pl.ds(slot_at * half, half)
+            both = jnp.concatenate([grad_keys[here, :] * scale, grad_values[here, :]], axis=1)
+
+            @pl.when((relative & 1) == 0)
+            def _():
+                grad_mine_ref[place, rows, :] = both
+
+            @pl.when((relative & 1) == 1)
+            def _():
+                grad_other_ref[place, rows, :] = both.astype(jnp.bfloat16)
+
+
+def attend_back(meta, query, mine, other, log_total, mixed, grad, scale):
+    token_rows, group_width = query.shape[1:]
+    half = token_rows // 2
+    count = group_width // HEAD_SIZE
+    everything = 8 * token_rows
+    span = min(256, everything)
+    arrays = [query, mine, other, log_total] + list(mixed) + list(grad)
+    outs = [
+        shape_of(query.shape, jnp.bfloat16),
+        shape_of(mine.shape, jnp.float32),
+        shape_of(mine.shape, jnp.bfloat16),
+    ]
+    return call(
+        functools.partial(attend_back_kernel, scale, span),
+        "attend_back",
+        meta,
+        arrays,
+        (8,),
+        [
+            pl.BlockSpec((1, half, group_width), lambda i, m: (i // 2, i % 2, 0)),
+            whole(mine),
+            whole(other),
+            pl.BlockSpec((1, 1, count * half), lambda i, m: (i, 0, 0)),
+        ]
+        + [whole(a) for a in arrays[4:]],
+        [
+            pl.BlockSpec((1, half, group_width), lambda i, m: (i // 2, i % 2, 0)),
+            whole(outs[1]),
+            whole(outs[2]),
+        ],
+        outs,
+        [
+            pltpu.VMEM((everything, HEAD_SIZE), jnp.bfloat16),
+            pltpu.VMEM((everything, HEAD_SIZE), jnp.bfloat16),
+            pltpu.VMEM((HEAD_SIZE, everything), jnp.bfloat16),
+            pltpu.VMEM((everything, HEAD_SIZE), jnp.float32),
+            pltpu.VMEM((everything, HEAD_SIZE), jnp.float32),
+            pltpu.VMEM((half, group_width), jnp.bfloat16),
+            pltpu.VMEM((half, group_width), jnp.bfloat16),
+        ],
+        5 * 2 * 4 * token_rows * everything * group_width,
+        size_of(arrays) + size_of(outs),
+    )
+
+
+def leave_kernel(meta, *refs):
+    parts, mine, other = refs[:4], refs[4:8], refs[8:12]
+    states_ref, gain_ref, weight_ref, middle_ref, normed_ref = refs[12:]
+    core, chip, shard = meta[0] & 1, meta[0] >> 1, meta[1]
+    rows = mine[0].shape[0]
+    for i in range(4):
+        at = 2 * (chip ^ shard ^ i)
+        weight_ref[pl.ds(aligned(at + core, rows), rows), :] = mine[i][...]
+        weight_ref[pl.ds(aligned(at + 1 - core, rows), rows), :] = other[i][...]
+    middle = states_ref[...].astype(jnp.float32)
+    for r in range(4):
+        middle += dot_plain(parts[r][...], weight_ref[2 * rows * r : 2 * rows * (r + 1), :])
+    middle_ref[...] = middle
+    inverse = lax.rsqrt(jnp.mean(middle * middle, axis=-1, keepdims=True) + norm_eps)
+    normed_ref[...] = (middle * inverse * gain_ref[...]).astype(jnp.bfloat16)
+
+
+def leave(meta, parts, mine, other, states, gain):
+    token_rows, width = states.shape
+    arrays = list(parts) + list(mine) + list(other) + [states, gain]
+    outs = [
+        shape_of((8 * mine[0].shape[0], width), jnp.bfloat16),
+        shape_of((token_rows, width), jnp.float32),
+        shape_of((token_rows, width), jnp.bfloat16),
+    ]
+    return call(
+        leave_kernel,
+        "leave",
+        meta,
+        arrays,
+        (1,),
+        [whole(a) for a in arrays],
+        [whole(a) for a in outs],
+        outs,
+        [],
+        2 * token_rows * width * width,
+        size_of(arrays) + size_of(outs),
+    )
+
+
+def norm_back_rows(grad_normed, states, gain):
+    inverse = lax.rsqrt(jnp.mean(states * states, axis=-1, keepdims=True) + norm_eps)
+    scaled = states * inverse
+    gain_grad = jnp.sum(grad_normed * scaled, axis=0, keepdims=True)
+    grad_scaled = grad_normed * gain
+    shift = jnp.mean(grad_scaled * scaled, axis=-1, keepdims=True)
+    return inverse * (grad_scaled - scaled * shift), gain_grad
+
+
+def enter_back_kernel(meta, final_ref, normed_ref, middle_ref, gain_ref, weight_ref, *refs):
+    grad_ref, branch_ref, gain_grad_ref = refs[:3]
+    grad, gain_grad = norm_back_rows(normed_ref[...], middle_ref[...], gain_ref[...])
+    grad = grad + final_ref[...]
+    grad_ref[...] = grad
+    gain_grad_ref[...] = gain_grad
+    branch = grad.astype(jnp.bfloat16)
+    branch_ref[...] = branch
+    rows = weight_ref.shape[0] // 4
+    for r in range(4):
+        refs[3 + r][...] = dot_last(branch, weight_ref[rows * r : rows * (r + 1), :]).astype(
+            jnp.bfloat16
+        )
+
+
+def enter_back(meta, grad_final, grad_normed, middle, gain, weight):
+    token_rows, width = middle.shape
+    arrays = [grad_final, grad_normed, middle, gain, weight]
+    outs = [
+        shape_of((token_rows, width), jnp.float32),
+        shape_of((token_rows, width), jnp.bfloat16),
+        shape_of((1, width), jnp.float32),
+    ] + [shape_of((token_rows, weight.shape[0] // 4), jnp.bfloat16)] * 4
+    return call(
+        enter_back_kernel,
+        "enter_back",
+        meta,
+        arrays,
+        (1,),
+        [whole(a) for a in arrays],
+        [whole(a) for a in outs],
+        outs,
+        [],
+        2 * token_rows * width * width,
+        size_of(arrays) + size_of(outs),
+    )
+
+
+def finish_kernel(meta, *refs):
+    parts, mine, other = refs[:4], refs[4:8], refs[8:12]
+    states_ref, middle_ref, gain_ref, grad_ref, gain_grad_ref, total = refs[12:]
+    core = meta[0] & 1
+    columns = mine[0].shape[0]
+    for at, weights in ((core, mine), (1 - core, other)):
+        total[:, pl.ds(aligned(at, columns), columns)] = sum(
+            dot_last(parts[r][...], weights[r][...]) for r in range(4)
+        )
+    grad, gain_grad = norm_back_rows(
+        total[...], states_ref[...].astype(jnp.float32), gain_ref[...]
+    )
+    grad_ref[0] = grad + middle_ref[...]
+    gain_grad_ref[...] = gain_grad
+
+
+def finish(meta, parts, mine, other, states, grad_middle, gain):
+    token_rows, width = states.shape
+    arrays = list(parts) + list(mine) + list(other) + [states, grad_middle, gain]
+    outs = [
+        shape_of((1, token_rows, width), jnp.float32),
+        shape_of((1, width), jnp.float32),
+    ]
+    return call(
+        finish_kernel,
+        "finish",
+        meta,
+        arrays,
+        (1,),
+        [whole(a) for a in arrays],
+        [whole(a) for a in outs],
+        outs,
+        [pltpu.VMEM((token_rows, width), jnp.float32)],
+        2 * token_rows * width * 4 * parts[0].shape[1],
+        size_of(arrays) + size_of(outs),
+    )
+
+
+def gated(gate_up, units):
+    gate_part = gate_up[:, :units]
+    sigma = 1.0 / (1.0 + jnp.exp(-gate_part))
+    return gate_part * sigma * gate_up[:, units:]
+
+
+def gated_back(grad_act, gate_up, units):
+    gate_part = gate_up[:, :units].astype(jnp.float32)
+    up_part = gate_up[:, units:].astype(jnp.float32)
+    sigma = 1.0 / (1.0 + jnp.exp(-gate_part))
+    linear = gate_part * sigma
+    grad_gate = grad_act * up_part * (sigma * (1.0 + gate_part * (1.0 - sigma)))
+    return grad_gate, grad_act * linear, linear * up_part
+
+
+def experts_kernel(
+    meta, rows_ref, gates_ref, expert_ref, shared_ref, gate_up_ref, shared_gate_up_ref, out_ref, total
+):
+    expert = pl.program_id(0)
+    rows = rows_ref[...]
+
+    @pl.when(expert == 0)
+    def _():
+        units = shared_ref.shape[1] // 3
+        gate_up = dot_plain(rows, shared_ref[:, : 2 * units])
+        shared_gate_up_ref[...] = gate_up.astype(jnp.bfloat16)
+        act = gated(gate_up, units).astype(jnp.bfloat16)
+        total[...] = dot_last(act, shared_ref[:, 2 * units :])
+
+    gate_up = dot_plain(rows, expert_ref[0, :, : 2 * F])
+    gate_up_ref[0] = gate_up.astype(jnp.bfloat16)
+    act = (gated(gate_up, F) * gates_ref[0]).astype(jnp.bfloat16)
+    total[...] += dot_last(act, expert_ref[0, :, 2 * F :])
+
+    @pl.when(expert == pl.num_programs(0) - 1)
+    def _():
+        out_ref[...] = total[...].astype(jnp.bfloat16)
+
+
+def experts(meta, rows, gates, expert_weight, shared_slice):
+    local_experts, width, _ = expert_weight.shape
+    token_rows = rows.shape[0]
+    shared_units = shared_slice.shape[1] // 3
+    arrays = [rows, gates, expert_weight, shared_slice]
+    outs = [
+        shape_of((local_experts, token_rows, 2 * F), jnp.bfloat16),
+        shape_of((token_rows, 2 * shared_units), jnp.bfloat16),
+        shape_of((token_rows, width), jnp.bfloat16),
+    ]
+    return call(
+        experts_kernel,
+        "experts",
+        meta,
+        arrays,
+        (local_experts,),
+        [
+            whole(rows),
+            pl.BlockSpec((1, token_rows, 1), lambda e, m: (e, 0, 0)),
+            pl.BlockSpec((1, width, 3 * F), lambda e, m: (e, 0, 0)),
+            whole(shared_slice),
+        ],
+        [
+            pl.BlockSpec((1, token_rows, 2 * F), lambda e, m: (e, 0, 0)),
+            whole(outs[1]),
+            whole(outs[2]),
+        ],
+        outs,
+        [pltpu.VMEM((token_rows, width), jnp.float32)],
+        2 * token_rows * width * 3 * (F * local_experts + shared_units),
+        size_of(arrays) + size_of(outs),
+    )
+
+
+def experts_back_kernel(
+    meta,
+    grad_ref,
+    gates_ref,
+    gate_up_ref,
+    shared_gate_up_ref,
+    expert_ref,
+    shared_ref,
+    grad_gate_up_ref,
+    act_ref,
+    shared_grad_ref,
+    shared_act_ref,
+    grad_rows_ref,
+    total,
+):
+    expert = pl.program_id(0)
+    grad = grad_ref[...]
+
+    @pl.when(expert == 0)
+    def _():
+        units = shared_ref.shape[1] // 3
+        grad_act = dot_plain(grad, shared_ref[:, 2 * units :])
+        grad_gate, grad_up, act = gated_back(grad_act, shared_gate_up_ref[...], units)
+        both = jnp.concatenate([grad_gate, grad_up], axis=1).astype(jnp.bfloat16)
+        shared_grad_ref[0] = both
+        shared_act_ref[0] = act.astype(jnp.bfloat16)
+        total[...] = dot_last(both, shared_ref[:, : 2 * units])
+
+    grad_act = dot_plain(grad, expert_ref[0, :, 2 * F :]) * gates_ref[0]
+    grad_gate, grad_up, act = gated_back(grad_act, gate_up_ref[0], F)
+    both = jnp.concatenate([grad_gate, grad_up], axis=1).astype(jnp.bfloat16)
+    grad_gate_up_ref[0] = both
+    act_ref[0] = (act * gates_ref[0]).astype(jnp.bfloat16)
+    total[...] += dot_last(both, expert_ref[0, :, : 2 * F])
+
+    @pl.when(expert == pl.num_programs(0) - 1)
+    def _():
+        grad_rows_ref[...] = total[...].astype(jnp.bfloat16)
+
+
+def experts_back(meta, grad, gates, gate_up, shared_gate_up, expert_weight, shared_slice):
+    local_experts, width, _ = expert_weight.shape
+    token_rows = grad.shape[0]
+    shared_units = shared_slice.shape[1] // 3
+    arrays = [grad, gates, gate_up, shared_gate_up, expert_weight, shared_slice]
+    outs = [
+        shape_of((local_experts, token_rows, 2 * F), jnp.bfloat16),
+        shape_of((local_experts, token_rows, F), jnp.bfloat16),
+        shape_of((1, token_rows, 2 * shared_units), jnp.bfloat16),
+        shape_of((1, token_rows, shared_units), jnp.bfloat16),
+        shape_of((token_rows, width), jnp.bfloat16),
+    ]
+    return call(
+        experts_back_kernel,
+        "experts_back",
+        meta,
+        arrays,
+        (local_experts,),
+        [
+            whole(grad),
+            pl.BlockSpec((1, token_rows, 1), lambda e, m: (e, 0, 0)),
+            pl.BlockSpec((1, token_rows, 2 * F), lambda e, m: (e, 0, 0)),
+            whole(shared_gate_up),
+            pl.BlockSpec((1, width, 3 * F), lambda e, m: (e, 0, 0)),
+            whole(shared_slice),
+        ],
+        [
+            pl.BlockSpec((1, token_rows, 2 * F), lambda e, m: (e, 0, 0)),
+            pl.BlockSpec((1, token_rows, F), lambda e, m: (e, 0, 0)),
+            whole(outs[2]),
+            whole(outs[3]),
+            whole(outs[4]),
+        ],
+        outs,
+        [pltpu.VMEM((token_rows, width), jnp.float32)],
+        2 * token_rows * width * 3 * (F * local_experts + shared_units),
+        size_of(arrays) + size_of(outs),
+    )
+
+
+def weight_grad_kernel(pairs, core_at, meta, *refs):
+    keep_ref, give_ref = refs[-2:]
+    at = 0
+    columns = 0
+    parts = []
+    for count in pairs:
+        lefts, rights = refs[at : at + count], refs[at + count : at + 2 * count]
+        at += 2 * count
+        parts.append(
+            sum(dot_first(a[...], b[0]) for a, b in zip(lefts, rights)).astype(jnp.bfloat16)
+        )
+    half = keep_ref.shape[1]
+
+    for core, (first, second) in ((0, (keep_ref, give_ref)), (1, (give_ref, keep_ref))):
+
+        @pl.when((meta[core_at] & 1) == core)
+        def _():
+            start = 0
+            for part in parts:
+                stop = start + part.shape[1]
+                first[0, :, start:stop] = part[:half]
+                second[0, :, start:stop] = part[half:]
+                start = stop
+
+
+def weight_grad(meta, order, operands, index):
+    token_rows, width = operands[0][0][0].shape
+    tile = width // 4
+    scalars = jnp.stack([order, meta[0]])
+    arrays, in_specs, columns = [], [], 0
+    for lefts, rights in operands:
+        arrays += list(lefts) + list(rights)
+        in_specs += [pl.BlockSpec((token_rows, tile), lambda i, m: (0, i ^ m[0]))] * len(lefts)
+        units = rights[0].shape[-1]
+        in_specs += [
+            pl.BlockSpec((1, token_rows, units), lambda i, m, at=index: (at, 0, 0))
+        ] * len(rights)
+        columns += units
+    outs = [shape_of((4, tile // 2, columns), jnp.bfloat16)] * 2
+    tokens = token_rows * len(operands[0][0])
+    return call(
+        functools.partial(weight_grad_kernel, [len(left) for left, _ in operands], 1),
+        "weight_grad",
+        scalars,
+        arrays,
+        (4,),
+        in_specs,
+        [pl.BlockSpec((1, tile // 2, columns), lambda i, m: (i, 0, 0))] * 2,
+        outs,
+        [],
+        2 * tokens * width * columns,
+        size_of(outs) + 4 * tokens * width + 2 * tokens * columns,
+    )
+
+
+def place_expert_kernel(meta, *refs):
+    mine, other, out_ref = refs[-9:-5], refs[-5:-1], refs[-1]
+    step = pl.program_id(0)
+    core = meta[0] & 1
+    rows = mine[0].shape[0]
+    for r in range(4):
+
+        @pl.when(step == r)
+        def _():
+            out_ref[0, pl.ds(aligned(core, rows), rows), :] = mine[r][...].astype(jnp.float32)
+            out_ref[0, pl.ds(aligned(1 - core, rows), rows), :] = other[r][...].astype(
+                jnp.float32
+            )
+
+
+def place_expert(meta, total, index, shape, mine, other):
+    rows, columns = mine[0].shape
+    arrays = list(mine) + list(other)
+    in_specs = [whole(a) for a in arrays]
+    aliases = {}
+    if total is not None:
+        arrays = [total] + arrays
+        in_specs = [pl.BlockSpec(memory_space=pl.ANY)] + in_specs
+        aliases = {1: 0}
+    return pl.pallas_call(
+        place_expert_kernel,
+        grid_spec=pltpu.PrefetchScalarGridSpec(
+            num_scalar_prefetch=1,
+            grid=(4,),
+            in_specs=in_specs,
+            out_specs=pl.BlockSpec(
+                (1, 2 * rows, columns), lambda r, m: (index, (m[0] >> 1) ^ r, 0)
+            ),
+        ),
+        out_shape=shape_of(shape, jnp.float32),
+        input_output_aliases=aliases,
+        compiler_params=pltpu.CompilerParams(vmem_limit_bytes=48 * 1024 * 1024),
+        cost_estimate=pl.CostEstimate(
+            flops=0, bytes_accessed=8 * rows * columns * 6, transcendentals=0
+        ),
+        name="place_expert",
+    )(meta, *arrays)
+
+
+def place_shared_kernel(meta, mine, other, out_ref):
+    core = meta[0] & 1
+    rows = mine.shape[1]
+    out_ref[pl.ds(aligned(core, rows), rows), :] = mine[0].astype(jnp.float32)
+    out_ref[pl.ds(aligned(1 - core, rows), rows), :] = other[0].astype(jnp.float32)
+
+
+def place_shared(meta, mine, other):
+    _, rows, columns = mine.shape
+    units = columns // 3
+    block = pl.BlockSpec((1, rows, units), lambda i, j, m: (i, 0, j))
+    outs = shape_of((2 * rows, 4 * columns), jnp.float32)
+    return call(
+        place_shared_kernel,
+        "place_shared",
+        meta,
+        [mine, other],
+        (4, 3),
+        [block, block],
+        pl.BlockSpec((2 * rows, units), lambda i, j, m: (0, 4 * j + (m[1] ^ i))),
+        outs,
+        [],
+        0,
+        size_of([mine, other, outs]),
+    )
+
+
+def place_heads_kernel(meta, *refs):
+    mine, other, out_ref = refs[:4], refs[4:8], refs[8]
+    core, chip = meta[0] & 1, meta[0] >> 1
+    rows, columns = mine[0].shape
+    group_width = columns - 2 * HEAD_SIZE
+    for r in range(4):
+        head = chip ^ r
+        for at, pieces in ((core, mine), (1 - core, other)):
+            to = pl.ds(aligned(at, rows), rows)
+            values = pieces[r][...].astype(jnp.float32)
+            out_ref[to, pl.ds(aligned(head, group_width), group_width)] = values[:, :group_width]
+            out_ref[to, pl.ds(aligned(4 * group_width // HEAD_SIZE + head, HEAD_SIZE), HEAD_SIZE)] = (
+                values[:, group_width : group_width + HEAD_SIZE]
+            )
+            out_ref[
+                to, pl.ds(aligned(4 * group_width // HEAD_SIZE + 4 + head, HEAD_SIZE), HEAD_SIZE)
+            ] = values[:, group_width + HEAD_SIZE :]
+
+
+def place_heads(meta, mine, other):
+    rows, columns = mine[0].shape
+    arrays = list(mine) + list(other)
+    outs = shape_of((2 * rows, 4 * columns), jnp.float32)
+    return call(
+        place_heads_kernel,
+        "place_heads",
+        meta,
+        arrays,
+        (1,),
+        [whole(a) for a in arrays],
+        whole(outs),
+        outs,
+        [],
+        0,
+        size_of(arrays + [outs]),
+    )
+
+
+def join_shared_kernel(meta, mine, other, out_ref):
+    step = pl.program_id(0)
+    rows = mine.shape[2]
+    first = meta[0] ^ (2 * step)
+    for i in range(4):
+        at = 8 * (meta[1] ^ i)
+        out_ref[pl.ds(aligned(at + first, rows), rows), :] = mine[0, i]
+        out_ref[pl.ds(aligned(at + (first ^ 1), rows), rows), :] = other[0, i]
+
+
+def join_shared(meta, mine, other):
+    _, _, rows, columns = mine.shape
+    block = pl.BlockSpec((1, 4, rows, columns), lambda r, m: (r, 0, 0, 0))
+    outs = shape_of((32 * rows, columns), jnp.bfloat16)
+    return call(
+        join_shared_kernel,
+        "join_shared",
+        meta,
+        [mine, other],
+        (4,),
+        [block, block],
+        whole(outs),
+        outs,
+        [],
+        0,
+        size_of([mine, other, outs]),
+    )
+
+
+def fast_device(
+    hidden,
+    teacher,
+    valid_mask,
+    routes,
+    route_gates,
+    gain_in,
+    query_key_value_weight,
+    out_weight,
+    gain_mid,
+    shared_weight,
+    expert_weight,
+):
+    token_rows, width = hidden.shape[1:]
+    context_count, shard_count = 8, 4
+    context_index = lax.axis_index("ctx").astype(jnp.int32)
+    shard_index = lax.axis_index("wt").astype(jnp.int32)
+    meta = jnp.stack([context_index, shard_index])
+    core = context_index & 1
+    chip = context_index >> 1
+    at_end = (shard_index == 0) | (shard_index == shard_count - 1)
+    group_width = QUERY_HEADS // KEY_VALUE_HEADS * HEAD_SIZE
+    query_width = QUERY_HEADS * HEAD_SIZE
+    kv_width = KEY_VALUE_HEADS * HEAD_SIZE
+    slice_width = group_width + 2 * HEAD_SIZE
+    scale = 1.0 / math.sqrt(HEAD_SIZE)
+    all_tokens = token_rows * context_count * shard_count
+    shard_rows = query_key_value_weight.shape[0]
+    half_rows = shard_rows // 2
+    local_experts = expert_weight.shape[0]
+    bf16, f32 = jnp.bfloat16, jnp.float32
+    states = hidden[0]
+
+    blocks = chips_swap([states] * 4)
+
+    qkv_half = lax.dynamic_slice_in_dim(query_key_value_weight, core * half_rows, half_rows, 0)
+    qkv_half = jnp.concatenate(
+        [
+            lax.dynamic_slice_in_dim(qkv_half, chip * group_width, group_width, 1),
+            lax.dynamic_slice_in_dim(qkv_half, query_width + chip * HEAD_SIZE, HEAD_SIZE, 1),
+            lax.dynamic_slice_in_dim(
+                qkv_half, query_width + kv_width + chip * HEAD_SIZE, HEAD_SIZE, 1
+            ),
+        ],
+        axis=1,
+    )
+    qkv_mine = [qkv_half] + [line_swap(qkv_half, i) for i in (1, 2, 3)]
+    qkv_other = core_swap(qkv_mine)
+
+    gains = jnp.stack([gain_in, gain_mid])
+    gains = jnp.stack([gains] + [line_swap(gains, i) for i in (1, 2, 3)])
+    gains = jnp.stack([pick(gains, shard_index ^ i) for i in range(4)], axis=1)
+    gains = gains.reshape(2, 1, width).astype(f32)
+
+    normed_in, query, pair, qkv_slice = project(
+        meta, blocks, gains[0], qkv_mine, qkv_other, group_width
+    )
+    pair_other = flip(pair, 1)
+
+    out_half = lax.dynamic_slice_in_dim(out_weight, core * half_rows, half_rows, 0)
+    out_mine = line_gather(out_half, at_end)
+    out_other = core_swap(out_mine)
+
+    eighth = shard_rows // 8
+    shared_units = SF // shard_count
+    shared_piece = lax.dynamic_slice_in_dim(shared_weight, context_index * eighth, eighth, 0)
+    shared_piece = shared_piece.reshape(eighth, 3, shard_count, shared_units)
+
+    def shared_columns(index):
+        part = lax.dynamic_index_in_dim(shared_piece, shard_index ^ index, 2, keepdims=False)
+        return part.reshape(eighth, 3 * shared_units)
+
+    shared_pieces = jnp.stack(
+        [shared_columns(0)] + [line_swap(shared_columns(i), i) for i in (1, 2, 3)]
+    )
+    shared_mine = jnp.stack(chips_gather(shared_pieces, False))
+    shared_slice = join_shared(meta, shared_mine, flip(shared_mine, 1))
+
+    expert_ids = jnp.arange(EXPERTS, dtype=jnp.int32)
+    gate_matrix = jnp.sum(
+        jnp.where(
+            routes[0][None, :, :] == expert_ids[:, None, None], route_gates[0][None, :, :], 0.0
+        ),
+        axis=-1,
+    ).reshape(shard_count, local_experts, token_rows)
+    gates = [pick(gate_matrix, shard_index)] + [
+        line_swap(pick(gate_matrix, shard_index ^ i), i) for i in (1, 2, 3)
+    ]
+    gates = [part[..., None] for part in gates]
+
+    valid_float = valid_mask[0].astype(f32)
+    valid_count = everywhere_sum(jnp.full((8, 128), jnp.sum(valid_float), f32))[0, 0]
+
+    mixed_heads, log_total = attend(meta, query, pair, pair_other, scale)
+    mixed = chips_swap(mixed_heads)
+    out_rel, middle, normed_mid = leave(meta, mixed, out_mine, out_other, states, gains[1])
+
+    line_rows = line_gather(normed_mid, at_end)
+    forward = [
+        experts(meta, line_rows[i], gates[i], expert_weight, shared_slice) for i in range(4)
+    ]
+    gate_ups, shared_gate_ups, partial_out = zip(*forward)
+    final_state = middle + line_reduce(partial_out)
+
+    deviation = final_state - teacher[0].astype(f32)
+    squared = jnp.sum(valid_float[:, None] * deviation * deviation)
+    grad_final = all_tokens / valid_count * valid_float[:, None] * deviation
+
+    line_grads = line_gather(grad_final.astype(bf16), at_end)
+    backward = [
+        experts_back(
+            meta,
+            line_grads[i],
+            gates[i],
+            gate_ups[i],
+            shared_gate_ups[i],
+            expert_weight,
+            shared_slice,
+        )
+        for i in range(4)
+    ]
+    grad_gate_ups, acts, shared_grads, shared_acts, partial_rows = zip(*backward)
+    grad_normed_mid = line_reduce(partial_rows)
+
+    grad_middle, grad_branch, grad_gain_mid, *grad_mixed = enter_back(
+        meta, grad_final, grad_normed_mid, middle, gains[1], out_rel
+    )
+    grad_mixed = chips_swap(grad_mixed)
+
+    grad_query, grad_pair, grad_pair_other = attend_back(
+        meta, query, pair, pair_other, log_total, mixed_heads, grad_mixed, scale
+    )
+    grad_pair = grad_pair + flip(grad_pair_other, 1).astype(f32)
+    grad_projected = jnp.concatenate([grad_query, grad_pair.astype(bf16)], axis=-1)
+
+    keep, give = weight_grad(
+        meta,
+        shard_index,
+        [([normed_in.reshape(4 * token_rows, width)], [grad_projected.reshape(1, 4 * token_rows, -1)])],
+        0,
+    )
+    came = flip(give, 1)
+    grad_qkv = line_reduce([keep[i] + came[i] for i in range(4)]).astype(bf16)
+    grad_qkv = chips_gather(grad_qkv, False)
+    grad_qkv = place_heads(meta, grad_qkv, core_swap(grad_qkv))
+
+    qkv_rel = chips_gather(
+        lax.dynamic_slice_in_dim(qkv_slice, core * (width // 2), width // 2, 0), True
+    )
+    grad_parts = chips_swap([grad_projected[r] for r in range(4)])
+    grad_hidden, grad_gain_in = finish(
+        meta, grad_parts, qkv_rel, core_swap(qkv_rel), states, grad_middle, gains[0]
+    )
+
+    grad_experts = None
+    for expert in range(local_experts):
+        keep, give = weight_grad(
+            meta, chip, [(line_rows, grad_gate_ups), (line_grads, acts)], expert
+        )
+        reduced = chips_reduce(keep, flip(give, 1))
+        reduced = chips_gather(reduced, expert % 2 == 1)
+        grad_experts = place_expert(
+            meta, grad_experts, expert, expert_weight.shape, reduced, core_swap(reduced)
+        )
+
+    keep, give = weight_grad(
+        meta, shard_index, [(line_rows, shared_grads), (line_grads, shared_acts)], 0
+    )
+    came = flip(give, 1)
+    grad_shared = [keep[0] + came[0]] + [line_swap(keep[i] + came[i], i) for i in (1, 2, 3)]
+    grad_shared = jnp.stack(grad_shared)
+
+    def chips_sum(value, axis):
+        upper, lower = jnp.split(value, 2, axis=axis)
+        upper = upper + flip(upper, 2)
+        lower = lower + flip(lower, 4)
+        upper = upper + flip(upper, 4)
+        lower = lower + flip(lower, 2)
+        return jnp.concatenate([upper, lower], axis=axis)
+
+    grad_shared = chips_sum(grad_shared, 0)
+    grad_shared = place_shared(meta, grad_shared, flip(grad_shared, 1))
+
+    keep, give = weight_grad(
+        meta, chip ^ shard_index, [([jnp.concatenate(mixed, axis=1)], [grad_branch[None]])], 0
+    )
+    came = flip(give, 1)
+    grad_out = line_reduce([keep[i] + came[i] for i in range(4)]).astype(bf16)
+    grad_out = chips_sum(grad_out, 0)
+    came = flip(grad_out, 1)
+    grad_out = jnp.where(
+        core == 0,
+        jnp.concatenate([grad_out, came], axis=0),
+        jnp.concatenate([came, grad_out], axis=0),
+    ).astype(f32)
+
+    sums = jnp.concatenate(
+        [grad_gain_in, grad_gain_mid, jnp.full((6, width), squared, f32)], axis=0
+    )
+    sums = everywhere_sum(sums)
+    own = lax.dynamic_slice_in_dim(sums, shard_index * shard_rows, shard_rows, 1)
+    loss_value = 0.5 * sums[2, 0] / (valid_count * width)
+
+    return (
+        final_state.astype(bf16)[None],
+        loss_value,
+        grad_hidden,
+        own[0],
+        grad_qkv,
+        grad_out,
+        own[1],
+        grad_shared,
+        grad_experts,
+    )
+
+
 def solution(mesh):
     in_specs = (
         P("wt", "ctx", None),
@@ -464,6 +1598,7 @@
         P("wt", None),
         P("wt", None, None),
     )
+    plane_of_eight = dict(mesh.shape) == {"ctx": 8, "wt": 4}
     return jax.shard_map(
-        on_device, mesh=mesh, in_specs=in_specs, out_specs=out_specs, check_vma=False
-    )
+        fast_device if plane_of_eight else on_device, mesh=mesh, in_specs=in_specs, out_specs=out_specs, check_vma=False
+    )

time: 2100 us -> 931 us (0.44)
  waiting for transfers between devices: 1320 us -> 350 us
  Pallas kernels: 0 us -> 259 us
  blocking collectives: 230 us -> 0 us
  matrix products: 225 us -> 0 us
  starting transfers between devices: 17.1 us -> 189 us
  other arithmetic: 149 us -> 48.4 us
  local copies, waits for them, and re-layouts: 137 us -> 66.5 us
    all_to_all x3 -> x0, waiting for transfers between devices: 534 us -> none  [the longest x1 281 us: on_device(): lax.all_to_all(expert_rows, 'wt', split_axis=0, concat_axis=0, tiled=True)]
    reduce_scatter x4 -> x0, waiting for transfers between devices: 374 us -> none  [the longest x1 139 us: on_device(): lax.psum_scatter(grad_qkv_local.astype(jnp.bfloat16), 'wt', scatter_dimen...]
    ppermute x0 -> x161, waiting for transfers between devices: none -> 350 us  [the longest x107 213 us: flip(): lax.ppermute(value, 'ctx', [(index, index ^ bit) for index in range(8)])]
    psum x1 -> x0, waiting for transfers between devices: 268 us -> none  [on_device(): lax.psum(expert_grad.astype(jnp.bfloat16), 'ctx').astype(jnp.float32)]
    pallas_call x0 -> x28, Pallas kernels: none -> 259 us  [the longest x24 241 us: call(): pl.pallas_call(kernel, grid_spec=pltpu.PrefetchScalarGridSpec(num_scalar_...]
    dot_general x46 -> x0, matrix products: 225 us -> none  [the longest x4 24.9 us: online_step(): jnp.einsum('qhgk,khd->qhgd', powers.astype(jnp.bfloat16), value_block, pr...]
    ppermute x0 -> x161, starting transfers between devices: none -> 189 us  [the longest x107 75 us: flip(): lax.ppermute(value, 'ctx', [(index, index ^ bit) for index in range(8)])]
    all_to_all x1 -> x0, blocking collectives: 142 us -> none  [on_device(): lax.all_to_all(grad_expert_out, 'wt', split_axis=0, concat_axis=0, tiled=...]
  transfers between devices with their start and end apart: 12 -> 161, of which waited for: 11 -> 60; matrix products, arithmetic and copies ran while one was open for 11% -> 7% of each run, Pallas kernels for 0% -> 25%
where the time goes in v2:
time: 931 us; the launch traced here: 920 us
  waiting for transfers between devices  350 us (38%)
  Pallas kernels  259 us (28%)
  starting transfers between devices  189 us (20%)
  local copies, waits for them, and re-layouts  66.5 us (7%)
  other arithmetic  48.4 us (5%)
    pallas_call x24, Pallas kernels, call(): pl.pallas_call(kernel, grid_spec=pltpu.PrefetchScalarGridSpec(num_scalar_...  241 us
    ppermute x107, waiting for transfers between devices, flip(): lax.ppermute(value, 'ctx', [(index, index ^ bit) for index in range(8)])  213 us
    ppermute x26, waiting for transfers between devices, line_swap(): lax.ppermute(value, 'wt', [(index, index ^ offset) for index in range(4)])  118 us
    ppermute x107, starting transfers between devices, flip(): lax.ppermute(value, 'ctx', [(index, index ^ bit) for index in range(8)])  75 us
    ppermute x26, starting transfers between devices, line_swap(): lax.ppermute(value, 'wt', [(index, index ^ offset) for index in range(4)])  60.8 us
    unnamed x393, local copies, waits for them, and re-layouts  37 us
    ppermute x8, starting transfers between devices, line_inward(): return lax.ppermute(value, 'wt', [(0, 1), (3, 2)])  30.6 us
  transfers between devices with their start and end apart: 161, of which 60 were waited for; matrix products, arithmetic and copies ran while one was open for 7% of the time, Pallas kernels for 25%

profile of v2, /device:TPU:0, one launch (start us, length us, event | category | flops | bytes accessed | tf_op | source)
XLA Modules:
  0.0 920.1 jit_solution(6536307751979285455)
XLA Ops:
  21.2 14.2 %collective-permute-done.7.refs_7_ = bf16[192,640]{1,0:T(8,128)(2,1)} collective-permute-done((bf16[192,640]{1,0:T(8,128)(2,1)S(1)}, bf16[192,640]{1,0:T(8,128)(2,1)}, u32[]{:S(2)}, u32[]{:S(2)}) %collective-permute-start.7) | collective-permute-done | bytes 245792 | tf_op jit(solution)/shard_map/ppermute | solution.py:450
  47.0 10.2 %collective-permute-done.2.refs_3_ = bf16[256,1536]{1,0:T(8,128)(2,1)} collective-permute-done((bf16[256,1536]{1,0:T(8,128)(2,1)S(1)}, bf16[256,1536]{1,0:T(8,128)(2,1)}, u32[]{:S(2)}, u32[]{:S(2)}) %collective-permute-start.2) | collective-permute-done | bytes 786464 | tf_op jit(solution)/shard_map/ppermute | solution.py:446
  57.3 15.9 %collective-permute-done.1.refs_2_ = bf16[256,1536]{1,0:T(8,128)(2,1)} collective-permute-done((bf16[256,1536]{1,0:T(8,128)(2,1)S(1)}, bf16[256,1536]{1,0:T(8,128)(2,1)}, u32[]{:S(2)}, u32[]{:S(2)}) %collective-permute-start.1) | collective-permute-done | bytes 786464 | tf_op jit(solution)/shard_map/ppermute | solution.py:446
  75.5 8.0 project.1
  84.3 6.8 collective-permute-done.21
  91.3 20.2 %attend.1 = (bf16[256,384]{1,0:T(8,128)(2,1)S(1)}, bf16[256,384]{1,0:T(8,128)(2,1)}, bf16[256,384]{1,0:T(8,128)(2,1)}, bf16[256,384]{1,0:T(8,128)(2,1)}, f32[8,1,384]{2,1,0:T(1,128)S(1)}) custom-call(s32[2]{0:T(128)S(1)} %pad_add_fusion.meta, bf16[4,256,384]{2,1,0:T(8,128)(2,1)S(1)} %get-tuple-element.79.query_ref, ...), custom_call_target="tpu_custom_call" | custom-call | flops 3221225472 | bytes 2633728 | tf_op jit(solution)/shard_map/attend/pallas_call | solution.py:550
  120.4 6.2 collective-permute-done.15.refs_2_
  129.6 6.3 leave.1
  145.2 13.4 %collective-permute-done.26 = bf16[48,768]{1,0:T(8,128)(2,1)S(1)} collective-permute-done((bf16[48,768]{1,0:T(8,128)(2,1)S(1)}, bf16[48,768]{1,0:T(8,128)(2,1)S(1)}, u32[]{:S(2)}, u32[]{:S(2)}) %collective-permute-start.26) | collective-permute-done | bytes 73760 | tf_op jit(solution)/shard_map/ppermute | solution.py:450
  179.1 14.6 %collective-permute-start.38 = (f32[4,256]{1,0:T(4,128)S(1)}, f32[4,256]{1,0:T(4,128)S(1)}, u32[]{:S(2)}, u32[]{:S(2)}) collective-permute-start(f32[4,256]{1,0:T(4,128)S(1)} %get-tuple-element.186), channel_id=1, source_target_pairs={{0,2},{1,3},{2,0},{3,1},{4,6},{5,7},{6,4},{7,5},{8,10},{9,11},{10,... | collective-permute-start | bytes 12296 | tf_op jit(solution)/shard_map/ppermute | solution.py:450
  196.1 6.7 collective-permute-done.38
  211.2 11.7 %experts.7 = (bf16[4,256,1024]{2,1,0:T(8,128)(2,1)S(1)}, bf16[256,512]{1,0:T(8,128)(2,1)S(1)}, bf16[256,1536]{1,0:T(8,128)(2,1)S(1)}) custom-call(s32[2]{0:T(128)S(1)} %pad_add_fusion.meta, bf16[256,1536]{1,0:T(8,128)(2,1)S(1)} %broadcast_select_fusion.2.rows_ref.refs_3_, f32[4,256,1]{2,1,0:T(8,128)S(1)} %copy.38.gates_ref, ...), custom_call_target="tpu_custom_call" | custom-call | flops 5435817984 | bytes 25169920 | tf_op jit(solution)/shard_map/experts/pallas_call | solution.py:550
  229.2 11.7 %experts.6 = (bf16[4,256,1024]{2,1,0:T(8,128)(2,1)S(1)}, bf16[256,512]{1,0:T(8,128)(2,1)S(1)}, bf16[256,1536]{1,0:T(8,128)(2,1)S(1)}) custom-call(s32[2]{0:T(128)S(1)} %pad_add_fusion.meta, bf16[256,1536]{1,0:T(8,128)(2,1)S(1)} %broadcast_select_fusion.3.rows_ref.refs_2_, f32[4,256,1]{2,1,0:T(8,128)S(1)} %copy-done.27, bf16[4,1536,1536]{2,1,0:T(8,128)(2,1)} %expert_ref.15, ...), custom_call_target="tpu_custom_call" | custom-call | flops 5435817984 | bytes 25169920 | tf_op jit(solution)/shard_map/experts/pallas_call | solution.py:550
  259.4 11.7 %experts.5 = (bf16[4,256,1024]{2,1,0:T(8,128)(2,1)S(1)}, bf16[256,512]{1,0:T(8,128)(2,1)S(1)}, bf16[256,1536]{1,0:T(8,128)(2,1)S(1)}) custom-call(s32[2]{0:T(128)S(1)} %pad_add_fusion.meta, bf16[256,1536]{1,0:T(8,128)(2,1)S(1)} %collective-permute-done.33.rows_ref.refs_1_, f32[4,256,1]{2,1,0:T(8,128)S(1)} %copy-done.29, bf16[4,1536,1536]{2,1,0:T(8,128)(2,1)} %expert_ref.15, ...), custom_call_target="tpu_custom_call" | custom-call | flops 5435817984 | bytes 25169920 | tf_op jit(solution)/shard_map/experts/pallas_call | solution.py:550
  285.4 8.3 collective-permute-done.49
  299.4 11.9 %experts.4 = (bf16[4,256,1024]{2,1,0:T(8,128)(2,1)S(1)}, bf16[256,512]{1,0:T(8,128)(2,1)S(1)}, bf16[256,1536]{1,0:T(8,128)(2,1)S(1)}) custom-call(s32[2]{0:T(128)S(1)} %pad_add_fusion.meta, bf16[256,1536]{1,0:T(8,128)(2,1)S(1)} %copy-done.12, f32[4,256,1]{2,1,0:T(8,128)S(1)} %copy.35.gates_ref, bf16[4,1536,1536]{2,1,0:T(8,128)(2,1)} %expert_ref.15, ...), custom_call_target="tpu_custom_call" | custom-call | flops 5435817984 | bytes 25169920 | tf_op jit(solution)/shard_map/experts/pallas_call | solution.py:550
  322.6 14.7 %collective-permute-done.51.grad_ref.refs_9_ = bf16[256,1536]{1,0:T(8,128)(2,1)S(1)} collective-permute-done((bf16[256,1536]{1,0:T(8,128)(2,1)S(1)}, bf16[256,1536]{1,0:T(8,128)(2,1)S(1)}, u32[]{:S(2)}, u32[]{:S(2)}) %collective-permute-start.51) | collective-permute-done | bytes 786464 | tf_op jit(solution)/shard_map/ppermute | solution.py:450
  338.4 13.0 %experts_back.4 = (bf16[4,256,1024]{2,1,0:T(8,128)(2,1)S(1)}, bf16[4,256,512]{2,1,0:T(8,128)(2,1)S(1)}, bf16[1,256,512]{2,1,0:T(8,128)(2,1)S(1)}, bf16[1,256,256]{2,1,0:T(8,128)(2,1)S(1)}, bf16[256,1536]{1,0:T(8,128)(2,1)S(1)}) custom-call(s32[2]{0:T(128)S(1)} %pad_add_fusion.meta, bf16[256,1536]{1,0:T(8,128)(2,1)S(1)} %get-tuple-element.157.grad_ref.refs_8_, ...), custom_call_target="tpu_custom_call" | custom-call | flops 5435817984 | bytes 28708864 | tf_op jit(solution)/shard_map/experts_back/pallas_call | solution.py:550
  354.8 13.0 %experts_back.5 = (bf16[4,256,1024]{2,1,0:T(8,128)(2,1)S(1)}, bf16[4,256,512]{2,1,0:T(8,128)(2,1)S(1)}, bf16[1,256,512]{2,1,0:T(8,128)(2,1)S(1)}, bf16[1,256,256]{2,1,0:T(8,128)(2,1)S(1)}, bf16[256,1536]{1,0:T(8,128)(2,1)S(1)}) custom-call(s32[2]{0:T(128)S(1)} %pad_add_fusion.meta, bf16[256,1536]{1,0:T(8,128)(2,1)S(1)} %collective-permute-done.51.grad_ref.refs_9_, ...), custom_call_target="tpu_custom_call" | custom-call | flops 5435817984 | bytes 28708864 | tf_op jit(solution)/shard_map/experts_back/pallas_call | solution.py:550
  370.8 13.0 %experts_back.6 = (bf16[4,256,1024]{2,1,0:T(8,128)(2,1)S(1)}, bf16[4,256,512]{2,1,0:T(8,128)(2,1)S(1)}, bf16[1,256,512]{2,1,0:T(8,128)(2,1)S(1)}, bf16[1,256,256]{2,1,0:T(8,128)(2,1)S(1)}, bf16[256,1536]{1,0:T(8,128)(2,1)S(1)}) custom-call(s32[2]{0:T(128)S(1)} %pad_add_fusion.meta, bf16[256,1536]{1,0:T(8,128)(2,1)S(1)} %broadcast_select_fusion.1.grad_ref.refs_10_, ...), custom_call_target="tpu_custom_call" | custom-call | flops 5435817984 | bytes 28708864 | tf_op jit(solution)/shard_map/experts_back/pallas_call | solution.py:550
  386.6 13.0 %experts_back.7 = (bf16[4,256,1024]{2,1,0:T(8,128)(2,1)S(1)}, bf16[4,256,512]{2,1,0:T(8,128)(2,1)S(1)}, bf16[1,256,512]{2,1,0:T(8,128)(2,1)S(1)}, bf16[1,256,256]{2,1,0:T(8,128)(2,1)S(1)}, bf16[256,1536]{1,0:T(8,128)(2,1)S(1)}) custom-call(s32[2]{0:T(128)S(1)} %pad_add_fusion.meta, bf16[256,1536]{1,0:T(8,128)(2,1)S(1)} %broadcast_select_fusion.grad_ref.refs_11_, ...), custom_call_target="tpu_custom_call" | custom-call | flops 5435817984 | bytes 28708864 | tf_op jit(solution)/shard_map/experts_back/pallas_call | solution.py:550
  402.8 6.9 weight_grad.9
  419.6 10.5 %weight_grad.13 = (bf16[4,192,1536]{2,1,0:T(8,128)(2,1)}, bf16[4,192,1536]{2,1,0:T(8,128)(2,1)}) custom-call(s32[2]{0:T(128)S(1)} %pad_add_fusion.3.meta, bf16[256,1536]{1,0:T(8,128)(2,1)S(1)} %copy-done.14, bf16[256,1536]{1,0:T(8,128)(2,1)S(1)} %copy-done.17, bf16[256,1536]{1,0:T(8,128)(2,1)S(1)} %broadcast_select_fusion.3.rows_ref.refs_2_, ...), custom_call_target="tpu_custom_call" | custom-call | flops 4831838208 | bytes 14155776 | tf_op jit(solution)/shard_map/weight_grad/pallas_call | solution.py:550
  439.2 10.5 %weight_grad.12 = (bf16[4,192,1536]{2,1,0:T(8,128)(2,1)}, bf16[4,192,1536]{2,1,0:T(8,128)(2,1)}) custom-call(s32[2]{0:T(128)S(1)} %pad_add_fusion.3.meta, bf16[256,1536]{1,0:T(8,128)(2,1)S(1)} %copy-done.14, bf16[256,1536]{1,0:T(8,128)(2,1)S(1)} %copy-done.17, bf16[256,1536]{1,0:T(8,128)(2,1)S(1)} %broadcast_select_fusion.3.rows_ref.refs_2_, ...), custom_call_target="tpu_custom_call" | custom-call | flops 4831838208 | bytes 14155776 | tf_op jit(solution)/shard_map/weight_grad/pallas_call | solution.py:550
  449.7 12.8 %collective-permute-done.109 = bf16[192,768]{1,0:T(8,128)(2,1)S(1)} collective-permute-done((bf16[192,768]{1,0:T(8,128)(2,1)S(1)}, bf16[192,768]{1,0:T(8,128)(2,1)S(1)}, u32[]{:S(2)}, u32[]{:S(2)}) %collective-permute-start.109) | collective-permute-done | bytes 294944 | tf_op jit(solution)/shard_map/ppermute | solution.py:450
  467.9 10.5 %weight_grad.11 = (bf16[4,192,1536]{2,1,0:T(8,128)(2,1)}, bf16[4,192,1536]{2,1,0:T(8,128)(2,1)}) custom-call(s32[2]{0:T(128)S(1)} %pad_add_fusion.3.meta, bf16[256,1536]{1,0:T(8,128)(2,1)S(1)} %copy-done.14, bf16[256,1536]{1,0:T(8,128)(2,1)S(1)} %copy-done.17, bf16[256,1536]{1,0:T(8,128)(2,1)S(1)} %broadcast_select_fusion.3.rows_ref.refs_2_, ...), custom_call_target="tpu_custom_call" | custom-call | flops 4831838208 | bytes 14155776 | tf_op jit(solution)/shard_map/weight_grad/pallas_call | solution.py:550
  484.8 10.5 %weight_grad.10 = (bf16[4,192,1536]{2,1,0:T(8,128)(2,1)}, bf16[4,192,1536]{2,1,0:T(8,128)(2,1)}) custom-call(s32[2]{0:T(128)S(1)} %pad_add_fusion.3.meta, bf16[256,1536]{1,0:T(8,128)(2,1)S(1)} %copy-done.14, bf16[256,1536]{1,0:T(8,128)(2,1)S(1)} %copy-done.17, bf16[256,1536]{1,0:T(8,128)(2,1)S(1)} %broadcast_select_fusion.3.rows_ref.refs_2_, ...), custom_call_target="tpu_custom_call" | custom-call | flops 4831838208 | bytes 14155776 | tf_op jit(solution)/shard_map/weight_grad/pallas_call | solution.py:550
  512.7 11.4 %collective-permute-done.58 = bf16[256,1536]{1,0:T(8,128)(2,1)S(1)} collective-permute-done((bf16[256,1536]{1,0:T(8,128)(2,1)S(1)}, bf16[256,1536]{1,0:T(8,128)(2,1)S(1)}, u32[]{:S(2)}, u32[]{:S(2)}) %collective-permute-start.58) | collective-permute-done | bytes 786464 | tf_op jit(solution)/shard_map/ppermute | solution.py:450
  525.9 6.3 enter_back.1
  555.9 21.6 %attend_back.1 = (bf16[4,256,384]{2,1,0:T(8,128)(2,1)S(1)}, f32[4,256,256]{2,1,0:T(8,128)S(1)}, bf16[4,256,256]{2,1,0:T(8,128)(2,1)S(1)}) custom-call(s32[2]{0:T(128)S(1)} %pad_add_fusion.meta, bf16[4,256,384]{2,1,0:T(8,128)(2,1)S(1)} %copy-done.126, bf16[4,256,256]{2,1,0:T(8,128)(2,1)S(1)} %copy-done.120, bf16[4,256,256]{2,1,0:T(8,128)(2,1)S(1)} %copy-done.122, ...), custom_call_target="tpu_custom_call" | custom-call | flops 8053063680 | bytes 5779456 | tf_op jit(solution)/shard_map/attend_back/pallas_call | solution.py:550
  577.5 29.7 %collective-permute-done.111 = bf16[2,192,768]{2,1,0:T(8,128)(2,1)} collective-permute-done((bf16[2,192,768]{2,1,0:T(8,128)(2,1)S(1)}, bf16[2,192,768]{2,1,0:T(8,128)(2,1)}, u32[]{:S(2)}, u32[]{:S(2)}) %collective-permute-start.111) | collective-permute-done | bytes 589856 | tf_op jit(solution)/shard_map/ppermute | solution.py:446
  611.5 9.5 %collective-permute-done.152 = bf16[2,96,1536]{2,1,0:T(8,128)(2,1)S(1)} collective-permute-done((bf16[2,96,1536]{2,1,0:T(8,128)(2,1)}, bf16[2,96,1536]{2,1,0:T(8,128)(2,1)S(1)}, u32[]{:S(2)}, u32[]{:S(2)}) %collective-permute-start.152) | collective-permute-done | bytes 589856 | tf_op jit(solution)/shard_map/ppermute | solution.py:446
  625.6 8.9 collective-permute-done.140
  639.8 8.1 collective-permute-done.128
  665.1 5.6 weight_grad.7
  672.5 7.7 collective-permute-done.151
  681.5 6.0 collective-permute-done.141
  691.2 9.9 %collective-permute-done.139 = bf16[96,1536]{1,0:T(8,128)(2,1)S(1)} collective-permute-done((bf16[96,1536]{1,0:T(8,128)(2,1)S(1)}, bf16[96,1536]{1,0:T(8,128)(2,1)S(1)}, u32[]{:S(2)}, u32[]{:S(2)}) %collective-permute-start.139) | collective-permute-done | bytes 294944 | tf_op jit(solution)/shard_map/ppermute | solution.py:446
  713.0 7.7 finish.1
  739.5 13.0 %collective-permute-done.79 = f32[8,1536]{1,0:T(8,128)S(1)} collective-permute-done((f32[8,1536]{1,0:T(8,128)S(1)}, f32[8,1536]{1,0:T(8,128)S(1)}, u32[]{:S(2)}, u32[]{:S(2)}) %collective-permute-start.79) | collective-permute-done | bytes 49184 | tf_op jit(solution)/shard_map/ppermute | solution.py:450
  756.9 11.9 %collective-permute-done.154.refs_2_ = bf16[192,1536]{1,0:T(8,128)(2,1)S(1)} collective-permute-done((bf16[192,1536]{1,0:T(8,128)(2,1)S(1)}, bf16[192,1536]{1,0:T(8,128)(2,1)S(1)}, u32[]{:S(2)}, u32[]{:S(2)}) %collective-permute-start.154) | collective-permute-done | bytes 589856 | tf_op jit(solution)/shard_map/ppermute | solution.py:446
  773.2 6.0 collective-permute-done.142.refs_2_
  789.1 8.0 collective-permute-done.130.refs_2_
  807.1 8.7 collective-permute-done.81
  828.0 6.2 collective-permute-done.144.refs_4_
  841.3 7.3 collective-permute-done.132.refs_4_
  856.7 5.7 collective-permute-done.83
  886.9 5.5 place_shared.1
  (828 shorter events, 402.3 us)
Async XLA Ops:
  16.7 27.4 %collective-permute-start.17 = (bf16[192,1536]{1,0:T(8,128)(2,1)}, bf16[192,1536]{1,0:T(8,128)(2,1)}, u32[]{:S(2)}, u32[]{:S(2)}) collective-permute-start(bf16[192,1536]{1,0:T(8,128)(2,1)} %constant_dynamic-slice_fusion.3.refs_4_), channel_id=1, source_target_pairs={{0,1},{1,0},{2,3},{3,2},{4,5},{5,4},{6,7},{7,6},{8,9},{9,8},{10,11... | collective-permute-start | bytes 1769480 | tf_op jit(solution)/shard_map/ppermute | solution.py:450
  18.8 26.8 %collective-permute-start.18 = (bf16[192,1536]{1,0:T(8,128)(2,1)}, bf16[192,1536]{1,0:T(8,128)(2,1)}, u32[]{:S(2)}, u32[]{:S(2)}) collective-permute-start(bf16[192,1536]{1,0:T(8,128)(2,1)} %constant_dynamic-slice_fusion.3.refs_4_), channel_id=1, source_target_pairs={{1,2},{2,1},{5,6},{6,5},{9,10},{10,9},{13,14},{14,13},{17,18},{18,... | collective-permute-start | bytes 1769480 | tf_op jit(solution)/shard_map/ppermute | solution.py:454
  38.2 35.0 %collective-permute-start.1 = (bf16[256,1536]{1,0:T(8,128)(2,1)S(1)}, bf16[256,1536]{1,0:T(8,128)(2,1)}, u32[]{:S(2)}, u32[]{:S(2)}) collective-permute-start(bf16[256,1536]{1,0:T(8,128)(2,1)S(1)} %bitcast.161), channel_id=1, source_target_pairs={{0,16},{4,20},{8,24},{12,28},{16,0},{20,4},{24,8},{28,12},{1,17},{... | collective-permute-start | bytes 2359304 | tf_op jit(solution)/shard_map/ppermute | solution.py:446
  38.8 35.7 %collective-permute-start = (bf16[256,1536]{1,0:T(8,128)(2,1)S(1)}, bf16[256,1536]{1,0:T(8,128)(2,1)}, u32[]{:S(2)}, u32[]{:S(2)}) collective-permute-start(bf16[256,1536]{1,0:T(8,128)(2,1)S(1)} %bitcast.162), channel_id=1, source_target_pairs={{0,8},{4,12},{8,0},{12,4},{16,24},{20,28},{24,16},{28,20},{1,9},{5... | collective-permute-start | bytes 2359304 | tf_op jit(solution)/shard_map/ppermute | solution.py:446
  44.0 29.2 %collective-permute-start.20 = (bf16[192,1536]{1,0:T(8,128)(2,1)}, bf16[192,1536]{1,0:T(8,128)(2,1)}, u32[]{:S(2)}, u32[]{:S(2)}) collective-permute-start(bf16[192,1536]{1,0:T(8,128)(2,1)} %collective-permute-done.17.refs_5_), channel_id=1, source_target_pairs={{1,2},{2,1},{5,6},{6,5},{9,10},{10,9},{13,14},{14,13},{17,18},{18,... | collective-permute-start | bytes 1769480 | tf_op jit(solution)/shard_map/ppermute | solution.py:454
  45.7 38.4 %collective-permute-start.19 = (bf16[192,1536]{1,0:T(8,128)(2,1)}, bf16[192,1536]{1,0:T(8,128)(2,1)S(1)}, u32[]{:S(2)}, u32[]{:S(2)}) collective-permute-start(bf16[192,1536]{1,0:T(8,128)(2,1)} %collective-permute-done.18), channel_id=1, source_target_pairs={{1,0},{2,3},{5,4},{6,7},{9,8},{10,11},{13,12},{14,15},{17,16},{18,... | collective-permute-start | bytes 1769480 | tf_op jit(solution)/shard_map/ppermute | solution.py:458
  57.3 56.9 %collective-permute-start.22 = (bf16[192,1536]{1,0:T(8,128)(2,1)}, bf16[192,1536]{1,0:T(8,128)(2,1)S(1)}, u32[]{:S(2)}, u32[]{:S(2)}) collective-permute-start(bf16[192,1536]{1,0:T(8,128)(2,1)} %constant_dynamic-slice_fusion.3.refs_4_), channel_id=1, source_target_pairs={{0,4},{4,0},{8,12},{12,8},{16,20},{20,16},{24,28},{28,24},{1,5},{5... | collective-permute-start | bytes 1769480 | tf_op jit(solution)/shard_map/ppermute | solution.py:446
  73.2 43.3 %collective-permute-start.23 = (bf16[192,1536]{1,0:T(8,128)(2,1)}, bf16[192,1536]{1,0:T(8,128)(2,1)S(1)}, u32[]{:S(2)}, u32[]{:S(2)}) collective-permute-start(bf16[192,1536]{1,0:T(8,128)(2,1)} %collective-permute-done.17.refs_5_), channel_id=1, source_target_pairs={{0,4},{4,0},{8,12},{12,8},{16,20},{20,16},{24,28},{28,24},{1,5},{5... | collective-permute-start | bytes 1769480 | tf_op jit(solution)/shard_map/ppermute | solution.py:446
  84.2 42.4 %collective-permute-start.24 = (bf16[192,1536]{1,0:T(8,128)(2,1)S(1)}, bf16[192,1536]{1,0:T(8,128)(2,1)}, u32[]{:S(2)}, u32[]{:S(2)}) collective-permute-start(bf16[192,1536]{1,0:T(8,128)(2,1)S(1)} %broadcast_select_fusion.5.refs_6_), channel_id=1, source_target_pairs={{0,4},{4,0},{8,12},{12,8},{16,20},{20,16},{24,28},{28,24},{1,5},{5... | collective-permute-start | bytes 1769480 | tf_op jit(solution)/shard_map/ppermute | solution.py:446
  91.2 35.4 %collective-permute-start.25 = (bf16[192,1536]{1,0:T(8,128)(2,1)S(1)}, bf16[192,1536]{1,0:T(8,128)(2,1)}, u32[]{:S(2)}, u32[]{:S(2)}) collective-permute-start(bf16[192,1536]{1,0:T(8,128)(2,1)S(1)} %broadcast_select_fusion.4.refs_7_), channel_id=1, source_target_pairs={{0,4},{4,0},{8,12},{12,8},{16,20},{20,16},{24,28},{28,24},{1,5},{5... | collective-permute-start | bytes 1769480 | tf_op jit(solution)/shard_map/ppermute | solution.py:446
  135.9 33.6 %collective-permute-start.33 = (bf16[256,1536]{1,0:T(8,128)(2,1)}, bf16[256,1536]{1,0:T(8,128)(2,1)S(1)}, u32[]{:S(2)}, u32[]{:S(2)}) collective-permute-start(bf16[256,1536]{1,0:T(8,128)(2,1)} %get-tuple-element.86.rows_ref.refs_0_), channel_id=1, source_target_pairs={{0,1},{1,0},{2,3},{3,2},{4,5},{5,4},{6,7},{7,6},{8,9},{9,8},{10,11... | collective-permute-start | bytes 2359304 | tf_op jit(solution)/shard_map/ppermute | solution.py:450
  176.1 28.0 %collective-permute-start.32 = (bf16[4,4,48,768]{3,2,1,0:T(8,128)(2,1)}, bf16[4,4,48,768]{3,2,1,0:T(8,128)(2,1)}, u32[]{:S(2)}, u32[]{:S(2)}) collective-permute-start(bf16[4,4,48,768]{3,2,1,0:T(8,128)(2,1)} %pad_maximum_fusion.1.mine), channel_id=1, source_target_pairs={{0,4},{4,0},{8,12},{12,8},{16,20},{20,16},{24,28},{28,24},{1,5},{5... | collective-permute-start | bytes 3538952 | tf_op jit(solution)/shard_map/ppermute | solution.py:446
  176.1 32.4 %collective-permute-start.35 = (bf16[256,1536]{1,0:T(8,128)(2,1)S(1)}, bf16[256,1536]{1,0:T(8,128)(2,1)}, u32[]{:S(2)}, u32[]{:S(2)}) collective-permute-start(bf16[256,1536]{1,0:T(8,128)(2,1)S(1)} %copy-done.12), channel_id=1, source_target_pairs={{1,2},{2,1},{5,6},{6,5},{9,10},{10,9},{13,14},{14,13},{17,18},{18,... | collective-permute-start | bytes 2359304 | tf_op jit(solution)/shard_map/ppermute | solution.py:454
  177.7 32.3 %collective-permute-start.39 = (bf16[256,1536]{1,0:T(8,128)(2,1)S(1)}, bf16[256,1536]{1,0:T(8,128)(2,1)}, u32[]{:S(2)}, u32[]{:S(2)}) collective-permute-start(bf16[256,1536]{1,0:T(8,128)(2,1)S(1)} %collective-permute-done.37), channel_id=1, source_target_pairs={{1,0},{2,3},{5,4},{6,7},{9,8},{10,11},{13,12},{14,15},{17,16},{18,... | collective-permute-start | bytes 2359304 | tf_op jit(solution)/shard_map/ppermute | solution.py:458
  243.4 27.8 %collective-permute-start.44 = (bf16[256,1536]{1,0:T(8,128)(2,1)}, bf16[256,1536]{1,0:T(8,128)(2,1)}, u32[]{:S(2)}, u32[]{:S(2)}) collective-permute-start(bf16[256,1536]{1,0:T(8,128)(2,1)} %add.326), channel_id=1, source_target_pairs={{0,1},{3,2},{4,5},{7,6},{8,9},{11,10},{12,13},{15,14},{16,17},{19,... | collective-permute-start | bytes 2359304 | tf_op jit(solution)/shard_map/ppermute | solution.py:462
  247.4 28.1 %collective-permute-start.42 = (bf16[256,1536]{1,0:T(8,128)(2,1)}, bf16[256,1536]{1,0:T(8,128)(2,1)}, u32[]{:S(2)}, u32[]{:S(2)}) collective-permute-start(bf16[256,1536]{1,0:T(8,128)(2,1)} %add.326), channel_id=1, source_target_pairs={{1,2},{2,1},{5,6},{6,5},{9,10},{10,9},{13,14},{14,13},{17,18},{18,... | collective-permute-start | bytes 2359304 | tf_op jit(solution)/shard_map/ppermute | solution.py:454
  252.3 28.7 %collective-permute-start.47 = (f32[8,128]{1,0:T(8,128)S(1)}, f32[8,128]{1,0:T(8,128)S(1)}, u32[]{:S(2)}, u32[]{:S(2)}) collective-permute-start(f32[8,128]{1,0:T(8,128)S(1)} %broadcast_add_fusion), channel_id=1, source_target_pairs={{0,8},{4,12},{8,0},{12,4},{16,24},{20,28},{24,16},{28,20},{1,9},{5... | collective-permute-start | bytes 12296 | tf_op jit(solution)/shard_map/ppermute | solution.py:446
  273.9 37.4 %collective-permute-start.45 = (bf16[256,1536]{1,0:T(8,128)(2,1)}, bf16[256,1536]{1,0:T(8,128)(2,1)}, u32[]{:S(2)}, u32[]{:S(2)}) collective-permute-start(bf16[256,1536]{1,0:T(8,128)(2,1)} %add.329), channel_id=1, source_target_pairs={{1,2},{2,1},{5,6},{6,5},{9,10},{10,9},{13,14},{14,13},{17,18},{18,... | collective-permute-start | bytes 2359304 | tf_op jit(solution)/shard_map/ppermute | solution.py:454
  277.8 33.6 %collective-permute-start.43 = (bf16[256,1536]{1,0:T(8,128)(2,1)}, bf16[256,1536]{1,0:T(8,128)(2,1)}, u32[]{:S(2)}, u32[]{:S(2)}) collective-permute-start(bf16[256,1536]{1,0:T(8,128)(2,1)} %add.327), channel_id=1, source_target_pairs={{0,1},{1,0},{2,3},{3,2},{4,5},{5,4},{6,7},{7,6},{8,9},{9,8},{10,11... | collective-permute-start | bytes 2359304 | tf_op jit(solution)/shard_map/ppermute | solution.py:450
  321.3 49.4 %collective-permute-start.53 = (bf16[256,1536]{1,0:T(8,128)(2,1)S(1)}, bf16[256,1536]{1,0:T(8,128)(2,1)S(1)}, u32[]{:S(2)}, u32[]{:S(2)}) collective-permute-start(bf16[256,1536]{1,0:T(8,128)(2,1)S(1)} %collective-permute-done.52), channel_id=1, source_target_pairs={{1,0},{2,3},{5,4},{6,7},{9,8},{10,11},{13,12},{14,15},{17,16},{18,... | collective-permute-start | bytes 2359304 | tf_op jit(solution)/shard_map/ppermute | solution.py:458
  337.3 31.8 %collective-permute-start.54 = (bf16[256,1536]{1,0:T(8,128)(2,1)S(1)}, bf16[256,1536]{1,0:T(8,128)(2,1)S(1)}, u32[]{:S(2)}, u32[]{:S(2)}) collective-permute-start(bf16[256,1536]{1,0:T(8,128)(2,1)S(1)} %collective-permute-done.51.grad_ref.refs_9_), channel_id=1, source_target_pairs={{1,2},{2,1},{5,6},{6,5},{9,10},{10,9},{13,14},{14,13},{17,18},{18,... | collective-permute-start | bytes 2359304 | tf_op jit(solution)/shard_map/ppermute | solution.py:454
  409.7 26.9 %collective-permute-start.104 = (bf16[4,192,768]{2,1,0:T(8,128)(2,1)}, bf16[4,192,768]{2,1,0:T(8,128)(2,1)}, u32[]{:S(2)}, u32[]{:S(2)}) collective-permute-start(bf16[4,192,768]{2,1,0:T(8,128)(2,1)} %get-tuple-element.132), channel_id=1, source_target_pairs={{0,4},{4,0},{8,12},{12,8},{16,20},{20,16},{24,28},{28,24},{1,5},{5... | collective-permute-start | bytes 3538952 | tf_op jit(solution)/shard_map/ppermute | solution.py:446
  430.1 70.1 %collective-permute-start.149 = (bf16[4,192,1536]{2,1,0:T(8,128)(2,1)}, bf16[4,192,1536]{2,1,0:T(8,128)(2,1)S(1)}, u32[]{:S(2)}, u32[]{:S(2)}) collective-permute-start(bf16[4,192,1536]{2,1,0:T(8,128)(2,1)} %get-tuple-element.148), channel_id=1, source_target_pairs={{0,4},{4,0},{8,12},{12,8},{16,20},{20,16},{24,28},{28,24},{1,5},{5... | collective-permute-start | bytes 7077896 | tf_op jit(solution)/shard_map/ppermute | solution.py:446
  432.4 46.9 %collective-permute-start.59 = (bf16[256,1536]{1,0:T(8,128)(2,1)S(1)}, bf16[256,1536]{1,0:T(8,128)(2,1)S(1)}, u32[]{:S(2)}, u32[]{:S(2)}) collective-permute-start(bf16[256,1536]{1,0:T(8,128)(2,1)S(1)} %add.337), channel_id=1, source_target_pairs={{0,1},{3,2},{4,5},{7,6},{8,9},{11,10},{12,13},{15,14},{16,17},{19,... | collective-permute-start | bytes 2359304 | tf_op jit(solution)/shard_map/ppermute | solution.py:462
  438.1 24.4 %collective-permute-start.109 = (bf16[192,768]{1,0:T(8,128)(2,1)S(1)}, bf16[192,768]{1,0:T(8,128)(2,1)S(1)}, u32[]{:S(2)}, u32[]{:S(2)}) collective-permute-start(bf16[192,768]{1,0:T(8,128)(2,1)S(1)} %get-tuple-element.168), channel_id=1, source_target_pairs={{0,3},{1,2},{2,1},{3,0},{4,7},{5,6},{6,5},{7,4},{8,11},{9,10},{10,... | collective-permute-start | bytes 884744 | tf_op jit(solution)/shard_map/ppermute | solution.py:450
  439.2 26.6 %collective-permute-start.108 = (bf16[192,768]{1,0:T(8,128)(2,1)S(1)}, bf16[192,768]{1,0:T(8,128)(2,1)S(1)}, u32[]{:S(2)}, u32[]{:S(2)}) collective-permute-start(bf16[192,768]{1,0:T(8,128)(2,1)S(1)} %get-tuple-element.169), channel_id=1, source_target_pairs={{0,2},{1,3},{2,0},{3,1},{4,6},{5,7},{6,4},{7,5},{8,10},{9,11},{10,... | collective-permute-start | bytes 884744 | tf_op jit(solution)/shard_map/ppermute | solution.py:450
  449.7 52.5 %collective-permute-start.137 = (bf16[4,192,1536]{2,1,0:T(8,128)(2,1)}, bf16[4,192,1536]{2,1,0:T(8,128)(2,1)}, u32[]{:S(2)}, u32[]{:S(2)}) collective-permute-start(bf16[4,192,1536]{2,1,0:T(8,128)(2,1)} %get-tuple-element.146), channel_id=1, source_target_pairs={{0,4},{4,0},{8,12},{12,8},{16,20},{20,16},{24,28},{28,24},{1,5},{5... | collective-permute-start | bytes 7077896 | tf_op jit(solution)/shard_map/ppermute | solution.py:446
  479.3 30.1 %collective-permute-start.125 = (bf16[4,192,1536]{2,1,0:T(8,128)(2,1)}, bf16[4,192,1536]{2,1,0:T(8,128)(2,1)}, u32[]{:S(2)}, u32[]{:S(2)}) collective-permute-start(bf16[4,192,1536]{2,1,0:T(8,128)(2,1)} %get-tuple-element.144), channel_id=1, source_target_pairs={{0,4},{4,0},{8,12},{12,8},{16,20},{20,16},{24,28},{28,24},{1,5},{5... | collective-permute-start | bytes 7077896 | tf_op jit(solution)/shard_map/ppermute | solution.py:446
  496.6 191.7 %collective-permute-start.71 = (bf16[768,640]{1,0:T(8,128)(2,1)S(1)}, bf16[768,640]{1,0:T(8,128)(2,1)}, u32[]{:S(2)}, u32[]{:S(2)}) collective-permute-start(bf16[768,640]{1,0:T(8,128)(2,1)S(1)} %constant_dynamic-slice_fusion.1.refs_4_), channel_id=1, source_target_pairs={{0,4},{4,0},{8,12},{12,8},{16,20},{20,16},{24,28},{28,24},{1,5},{5... | collective-permute-start | bytes 2949128 | tf_op jit(solution)/shard_map/ppermute | solution.py:446
  499.1 36.0 %collective-permute-start.113 = (bf16[4,192,1536]{2,1,0:T(8,128)(2,1)}, bf16[4,192,1536]{2,1,0:T(8,128)(2,1)}, u32[]{:S(2)}, u32[]{:S(2)}) collective-permute-start(bf16[4,192,1536]{2,1,0:T(8,128)(2,1)} %get-tuple-element.142), channel_id=1, source_target_pairs={{0,4},{4,0},{8,12},{12,8},{16,20},{20,16},{24,28},{28,24},{1,5},{5... | collective-permute-start | bytes 7077896 | tf_op jit(solution)/shard_map/ppermute | solution.py:446
  509.3 41.8 %collective-permute-start.69 = (bf16[768,640]{1,0:T(8,128)(2,1)S(1)}, bf16[768,640]{1,0:T(8,128)(2,1)S(1)}, u32[]{:S(2)}, u32[]{:S(2)}) collective-permute-start(bf16[768,640]{1,0:T(8,128)(2,1)S(1)} %constant_dynamic-slice_fusion.1.refs_4_), channel_id=1, source_target_pairs={{0,16},{4,20},{8,24},{12,28},{16,0},{20,4},{24,8},{28,12},{1,17},{... | collective-permute-start | bytes 2949128 | tf_op jit(solution)/shard_map/ppermute | solution.py:446
  551.1 103.0 %collective-permute-start.68 = (bf16[768,640]{1,0:T(8,128)(2,1)S(1)}, bf16[768,640]{1,0:T(8,128)(2,1)S(1)}, u32[]{:S(2)}, u32[]{:S(2)}) collective-permute-start(bf16[768,640]{1,0:T(8,128)(2,1)S(1)} %constant_dynamic-slice_fusion.1.refs_4_), channel_id=1, source_target_pairs={{0,8},{4,12},{8,0},{12,4},{16,24},{20,28},{24,16},{28,20},{1,9},{5... | collective-permute-start | bytes 2949128 | tf_op jit(solution)/shard_map/ppermute | solution.py:446
  552.4 101.6 %collective-permute-start.70 = (bf16[768,640]{1,0:T(8,128)(2,1)S(1)}, bf16[768,640]{1,0:T(8,128)(2,1)S(1)}, u32[]{:S(2)}, u32[]{:S(2)}) collective-permute-start(bf16[768,640]{1,0:T(8,128)(2,1)S(1)} %collective-permute-done.69.refs_6_), channel_id=1, source_target_pairs={{0,8},{4,12},{8,0},{12,4},{16,24},{20,28},{24,16},{28,20},{1,9},{5... | collective-permute-start | bytes 2949128 | tf_op jit(solution)/shard_map/ppermute | solution.py:446
  553.1 54.1 %collective-permute-start.111 = (bf16[2,192,768]{2,1,0:T(8,128)(2,1)S(1)}, bf16[2,192,768]{2,1,0:T(8,128)(2,1)}, u32[]{:S(2)}, u32[]{:S(2)}) collective-permute-start(bf16[2,192,768]{2,1,0:T(8,128)(2,1)S(1)} %copy-done.178), channel_id=1, source_target_pairs={{0,8},{4,12},{8,0},{12,4},{16,24},{20,28},{24,16},{28,20},{1,9},{5... | collective-permute-start | bytes 1769480 | tf_op jit(solution)/shard_map/ppermute | solution.py:446
  554.5 55.3 %collective-permute-start.107 = (bf16[2,192,768]{2,1,0:T(8,128)(2,1)S(1)}, bf16[2,192,768]{2,1,0:T(8,128)(2,1)S(1)}, u32[]{:S(2)}, u32[]{:S(2)}) collective-permute-start(bf16[2,192,768]{2,1,0:T(8,128)(2,1)S(1)} %copy-done.177), channel_id=1, source_target_pairs={{0,16},{4,20},{8,24},{12,28},{16,0},{20,4},{24,8},{28,12},{1,17},{... | collective-permute-start | bytes 1769480 | tf_op jit(solution)/shard_map/ppermute | solution.py:446
  654.1 36.4 %collective-permute-start.73 = (bf16[768,640]{1,0:T(8,128)(2,1)S(1)}, bf16[768,640]{1,0:T(8,128)(2,1)}, u32[]{:S(2)}, u32[]{:S(2)}) collective-permute-start(bf16[768,640]{1,0:T(8,128)(2,1)S(1)} %collective-permute-done.69.refs_6_), channel_id=1, source_target_pairs={{0,4},{4,0},{8,12},{12,8},{16,20},{20,16},{24,28},{28,24},{1,5},{5... | collective-permute-start | bytes 2949128 | tf_op jit(solution)/shard_map/ppermute | solution.py:446
  654.1 47.7 %collective-permute-start.72 = (bf16[768,640]{1,0:T(8,128)(2,1)S(1)}, bf16[768,640]{1,0:T(8,128)(2,1)}, u32[]{:S(2)}, u32[]{:S(2)}) collective-permute-start(bf16[768,640]{1,0:T(8,128)(2,1)S(1)} %collective-permute-done.68.refs_5_), channel_id=1, source_target_pairs={{0,4},{4,0},{8,12},{12,8},{16,20},{20,16},{24,28},{28,24},{1,5},{5... | collective-permute-start | bytes 2949128 | tf_op jit(solution)/shard_map/ppermute | solution.py:446
  658.4 43.5 %collective-permute-start.74 = (bf16[768,640]{1,0:T(8,128)(2,1)S(1)}, bf16[768,640]{1,0:T(8,128)(2,1)}, u32[]{:S(2)}, u32[]{:S(2)}) collective-permute-start(bf16[768,640]{1,0:T(8,128)(2,1)S(1)} %collective-permute-done.70.refs_7_), channel_id=1, source_target_pairs={{0,4},{4,0},{8,12},{12,8},{16,20},{20,16},{24,28},{28,24},{1,5},{5... | collective-permute-start | bytes 2949128 | tf_op jit(solution)/shard_map/ppermute | solution.py:446
  701.8 30.6 %collective-permute-start.93 = (bf16[4,192,1536]{2,1,0:T(8,128)(2,1)}, bf16[4,192,1536]{2,1,0:T(8,128)(2,1)}, u32[]{:S(2)}, u32[]{:S(2)}) collective-permute-start(bf16[4,192,1536]{2,1,0:T(8,128)(2,1)} %get-tuple-element.122), channel_id=1, source_target_pairs={{0,4},{4,0},{8,12},{12,8},{16,20},{20,16},{24,28},{28,24},{1,5},{5... | collective-permute-start | bytes 7077896 | tf_op jit(solution)/shard_map/ppermute | solution.py:446
  701.8 50.7 %collective-permute-start.112 = (bf16[4,192,768]{2,1,0:T(8,128)(2,1)S(1)}, bf16[4,192,768]{2,1,0:T(8,128)(2,1)S(1)}, u32[]{:S(2)}, u32[]{:S(2)}) collective-permute-start(bf16[4,192,768]{2,1,0:T(8,128)(2,1)S(1)} %pad_maximum_fusion.2.mine), channel_id=1, source_target_pairs={{0,4},{4,0},{8,12},{12,8},{16,20},{20,16},{24,28},{28,24},{1,5},{5... | collective-permute-start | bytes 3538952 | tf_op jit(solution)/shard_map/ppermute | solution.py:446
  753.5 25.7 %collective-permute-start.142 = (bf16[192,1536]{1,0:T(8,128)(2,1)S(1)}, bf16[192,1536]{1,0:T(8,128)(2,1)S(1)}, u32[]{:S(2)}, u32[]{:S(2)}) collective-permute-start(bf16[192,1536]{1,0:T(8,128)(2,1)S(1)} %pad_maximum_fusion.9.refs_1_), channel_id=1, source_target_pairs={{0,8},{4,12},{8,0},{12,4},{16,24},{20,28},{24,16},{28,20},{1,9},{5... | collective-permute-start | bytes 1769480 | tf_op jit(solution)/shard_map/ppermute | solution.py:446
  755.6 24.4 %collective-permute-start.133 = (bf16[192,1536]{1,0:T(8,128)(2,1)S(1)}, bf16[192,1536]{1,0:T(8,128)(2,1)S(1)}, u32[]{:S(2)}, u32[]{:S(2)}) collective-permute-start(bf16[192,1536]{1,0:T(8,128)(2,1)S(1)} %pad_maximum_fusion.8.refs_1_), channel_id=1, source_target_pairs={{0,4},{4,0},{8,12},{12,8},{16,20},{20,16},{24,28},{28,24},{1,5},{5... | collective-permute-start | bytes 1769480 | tf_op jit(solution)/shard_map/ppermute | solution.py:446
  768.8 29.0 %collective-permute-start.80 = (bf16[4,192,640]{2,1,0:T(8,128)(2,1)S(1)}, bf16[4,192,640]{2,1,0:T(8,128)(2,1)S(1)}, u32[]{:S(2)}, u32[]{:S(2)}) collective-permute-start(bf16[4,192,640]{2,1,0:T(8,128)(2,1)S(1)} %get-tuple-element.119), channel_id=1, source_target_pairs={{0,4},{4,0},{8,12},{12,8},{16,20},{20,16},{24,28},{28,24},{1,5},{5... | collective-permute-start | bytes 2949128 | tf_op jit(solution)/shard_map/ppermute | solution.py:446
  867.5 48.0 %collective-permute-start.103 = (bf16[192,1536]{1,0:T(8,128)(2,1)}, bf16[192,1536]{1,0:T(8,128)(2,1)}, u32[]{:S(2)}, u32[]{:S(2)}) collective-permute-start(bf16[192,1536]{1,0:T(8,128)(2,1)} %pad_maximum_fusion.4), channel_id=1, source_target_pairs={{0,4},{4,0},{8,12},{12,8},{16,20},{20,16},{24,28},{28,24},{1,5},{5... | collective-permute-start | bytes 1769480 | tf_op jit(solution)/shard_map/ppermute | solution.py:446
  874.8 35.9 %collective-permute-start.89 = (bf16[192,640]{1,0:T(8,128)(2,1)}, bf16[192,640]{1,0:T(8,128)(2,1)}, u32[]{:S(2)}, u32[]{:S(2)}) collective-permute-start(bf16[192,640]{1,0:T(8,128)(2,1)} %fusion.12.refs_0_), channel_id=1, source_target_pairs={{0,4},{4,0},{8,12},{12,8},{16,20},{20,16},{24,28},{28,24},{1,5},{5... | collective-permute-start | bytes 737288 | tf_op jit(solution)/shard_map/ppermute | solution.py:446
  875.6 35.1 %collective-permute-start.90 = (bf16[192,640]{1,0:T(8,128)(2,1)}, bf16[192,640]{1,0:T(8,128)(2,1)}, u32[]{:S(2)}, u32[]{:S(2)}) collective-permute-start(bf16[192,640]{1,0:T(8,128)(2,1)} %collective-permute-done.86.refs_1_), channel_id=1, source_target_pairs={{0,4},{4,0},{8,12},{12,8},{16,20},{20,16},{24,28},{28,24},{1,5},{5... | collective-permute-start | bytes 737288 | tf_op jit(solution)/shard_map/ppermute | solution.py:446
  877.6 33.2 %collective-permute-start.91 = (bf16[192,640]{1,0:T(8,128)(2,1)}, bf16[192,640]{1,0:T(8,128)(2,1)}, u32[]{:S(2)}, u32[]{:S(2)}) collective-permute-start(bf16[192,640]{1,0:T(8,128)(2,1)} %collective-permute-done.87.refs_2_), channel_id=1, source_target_pairs={{0,4},{4,0},{8,12},{12,8},{16,20},{20,16},{24,28},{28,24},{1,5},{5... | collective-permute-start | bytes 737288 | tf_op jit(solution)/shard_map/ppermute | solution.py:446
  882.3 28.5 %collective-permute-start.92 = (bf16[192,640]{1,0:T(8,128)(2,1)}, bf16[192,640]{1,0:T(8,128)(2,1)}, u32[]{:S(2)}, u32[]{:S(2)}) collective-permute-start(bf16[192,640]{1,0:T(8,128)(2,1)} %collective-permute-done.88.refs_3_), channel_id=1, source_target_pairs={{0,4},{4,0},{8,12},{12,8},{16,20},{20,16},{24,28},{28,24},{1,5},{5... | collective-permute-start | bytes 737288 | tf_op jit(solution)/shard_map/ppermute | solution.py:446
  (307 other events, 3973.7 us)

commit v3 on v2

--- a/solution.py
+++ b/solution.py
@@ -442,6 +442,9 @@
     )
 
 
+COST_SHARE = 20
+
+
 def flip(value, bit):
     return lax.ppermute(value, "ctx", [(index, index ^ bit) for index in range(8)])
 
@@ -559,7 +562,9 @@
         out_shape=out_shape,
         compiler_params=pltpu.CompilerParams(vmem_limit_bytes=48 * 1024 * 1024),
         cost_estimate=pl.CostEstimate(
-            flops=int(flops), bytes_accessed=int(moved), transcendentals=0
+            flops=int(flops) // COST_SHARE,
+            bytes_accessed=int(moved) // COST_SHARE,
+            transcendentals=0,
         ),
         name=name,
     )(meta, *arrays)
@@ -583,19 +588,18 @@
 
 
 def project_kernel(meta, *refs):
-    blocks, gain_ref = refs[:4], refs[4]
-    mine, other = refs[5:9], refs[9:13]
-    normed_ref, query_ref, pair_ref, weight_ref, held = refs[13:]
+    blocks, gain_ref, mine, other = refs[:4], refs[4], refs[5], refs[6]
+    normed_ref, query_ref, pair_ref, weight_ref, held = refs[7:]
     step = pl.program_id(0)
     core, shard = meta[0] & 1, meta[1]
-    rows = mine[0].shape[0]
+    rows = mine.shape[1]
 
     @pl.when(step == 0)
     def _():
         for i in range(4):
             at = 2 * (shard ^ i)
-            weight_ref[pl.ds(aligned(at + core, rows), rows), :] = mine[i][...]
-            weight_ref[pl.ds(aligned(at + 1 - core, rows), rows), :] = other[i][...]
+            weight_ref[pl.ds(aligned(at + core, rows), rows), :] = mine[i]
+            weight_ref[pl.ds(aligned(at + 1 - core, rows), rows), :] = other[i]
 
     for r in range(4):
 
@@ -615,8 +619,8 @@
 
 def project(meta, blocks, gain, mine, other, query_width):
     token_rows, width = blocks[0].shape
-    columns = mine[0].shape[1]
-    arrays = list(blocks) + [gain] + list(mine) + list(other)
+    columns = mine.shape[2]
+    arrays = list(blocks) + [gain, mine, other]
     outs = [
         shape_of((4, token_rows, width), jnp.bfloat16),
         shape_of((4, token_rows, query_width), jnp.bfloat16),
@@ -887,14 +891,14 @@
 
 
 def leave_kernel(meta, *refs):
-    parts, mine, other = refs[:4], refs[4:8], refs[8:12]
-    states_ref, gain_ref, weight_ref, middle_ref, normed_ref = refs[12:]
+    parts, mine, other = refs[:4], refs[4:8], refs[8]
+    states_ref, gain_ref, weight_ref, middle_ref, normed_ref = refs[9:]
     core, chip, shard = meta[0] & 1, meta[0] >> 1, meta[1]
     rows = mine[0].shape[0]
     for i in range(4):
         at = 2 * (chip ^ shard ^ i)
         weight_ref[pl.ds(aligned(at + core, rows), rows), :] = mine[i][...]
-        weight_ref[pl.ds(aligned(at + 1 - core, rows), rows), :] = other[i][...]
+        weight_ref[pl.ds(aligned(at + 1 - core, rows), rows), :] = other[i]
     middle = states_ref[...].astype(jnp.float32)
     for r in range(4):
         middle += dot_plain(parts[r][...], weight_ref[2 * rows * r : 2 * rows * (r + 1), :])
@@ -905,7 +909,7 @@
 
 def leave(meta, parts, mine, other, states, gain):
     token_rows, width = states.shape
-    arrays = list(parts) + list(mine) + list(other) + [states, gain]
+    arrays = list(parts) + list(mine) + [other, states, gain]
     outs = [
         shape_of((8 * mine[0].shape[0], width), jnp.bfloat16),
         shape_of((token_rows, width), jnp.float32),
@@ -974,13 +978,13 @@
 
 
 def finish_kernel(meta, *refs):
-    parts, mine, other = refs[:4], refs[4:8], refs[8:12]
-    states_ref, middle_ref, gain_ref, grad_ref, gain_grad_ref, total = refs[12:]
+    parts, mine, other = refs[:4], refs[4], refs[5]
+    states_ref, middle_ref, gain_ref, grad_ref, gain_grad_ref, total = refs[6:]
     core = meta[0] & 1
-    columns = mine[0].shape[0]
+    columns = mine.shape[1]
     for at, weights in ((core, mine), (1 - core, other)):
         total[:, pl.ds(aligned(at, columns), columns)] = sum(
-            dot_last(parts[r][...], weights[r][...]) for r in range(4)
+            dot_last(parts[r][...], weights[r]) for r in range(4)
         )
     grad, gain_grad = norm_back_rows(
         total[...], states_ref[...].astype(jnp.float32), gain_ref[...]
@@ -991,7 +995,7 @@
 
 def finish(meta, parts, mine, other, states, grad_middle, gain):
     token_rows, width = states.shape
-    arrays = list(parts) + list(mine) + list(other) + [states, grad_middle, gain]
+    arrays = list(parts) + [mine, other, states, grad_middle, gain]
     outs = [
         shape_of((1, token_rows, width), jnp.float32),
         shape_of((1, width), jnp.float32),
@@ -1189,7 +1193,17 @@
                 start = stop
 
 
-def weight_grad(meta, order, operands, index):
+def weight_grad_whole_kernel(pairs, meta, *refs):
+    at, start = 0, 0
+    for count in pairs:
+        lefts, rights = refs[at : at + count], refs[at + count : at + 2 * count]
+        at += 2 * count
+        part = sum(dot_first(a[...], b[0]) for a, b in zip(lefts, rights)).astype(jnp.bfloat16)
+        refs[-1][:, start : start + part.shape[1]] = part
+        start += part.shape[1]
+
+
+def weight_grad(meta, order, operands, index, split=True):
     token_rows, width = operands[0][0][0].shape
     tile = width // 4
     scalars = jnp.stack([order, meta[0]])
@@ -1198,14 +1212,30 @@
         arrays += list(lefts) + list(rights)
         in_specs += [pl.BlockSpec((token_rows, tile), lambda i, m: (0, i ^ m[0]))] * len(lefts)
         units = rights[0].shape[-1]
+        at = index if rights[0].shape[0] > 1 else 0
         in_specs += [
-            pl.BlockSpec((1, token_rows, units), lambda i, m, at=index: (at, 0, 0))
+            pl.BlockSpec((1, token_rows, units), lambda i, m, at=at: (at, 0, 0))
         ] * len(rights)
         columns += units
+    tokens = token_rows * len(operands[0][0])
+    counts = [len(left) for left, _ in operands]
+    if not split:
+        return call(
+            functools.partial(weight_grad_whole_kernel, counts),
+            "weight_grad_whole",
+            scalars,
+            arrays,
+            (4,),
+            in_specs,
+            pl.BlockSpec((tile, columns), lambda i, m: (i, 0)),
+            shape_of((width, columns), jnp.bfloat16),
+            [],
+            2 * tokens * width * columns,
+            2 * width * columns + 4 * tokens * width + 2 * tokens * columns,
+        )
     outs = [shape_of((4, tile // 2, columns), jnp.bfloat16)] * 2
-    tokens = token_rows * len(operands[0][0])
     return call(
-        functools.partial(weight_grad_kernel, [len(left) for left, _ in operands], 1),
+        functools.partial(weight_grad_kernel, counts, 1),
         "weight_grad",
         scalars,
         arrays,
@@ -1220,47 +1250,74 @@
 
 
 def place_expert_kernel(meta, *refs):
-    mine, other, out_ref = refs[-9:-5], refs[-5:-1], refs[-1]
+    mine, other, out_ref = refs[-6:-2], refs[-2], refs[-1]
     step = pl.program_id(0)
     core = meta[0] & 1
     rows = mine[0].shape[0]
+    columns = out_ref.shape[2]
+    out_ref[0, pl.ds(aligned(1 - core, rows), rows), :] = other[0, :, :columns].astype(
+        jnp.float32
+    )
     for r in range(4):
 
         @pl.when(step == r)
         def _():
-            out_ref[0, pl.ds(aligned(core, rows), rows), :] = mine[r][...].astype(jnp.float32)
-            out_ref[0, pl.ds(aligned(1 - core, rows), rows), :] = other[r][...].astype(
+            out_ref[0, pl.ds(aligned(core, rows), rows), :] = mine[r][:, :columns].astype(
                 jnp.float32
             )
 
 
-def place_expert(meta, total, index, shape, mine, other):
-    rows, columns = mine[0].shape
-    arrays = list(mine) + list(other)
-    in_specs = [whole(a) for a in arrays]
+def place_total_kernel(meta, *refs):
+    refs[-1][0] = refs[-2][...].astype(jnp.float32)
+
+
+def place_call(kernel, name, meta, total, arrays, in_specs, out_spec, shape, moved):
     aliases = {}
     if total is not None:
         arrays = [total] + arrays
         in_specs = [pl.BlockSpec(memory_space=pl.ANY)] + in_specs
         aliases = {1: 0}
     return pl.pallas_call(
-        place_expert_kernel,
+        kernel,
         grid_spec=pltpu.PrefetchScalarGridSpec(
-            num_scalar_prefetch=1,
-            grid=(4,),
-            in_specs=in_specs,
-            out_specs=pl.BlockSpec(
-                (1, 2 * rows, columns), lambda r, m: (index, (m[0] >> 1) ^ r, 0)
-            ),
+            num_scalar_prefetch=1, grid=(4,), in_specs=in_specs, out_specs=out_spec
         ),
         out_shape=shape_of(shape, jnp.float32),
         input_output_aliases=aliases,
         compiler_params=pltpu.CompilerParams(vmem_limit_bytes=48 * 1024 * 1024),
-        cost_estimate=pl.CostEstimate(
-            flops=0, bytes_accessed=8 * rows * columns * 6, transcendentals=0
-        ),
-        name="place_expert",
+        cost_estimate=pl.CostEstimate(flops=0, bytes_accessed=moved // COST_SHARE, transcendentals=0),
+        name=name,
     )(meta, *arrays)
+
+
+def place_expert(meta, total, index, shape, mine, other):
+    rows, columns = mine[0].shape
+    return place_call(
+        place_expert_kernel,
+        "place_expert",
+        meta,
+        total,
+        list(mine) + [other],
+        [whole(a) for a in mine] + [pl.BlockSpec((1, rows, columns), lambda r, m: (r, 0, 0))],
+        pl.BlockSpec((1, 2 * rows, shape[2]), lambda r, m: (index, (m[0] >> 1) ^ r, 0)),
+        shape,
+        8 * rows * columns * 6,
+    )
+
+
+def place_total(meta, total, index, shape, value):
+    rows, columns = value.shape
+    return place_call(
+        place_total_kernel,
+        "place_total",
+        meta,
+        total,
+        [value],
+        [pl.BlockSpec((rows // 4, columns), lambda r, m: (r, 0))],
+        pl.BlockSpec((1, rows // 4, columns), lambda r, m: (index, r, 0)),
+        shape,
+        rows * columns * 6,
+    )
 
 
 def place_shared_kernel(meta, mine, other, out_ref):
@@ -1291,15 +1348,15 @@
 
 
 def place_heads_kernel(meta, *refs):
-    mine, other, out_ref = refs[:4], refs[4:8], refs[8]
+    mine, other, out_ref = refs[:4], refs[4], refs[5]
     core, chip = meta[0] & 1, meta[0] >> 1
     rows, columns = mine[0].shape
     group_width = columns - 2 * HEAD_SIZE
     for r in range(4):
         head = chip ^ r
-        for at, pieces in ((core, mine), (1 - core, other)):
+        for at, pieces in ((core, [piece[...] for piece in mine]), (1 - core, other)):
             to = pl.ds(aligned(at, rows), rows)
-            values = pieces[r][...].astype(jnp.float32)
+            values = pieces[r].astype(jnp.float32)
             out_ref[to, pl.ds(aligned(head, group_width), group_width)] = values[:, :group_width]
             out_ref[to, pl.ds(aligned(4 * group_width // HEAD_SIZE + head, HEAD_SIZE), HEAD_SIZE)] = (
                 values[:, group_width : group_width + HEAD_SIZE]
@@ -1311,7 +1368,7 @@
 
 def place_heads(meta, mine, other):
     rows, columns = mine[0].shape
-    arrays = list(mine) + list(other)
+    arrays = list(mine) + [other]
     outs = shape_of((2 * rows, 4 * columns), jnp.float32)
     return call(
         place_heads_kernel,
@@ -1355,6 +1412,34 @@
         0,
         size_of([mine, other, outs]),
     )
+
+
+class Clock:
+    def __init__(self):
+        self.last = None
+
+    def __call__(self, *values):
+        if self.last is None:
+            return values if len(values) > 1 else values[0]
+        held = lax.optimization_barrier(tuple(values) + (self.last,))[:-1]
+        return held if len(held) > 1 else held[0]
+
+    def mark(self, value):
+        self.last = value
+        return value
+
+
+SUMMED = 0
+SHARED_WITH = 0
+EARLY = (
+    "H", "W", "K", "K", "W", "S", "O", "K", "S", "W", "O", "M", "S", "O", "M", "S", "O", "O", "S", "M", "S", "M", "R", "K",
+    "M", "M", "K", "M", "R", "K", "M", "M", "K", "M", "R", "M", "M", "M", "M",
+)
+LATE = (
+    "L", "2", "0", "2", "3", "0", "L", "3", "1", "2", "L", "1", "3", "L", "2", "O", "0", "3", "1", "O", "L", "2", "O", "3",
+    "0", "1", "O", "2", "3", "O", "L", "2", "Q", "O", "3", "Q", "0", "1", "L", "O", "Q", "O", "L", "Q", "Q", "1", "0", "S",
+    "Q", "1", "0", "L", "Q", "L", "Q", "S", "L", "L", "S",
+)
 
 
 def fast_device(
@@ -1374,14 +1459,13 @@
     context_count, shard_count = 8, 4
     context_index = lax.axis_index("ctx").astype(jnp.int32)
     shard_index = lax.axis_index("wt").astype(jnp.int32)
-    meta = jnp.stack([context_index, shard_index])
+    plain_meta = jnp.stack([context_index, shard_index])
     core = context_index & 1
     chip = context_index >> 1
     at_end = (shard_index == 0) | (shard_index == shard_count - 1)
     group_width = QUERY_HEADS // KEY_VALUE_HEADS * HEAD_SIZE
     query_width = QUERY_HEADS * HEAD_SIZE
     kv_width = KEY_VALUE_HEADS * HEAD_SIZE
-    slice_width = group_width + 2 * HEAD_SIZE
     scale = 1.0 / math.sqrt(HEAD_SIZE)
     all_tokens = token_rows * context_count * shard_count
     shard_rows = query_key_value_weight.shape[0]
@@ -1389,187 +1473,505 @@
     local_experts = expert_weight.shape[0]
     bf16, f32 = jnp.bfloat16, jnp.float32
     states = hidden[0]
-
-    blocks = chips_swap([states] * 4)
-
-    qkv_half = lax.dynamic_slice_in_dim(query_key_value_weight, core * half_rows, half_rows, 0)
-    qkv_half = jnp.concatenate(
-        [
-            lax.dynamic_slice_in_dim(qkv_half, chip * group_width, group_width, 1),
-            lax.dynamic_slice_in_dim(qkv_half, query_width + chip * HEAD_SIZE, HEAD_SIZE, 1),
+    clock = Clock()
+    have = {}
+
+    def meta():
+        return clock(plain_meta)
+
+    def now(*values):
+        return clock(*values)
+
+
+    def hidden_chain():
+        have["blocks"] = chips_swap([states] * 4)
+        yield
+
+    def qkv_chain():
+        rows = lax.dynamic_slice_in_dim(query_key_value_weight, core * half_rows, half_rows, 0)
+        half = jnp.concatenate(
+            [
+                lax.dynamic_slice_in_dim(rows, chip * group_width, group_width, 1),
+                lax.dynamic_slice_in_dim(rows, query_width + chip * HEAD_SIZE, HEAD_SIZE, 1),
+                lax.dynamic_slice_in_dim(
+                    rows, query_width + kv_width + chip * HEAD_SIZE, HEAD_SIZE, 1
+                ),
+            ],
+            axis=1,
+        )
+        came = line_swap(half, 1)
+        yield
+        pair = clock.mark(jnp.stack([half, now(came)]))
+        came = line_swap(pair, 2)
+        yield
+        have["qkv_mine"] = clock.mark(jnp.concatenate([pair, now(came)]))
+        have["qkv_other"] = flip(have["qkv_mine"], 1)
+        yield
+
+    def small_chain():
+        expert_ids = jnp.arange(EXPERTS, dtype=jnp.int32)
+        matrix = jnp.sum(
+            jnp.where(
+                routes[0][None, :, :] == expert_ids[:, None, None], route_gates[0][None, :, :], 0.0
+            ),
+            axis=-1,
+        )
+        have["valid"] = valid_mask[0].astype(f32)
+        gains = jnp.concatenate([gain_in, gain_mid]).astype(f32).reshape(-1, token_rows)
+        gain_rows = gains.shape[0]
+        filled = EXPERTS + gain_rows
+        pack = jnp.concatenate(
+            [
+                matrix,
+                gains,
+                jnp.full((32 - filled, token_rows), jnp.sum(have["valid"]), f32),
+            ]
+        )
+        came = line_swap(pack, 1)
+        yield
+        pair = clock.mark(jnp.stack([pack, now(came)]))
+        came = line_swap(pair, 2)
+        yield
+        all_packs = clock.mark(jnp.concatenate([pair, now(came)]))
+        have["gates"] = [
             lax.dynamic_slice_in_dim(
-                qkv_half, query_width + kv_width + chip * HEAD_SIZE, HEAD_SIZE, 1
-            ),
-        ],
-        axis=1,
-    )
-    qkv_mine = [qkv_half] + [line_swap(qkv_half, i) for i in (1, 2, 3)]
-    qkv_other = core_swap(qkv_mine)
-
-    gains = jnp.stack([gain_in, gain_mid])
-    gains = jnp.stack([gains] + [line_swap(gains, i) for i in (1, 2, 3)])
-    gains = jnp.stack([pick(gains, shard_index ^ i) for i in range(4)], axis=1)
-    gains = gains.reshape(2, 1, width).astype(f32)
-
-    normed_in, query, pair, qkv_slice = project(
-        meta, blocks, gains[0], qkv_mine, qkv_other, group_width
-    )
-    pair_other = flip(pair, 1)
-
-    out_half = lax.dynamic_slice_in_dim(out_weight, core * half_rows, half_rows, 0)
-    out_mine = line_gather(out_half, at_end)
-    out_other = core_swap(out_mine)
-
-    eighth = shard_rows // 8
-    shared_units = SF // shard_count
-    shared_piece = lax.dynamic_slice_in_dim(shared_weight, context_index * eighth, eighth, 0)
-    shared_piece = shared_piece.reshape(eighth, 3, shard_count, shared_units)
-
-    def shared_columns(index):
-        part = lax.dynamic_index_in_dim(shared_piece, shard_index ^ index, 2, keepdims=False)
-        return part.reshape(eighth, 3 * shared_units)
-
-    shared_pieces = jnp.stack(
-        [shared_columns(0)] + [line_swap(shared_columns(i), i) for i in (1, 2, 3)]
-    )
-    shared_mine = jnp.stack(chips_gather(shared_pieces, False))
-    shared_slice = join_shared(meta, shared_mine, flip(shared_mine, 1))
-
-    expert_ids = jnp.arange(EXPERTS, dtype=jnp.int32)
-    gate_matrix = jnp.sum(
-        jnp.where(
-            routes[0][None, :, :] == expert_ids[:, None, None], route_gates[0][None, :, :], 0.0
-        ),
-        axis=-1,
-    ).reshape(shard_count, local_experts, token_rows)
-    gates = [pick(gate_matrix, shard_index)] + [
-        line_swap(pick(gate_matrix, shard_index ^ i), i) for i in (1, 2, 3)
-    ]
-    gates = [part[..., None] for part in gates]
-
-    valid_float = valid_mask[0].astype(f32)
-    valid_count = everywhere_sum(jnp.full((8, 128), jnp.sum(valid_float), f32))[0, 0]
-
-    mixed_heads, log_total = attend(meta, query, pair, pair_other, scale)
-    mixed = chips_swap(mixed_heads)
-    out_rel, middle, normed_mid = leave(meta, mixed, out_mine, out_other, states, gains[1])
-
-    line_rows = line_gather(normed_mid, at_end)
-    forward = [
-        experts(meta, line_rows[i], gates[i], expert_weight, shared_slice) for i in range(4)
-    ]
-    gate_ups, shared_gate_ups, partial_out = zip(*forward)
-    final_state = middle + line_reduce(partial_out)
-
-    deviation = final_state - teacher[0].astype(f32)
-    squared = jnp.sum(valid_float[:, None] * deviation * deviation)
-    grad_final = all_tokens / valid_count * valid_float[:, None] * deviation
-
-    line_grads = line_gather(grad_final.astype(bf16), at_end)
-    backward = [
-        experts_back(
-            meta,
-            line_grads[i],
-            gates[i],
-            gate_ups[i],
-            shared_gate_ups[i],
-            expert_weight,
-            shared_slice,
-        )
-        for i in range(4)
-    ]
-    grad_gate_ups, acts, shared_grads, shared_acts, partial_rows = zip(*backward)
-    grad_normed_mid = line_reduce(partial_rows)
-
-    grad_middle, grad_branch, grad_gain_mid, *grad_mixed = enter_back(
-        meta, grad_final, grad_normed_mid, middle, gains[1], out_rel
-    )
-    grad_mixed = chips_swap(grad_mixed)
-
-    grad_query, grad_pair, grad_pair_other = attend_back(
-        meta, query, pair, pair_other, log_total, mixed_heads, grad_mixed, scale
-    )
-    grad_pair = grad_pair + flip(grad_pair_other, 1).astype(f32)
-    grad_projected = jnp.concatenate([grad_query, grad_pair.astype(bf16)], axis=-1)
-
-    keep, give = weight_grad(
-        meta,
-        shard_index,
-        [([normed_in.reshape(4 * token_rows, width)], [grad_projected.reshape(1, 4 * token_rows, -1)])],
-        0,
-    )
-    came = flip(give, 1)
-    grad_qkv = line_reduce([keep[i] + came[i] for i in range(4)]).astype(bf16)
-    grad_qkv = chips_gather(grad_qkv, False)
-    grad_qkv = place_heads(meta, grad_qkv, core_swap(grad_qkv))
-
-    qkv_rel = chips_gather(
-        lax.dynamic_slice_in_dim(qkv_slice, core * (width // 2), width // 2, 0), True
-    )
-    grad_parts = chips_swap([grad_projected[r] for r in range(4)])
-    grad_hidden, grad_gain_in = finish(
-        meta, grad_parts, qkv_rel, core_swap(qkv_rel), states, grad_middle, gains[0]
-    )
-
-    grad_experts = None
-    for expert in range(local_experts):
+                all_packs[i], shard_index * local_experts, local_experts, 0
+            )[..., None]
+            for i in range(4)
+        ]
+        gains = all_packs[:, EXPERTS:filled].reshape(4, 2, shard_rows)
+        gains = jnp.stack([pick(gains, shard_index ^ i) for i in range(4)], axis=1)
+        have["gains"] = gains.reshape(2, 1, width)
+        total = jnp.broadcast_to(jnp.sum(all_packs[:, filled, 0]), (8, 128))
+        yield
+        total = now(total)
+        for bit in (1, 2, 4):
+            came = flip(total, bit)
+            yield
+            total = clock.mark(total + now(came))
+        have["count"] = total[0, 0]
+        yield
+
+    def shared_chain():
+        eighth = shard_rows // 8
+        units = SF // shard_count
+        piece = lax.dynamic_slice_in_dim(shared_weight, context_index * eighth, eighth, 0)
+        piece = piece.reshape(eighth, 3, shard_count, units)
+
+        def columns(index):
+            part = lax.dynamic_index_in_dim(piece, shard_index ^ index, 2, keepdims=False)
+            return part.reshape(eighth, 3 * units)
+
+        first = now(jnp.stack([columns(0), columns(2)]))
+        came = line_swap(now(jnp.stack([columns(1), columns(3)])), 1)
+        yield
+        came = now(came)
+        mine = jnp.stack([first[0], came[0]])
+        came = line_swap(clock.mark(jnp.stack([first[1], came[1]])), 2)
+        yield
+        pieces = clock.mark(jnp.concatenate([mine, now(came)]))
+        came = flip(pieces, 2)
+        yield
+        pair = clock.mark(jnp.stack([pieces, now(came)]))
+        came = flip(pair, 4)
+        yield
+        mine = clock.mark(jnp.concatenate([pair, now(came)]))
+        other = flip(mine, 1)
+        yield
+        have["shared"] = join_shared(meta(), mine, other)
+        clock.mark(have["shared"])
+        yield
+
+    def out_chain():
+        half = lax.dynamic_slice_in_dim(now(out_weight), core * half_rows, half_rows, 0)
+        near = line_swap(half, 1)
+        yield
+        near = now(near)
+        middle = line_middle(now(half))
+        middle_far = line_middle(near)
+        yield
+        outward = line_outward(now(middle))
+        yield
+        outward_far = line_outward(now(middle_far))
+        yield
+        outward, outward_far = now(outward, outward_far)
+        third = jnp.where(at_end, outward, middle_far)
+        fourth = jnp.where(at_end, outward_far, middle)
+        have["out_mine"] = [half, near, third, fourth]
+        have["out_other"] = flip(clock.mark(jnp.stack(have["out_mine"])), 1)
+        yield
+
+    def qkv_all_chain():
+        half = lax.dynamic_slice_in_dim(
+            now(have["qkv_slice"]), core * (width // 2), width // 2, 0
+        )
+        came = flip(half, 2)
+        yield
+        pair = clock.mark(jnp.stack([half, now(came)]))
+        came = flip(pair, 4)
+        yield
+        have["rel_mine"] = clock.mark(jnp.concatenate([pair, now(came)]))
+        have["rel_other"] = flip(have["rel_mine"], 1)
+        yield
+
+    def main_chain():
+        gains = have["gains"]
+        normed_in, query, pair, qkv_slice = project(
+            meta(), have["blocks"], gains[0], have["qkv_mine"], have["qkv_other"], group_width
+        )
+        clock.mark(pair)
+        have["normed_in"], have["qkv_slice"] = normed_in, qkv_slice
+        pair_other = flip(pair, 1)
+        yield
+        mixed_heads, log_total = attend(meta(), query, pair, pair_other, scale)
+        clock.mark(log_total)
+        have["attend"] = (query, pair, pair_other, log_total, mixed_heads)
+        mixed = chips_swap(mixed_heads)
+        have["mixed"] = mixed
+        yield
+        out_rel, middle, normed_mid = leave(
+            meta(), mixed, have["out_mine"], have["out_other"], states, gains[1]
+        )
+        have["out_rel"], have["middle"] = out_rel, middle
+        clock.mark(normed_mid)
+
+        near, center = line_swap(normed_mid, 1), line_middle(normed_mid)
+        yield
+        gates, shared_slice = have["gates"], have["shared"]
+        gate_ups, shared_gate_ups, outs = [], [], []
+
+        def forward(rows, i):
+            result = experts(meta(), rows, gates[i], expert_weight, shared_slice)
+            clock.mark(result[2])
+            gate_ups.append(result[0])
+            shared_gate_ups.append(result[1])
+            outs.append(result[2])
+
+        forward(normed_mid, 0)
+        yield
+        near, center = now(near, center)
+        far, outward = line_middle(near), line_outward(center)
+        forward(near, 1)
+        yield
+        far, outward = now(far, outward)
+        outward_far = line_outward(far)
+        third = clock.mark(jnp.where(at_end, outward, far))
+        forward(third, 2)
+        yield
+        outward_far = now(outward_far)
+        fourth = clock.mark(jnp.where(at_end, outward_far, center))
+        forward(fourth, 3)
+        line_rows = [normed_mid, near, third, fourth]
+        came = line_inward(outs[3])
+        yield
+        carried = clock.mark(outs[2] + now(came))
+        inward, crossed = line_inward(carried), line_middle(carried)
+        yield
+        inward, crossed = now(inward, crossed)
+        near_out = clock.mark(outs[1] + crossed)
+        middle_out = clock.mark(outs[3] + inward)
+        near_out, middle_out = line_swap(near_out, 1), line_middle(middle_out)
+        yield
+        near_out, middle_out = now(near_out, middle_out)
+        final_state = (
+            middle + outs[0].astype(f32) + near_out.astype(f32) + middle_out.astype(f32)
+        )
+        valid = have["valid"]
+        deviation = final_state - teacher[0].astype(f32)
+        have["squared"] = jnp.sum(valid[:, None] * deviation * deviation)
+        grad_final = all_tokens / have["count"] * valid[:, None] * deviation
+        have["final"], have["grad_final"] = final_state.astype(bf16)[None], grad_final
+        grad_low = clock.mark(grad_final.astype(bf16))
+        near, center = line_swap(grad_low, 1), line_middle(grad_low)
+        yield
+        kept = []
+
+        def backward(grads, i):
+            kept.append(
+                experts_back(
+                    meta(),
+                    grads,
+                    gates[i],
+                    gate_ups[i],
+                    shared_gate_ups[i],
+                    expert_weight,
+                    shared_slice,
+                )
+            )
+            clock.mark(kept[-1][4])
+
+        backward(grad_low, 0)
+        yield
+        near, center = now(near, center)
+        far, outward = line_middle(near), line_outward(center)
+        backward(near, 1)
+        yield
+        far, outward = now(far, outward)
+        outward_far = line_outward(far)
+        third = clock.mark(jnp.where(at_end, outward, far))
+        backward(third, 2)
+        yield
+        outward_far = now(outward_far)
+        fourth = clock.mark(jnp.where(at_end, outward_far, center))
+        backward(fourth, 3)
+        have["line"] = (line_rows, [grad_low, near, third, fourth])
+        have["experts"] = list(zip(*kept))
+        yield
+
+
+    def states_chain():
+        outs = have["experts"][4]
+        came = line_inward(outs[3])
+        yield
+        carried = clock.mark(outs[2] + now(came))
+        inward, crossed = line_inward(carried), line_middle(carried)
+        yield
+        inward, crossed = now(inward, crossed)
+        near_out = clock.mark(outs[1] + crossed)
+        middle_out = clock.mark(outs[3] + inward)
+        near_out, middle_out = line_swap(near_out, 1), line_middle(middle_out)
+        yield
+        near_out, middle_out = now(near_out, middle_out)
+        grad_normed = clock.mark(
+            outs[0].astype(f32) + near_out.astype(f32) + middle_out.astype(f32)
+        )
+        grad_middle, grad_branch, grad_gain_mid, *grad_mixed = enter_back(
+            meta(),
+            have["grad_final"],
+            grad_normed,
+            have["middle"],
+            have["gains"][1],
+            have["out_rel"],
+        )
+        clock.mark(grad_branch)
+        have["grad_branch"], have["grad_gain_mid"] = grad_branch, grad_gain_mid
+        grad_mixed = chips_swap(grad_mixed)
+        yield
+        query, pair, pair_other, log_total, mixed_heads = have["attend"]
+        grad_query, grad_pair, grad_other = attend_back(
+            meta(), query, pair, pair_other, log_total, mixed_heads, grad_mixed, scale
+        )
+        clock.mark(grad_query)
+        came = flip(grad_other, 1)
+        yield
+        grad_pair = grad_pair + now(came).astype(f32)
+        projected = clock.mark(jnp.concatenate([grad_query, grad_pair.astype(bf16)], axis=-1))
+        have["grad_projected"] = projected
+        parts = chips_swap([projected[r] for r in range(4)])
+        yield
+        grad_hidden, grad_gain_in = finish(
+            meta(),
+            parts,
+            have["rel_mine"],
+            have["rel_other"],
+            states,
+            grad_middle,
+            have["gains"][0],
+        )
+        clock.mark(grad_gain_in)
+        have["grad_hidden"] = grad_hidden
+        sums = jnp.concatenate(
+            [grad_gain_in, have["grad_gain_mid"], jnp.full((6, width), have["squared"], f32)],
+            axis=0,
+        )
+        for bit in (1, 2, 4):
+            came = flip(sums, bit)
+            yield
+            sums = clock.mark(sums + now(came))
+        for offset in (1, 2):
+            came = line_swap(sums, offset)
+            yield
+            sums = clock.mark(sums + now(came))
+        own = lax.dynamic_slice_in_dim(sums, shard_index * shard_rows, shard_rows, 1)
+        have["sums"] = (own, 0.5 * sums[2, 0] / (have["count"] * width))
+        yield
+
+    def expert_chain(expert):
+        line_rows, line_grads = have["line"]
+        grad_gate_ups, acts, shared_grads, shared_acts = have["experts"][:4]
+        operands = [(line_rows, grad_gate_ups), (line_grads, acts)]
+        if expert == SHARED_WITH:
+            operands += [(line_rows, shared_grads), (line_grads, shared_acts)]
+        keep, give = weight_grad(meta(), chip, operands, expert)
+        clock.mark(keep)
+        came = flip(give, 1)
+        yield
+        came = now(came)
+        if expert % 2 == 0:
+            first, second = 2, 4
+            give = clock.mark(keep[1::2] + came[1::2])
+            keep = keep[0::2] + came[0::2]
+        else:
+            first, second = 4, 2
+            give = clock.mark(keep[2:] + came[2:])
+            keep = keep[:2] + came[:2]
+        came = flip(give, first)
+        yield
+        came = now(came)
+        give = clock.mark(keep[1] + came[1])
+        keep = keep[0] + came[0]
+        came = flip(give, second)
+        yield
+        own = clock.mark(keep + now(came))
+        came = flip(own, second)
+        yield
+        pair = clock.mark(jnp.stack([own, now(came)]))
+        came = flip(pair, first)
+        yield
+        came = now(came)
+        if expert % 2 == 0:
+            mine = [own, came[0], pair[1], came[1]]
+        else:
+            mine = [own, pair[1], came[0], came[1]]
+        stacked = clock.mark(jnp.stack(mine))
+        other = flip(stacked, 1)
+        if expert == SHARED_WITH:
+            have["shared_sum"] = stacked[:, :, 3 * F :]
+        yield
+        have["grad_experts"] = place_expert(
+            meta(), have.get("grad_experts"), expert, expert_weight.shape, mine, other
+        )
+        clock.mark(have["grad_experts"])
+        yield
+
+    def shared_grad_chain():
+        total = now(have["shared_sum"])
+        parts = [pick(total, chip ^ shard_index ^ i) for i in range(4)]
+        parts = [parts[0]] + [line_swap(clock.mark(parts[i]), i) for i in (1, 2, 3)]
+        yield
+        mine = clock.mark(jnp.stack(now(*parts)))
+        other = flip(mine, 1)
+        yield
+        have["grad_shared"] = clock.mark(place_shared(meta(), mine, other))
+        yield
+
+    def summed_chain():
+        line_rows, line_grads = have["line"]
+        grad_gate_ups, acts = have["experts"][:2]
+        sums = []
+        for expert in range(SUMMED):
+            sums.append(
+                weight_grad(
+                    meta(),
+                    jnp.int32(0),
+                    [(line_rows, grad_gate_ups), (line_grads, acts)],
+                    expert,
+                    split=False,
+                )
+            )
+            clock.mark(sums[-1])
+        sums = lax.psum(sums, "ctx")
+        yield
+        for expert in range(SUMMED):
+            have["grad_experts"] = place_total(
+                meta(), have.get("grad_experts"), expert, expert_weight.shape, sums[expert]
+            )
+            clock.mark(have["grad_experts"])
+        yield
+
+    def line_reduce_steps(keep, came):
+        came = now(came)
+        parts = [keep[i] + came[i] for i in range(4)]
+        came = line_inward(clock.mark(parts[3]))
+        yield
+        carried = clock.mark(parts[2] + now(came))
+        inward, crossed = line_inward(carried), line_middle(carried)
+        yield
+        inward, crossed = now(inward, crossed)
+        near_out = clock.mark(parts[1] + crossed)
+        middle_out = clock.mark(parts[3] + inward)
+        near_out, middle_out = line_swap(near_out, 1), line_middle(middle_out)
+        yield
+        near_out, middle_out = now(near_out, middle_out)
+        have["line_sum"] = clock.mark(
+            (parts[0].astype(f32) + near_out.astype(f32) + middle_out.astype(f32)).astype(bf16)
+        )
+
+    def out_grad_chain():
+        mixed = jnp.concatenate(have["mixed"], axis=1)
         keep, give = weight_grad(
-            meta, chip, [(line_rows, grad_gate_ups), (line_grads, acts)], expert
-        )
-        reduced = chips_reduce(keep, flip(give, 1))
-        reduced = chips_gather(reduced, expert % 2 == 1)
-        grad_experts = place_expert(
-            meta, grad_experts, expert, expert_weight.shape, reduced, core_swap(reduced)
-        )
-
-    keep, give = weight_grad(
-        meta, shard_index, [(line_rows, shared_grads), (line_grads, shared_acts)], 0
-    )
-    came = flip(give, 1)
-    grad_shared = [keep[0] + came[0]] + [line_swap(keep[i] + came[i], i) for i in (1, 2, 3)]
-    grad_shared = jnp.stack(grad_shared)
-
-    def chips_sum(value, axis):
-        upper, lower = jnp.split(value, 2, axis=axis)
-        upper = upper + flip(upper, 2)
-        lower = lower + flip(lower, 4)
-        upper = upper + flip(upper, 4)
-        lower = lower + flip(lower, 2)
-        return jnp.concatenate([upper, lower], axis=axis)
-
-    grad_shared = chips_sum(grad_shared, 0)
-    grad_shared = place_shared(meta, grad_shared, flip(grad_shared, 1))
-
-    keep, give = weight_grad(
-        meta, chip ^ shard_index, [([jnp.concatenate(mixed, axis=1)], [grad_branch[None]])], 0
-    )
-    came = flip(give, 1)
-    grad_out = line_reduce([keep[i] + came[i] for i in range(4)]).astype(bf16)
-    grad_out = chips_sum(grad_out, 0)
-    came = flip(grad_out, 1)
-    grad_out = jnp.where(
-        core == 0,
-        jnp.concatenate([grad_out, came], axis=0),
-        jnp.concatenate([came, grad_out], axis=0),
-    ).astype(f32)
-
-    sums = jnp.concatenate(
-        [grad_gain_in, grad_gain_mid, jnp.full((6, width), squared, f32)], axis=0
-    )
-    sums = everywhere_sum(sums)
-    own = lax.dynamic_slice_in_dim(sums, shard_index * shard_rows, shard_rows, 1)
-    loss_value = 0.5 * sums[2, 0] / (valid_count * width)
-
+            meta(), chip ^ shard_index, [([mixed], [have["grad_branch"][None]])], 0
+        )
+        clock.mark(keep)
+        came = flip(give, 1)
+        yield
+        yield from line_reduce_steps(keep, came)
+        total = have["line_sum"]
+        came = flip(total, 2)
+        yield
+        total = clock.mark(total + now(came))
+        came = flip(total, 4)
+        yield
+        mine = clock.mark(total + now(came))
+        other = flip(mine, 1)
+        yield
+        mine, other = now(mine, other)
+        have["grad_out"] = clock.mark(
+            jnp.where(
+                core == 0,
+                jnp.concatenate([mine, other], axis=0),
+                jnp.concatenate([other, mine], axis=0),
+            ).astype(f32)
+        )
+        yield
+
+    def qkv_grad_chain():
+        normed_in = have["normed_in"].reshape(4 * token_rows, width)
+        projected = have["grad_projected"].reshape(1, 4 * token_rows, -1)
+        keep, give = weight_grad(meta(), shard_index, [([normed_in], [projected])], 0)
+        clock.mark(keep)
+        came = flip(give, 1)
+        yield
+        yield from line_reduce_steps(keep, came)
+        own = have["line_sum"]
+        came = flip(own, 2)
+        yield
+        pair = clock.mark(jnp.stack([own, now(came)]))
+        came = flip(pair, 4)
+        yield
+        mine = clock.mark(jnp.concatenate([pair, now(came)]))
+        other = flip(mine, 1)
+        yield
+        have["grad_qkv"] = clock.mark(place_heads(meta(), [mine[r] for r in range(4)], other))
+        yield
+
+    early = {
+        "H": hidden_chain(),
+        "W": qkv_chain(),
+        "S": shared_chain(),
+        "O": out_chain(),
+        "K": small_chain(),
+        "R": qkv_all_chain(),
+        "M": main_chain(),
+    }
+    late = {
+        "L": states_chain(),
+        "S": shared_grad_chain(),
+        "O": out_grad_chain(),
+        "Q": qkv_grad_chain(),
+    }
+    if SUMMED:
+        late["A"] = summed_chain()
+    for expert in range(SUMMED, local_experts):
+        late[str(expert)] = expert_chain(expert)
+    for chains, order in ((early, EARLY), (late, LATE)):
+        for name in order:
+            next(chains[name], None)
+        for name in chains:
+            for _ in chains[name]:
+                pass
+
+    own, loss_value = have["sums"]
     return (
-        final_state.astype(bf16)[None],
+        have["final"],
         loss_value,
-        grad_hidden,
+        have["grad_hidden"],
         own[0],
-        grad_qkv,
-        grad_out,
+        have["grad_qkv"],
+        have["grad_out"],
         own[1],
-        grad_shared,
-        grad_experts,
+        have["grad_shared"],
+        have["grad_experts"],
     )
 
 

time: 931 us -> 853 us (0.916)
  waiting for transfers between devices: 350 us -> 310 us
  local copies, waits for them, and re-layouts: 66.5 us -> 38.9 us
  starting transfers between devices: 189 us -> 171 us
  other arithmetic: 48.4 us -> 63.1 us
    ppermute x26 -> x18, waiting for transfers between devices: 118 us -> 66.6 us  [line_swap(): lax.ppermute(value, 'wt', [(index, index ^ offset) for index in range(4)])]
    ppermute x107 -> x61, waiting for transfers between devices: 213 us -> 165 us  [flip(): lax.ppermute(value, 'ctx', [(index, index ^ bit) for index in range(8)])]
    ppermute x8, waiting for transfers between devices: 12.2 us -> 49.2 us  [line_inward(): return lax.ppermute(value, 'wt', [(0, 1), (3, 2)])]
    ppermute x107 -> x61, starting transfers between devices: 75 us -> 47.6 us  [flip(): lax.ppermute(value, 'ctx', [(index, index ^ bit) for index in range(8)])]
    ppermute x6, waiting for transfers between devices: 6.81 us -> 29 us  [line_outward(): return lax.ppermute(value, 'wt', [(1, 0), (2, 3)])]
    ppermute x26 -> x18, starting transfers between devices: 60.8 us -> 41.9 us  [line_swap(): lax.ppermute(value, 'wt', [(index, index ^ offset) for index in range(4)])]
    ppermute x8, starting transfers between devices: 30.6 us -> 45.8 us  [line_inward(): return lax.ppermute(value, 'wt', [(0, 1), (3, 2)])]
    ppermute x14, starting transfers between devices: 14.4 us -> 27.9 us  [line_middle(): return lax.ppermute(value, 'wt', [(1, 2), (2, 1)])]
  transfers between devices with their start and end apart: 161 -> 107, of which waited for: 60 -> 40; matrix products, arithmetic and copies ran while one was open for 7% -> 8% of each run, Pallas kernels for 25% -> 26%
where the time goes in v3:
time: 853 us; the launch traced here: 848 us
  waiting for transfers between devices  310 us (36%)
  Pallas kernels  259 us (30%)
  starting transfers between devices  171 us (20%)
  other arithmetic  63.1 us (7%)
  local copies, waits for them, and re-layouts  38.9 us (5%)
    pallas_call x23, Pallas kernels, call(): pl.pallas_call(kernel, grid_spec=pltpu.PrefetchScalarGridSpec(num_scalar_...  235 us
    ppermute x61, waiting for transfers between devices, flip(): lax.ppermute(value, 'ctx', [(index, index ^ bit) for index in range(8)])  165 us
    ppermute x18, waiting for transfers between devices, line_swap(): lax.ppermute(value, 'wt', [(index, index ^ offset) for index in range(4)])  66.6 us
    ppermute x8, waiting for transfers between devices, line_inward(): return lax.ppermute(value, 'wt', [(0, 1), (3, 2)])  49.2 us
    ppermute x61, starting transfers between devices, flip(): lax.ppermute(value, 'ctx', [(index, index ^ bit) for index in range(8)])  47.6 us
    ppermute x8, starting transfers between devices, line_inward(): return lax.ppermute(value, 'wt', [(0, 1), (3, 2)])  45.8 us
    ppermute x18, starting transfers between devices, line_swap(): lax.ppermute(value, 'wt', [(index, index ^ offset) for index in range(4)])  41.9 us
    ppermute x6, waiting for transfers between devices, line_outward(): return lax.ppermute(value, 'wt', [(1, 0), (2, 3)])  29 us
  transfers between devices with their start and end apart: 107, of which 40 were waited for; matrix products, arithmetic and copies ran while one was open for 8% of the time, Pallas kernels for 26%

profile of v3, /device:TPU:0, one launch (start us, length us, event | category | flops | bytes accessed | tf_op | source)
XLA Modules:
  0.0 847.6 jit_solution(15397956671644190232)
XLA Ops:
  21.7 12.4 %collective-permute-done.3 = f32[2,32,256]{2,1,0:T(8,128)S(1)} collective-permute-done((f32[2,32,256]{2,1,0:T(8,128)S(1)}, f32[2,32,256]{2,1,0:T(8,128)S(1)}, u32[]{:S(2)}, u32[]{:S(2)}) %collective-permute-start.3) | collective-permute-done | bytes 65568 | tf_op jit(solution)/shard_map/ppermute | solution.py:453
  34.8 9.7 %collective-permute-done.5 = bf16[2,192,640]{2,1,0:T(8,128)(2,1)S(1)} collective-permute-done((bf16[2,192,640]{2,1,0:T(8,128)(2,1)S(1)}, bf16[2,192,640]{2,1,0:T(8,128)(2,1)S(1)}, u32[]{:S(2)}, u32[]{:S(2)}) %collective-permute-start.5) | collective-permute-done | bytes 491552 | tf_op jit(solution)/shard_map/ppermute | solution.py:453
  50.0 15.7 %collective-permute-done.8.refs_3_ = bf16[256,1536]{1,0:T(8,128)(2,1)} collective-permute-done((bf16[256,1536]{1,0:T(8,128)(2,1)S(1)}, bf16[256,1536]{1,0:T(8,128)(2,1)}, u32[]{:S(2)}, u32[]{:S(2)}) %collective-permute-start.8) | collective-permute-done | bytes 786464 | tf_op jit(solution)/shard_map/ppermute | solution.py:449
  65.7 7.8 project.1
  77.1 19.3 %attend.1 = (bf16[256,384]{1,0:T(8,128)(2,1)S(1)}, bf16[256,384]{1,0:T(8,128)(2,1)S(1)}, bf16[256,384]{1,0:T(8,128)(2,1)S(1)}, bf16[256,384]{1,0:T(8,128)(2,1)S(1)}, f32[8,1,384]{2,1,0:T(1,128)S(1)}) custom-call(s32[2]{0:T(128)S(1)} %pad_add_fusion.meta, bf16[4,256,384]{2,1,0:T(8,128)(2,1)S(1)} %get-tuple-element.206.query_ref, ...), custom_call_target="tpu_custom_call" | custom-call | flops 161061280 | bytes 131686 | tf_op jit(solution)/shard_map/attend/pallas_call | solution.py:553
  99.9 16.0 %collective-permute-done.17 = bf16[192,1536]{1,0:T(8,128)(2,1)} collective-permute-done((bf16[192,1536]{1,0:T(8,128)(2,1)}, bf16[192,1536]{1,0:T(8,128)(2,1)}, u32[]{:S(2)}, u32[]{:S(2)}) %collective-permute-start.17) | collective-permute-done | bytes 589856 | tf_op jit(solution)/shard_map/ppermute | solution.py:461
  119.9 14.5 %collective-permute-done.12 = bf16[2,4,48,768]{3,2,1,0:T(8,128)(2,1)S(1)} collective-permute-done((bf16[2,4,48,768]{3,2,1,0:T(8,128)(2,1)S(1)}, bf16[2,4,48,768]{3,2,1,0:T(8,128)(2,1)S(1)}, u32[]{:S(2)}, u32[]{:S(2)}) %collective-permute-start.12) | collective-permute-done | bytes 589856 | tf_op jit(solution)/shard_map/ppermute | solution.py:449
  148.8 5.5 leave.1
  161.2 11.7 %experts.4 = (bf16[4,256,1024]{2,1,0:T(8,128)(2,1)S(1)}, bf16[256,512]{1,0:T(8,128)(2,1)S(1)}, bf16[256,1536]{1,0:T(8,128)(2,1)S(1)}) custom-call(s32[2]{0:T(128)S(1)} %pad_add_fusion.meta, bf16[256,1536]{1,0:T(8,128)(2,1)S(1)} %get-tuple-element.223.rows_ref.refs_0_.refs_16_, f32[4,256,1]{2,1,0:T(8,128)S(1)} %copy.39.gates_ref, ...), custom_call_target="tpu_custom_call" | custom-call | flops 271790912 | bytes 1258496 | tf_op jit(solution)/shard_map/experts/pallas_call | solution.py:553
  179.5 11.9 %experts.5 = (bf16[4,256,1024]{2,1,0:T(8,128)(2,1)S(1)}, bf16[256,512]{1,0:T(8,128)(2,1)S(1)}, bf16[256,1536]{1,0:T(8,128)(2,1)S(1)}) custom-call(s32[2]{0:T(128)S(1)} %pad_add_fusion.meta, bf16[256,1536]{1,0:T(8,128)(2,1)S(1)} %collective-permute-done.23.rows_ref.refs_1_.refs_17_, f32[4,256,1]{2,1,0:T(8,128)S(1)} %copy.40.gates_ref, ...), custom_call_target="tpu_custom_call" | custom-call | flops 271790912 | bytes 1258496 | tf_op jit(solution)/shard_map/experts/pallas_call | solution.py:553
  192.7 7.2 collective-permute-done.26
  205.2 11.7 %experts.6 = (bf16[4,256,1024]{2,1,0:T(8,128)(2,1)S(1)}, bf16[256,512]{1,0:T(8,128)(2,1)S(1)}, bf16[256,1536]{1,0:T(8,128)(2,1)S(1)}) custom-call(s32[2]{0:T(128)S(1)} %pad_add_fusion.meta, bf16[256,1536]{1,0:T(8,128)(2,1)S(1)} %broadcast_select_fusion.3.rows_ref.refs_2_.refs_18_, f32[4,256,1]{2,1,0:T(8,128)S(1)} %copy.41.gates_ref, ...), custom_call_target="tpu_custom_call" | custom-call | flops 271790912 | bytes 1258496 | tf_op jit(solution)/shard_map/experts/pallas_call | solution.py:553
  219.4 11.7 %experts.7 = (bf16[4,256,1024]{2,1,0:T(8,128)(2,1)S(1)}, bf16[256,512]{1,0:T(8,128)(2,1)S(1)}, bf16[256,1536]{1,0:T(8,128)(2,1)S(1)}) custom-call(s32[2]{0:T(128)S(1)} %pad_add_fusion.meta, bf16[256,1536]{1,0:T(8,128)(2,1)S(1)} %broadcast_select_fusion.2.rows_ref.refs_3_.refs_19_, f32[4,256,1]{2,1,0:T(8,128)S(1)} %copy.42.gates_ref, ...), custom_call_target="tpu_custom_call" | custom-call | flops 271790912 | bytes 1258496 | tf_op jit(solution)/shard_map/experts/pallas_call | solution.py:553
  239.7 13.3 %collective-permute-done.29 = bf16[256,1536]{1,0:T(8,128)(2,1)S(1)} collective-permute-done((bf16[256,1536]{1,0:T(8,128)(2,1)S(1)}, bf16[256,1536]{1,0:T(8,128)(2,1)S(1)}, u32[]{:S(2)}, u32[]{:S(2)}) %collective-permute-start.29) | collective-permute-done | bytes 786464 | tf_op jit(solution)/shard_map/ppermute | solution.py:465
  258.4 15.5 %collective-permute-done.32 = bf16[256,1536]{1,0:T(8,128)(2,1)S(1)} collective-permute-done((bf16[256,1536]{1,0:T(8,128)(2,1)S(1)}, bf16[256,1536]{1,0:T(8,128)(2,1)S(1)}, u32[]{:S(2)}, u32[]{:S(2)}) %collective-permute-start.32) | collective-permute-done | bytes 786464 | tf_op jit(solution)/shard_map/ppermute | solution.py:465
  281.0 40.9 %collective-permute-done.36 = f32[8,128]{1,0:T(8,128)S(1)} collective-permute-done((f32[8,128]{1,0:T(8,128)S(1)}, f32[8,128]{1,0:T(8,128)S(1)}, u32[]{:S(2)}, u32[]{:S(2)}) %collective-permute-start.36) | collective-permute-done | bytes 4128 | tf_op jit(solution)/shard_map/ppermute | solution.py:449
  328.5 12.7 %collective-permute-start.38 = (bf16[256,1536]{1,0:T(8,128)(2,1)S(1)}, bf16[256,1536]{1,0:T(8,128)(2,1)}, u32[]{:S(2)}, u32[]{:S(2)}) collective-permute-start(bf16[256,1536]{1,0:T(8,128)(2,1)S(1)} %get-tuple-element.391.grad_ref.refs_8_.refs_24_), channel_id=1, source_target_pairs={{1,2},{2,1},{5,6},{6,5},{9,10},{10,9},{13,14},{14,13},{17,18},{18,... | collective-permute-start | bytes 2359304 | tf_op jit(solution)/shard_map/ppermute | solution.py:457
  343.5 13.0 %experts_back.4 = (bf16[4,256,1024]{2,1,0:T(8,128)(2,1)S(1)}, bf16[4,256,512]{2,1,0:T(8,128)(2,1)S(1)}, bf16[1,256,512]{2,1,0:T(8,128)(2,1)S(1)}, bf16[1,256,256]{2,1,0:T(8,128)(2,1)S(1)}, bf16[256,1536]{1,0:T(8,128)(2,1)S(1)}) custom-call(s32[2]{0:T(128)S(1)} %pad_add_fusion.meta, bf16[256,1536]{1,0:T(8,128)(2,1)S(1)} %get-tuple-element.391.grad_ref.refs_8_.refs_24_, ...), custom_call_target="tpu_custom_call" | custom-call | flops 271790912 | bytes 1435443 | tf_op jit(solution)/shard_map/experts_back/pallas_call | solution.py:553
  360.9 13.0 %experts_back.5 = (bf16[4,256,1024]{2,1,0:T(8,128)(2,1)S(1)}, bf16[4,256,512]{2,1,0:T(8,128)(2,1)S(1)}, bf16[1,256,512]{2,1,0:T(8,128)(2,1)S(1)}, bf16[1,256,256]{2,1,0:T(8,128)(2,1)S(1)}, bf16[256,1536]{1,0:T(8,128)(2,1)S(1)}) custom-call(s32[2]{0:T(128)S(1)} %pad_add_fusion.meta, bf16[256,1536]{1,0:T(8,128)(2,1)S(1)} %collective-permute-done.37.grad_ref.refs_9_.refs_25_, ...), custom_call_target="tpu_custom_call" | custom-call | flops 271790912 | bytes 1435443 | tf_op jit(solution)/shard_map/experts_back/pallas_call | solution.py:553
  379.8 13.0 %experts_back.6 = (bf16[4,256,1024]{2,1,0:T(8,128)(2,1)S(1)}, bf16[4,256,512]{2,1,0:T(8,128)(2,1)S(1)}, bf16[1,256,512]{2,1,0:T(8,128)(2,1)S(1)}, bf16[1,256,256]{2,1,0:T(8,128)(2,1)S(1)}, bf16[256,1536]{1,0:T(8,128)(2,1)S(1)}) custom-call(s32[2]{0:T(128)S(1)} %pad_add_fusion.meta, bf16[256,1536]{1,0:T(8,128)(2,1)S(1)} %broadcast_select_fusion.1.grad_ref.refs_10_.refs_26_, ...), custom_call_target="tpu_custom_call" | custom-call | flops 271790912 | bytes 1435443 | tf_op jit(solution)/shard_map/experts_back/pallas_call | solution.py:553
  396.1 13.0 %experts_back.7 = (bf16[4,256,1024]{2,1,0:T(8,128)(2,1)S(1)}, bf16[4,256,512]{2,1,0:T(8,128)(2,1)S(1)}, bf16[1,256,512]{2,1,0:T(8,128)(2,1)S(1)}, bf16[1,256,256]{2,1,0:T(8,128)(2,1)S(1)}, bf16[256,1536]{1,0:T(8,128)(2,1)S(1)}) custom-call(s32[2]{0:T(128)S(1)} %pad_add_fusion.meta, bf16[256,1536]{1,0:T(8,128)(2,1)S(1)} %broadcast_select_fusion.grad_ref.refs_11_.refs_27_, ...), custom_call_target="tpu_custom_call" | custom-call | flops 271790912 | bytes 1435443 | tf_op jit(solution)/shard_map/experts_back/pallas_call | solution.py:553
  411.6 10.5 %weight_grad.6 = (bf16[4,192,1536]{2,1,0:T(8,128)(2,1)}, bf16[4,192,1536]{2,1,0:T(8,128)(2,1)}) custom-call(s32[2]{0:T(128)S(1)} %pad_add_fusion.1.meta, bf16[256,1536]{1,0:T(8,128)(2,1)S(1)} %get-tuple-element.223.rows_ref.refs_0_.refs_16_, bf16[256,1536]{1,0:T(8,128)(2,1)S(1)} %collective-permute-done.23.rows_ref.refs_1_.refs_17_, ...), custom_call_target="tpu_custom_call" | custom-call | flops 241591904 | bytes 707788 | tf_op jit(solution)/shard_map/weight_grad/pallas_call | solution.py:553
  422.2 14.6 %weight_grad.7 = (bf16[4,192,2304]{2,1,0:T(8,128)(2,1)}, bf16[4,192,2304]{2,1,0:T(8,128)(2,1)}) custom-call(s32[2]{0:T(128)S(1)} %pad_add_fusion.2.meta, bf16[256,1536]{1,0:T(8,128)(2,1)S(1)} %get-tuple-element.223.rows_ref.refs_0_.refs_16_, bf16[256,1536]{1,0:T(8,128)(2,1)S(1)} %collective-permute-done.23.rows_ref.refs_1_.refs_17_, ...), custom_call_target="tpu_custom_call" | custom-call | flops 362387872 | bytes 904396 | tf_op jit(solution)/shard_map/weight_grad/pallas_call | solution.py:553
  440.8 10.7 %weight_grad.8 = (bf16[4,192,1536]{2,1,0:T(8,128)(2,1)}, bf16[4,192,1536]{2,1,0:T(8,128)(2,1)}) custom-call(s32[2]{0:T(128)S(1)} %pad_add_fusion.3.meta, bf16[256,1536]{1,0:T(8,128)(2,1)S(1)} %get-tuple-element.223.rows_ref.refs_0_.refs_16_, bf16[256,1536]{1,0:T(8,128)(2,1)S(1)} %collective-permute-done.23.rows_ref.refs_1_.refs_17_, ...), custom_call_target="tpu_custom_call" | custom-call | flops 241591904 | bytes 707788 | tf_op jit(solution)/shard_map/weight_grad/pallas_call | solution.py:553
  451.6 5.9 collective-permute-start.45
  461.7 12.8 %collective-permute-done.45 = bf16[256,1536]{1,0:T(8,128)(2,1)S(1)} collective-permute-done((bf16[256,1536]{1,0:T(8,128)(2,1)S(1)}, bf16[256,1536]{1,0:T(8,128)(2,1)S(1)}, u32[]{:S(2)}, u32[]{:S(2)}) %collective-permute-start.45) | collective-permute-done | bytes 786464 | tf_op jit(solution)/shard_map/ppermute | solution.py:465
  477.4 10.5 %weight_grad.9 = (bf16[4,192,1536]{2,1,0:T(8,128)(2,1)}, bf16[4,192,1536]{2,1,0:T(8,128)(2,1)}) custom-call(s32[2]{0:T(128)S(1)} %pad_add_fusion.4.meta, bf16[256,1536]{1,0:T(8,128)(2,1)S(1)} %get-tuple-element.223.rows_ref.refs_0_.refs_16_, bf16[256,1536]{1,0:T(8,128)(2,1)S(1)} %collective-permute-done.23.rows_ref.refs_1_.refs_17_, ...), custom_call_target="tpu_custom_call" | custom-call | flops 241591904 | bytes 707788 | tf_op jit(solution)/shard_map/weight_grad/pallas_call | solution.py:553
  498.1 18.5 %collective-permute-done.50 = bf16[2,192,1536]{2,1,0:T(8,128)(2,1)} collective-permute-done((bf16[2,192,1536]{2,1,0:T(8,128)(2,1)}, bf16[2,192,1536]{2,1,0:T(8,128)(2,1)}, u32[]{:S(2)}, u32[]{:S(2)}) %collective-permute-start.50) | collective-permute-done | bytes 1179680 | tf_op jit(solution)/shard_map/ppermute | solution.py:449
  530.1 10.9 %collective-permute-done.56 = bf16[256,1536]{1,0:T(8,128)(2,1)S(1)} collective-permute-done((bf16[256,1536]{1,0:T(8,128)(2,1)S(1)}, bf16[256,1536]{1,0:T(8,128)(2,1)S(1)}, u32[]{:S(2)}, u32[]{:S(2)}) %collective-permute-start.56) | collective-permute-done | bytes 786464 | tf_op jit(solution)/shard_map/ppermute | solution.py:453
  542.5 6.3 enter_back.1
  560.9 11.2 %collective-permute-done.53 = bf16[192,1536]{1,0:T(8,128)(2,1)S(1)} collective-permute-done((bf16[192,1536]{1,0:T(8,128)(2,1)S(1)}, bf16[192,1536]{1,0:T(8,128)(2,1)S(1)}, u32[]{:S(2)}, u32[]{:S(2)}) %collective-permute-start.53) | collective-permute-done | bytes 589856 | tf_op jit(solution)/shard_map/ppermute | solution.py:449
  572.2 12.0 %collective-permute-done.51 = bf16[2,192,1536]{2,1,0:T(8,128)(2,1)S(1)} collective-permute-done((bf16[2,192,1536]{2,1,0:T(8,128)(2,1)S(1)}, bf16[2,192,1536]{2,1,0:T(8,128)(2,1)S(1)}, u32[]{:S(2)}, u32[]{:S(2)}) %collective-permute-start.51) | collective-permute-done | bytes 1179680 | tf_op jit(solution)/shard_map/ppermute | solution.py:449
  585.3 8.0 collective-permute-start.62
  608.4 20.5 %attend_back.1 = (bf16[4,256,384]{2,1,0:T(8,128)(2,1)S(1)}, f32[4,256,256]{2,1,0:T(8,128)S(1)}, bf16[4,256,256]{2,1,0:T(8,128)(2,1)S(1)}) custom-call(s32[2]{0:T(128)S(1)} %pad_add_fusion.meta, bf16[4,256,384]{2,1,0:T(8,128)(2,1)S(1)} %copy-done.31, bf16[4,256,256]{2,1,0:T(8,128)(2,1)S(1)} %copy-done.38, bf16[4,256,256]{2,1,0:T(8,128)(2,1)S(1)} %copy-done.40, ...), custom_call_target="tpu_custom_call" | custom-call | flops 402653184 | bytes 288972 | tf_op jit(solution)/shard_map/attend_back/pallas_call | solution.py:553
  632.1 6.0 collective-permute-start.70
  649.5 7.0 collective-permute-done.75
  657.7 6.3 collective-permute-start.72
  668.0 9.5 %collective-permute-done.72 = bf16[192,1536]{1,0:T(8,128)(2,1)S(1)} collective-permute-done((bf16[192,1536]{1,0:T(8,128)(2,1)S(1)}, bf16[192,1536]{1,0:T(8,128)(2,1)S(1)}, u32[]{:S(2)}, u32[]{:S(2)}) %collective-permute-start.72) | collective-permute-done | bytes 589856 | tf_op jit(solution)/shard_map/ppermute | solution.py:453
  684.9 6.3 weight_grad.11
  698.9 6.3 place_expert.5.refs_0_
  707.5 8.1 collective-permute-done.68.refs_3_
  718.2 6.1 collective-permute-start.87
  730.4 8.5 finish.1
  782.2 6.3 place_expert.6.refs_0_
  788.5 6.8 place_expert.7
  812.2 10.6 %collective-permute-done.102 = bf16[192,768]{1,0:T(8,128)(2,1)S(1)} collective-permute-done((bf16[192,768]{1,0:T(8,128)(2,1)S(1)}, bf16[192,768]{1,0:T(8,128)(2,1)S(1)}, u32[]{:S(2)}, u32[]{:S(2)}) %collective-permute-start.102) | collective-permute-done | bytes 294944 | tf_op jit(solution)/shard_map/ppermute | solution.py:453
  823.0 6.1 collective-permute-start.100
  840.7 5.5 place_shared.1
  (556 shorter events, 300.3 us)
Async XLA Ops:
  0.7 45.1 %collective-permute-start.6 = (bf16[256,1536]{1,0:T(8,128)(2,1)}, bf16[256,1536]{1,0:T(8,128)(2,1)}, u32[]{:S(2)}, u32[]{:S(2)}) collective-permute-start(bf16[256,1536]{1,0:T(8,128)(2,1)} %bitcast.163), channel_id=1, source_target_pairs={{0,8},{4,12},{8,0},{12,4},{16,24},{20,28},{24,16},{28,20},{1,9},{5... | collective-permute-start | bytes 2359304 | tf_op jit(solution)/shard_map/ppermute | solution.py:449
  3.7 44.9 %collective-permute-start.7 = (bf16[256,1536]{1,0:T(8,128)(2,1)}, bf16[256,1536]{1,0:T(8,128)(2,1)}, u32[]{:S(2)}, u32[]{:S(2)}) collective-permute-start(bf16[256,1536]{1,0:T(8,128)(2,1)} %bitcast.164), channel_id=1, source_target_pairs={{0,16},{4,20},{8,24},{12,28},{16,0},{20,4},{24,8},{28,12},{1,17},{... | collective-permute-start | bytes 2359304 | tf_op jit(solution)/shard_map/ppermute | solution.py:449
  20.5 24.0 %collective-permute-start.5 = (bf16[2,192,640]{2,1,0:T(8,128)(2,1)S(1)}, bf16[2,192,640]{2,1,0:T(8,128)(2,1)S(1)}, u32[]{:S(2)}, u32[]{:S(2)}) collective-permute-start(bf16[2,192,640]{2,1,0:T(8,128)(2,1)S(1)} %pad_maximum_fusion.18), channel_id=1, source_target_pairs={{0,2},{1,3},{2,0},{3,1},{4,6},{5,7},{6,4},{7,5},{8,10},{9,11},{10,... | collective-permute-start | bytes 1474568 | tf_op jit(solution)/shard_map/ppermute | solution.py:453
  45.4 28.2 %collective-permute-start.13 = (bf16[192,1536]{1,0:T(8,128)(2,1)S(1)}, bf16[192,1536]{1,0:T(8,128)(2,1)S(1)}, u32[]{:S(2)}, u32[]{:S(2)}) collective-permute-start(bf16[192,1536]{1,0:T(8,128)(2,1)S(1)} %constant_dynamic-slice_fusion.6.refs_4_), channel_id=1, source_target_pairs={{0,1},{1,0},{2,3},{3,2},{4,5},{5,4},{6,7},{7,6},{8,9},{9,8},{10,11... | collective-permute-start | bytes 1769480 | tf_op jit(solution)/shard_map/ppermute | solution.py:453
  45.7 29.4 %collective-permute-start.4 = (bf16[2,48,768]{2,1,0:T(8,128)(2,1)}, bf16[2,48,768]{2,1,0:T(8,128)(2,1)S(1)}, u32[]{:S(2)}, u32[]{:S(2)}) collective-permute-start(bf16[2,48,768]{2,1,0:T(8,128)(2,1)} %pad_maximum_fusion.24), channel_id=1, source_target_pairs={{0,2},{1,3},{2,0},{3,1},{4,6},{5,7},{6,4},{7,5},{8,10},{9,11},{10,... | collective-permute-start | bytes 442376 | tf_op jit(solution)/shard_map/ppermute | solution.py:453
  48.5 27.3 %collective-permute-start.14 = (bf16[192,1536]{1,0:T(8,128)(2,1)S(1)}, bf16[192,1536]{1,0:T(8,128)(2,1)}, u32[]{:S(2)}, u32[]{:S(2)}) collective-permute-start(bf16[192,1536]{1,0:T(8,128)(2,1)S(1)} %constant_dynamic-slice_fusion.6.refs_4_), channel_id=1, source_target_pairs={{1,2},{2,1},{5,6},{6,5},{9,10},{10,9},{13,14},{14,13},{17,18},{18,... | collective-permute-start | bytes 1769480 | tf_op jit(solution)/shard_map/ppermute | solution.py:457
  73.6 23.8 %collective-permute-start.16 = (bf16[192,1536]{1,0:T(8,128)(2,1)S(1)}, bf16[192,1536]{1,0:T(8,128)(2,1)}, u32[]{:S(2)}, u32[]{:S(2)}) collective-permute-start(bf16[192,1536]{1,0:T(8,128)(2,1)S(1)} %collective-permute-done.13.refs_5_), channel_id=1, source_target_pairs={{1,2},{2,1},{5,6},{6,5},{9,10},{10,9},{13,14},{14,13},{17,18},{18,... | collective-permute-start | bytes 1769480 | tf_op jit(solution)/shard_map/ppermute | solution.py:457
  75.8 24.1 %collective-permute-start.15 = (bf16[192,1536]{1,0:T(8,128)(2,1)}, bf16[192,1536]{1,0:T(8,128)(2,1)}, u32[]{:S(2)}, u32[]{:S(2)}) collective-permute-start(bf16[192,1536]{1,0:T(8,128)(2,1)} %collective-permute-done.14), channel_id=1, source_target_pairs={{1,0},{2,3},{5,4},{6,7},{9,8},{10,11},{13,12},{14,15},{17,16},{18,... | collective-permute-start | bytes 1769480 | tf_op jit(solution)/shard_map/ppermute | solution.py:461
  118.6 28.8 %collective-permute-start.21 = (bf16[4,192,1536]{2,1,0:T(8,128)(2,1)S(1)}, bf16[4,192,1536]{2,1,0:T(8,128)(2,1)S(1)}, u32[]{:S(2)}, u32[]{:S(2)}) collective-permute-start(bf16[4,192,1536]{2,1,0:T(8,128)(2,1)S(1)} %pad_maximum_fusion.2), channel_id=1, source_target_pairs={{0,4},{4,0},{8,12},{12,8},{16,20},{20,16},{24,28},{28,24},{1,5},{5... | collective-permute-start | bytes 7077896 | tf_op jit(solution)/shard_map/ppermute | solution.py:449
  134.5 22.5 %collective-permute-start.22 = (bf16[4,4,48,768]{3,2,1,0:T(8,128)(2,1)S(1)}, bf16[4,4,48,768]{3,2,1,0:T(8,128)(2,1)}, u32[]{:S(2)}, u32[]{:S(2)}) collective-permute-start(bf16[4,4,48,768]{3,2,1,0:T(8,128)(2,1)S(1)} %pad_maximum_fusion.9.mine), channel_id=1, source_target_pairs={{0,4},{4,0},{8,12},{12,8},{16,20},{20,16},{24,28},{28,24},{1,5},{5... | collective-permute-start | bytes 3538952 | tf_op jit(solution)/shard_map/ppermute | solution.py:449
  177.4 22.5 %collective-permute-start.26 = (bf16[256,1536]{1,0:T(8,128)(2,1)}, bf16[256,1536]{1,0:T(8,128)(2,1)}, u32[]{:S(2)}, u32[]{:S(2)}) collective-permute-start(bf16[256,1536]{1,0:T(8,128)(2,1)} %collective-permute-done.24), channel_id=1, source_target_pairs={{1,0},{2,3},{5,4},{6,7},{9,8},{10,11},{13,12},{14,15},{17,16},{18,... | collective-permute-start | bytes 2359304 | tf_op jit(solution)/shard_map/ppermute | solution.py:461
  203.4 34.2 %collective-permute-start.31 = (bf16[768,640]{1,0:T(8,128)(2,1)S(1)}, bf16[768,640]{1,0:T(8,128)(2,1)S(1)}, u32[]{:S(2)}, u32[]{:S(2)}) collective-permute-start(bf16[768,640]{1,0:T(8,128)(2,1)S(1)} %constant_dynamic-slice_fusion.1), channel_id=1, source_target_pairs={{0,8},{4,12},{8,0},{12,4},{16,24},{20,28},{24,16},{28,20},{1,9},{5... | collective-permute-start | bytes 2949128 | tf_op jit(solution)/shard_map/ppermute | solution.py:449
  274.2 49.1 %collective-permute-start.34 = (bf16[256,1536]{1,0:T(8,128)(2,1)S(1)}, bf16[256,1536]{1,0:T(8,128)(2,1)S(1)}, u32[]{:S(2)}, u32[]{:S(2)}) collective-permute-start(bf16[256,1536]{1,0:T(8,128)(2,1)S(1)} %add.312), channel_id=1, source_target_pairs={{0,1},{1,0},{2,3},{3,2},{4,5},{5,4},{6,7},{7,6},{8,9},{9,8},{10,11... | collective-permute-start | bytes 2359304 | tf_op jit(solution)/shard_map/ppermute | solution.py:453
  278.2 45.1 %collective-permute-start.35 = (bf16[256,1536]{1,0:T(8,128)(2,1)S(1)}, bf16[256,1536]{1,0:T(8,128)(2,1)S(1)}, u32[]{:S(2)}, u32[]{:S(2)}) collective-permute-start(bf16[256,1536]{1,0:T(8,128)(2,1)S(1)} %add.313), channel_id=1, source_target_pairs={{1,2},{2,1},{5,6},{6,5},{9,10},{10,9},{13,14},{14,13},{17,18},{18,... | collective-permute-start | bytes 2359304 | tf_op jit(solution)/shard_map/ppermute | solution.py:457
  278.9 62.4 %collective-permute-start.39 = (bf16[2,768,640]{2,1,0:T(8,128)(2,1)S(1)}, bf16[2,768,640]{2,1,0:T(8,128)(2,1)S(1)}, u32[]{:S(2)}, u32[]{:S(2)}) collective-permute-start(bf16[2,768,640]{2,1,0:T(8,128)(2,1)S(1)} %pad_maximum_fusion.7), channel_id=1, source_target_pairs={{0,16},{4,20},{8,24},{12,28},{16,0},{20,4},{24,8},{28,12},{1,17},{... | collective-permute-start | bytes 5898248 | tf_op jit(solution)/shard_map/ppermute | solution.py:449
  280.5 41.5 %collective-permute-start.36 = (f32[8,128]{1,0:T(8,128)S(1)}, f32[8,128]{1,0:T(8,128)S(1)}, u32[]{:S(2)}, u32[]{:S(2)}) collective-permute-start(f32[8,128]{1,0:T(8,128)S(1)} %add.310), channel_id=1, source_target_pairs={{0,16},{4,20},{8,24},{12,28},{16,0},{20,4},{24,8},{28,12},{1,17},{... | collective-permute-start | bytes 12296 | tf_op jit(solution)/shard_map/ppermute | solution.py:449
  325.9 31.9 %collective-permute-start.37 = (bf16[256,1536]{1,0:T(8,128)(2,1)S(1)}, bf16[256,1536]{1,0:T(8,128)(2,1)S(1)}, u32[]{:S(2)}, u32[]{:S(2)}) collective-permute-start(bf16[256,1536]{1,0:T(8,128)(2,1)S(1)} %get-tuple-element.391.grad_ref.refs_8_.refs_24_), channel_id=1, source_target_pairs={{0,1},{1,0},{2,3},{3,2},{4,5},{5,4},{6,7},{7,6},{8,9},{9,8},{10,11... | collective-permute-start | bytes 2359304 | tf_op jit(solution)/shard_map/ppermute | solution.py:453
  328.5 29.3 %collective-permute-start.38 = (bf16[256,1536]{1,0:T(8,128)(2,1)S(1)}, bf16[256,1536]{1,0:T(8,128)(2,1)}, u32[]{:S(2)}, u32[]{:S(2)}) collective-permute-start(bf16[256,1536]{1,0:T(8,128)(2,1)S(1)} %get-tuple-element.391.grad_ref.refs_8_.refs_24_), channel_id=1, source_target_pairs={{1,2},{2,1},{5,6},{6,5},{9,10},{10,9},{13,14},{14,13},{17,18},{18,... | collective-permute-start | bytes 2359304 | tf_op jit(solution)/shard_map/ppermute | solution.py:457
  451.6 24.0 %collective-permute-start.44 = (bf16[4,192,1536]{2,1,0:T(8,128)(2,1)}, bf16[4,192,1536]{2,1,0:T(8,128)(2,1)S(1)}, u32[]{:S(2)}, u32[]{:S(2)}) collective-permute-start(bf16[4,192,1536]{2,1,0:T(8,128)(2,1)} %get-tuple-element.296), channel_id=1, source_target_pairs={{0,4},{4,0},{8,12},{12,8},{16,20},{20,16},{24,28},{28,24},{1,5},{5... | collective-permute-start | bytes 7077896 | tf_op jit(solution)/shard_map/ppermute | solution.py:449
  451.6 22.9 %collective-permute-start.45 = (bf16[256,1536]{1,0:T(8,128)(2,1)S(1)}, bf16[256,1536]{1,0:T(8,128)(2,1)S(1)}, u32[]{:S(2)}, u32[]{:S(2)}) collective-permute-start(bf16[256,1536]{1,0:T(8,128)(2,1)S(1)} %get-tuple-element.271), channel_id=1, source_target_pairs={{0,1},{3,2},{4,5},{7,6},{8,9},{11,10},{12,13},{15,14},{16,17},{19,... | collective-permute-start | bytes 2359304 | tf_op jit(solution)/shard_map/ppermute | solution.py:465
  487.9 37.5 %collective-permute-start.47 = (bf16[4,192,1536]{2,1,0:T(8,128)(2,1)}, bf16[4,192,1536]{2,1,0:T(8,128)(2,1)}, u32[]{:S(2)}, u32[]{:S(2)}) collective-permute-start(bf16[4,192,1536]{2,1,0:T(8,128)(2,1)} %get-tuple-element.303), channel_id=1, source_target_pairs={{0,4},{4,0},{8,12},{12,8},{16,20},{20,16},{24,28},{28,24},{1,5},{5... | collective-permute-start | bytes 7077896 | tf_op jit(solution)/shard_map/ppermute | solution.py:449
  487.9 28.7 %collective-permute-start.50 = (bf16[2,192,1536]{2,1,0:T(8,128)(2,1)}, bf16[2,192,1536]{2,1,0:T(8,128)(2,1)}, u32[]{:S(2)}, u32[]{:S(2)}) collective-permute-start(bf16[2,192,1536]{2,1,0:T(8,128)(2,1)} %get-tuple-element.400), channel_id=1, source_target_pairs={{0,8},{4,12},{8,0},{12,4},{16,24},{20,28},{24,16},{28,20},{1,9},{5... | collective-permute-start | bytes 3538952 | tf_op jit(solution)/shard_map/ppermute | solution.py:449
  489.5 30.0 %collective-permute-start.48 = (bf16[256,1536]{1,0:T(8,128)(2,1)}, bf16[256,1536]{1,0:T(8,128)(2,1)}, u32[]{:S(2)}, u32[]{:S(2)}) collective-permute-start(bf16[256,1536]{1,0:T(8,128)(2,1)} %add.319), channel_id=1, source_target_pairs={{0,1},{3,2},{4,5},{7,6},{8,9},{11,10},{12,13},{15,14},{16,17},{19,... | collective-permute-start | bytes 2359304 | tf_op jit(solution)/shard_map/ppermute | solution.py:465
  494.8 25.4 %collective-permute-start.49 = (bf16[256,1536]{1,0:T(8,128)(2,1)}, bf16[256,1536]{1,0:T(8,128)(2,1)}, u32[]{:S(2)}, u32[]{:S(2)}) collective-permute-start(bf16[256,1536]{1,0:T(8,128)(2,1)} %add.319), channel_id=1, source_target_pairs={{1,2},{2,1},{5,6},{6,5},{9,10},{10,9},{13,14},{14,13},{17,18},{18,... | collective-permute-start | bytes 2359304 | tf_op jit(solution)/shard_map/ppermute | solution.py:457
  496.4 32.8 %collective-permute-start.52 = (bf16[2,192,1536]{2,1,0:T(8,128)(2,1)}, bf16[2,192,1536]{2,1,0:T(8,128)(2,1)S(1)}, u32[]{:S(2)}, u32[]{:S(2)}) collective-permute-start(bf16[2,192,1536]{2,1,0:T(8,128)(2,1)} %get-tuple-element.398), channel_id=1, source_target_pairs={{0,16},{4,20},{8,24},{12,28},{16,0},{20,4},{24,8},{28,12},{1,17},{... | collective-permute-start | bytes 3538952 | tf_op jit(solution)/shard_map/ppermute | solution.py:449
  516.6 42.1 %collective-permute-start.54 = (bf16[2,192,2304]{2,1,0:T(8,128)(2,1)}, bf16[2,192,2304]{2,1,0:T(8,128)(2,1)}, u32[]{:S(2)}, u32[]{:S(2)}) collective-permute-start(bf16[2,192,2304]{2,1,0:T(8,128)(2,1)} %get-tuple-element.394), channel_id=1, source_target_pairs={{0,8},{4,12},{8,0},{12,4},{16,24},{20,28},{24,16},{28,20},{1,9},{5... | collective-permute-start | bytes 5308424 | tf_op jit(solution)/shard_map/ppermute | solution.py:449
  519.5 29.2 %collective-permute-start.55 = (bf16[192,1536]{1,0:T(8,128)(2,1)S(1)}, bf16[192,1536]{1,0:T(8,128)(2,1)S(1)}, u32[]{:S(2)}, u32[]{:S(2)}) collective-permute-start(bf16[192,1536]{1,0:T(8,128)(2,1)S(1)} %fusion.16), channel_id=1, source_target_pairs={{0,16},{4,20},{8,24},{12,28},{16,0},{20,4},{24,8},{28,12},{1,17},{... | collective-permute-start | bytes 1769480 | tf_op jit(solution)/shard_map/ppermute | solution.py:449
  555.4 29.9 %collective-permute-start.61 = (bf16[4,192,1536]{2,1,0:T(8,128)(2,1)}, bf16[4,192,1536]{2,1,0:T(8,128)(2,1)S(1)}, u32[]{:S(2)}, u32[]{:S(2)}) collective-permute-start(bf16[4,192,1536]{2,1,0:T(8,128)(2,1)} %get-tuple-element.320), channel_id=1, source_target_pairs={{0,4},{4,0},{8,12},{12,8},{16,20},{20,16},{24,28},{28,24},{1,5},{5... | collective-permute-start | bytes 7077896 | tf_op jit(solution)/shard_map/ppermute | solution.py:449
  555.4 28.8 %collective-permute-start.51 = (bf16[2,192,1536]{2,1,0:T(8,128)(2,1)S(1)}, bf16[2,192,1536]{2,1,0:T(8,128)(2,1)S(1)}, u32[]{:S(2)}, u32[]{:S(2)}) collective-permute-start(bf16[2,192,1536]{2,1,0:T(8,128)(2,1)S(1)} %copy-done.93), channel_id=1, source_target_pairs={{0,16},{4,20},{8,24},{12,28},{16,0},{20,4},{24,8},{28,12},{1,17},{... | collective-permute-start | bytes 3538952 | tf_op jit(solution)/shard_map/ppermute | solution.py:449
  557.4 71.6 %collective-permute-start.63 = (bf16[192,1536]{1,0:T(8,128)(2,1)S(1)}, bf16[192,1536]{1,0:T(8,128)(2,1)S(1)}, u32[]{:S(2)}, u32[]{:S(2)}) collective-permute-start(bf16[192,1536]{1,0:T(8,128)(2,1)S(1)} %fusion.10.refs_0_), channel_id=1, source_target_pairs={{0,16},{4,20},{8,24},{12,28},{16,0},{20,4},{24,8},{28,12},{1,17},{... | collective-permute-start | bytes 1769480 | tf_op jit(solution)/shard_map/ppermute | solution.py:449
  585.3 44.6 %collective-permute-start.62 = (bf16[192,1536]{1,0:T(8,128)(2,1)S(1)}, bf16[192,1536]{1,0:T(8,128)(2,1)}, u32[]{:S(2)}, u32[]{:S(2)}) collective-permute-start(bf16[192,1536]{1,0:T(8,128)(2,1)S(1)} %add_bitcast_fusion), channel_id=1, source_target_pairs={{0,1},{3,2},{4,5},{7,6},{8,9},{11,10},{12,13},{15,14},{16,17},{19,... | collective-permute-start | bytes 1769480 | tf_op jit(solution)/shard_map/ppermute | solution.py:465
  601.1 38.0 %collective-permute-start.59 = (bf16[192,2304]{1,0:T(8,128)(2,1)}, bf16[192,2304]{1,0:T(8,128)(2,1)S(1)}, u32[]{:S(2)}, u32[]{:S(2)}) collective-permute-start(bf16[192,2304]{1,0:T(8,128)(2,1)} %fusion.7), channel_id=1, source_target_pairs={{0,16},{4,20},{8,24},{12,28},{16,0},{20,4},{24,8},{28,12},{1,17},{... | collective-permute-start | bytes 2654216 | tf_op jit(solution)/shard_map/ppermute | solution.py:449
  606.4 31.7 %collective-permute-start.60 = (bf16[192,1536]{1,0:T(8,128)(2,1)S(1)}, bf16[192,1536]{1,0:T(8,128)(2,1)S(1)}, u32[]{:S(2)}, u32[]{:S(2)}) collective-permute-start(bf16[192,1536]{1,0:T(8,128)(2,1)S(1)} %fusion.13.refs_1_), channel_id=1, source_target_pairs={{0,8},{4,12},{8,0},{12,4},{16,24},{20,28},{24,16},{28,20},{1,9},{5... | collective-permute-start | bytes 1769480 | tf_op jit(solution)/shard_map/ppermute | solution.py:449
  607.2 35.7 %collective-permute-start.58 = (bf16[192,1536]{1,0:T(8,128)(2,1)S(1)}, bf16[192,1536]{1,0:T(8,128)(2,1)}, u32[]{:S(2)}, u32[]{:S(2)}) collective-permute-start(bf16[192,1536]{1,0:T(8,128)(2,1)S(1)} %fusion.8), channel_id=1, source_target_pairs={{0,8},{4,12},{8,0},{12,4},{16,24},{20,28},{24,16},{28,20},{1,9},{5... | collective-permute-start | bytes 1769480 | tf_op jit(solution)/shard_map/ppermute | solution.py:449
  629.1 27.5 %collective-permute-start.75 = (bf16[2,192,1536]{2,1,0:T(8,128)(2,1)S(1)}, bf16[2,192,1536]{2,1,0:T(8,128)(2,1)S(1)}, u32[]{:S(2)}, u32[]{:S(2)}) collective-permute-start(bf16[2,192,1536]{2,1,0:T(8,128)(2,1)S(1)} %pad_maximum_fusion.10), channel_id=1, source_target_pairs={{0,8},{4,12},{8,0},{12,4},{16,24},{20,28},{24,16},{28,20},{1,9},{5... | collective-permute-start | bytes 3538952 | tf_op jit(solution)/shard_map/ppermute | solution.py:449
  640.0 26.2 %collective-permute-start.74 = (bf16[2,192,1536]{2,1,0:T(8,128)(2,1)S(1)}, bf16[2,192,1536]{2,1,0:T(8,128)(2,1)S(1)}, u32[]{:S(2)}, u32[]{:S(2)}) collective-permute-start(bf16[2,192,1536]{2,1,0:T(8,128)(2,1)S(1)} %pad_maximum_fusion.11), channel_id=1, source_target_pairs={{0,16},{4,20},{8,24},{12,28},{16,0},{20,4},{24,8},{28,12},{1,17},{... | collective-permute-start | bytes 3538952 | tf_op jit(solution)/shard_map/ppermute | solution.py:449
  657.0 23.2 %collective-permute-start.76 = (bf16[4,192,1536]{2,1,0:T(8,128)(2,1)S(1)}, bf16[4,192,1536]{2,1,0:T(8,128)(2,1)S(1)}, u32[]{:S(2)}, u32[]{:S(2)}) collective-permute-start(bf16[4,192,1536]{2,1,0:T(8,128)(2,1)S(1)} %pad_maximum_fusion.3), channel_id=1, source_target_pairs={{0,4},{4,0},{8,12},{12,8},{16,20},{20,16},{24,28},{28,24},{1,5},{5... | collective-permute-start | bytes 7077896 | tf_op jit(solution)/shard_map/ppermute | solution.py:449
  657.1 61.1 %collective-permute-start.83 = (bf16[4,768,640]{2,1,0:T(8,128)(2,1)}, bf16[4,768,640]{2,1,0:T(8,128)(2,1)}, u32[]{:S(2)}, u32[]{:S(2)}) collective-permute-start(bf16[4,768,640]{2,1,0:T(8,128)(2,1)} %pad_maximum_fusion.refs_4_), channel_id=1, source_target_pairs={{0,4},{4,0},{8,12},{12,8},{16,20},{20,16},{24,28},{28,24},{1,5},{5... | collective-permute-start | bytes 11796488 | tf_op jit(solution)/shard_map/ppermute | solution.py:449
  668.0 30.1 %collective-permute-start.79 = (bf16[4,192,1536]{2,1,0:T(8,128)(2,1)}, bf16[4,192,1536]{2,1,0:T(8,128)(2,1)}, u32[]{:S(2)}, u32[]{:S(2)}) collective-permute-start(bf16[4,192,1536]{2,1,0:T(8,128)(2,1)} %pad_maximum_fusion.4), channel_id=1, source_target_pairs={{0,4},{4,0},{8,12},{12,8},{16,20},{20,16},{24,28},{28,24},{1,5},{5... | collective-permute-start | bytes 7077896 | tf_op jit(solution)/shard_map/ppermute | solution.py:449
  693.2 22.5 %collective-permute-start.68 = (bf16[192,2304]{1,0:T(8,128)(2,1)S(1)}, bf16[192,2304]{1,0:T(8,128)(2,1)S(1)}, u32[]{:S(2)}, u32[]{:S(2)}) collective-permute-start(bf16[192,2304]{1,0:T(8,128)(2,1)S(1)} %fusion.6.refs_1_), channel_id=1, source_target_pairs={{0,16},{4,20},{8,24},{12,28},{16,0},{20,4},{24,8},{28,12},{1,17},{... | collective-permute-start | bytes 2654216 | tf_op jit(solution)/shard_map/ppermute | solution.py:449
  698.1 26.2 %collective-permute-start.80 = (bf16[256,640]{1,0:T(8,128)(2,1)S(1)}, bf16[256,640]{1,0:T(8,128)(2,1)S(1)}, u32[]{:S(2)}, u32[]{:S(2)}) collective-permute-start(bf16[256,640]{1,0:T(8,128)(2,1)S(1)} %get-tuple-element.410), channel_id=1, source_target_pairs={{0,8},{4,12},{8,0},{12,4},{16,24},{20,28},{24,16},{28,20},{1,9},{5... | collective-permute-start | bytes 983048 | tf_op jit(solution)/shard_map/ppermute | solution.py:449
  705.2 24.5 %collective-permute-start.81 = (bf16[256,640]{1,0:T(8,128)(2,1)S(1)}, bf16[256,640]{1,0:T(8,128)(2,1)S(1)}, u32[]{:S(2)}, u32[]{:S(2)}) collective-permute-start(bf16[256,640]{1,0:T(8,128)(2,1)S(1)} %get-tuple-element.411), channel_id=1, source_target_pairs={{0,16},{4,20},{8,24},{12,28},{16,0},{20,4},{24,8},{28,12},{1,17},{... | collective-permute-start | bytes 983048 | tf_op jit(solution)/shard_map/ppermute | solution.py:449
  717.1 25.2 %collective-permute-start.85 = (bf16[192,1536]{1,0:T(8,128)(2,1)S(1)}, bf16[192,1536]{1,0:T(8,128)(2,1)S(1)}, u32[]{:S(2)}, u32[]{:S(2)}) collective-permute-start(bf16[192,1536]{1,0:T(8,128)(2,1)S(1)} %add.363), channel_id=1, source_target_pairs={{0,16},{4,20},{8,24},{12,28},{16,0},{20,4},{24,8},{28,12},{1,17},{... | collective-permute-start | bytes 1769480 | tf_op jit(solution)/shard_map/ppermute | solution.py:449
  718.2 24.9 %collective-permute-start.87 = (bf16[192,640]{1,0:T(8,128)(2,1)S(1)}, bf16[192,640]{1,0:T(8,128)(2,1)}, u32[]{:S(2)}, u32[]{:S(2)}) collective-permute-start(bf16[192,640]{1,0:T(8,128)(2,1)S(1)} %add_bitcast_fusion.1), channel_id=1, source_target_pairs={{0,1},{3,2},{4,5},{7,6},{8,9},{11,10},{12,13},{15,14},{16,17},{19,... | collective-permute-start | bytes 737288 | tf_op jit(solution)/shard_map/ppermute | solution.py:465
  724.3 44.5 %collective-permute-start.94 = (bf16[2,192,2304]{2,1,0:T(8,128)(2,1)S(1)}, bf16[2,192,2304]{2,1,0:T(8,128)(2,1)S(1)}, u32[]{:S(2)}, u32[]{:S(2)}) collective-permute-start(bf16[2,192,2304]{2,1,0:T(8,128)(2,1)S(1)} %pad_maximum_fusion.8), channel_id=1, source_target_pairs={{0,8},{4,12},{8,0},{12,4},{16,24},{20,28},{24,16},{28,20},{1,9},{5... | collective-permute-start | bytes 5308424 | tf_op jit(solution)/shard_map/ppermute | solution.py:449
  729.7 37.3 %collective-permute-start.95 = (bf16[2,192,1536]{2,1,0:T(8,128)(2,1)S(1)}, bf16[2,192,1536]{2,1,0:T(8,128)(2,1)S(1)}, u32[]{:S(2)}, u32[]{:S(2)}) collective-permute-start(bf16[2,192,1536]{2,1,0:T(8,128)(2,1)S(1)} %pad_maximum_fusion.12), channel_id=1, source_target_pairs={{0,16},{4,20},{8,24},{12,28},{16,0},{20,4},{24,8},{28,12},{1,17},{... | collective-permute-start | bytes 3538952 | tf_op jit(solution)/shard_map/ppermute | solution.py:449
  799.4 23.4 %collective-permute-start.102 = (bf16[192,768]{1,0:T(8,128)(2,1)S(1)}, bf16[192,768]{1,0:T(8,128)(2,1)S(1)}, u32[]{:S(2)}, u32[]{:S(2)}) collective-permute-start(bf16[192,768]{1,0:T(8,128)(2,1)S(1)} %get-tuple-element.412), channel_id=1, source_target_pairs={{0,2},{1,3},{2,0},{3,1},{4,6},{5,7},{6,4},{7,5},{8,10},{9,11},{10,... | collective-permute-start | bytes 884744 | tf_op jit(solution)/shard_map/ppermute | solution.py:453
  799.5 23.3 %collective-permute-start.103 = (bf16[192,768]{1,0:T(8,128)(2,1)S(1)}, bf16[192,768]{1,0:T(8,128)(2,1)S(1)}, u32[]{:S(2)}, u32[]{:S(2)}) collective-permute-start(bf16[192,768]{1,0:T(8,128)(2,1)S(1)} %get-tuple-element.415), channel_id=1, source_target_pairs={{0,3},{1,2},{2,1},{3,0},{4,7},{5,6},{6,5},{7,4},{8,11},{9,10},{10,... | collective-permute-start | bytes 884744 | tf_op jit(solution)/shard_map/ppermute | solution.py:453
  (169 other events, 2393.2 us)

commit v4 on v3

--- a/solution.py
+++ b/solution.py
@@ -442,7 +442,28 @@
     )
 
 
-COST_SHARE = 20
+PLANE = [[0, 2, 4, 6], [1, 3, 5, 7]]
+COSTS = {
+    "project": 0.3,
+    "attend": 0.3,
+    "leave": 0.3,
+    "join_shared": 0.3,
+    "experts": 0.3,
+    "experts_back": 0.3,
+    "enter_back": 0.3,
+    "attend_back": 0.3,
+    "finish": 0.3,
+    "weight_grad": 0.3,
+    "expert_grad": 0.3,
+    "blend_split": 0.3,
+    "blend_pair": 0.3,
+    "blend_sum": 0.3,
+    "blend_stack": 0.3,
+    "blend_four": 0.3,
+    "place_pair": 0.3,
+    "place_shared": 0.3,
+    "place_heads": 0.3,
+}
 
 
 def flip(value, bit):
@@ -491,8 +512,19 @@
     )
 
 
-def chips_swap(values):
-    return [values[0]] + [flip(values[r], 2 * r) for r in (1, 2, 3)]
+def chips_exchange(blocks):
+    return lax.all_to_all(
+        blocks,
+        "ctx",
+        split_axis=0,
+        concat_axis=0,
+        tiled=True,
+        axis_index_groups=PLANE,
+    )
+
+
+def line_exchange(blocks):
+    return lax.all_to_all(blocks, "wt", split_axis=0, concat_axis=0, tiled=True)
 
 
 def chips_gather(value, x_last):
@@ -562,9 +594,7 @@
         out_shape=out_shape,
         compiler_params=pltpu.CompilerParams(vmem_limit_bytes=48 * 1024 * 1024),
         cost_estimate=pl.CostEstimate(
-            flops=int(flops) // COST_SHARE,
-            bytes_accessed=int(moved) // COST_SHARE,
-            transcendentals=0,
+            flops=int(COSTS.get(name, 1.0) * 1e9), bytes_accessed=1000, transcendentals=0
         ),
         name=name,
     )(meta, *arrays)
@@ -583,23 +613,59 @@
     return sum(math.prod(a.shape) * a.dtype.itemsize for a in arrays)
 
 
+def blend(meta, name, function, arrays, pieces=4):
+    rows = arrays[0].shape[-2]
+    tile = rows // pieces
+    outs = jax.eval_shape(function, *[shape_of(a.shape, a.dtype) for a in arrays])
+    many = isinstance(outs, (list, tuple))
+    outs = list(outs) if many else [outs]
+
+    def spec(a):
+        rank = len(a.shape)
+        lead = a.shape[:-2]
+        return pl.BlockSpec(
+            tuple(lead) + (tile, a.shape[-1]),
+            lambda i, m: (0,) * (rank - 2) + (i, 0),
+        )
+
+    def kernel(meta_ref, *refs):
+        result = function(*[ref[...] for ref in refs[: len(arrays)]])
+        result = list(result) if many else [result]
+        for ref, value in zip(refs[len(arrays) :], result):
+            ref[...] = value
+
+    result = call(
+        kernel,
+        name,
+        meta,
+        arrays,
+        (pieces,),
+        [spec(a) for a in arrays],
+        [spec(a) for a in outs],
+        outs,
+        [],
+        0,
+        0,
+    )
+    return result if many else result[0]
+
+
 def aligned(value, step):
     return pl.multiple_of(value * step, step)
 
 
 def project_kernel(meta, *refs):
-    blocks, gain_ref, mine, other = refs[:4], refs[4], refs[5], refs[6]
+    blocks, (gain_ref, mine, other) = refs[:4], refs[4:7]
     normed_ref, query_ref, pair_ref, weight_ref, held = refs[7:]
     step = pl.program_id(0)
-    core, shard = meta[0] & 1, meta[1]
+    core = meta[0] & 1
     rows = mine.shape[1]
 
     @pl.when(step == 0)
     def _():
         for i in range(4):
-            at = 2 * (shard ^ i)
-            weight_ref[pl.ds(aligned(at + core, rows), rows), :] = mine[i]
-            weight_ref[pl.ds(aligned(at + 1 - core, rows), rows), :] = other[i]
+            weight_ref[pl.ds(aligned(2 * i + core, rows), rows), :] = mine[i]
+            weight_ref[pl.ds(aligned(2 * i + 1 - core, rows), rows), :] = other[i]
 
     for r in range(4):
 
@@ -627,6 +693,10 @@
         shape_of((4, token_rows, columns - query_width), jnp.bfloat16),
         shape_of((width, columns), jnp.bfloat16),
     ]
+
+    def at_chip(r, m):
+        return ((m[0] >> 1) ^ r, 0, 0)
+
     return call(
         project_kernel,
         "project",
@@ -635,9 +705,9 @@
         (4,),
         [whole(a) for a in arrays],
         [
-            pl.BlockSpec((1, token_rows, width), lambda r, m: (r, 0, 0)),
-            pl.BlockSpec((1, token_rows, query_width), lambda r, m: (r, 0, 0)),
-            pl.BlockSpec((1, token_rows, columns - query_width), lambda r, m: (r, 0, 0)),
+            pl.BlockSpec((1, token_rows, width), at_chip),
+            pl.BlockSpec((1, token_rows, query_width), at_chip),
+            pl.BlockSpec((1, token_rows, columns - query_width), at_chip),
             whole(outs[3]),
         ],
         outs,
@@ -651,17 +721,16 @@
     half = mine_ref.shape[1] // 2
     for slot in range(16):
         block, part = (slot, 0) if slot < 8 else (15 - slot, 1)
-        relative = meta[0] ^ block
-        place = relative >> 1
+        place = block >> 1
         rows = pl.ds(part * half, half)
         to = pl.ds(slot * half, half)
 
-        @pl.when((relative & 1) == 0)
+        @pl.when((meta[0] & 1) == (block & 1))
         def _():
             keys[to, :] = mine_ref[place, rows, :HEAD_SIZE]
             values[to, :] = mine_ref[place, rows, HEAD_SIZE:]
 
-        @pl.when((relative & 1) == 1)
+        @pl.when((meta[0] & 1) != (block & 1))
         def _():
             keys[to, :] = other_ref[place, rows, :HEAD_SIZE]
             values[to, :] = other_ref[place, rows, HEAD_SIZE:]
@@ -681,67 +750,62 @@
 
 def step_slot(meta):
     step = pl.program_id(0)
-    block = meta[0] ^ (2 * (step >> 1))
+    block = 2 * (step >> 1) + (meta[0] & 1)
     return jnp.where((step & 1) == 0, block, 15 - block)
 
 
-def allowed_pairs(key_block, slot, shape, half):
-    key_place = key_block * shape[0] + lax.broadcasted_iota(jnp.int32, shape, 0)
+def allowed_pairs(start, slot, shape, half):
+    key_place = start + lax.broadcasted_iota(jnp.int32, shape, 0)
     query_place = slot * half + (lax.broadcasted_iota(jnp.int32, shape, 1) & (half - 1))
     return key_place <= query_place
 
 
+def key_spans(step, half, span):
+    pairs = (step // 2 if step % 2 == 0 else 7 - step // 2) + 1
+    rows = pairs * 2 * half
+    return [(at, min(span, rows - at)) for at in range(0, rows, span)]
+
+
 def attend_kernel(scale, span, meta, query_ref, mine_ref, other_ref, *refs):
-    outs, log_ref = refs[:4], refs[4]
-    keys, values, values_turned = refs[5:]
-    step = pl.program_id(0)
+    out_ref, log_ref, keys, values, values_turned = refs
     half, group_width = query_ref.shape[1:]
     count = group_width // HEAD_SIZE
 
-    @pl.when(step == 0)
+    @pl.when(pl.program_id(0) == 0)
     def _():
         sort_pairs(meta, mine_ref, other_ref, keys, values)
         values_turned[...] = values[...].T
 
     slot = step_slot(meta)
     query = stack_heads(query_ref[0])
-    last = slot * half // span
-
-    def scores_of(key_block):
-        at = pl.ds(aligned(key_block, span), span)
-        return at, dot_last(keys[at, :], query) * scale
-
-    def add(carry, at, scores):
-        highest, total, mixed = carry
-        new = jnp.maximum(highest, jnp.max(scores, axis=0, keepdims=True))
-        rescale = jnp.exp(highest - new)
-        powers = jnp.exp(scores - new)
-        total = total * rescale + jnp.sum(powers, axis=0, keepdims=True)
-        mixed = mixed * rescale + dot_plain(values_turned[:, at], powers.astype(jnp.bfloat16))
-        return new, total, mixed
-
-    def body(key_block, carry):
-        at, scores = scores_of(key_block)
-        return add(carry, at, scores)
-
     wide = count * half
-    carry = (
-        jnp.full((1, wide), masked_score, jnp.float32),
-        jnp.zeros((1, wide), jnp.float32),
-        jnp.zeros((HEAD_SIZE, wide), jnp.float32),
-    )
-    carry = lax.fori_loop(0, last, body, carry)
-    at, scores = scores_of(last)
-    scores = jnp.where(allowed_pairs(last, slot, scores.shape, half), scores, masked_score)
-    highest, total, mixed = add(carry, at, scores)
-    log_ref[0] = highest + jnp.log(total)
-    result = unstack_heads((mixed / total).T, count).astype(jnp.bfloat16)
-    for r in range(4):
-        for part in range(2):
-
-            @pl.when(step == 2 * r + part)
-            def _():
-                outs[r][part * half : (part + 1) * half, :] = result
+
+    def run(spans):
+        highest = jnp.full((1, wide), masked_score, jnp.float32)
+        total = jnp.zeros((1, wide), jnp.float32)
+        mixed = jnp.zeros((HEAD_SIZE, wide), jnp.float32)
+        for start, size in spans:
+            at = pl.ds(start, size)
+            scores = dot_last(keys[at, :], query) * scale
+            if start == spans[-1][0]:
+                seen = allowed_pairs(start, slot, scores.shape, half)
+                scores = jnp.where(seen, scores, masked_score)
+            new = jnp.maximum(highest, jnp.max(scores, axis=0, keepdims=True))
+            rescale = jnp.exp(highest - new)
+            powers = jnp.exp(scores - new)
+            total = total * rescale + jnp.sum(powers, axis=0, keepdims=True)
+            mixed = mixed * rescale + dot_plain(
+                values_turned[:, at], powers.astype(jnp.bfloat16)
+            )
+            highest = new
+        log_ref[0] = highest + jnp.log(total)
+        out_ref[0] = unstack_heads((mixed / total).T, count).astype(jnp.bfloat16)
+
+    for step in range(8):
+
+        @pl.when(pl.program_id(0) == step)
+        def _():
+            run(key_spans(step, half, span))
 
 
 def attend(meta, query, mine, other, scale):
@@ -749,11 +813,13 @@
     half = token_rows // 2
     count = group_width // HEAD_SIZE
     everything = 8 * token_rows
-    span = min(256, everything)
+    span = 1024
     arrays = [query, mine, other]
-    outs = [shape_of((token_rows, group_width), jnp.bfloat16)] * 4
-    outs = outs + [shape_of((8, 1, count * half), jnp.float32)]
-    result = call(
+    outs = [
+        shape_of(query.shape, jnp.bfloat16),
+        shape_of((8, 1, count * half), jnp.float32),
+    ]
+    return call(
         functools.partial(attend_kernel, scale, span),
         "attend",
         meta,
@@ -764,8 +830,10 @@
             whole(mine),
             whole(other),
         ],
-        [whole(a) for a in outs[:4]]
-        + [pl.BlockSpec((1, 1, count * half), lambda i, m: (i, 0, 0))],
+        [
+            pl.BlockSpec((1, half, group_width), lambda i, m: (i // 2, i % 2, 0)),
+            pl.BlockSpec((1, 1, count * half), lambda i, m: (i, 0, 0)),
+        ],
         outs,
         [
             pltpu.VMEM((everything, HEAD_SIZE), jnp.bfloat16),
@@ -775,13 +843,11 @@
         2 * 2 * 4 * token_rows * everything * group_width,
         size_of(arrays) + size_of(outs),
     )
-    return result[:4], result[4]
 
 
 def attend_back_kernel(scale, span, meta, query_ref, mine_ref, other_ref, log_ref, *refs):
-    mixed_refs, grad_refs = refs[:4], refs[4:8]
-    grad_query_ref, grad_mine_ref, grad_other_ref = refs[8:11]
-    keys, values, keys_turned, grad_keys, grad_values, mixed_held, grad_held = refs[11:]
+    mixed_ref, grad_ref, grad_query_ref, grad_mine_ref, grad_other_ref = refs[:5]
+    keys, values, keys_turned, grad_keys, grad_values = refs[5:]
     step = pl.program_id(0)
     half, group_width = query_ref.shape[1:]
     count = group_width // HEAD_SIZE
@@ -793,54 +859,48 @@
         grad_keys[...] = jnp.zeros_like(grad_keys)
         grad_values[...] = jnp.zeros_like(grad_values)
 
-    for r in range(4):
-        for part in range(2):
-
-            @pl.when(step == 2 * r + part)
-            def _():
-                mixed_held[...] = mixed_refs[r][part * half : (part + 1) * half, :]
-                grad_held[...] = grad_refs[r][part * half : (part + 1) * half, :]
-
     slot = step_slot(meta)
     query = stack_heads(query_ref[0])
-    mixed = stack_heads(mixed_held[...]).astype(jnp.float32)
-    grad = stack_heads(grad_held[...])
+    mixed = stack_heads(mixed_ref[0]).astype(jnp.float32)
+    grad = stack_heads(grad_ref[0])
     delta = jnp.sum((mixed * grad.astype(jnp.float32)).T, axis=0, keepdims=True)
     log_total = log_ref[0]
-    last = slot * half // span
-
-    def one(key_block, grad_turned, masked):
-        at = pl.ds(aligned(key_block, span), span)
-        scores = dot_last(keys[at, :], query) * scale
-        probs = jnp.exp(scores - log_total)
-        if masked:
-            probs = jnp.where(allowed_pairs(key_block, slot, probs.shape, half), probs, 0.0)
-        grad_probs = dot_last(values[at, :], grad)
-        grad_scores = (probs * (grad_probs - delta)).astype(jnp.bfloat16)
-        grad_values[at, :] += dot_plain(probs.astype(jnp.bfloat16), grad)
-        grad_keys[at, :] += dot_plain(grad_scores, query)
-        return grad_turned + dot_plain(keys_turned[:, at], grad_scores)
-
-    grad_turned = jnp.zeros((HEAD_SIZE, count * half), jnp.float32)
-    grad_turned = lax.fori_loop(0, last, lambda b, total: one(b, total, False), grad_turned)
-    grad_turned = one(last, grad_turned, True)
-    grad_query_ref[0] = unstack_heads((grad_turned * scale).T, count).astype(jnp.bfloat16)
+
+    def run(spans):
+        grad_turned = jnp.zeros((HEAD_SIZE, count * half), jnp.float32)
+        for start, size in spans:
+            at = pl.ds(start, size)
+            scores = dot_last(keys[at, :], query) * scale
+            probs = jnp.exp(scores - log_total)
+            if start == spans[-1][0]:
+                probs = jnp.where(allowed_pairs(start, slot, probs.shape, half), probs, 0.0)
+            grad_probs = dot_last(values[at, :], grad)
+            grad_scores = (probs * (grad_probs - delta)).astype(jnp.bfloat16)
+            grad_values[at, :] += dot_plain(probs.astype(jnp.bfloat16), grad)
+            grad_keys[at, :] += dot_plain(grad_scores, query)
+            grad_turned += dot_plain(keys_turned[:, at], grad_scores)
+        grad_query_ref[0] = unstack_heads((grad_turned * scale).T, count).astype(jnp.bfloat16)
+
+    for at_step in range(8):
+
+        @pl.when(step == at_step)
+        def _():
+            run(key_spans(at_step, half, span))
 
     @pl.when(step == 7)
     def _():
         for slot_at in range(16):
             block, part = (slot_at, 0) if slot_at < 8 else (15 - slot_at, 1)
-            relative = meta[0] ^ block
-            place = relative >> 1
+            place = block >> 1
             rows = pl.ds(part * half, half)
             here = pl.ds(slot_at * half, half)
             both = jnp.concatenate([grad_keys[here, :] * scale, grad_values[here, :]], axis=1)
 
-            @pl.when((relative & 1) == 0)
+            @pl.when((meta[0] & 1) == (block & 1))
             def _():
                 grad_mine_ref[place, rows, :] = both
 
-            @pl.when((relative & 1) == 1)
+            @pl.when((meta[0] & 1) != (block & 1))
             def _():
                 grad_other_ref[place, rows, :] = both.astype(jnp.bfloat16)
 
@@ -850,8 +910,8 @@
     half = token_rows // 2
     count = group_width // HEAD_SIZE
     everything = 8 * token_rows
-    span = min(256, everything)
-    arrays = [query, mine, other, log_total] + list(mixed) + list(grad)
+    span = 512
+    arrays = [query, mine, other, log_total, mixed, grad]
     outs = [
         shape_of(query.shape, jnp.bfloat16),
         shape_of(mine.shape, jnp.float32),
@@ -868,8 +928,9 @@
             whole(mine),
             whole(other),
             pl.BlockSpec((1, 1, count * half), lambda i, m: (i, 0, 0)),
-        ]
-        + [whole(a) for a in arrays[4:]],
+            pl.BlockSpec((1, half, group_width), lambda i, m: (i // 2, i % 2, 0)),
+            pl.BlockSpec((1, half, group_width), lambda i, m: (i // 2, i % 2, 0)),
+        ],
         [
             pl.BlockSpec((1, half, group_width), lambda i, m: (i // 2, i % 2, 0)),
             whole(outs[1]),
@@ -882,8 +943,6 @@
             pltpu.VMEM((HEAD_SIZE, everything), jnp.bfloat16),
             pltpu.VMEM((everything, HEAD_SIZE), jnp.float32),
             pltpu.VMEM((everything, HEAD_SIZE), jnp.float32),
-            pltpu.VMEM((half, group_width), jnp.bfloat16),
-            pltpu.VMEM((half, group_width), jnp.bfloat16),
         ],
         5 * 2 * 4 * token_rows * everything * group_width,
         size_of(arrays) + size_of(outs),
@@ -891,17 +950,17 @@
 
 
 def leave_kernel(meta, *refs):
-    parts, mine, other = refs[:4], refs[4:8], refs[8]
-    states_ref, gain_ref, weight_ref, middle_ref, normed_ref = refs[9:]
-    core, chip, shard = meta[0] & 1, meta[0] >> 1, meta[1]
-    rows = mine[0].shape[0]
+    parts, mine, other, states_ref, gain_ref = refs[:4], *refs[4:8]
+    weight_ref, middle_ref, normed_ref = refs[8:]
+    core, chip = meta[0] & 1, meta[0] >> 1
+    rows = mine.shape[1]
     for i in range(4):
-        at = 2 * (chip ^ shard ^ i)
-        weight_ref[pl.ds(aligned(at + core, rows), rows), :] = mine[i][...]
-        weight_ref[pl.ds(aligned(at + 1 - core, rows), rows), :] = other[i]
+        weight_ref[pl.ds(aligned(2 * i + core, rows), rows), :] = mine[i]
+        weight_ref[pl.ds(aligned(2 * i + 1 - core, rows), rows), :] = other[i]
     middle = states_ref[...].astype(jnp.float32)
     for r in range(4):
-        middle += dot_plain(parts[r][...], weight_ref[2 * rows * r : 2 * rows * (r + 1), :])
+        at = pl.ds(aligned(chip ^ r, 2 * rows), 2 * rows)
+        middle += dot_plain(parts[r][...], weight_ref[at, :])
     middle_ref[...] = middle
     inverse = lax.rsqrt(jnp.mean(middle * middle, axis=-1, keepdims=True) + norm_eps)
     normed_ref[...] = (middle * inverse * gain_ref[...]).astype(jnp.bfloat16)
@@ -909,9 +968,9 @@
 
 def leave(meta, parts, mine, other, states, gain):
     token_rows, width = states.shape
-    arrays = list(parts) + list(mine) + [other, states, gain]
+    arrays = list(parts) + [mine, other, states, gain]
     outs = [
-        shape_of((8 * mine[0].shape[0], width), jnp.bfloat16),
+        shape_of((8 * mine.shape[1], width), jnp.bfloat16),
         shape_of((token_rows, width), jnp.float32),
         shape_of((token_rows, width), jnp.bfloat16),
     ]
@@ -940,7 +999,7 @@
 
 
 def enter_back_kernel(meta, final_ref, normed_ref, middle_ref, gain_ref, weight_ref, *refs):
-    grad_ref, branch_ref, gain_grad_ref = refs[:3]
+    grad_ref, branch_ref, gain_grad_ref, mixed_ref = refs
     grad, gain_grad = norm_back_rows(normed_ref[...], middle_ref[...], gain_ref[...])
     grad = grad + final_ref[...]
     grad_ref[...] = grad
@@ -949,7 +1008,7 @@
     branch_ref[...] = branch
     rows = weight_ref.shape[0] // 4
     for r in range(4):
-        refs[3 + r][...] = dot_last(branch, weight_ref[rows * r : rows * (r + 1), :]).astype(
+        mixed_ref[r] = dot_last(branch, weight_ref[rows * r : rows * (r + 1), :]).astype(
             jnp.bfloat16
         )
 
@@ -961,7 +1020,8 @@
         shape_of((token_rows, width), jnp.float32),
         shape_of((token_rows, width), jnp.bfloat16),
         shape_of((1, width), jnp.float32),
-    ] + [shape_of((token_rows, weight.shape[0] // 4), jnp.bfloat16)] * 4
+        shape_of((4, token_rows, weight.shape[0] // 4), jnp.bfloat16),
+    ]
     return call(
         enter_back_kernel,
         "enter_back",
@@ -978,13 +1038,13 @@
 
 
 def finish_kernel(meta, *refs):
-    parts, mine, other = refs[:4], refs[4], refs[5]
-    states_ref, middle_ref, gain_ref, grad_ref, gain_grad_ref, total = refs[6:]
-    core = meta[0] & 1
+    parts, mine, other = refs[:3]
+    states_ref, middle_ref, gain_ref, grad_ref, gain_grad_ref, total = refs[3:]
+    core, chip = meta[0] & 1, meta[0] >> 1
     columns = mine.shape[1]
     for at, weights in ((core, mine), (1 - core, other)):
         total[:, pl.ds(aligned(at, columns), columns)] = sum(
-            dot_last(parts[r][...], weights[r]) for r in range(4)
+            dot_last(parts[r], weights[chip ^ r]) for r in range(4)
         )
     grad, gain_grad = norm_back_rows(
         total[...], states_ref[...].astype(jnp.float32), gain_ref[...]
@@ -995,7 +1055,7 @@
 
 def finish(meta, parts, mine, other, states, grad_middle, gain):
     token_rows, width = states.shape
-    arrays = list(parts) + [mine, other, states, grad_middle, gain]
+    arrays = [parts, mine, other, states, grad_middle, gain]
     outs = [
         shape_of((1, token_rows, width), jnp.float32),
         shape_of((1, width), jnp.float32),
@@ -1010,7 +1070,7 @@
         [whole(a) for a in outs],
         outs,
         [pltpu.VMEM((token_rows, width), jnp.float32)],
-        2 * token_rows * width * 4 * parts[0].shape[1],
+        2 * token_rows * width * 4 * parts.shape[2],
         size_of(arrays) + size_of(outs),
     )
 
@@ -1193,17 +1253,67 @@
                 start = stop
 
 
-def weight_grad_whole_kernel(pairs, meta, *refs):
-    at, start = 0, 0
-    for count in pairs:
-        lefts, rights = refs[at : at + count], refs[at + count : at + 2 * count]
-        at += 2 * count
-        part = sum(dot_first(a[...], b[0]) for a, b in zip(lefts, rights)).astype(jnp.bfloat16)
-        refs[-1][:, start : start + part.shape[1]] = part
-        start += part.shape[1]
-
-
-def weight_grad(meta, order, operands, index, split=True):
+def expert_grad_kernel(count, meta, *refs):
+    rows, grads, front, acts = (refs[i * count : (i + 1) * count] for i in range(4))
+    out_ref = refs[-1] if len(refs) == 4 * count + 1 else refs[-2]
+    tile = rows[0].shape[1]
+    both = 3 * F
+
+    def pair(front_refs, act_refs):
+        return [
+            sum(dot_first(a[...], b[0]) for a, b in zip(left, right)).astype(jnp.bfloat16)
+            for left, right in ((rows, front_refs), (grads, act_refs))
+        ]
+
+    left, right = pair(front, acts)
+    out_ref[0, :tile, : left.shape[1]] = left
+    out_ref[0, :tile, left.shape[1] : both] = right
+    if len(refs) > 4 * count + 1:
+        held = refs[-1]
+        left, right = pair(refs[4 * count : 5 * count], refs[5 * count : 6 * count])
+        split, columns = left.shape[1], left.shape[1] + right.shape[1]
+        held[:, :split] = left
+        held[:, split:] = right
+        quarter = tile // 4
+        first = 2 * meta[2]
+        out_ref[0, tile:, :columns] = held[pl.ds(aligned(first, quarter), quarter), :]
+        out_ref[0, tile:, columns:] = held[pl.ds(aligned(first + 1, quarter), quarter), :]
+
+
+def expert_grad(meta, expert, half, rows, grads, front, acts, shared=None):
+    count = len(rows)
+    token_rows, width = rows[0].shape
+    tile = width // 4
+    arrays = list(rows) + list(grads) + list(front) + list(acts)
+    column = pl.BlockSpec((token_rows, tile), lambda i, m: (0, i ^ m[0]))
+
+    def of_expert(a):
+        return pl.BlockSpec((1,) + a.shape[1:], lambda i, m: (m[1], 0, 0))
+
+    in_specs = [column] * (2 * count) + [of_expert(a) for a in arrays[2 * count :]]
+    below, scratch = 0, []
+    if shared is not None:
+        arrays += list(shared[0]) + list(shared[1])
+        in_specs += [whole(a) for a in arrays[4 * count :]]
+        below = tile // 4
+        columns = shared[0][0].shape[-1] + shared[1][0].shape[-1]
+        scratch = [pltpu.VMEM((tile, columns), jnp.bfloat16)]
+    return call(
+        functools.partial(expert_grad_kernel, count),
+        "expert_grad",
+        jnp.stack([meta[0] >> 1, expert, half]),
+        arrays,
+        (4,),
+        in_specs,
+        pl.BlockSpec((1, tile + below, 3 * F), lambda i, m: (i, 0, 0)),
+        shape_of((4, tile + below, 3 * F), jnp.bfloat16),
+        scratch,
+        0,
+        0,
+    )
+
+
+def weight_grad(meta, order, operands, index):
     token_rows, width = operands[0][0][0].shape
     tile = width // 4
     scalars = jnp.stack([order, meta[0]])
@@ -1219,20 +1329,6 @@
         columns += units
     tokens = token_rows * len(operands[0][0])
     counts = [len(left) for left, _ in operands]
-    if not split:
-        return call(
-            functools.partial(weight_grad_whole_kernel, counts),
-            "weight_grad_whole",
-            scalars,
-            arrays,
-            (4,),
-            in_specs,
-            pl.BlockSpec((tile, columns), lambda i, m: (i, 0)),
-            shape_of((width, columns), jnp.bfloat16),
-            [],
-            2 * tokens * width * columns,
-            2 * width * columns + 4 * tokens * width + 2 * tokens * columns,
-        )
     outs = [shape_of((4, tile // 2, columns), jnp.bfloat16)] * 2
     return call(
         functools.partial(weight_grad_kernel, counts, 1),
@@ -1249,101 +1345,78 @@
     )
 
 
-def place_expert_kernel(meta, *refs):
-    mine, other, out_ref = refs[-6:-2], refs[-2], refs[-1]
-    step = pl.program_id(0)
-    core = meta[0] & 1
-    rows = mine[0].shape[0]
-    columns = out_ref.shape[2]
-    out_ref[0, pl.ds(aligned(1 - core, rows), rows), :] = other[0, :, :columns].astype(
-        jnp.float32
-    )
-    for r in range(4):
-
-        @pl.when(step == r)
-        def _():
-            out_ref[0, pl.ds(aligned(core, rows), rows), :] = mine[r][:, :columns].astype(
-                jnp.float32
-            )
-
-
-def place_total_kernel(meta, *refs):
-    refs[-1][0] = refs[-2][...].astype(jnp.float32)
-
-
-def place_call(kernel, name, meta, total, arrays, in_specs, out_spec, shape, moved):
+def place_pair_kernel(meta, *refs):
+    mine, other, out_ref = refs[-3:]
+    rows = out_ref.shape[1]
+
+    @pl.when(pl.program_id(0) == 0)
+    def _():
+        out_ref[0] = mine[0, :rows].astype(jnp.float32)
+
+    @pl.when(pl.program_id(0) == 1)
+    def _():
+        out_ref[0] = other[0, :rows].astype(jnp.float32)
+
+
+def place_pair(meta, total, index, shape, mine, other):
+    _, rows, columns = mine.shape
+    arrays = [mine, other]
+    in_specs = [
+        pl.BlockSpec((1, rows, columns), lambda k, r, m: ((1 - k) * r + 3 * k, 0, 0)),
+        pl.BlockSpec((1, rows, columns), lambda k, r, m: (k * r, 0, 0)),
+    ]
     aliases = {}
     if total is not None:
         arrays = [total] + arrays
         in_specs = [pl.BlockSpec(memory_space=pl.ANY)] + in_specs
         aliases = {1: 0}
     return pl.pallas_call(
-        kernel,
+        place_pair_kernel,
         grid_spec=pltpu.PrefetchScalarGridSpec(
-            num_scalar_prefetch=1, grid=(4,), in_specs=in_specs, out_specs=out_spec
+            num_scalar_prefetch=1,
+            grid=(2, 4),
+            in_specs=in_specs,
+            out_specs=pl.BlockSpec(
+                (1, shape[1] // 4, shape[2]),
+                lambda k, r, m: (2 * ((m[0] & 1) ^ k) + index, (m[0] >> 1) ^ r, 0),
+            ),
         ),
         out_shape=shape_of(shape, jnp.float32),
         input_output_aliases=aliases,
         compiler_params=pltpu.CompilerParams(vmem_limit_bytes=48 * 1024 * 1024),
-        cost_estimate=pl.CostEstimate(flops=0, bytes_accessed=moved // COST_SHARE, transcendentals=0),
-        name=name,
+        cost_estimate=pl.CostEstimate(
+            flops=int(COSTS.get("place_pair", 1.0) * 1e9), bytes_accessed=1000, transcendentals=0
+        ),
+        name="place_pair",
     )(meta, *arrays)
 
 
-def place_expert(meta, total, index, shape, mine, other):
-    rows, columns = mine[0].shape
-    return place_call(
-        place_expert_kernel,
-        "place_expert",
-        meta,
-        total,
-        list(mine) + [other],
-        [whole(a) for a in mine] + [pl.BlockSpec((1, rows, columns), lambda r, m: (r, 0, 0))],
-        pl.BlockSpec((1, 2 * rows, shape[2]), lambda r, m: (index, (m[0] >> 1) ^ r, 0)),
-        shape,
-        8 * rows * columns * 6,
-    )
-
-
-def place_total(meta, total, index, shape, value):
-    rows, columns = value.shape
-    return place_call(
-        place_total_kernel,
-        "place_total",
-        meta,
-        total,
-        [value],
-        [pl.BlockSpec((rows // 4, columns), lambda r, m: (r, 0))],
-        pl.BlockSpec((1, rows // 4, columns), lambda r, m: (index, r, 0)),
-        shape,
-        rows * columns * 6,
-    )
-
-
-def place_shared_kernel(meta, mine, other, out_ref):
+def place_shared_kernel(meta, mine_low, mine_high, other_low, other_high, out_ref):
     core = meta[0] & 1
-    rows = mine.shape[1]
-    out_ref[pl.ds(aligned(core, rows), rows), :] = mine[0].astype(jnp.float32)
-    out_ref[pl.ds(aligned(1 - core, rows), rows), :] = other[0].astype(jnp.float32)
+    rows = mine_low.shape[1]
+    for at, low, high in ((core, mine_low, mine_high), (1 - core, other_low, other_high)):
+        out_ref[pl.ds(aligned(2 * at, rows), rows), :] = low[0].astype(jnp.float32)
+        out_ref[pl.ds(aligned(2 * at + 1, rows), rows), :] = high[0].astype(jnp.float32)
 
 
 def place_shared(meta, mine, other):
     _, rows, columns = mine.shape
-    units = columns // 3
-    block = pl.BlockSpec((1, rows, units), lambda i, j, m: (i, 0, j))
-    outs = shape_of((2 * rows, 4 * columns), jnp.float32)
+    units = columns // 6
+    low = pl.BlockSpec((1, rows, units), lambda i, j, m: (i, 0, j))
+    high = pl.BlockSpec((1, rows, units), lambda i, j, m: (i, 0, 3 + j))
+    outs = shape_of((4 * rows, 2 * columns), jnp.float32)
     return call(
         place_shared_kernel,
         "place_shared",
         meta,
-        [mine, other],
+        [mine, mine, other, other],
         (4, 3),
-        [block, block],
-        pl.BlockSpec((2 * rows, units), lambda i, j, m: (0, 4 * j + (m[1] ^ i))),
+        [low, high, low, high],
+        pl.BlockSpec((4 * rows, units), lambda i, j, m: (0, 4 * j + (m[1] ^ i))),
         outs,
         [],
         0,
-        size_of([mine, other, outs]),
+        0,
     )
 
 
@@ -1419,9 +1492,8 @@
         self.last = None
 
     def __call__(self, *values):
-        if self.last is None:
-            return values if len(values) > 1 else values[0]
-        held = lax.optimization_barrier(tuple(values) + (self.last,))[:-1]
+        last = () if self.last is None else (self.last,)
+        held = lax.optimization_barrier(tuple(values) + last)[: len(values)]
         return held if len(held) > 1 else held[0]
 
     def mark(self, value):
@@ -1429,16 +1501,13 @@
         return value
 
 
-SUMMED = 0
-SHARED_WITH = 0
 EARLY = (
-    "H", "W", "K", "K", "W", "S", "O", "K", "S", "W", "O", "M", "S", "O", "M", "S", "O", "O", "S", "M", "S", "M", "R", "K",
-    "M", "M", "K", "M", "R", "K", "M", "M", "K", "M", "R", "M", "M", "M", "M",
+    "H", "W", "K", "S", "K", "S", "W", "K", "O", "S", "S", "M", "M", "S", "O", "M", "S", "M", "R", "M", "K", "M", "K", "M",
+    "K", "R", "M", "K", "M", "M", "M", "M", "R", "M", "M",
 )
 LATE = (
-    "L", "2", "0", "2", "3", "0", "L", "3", "1", "2", "L", "1", "3", "L", "2", "O", "0", "3", "1", "O", "L", "2", "O", "3",
-    "0", "1", "O", "2", "3", "O", "L", "2", "Q", "O", "3", "Q", "0", "1", "L", "O", "Q", "O", "L", "Q", "Q", "1", "0", "S",
-    "Q", "1", "0", "L", "Q", "L", "Q", "S", "L", "L", "S",
+    "L", "0", "0", "1", "0", "L", "1", "1", "L", "L", "0", "1", "L", "O", "L", "1", "0", "O", "Q", "1", "O", "L", "Q", "0",
+    "O", "L", "Q", "Q", "O", "Q", "1", "0", "S", "L", "O", "Q", "1", "0", "O", "Q", "S", "L", "O", "Q", "S", "L", "L",
 )
 
 
@@ -1482,9 +1551,15 @@
     def now(*values):
         return clock(*values)
 
+    def ready(*values):
+        values = clock(*values)
+        clock.mark(values[0] if isinstance(values, tuple) or isinstance(values, list) else values)
+        return values
+
 
     def hidden_chain():
-        have["blocks"] = chips_swap([states] * 4)
+        own = ready(states)
+        have["blocks"] = [own] + [flip(own, 2 * r) for r in (1, 2, 3)]
         yield
 
     def qkv_chain():
@@ -1499,12 +1574,9 @@
             ],
             axis=1,
         )
-        came = line_swap(half, 1)
-        yield
-        pair = clock.mark(jnp.stack([half, now(came)]))
-        came = line_swap(pair, 2)
-        yield
-        have["qkv_mine"] = clock.mark(jnp.concatenate([pair, now(came)]))
+        came = line_exchange(ready(jnp.broadcast_to(half, (4,) + half.shape)))
+        yield
+        have["qkv_mine"] = clock.mark(now(came))
         have["qkv_other"] = flip(have["qkv_mine"], 1)
         yield
 
@@ -1558,16 +1630,13 @@
         piece = lax.dynamic_slice_in_dim(shared_weight, context_index * eighth, eighth, 0)
         piece = piece.reshape(eighth, 3, shard_count, units)
 
-        def columns(index):
-            part = lax.dynamic_index_in_dim(piece, shard_index ^ index, 2, keepdims=False)
-            return part.reshape(eighth, 3 * units)
-
-        first = now(jnp.stack([columns(0), columns(2)]))
-        came = line_swap(now(jnp.stack([columns(1), columns(3)])), 1)
+        piece = jnp.transpose(piece, (2, 0, 1, 3)).reshape(shard_count, eighth, 3 * units)
+        parts = [pick(piece, shard_index ^ i) for i in range(4)]
+        came = line_swap(now(jnp.stack([parts[1], parts[3]])), 1)
         yield
         came = now(came)
-        mine = jnp.stack([first[0], came[0]])
-        came = line_swap(clock.mark(jnp.stack([first[1], came[1]])), 2)
+        mine = jnp.stack([parts[0], came[0]])
+        came = line_swap(clock.mark(jnp.stack([parts[2], came[1]])), 2)
         yield
         pieces = clock.mark(jnp.concatenate([mine, now(came)]))
         came = flip(pieces, 2)
@@ -1584,21 +1653,10 @@
 
     def out_chain():
         half = lax.dynamic_slice_in_dim(now(out_weight), core * half_rows, half_rows, 0)
-        near = line_swap(half, 1)
-        yield
-        near = now(near)
-        middle = line_middle(now(half))
-        middle_far = line_middle(near)
-        yield
-        outward = line_outward(now(middle))
-        yield
-        outward_far = line_outward(now(middle_far))
-        yield
-        outward, outward_far = now(outward, outward_far)
-        third = jnp.where(at_end, outward, middle_far)
-        fourth = jnp.where(at_end, outward_far, middle)
-        have["out_mine"] = [half, near, third, fourth]
-        have["out_other"] = flip(clock.mark(jnp.stack(have["out_mine"])), 1)
+        came = line_exchange(ready(jnp.broadcast_to(half, (4,) + half.shape)))
+        yield
+        have["out_mine"] = clock.mark(now(came))
+        have["out_other"] = flip(have["out_mine"], 1)
         yield
 
     def qkv_all_chain():
@@ -1626,13 +1684,14 @@
         mixed_heads, log_total = attend(meta(), query, pair, pair_other, scale)
         clock.mark(log_total)
         have["attend"] = (query, pair, pair_other, log_total, mixed_heads)
-        mixed = chips_swap(mixed_heads)
+        parts = ready(*[pick(mixed_heads, chip ^ r) for r in range(4)])
+        mixed = [parts[0]] + [flip(parts[r], 2 * r) for r in (1, 2, 3)]
         have["mixed"] = mixed
         yield
-        out_rel, middle, normed_mid = leave(
+        out_full, middle, normed_mid = leave(
             meta(), mixed, have["out_mine"], have["out_other"], states, gains[1]
         )
-        have["out_rel"], have["middle"] = out_rel, middle
+        have["out_full"], have["middle"] = out_full, middle
         clock.mark(normed_mid)
 
         near, center = line_swap(normed_mid, 1), line_middle(normed_mid)
@@ -1668,8 +1727,7 @@
         inward, crossed = line_inward(carried), line_middle(carried)
         yield
         inward, crossed = now(inward, crossed)
-        near_out = clock.mark(outs[1] + crossed)
-        middle_out = clock.mark(outs[3] + inward)
+        near_out, middle_out = ready(outs[1] + crossed, outs[3] + inward)
         near_out, middle_out = line_swap(near_out, 1), line_middle(middle_out)
         yield
         near_out, middle_out = now(near_out, middle_out)
@@ -1727,25 +1785,24 @@
         inward, crossed = line_inward(carried), line_middle(carried)
         yield
         inward, crossed = now(inward, crossed)
-        near_out = clock.mark(outs[1] + crossed)
-        middle_out = clock.mark(outs[3] + inward)
+        near_out, middle_out = ready(outs[1] + crossed, outs[3] + inward)
         near_out, middle_out = line_swap(near_out, 1), line_middle(middle_out)
         yield
         near_out, middle_out = now(near_out, middle_out)
         grad_normed = clock.mark(
             outs[0].astype(f32) + near_out.astype(f32) + middle_out.astype(f32)
         )
-        grad_middle, grad_branch, grad_gain_mid, *grad_mixed = enter_back(
+        grad_middle, grad_branch, grad_gain_mid, grad_mixed = enter_back(
             meta(),
             have["grad_final"],
             grad_normed,
             have["middle"],
             have["gains"][1],
-            have["out_rel"],
+            have["out_full"],
         )
         clock.mark(grad_branch)
         have["grad_branch"], have["grad_gain_mid"] = grad_branch, grad_gain_mid
-        grad_mixed = chips_swap(grad_mixed)
+        grad_mixed = chips_exchange(ready(grad_mixed))
         yield
         query, pair, pair_other, log_total, mixed_heads = have["attend"]
         grad_query, grad_pair, grad_other = attend_back(
@@ -1757,7 +1814,7 @@
         grad_pair = grad_pair + now(came).astype(f32)
         projected = clock.mark(jnp.concatenate([grad_query, grad_pair.astype(bf16)], axis=-1))
         have["grad_projected"] = projected
-        parts = chips_swap([projected[r] for r in range(4)])
+        parts = chips_exchange(ready(projected))
         yield
         grad_hidden, grad_gain_in = finish(
             meta(),
@@ -1774,99 +1831,95 @@
             [grad_gain_in, have["grad_gain_mid"], jnp.full((6, width), have["squared"], f32)],
             axis=0,
         )
+        for offset in (1, 2):
+            came = line_swap(sums, offset)
+            yield
+            sums = clock.mark(sums + now(came))
         for bit in (1, 2, 4):
             came = flip(sums, bit)
             yield
             sums = clock.mark(sums + now(came))
-        for offset in (1, 2):
-            came = line_swap(sums, offset)
-            yield
-            sums = clock.mark(sums + now(came))
         own = lax.dynamic_slice_in_dim(sums, shard_index * shard_rows, shard_rows, 1)
         have["sums"] = (own, 0.5 * sums[2, 0] / (have["count"] * width))
         yield
 
-    def expert_chain(expert):
+    def expert_chain(index):
         line_rows, line_grads = have["line"]
         grad_gate_ups, acts, shared_grads, shared_acts = have["experts"][:4]
-        operands = [(line_rows, grad_gate_ups), (line_grads, acts)]
-        if expert == SHARED_WITH:
-            operands += [(line_rows, shared_grads), (line_grads, shared_acts)]
-        keep, give = weight_grad(meta(), chip, operands, expert)
-        clock.mark(keep)
-        came = flip(give, 1)
-        yield
-        came = now(came)
-        if expert % 2 == 0:
-            first, second = 2, 4
-            give = clock.mark(keep[1::2] + came[1::2])
-            keep = keep[0::2] + came[0::2]
-        else:
-            first, second = 4, 2
-            give = clock.mark(keep[2:] + came[2:])
-            keep = keep[:2] + came[:2]
+        shared = (shared_grads, shared_acts) if index == 0 else None
+
+        def grad_of(at):
+            return clock.mark(
+                expert_grad(
+                    meta(),
+                    2 * at + index,
+                    at,
+                    line_rows,
+                    line_grads,
+                    grad_gate_ups,
+                    acts,
+                    shared,
+                )
+            )
+
+        came = flip(grad_of(1 - core), 1)
+        yield
+        keep = grad_of(core)
+        yield
+        x_first = index % 2 == 0
+        first, second = (2, 4) if x_first else (4, 2)
+        picked = ((1, 3), (0, 2)) if x_first else ((2, 3), (0, 1))
+        pieces = keep.shape[1] // 96
+
+        def split_sum(keep, came):
+            return [
+                jnp.stack([keep[i] + came[i] for i in places]) for places in picked
+            ]
+
+        give, keep = blend(meta(), "blend_split", split_sum, [keep, came], pieces)
+        clock.mark(give)
         came = flip(give, first)
         yield
-        came = now(came)
-        give = clock.mark(keep[1] + came[1])
-        keep = keep[0] + came[0]
+        give, keep = blend(
+            meta(), "blend_pair", lambda k, c: [k[1] + c[1], k[0] + c[0]], [keep, came], pieces
+        )
+        clock.mark(give)
         came = flip(give, second)
         yield
-        own = clock.mark(keep + now(came))
+        own = clock.mark(blend(meta(), "blend_sum", lambda k, c: k + c, [keep, came], pieces))
         came = flip(own, second)
         yield
-        pair = clock.mark(jnp.stack([own, now(came)]))
+        pair = clock.mark(
+            blend(meta(), "blend_stack", lambda a, b: jnp.stack([a, b]), [own, came], pieces)
+        )
         came = flip(pair, first)
         yield
-        came = now(came)
-        if expert % 2 == 0:
-            mine = [own, came[0], pair[1], came[1]]
-        else:
-            mine = [own, pair[1], came[0], came[1]]
-        stacked = clock.mark(jnp.stack(mine))
+
+        def stack_four(near, far):
+            if x_first:
+                return jnp.stack([near[0], far[0], near[1], far[1]])
+            return jnp.stack([near[0], near[1], far[0], far[1]])
+
+        stacked = clock.mark(blend(meta(), "blend_four", stack_four, [pair, came], pieces))
         other = flip(stacked, 1)
-        if expert == SHARED_WITH:
-            have["shared_sum"] = stacked[:, :, 3 * F :]
-        yield
-        have["grad_experts"] = place_expert(
-            meta(), have.get("grad_experts"), expert, expert_weight.shape, mine, other
+        if index == 0:
+            have["shared_sum"] = stacked[:, shard_rows:]
+        yield
+        have["grad_experts"] = place_pair(
+            meta(), have.get("grad_experts"), index, expert_weight.shape, stacked, other
         )
         clock.mark(have["grad_experts"])
         yield
 
     def shared_grad_chain():
         total = now(have["shared_sum"])
-        parts = [pick(total, chip ^ shard_index ^ i) for i in range(4)]
-        parts = [parts[0]] + [line_swap(clock.mark(parts[i]), i) for i in (1, 2, 3)]
-        yield
-        mine = clock.mark(jnp.stack(now(*parts)))
+        parts = ready(*[pick(total, chip ^ shard_index ^ i) for i in range(4)])
+        came = [line_swap(parts[i], i) for i in (1, 2, 3)]
+        yield
+        mine = clock.mark(jnp.stack([parts[0]] + list(now(*came))))
         other = flip(mine, 1)
         yield
         have["grad_shared"] = clock.mark(place_shared(meta(), mine, other))
-        yield
-
-    def summed_chain():
-        line_rows, line_grads = have["line"]
-        grad_gate_ups, acts = have["experts"][:2]
-        sums = []
-        for expert in range(SUMMED):
-            sums.append(
-                weight_grad(
-                    meta(),
-                    jnp.int32(0),
-                    [(line_rows, grad_gate_ups), (line_grads, acts)],
-                    expert,
-                    split=False,
-                )
-            )
-            clock.mark(sums[-1])
-        sums = lax.psum(sums, "ctx")
-        yield
-        for expert in range(SUMMED):
-            have["grad_experts"] = place_total(
-                meta(), have.get("grad_experts"), expert, expert_weight.shape, sums[expert]
-            )
-            clock.mark(have["grad_experts"])
         yield
 
     def line_reduce_steps(keep, came):
@@ -1878,8 +1931,7 @@
         inward, crossed = line_inward(carried), line_middle(carried)
         yield
         inward, crossed = now(inward, crossed)
-        near_out = clock.mark(parts[1] + crossed)
-        middle_out = clock.mark(parts[3] + inward)
+        near_out, middle_out = ready(parts[1] + crossed, parts[3] + inward)
         near_out, middle_out = line_swap(near_out, 1), line_middle(middle_out)
         yield
         near_out, middle_out = now(near_out, middle_out)
@@ -1950,10 +2002,8 @@
         "O": out_grad_chain(),
         "Q": qkv_grad_chain(),
     }
-    if SUMMED:
-        late["A"] = summed_chain()
-    for expert in range(SUMMED, local_experts):
-        late[str(expert)] = expert_chain(expert)
+    for index in range(local_experts // 2):
+        late[str(index)] = expert_chain(index)
     for chains, order in ((early, EARLY), (late, LATE)):
         for name in order:
             next(chains[name], None)

time: 853 us -> 833 us (0.977)
  starting transfers between devices: 171 us -> 134 us
  waiting for transfers between devices: 310 us -> 273 us
  Pallas kernels: 259 us -> 293 us
  local copies, waits for them, and re-layouts: 38.9 us -> 72 us
  other arithmetic: 63.1 us -> 41.8 us
    ppermute x61 -> x43, waiting for transfers between devices: 165 us -> 107 us  [flip(): lax.ppermute(value, 'ctx', [(index, index ^ bit) for index in range(8)])]
    ppermute x18 -> x15, waiting for transfers between devices: 66.6 us -> 103 us  [line_swap(): lax.ppermute(value, 'wt', [(index, index ^ offset) for index in range(4)])]
    pallas_call x23 -> x33, Pallas kernels: 235 us -> 269 us  [call(): pl.pallas_call(kernel, grid_spec=pltpu.PrefetchScalarGridSpec(num_scalar_...]
    unnamed x225 -> x321, local copies, waits for them, and re-layouts: 24 us -> 51.1 us
    ppermute x6 -> x4, waiting for transfers between devices: 29 us -> 5.89 us  [line_outward(): return lax.ppermute(value, 'wt', [(1, 0), (2, 3)])]
    all_to_all x0 -> x4, starting transfers between devices: none -> 19.6 us  [the longest x2 11 us: line_exchange(): return lax.all_to_all(blocks, 'wt', split_axis=0, concat_axis=0, tiled=True)]
    ppermute x61 -> x43, starting transfers between devices: 47.6 us -> 28.9 us  [flip(): lax.ppermute(value, 'ctx', [(index, index ^ bit) for index in range(8)])]
    all_to_all x0 -> x4, waiting for transfers between devices: none -> 18.4 us  [the longest x2 17.8 us: chips_exchange(): lax.all_to_all(blocks, 'ctx', split_axis=0, concat_axis=0, tiled=True, ax...]
  transfers between devices with their start and end apart: 107 -> 86, of which waited for: 40 -> 32; matrix products, arithmetic and copies ran while one was open for 8% -> 6% of each run, Pallas kernels for 26% -> 30%
where the time goes in v4:
time: 833 us; the launch traced here: 820 us
  Pallas kernels  293 us (35%)
  waiting for transfers between devices  273 us (33%)
  starting transfers between devices  134 us (16%)
  local copies, waits for them, and re-layouts  72 us (9%)
  other arithmetic  41.8 us (5%)
    pallas_call x33, Pallas kernels, call(): pl.pallas_call(kernel, grid_spec=pltpu.PrefetchScalarGridSpec(num_scalar_...  269 us
    ppermute x43, waiting for transfers between devices, flip(): lax.ppermute(value, 'ctx', [(index, index ^ bit) for index in range(8)])  107 us
    ppermute x15, waiting for transfers between devices, line_swap(): lax.ppermute(value, 'wt', [(index, index ^ offset) for index in range(4)])  103 us
    unnamed x321, local copies, waits for them, and re-layouts  51.1 us
    ppermute x8, waiting for transfers between devices, line_inward(): return lax.ppermute(value, 'wt', [(0, 1), (3, 2)])  38.5 us
    ppermute x15, starting transfers between devices, line_swap(): lax.ppermute(value, 'wt', [(index, index ^ offset) for index in range(4)])  35.1 us
    ppermute x8, starting transfers between devices, line_inward(): return lax.ppermute(value, 'wt', [(0, 1), (3, 2)])  31.6 us
    ppermute x43, starting transfers between devices, flip(): lax.ppermute(value, 'ctx', [(index, index ^ bit) for index in range(8)])  28.9 us
  transfers between devices with their start and end apart: 86, of which 32 were waited for; matrix products, arithmetic and copies ran while one was open for 6% of the time, Pallas kernels for 30%

profile of v4, /device:TPU:0, one launch (start us, length us, event | category | flops | bytes accessed | tf_op | source)
XLA Modules:
  0.0 819.8 jit_solution(10962388436231673611)
XLA Ops:
  4.0 6.3 all-to-all-start
  16.6 13.6 %collective-permute-done = f32[32,256]{1,0:T(8,128)S(1)} collective-permute-done((f32[32,256]{1,0:T(8,128)S(1)}, f32[32,256]{1,0:T(8,128)S(1)}, u32[]{:S(2)}, u32[]{:S(2)}) %collective-permute-start) | collective-permute-done | bytes 32800 | tf_op jit(solution)/shard_map/ppermute | solution.py:474
  30.2 4.7 collective-permute-start.1
  40.7 4.6 all-to-all-start.1
  51.9 52.0 %collective-permute-done.3 = bf16[2,48,768]{2,1,0:T(8,128)(2,1)S(1)} collective-permute-done((bf16[2,48,768]{2,1,0:T(8,128)(2,1)S(1)}, bf16[2,48,768]{2,1,0:T(8,128)(2,1)S(1)}, u32[]{:S(2)}, u32[]{:S(2)}) %collective-permute-start.3) | collective-permute-done | bytes 147488 | tf_op jit(solution)/shard_map/ppermute | solution.py:474
  106.1 5.8 collective-permute-done.4
  114.9 7.3 project.1
  127.8 10.7 %attend.1 = (bf16[4,256,384]{2,1,0:T(8,128)(2,1)S(1)}, f32[8,1,384]{2,1,0:T(1,128)S(1)}) custom-call(s32[2]{0:T(128)S(1)} %pad_add_fusion.meta.meta_ref, bf16[4,256,384]{2,1,0:T(8,128)(2,1)S(1)} %copy-done.47, bf16[4,256,256]{2,1,0:T(8,128)(2,1)S(1)} %copy-done.58, bf16[4,256,256]{2,1,0:T(8,128)(2,1)S(1)} %collective-permute-done.10.other_ref), custom_call_target="tpu_custom_call" | custom-call | flops 300000000 | bytes 1000 | tf_op jit(solution)/shard_map/attend/pallas_call | solution.py:585
  156.5 6.2 leave.1
  171.6 11.7 %experts.4 = (bf16[4,256,1024]{2,1,0:T(8,128)(2,1)S(1)}, bf16[256,512]{1,0:T(8,128)(2,1)S(1)}, bf16[256,1536]{1,0:T(8,128)(2,1)S(1)}) custom-call(s32[2]{0:T(128)S(1)} %pad_add_fusion.meta.meta_ref, bf16[256,1536]{1,0:T(8,128)(2,1)S(1)} %get-tuple-element.215.rows_ref.refs_0_, f32[4,256,1]{2,1,0:T(8,128)S(1)} %copy-done.38, ...), custom_call_target="tpu_custom_call" | custom-call | flops 300000000 | bytes 1000 | tf_op jit(solution)/shard_map/experts/pallas_call | solution.py:585
  192.3 12.0 %experts.5 = (bf16[4,256,1024]{2,1,0:T(8,128)(2,1)S(1)}, bf16[256,512]{1,0:T(8,128)(2,1)S(1)}, bf16[256,1536]{1,0:T(8,128)(2,1)S(1)}) custom-call(s32[2]{0:T(128)S(1)} %pad_add_fusion.meta.meta_ref, bf16[256,1536]{1,0:T(8,128)(2,1)} %collective-permute-done.16.rows_ref.refs_1_, f32[4,256,1]{2,1,0:T(8,128)S(1)} %copy.40.gates_ref, ...), custom_call_target="tpu_custom_call" | custom-call | flops 300000000 | bytes 1000 | tf_op jit(solution)/shard_map/experts/pallas_call | solution.py:585
  215.6 11.7 %experts.6 = (bf16[4,256,1024]{2,1,0:T(8,128)(2,1)S(1)}, bf16[256,512]{1,0:T(8,128)(2,1)S(1)}, bf16[256,1536]{1,0:T(8,128)(2,1)S(1)}) custom-call(s32[2]{0:T(128)S(1)} %pad_add_fusion.meta.meta_ref, bf16[256,1536]{1,0:T(8,128)(2,1)S(1)} %broadcast_select_fusion.3.rows_ref.refs_2_, f32[4,256,1]{2,1,0:T(8,128)S(1)} %copy-done.36, ...), custom_call_target="tpu_custom_call" | custom-call | flops 300000000 | bytes 1000 | tf_op jit(solution)/shard_map/experts/pallas_call | solution.py:585
  230.4 11.7 %experts.7 = (bf16[4,256,1024]{2,1,0:T(8,128)(2,1)S(1)}, bf16[256,512]{1,0:T(8,128)(2,1)S(1)}, bf16[256,1536]{1,0:T(8,128)(2,1)S(1)}) custom-call(s32[2]{0:T(128)S(1)} %pad_add_fusion.meta.meta_ref, bf16[256,1536]{1,0:T(8,128)(2,1)S(1)} %broadcast_select_fusion.2.rows_ref.refs_3_, f32[4,256,1]{2,1,0:T(8,128)S(1)} %copy-done.34, ...), custom_call_target="tpu_custom_call" | custom-call | flops 300000000 | bytes 1000 | tf_op jit(solution)/shard_map/experts/pallas_call | solution.py:585
  242.1 4.9 collective-permute-start.22
  251.0 13.5 %collective-permute-done.22 = bf16[256,1536]{1,0:T(8,128)(2,1)S(1)} collective-permute-done((bf16[256,1536]{1,0:T(8,128)(2,1)S(1)}, bf16[256,1536]{1,0:T(8,128)(2,1)S(1)}, u32[]{:S(2)}, u32[]{:S(2)}) %collective-permute-start.22) | collective-permute-done | bytes 786464 | tf_op jit(solution)/shard_map/ppermute | solution.py:486
  264.6 4.8 collective-permute-start.25
  273.9 11.8 %collective-permute-done.25 = bf16[256,1536]{1,0:T(8,128)(2,1)S(1)} collective-permute-done((bf16[256,1536]{1,0:T(8,128)(2,1)S(1)}, bf16[256,1536]{1,0:T(8,128)(2,1)S(1)}, u32[]{:S(2)}, u32[]{:S(2)}) %collective-permute-start.25) | collective-permute-done | bytes 786464 | tf_op jit(solution)/shard_map/ppermute | solution.py:486
  292.9 14.0 %collective-permute-done.28 = bf16[256,1536]{1,0:T(8,128)(2,1)S(1)} collective-permute-done((bf16[256,1536]{1,0:T(8,128)(2,1)S(1)}, bf16[256,1536]{1,0:T(8,128)(2,1)S(1)}, u32[]{:S(2)}, u32[]{:S(2)}) %collective-permute-start.28) | collective-permute-done | bytes 786464 | tf_op jit(solution)/shard_map/ppermute | solution.py:474
  314.4 13.0 %experts_back.4 = (bf16[4,256,1024]{2,1,0:T(8,128)(2,1)S(1)}, bf16[4,256,512]{2,1,0:T(8,128)(2,1)S(1)}, bf16[1,256,512]{2,1,0:T(8,128)(2,1)S(1)}, bf16[1,256,256]{2,1,0:T(8,128)(2,1)S(1)}, bf16[256,1536]{1,0:T(8,128)(2,1)S(1)}) custom-call(s32[2]{0:T(128)S(1)} %pad_add_fusion.meta.meta_ref, bf16[256,1536]{1,0:T(8,128)(2,1)S(1)} %get-tuple-element.377.grad_ref.refs_4_, ...), custom_call_target="tpu_custom_call" | custom-call | flops 300000000 | bytes 1000 | tf_op jit(solution)/shard_map/experts_back/pallas_call | solution.py:585
  333.7 13.0 %experts_back.5 = (bf16[4,256,1024]{2,1,0:T(8,128)(2,1)S(1)}, bf16[4,256,512]{2,1,0:T(8,128)(2,1)S(1)}, bf16[1,256,512]{2,1,0:T(8,128)(2,1)S(1)}, bf16[1,256,256]{2,1,0:T(8,128)(2,1)S(1)}, bf16[256,1536]{1,0:T(8,128)(2,1)S(1)}) custom-call(s32[2]{0:T(128)S(1)} %pad_add_fusion.meta.meta_ref, bf16[256,1536]{1,0:T(8,128)(2,1)S(1)} %collective-permute-done.30.grad_ref.refs_5_, ...), custom_call_target="tpu_custom_call" | custom-call | flops 300000000 | bytes 1000 | tf_op jit(solution)/shard_map/experts_back/pallas_call | solution.py:585
  357.2 13.0 %experts_back.6 = (bf16[4,256,1024]{2,1,0:T(8,128)(2,1)S(1)}, bf16[4,256,512]{2,1,0:T(8,128)(2,1)S(1)}, bf16[1,256,512]{2,1,0:T(8,128)(2,1)S(1)}, bf16[1,256,256]{2,1,0:T(8,128)(2,1)S(1)}, bf16[256,1536]{1,0:T(8,128)(2,1)S(1)}) custom-call(s32[2]{0:T(128)S(1)} %pad_add_fusion.meta.meta_ref, bf16[256,1536]{1,0:T(8,128)(2,1)S(1)} %broadcast_select_fusion.1.grad_ref.refs_6_, ...), custom_call_target="tpu_custom_call" | custom-call | flops 300000000 | bytes 1000 | tf_op jit(solution)/shard_map/experts_back/pallas_call | solution.py:585
  373.7 13.5 %experts_back.7 = (bf16[4,256,1024]{2,1,0:T(8,128)(2,1)S(1)}, bf16[4,256,512]{2,1,0:T(8,128)(2,1)S(1)}, bf16[1,256,512]{2,1,0:T(8,128)(2,1)S(1)}, bf16[1,256,256]{2,1,0:T(8,128)(2,1)S(1)}, bf16[256,1536]{1,0:T(8,128)(2,1)S(1)}) custom-call(s32[2]{0:T(128)S(1)} %pad_add_fusion.meta.meta_ref, bf16[256,1536]{1,0:T(8,128)(2,1)S(1)} %broadcast_select_fusion.grad_ref.refs_7_, ...), custom_call_target="tpu_custom_call" | custom-call | flops 300000000 | bytes 1000 | tf_op jit(solution)/shard_map/experts_back/pallas_call | solution.py:585
  389.7 13.0 %expert_grad.4 = bf16[4,480,1536]{2,1,0:T(8,128)(2,1)} custom-call(s32[3]{0:T(128)S(1)} %add_add_fusion.meta, bf16[256,1536]{1,0:T(8,128)(2,1)S(1)} %copy-done.18, bf16[256,1536]{1,0:T(8,128)(2,1)} %collective-permute-done.16.rows_ref.refs_1_, bf16[256,1536]{1,0:T(8,128)(2,1)S(1)} %broadcast_select_fusion.3.rows_ref.refs_2_, ...), custom_call_target="tpu_custom_call" | custom-call | flops 300000000 | bytes 1000 | tf_op jit(solution)/shard_map/expert_grad/pallas_call | solution.py:585
  411.6 12.9 %expert_grad.5.refs_0_ = bf16[4,480,1536]{2,1,0:T(8,128)(2,1)} custom-call(s32[3]{0:T(128)S(1)} %add_add_fusion.1.meta, bf16[256,1536]{1,0:T(8,128)(2,1)S(1)} %copy-done.19, bf16[256,1536]{1,0:T(8,128)(2,1)} %collective-permute-done.16.rows_ref.refs_1_, bf16[256,1536]{1,0:T(8,128)(2,1)S(1)} %broadcast_select_fusion.3.rows_ref.refs_2_, ...), custom_call_target="tpu_custom_call" | custom-call | flops 300000000 | bytes 1000 | tf_op jit(solution)/shard_map/expert_grad/pallas_call | solution.py:585
  424.6 10.1 %expert_grad.6 = bf16[4,384,1536]{2,1,0:T(8,128)(2,1)} custom-call(s32[3]{0:T(128)S(1)} %add_add_fusion.2.meta, bf16[256,1536]{1,0:T(8,128)(2,1)S(1)} %copy-done.19, bf16[256,1536]{1,0:T(8,128)(2,1)} %collective-permute-done.16.rows_ref.refs_1_, bf16[256,1536]{1,0:T(8,128)(2,1)S(1)} %broadcast_select_fusion.3.rows_ref.refs_2_, ...), custom_call_target="tpu_custom_call" | custom-call | flops 300000000 | bytes 1000 | tf_op jit(solution)/shard_map/expert_grad/pallas_call | solution.py:585
  435.2 4.8 collective-permute-start.36
  440.1 7.8 blend_split.2
  449.9 7.2 collective-permute-done.36
  458.2 5.3 collective-permute-start.38
  467.8 10.1 %expert_grad.7.refs_0_ = bf16[4,384,1536]{2,1,0:T(8,128)(2,1)} custom-call(s32[3]{0:T(128)S(1)} %add_add_fusion.3.meta, bf16[256,1536]{1,0:T(8,128)(2,1)S(1)} %copy-done.20, bf16[256,1536]{1,0:T(8,128)(2,1)} %collective-permute-done.16.rows_ref.refs_1_, bf16[256,1536]{1,0:T(8,128)(2,1)S(1)} %broadcast_select_fusion.3.rows_ref.refs_2_, ...), custom_call_target="tpu_custom_call" | custom-call | flops 300000000 | bytes 1000 | tf_op jit(solution)/shard_map/expert_grad/pallas_call | solution.py:585
  477.9 6.1 blend_split.3
  488.8 17.7 %collective-permute-done.41 = bf16[256,1536]{1,0:T(8,128)(2,1)S(1)} collective-permute-done((bf16[256,1536]{1,0:T(8,128)(2,1)S(1)}, bf16[256,1536]{1,0:T(8,128)(2,1)S(1)}, u32[]{:S(2)}, u32[]{:S(2)}) %collective-permute-start.41) | collective-permute-done | bytes 786464 | tf_op jit(solution)/shard_map/ppermute | solution.py:474
  508.1 7.2 enter_back.1
  527.5 15.2 %collective-permute-done.44.refs_1_ = bf16[2,384,1536]{2,1,0:T(8,128)(2,1)} collective-permute-done((bf16[2,384,1536]{2,1,0:T(8,128)(2,1)}, bf16[2,384,1536]{2,1,0:T(8,128)(2,1)}, u32[]{:S(2)}, u32[]{:S(2)}) %collective-permute-start.44) | collective-permute-done | bytes 2359328 | tf_op jit(solution)/shard_map/ppermute | solution.py:470
  551.4 15.4 %attend_back.1 = (bf16[4,256,384]{2,1,0:T(8,128)(2,1)S(1)}, f32[4,256,256]{2,1,0:T(8,128)S(1)}, bf16[4,256,256]{2,1,0:T(8,128)(2,1)S(1)}) custom-call(s32[2]{0:T(128)S(1)} %pad_add_fusion.meta.meta_ref, bf16[4,256,384]{2,1,0:T(8,128)(2,1)S(1)} %copy-done.48, bf16[4,256,256]{2,1,0:T(8,128)(2,1)S(1)} %copy-done.59, bf16[4,256,256]{2,1,0:T(8,128)(2,1)S(1)} %copy-done.61, ...), custom_call_target="tpu_custom_call" | custom-call | flops 300000000 | bytes 1000 | tf_op jit(solution)/shard_map/attend_back/pallas_call | solution.py:585
  573.7 6.9 collective-permute-done.46
  581.9 17.9 %collective-permute-done.47.refs_1_ = bf16[384,1536]{1,0:T(8,128)(2,1)S(1)} collective-permute-done((bf16[384,1536]{1,0:T(8,128)(2,1)S(1)}, bf16[384,1536]{1,0:T(8,128)(2,1)S(1)}, u32[]{:S(2)}, u32[]{:S(2)}) %collective-permute-start.47) | collective-permute-done | bytes 1179680 | tf_op jit(solution)/shard_map/ppermute | solution.py:470
  617.4 6.8 weight_grad.3
  640.5 17.8 %all-to-all-done.3.refs_0_ = bf16[4,256,640]{2,1,0:T(8,128)(2,1)} async-done(((bf16[4,256,640]{2,1,0:T(8,128)(2,1)}), bf16[4,256,640]{2,1,0:T(8,128)(2,1)}, u32[]{:S(2)}, u32[]{:S(2)}) %all-to-all-start.3) | async-done | bytes 1310752 | tf_op jit(solution)/shard_map/all_to_all | solution.py:516
  658.3 8.8 %finish.1 = (f32[1,256,1536]{2,1,0:T(8,128)}, f32[1,1536]{1,0:T(1,128)S(1)}) custom-call(s32[2]{0:T(128)S(1)} %pad_add_fusion.meta.meta_ref, bf16[4,256,640]{2,1,0:T(8,128)(2,1)} %all-to-all-done.3.refs_0_, bf16[4,768,640]{2,1,0:T(8,128)(2,1)} %pad_maximum_fusion.refs_1_, bf16[4,768,640]{2,1,0:T(8,128)(2,1)} %collective-permute-done.51.refs_2_, ...), custom_call_target="tpu_custom_call" | custom-call | flops 300000000 | bytes 1000 | tf_op jit(solution)/shard_map/finish/pallas_call | solution.py:585
  686.7 5.6 collective-permute-done.59
  694.1 12.6 %collective-permute-start.61 = (bf16[192,640]{1,0:T(8,128)(2,1)S(1)}, bf16[192,640]{1,0:T(8,128)(2,1)S(1)}, u32[]{:S(2)}, u32[]{:S(2)}) collective-permute-start(bf16[192,640]{1,0:T(8,128)(2,1)S(1)} %bitcast_add_fusion.3), channel_id=1, source_target_pairs={{0,1},{1,0},{2,3},{3,2},{4,5},{5,4},{6,7},{7,6},{8,9},{9,8},{10,11... | collective-permute-start | bytes 737288 | tf_op jit(solution)/shard_map/ppermute | solution.py:474
  711.9 5.7 blend_four.2.refs_0_
  717.7 17.0 %collective-permute-done.66.refs_1_ = bf16[2,480,1536]{2,1,0:T(8,128)(2,1)S(1)} collective-permute-done((bf16[2,480,1536]{2,1,0:T(8,128)(2,1)S(1)}, bf16[2,480,1536]{2,1,0:T(8,128)(2,1)S(1)}, u32[]{:S(2)}, u32[]{:S(2)}) %collective-permute-start.66) | collective-permute-done | bytes 2949152 | tf_op jit(solution)/shard_map/ppermute | solution.py:470
  744.5 11.5 %collective-permute-done.72 = bf16[192,1536]{1,0:T(8,128)(2,1)S(1)} collective-permute-done((bf16[192,1536]{1,0:T(8,128)(2,1)S(1)}, bf16[192,1536]{1,0:T(8,128)(2,1)S(1)}, u32[]{:S(2)}, u32[]{:S(2)}) %collective-permute-start.72) | collective-permute-done | bytes 589856 | tf_op jit(solution)/shard_map/ppermute | solution.py:470
  764.9 12.3 %place_pair.2.refs_0_ = f32[4,1536,1536]{2,1,0:T(8,128)} custom-call(s32[2]{0:T(128)S(1)} %pad_add_fusion.meta.meta_ref, bf16[4,384,1536]{2,1,0:T(8,128)(2,1)} %blend_four.2.refs_0_, bf16[4,384,1536]{2,1,0:T(8,128)(2,1)} %collective-permute-done.75.refs_1_), custom_call_target="tpu_custom_call" | custom-call | flops 300000000 | bytes 1000 | tf_op jit(solution)/shard_map/place_pair/pallas_call | solution.py:1373
  777.2 11.6 %place_pair.3 = f32[4,1536,1536]{2,1,0:T(8,128)} custom-call(s32[2]{0:T(128)S(1)} %pad_add_fusion.meta.meta_ref, f32[4,1536,1536]{2,1,0:T(8,128)} %place_pair.2.refs_0_, bf16[4,480,1536]{2,1,0:T(8,128)(2,1)S(1)} %bitcast.104, bf16[4,480,1536]{2,1,0:T(8,128)(2,1)} %collective-permute-done.76.refs_2_), custom_call_target="tpu_custom_call", output_to_operand_aliasing={{}: (1, {})} | custom-call | flops 300000000 | bytes 1000 | tf_op jit(solution)/shard_map/place_pair/pallas_call | solution.py:1373
  804.1 8.2 place_shared.1
  (588 shorter events, 278.2 us)
Async XLA Ops:
  4.0 31.5 %all-to-all-start = ((bf16[4,192,640]{2,1,0:T(8,128)(2,1)}), bf16[4,192,640]{2,1,0:T(8,128)(2,1)S(1)}, u32[]{:S(2)}, u32[]{:S(2)}) async-start(bf16[4,192,640]{2,1,0:T(8,128)(2,1)} %broadcast_in_dim.54), calls=%async_computation | async-start | bytes 1966080 | tf_op jit(solution)/shard_map/all_to_all | solution.py:527
  12.9 22.0 %collective-permute-start.2 = (bf16[2,48,768]{2,1,0:T(8,128)(2,1)S(1)}, bf16[2,48,768]{2,1,0:T(8,128)(2,1)S(1)}, u32[]{:S(2)}, u32[]{:S(2)}) collective-permute-start(bf16[2,48,768]{2,1,0:T(8,128)(2,1)S(1)} %pad_maximum_fusion.11), channel_id=1, source_target_pairs={{0,1},{1,0},{2,3},{3,2},{4,5},{5,4},{6,7},{7,6},{8,9},{9,8},{10,11... | collective-permute-start | bytes 442376 | tf_op jit(solution)/shard_map/ppermute | solution.py:474
  40.7 101.5 %all-to-all-start.1 = ((bf16[4,192,1536]{2,1,0:T(8,128)(2,1)}), bf16[4,192,1536]{2,1,0:T(8,128)(2,1)}, u32[]{:S(2)}, u32[]{:S(2)}) async-start(bf16[4,192,1536]{2,1,0:T(8,128)(2,1)} %broadcast_in_dim.55), calls=%async_computation.1 | async-start | bytes 4718592 | tf_op jit(solution)/shard_map/all_to_all | solution.py:527
  45.3 68.5 %collective-permute-start.9 = (bf16[4,192,640]{2,1,0:T(8,128)(2,1)S(1)}, bf16[4,192,640]{2,1,0:T(8,128)(2,1)}, u32[]{:S(2)}, u32[]{:S(2)}) collective-permute-start(bf16[4,192,640]{2,1,0:T(8,128)(2,1)S(1)} %copy-done.45), channel_id=1, source_target_pairs={{0,4},{4,0},{8,12},{12,8},{16,20},{20,16},{24,28},{28,24},{1,5},{5... | collective-permute-start | bytes 2949128 | tf_op jit(solution)/shard_map/ppermute | solution.py:470
  45.4 67.5 %collective-permute-start.6 = (bf16[256,1536]{1,0:T(8,128)(2,1)S(1)}, bf16[256,1536]{1,0:T(8,128)(2,1)S(1)}, u32[]{:S(2)}, u32[]{:S(2)}) collective-permute-start(bf16[256,1536]{1,0:T(8,128)(2,1)S(1)} %bitcast.105), channel_id=1, source_target_pairs={{0,8},{4,12},{8,0},{12,4},{16,24},{20,28},{24,16},{28,20},{1,9},{5... | collective-permute-start | bytes 2359304 | tf_op jit(solution)/shard_map/ppermute | solution.py:470
  47.0 66.8 %collective-permute-start.7 = (bf16[256,1536]{1,0:T(8,128)(2,1)S(1)}, bf16[256,1536]{1,0:T(8,128)(2,1)}, u32[]{:S(2)}, u32[]{:S(2)}) collective-permute-start(bf16[256,1536]{1,0:T(8,128)(2,1)S(1)} %bitcast.106), channel_id=1, source_target_pairs={{0,16},{4,20},{8,24},{12,28},{16,0},{20,4},{24,8},{28,12},{1,17},{... | collective-permute-start | bytes 2359304 | tf_op jit(solution)/shard_map/ppermute | solution.py:470
  48.4 65.3 %collective-permute-start.8 = (bf16[256,1536]{1,0:T(8,128)(2,1)S(1)}, bf16[256,1536]{1,0:T(8,128)(2,1)}, u32[]{:S(2)}, u32[]{:S(2)}) collective-permute-start(bf16[256,1536]{1,0:T(8,128)(2,1)S(1)} %bitcast.107), channel_id=1, source_target_pairs={{0,24},{4,28},{8,16},{12,20},{16,8},{20,12},{24,0},{28,4},{1,25},{... | collective-permute-start | bytes 2359304 | tf_op jit(solution)/shard_map/ppermute | solution.py:470
  49.0 54.9 %collective-permute-start.3 = (bf16[2,48,768]{2,1,0:T(8,128)(2,1)S(1)}, bf16[2,48,768]{2,1,0:T(8,128)(2,1)S(1)}, u32[]{:S(2)}, u32[]{:S(2)}) collective-permute-start(bf16[2,48,768]{2,1,0:T(8,128)(2,1)S(1)} %pad_maximum_fusion.12), channel_id=1, source_target_pairs={{0,2},{1,3},{2,0},{3,1},{4,6},{5,7},{6,4},{7,5},{8,10},{9,11},{10,... | collective-permute-start | bytes 442376 | tf_op jit(solution)/shard_map/ppermute | solution.py:474
  142.2 25.0 %collective-permute-start.15 = (bf16[4,4,48,768]{3,2,1,0:T(8,128)(2,1)}, bf16[4,4,48,768]{3,2,1,0:T(8,128)(2,1)}, u32[]{:S(2)}, u32[]{:S(2)}) collective-permute-start(bf16[4,4,48,768]{3,2,1,0:T(8,128)(2,1)} %pad_maximum_fusion.3.mine), channel_id=1, source_target_pairs={{0,4},{4,0},{8,12},{12,8},{16,20},{20,16},{24,28},{28,24},{1,5},{5... | collective-permute-start | bytes 3538952 | tf_op jit(solution)/shard_map/ppermute | solution.py:470
  163.8 21.7 %collective-permute-start.16 = (bf16[256,1536]{1,0:T(8,128)(2,1)S(1)}, bf16[256,1536]{1,0:T(8,128)(2,1)}, u32[]{:S(2)}, u32[]{:S(2)}) collective-permute-start(bf16[256,1536]{1,0:T(8,128)(2,1)S(1)} %get-tuple-element.215.rows_ref.refs_0_), channel_id=1, source_target_pairs={{0,1},{1,0},{2,3},{3,2},{4,5},{5,4},{6,7},{7,6},{8,9},{9,8},{10,11... | collective-permute-start | bytes 2359304 | tf_op jit(solution)/shard_map/ppermute | solution.py:474
  163.9 21.7 %collective-permute-start.17 = (bf16[256,1536]{1,0:T(8,128)(2,1)S(1)}, bf16[256,1536]{1,0:T(8,128)(2,1)}, u32[]{:S(2)}, u32[]{:S(2)}) collective-permute-start(bf16[256,1536]{1,0:T(8,128)(2,1)S(1)} %get-tuple-element.215.rows_ref.refs_0_), channel_id=1, source_target_pairs={{1,2},{2,1},{5,6},{6,5},{9,10},{10,9},{13,14},{14,13},{17,18},{18,... | collective-permute-start | bytes 2359304 | tf_op jit(solution)/shard_map/ppermute | solution.py:478
  187.2 22.2 %collective-permute-start.19 = (bf16[256,1536]{1,0:T(8,128)(2,1)}, bf16[256,1536]{1,0:T(8,128)(2,1)}, u32[]{:S(2)}, u32[]{:S(2)}) collective-permute-start(bf16[256,1536]{1,0:T(8,128)(2,1)} %collective-permute-done.17), channel_id=1, source_target_pairs={{1,0},{2,3},{5,4},{6,7},{9,8},{10,11},{13,12},{14,15},{17,16},{18,... | collective-permute-start | bytes 2359304 | tf_op jit(solution)/shard_map/ppermute | solution.py:482
  212.0 38.7 %collective-permute-start.23 = (bf16[768,640]{1,0:T(8,128)(2,1)S(1)}, bf16[768,640]{1,0:T(8,128)(2,1)S(1)}, u32[]{:S(2)}, u32[]{:S(2)}) collective-permute-start(bf16[768,640]{1,0:T(8,128)(2,1)S(1)} %constant_dynamic-slice_fusion.1), channel_id=1, source_target_pairs={{0,8},{4,12},{8,0},{12,4},{16,24},{20,28},{24,16},{28,20},{1,9},{5... | collective-permute-start | bytes 2949128 | tf_op jit(solution)/shard_map/ppermute | solution.py:470
  242.1 22.3 %collective-permute-start.22 = (bf16[256,1536]{1,0:T(8,128)(2,1)S(1)}, bf16[256,1536]{1,0:T(8,128)(2,1)S(1)}, u32[]{:S(2)}, u32[]{:S(2)}) collective-permute-start(bf16[256,1536]{1,0:T(8,128)(2,1)S(1)} %get-tuple-element.231), channel_id=1, source_target_pairs={{0,1},{3,2},{4,5},{7,6},{8,9},{11,10},{12,13},{15,14},{16,17},{19,... | collective-permute-start | bytes 2359304 | tf_op jit(solution)/shard_map/ppermute | solution.py:486
  264.6 21.0 %collective-permute-start.25 = (bf16[256,1536]{1,0:T(8,128)(2,1)S(1)}, bf16[256,1536]{1,0:T(8,128)(2,1)S(1)}, u32[]{:S(2)}, u32[]{:S(2)}) collective-permute-start(bf16[256,1536]{1,0:T(8,128)(2,1)S(1)} %add.250), channel_id=1, source_target_pairs={{0,1},{3,2},{4,5},{7,6},{8,9},{11,10},{12,13},{15,14},{16,17},{19,... | collective-permute-start | bytes 2359304 | tf_op jit(solution)/shard_map/ppermute | solution.py:486
  286.1 20.8 %collective-permute-start.28 = (bf16[256,1536]{1,0:T(8,128)(2,1)S(1)}, bf16[256,1536]{1,0:T(8,128)(2,1)S(1)}, u32[]{:S(2)}, u32[]{:S(2)}) collective-permute-start(bf16[256,1536]{1,0:T(8,128)(2,1)S(1)} %add.252), channel_id=1, source_target_pairs={{0,1},{1,0},{2,3},{3,2},{4,5},{5,4},{6,7},{7,6},{8,9},{9,8},{10,11... | collective-permute-start | bytes 2359304 | tf_op jit(solution)/shard_map/ppermute | solution.py:474
  291.1 55.7 %collective-permute-start.34 = (bf16[2,768,640]{2,1,0:T(8,128)(2,1)S(1)}, bf16[2,768,640]{2,1,0:T(8,128)(2,1)S(1)}, u32[]{:S(2)}, u32[]{:S(2)}) collective-permute-start(bf16[2,768,640]{2,1,0:T(8,128)(2,1)S(1)} %pad_maximum_fusion.1), channel_id=1, source_target_pairs={{0,16},{4,20},{8,24},{12,28},{16,0},{20,4},{24,8},{28,12},{1,17},{... | collective-permute-start | bytes 5898248 | tf_op jit(solution)/shard_map/ppermute | solution.py:470
  309.9 20.9 %collective-permute-start.30 = (bf16[256,1536]{1,0:T(8,128)(2,1)S(1)}, bf16[256,1536]{1,0:T(8,128)(2,1)S(1)}, u32[]{:S(2)}, u32[]{:S(2)}) collective-permute-start(bf16[256,1536]{1,0:T(8,128)(2,1)S(1)} %get-tuple-element.377.grad_ref.refs_4_), channel_id=1, source_target_pairs={{0,1},{1,0},{2,3},{3,2},{4,5},{5,4},{6,7},{7,6},{8,9},{9,8},{10,11... | collective-permute-start | bytes 2359304 | tf_op jit(solution)/shard_map/ppermute | solution.py:474
  402.8 37.2 %collective-permute-start.37 = (bf16[4,480,1536]{2,1,0:T(8,128)(2,1)}, bf16[4,480,1536]{2,1,0:T(8,128)(2,1)}, u32[]{:S(2)}, u32[]{:S(2)}) collective-permute-start(bf16[4,480,1536]{2,1,0:T(8,128)(2,1)} %expert_grad.4), channel_id=1, source_target_pairs={{0,4},{4,0},{8,12},{12,8},{16,20},{20,16},{24,28},{28,24},{1,5},{5... | collective-permute-start | bytes 17694728 | tf_op jit(solution)/shard_map/ppermute | solution.py:470
  434.7 43.2 %collective-permute-start.40 = (bf16[4,384,1536]{2,1,0:T(8,128)(2,1)}, bf16[4,384,1536]{2,1,0:T(8,128)(2,1)}, u32[]{:S(2)}, u32[]{:S(2)}) collective-permute-start(bf16[4,384,1536]{2,1,0:T(8,128)(2,1)} %expert_grad.6), channel_id=1, source_target_pairs={{0,4},{4,0},{8,12},{12,8},{16,20},{20,16},{24,28},{28,24},{1,5},{5... | collective-permute-start | bytes 14155784 | tf_op jit(solution)/shard_map/ppermute | solution.py:470
  435.2 21.9 %collective-permute-start.36 = (bf16[256,1536]{1,0:T(8,128)(2,1)S(1)}, bf16[256,1536]{1,0:T(8,128)(2,1)S(1)}, u32[]{:S(2)}, u32[]{:S(2)}) collective-permute-start(bf16[256,1536]{1,0:T(8,128)(2,1)S(1)} %copy-done.89), channel_id=1, source_target_pairs={{0,1},{3,2},{4,5},{7,6},{8,9},{11,10},{12,13},{15,14},{16,17},{19,... | collective-permute-start | bytes 2359304 | tf_op jit(solution)/shard_map/ppermute | solution.py:486
  449.4 72.0 %collective-permute-start.43 = (bf16[2,480,1536]{2,1,0:T(8,128)(2,1)}, bf16[2,480,1536]{2,1,0:T(8,128)(2,1)}, u32[]{:S(2)}, u32[]{:S(2)}) collective-permute-start(bf16[2,480,1536]{2,1,0:T(8,128)(2,1)} %get-tuple-element.286), channel_id=1, source_target_pairs={{0,8},{4,12},{8,0},{12,4},{16,24},{20,28},{24,16},{28,20},{1,9},{5... | collective-permute-start | bytes 8847368 | tf_op jit(solution)/shard_map/ppermute | solution.py:470
  458.2 26.4 %collective-permute-start.38 = (bf16[256,1536]{1,0:T(8,128)(2,1)}, bf16[256,1536]{1,0:T(8,128)(2,1)}, u32[]{:S(2)}, u32[]{:S(2)}) collective-permute-start(bf16[256,1536]{1,0:T(8,128)(2,1)} %add.257), channel_id=1, source_target_pairs={{0,1},{3,2},{4,5},{7,6},{8,9},{11,10},{12,13},{15,14},{16,17},{19,... | collective-permute-start | bytes 2359304 | tf_op jit(solution)/shard_map/ppermute | solution.py:486
  463.5 21.1 %collective-permute-start.39 = (bf16[256,1536]{1,0:T(8,128)(2,1)}, bf16[256,1536]{1,0:T(8,128)(2,1)}, u32[]{:S(2)}, u32[]{:S(2)}) collective-permute-start(bf16[256,1536]{1,0:T(8,128)(2,1)} %add.257), channel_id=1, source_target_pairs={{1,2},{2,1},{5,6},{6,5},{9,10},{10,9},{13,14},{14,13},{17,18},{18,... | collective-permute-start | bytes 2359304 | tf_op jit(solution)/shard_map/ppermute | solution.py:478
  484.1 58.7 %collective-permute-start.44 = (bf16[2,384,1536]{2,1,0:T(8,128)(2,1)}, bf16[2,384,1536]{2,1,0:T(8,128)(2,1)}, u32[]{:S(2)}, u32[]{:S(2)}) collective-permute-start(bf16[2,384,1536]{2,1,0:T(8,128)(2,1)} %get-tuple-element.290), channel_id=1, source_target_pairs={{0,16},{4,20},{8,24},{12,28},{16,0},{20,4},{24,8},{28,12},{1,17},{... | collective-permute-start | bytes 7077896 | tf_op jit(solution)/shard_map/ppermute | solution.py:470
  517.0 31.1 %all-to-all-start.2 = ((bf16[4,256,384]{2,1,0:T(8,128)(2,1)}), bf16[4,256,384]{2,1,0:T(8,128)(2,1)}, u32[]{:S(2)}, u32[]{:S(2)}) async-start(bf16[4,256,384]{2,1,0:T(8,128)(2,1)} %get-tuple-element.301), calls=%async_computation.2 | async-start | bytes 1572864 | tf_op jit(solution)/shard_map/all_to_all | solution.py:516
  571.2 38.0 %collective-permute-start.45 = (bf16[4,192,1536]{2,1,0:T(8,128)(2,1)}, bf16[4,192,1536]{2,1,0:T(8,128)(2,1)S(1)}, u32[]{:S(2)}, u32[]{:S(2)}) collective-permute-start(bf16[4,192,1536]{2,1,0:T(8,128)(2,1)} %get-tuple-element.312), channel_id=1, source_target_pairs={{0,4},{4,0},{8,12},{12,8},{16,20},{20,16},{24,28},{28,24},{1,5},{5... | collective-permute-start | bytes 7077896 | tf_op jit(solution)/shard_map/ppermute | solution.py:470
  571.2 67.8 %collective-permute-start.51 = (bf16[4,768,640]{2,1,0:T(8,128)(2,1)}, bf16[4,768,640]{2,1,0:T(8,128)(2,1)}, u32[]{:S(2)}, u32[]{:S(2)}) collective-permute-start(bf16[4,768,640]{2,1,0:T(8,128)(2,1)} %pad_maximum_fusion.refs_1_), channel_id=1, source_target_pairs={{0,4},{4,0},{8,12},{12,8},{16,20},{20,16},{24,28},{28,24},{1,5},{5... | collective-permute-start | bytes 11796488 | tf_op jit(solution)/shard_map/ppermute | solution.py:470
  571.7 34.2 %collective-permute-start.48 = (bf16[480,1536]{1,0:T(8,128)(2,1)S(1)}, bf16[480,1536]{1,0:T(8,128)(2,1)S(1)}, u32[]{:S(2)}, u32[]{:S(2)}) collective-permute-start(bf16[480,1536]{1,0:T(8,128)(2,1)S(1)} %copy-done.126), channel_id=1, source_target_pairs={{0,16},{4,20},{8,24},{12,28},{16,0},{20,4},{24,8},{28,12},{1,17},{... | collective-permute-start | bytes 4423688 | tf_op jit(solution)/shard_map/ppermute | solution.py:470
  572.3 27.6 %collective-permute-start.47 = (bf16[384,1536]{1,0:T(8,128)(2,1)S(1)}, bf16[384,1536]{1,0:T(8,128)(2,1)S(1)}, u32[]{:S(2)}, u32[]{:S(2)}) collective-permute-start(bf16[384,1536]{1,0:T(8,128)(2,1)S(1)} %copy-done.128), channel_id=1, source_target_pairs={{0,8},{4,12},{8,0},{12,4},{16,24},{20,28},{24,16},{28,20},{1,9},{5... | collective-permute-start | bytes 3538952 | tf_op jit(solution)/shard_map/ppermute | solution.py:470
  600.6 29.1 %collective-permute-start.50 = (bf16[384,1536]{1,0:T(8,128)(2,1)S(1)}, bf16[384,1536]{1,0:T(8,128)(2,1)}, u32[]{:S(2)}, u32[]{:S(2)}) collective-permute-start(bf16[384,1536]{1,0:T(8,128)(2,1)S(1)} %blend_sum.2.refs_0_), channel_id=1, source_target_pairs={{0,8},{4,12},{8,0},{12,4},{16,24},{20,28},{24,16},{28,20},{1,9},{5... | collective-permute-start | bytes 3538952 | tf_op jit(solution)/shard_map/ppermute | solution.py:470
  608.7 59.4 %collective-permute-start.56 = (bf16[480,1536]{1,0:T(8,128)(2,1)}, bf16[480,1536]{1,0:T(8,128)(2,1)}, u32[]{:S(2)}, u32[]{:S(2)}) collective-permute-start(bf16[480,1536]{1,0:T(8,128)(2,1)} %blend_sum.3.refs_0_), channel_id=1, source_target_pairs={{0,16},{4,20},{8,24},{12,28},{16,0},{20,4},{24,8},{28,12},{1,17},{... | collective-permute-start | bytes 4423688 | tf_op jit(solution)/shard_map/ppermute | solution.py:470
  610.9 24.5 %collective-permute-start.49 = (bf16[192,1536]{1,0:T(8,128)(2,1)}, bf16[192,1536]{1,0:T(8,128)(2,1)}, u32[]{:S(2)}, u32[]{:S(2)}) collective-permute-start(bf16[192,1536]{1,0:T(8,128)(2,1)} %add_bitcast_fusion), channel_id=1, source_target_pairs={{0,1},{3,2},{4,5},{7,6},{8,9},{11,10},{12,13},{15,14},{16,17},{19,... | collective-permute-start | bytes 1769480 | tf_op jit(solution)/shard_map/ppermute | solution.py:486
  613.0 45.3 %all-to-all-start.3 = ((bf16[4,256,640]{2,1,0:T(8,128)(2,1)}), bf16[4,256,640]{2,1,0:T(8,128)(2,1)}, u32[]{:S(2)}, u32[]{:S(2)}) async-start(bf16[4,256,640]{2,1,0:T(8,128)(2,1)} %pad_maximum_fusion.2), calls=%async_computation.3 | async-start | bytes 2621440 | tf_op jit(solution)/shard_map/all_to_all | solution.py:516
  625.1 42.0 %collective-permute-start.55 = (bf16[4,192,640]{2,1,0:T(8,128)(2,1)}, bf16[4,192,640]{2,1,0:T(8,128)(2,1)}, u32[]{:S(2)}, u32[]{:S(2)}) collective-permute-start(bf16[4,192,640]{2,1,0:T(8,128)(2,1)} %get-tuple-element.331), channel_id=1, source_target_pairs={{0,4},{4,0},{8,12},{12,8},{16,20},{20,16},{24,28},{28,24},{1,5},{5... | collective-permute-start | bytes 2949128 | tf_op jit(solution)/shard_map/ppermute | solution.py:470
  633.9 78.0 %collective-permute-start.65 = (bf16[2,384,1536]{2,1,0:T(8,128)(2,1)}, bf16[2,384,1536]{2,1,0:T(8,128)(2,1)}, u32[]{:S(2)}, u32[]{:S(2)}) collective-permute-start(bf16[2,384,1536]{2,1,0:T(8,128)(2,1)} %blend_stack.2.refs_0_), channel_id=1, source_target_pairs={{0,16},{4,20},{8,24},{12,28},{16,0},{20,4},{24,8},{28,12},{1,17},{... | collective-permute-start | bytes 7077896 | tf_op jit(solution)/shard_map/ppermute | solution.py:470
  637.7 35.2 %collective-permute-start.53 = (bf16[192,1536]{1,0:T(8,128)(2,1)}, bf16[192,1536]{1,0:T(8,128)(2,1)S(1)}, u32[]{:S(2)}, u32[]{:S(2)}) collective-permute-start(bf16[192,1536]{1,0:T(8,128)(2,1)} %bitcast_add_fusion.1), channel_id=1, source_target_pairs={{0,1},{3,2},{4,5},{7,6},{8,9},{11,10},{12,13},{15,14},{16,17},{19,... | collective-permute-start | bytes 1769480 | tf_op jit(solution)/shard_map/ppermute | solution.py:486
  639.0 37.8 %collective-permute-start.54 = (bf16[192,1536]{1,0:T(8,128)(2,1)}, bf16[192,1536]{1,0:T(8,128)(2,1)}, u32[]{:S(2)}, u32[]{:S(2)}) collective-permute-start(bf16[192,1536]{1,0:T(8,128)(2,1)} %bitcast_add_fusion.1), channel_id=1, source_target_pairs={{1,2},{2,1},{5,6},{6,5},{9,10},{10,9},{13,14},{14,13},{17,18},{18,... | collective-permute-start | bytes 1769480 | tf_op jit(solution)/shard_map/ppermute | solution.py:478
  672.3 62.4 %collective-permute-start.66 = (bf16[2,480,1536]{2,1,0:T(8,128)(2,1)S(1)}, bf16[2,480,1536]{2,1,0:T(8,128)(2,1)S(1)}, u32[]{:S(2)}, u32[]{:S(2)}) collective-permute-start(bf16[2,480,1536]{2,1,0:T(8,128)(2,1)S(1)} %blend_stack.3.refs_0_), channel_id=1, source_target_pairs={{0,8},{4,12},{8,0},{12,4},{16,24},{20,28},{24,16},{28,20},{1,9},{5... | collective-permute-start | bytes 8847368 | tf_op jit(solution)/shard_map/ppermute | solution.py:470
  685.9 20.7 %collective-permute-start.63 = (bf16[192,1536]{1,0:T(8,128)(2,1)S(1)}, bf16[192,1536]{1,0:T(8,128)(2,1)S(1)}, u32[]{:S(2)}, u32[]{:S(2)}) collective-permute-start(bf16[192,1536]{1,0:T(8,128)(2,1)S(1)} %bitcast_add_fusion), channel_id=1, source_target_pairs={{0,1},{1,0},{2,3},{3,2},{4,5},{5,4},{6,7},{7,6},{8,9},{9,8},{10,11... | collective-permute-start | bytes 1769480 | tf_op jit(solution)/shard_map/ppermute | solution.py:474
  686.0 21.3 %collective-permute-start.64 = (bf16[192,1536]{1,0:T(8,128)(2,1)S(1)}, bf16[192,1536]{1,0:T(8,128)(2,1)S(1)}, u32[]{:S(2)}, u32[]{:S(2)}) collective-permute-start(bf16[192,1536]{1,0:T(8,128)(2,1)S(1)} %add.274), channel_id=1, source_target_pairs={{1,2},{2,1},{5,6},{6,5},{9,10},{10,9},{13,14},{14,13},{17,18},{18,... | collective-permute-start | bytes 1769480 | tf_op jit(solution)/shard_map/ppermute | solution.py:478
  738.9 24.1 %collective-permute-start.76 = (bf16[4,480,1536]{2,1,0:T(8,128)(2,1)}, bf16[4,480,1536]{2,1,0:T(8,128)(2,1)}, u32[]{:S(2)}, u32[]{:S(2)}) collective-permute-start(bf16[4,480,1536]{2,1,0:T(8,128)(2,1)} %blend_four.3.refs_1_), channel_id=1, source_target_pairs={{0,4},{4,0},{8,12},{12,8},{16,20},{20,16},{24,28},{28,24},{1,5},{5... | collective-permute-start | bytes 17694728 | tf_op jit(solution)/shard_map/ppermute | solution.py:470
  738.9 23.0 %collective-permute-start.75 = (bf16[4,384,1536]{2,1,0:T(8,128)(2,1)}, bf16[4,384,1536]{2,1,0:T(8,128)(2,1)}, u32[]{:S(2)}, u32[]{:S(2)}) collective-permute-start(bf16[4,384,1536]{2,1,0:T(8,128)(2,1)} %blend_four.2.refs_0_), channel_id=1, source_target_pairs={{0,4},{4,0},{8,12},{12,8},{16,20},{20,16},{24,28},{28,24},{1,5},{5... | collective-permute-start | bytes 14155784 | tf_op jit(solution)/shard_map/ppermute | solution.py:470
  756.1 32.7 %collective-permute-start.74 = (bf16[192,1536]{1,0:T(8,128)(2,1)S(1)}, bf16[192,1536]{1,0:T(8,128)(2,1)S(1)}, u32[]{:S(2)}, u32[]{:S(2)}) collective-permute-start(bf16[192,1536]{1,0:T(8,128)(2,1)S(1)} %add.294), channel_id=1, source_target_pairs={{0,16},{4,20},{8,24},{12,28},{16,0},{20,4},{24,8},{28,12},{1,17},{... | collective-permute-start | bytes 1769480 | tf_op jit(solution)/shard_map/ppermute | solution.py:470
  760.1 29.7 %collective-permute-start.73 = (bf16[2,192,640]{2,1,0:T(8,128)(2,1)S(1)}, bf16[2,192,640]{2,1,0:T(8,128)(2,1)S(1)}, u32[]{:S(2)}, u32[]{:S(2)}) collective-permute-start(bf16[2,192,640]{2,1,0:T(8,128)(2,1)S(1)} %pad_maximum_fusion.8), channel_id=1, source_target_pairs={{0,16},{4,20},{8,24},{12,28},{16,0},{20,4},{24,8},{28,12},{1,17},{... | collective-permute-start | bytes 1474568 | tf_op jit(solution)/shard_map/ppermute | solution.py:470
  760.5 30.4 %collective-permute-start.68 = (bf16[96,1536]{1,0:T(8,128)(2,1)S(1)}, bf16[96,1536]{1,0:T(8,128)(2,1)S(1)}, u32[]{:S(2)}, u32[]{:S(2)}) collective-permute-start(bf16[96,1536]{1,0:T(8,128)(2,1)S(1)} %get-tuple-element.353), channel_id=1, source_target_pairs={{0,1},{1,0},{2,3},{3,2},{4,5},{5,4},{6,7},{7,6},{8,9},{9,8},{10,11... | collective-permute-start | bytes 884744 | tf_op jit(solution)/shard_map/ppermute | solution.py:474
  761.9 29.0 %collective-permute-start.69 = (bf16[96,1536]{1,0:T(8,128)(2,1)S(1)}, bf16[96,1536]{1,0:T(8,128)(2,1)S(1)}, u32[]{:S(2)}, u32[]{:S(2)}) collective-permute-start(bf16[96,1536]{1,0:T(8,128)(2,1)S(1)} %get-tuple-element.354), channel_id=1, source_target_pairs={{0,2},{1,3},{2,0},{3,1},{4,6},{5,7},{6,4},{7,5},{8,10},{9,11},{10,... | collective-permute-start | bytes 884744 | tf_op jit(solution)/shard_map/ppermute | solution.py:474
  763.0 27.8 %collective-permute-start.70 = (bf16[96,1536]{1,0:T(8,128)(2,1)S(1)}, bf16[96,1536]{1,0:T(8,128)(2,1)S(1)}, u32[]{:S(2)}, u32[]{:S(2)}) collective-permute-start(bf16[96,1536]{1,0:T(8,128)(2,1)S(1)} %get-tuple-element.355), channel_id=1, source_target_pairs={{0,3},{1,2},{2,1},{3,0},{4,7},{5,6},{6,5},{7,4},{8,11},{9,10},{10,... | collective-permute-start | bytes 884744 | tf_op jit(solution)/shard_map/ppermute | solution.py:474
  (196 other events, 1883.9 us)

commit v5 on v4

--- a/solution.py
+++ b/solution.py
@@ -654,26 +654,19 @@
     return pl.multiple_of(value * step, step)
 
 
-def project_kernel(meta, *refs):
-    blocks, (gain_ref, mine, other) = refs[:4], refs[4:7]
-    normed_ref, query_ref, pair_ref, weight_ref, held = refs[7:]
-    step = pl.program_id(0)
+def project_kernel(meta, blocks_ref, gain_ref, mine, other, *refs):
+    normed_ref, query_ref, pair_ref, weight_ref = refs
     core = meta[0] & 1
     rows = mine.shape[1]
 
-    @pl.when(step == 0)
+    @pl.when(pl.program_id(0) == 0)
     def _():
         for i in range(4):
-            weight_ref[pl.ds(aligned(2 * i + core, rows), rows), :] = mine[i]
-            weight_ref[pl.ds(aligned(2 * i + 1 - core, rows), rows), :] = other[i]
-
-    for r in range(4):
-
-        @pl.when(step == r)
-        def _():
-            held[...] = blocks[r][...]
-
-    states = held[...].astype(jnp.float32)
+            at = 2 * (meta[1] ^ i)
+            weight_ref[pl.ds(aligned(at + core, rows), rows), :] = mine[i]
+            weight_ref[pl.ds(aligned(at + 1 - core, rows), rows), :] = other[i]
+
+    states = blocks_ref[0].astype(jnp.float32)
     inverse = lax.rsqrt(jnp.mean(states * states, axis=-1, keepdims=True) + norm_eps)
     normed = (states * inverse * gain_ref[...]).astype(jnp.bfloat16)
     normed_ref[0] = normed
@@ -684,34 +677,31 @@
 
 
 def project(meta, blocks, gain, mine, other, query_width):
-    token_rows, width = blocks[0].shape
+    _, token_rows, width = blocks.shape
     columns = mine.shape[2]
-    arrays = list(blocks) + [gain, mine, other]
+    arrays = [blocks, gain, mine, other]
     outs = [
         shape_of((4, token_rows, width), jnp.bfloat16),
         shape_of((4, token_rows, query_width), jnp.bfloat16),
         shape_of((4, token_rows, columns - query_width), jnp.bfloat16),
         shape_of((width, columns), jnp.bfloat16),
     ]
-
-    def at_chip(r, m):
-        return ((m[0] >> 1) ^ r, 0, 0)
-
     return call(
         project_kernel,
         "project",
         meta,
         arrays,
         (4,),
-        [whole(a) for a in arrays],
+        [pl.BlockSpec((1, token_rows, width), lambda r, m: (r, 0, 0))]
+        + [whole(a) for a in arrays[1:]],
         [
-            pl.BlockSpec((1, token_rows, width), at_chip),
-            pl.BlockSpec((1, token_rows, query_width), at_chip),
-            pl.BlockSpec((1, token_rows, columns - query_width), at_chip),
+            pl.BlockSpec((1, token_rows, width), lambda r, m: (r, 0, 0)),
+            pl.BlockSpec((1, token_rows, query_width), lambda r, m: (r, 0, 0)),
+            pl.BlockSpec((1, token_rows, columns - query_width), lambda r, m: (r, 0, 0)),
             whole(outs[3]),
         ],
         outs,
-        [pltpu.VMEM((token_rows, width), jnp.bfloat16)],
+        [],
         2 * 4 * token_rows * width * columns,
         size_of(arrays) + size_of(outs),
     )
@@ -1492,8 +1482,9 @@
         self.last = None
 
     def __call__(self, *values):
-        last = () if self.last is None else (self.last,)
-        held = lax.optimization_barrier(tuple(values) + last)[: len(values)]
+        if self.last is None:
+            return values if len(values) > 1 else values[0]
+        held = lax.optimization_barrier(tuple(values) + (self.last,))[:-1]
         return held if len(held) > 1 else held[0]
 
     def mark(self, value):
@@ -1502,12 +1493,13 @@
 
 
 EARLY = (
-    "H", "W", "K", "S", "K", "S", "W", "K", "O", "S", "S", "M", "M", "S", "O", "M", "S", "M", "R", "M", "K", "M", "K", "M",
-    "K", "R", "M", "K", "M", "M", "M", "M", "R", "M", "M",
+    "H", "W", "K", "S", "K", "W", "S", "W", "K", "S", "O", "S", "M", "M", "S", "O", "M", "S", "M", "R", "M", "K", "M", "K",
+    "M", "K", "R", "M", "K", "M", "M", "M", "M", "R", "M", "M",
 )
 LATE = (
-    "L", "0", "0", "1", "0", "L", "1", "1", "L", "L", "0", "1", "L", "O", "L", "1", "0", "O", "Q", "1", "O", "L", "Q", "0",
-    "O", "L", "Q", "Q", "O", "Q", "1", "0", "S", "L", "O", "Q", "1", "0", "O", "Q", "S", "L", "O", "Q", "S", "L", "L",
+    "L", "0", "0", "0", "1", "L", "1", "1", "L", "L", "O", "0", "1", "L", "L", "1", "0", "O", "Q", "1", "O", "L", "Q", "0",
+    "O", "L", "Q", "Q", "O", "Q", "1", "0", "O", "Q", "S", "O", "Q", "1", "0", "S", "O", "Q", "L", "L", "L", "Q", "O", "S",
+    "L",
 )
 
 
@@ -1558,8 +1550,7 @@
 
 
     def hidden_chain():
-        own = ready(states)
-        have["blocks"] = [own] + [flip(own, 2 * r) for r in (1, 2, 3)]
+        have["blocks"] = chips_exchange(jnp.broadcast_to(states, (4,) + states.shape))
         yield
 
     def qkv_chain():
@@ -1574,9 +1565,12 @@
             ],
             axis=1,
         )
-        came = line_exchange(ready(jnp.broadcast_to(half, (4,) + half.shape)))
-        yield
-        have["qkv_mine"] = clock.mark(now(came))
+        came = line_swap(half, 1)
+        yield
+        pair = clock.mark(jnp.stack([half, now(came)]))
+        came = line_swap(pair, 2)
+        yield
+        have["qkv_mine"] = clock.mark(jnp.concatenate([pair, now(came)]))
         have["qkv_other"] = flip(have["qkv_mine"], 1)
         yield
 
@@ -1653,7 +1647,7 @@
 
     def out_chain():
         half = lax.dynamic_slice_in_dim(now(out_weight), core * half_rows, half_rows, 0)
-        came = line_exchange(ready(jnp.broadcast_to(half, (4,) + half.shape)))
+        came = line_exchange(jnp.broadcast_to(half, (4,) + half.shape))
         yield
         have["out_mine"] = clock.mark(now(came))
         have["out_other"] = flip(have["out_mine"], 1)
@@ -1862,10 +1856,16 @@
                 )
             )
 
-        came = flip(grad_of(1 - core), 1)
-        yield
-        keep = grad_of(core)
-        yield
+        if index == 0:
+            came = flip(grad_of(1 - core), 1)
+            yield
+            keep = grad_of(core)
+            yield
+        else:
+            keep = grad_of(core)
+            yield
+            came = flip(grad_of(1 - core), 1)
+            yield
         x_first = index % 2 == 0
         first, second = (2, 4) if x_first else (4, 2)
         picked = ((1, 3), (0, 2)) if x_first else ((2, 3), (0, 1))
@@ -1949,6 +1949,8 @@
         yield
         yield from line_reduce_steps(keep, came)
         total = have["line_sum"]
+        yield
+        total = ready(total)
         came = flip(total, 2)
         yield
         total = clock.mark(total + now(came))
@@ -1976,6 +1978,8 @@
         yield
         yield from line_reduce_steps(keep, came)
         own = have["line_sum"]
+        yield
+        own = ready(own)
         came = flip(own, 2)
         yield
         pair = clock.mark(jnp.stack([own, now(came)]))

time: 833 us -> 777 us (0.933)
  waiting for transfers between devices: 273 us -> 219 us
    ppermute x15 -> x17, waiting for transfers between devices: 103 us -> 64.7 us  [line_swap(): lax.ppermute(value, 'wt', [(index, index ^ offset) for index in range(4)])]
    ppermute x43 -> x40, waiting for transfers between devices: 107 us -> 90.8 us  [flip(): lax.ppermute(value, 'ctx', [(index, index ^ bit) for index in range(8)])]
    all_to_all x2 -> x1, waiting for transfers between devices: 0.61 us -> 12.1 us  [line_exchange(): return lax.all_to_all(blocks, 'wt', split_axis=0, concat_axis=0, tiled=True)]
    all_to_all x2 -> x3, waiting for transfers between devices: 17.8 us -> 11.5 us  [chips_exchange(): lax.all_to_all(blocks, 'ctx', split_axis=0, concat_axis=0, tiled=True, ax...]
    unnamed x321 -> x291, local copies, waits for them, and re-layouts: 51.1 us -> 48.7 us
    ppermute x43 -> x40, starting transfers between devices: 28.9 us -> 26.6 us  [flip(): lax.ppermute(value, 'ctx', [(index, index ^ bit) for index in range(8)])]
    ppermute x15 -> x17, starting transfers between devices: 35.1 us -> 36.5 us  [line_swap(): lax.ppermute(value, 'wt', [(index, index ^ offset) for index in range(4)])]
  transfers between devices with their start and end apart: 86 -> 85, of which waited for: 32 -> 38; matrix products, arithmetic and copies ran while one was open for 6% -> 7% of each run, Pallas kernels for 30% -> 34%
where the time goes in v5:
time: 777 us; the launch traced here: 769 us
  Pallas kernels  300 us (39%)
  waiting for transfers between devices  219 us (28%)
  starting transfers between devices  130 us (17%)
  local copies, waits for them, and re-layouts  68.7 us (9%)
  other arithmetic  46.7 us (6%)
    pallas_call x33, Pallas kernels, call(): pl.pallas_call(kernel, grid_spec=pltpu.PrefetchScalarGridSpec(num_scalar_...  275 us
    ppermute x40, waiting for transfers between devices, flip(): lax.ppermute(value, 'ctx', [(index, index ^ bit) for index in range(8)])  90.8 us
    ppermute x17, waiting for transfers between devices, line_swap(): lax.ppermute(value, 'wt', [(index, index ^ offset) for index in range(4)])  64.7 us
    unnamed x291, local copies, waits for them, and re-layouts  48.7 us
    ppermute x17, starting transfers between devices, line_swap(): lax.ppermute(value, 'wt', [(index, index ^ offset) for index in range(4)])  36.5 us
    ppermute x8, waiting for transfers between devices, line_inward(): return lax.ppermute(value, 'wt', [(0, 1), (3, 2)])  33.9 us
    ppermute x8, starting transfers between devices, line_inward(): return lax.ppermute(value, 'wt', [(0, 1), (3, 2)])  30.1 us
    ppermute x40, starting transfers between devices, flip(): lax.ppermute(value, 'ctx', [(index, index ^ bit) for index in range(8)])  26.6 us
  transfers between devices with their start and end apart: 85, of which 38 were waited for; matrix products, arithmetic and copies ran while one was open for 7% of the time, Pallas kernels for 34%

profile of v5, /device:TPU:0, one launch (start us, length us, event | category | flops | bytes accessed | tf_op | source)
XLA Modules:
  0.0 769.2 jit_solution(13826255900118494120)
XLA Ops:
  9.8 4.8 all-to-all-start.1
  27.0 22.9 %collective-permute-done.5 = bf16[2,192,640]{2,1,0:T(8,128)(2,1)S(1)} collective-permute-done((bf16[2,192,640]{2,1,0:T(8,128)(2,1)S(1)}, bf16[2,192,640]{2,1,0:T(8,128)(2,1)S(1)}, u32[]{:S(2)}, u32[]{:S(2)}) %collective-permute-start.5) | collective-permute-done | bytes 491552 | tf_op jit(solution)/shard_map/ppermute | solution.py:474
  54.1 4.7 all-to-all-start
  61.7 6.9 collective-permute-done.6
  71.7 6.8 project.1
  84.1 11.5 %attend.1 = (bf16[4,256,384]{2,1,0:T(8,128)(2,1)S(1)}, f32[8,1,384]{2,1,0:T(1,128)S(1)}) custom-call(s32[2]{0:T(128)S(1)} %pad_add_fusion.meta.meta_ref, bf16[4,256,384]{2,1,0:T(8,128)(2,1)S(1)} %copy-done.44, bf16[4,256,256]{2,1,0:T(8,128)(2,1)} %get-tuple-element.198.mine_ref, bf16[4,256,256]{2,1,0:T(8,128)(2,1)S(1)} %collective-permute-done.9.other_ref), custom_call_target="tpu_custom_call" | custom-call | flops 300000000 | bytes 1000 | tf_op jit(solution)/shard_map/attend/pallas_call | solution.py:585
  99.1 12.1 %all-to-all-done.refs_4_ = bf16[4,192,1536]{2,1,0:T(8,128)(2,1)} async-done(((bf16[4,192,1536]{2,1,0:T(8,128)(2,1)}), bf16[4,192,1536]{2,1,0:T(8,128)(2,1)}, u32[]{:S(2)}, u32[]{:S(2)}) %all-to-all-start) | async-done | bytes 2359328 | tf_op jit(solution)/shard_map/all_to_all | solution.py:527
  119.7 5.0 collective-permute-done.11.refs_2_
  126.2 6.2 leave.1
  141.7 11.7 %experts.4 = (bf16[4,256,1024]{2,1,0:T(8,128)(2,1)S(1)}, bf16[256,512]{1,0:T(8,128)(2,1)S(1)}, bf16[256,1536]{1,0:T(8,128)(2,1)S(1)}) custom-call(s32[2]{0:T(128)S(1)} %pad_add_fusion.meta.meta_ref, bf16[256,1536]{1,0:T(8,128)(2,1)S(1)} %get-tuple-element.211.rows_ref.refs_0_, f32[4,256,1]{2,1,0:T(8,128)S(1)} %copy-done.39, ...), custom_call_target="tpu_custom_call" | custom-call | flops 300000000 | bytes 1000 | tf_op jit(solution)/shard_map/experts/pallas_call | solution.py:585
  162.4 12.0 %experts.5 = (bf16[4,256,1024]{2,1,0:T(8,128)(2,1)S(1)}, bf16[256,512]{1,0:T(8,128)(2,1)S(1)}, bf16[256,1536]{1,0:T(8,128)(2,1)S(1)}) custom-call(s32[2]{0:T(128)S(1)} %pad_add_fusion.meta.meta_ref, bf16[256,1536]{1,0:T(8,128)(2,1)} %collective-permute-done.15.rows_ref.refs_1_, f32[4,256,1]{2,1,0:T(8,128)S(1)} %copy.40.gates_ref, ...), custom_call_target="tpu_custom_call" | custom-call | flops 300000000 | bytes 1000 | tf_op jit(solution)/shard_map/experts/pallas_call | solution.py:585
  185.5 11.7 %experts.6 = (bf16[4,256,1024]{2,1,0:T(8,128)(2,1)S(1)}, bf16[256,512]{1,0:T(8,128)(2,1)S(1)}, bf16[256,1536]{1,0:T(8,128)(2,1)S(1)}) custom-call(s32[2]{0:T(128)S(1)} %pad_add_fusion.meta.meta_ref, bf16[256,1536]{1,0:T(8,128)(2,1)S(1)} %broadcast_select_fusion.3.rows_ref.refs_2_, f32[4,256,1]{2,1,0:T(8,128)S(1)} %copy-done.37, ...), custom_call_target="tpu_custom_call" | custom-call | flops 300000000 | bytes 1000 | tf_op jit(solution)/shard_map/experts/pallas_call | solution.py:585
  200.3 11.7 %experts.7 = (bf16[4,256,1024]{2,1,0:T(8,128)(2,1)S(1)}, bf16[256,512]{1,0:T(8,128)(2,1)S(1)}, bf16[256,1536]{1,0:T(8,128)(2,1)S(1)}) custom-call(s32[2]{0:T(128)S(1)} %pad_add_fusion.meta.meta_ref, bf16[256,1536]{1,0:T(8,128)(2,1)S(1)} %broadcast_select_fusion.2.rows_ref.refs_3_, f32[4,256,1]{2,1,0:T(8,128)S(1)} %copy-done.35, ...), custom_call_target="tpu_custom_call" | custom-call | flops 300000000 | bytes 1000 | tf_op jit(solution)/shard_map/experts/pallas_call | solution.py:585
  212.1 4.9 collective-permute-start.21
  221.0 13.5 %collective-permute-done.21 = bf16[256,1536]{1,0:T(8,128)(2,1)S(1)} collective-permute-done((bf16[256,1536]{1,0:T(8,128)(2,1)S(1)}, bf16[256,1536]{1,0:T(8,128)(2,1)S(1)}, u32[]{:S(2)}, u32[]{:S(2)}) %collective-permute-start.21) | collective-permute-done | bytes 786464 | tf_op jit(solution)/shard_map/ppermute | solution.py:486
  243.5 12.2 %collective-permute-done.24 = bf16[256,1536]{1,0:T(8,128)(2,1)S(1)} collective-permute-done((bf16[256,1536]{1,0:T(8,128)(2,1)S(1)}, bf16[256,1536]{1,0:T(8,128)(2,1)S(1)}, u32[]{:S(2)}, u32[]{:S(2)}) %collective-permute-start.24) | collective-permute-done | bytes 786464 | tf_op jit(solution)/shard_map/ppermute | solution.py:486
  262.5 14.0 %collective-permute-done.27 = bf16[256,1536]{1,0:T(8,128)(2,1)S(1)} collective-permute-done((bf16[256,1536]{1,0:T(8,128)(2,1)S(1)}, bf16[256,1536]{1,0:T(8,128)(2,1)S(1)}, u32[]{:S(2)}, u32[]{:S(2)}) %collective-permute-start.27) | collective-permute-done | bytes 786464 | tf_op jit(solution)/shard_map/ppermute | solution.py:474
  284.0 13.0 %experts_back.4 = (bf16[4,256,1024]{2,1,0:T(8,128)(2,1)S(1)}, bf16[4,256,512]{2,1,0:T(8,128)(2,1)S(1)}, bf16[1,256,512]{2,1,0:T(8,128)(2,1)S(1)}, bf16[1,256,256]{2,1,0:T(8,128)(2,1)S(1)}, bf16[256,1536]{1,0:T(8,128)(2,1)S(1)}) custom-call(s32[2]{0:T(128)S(1)} %pad_add_fusion.meta.meta_ref, bf16[256,1536]{1,0:T(8,128)(2,1)S(1)} %get-tuple-element.375.grad_ref.refs_4_, ...), custom_call_target="tpu_custom_call" | custom-call | flops 300000000 | bytes 1000 | tf_op jit(solution)/shard_map/experts_back/pallas_call | solution.py:585
  303.2 13.0 %experts_back.5 = (bf16[4,256,1024]{2,1,0:T(8,128)(2,1)S(1)}, bf16[4,256,512]{2,1,0:T(8,128)(2,1)S(1)}, bf16[1,256,512]{2,1,0:T(8,128)(2,1)S(1)}, bf16[1,256,256]{2,1,0:T(8,128)(2,1)S(1)}, bf16[256,1536]{1,0:T(8,128)(2,1)S(1)}) custom-call(s32[2]{0:T(128)S(1)} %pad_add_fusion.meta.meta_ref, bf16[256,1536]{1,0:T(8,128)(2,1)S(1)} %collective-permute-done.29.grad_ref.refs_5_, ...), custom_call_target="tpu_custom_call" | custom-call | flops 300000000 | bytes 1000 | tf_op jit(solution)/shard_map/experts_back/pallas_call | solution.py:585
  326.7 13.0 %experts_back.6 = (bf16[4,256,1024]{2,1,0:T(8,128)(2,1)S(1)}, bf16[4,256,512]{2,1,0:T(8,128)(2,1)S(1)}, bf16[1,256,512]{2,1,0:T(8,128)(2,1)S(1)}, bf16[1,256,256]{2,1,0:T(8,128)(2,1)S(1)}, bf16[256,1536]{1,0:T(8,128)(2,1)S(1)}) custom-call(s32[2]{0:T(128)S(1)} %pad_add_fusion.meta.meta_ref, bf16[256,1536]{1,0:T(8,128)(2,1)S(1)} %broadcast_select_fusion.1.grad_ref.refs_6_, ...), custom_call_target="tpu_custom_call" | custom-call | flops 300000000 | bytes 1000 | tf_op jit(solution)/shard_map/experts_back/pallas_call | solution.py:585
  343.5 14.4 %experts_back.7 = (bf16[4,256,1024]{2,1,0:T(8,128)(2,1)S(1)}, bf16[4,256,512]{2,1,0:T(8,128)(2,1)S(1)}, bf16[1,256,512]{2,1,0:T(8,128)(2,1)S(1)}, bf16[1,256,256]{2,1,0:T(8,128)(2,1)S(1)}, bf16[256,1536]{1,0:T(8,128)(2,1)}) custom-call(s32[2]{0:T(128)S(1)} %pad_add_fusion.meta.meta_ref, bf16[256,1536]{1,0:T(8,128)(2,1)S(1)} %broadcast_select_fusion.grad_ref.refs_7_, ...), custom_call_target="tpu_custom_call" | custom-call | flops 300000000 | bytes 1000 | tf_op jit(solution)/shard_map/experts_back/pallas_call | solution.py:585
  360.4 13.0 %expert_grad.4 = bf16[4,480,1536]{2,1,0:T(8,128)(2,1)} custom-call(s32[3]{0:T(128)S(1)} %add_add_fusion.meta, bf16[256,1536]{1,0:T(8,128)(2,1)S(1)} %copy-done.18, bf16[256,1536]{1,0:T(8,128)(2,1)} %collective-permute-done.15.rows_ref.refs_1_, bf16[256,1536]{1,0:T(8,128)(2,1)S(1)} %broadcast_select_fusion.3.rows_ref.refs_2_, ...), custom_call_target="tpu_custom_call" | custom-call | flops 300000000 | bytes 1000 | tf_op jit(solution)/shard_map/expert_grad/pallas_call | solution.py:585
  373.5 5.5 collective-permute-start.35
  386.6 12.9 %expert_grad.5.refs_0_ = bf16[4,480,1536]{2,1,0:T(8,128)(2,1)} custom-call(s32[3]{0:T(128)S(1)} %add_add_fusion.1.meta, bf16[256,1536]{1,0:T(8,128)(2,1)S(1)} %copy-done.19, bf16[256,1536]{1,0:T(8,128)(2,1)} %collective-permute-done.15.rows_ref.refs_1_, bf16[256,1536]{1,0:T(8,128)(2,1)S(1)} %broadcast_select_fusion.3.rows_ref.refs_2_, ...), custom_call_target="tpu_custom_call" | custom-call | flops 300000000 | bytes 1000 | tf_op jit(solution)/shard_map/expert_grad/pallas_call | solution.py:585
  399.5 8.1 %blend_split.2 = (bf16[2,480,1536]{2,1,0:T(8,128)(2,1)}, bf16[2,480,1536]{2,1,0:T(8,128)(2,1)S(1)}) custom-call(s32[2]{0:T(128)S(1)} %pad_add_fusion.meta.meta_ref, bf16[4,480,1536]{2,1,0:T(8,128)(2,1)} %expert_grad.5.refs_0_, bf16[4,480,1536]{2,1,0:T(8,128)(2,1)} %collective-permute-done.36.refs_1_), custom_call_target="tpu_custom_call" | custom-call | flops 300000000 | bytes 1000 | tf_op jit(solution)/shard_map/blend_split/pallas_call | solution.py:585
  409.4 10.1 %expert_grad.6.refs_0_ = bf16[4,384,1536]{2,1,0:T(8,128)(2,1)} custom-call(s32[3]{0:T(128)S(1)} %add_add_fusion.2.meta, bf16[256,1536]{1,0:T(8,128)(2,1)S(1)} %copy-done.20, bf16[256,1536]{1,0:T(8,128)(2,1)} %collective-permute-done.15.rows_ref.refs_1_, bf16[256,1536]{1,0:T(8,128)(2,1)S(1)} %broadcast_select_fusion.3.rows_ref.refs_2_, ...), custom_call_target="tpu_custom_call" | custom-call | flops 300000000 | bytes 1000 | tf_op jit(solution)/shard_map/expert_grad/pallas_call | solution.py:585
  420.9 10.2 %expert_grad.7 = bf16[4,384,1536]{2,1,0:T(8,128)(2,1)} custom-call(s32[3]{0:T(128)S(1)} %add_add_fusion.3.meta, bf16[256,1536]{1,0:T(8,128)(2,1)S(1)} %copy-done.20, bf16[256,1536]{1,0:T(8,128)(2,1)} %collective-permute-done.15.rows_ref.refs_1_, bf16[256,1536]{1,0:T(8,128)(2,1)S(1)} %broadcast_select_fusion.3.rows_ref.refs_2_, ...), custom_call_target="tpu_custom_call" | custom-call | flops 300000000 | bytes 1000 | tf_op jit(solution)/shard_map/expert_grad/pallas_call | solution.py:585
  434.1 5.2 collective-permute-done.39.refs_1_
  441.5 6.1 blend_split.3
  457.5 15.6 %collective-permute-done.40 = bf16[256,1536]{1,0:T(8,128)(2,1)} collective-permute-done((bf16[256,1536]{1,0:T(8,128)(2,1)}, bf16[256,1536]{1,0:T(8,128)(2,1)}, u32[]{:S(2)}, u32[]{:S(2)}) %collective-permute-start.40) | collective-permute-done | bytes 786464 | tf_op jit(solution)/shard_map/ppermute | solution.py:474
  475.9 7.2 enter_back.1
  494.6 5.9 collective-permute-done.43.refs_1_
  502.4 5.2 blend_pair.2
  508.2 7.4 collective-permute-done.44.refs_1_
  523.7 16.2 %attend_back.1 = (bf16[4,256,384]{2,1,0:T(8,128)(2,1)S(1)}, f32[4,256,256]{2,1,0:T(8,128)S(1)}, bf16[4,256,256]{2,1,0:T(8,128)(2,1)S(1)}) custom-call(s32[2]{0:T(128)S(1)} %pad_add_fusion.meta.meta_ref, bf16[4,256,384]{2,1,0:T(8,128)(2,1)S(1)} %copy-done.45, bf16[4,256,256]{2,1,0:T(8,128)(2,1)} %get-tuple-element.198.mine_ref, ...), custom_call_target="tpu_custom_call" | custom-call | flops 300000000 | bytes 1000 | tf_op jit(solution)/shard_map/attend_back/pallas_call | solution.py:585
  566.1 6.3 weight_grad.3
  590.1 11.5 %all-to-all-done.3.refs_0_ = bf16[4,256,640]{2,1,0:T(8,128)(2,1)} async-done(((bf16[4,256,640]{2,1,0:T(8,128)(2,1)}), bf16[4,256,640]{2,1,0:T(8,128)(2,1)}, u32[]{:S(2)}, u32[]{:S(2)}) %all-to-all-start.3) | async-done | bytes 1310752 | tf_op jit(solution)/shard_map/all_to_all | solution.py:516
  601.6 9.0 %finish.1 = (f32[1,256,1536]{2,1,0:T(8,128)}, f32[1,1536]{1,0:T(1,128)S(1)}) custom-call(s32[2]{0:T(128)S(1)} %pad_add_fusion.meta.meta_ref, bf16[4,256,640]{2,1,0:T(8,128)(2,1)} %all-to-all-done.3.refs_0_, bf16[4,768,640]{2,1,0:T(8,128)(2,1)} %pad_maximum_fusion.refs_1_, bf16[4,768,640]{2,1,0:T(8,128)(2,1)} %collective-permute-done.50.refs_2_, ...), custom_call_target="tpu_custom_call" | custom-call | flops 300000000 | bytes 1000 | tf_op jit(solution)/shard_map/finish/pallas_call | solution.py:585
  629.7 5.6 collective-permute-done.58
  637.1 13.5 %collective-permute-start.60 = (bf16[192,640]{1,0:T(8,128)(2,1)S(1)}, bf16[192,640]{1,0:T(8,128)(2,1)S(1)}, u32[]{:S(2)}, u32[]{:S(2)}) collective-permute-start(bf16[192,640]{1,0:T(8,128)(2,1)S(1)} %bitcast_add_fusion.3), channel_id=1, source_target_pairs={{0,1},{1,0},{2,3},{3,2},{4,5},{5,4},{6,7},{7,6},{8,9},{9,8},{10,11... | collective-permute-start | bytes 737288 | tf_op jit(solution)/shard_map/ppermute | solution.py:474
  655.8 9.9 %collective-permute-done.64.refs_1_ = bf16[2,384,1536]{2,1,0:T(8,128)(2,1)} collective-permute-done((bf16[2,384,1536]{2,1,0:T(8,128)(2,1)S(1)}, bf16[2,384,1536]{2,1,0:T(8,128)(2,1)}, u32[]{:S(2)}, u32[]{:S(2)}) %collective-permute-start.64) | collective-permute-done | bytes 2359328 | tf_op jit(solution)/shard_map/ppermute | solution.py:470
  665.7 5.0 blend_four.2.refs_0_
  670.7 11.7 %collective-permute-done.65.refs_1_ = bf16[2,480,1536]{2,1,0:T(8,128)(2,1)S(1)} collective-permute-done((bf16[2,480,1536]{2,1,0:T(8,128)(2,1)S(1)}, bf16[2,480,1536]{2,1,0:T(8,128)(2,1)S(1)}, u32[]{:S(2)}, u32[]{:S(2)}) %collective-permute-start.65) | collective-permute-done | bytes 2949152 | tf_op jit(solution)/shard_map/ppermute | solution.py:470
  690.7 12.6 %collective-permute-done.67 = bf16[192,1536]{1,0:T(8,128)(2,1)S(1)} collective-permute-done((bf16[192,1536]{1,0:T(8,128)(2,1)S(1)}, bf16[192,1536]{1,0:T(8,128)(2,1)S(1)}, u32[]{:S(2)}, u32[]{:S(2)}) %collective-permute-start.67) | collective-permute-done | bytes 589856 | tf_op jit(solution)/shard_map/ppermute | solution.py:470
  711.8 12.8 %place_pair.2.refs_0_ = f32[4,1536,1536]{2,1,0:T(8,128)} custom-call(s32[2]{0:T(128)S(1)} %pad_add_fusion.meta.meta_ref, bf16[4,384,1536]{2,1,0:T(8,128)(2,1)} %blend_four.2.refs_0_, bf16[4,384,1536]{2,1,0:T(8,128)(2,1)} %collective-permute-done.73.refs_1_), custom_call_target="tpu_custom_call" | custom-call | flops 300000000 | bytes 1000 | tf_op jit(solution)/shard_map/place_pair/pallas_call | solution.py:1363
  724.6 11.6 %place_pair.3 = f32[4,1536,1536]{2,1,0:T(8,128)} custom-call(s32[2]{0:T(128)S(1)} %pad_add_fusion.meta.meta_ref, f32[4,1536,1536]{2,1,0:T(8,128)} %place_pair.2.refs_0_, bf16[4,480,1536]{2,1,0:T(8,128)(2,1)S(1)} %bitcast.107, bf16[4,480,1536]{2,1,0:T(8,128)(2,1)} %collective-permute-done.74.refs_2_), custom_call_target="tpu_custom_call", output_to_operand_aliasing={{}: (1, {})} | custom-call | flops 300000000 | bytes 1000 | tf_op jit(solution)/shard_map/place_pair/pallas_call | solution.py:1363
  739.8 5.0 collective-permute-done.56
  757.8 8.2 %place_shared.1 = f32[384,3072]{1,0:T(8,128)} custom-call(s32[2]{0:T(128)S(1)} %pad_add_fusion.meta.meta_ref, bf16[4,96,1536]{2,1,0:T(8,128)(2,1)S(1)} %pad_maximum_fusion.4.mine_low.mine_high, bf16[4,96,1536]{2,1,0:T(8,128)(2,1)S(1)} %pad_maximum_fusion.4.mine_low.mine_high, bf16[4,96,1536]{2,1,0:T(8,128)(2,1)} %collective-permute-done.80.other_low.other_high, ...), custom_call_target="tpu_custom_call" | custom-call | flops 300000000 | bytes 1000 | tf_op jit(solution)/shard_map/place_shared/pallas_call | solution.py:585
  (558 shorter events, 285.8 us)
Async XLA Ops:
  9.8 42.7 %all-to-all-start.1 = ((bf16[4,256,1536]{2,1,0:T(8,128)(2,1)}), bf16[4,256,1536]{2,1,0:T(8,128)(2,1)}, u32[]{:S(2)}, u32[]{:S(2)}) async-start(bf16[4,256,1536]{2,1,0:T(8,128)(2,1)} %broadcast_in_dim.55), calls=%async_computation.1 | async-start | bytes 6291456 | tf_op jit(solution)/shard_map/all_to_all | solution.py:516
  20.5 29.5 %collective-permute-start.5 = (bf16[2,192,640]{2,1,0:T(8,128)(2,1)S(1)}, bf16[2,192,640]{2,1,0:T(8,128)(2,1)S(1)}, u32[]{:S(2)}, u32[]{:S(2)}) collective-permute-start(bf16[2,192,640]{2,1,0:T(8,128)(2,1)S(1)} %pad_maximum_fusion.9), channel_id=1, source_target_pairs={{0,2},{1,3},{2,0},{3,1},{4,6},{5,7},{6,4},{7,5},{8,10},{9,11},{10,... | collective-permute-start | bytes 1474568 | tf_op jit(solution)/shard_map/ppermute | solution.py:474
  23.1 28.0 %collective-permute-start.4 = (f32[2,32,256]{2,1,0:T(8,128)S(1)}, f32[2,32,256]{2,1,0:T(8,128)S(1)}, u32[]{:S(2)}, u32[]{:S(2)}) collective-permute-start(f32[2,32,256]{2,1,0:T(8,128)S(1)} %pad_maximum_fusion.16), channel_id=1, source_target_pairs={{0,2},{1,3},{2,0},{3,1},{4,6},{5,7},{6,4},{7,5},{8,10},{9,11},{10,... | collective-permute-start | bytes 196616 | tf_op jit(solution)/shard_map/ppermute | solution.py:474
  24.7 27.7 %collective-permute-start.3 = (bf16[2,48,768]{2,1,0:T(8,128)(2,1)S(1)}, bf16[2,48,768]{2,1,0:T(8,128)(2,1)S(1)}, u32[]{:S(2)}, u32[]{:S(2)}) collective-permute-start(bf16[2,48,768]{2,1,0:T(8,128)(2,1)S(1)} %pad_maximum_fusion.14), channel_id=1, source_target_pairs={{0,2},{1,3},{2,0},{3,1},{4,6},{5,7},{6,4},{7,5},{8,10},{9,11},{10,... | collective-permute-start | bytes 442376 | tf_op jit(solution)/shard_map/ppermute | solution.py:474
  54.1 57.0 %all-to-all-start = ((bf16[4,192,1536]{2,1,0:T(8,128)(2,1)}), bf16[4,192,1536]{2,1,0:T(8,128)(2,1)}, u32[]{:S(2)}, u32[]{:S(2)}) async-start(bf16[4,192,1536]{2,1,0:T(8,128)(2,1)} %broadcast_in_dim.54), calls=%async_computation | async-start | bytes 4718592 | tf_op jit(solution)/shard_map/all_to_all | solution.py:527
  111.1 26.2 %collective-permute-start.14 = (bf16[4,4,48,768]{3,2,1,0:T(8,128)(2,1)}, bf16[4,4,48,768]{3,2,1,0:T(8,128)(2,1)}, u32[]{:S(2)}, u32[]{:S(2)}) collective-permute-start(bf16[4,4,48,768]{3,2,1,0:T(8,128)(2,1)} %pad_maximum_fusion.3.mine), channel_id=1, source_target_pairs={{0,4},{4,0},{8,12},{12,8},{16,20},{20,16},{24,28},{28,24},{1,5},{5... | collective-permute-start | bytes 3538952 | tf_op jit(solution)/shard_map/ppermute | solution.py:470
  133.6 22.1 %collective-permute-start.15 = (bf16[256,1536]{1,0:T(8,128)(2,1)S(1)}, bf16[256,1536]{1,0:T(8,128)(2,1)}, u32[]{:S(2)}, u32[]{:S(2)}) collective-permute-start(bf16[256,1536]{1,0:T(8,128)(2,1)S(1)} %get-tuple-element.211.rows_ref.refs_0_), channel_id=1, source_target_pairs={{0,1},{1,0},{2,3},{3,2},{4,5},{5,4},{6,7},{7,6},{8,9},{9,8},{10,11... | collective-permute-start | bytes 2359304 | tf_op jit(solution)/shard_map/ppermute | solution.py:474
  133.6 22.1 %collective-permute-start.16 = (bf16[256,1536]{1,0:T(8,128)(2,1)S(1)}, bf16[256,1536]{1,0:T(8,128)(2,1)}, u32[]{:S(2)}, u32[]{:S(2)}) collective-permute-start(bf16[256,1536]{1,0:T(8,128)(2,1)S(1)} %get-tuple-element.211.rows_ref.refs_0_), channel_id=1, source_target_pairs={{1,2},{2,1},{5,6},{6,5},{9,10},{10,9},{13,14},{14,13},{17,18},{18,... | collective-permute-start | bytes 2359304 | tf_op jit(solution)/shard_map/ppermute | solution.py:478
  155.7 20.1 %collective-permute-start.17 = (bf16[256,1536]{1,0:T(8,128)(2,1)}, bf16[256,1536]{1,0:T(8,128)(2,1)}, u32[]{:S(2)}, u32[]{:S(2)}) collective-permute-start(bf16[256,1536]{1,0:T(8,128)(2,1)} %collective-permute-done.15.rows_ref.refs_1_), channel_id=1, source_target_pairs={{1,2},{2,1},{5,6},{6,5},{9,10},{10,9},{13,14},{14,13},{17,18},{18,... | collective-permute-start | bytes 2359304 | tf_op jit(solution)/shard_map/ppermute | solution.py:478
  157.3 22.1 %collective-permute-start.18 = (bf16[256,1536]{1,0:T(8,128)(2,1)}, bf16[256,1536]{1,0:T(8,128)(2,1)}, u32[]{:S(2)}, u32[]{:S(2)}) collective-permute-start(bf16[256,1536]{1,0:T(8,128)(2,1)} %collective-permute-done.16), channel_id=1, source_target_pairs={{1,0},{2,3},{5,4},{6,7},{9,8},{10,11},{13,12},{14,15},{17,16},{18,... | collective-permute-start | bytes 2359304 | tf_op jit(solution)/shard_map/ppermute | solution.py:482
  179.4 20.0 %collective-permute-start.19 = (bf16[256,1536]{1,0:T(8,128)(2,1)}, bf16[256,1536]{1,0:T(8,128)(2,1)S(1)}, u32[]{:S(2)}, u32[]{:S(2)}) collective-permute-start(bf16[256,1536]{1,0:T(8,128)(2,1)} %collective-permute-done.17), channel_id=1, source_target_pairs={{1,0},{2,3},{5,4},{6,7},{9,8},{10,11},{13,12},{14,15},{17,16},{18,... | collective-permute-start | bytes 2359304 | tf_op jit(solution)/shard_map/ppermute | solution.py:482
  182.1 38.7 %collective-permute-start.22 = (bf16[768,640]{1,0:T(8,128)(2,1)S(1)}, bf16[768,640]{1,0:T(8,128)(2,1)S(1)}, u32[]{:S(2)}, u32[]{:S(2)}) collective-permute-start(bf16[768,640]{1,0:T(8,128)(2,1)S(1)} %constant_dynamic-slice_fusion.1), channel_id=1, source_target_pairs={{0,8},{4,12},{8,0},{12,4},{16,24},{20,28},{24,16},{28,20},{1,9},{5... | collective-permute-start | bytes 2949128 | tf_op jit(solution)/shard_map/ppermute | solution.py:470
  212.1 22.3 %collective-permute-start.21 = (bf16[256,1536]{1,0:T(8,128)(2,1)S(1)}, bf16[256,1536]{1,0:T(8,128)(2,1)S(1)}, u32[]{:S(2)}, u32[]{:S(2)}) collective-permute-start(bf16[256,1536]{1,0:T(8,128)(2,1)S(1)} %get-tuple-element.227), channel_id=1, source_target_pairs={{0,1},{3,2},{4,5},{7,6},{8,9},{11,10},{12,13},{15,14},{16,17},{19,... | collective-permute-start | bytes 2359304 | tf_op jit(solution)/shard_map/ppermute | solution.py:486
  234.6 21.0 %collective-permute-start.24 = (bf16[256,1536]{1,0:T(8,128)(2,1)S(1)}, bf16[256,1536]{1,0:T(8,128)(2,1)S(1)}, u32[]{:S(2)}, u32[]{:S(2)}) collective-permute-start(bf16[256,1536]{1,0:T(8,128)(2,1)S(1)} %add.250), channel_id=1, source_target_pairs={{0,1},{3,2},{4,5},{7,6},{8,9},{11,10},{12,13},{15,14},{16,17},{19,... | collective-permute-start | bytes 2359304 | tf_op jit(solution)/shard_map/ppermute | solution.py:486
  256.1 20.4 %collective-permute-start.27 = (bf16[256,1536]{1,0:T(8,128)(2,1)S(1)}, bf16[256,1536]{1,0:T(8,128)(2,1)S(1)}, u32[]{:S(2)}, u32[]{:S(2)}) collective-permute-start(bf16[256,1536]{1,0:T(8,128)(2,1)S(1)} %add.252), channel_id=1, source_target_pairs={{0,1},{1,0},{2,3},{3,2},{4,5},{5,4},{6,7},{7,6},{8,9},{9,8},{10,11... | collective-permute-start | bytes 2359304 | tf_op jit(solution)/shard_map/ppermute | solution.py:474
  260.6 55.7 %collective-permute-start.33 = (bf16[2,768,640]{2,1,0:T(8,128)(2,1)S(1)}, bf16[2,768,640]{2,1,0:T(8,128)(2,1)}, u32[]{:S(2)}, u32[]{:S(2)}) collective-permute-start(bf16[2,768,640]{2,1,0:T(8,128)(2,1)S(1)} %pad_maximum_fusion.1), channel_id=1, source_target_pairs={{0,16},{4,20},{8,24},{12,28},{16,0},{20,4},{24,8},{28,12},{1,17},{... | collective-permute-start | bytes 5898248 | tf_op jit(solution)/shard_map/ppermute | solution.py:470
  279.5 20.9 %collective-permute-start.29 = (bf16[256,1536]{1,0:T(8,128)(2,1)S(1)}, bf16[256,1536]{1,0:T(8,128)(2,1)S(1)}, u32[]{:S(2)}, u32[]{:S(2)}) collective-permute-start(bf16[256,1536]{1,0:T(8,128)(2,1)S(1)} %get-tuple-element.375.grad_ref.refs_4_), channel_id=1, source_target_pairs={{0,1},{1,0},{2,3},{3,2},{4,5},{5,4},{6,7},{7,6},{8,9},{9,8},{10,11... | collective-permute-start | bytes 2359304 | tf_op jit(solution)/shard_map/ppermute | solution.py:474
  300.4 20.5 %collective-permute-start.31 = (bf16[256,1536]{1,0:T(8,128)(2,1)S(1)}, bf16[256,1536]{1,0:T(8,128)(2,1)}, u32[]{:S(2)}, u32[]{:S(2)}) collective-permute-start(bf16[256,1536]{1,0:T(8,128)(2,1)S(1)} %collective-permute-done.29.grad_ref.refs_5_), channel_id=1, source_target_pairs={{1,2},{2,1},{5,6},{6,5},{9,10},{10,9},{13,14},{14,13},{17,18},{18,... | collective-permute-start | bytes 2359304 | tf_op jit(solution)/shard_map/ppermute | solution.py:478
  301.9 20.0 %collective-permute-start.32 = (bf16[256,1536]{1,0:T(8,128)(2,1)S(1)}, bf16[256,1536]{1,0:T(8,128)(2,1)S(1)}, u32[]{:S(2)}, u32[]{:S(2)}) collective-permute-start(bf16[256,1536]{1,0:T(8,128)(2,1)S(1)} %collective-permute-done.30), channel_id=1, source_target_pairs={{1,0},{2,3},{5,4},{6,7},{9,8},{10,11},{13,12},{14,15},{17,16},{18,... | collective-permute-start | bytes 2359304 | tf_op jit(solution)/shard_map/ppermute | solution.py:482
  322.8 19.3 %collective-permute-start.34 = (bf16[256,1536]{1,0:T(8,128)(2,1)}, bf16[256,1536]{1,0:T(8,128)(2,1)}, u32[]{:S(2)}, u32[]{:S(2)}) collective-permute-start(bf16[256,1536]{1,0:T(8,128)(2,1)} %collective-permute-done.31), channel_id=1, source_target_pairs={{1,0},{2,3},{5,4},{6,7},{9,8},{10,11},{13,12},{14,15},{17,16},{18,... | collective-permute-start | bytes 2359304 | tf_op jit(solution)/shard_map/ppermute | solution.py:482
  373.4 26.1 %collective-permute-start.36 = (bf16[4,480,1536]{2,1,0:T(8,128)(2,1)}, bf16[4,480,1536]{2,1,0:T(8,128)(2,1)}, u32[]{:S(2)}, u32[]{:S(2)}) collective-permute-start(bf16[4,480,1536]{2,1,0:T(8,128)(2,1)} %expert_grad.4), channel_id=1, source_target_pairs={{0,4},{4,0},{8,12},{12,8},{16,20},{20,16},{24,28},{28,24},{1,5},{5... | collective-permute-start | bytes 17694728 | tf_op jit(solution)/shard_map/ppermute | solution.py:470
  373.5 46.0 %collective-permute-start.35 = (bf16[256,1536]{1,0:T(8,128)(2,1)}, bf16[256,1536]{1,0:T(8,128)(2,1)}, u32[]{:S(2)}, u32[]{:S(2)}) collective-permute-start(bf16[256,1536]{1,0:T(8,128)(2,1)} %get-tuple-element.261), channel_id=1, source_target_pairs={{0,1},{3,2},{4,5},{7,6},{8,9},{11,10},{12,13},{15,14},{16,17},{19,... | collective-permute-start | bytes 2359304 | tf_op jit(solution)/shard_map/ppermute | solution.py:486
  433.4 67.1 %collective-permute-start.43 = (bf16[2,480,1536]{2,1,0:T(8,128)(2,1)}, bf16[2,480,1536]{2,1,0:T(8,128)(2,1)}, u32[]{:S(2)}, u32[]{:S(2)}) collective-permute-start(bf16[2,480,1536]{2,1,0:T(8,128)(2,1)} %get-tuple-element.281), channel_id=1, source_target_pairs={{0,8},{4,12},{8,0},{12,4},{16,24},{20,28},{24,16},{28,20},{1,9},{5... | collective-permute-start | bytes 8847368 | tf_op jit(solution)/shard_map/ppermute | solution.py:470
  452.7 20.4 %collective-permute-start.40 = (bf16[256,1536]{1,0:T(8,128)(2,1)}, bf16[256,1536]{1,0:T(8,128)(2,1)}, u32[]{:S(2)}, u32[]{:S(2)}) collective-permute-start(bf16[256,1536]{1,0:T(8,128)(2,1)} %add.259), channel_id=1, source_target_pairs={{0,1},{1,0},{2,3},{3,2},{4,5},{5,4},{6,7},{7,6},{8,9},{9,8},{10,11... | collective-permute-start | bytes 2359304 | tf_op jit(solution)/shard_map/ppermute | solution.py:474
  456.8 58.7 %collective-permute-start.44 = (bf16[2,384,1536]{2,1,0:T(8,128)(2,1)}, bf16[2,384,1536]{2,1,0:T(8,128)(2,1)}, u32[]{:S(2)}, u32[]{:S(2)}) collective-permute-start(bf16[2,384,1536]{2,1,0:T(8,128)(2,1)} %get-tuple-element.286), channel_id=1, source_target_pairs={{0,16},{4,20},{8,24},{12,28},{16,0},{20,4},{24,8},{28,12},{1,17},{... | collective-permute-start | bytes 7077896 | tf_op jit(solution)/shard_map/ppermute | solution.py:470
  489.9 65.6 %collective-permute-start.42 = (bf16[4,192,1536]{2,1,0:T(8,128)(2,1)}, bf16[4,192,1536]{2,1,0:T(8,128)(2,1)}, u32[]{:S(2)}, u32[]{:S(2)}) collective-permute-start(bf16[4,192,1536]{2,1,0:T(8,128)(2,1)} %get-tuple-element.300), channel_id=1, source_target_pairs={{0,4},{4,0},{8,12},{12,8},{16,20},{20,16},{24,28},{28,24},{1,5},{5... | collective-permute-start | bytes 7077896 | tf_op jit(solution)/shard_map/ppermute | solution.py:470
  489.9 100.2 %collective-permute-start.50 = (bf16[4,768,640]{2,1,0:T(8,128)(2,1)}, bf16[4,768,640]{2,1,0:T(8,128)(2,1)}, u32[]{:S(2)}, u32[]{:S(2)}) collective-permute-start(bf16[4,768,640]{2,1,0:T(8,128)(2,1)} %pad_maximum_fusion.refs_1_), channel_id=1, source_target_pairs={{0,4},{4,0},{8,12},{12,8},{16,20},{20,16},{24,28},{28,24},{1,5},{5... | collective-permute-start | bytes 11796488 | tf_op jit(solution)/shard_map/ppermute | solution.py:470
  490.4 31.1 %all-to-all-start.2 = ((bf16[4,256,384]{2,1,0:T(8,128)(2,1)}), bf16[4,256,384]{2,1,0:T(8,128)(2,1)}, u32[]{:S(2)}, u32[]{:S(2)}) async-start(bf16[4,256,384]{2,1,0:T(8,128)(2,1)} %get-tuple-element.297), calls=%async_computation.2 | async-start | bytes 1572864 | tf_op jit(solution)/shard_map/all_to_all | solution.py:516
  507.6 42.2 %collective-permute-start.47 = (bf16[480,1536]{1,0:T(8,128)(2,1)}, bf16[480,1536]{1,0:T(8,128)(2,1)}, u32[]{:S(2)}, u32[]{:S(2)}) collective-permute-start(bf16[480,1536]{1,0:T(8,128)(2,1)} %get-tuple-element.303), channel_id=1, source_target_pairs={{0,16},{4,20},{8,24},{12,28},{16,0},{20,4},{24,8},{28,12},{1,17},{... | collective-permute-start | bytes 4423688 | tf_op jit(solution)/shard_map/ppermute | solution.py:470
  520.9 25.3 %collective-permute-start.46 = (bf16[384,1536]{1,0:T(8,128)(2,1)}, bf16[384,1536]{1,0:T(8,128)(2,1)}, u32[]{:S(2)}, u32[]{:S(2)}) collective-permute-start(bf16[384,1536]{1,0:T(8,128)(2,1)} %get-tuple-element.306), channel_id=1, source_target_pairs={{0,8},{4,12},{8,0},{12,4},{16,24},{20,28},{24,16},{28,20},{1,9},{5... | collective-permute-start | bytes 3538952 | tf_op jit(solution)/shard_map/ppermute | solution.py:470
  548.9 29.1 %collective-permute-start.49 = (bf16[384,1536]{1,0:T(8,128)(2,1)S(1)}, bf16[384,1536]{1,0:T(8,128)(2,1)}, u32[]{:S(2)}, u32[]{:S(2)}) collective-permute-start(bf16[384,1536]{1,0:T(8,128)(2,1)S(1)} %blend_sum.2.refs_0_), channel_id=1, source_target_pairs={{0,8},{4,12},{8,0},{12,4},{16,24},{20,28},{24,16},{28,20},{1,9},{5... | collective-permute-start | bytes 3538952 | tf_op jit(solution)/shard_map/ppermute | solution.py:470
  554.5 61.1 %collective-permute-start.55 = (bf16[480,1536]{1,0:T(8,128)(2,1)}, bf16[480,1536]{1,0:T(8,128)(2,1)}, u32[]{:S(2)}, u32[]{:S(2)}) collective-permute-start(bf16[480,1536]{1,0:T(8,128)(2,1)} %blend_sum.3.refs_0_), channel_id=1, source_target_pairs={{0,16},{4,20},{8,24},{12,28},{16,0},{20,4},{24,8},{28,12},{1,17},{... | collective-permute-start | bytes 4423688 | tf_op jit(solution)/shard_map/ppermute | solution.py:470
  557.6 24.5 %collective-permute-start.48 = (bf16[192,1536]{1,0:T(8,128)(2,1)}, bf16[192,1536]{1,0:T(8,128)(2,1)}, u32[]{:S(2)}, u32[]{:S(2)}) collective-permute-start(bf16[192,1536]{1,0:T(8,128)(2,1)} %add_bitcast_fusion), channel_id=1, source_target_pairs={{0,1},{3,2},{4,5},{7,6},{8,9},{11,10},{12,13},{15,14},{16,17},{19,... | collective-permute-start | bytes 1769480 | tf_op jit(solution)/shard_map/ppermute | solution.py:486
  561.6 40.0 %all-to-all-start.3 = ((bf16[4,256,640]{2,1,0:T(8,128)(2,1)}), bf16[4,256,640]{2,1,0:T(8,128)(2,1)}, u32[]{:S(2)}, u32[]{:S(2)}) async-start(bf16[4,256,640]{2,1,0:T(8,128)(2,1)} %pad_maximum_fusion.2), calls=%async_computation.3 | async-start | bytes 2621440 | tf_op jit(solution)/shard_map/all_to_all | solution.py:516
  573.4 37.2 %collective-permute-start.54 = (bf16[4,192,640]{2,1,0:T(8,128)(2,1)}, bf16[4,192,640]{2,1,0:T(8,128)(2,1)}, u32[]{:S(2)}, u32[]{:S(2)}) collective-permute-start(bf16[4,192,640]{2,1,0:T(8,128)(2,1)} %get-tuple-element.327), channel_id=1, source_target_pairs={{0,4},{4,0},{8,12},{12,8},{16,20},{20,16},{24,28},{28,24},{1,5},{5... | collective-permute-start | bytes 2949128 | tf_op jit(solution)/shard_map/ppermute | solution.py:470
  584.6 36.6 %collective-permute-start.52 = (bf16[192,1536]{1,0:T(8,128)(2,1)}, bf16[192,1536]{1,0:T(8,128)(2,1)}, u32[]{:S(2)}, u32[]{:S(2)}) collective-permute-start(bf16[192,1536]{1,0:T(8,128)(2,1)} %bitcast_add_fusion.1), channel_id=1, source_target_pairs={{0,1},{3,2},{4,5},{7,6},{8,9},{11,10},{12,13},{15,14},{16,17},{19,... | collective-permute-start | bytes 1769480 | tf_op jit(solution)/shard_map/ppermute | solution.py:486
  588.6 32.6 %collective-permute-start.53 = (bf16[192,1536]{1,0:T(8,128)(2,1)}, bf16[192,1536]{1,0:T(8,128)(2,1)}, u32[]{:S(2)}, u32[]{:S(2)}) collective-permute-start(bf16[192,1536]{1,0:T(8,128)(2,1)} %bitcast_add_fusion.1), channel_id=1, source_target_pairs={{1,2},{2,1},{5,6},{6,5},{9,10},{10,9},{13,14},{14,13},{17,18},{18,... | collective-permute-start | bytes 1769480 | tf_op jit(solution)/shard_map/ppermute | solution.py:478
  615.0 50.7 %collective-permute-start.64 = (bf16[2,384,1536]{2,1,0:T(8,128)(2,1)S(1)}, bf16[2,384,1536]{2,1,0:T(8,128)(2,1)}, u32[]{:S(2)}, u32[]{:S(2)}) collective-permute-start(bf16[2,384,1536]{2,1,0:T(8,128)(2,1)S(1)} %copy-done.29), channel_id=1, source_target_pairs={{0,16},{4,20},{8,24},{12,28},{16,0},{20,4},{24,8},{28,12},{1,17},{... | collective-permute-start | bytes 7077896 | tf_op jit(solution)/shard_map/ppermute | solution.py:470
  619.6 62.7 %collective-permute-start.65 = (bf16[2,480,1536]{2,1,0:T(8,128)(2,1)S(1)}, bf16[2,480,1536]{2,1,0:T(8,128)(2,1)S(1)}, u32[]{:S(2)}, u32[]{:S(2)}) collective-permute-start(bf16[2,480,1536]{2,1,0:T(8,128)(2,1)S(1)} %blend_stack.3.refs_0_), channel_id=1, source_target_pairs={{0,8},{4,12},{8,0},{12,4},{16,24},{20,28},{24,16},{28,20},{1,9},{5... | collective-permute-start | bytes 8847368 | tf_op jit(solution)/shard_map/ppermute | solution.py:470
  629.0 21.6 %collective-permute-start.62 = (bf16[192,1536]{1,0:T(8,128)(2,1)S(1)}, bf16[192,1536]{1,0:T(8,128)(2,1)S(1)}, u32[]{:S(2)}, u32[]{:S(2)}) collective-permute-start(bf16[192,1536]{1,0:T(8,128)(2,1)S(1)} %bitcast_add_fusion), channel_id=1, source_target_pairs={{0,1},{1,0},{2,3},{3,2},{4,5},{5,4},{6,7},{7,6},{8,9},{9,8},{10,11... | collective-permute-start | bytes 1769480 | tf_op jit(solution)/shard_map/ppermute | solution.py:474
  629.0 22.2 %collective-permute-start.63 = (bf16[192,1536]{1,0:T(8,128)(2,1)S(1)}, bf16[192,1536]{1,0:T(8,128)(2,1)S(1)}, u32[]{:S(2)}, u32[]{:S(2)}) collective-permute-start(bf16[192,1536]{1,0:T(8,128)(2,1)S(1)} %add.274), channel_id=1, source_target_pairs={{1,2},{2,1},{5,6},{6,5},{9,10},{10,9},{13,14},{14,13},{17,18},{18,... | collective-permute-start | bytes 1769480 | tf_op jit(solution)/shard_map/ppermute | solution.py:478
  686.6 24.9 %collective-permute-start.74 = (bf16[4,480,1536]{2,1,0:T(8,128)(2,1)}, bf16[4,480,1536]{2,1,0:T(8,128)(2,1)}, u32[]{:S(2)}, u32[]{:S(2)}) collective-permute-start(bf16[4,480,1536]{2,1,0:T(8,128)(2,1)} %blend_four.3.refs_1_), channel_id=1, source_target_pairs={{0,4},{4,0},{8,12},{12,8},{16,20},{20,16},{24,28},{28,24},{1,5},{5... | collective-permute-start | bytes 17694728 | tf_op jit(solution)/shard_map/ppermute | solution.py:470
  686.6 23.1 %collective-permute-start.73 = (bf16[4,384,1536]{2,1,0:T(8,128)(2,1)}, bf16[4,384,1536]{2,1,0:T(8,128)(2,1)}, u32[]{:S(2)}, u32[]{:S(2)}) collective-permute-start(bf16[4,384,1536]{2,1,0:T(8,128)(2,1)} %blend_four.2.refs_0_), channel_id=1, source_target_pairs={{0,4},{4,0},{8,12},{12,8},{16,20},{20,16},{24,28},{28,24},{1,5},{5... | collective-permute-start | bytes 14155784 | tf_op jit(solution)/shard_map/ppermute | solution.py:470
  690.6 45.7 %collective-permute-start.70 = (bf16[96,1536]{1,0:T(8,128)(2,1)S(1)}, bf16[96,1536]{1,0:T(8,128)(2,1)S(1)}, u32[]{:S(2)}, u32[]{:S(2)}) collective-permute-start(bf16[96,1536]{1,0:T(8,128)(2,1)S(1)} %get-tuple-element.352), channel_id=1, source_target_pairs={{0,1},{1,0},{2,3},{3,2},{4,5},{5,4},{6,7},{7,6},{8,9},{9,8},{10,11... | collective-permute-start | bytes 884744 | tf_op jit(solution)/shard_map/ppermute | solution.py:474
  703.3 33.0 %collective-permute-start.71 = (bf16[96,1536]{1,0:T(8,128)(2,1)S(1)}, bf16[96,1536]{1,0:T(8,128)(2,1)S(1)}, u32[]{:S(2)}, u32[]{:S(2)}) collective-permute-start(bf16[96,1536]{1,0:T(8,128)(2,1)S(1)} %get-tuple-element.353), channel_id=1, source_target_pairs={{0,2},{1,3},{2,0},{3,1},{4,6},{5,7},{6,4},{7,5},{8,10},{9,11},{10,... | collective-permute-start | bytes 884744 | tf_op jit(solution)/shard_map/ppermute | solution.py:474
  707.6 28.7 %collective-permute-start.72 = (bf16[96,1536]{1,0:T(8,128)(2,1)S(1)}, bf16[96,1536]{1,0:T(8,128)(2,1)S(1)}, u32[]{:S(2)}, u32[]{:S(2)}) collective-permute-start(bf16[96,1536]{1,0:T(8,128)(2,1)S(1)} %get-tuple-element.354), channel_id=1, source_target_pairs={{0,3},{1,2},{2,1},{3,0},{4,7},{5,6},{6,5},{7,4},{8,11},{9,10},{10,... | collective-permute-start | bytes 884744 | tf_op jit(solution)/shard_map/ppermute | solution.py:474
  709.7 26.8 %collective-permute-start.69 = (bf16[192,1536]{1,0:T(8,128)(2,1)S(1)}, bf16[192,1536]{1,0:T(8,128)(2,1)S(1)}, u32[]{:S(2)}, u32[]{:S(2)}) collective-permute-start(bf16[192,1536]{1,0:T(8,128)(2,1)S(1)} %add.293), channel_id=1, source_target_pairs={{0,16},{4,20},{8,24},{12,28},{16,0},{20,4},{24,8},{28,12},{1,17},{... | collective-permute-start | bytes 1769480 | tf_op jit(solution)/shard_map/ppermute | solution.py:470
  711.5 25.9 %collective-permute-start.68 = (bf16[2,192,640]{2,1,0:T(8,128)(2,1)S(1)}, bf16[2,192,640]{2,1,0:T(8,128)(2,1)S(1)}, u32[]{:S(2)}, u32[]{:S(2)}) collective-permute-start(bf16[2,192,640]{2,1,0:T(8,128)(2,1)S(1)} %pad_maximum_fusion.10), channel_id=1, source_target_pairs={{0,16},{4,20},{8,24},{12,28},{16,0},{20,4},{24,8},{28,12},{1,17},{... | collective-permute-start | bytes 1474568 | tf_op jit(solution)/shard_map/ppermute | solution.py:470
  (180 other events, 1669.6 us)

commit v6 on v5

--- a/solution.py
+++ b/solution.py
@@ -1497,8 +1497,8 @@
     "M", "K", "R", "M", "K", "M", "M", "M", "M", "R", "M", "M",
 )
 LATE = (
-    "L", "0", "0", "0", "1", "L", "1", "1", "L", "L", "O", "0", "1", "L", "L", "1", "0", "O", "Q", "1", "O", "L", "Q", "0",
-    "O", "L", "Q", "Q", "O", "Q", "1", "0", "O", "Q", "S", "O", "Q", "1", "0", "S", "O", "Q", "L", "L", "L", "Q", "O", "S",
+    "L", "0", "1", "0", "0", "L", "1", "1", "L", "L", "0", "L", "L", "1", "O", "0", "1", "L", "Q", "1", "0", "O", "Q", "L",
+    "O", "Q", "O", "Q", "O", "Q", "1", "0", "O", "Q", "S", "O", "Q", "1", "0", "S", "O", "Q", "L", "L", "L", "Q", "O", "S",
     "L",
 )
 
@@ -1856,16 +1856,10 @@
                 )
             )
 
-        if index == 0:
-            came = flip(grad_of(1 - core), 1)
-            yield
-            keep = grad_of(core)
-            yield
-        else:
-            keep = grad_of(core)
-            yield
-            came = flip(grad_of(1 - core), 1)
-            yield
+        came = flip(grad_of(1 - core), 1)
+        yield
+        keep = grad_of(core)
+        yield
         x_first = index % 2 == 0
         first, second = (2, 4) if x_first else (4, 2)
         picked = ((1, 3), (0, 2)) if x_first else ((2, 3), (0, 1))

time: 777 us -> 801 us (1.031)
  local copies, waits for them, and re-layouts: 68.7 us -> 79.4 us
    ppermute x40, waiting for transfers between devices: 90.8 us -> 67.9 us  [flip(): lax.ppermute(value, 'ctx', [(index, index ^ bit) for index in range(8)])]
    ppermute x8, waiting for transfers between devices: 33.9 us -> 50.5 us  [line_inward(): return lax.ppermute(value, 'wt', [(0, 1), (3, 2)])]
    all_to_all x3, waiting for transfers between devices: 11.5 us -> 24.5 us  [chips_exchange(): lax.all_to_all(blocks, 'ctx', split_axis=0, concat_axis=0, tiled=True, ax...]
    unnamed x291 -> x303, local copies, waits for them, and re-layouts: 48.7 us -> 59.4 us
  transfers between devices with their start and end apart: 85 -> 85, of which waited for: 38 -> 34; matrix products, arithmetic and copies ran while one was open for 7% -> 7% of each run, Pallas kernels for 34% -> 34%
where the time goes in v6:
time: 801 us; the launch traced here: 793 us
  Pallas kernels  298 us (37%)
  waiting for transfers between devices  225 us (28%)
  starting transfers between devices  137 us (17%)
  local copies, waits for them, and re-layouts  79.4 us (10%)
  other arithmetic  47.1 us (6%)
    pallas_call x33, Pallas kernels, call(): pl.pallas_call(kernel, grid_spec=pltpu.PrefetchScalarGridSpec(num_scalar_...  274 us
    ppermute x40, waiting for transfers between devices, flip(): lax.ppermute(value, 'ctx', [(index, index ^ bit) for index in range(8)])  67.9 us
    ppermute x17, waiting for transfers between devices, line_swap(): lax.ppermute(value, 'wt', [(index, index ^ offset) for index in range(4)])  64.3 us
    unnamed x303, local copies, waits for them, and re-layouts  59.4 us
    ppermute x8, waiting for transfers between devices, line_inward(): return lax.ppermute(value, 'wt', [(0, 1), (3, 2)])  50.5 us
    ppermute x17, starting transfers between devices, line_swap(): lax.ppermute(value, 'wt', [(index, index ^ offset) for index in range(4)])  38.8 us
    ppermute x8, starting transfers between devices, line_inward(): return lax.ppermute(value, 'wt', [(0, 1), (3, 2)])  34.7 us
    ppermute x40, starting transfers between devices, flip(): lax.ppermute(value, 'ctx', [(index, index ^ bit) for index in range(8)])  28.4 us
  transfers between devices with their start and end apart: 85, of which 34 were waited for; matrix products, arithmetic and copies ran while one was open for 7% of the time, Pallas kernels for 34%

profile of v6, /device:TPU:0, one launch (start us, length us, event | category | flops | bytes accessed | tf_op | source)
XLA Modules:
  0.0 793.2 jit_solution(18389565022907960873)
XLA Ops:
  9.8 4.9 all-to-all-start.1
  27.0 22.9 %collective-permute-done.5 = bf16[2,192,640]{2,1,0:T(8,128)(2,1)S(1)} collective-permute-done((bf16[2,192,640]{2,1,0:T(8,128)(2,1)S(1)}, bf16[2,192,640]{2,1,0:T(8,128)(2,1)S(1)}, u32[]{:S(2)}, u32[]{:S(2)}) %collective-permute-start.5) | collective-permute-done | bytes 491552 | tf_op jit(solution)/shard_map/ppermute | solution.py:474
  54.2 4.7 all-to-all-start
  61.8 6.9 collective-permute-done.6
  71.8 6.8 project.1
  84.3 11.5 %attend.1 = (bf16[4,256,384]{2,1,0:T(8,128)(2,1)S(1)}, f32[8,1,384]{2,1,0:T(1,128)S(1)}) custom-call(s32[2]{0:T(128)S(1)} %pad_add_fusion.meta.meta_ref, bf16[4,256,384]{2,1,0:T(8,128)(2,1)S(1)} %copy-done.45, bf16[4,256,256]{2,1,0:T(8,128)(2,1)} %get-tuple-element.198.mine_ref, bf16[4,256,256]{2,1,0:T(8,128)(2,1)S(1)} %collective-permute-done.9.other_ref), custom_call_target="tpu_custom_call" | custom-call | flops 300000000 | bytes 1000 | tf_op jit(solution)/shard_map/attend/pallas_call | solution.py:585
  99.2 12.0 %all-to-all-done.refs_4_ = bf16[4,192,1536]{2,1,0:T(8,128)(2,1)} async-done(((bf16[4,192,1536]{2,1,0:T(8,128)(2,1)}), bf16[4,192,1536]{2,1,0:T(8,128)(2,1)}, u32[]{:S(2)}, u32[]{:S(2)}) %all-to-all-start) | async-done | bytes 2359328 | tf_op jit(solution)/shard_map/all_to_all | solution.py:527
  119.8 5.0 collective-permute-done.11.refs_2_
  126.3 6.2 leave.1
  141.8 11.7 %experts.4 = (bf16[4,256,1024]{2,1,0:T(8,128)(2,1)S(1)}, bf16[256,512]{1,0:T(8,128)(2,1)S(1)}, bf16[256,1536]{1,0:T(8,128)(2,1)S(1)}) custom-call(s32[2]{0:T(128)S(1)} %pad_add_fusion.meta.meta_ref, bf16[256,1536]{1,0:T(8,128)(2,1)S(1)} %get-tuple-element.211.rows_ref.refs_0_, f32[4,256,1]{2,1,0:T(8,128)S(1)} %copy-done.40, ...), custom_call_target="tpu_custom_call" | custom-call | flops 300000000 | bytes 1000 | tf_op jit(solution)/shard_map/experts/pallas_call | solution.py:585
  162.4 12.0 %experts.5 = (bf16[4,256,1024]{2,1,0:T(8,128)(2,1)S(1)}, bf16[256,512]{1,0:T(8,128)(2,1)S(1)}, bf16[256,1536]{1,0:T(8,128)(2,1)S(1)}) custom-call(s32[2]{0:T(128)S(1)} %pad_add_fusion.meta.meta_ref, bf16[256,1536]{1,0:T(8,128)(2,1)} %collective-permute-done.15.rows_ref.refs_1_, f32[4,256,1]{2,1,0:T(8,128)S(1)} %copy.40.gates_ref, ...), custom_call_target="tpu_custom_call" | custom-call | flops 300000000 | bytes 1000 | tf_op jit(solution)/shard_map/experts/pallas_call | solution.py:585
  185.5 11.7 %experts.6 = (bf16[4,256,1024]{2,1,0:T(8,128)(2,1)S(1)}, bf16[256,512]{1,0:T(8,128)(2,1)S(1)}, bf16[256,1536]{1,0:T(8,128)(2,1)S(1)}) custom-call(s32[2]{0:T(128)S(1)} %pad_add_fusion.meta.meta_ref, bf16[256,1536]{1,0:T(8,128)(2,1)S(1)} %broadcast_select_fusion.3.rows_ref.refs_2_, f32[4,256,1]{2,1,0:T(8,128)S(1)} %copy-done.38, ...), custom_call_target="tpu_custom_call" | custom-call | flops 300000000 | bytes 1000 | tf_op jit(solution)/shard_map/experts/pallas_call | solution.py:585
  200.4 11.7 %experts.7 = (bf16[4,256,1024]{2,1,0:T(8,128)(2,1)S(1)}, bf16[256,512]{1,0:T(8,128)(2,1)S(1)}, bf16[256,1536]{1,0:T(8,128)(2,1)S(1)}) custom-call(s32[2]{0:T(128)S(1)} %pad_add_fusion.meta.meta_ref, bf16[256,1536]{1,0:T(8,128)(2,1)S(1)} %broadcast_select_fusion.2.rows_ref.refs_3_, f32[4,256,1]{2,1,0:T(8,128)S(1)} %copy-done.36, ...), custom_call_target="tpu_custom_call" | custom-call | flops 300000000 | bytes 1000 | tf_op jit(solution)/shard_map/experts/pallas_call | solution.py:585
  212.2 4.9 collective-permute-start.21
  221.0 13.5 %collective-permute-done.21 = bf16[256,1536]{1,0:T(8,128)(2,1)S(1)} collective-permute-done((bf16[256,1536]{1,0:T(8,128)(2,1)S(1)}, bf16[256,1536]{1,0:T(8,128)(2,1)S(1)}, u32[]{:S(2)}, u32[]{:S(2)}) %collective-permute-start.21) | collective-permute-done | bytes 786464 | tf_op jit(solution)/shard_map/ppermute | solution.py:486
  243.6 12.2 %collective-permute-done.24 = bf16[256,1536]{1,0:T(8,128)(2,1)S(1)} collective-permute-done((bf16[256,1536]{1,0:T(8,128)(2,1)S(1)}, bf16[256,1536]{1,0:T(8,128)(2,1)S(1)}, u32[]{:S(2)}, u32[]{:S(2)}) %collective-permute-start.24) | collective-permute-done | bytes 786464 | tf_op jit(solution)/shard_map/ppermute | solution.py:486
  262.7 13.8 %collective-permute-done.27 = bf16[256,1536]{1,0:T(8,128)(2,1)S(1)} collective-permute-done((bf16[256,1536]{1,0:T(8,128)(2,1)S(1)}, bf16[256,1536]{1,0:T(8,128)(2,1)S(1)}, u32[]{:S(2)}, u32[]{:S(2)}) %collective-permute-start.27) | collective-permute-done | bytes 786464 | tf_op jit(solution)/shard_map/ppermute | solution.py:474
  284.1 13.0 %experts_back.4 = (bf16[4,256,1024]{2,1,0:T(8,128)(2,1)S(1)}, bf16[4,256,512]{2,1,0:T(8,128)(2,1)S(1)}, bf16[1,256,512]{2,1,0:T(8,128)(2,1)S(1)}, bf16[1,256,256]{2,1,0:T(8,128)(2,1)S(1)}, bf16[256,1536]{1,0:T(8,128)(2,1)S(1)}) custom-call(s32[2]{0:T(128)S(1)} %pad_add_fusion.meta.meta_ref, bf16[256,1536]{1,0:T(8,128)(2,1)S(1)} %get-tuple-element.375.grad_ref.refs_4_, ...), custom_call_target="tpu_custom_call" | custom-call | flops 300000000 | bytes 1000 | tf_op jit(solution)/shard_map/experts_back/pallas_call | solution.py:585
  303.2 13.0 %experts_back.5 = (bf16[4,256,1024]{2,1,0:T(8,128)(2,1)S(1)}, bf16[4,256,512]{2,1,0:T(8,128)(2,1)S(1)}, bf16[1,256,512]{2,1,0:T(8,128)(2,1)S(1)}, bf16[1,256,256]{2,1,0:T(8,128)(2,1)S(1)}, bf16[256,1536]{1,0:T(8,128)(2,1)S(1)}) custom-call(s32[2]{0:T(128)S(1)} %pad_add_fusion.meta.meta_ref, bf16[256,1536]{1,0:T(8,128)(2,1)S(1)} %collective-permute-done.29.grad_ref.refs_5_, ...), custom_call_target="tpu_custom_call" | custom-call | flops 300000000 | bytes 1000 | tf_op jit(solution)/shard_map/experts_back/pallas_call | solution.py:585
  316.3 4.5 pad_maximum_fusion.refs_1_
  326.7 13.0 %experts_back.6 = (bf16[4,256,1024]{2,1,0:T(8,128)(2,1)S(1)}, bf16[4,256,512]{2,1,0:T(8,128)(2,1)S(1)}, bf16[1,256,512]{2,1,0:T(8,128)(2,1)S(1)}, bf16[1,256,256]{2,1,0:T(8,128)(2,1)S(1)}, bf16[256,1536]{1,0:T(8,128)(2,1)S(1)}) custom-call(s32[2]{0:T(128)S(1)} %pad_add_fusion.meta.meta_ref, bf16[256,1536]{1,0:T(8,128)(2,1)S(1)} %broadcast_select_fusion.1.grad_ref.refs_6_, ...), custom_call_target="tpu_custom_call" | custom-call | flops 300000000 | bytes 1000 | tf_op jit(solution)/shard_map/experts_back/pallas_call | solution.py:585
  343.5 14.4 %experts_back.7 = (bf16[4,256,1024]{2,1,0:T(8,128)(2,1)S(1)}, bf16[4,256,512]{2,1,0:T(8,128)(2,1)S(1)}, bf16[1,256,512]{2,1,0:T(8,128)(2,1)S(1)}, bf16[1,256,256]{2,1,0:T(8,128)(2,1)S(1)}, bf16[256,1536]{1,0:T(8,128)(2,1)}) custom-call(s32[2]{0:T(128)S(1)} %pad_add_fusion.meta.meta_ref, bf16[256,1536]{1,0:T(8,128)(2,1)S(1)} %broadcast_select_fusion.grad_ref.refs_7_, ...), custom_call_target="tpu_custom_call" | custom-call | flops 300000000 | bytes 1000 | tf_op jit(solution)/shard_map/experts_back/pallas_call | solution.py:585
  360.5 13.0 %expert_grad.4 = bf16[4,480,1536]{2,1,0:T(8,128)(2,1)} custom-call(s32[3]{0:T(128)S(1)} %add_add_fusion.meta, bf16[256,1536]{1,0:T(8,128)(2,1)S(1)} %copy-done.20, bf16[256,1536]{1,0:T(8,128)(2,1)} %collective-permute-done.15.rows_ref.refs_1_, bf16[256,1536]{1,0:T(8,128)(2,1)S(1)} %broadcast_select_fusion.3.rows_ref.refs_2_, ...), custom_call_target="tpu_custom_call" | custom-call | flops 300000000 | bytes 1000 | tf_op jit(solution)/shard_map/expert_grad/pallas_call | solution.py:585
  376.0 10.2 %expert_grad.5 = bf16[4,384,1536]{2,1,0:T(8,128)(2,1)} custom-call(s32[3]{0:T(128)S(1)} %add_add_fusion.1.meta, bf16[256,1536]{1,0:T(8,128)(2,1)S(1)} %copy-done.21, bf16[256,1536]{1,0:T(8,128)(2,1)} %collective-permute-done.15.rows_ref.refs_1_, bf16[256,1536]{1,0:T(8,128)(2,1)S(1)} %broadcast_select_fusion.3.rows_ref.refs_2_, ...), custom_call_target="tpu_custom_call" | custom-call | flops 300000000 | bytes 1000 | tf_op jit(solution)/shard_map/expert_grad/pallas_call | solution.py:585
  386.7 5.4 collective-permute-start.35
  400.7 12.9 %expert_grad.6.refs_0_ = bf16[4,480,1536]{2,1,0:T(8,128)(2,1)} custom-call(s32[3]{0:T(128)S(1)} %add_add_fusion.2.meta, bf16[256,1536]{1,0:T(8,128)(2,1)S(1)} %copy-done.21, bf16[256,1536]{1,0:T(8,128)(2,1)} %collective-permute-done.15.rows_ref.refs_1_, bf16[256,1536]{1,0:T(8,128)(2,1)S(1)} %broadcast_select_fusion.3.rows_ref.refs_2_, ...), custom_call_target="tpu_custom_call" | custom-call | flops 300000000 | bytes 1000 | tf_op jit(solution)/shard_map/expert_grad/pallas_call | solution.py:585
  413.6 7.8 blend_split.2
  432.3 10.1 %expert_grad.7.refs_0_ = bf16[4,384,1536]{2,1,0:T(8,128)(2,1)} custom-call(s32[3]{0:T(128)S(1)} %add_add_fusion.3.meta, bf16[256,1536]{1,0:T(8,128)(2,1)S(1)} %copy-done.22, bf16[256,1536]{1,0:T(8,128)(2,1)} %collective-permute-done.15.rows_ref.refs_1_, bf16[256,1536]{1,0:T(8,128)(2,1)S(1)} %broadcast_select_fusion.3.rows_ref.refs_2_, ...), custom_call_target="tpu_custom_call" | custom-call | flops 300000000 | bytes 1000 | tf_op jit(solution)/shard_map/expert_grad/pallas_call | solution.py:585
  442.4 6.1 blend_split.3
  454.7 16.7 %collective-permute-done.40 = bf16[256,1536]{1,0:T(8,128)(2,1)S(1)} collective-permute-done((bf16[256,1536]{1,0:T(8,128)(2,1)S(1)}, bf16[256,1536]{1,0:T(8,128)(2,1)S(1)}, u32[]{:S(2)}, u32[]{:S(2)}) %collective-permute-start.40) | collective-permute-done | bytes 786464 | tf_op jit(solution)/shard_map/ppermute | solution.py:474
  472.9 7.1 enter_back.1
  498.1 16.6 %all-to-all-done.2.refs_1_ = bf16[4,256,384]{2,1,0:T(8,128)(2,1)S(1)} async-done(((bf16[4,256,384]{2,1,0:T(8,128)(2,1)}), bf16[4,256,384]{2,1,0:T(8,128)(2,1)S(1)}, u32[]{:S(2)}, u32[]{:S(2)}) %all-to-all-start.2) | async-done | bytes 786464 | tf_op jit(solution)/shard_map/all_to_all | solution.py:516
  519.6 16.3 %attend_back.1 = (bf16[4,256,384]{2,1,0:T(8,128)(2,1)S(1)}, f32[4,256,256]{2,1,0:T(8,128)S(1)}, bf16[4,256,256]{2,1,0:T(8,128)(2,1)}) custom-call(s32[2]{0:T(128)S(1)} %pad_add_fusion.meta.meta_ref, bf16[4,256,384]{2,1,0:T(8,128)(2,1)S(1)} %copy-done.46, bf16[4,256,256]{2,1,0:T(8,128)(2,1)} %get-tuple-element.198.mine_ref, ...), custom_call_target="tpu_custom_call" | custom-call | flops 300000000 | bytes 1000 | tf_op jit(solution)/shard_map/attend_back/pallas_call | solution.py:585
  559.4 12.8 %collective-permute-done.45.refs_1_ = bf16[480,1536]{1,0:T(8,128)(2,1)} collective-permute-done((bf16[480,1536]{1,0:T(8,128)(2,1)}, bf16[480,1536]{1,0:T(8,128)(2,1)}, u32[]{:S(2)}, u32[]{:S(2)}) %collective-permute-start.45) | collective-permute-done | bytes 1474592 | tf_op jit(solution)/shard_map/ppermute | solution.py:470
  572.2 4.6 blend_sum.2.refs_0_
  583.5 7.9 all-to-all-done.3.refs_0_
  592.9 8.8 %finish.1 = (f32[1,256,1536]{2,1,0:T(8,128)}, f32[1,1536]{1,0:T(1,128)S(1)}) custom-call(s32[2]{0:T(128)S(1)} %pad_add_fusion.meta.meta_ref, bf16[4,256,640]{2,1,0:T(8,128)(2,1)} %all-to-all-done.3.refs_0_, bf16[4,768,640]{2,1,0:T(8,128)(2,1)} %pad_maximum_fusion.refs_1_, bf16[4,768,640]{2,1,0:T(8,128)(2,1)} %collective-permute-done.47.refs_2_, ...), custom_call_target="tpu_custom_call" | custom-call | flops 300000000 | bytes 1000 | tf_op jit(solution)/shard_map/finish/pallas_call | solution.py:585
  601.7 6.4 weight_grad.3
  625.5 5.4 collective-permute-start.55
  632.5 10.0 %collective-permute-done.55 = bf16[192,1536]{1,0:T(8,128)(2,1)S(1)} collective-permute-done((bf16[192,1536]{1,0:T(8,128)(2,1)S(1)}, bf16[192,1536]{1,0:T(8,128)(2,1)S(1)}, u32[]{:S(2)}, u32[]{:S(2)}) %collective-permute-start.55) | collective-permute-done | bytes 589856 | tf_op jit(solution)/shard_map/ppermute | solution.py:486
  653.7 10.5 %collective-permute-done.54 = bf16[192,640]{1,0:T(8,128)(2,1)S(1)} collective-permute-done((bf16[192,640]{1,0:T(8,128)(2,1)S(1)}, bf16[192,640]{1,0:T(8,128)(2,1)S(1)}, u32[]{:S(2)}, u32[]{:S(2)}) %collective-permute-start.54) | collective-permute-done | bytes 245792 | tf_op jit(solution)/shard_map/ppermute | solution.py:486
  677.7 15.4 %collective-permute-start.60 = (bf16[192,640]{1,0:T(8,128)(2,1)S(1)}, bf16[192,640]{1,0:T(8,128)(2,1)S(1)}, u32[]{:S(2)}, u32[]{:S(2)}) collective-permute-start(bf16[192,640]{1,0:T(8,128)(2,1)S(1)} %bitcast_add_fusion.3), channel_id=1, source_target_pairs={{0,1},{1,0},{2,3},{3,2},{4,5},{5,4},{6,7},{7,6},{8,9},{9,8},{10,11... | collective-permute-start | bytes 737288 | tf_op jit(solution)/shard_map/ppermute | solution.py:474
  698.4 4.8 collective-permute-done.64.refs_1_
  715.2 12.6 %collective-permute-done.67 = bf16[192,1536]{1,0:T(8,128)(2,1)S(1)} collective-permute-done((bf16[192,1536]{1,0:T(8,128)(2,1)S(1)}, bf16[192,1536]{1,0:T(8,128)(2,1)S(1)}, u32[]{:S(2)}, u32[]{:S(2)}) %collective-permute-start.67) | collective-permute-done | bytes 589856 | tf_op jit(solution)/shard_map/ppermute | solution.py:470
  736.1 12.6 %place_pair.2.refs_0_ = f32[4,1536,1536]{2,1,0:T(8,128)} custom-call(s32[2]{0:T(128)S(1)} %pad_add_fusion.meta.meta_ref, bf16[4,384,1536]{2,1,0:T(8,128)(2,1)} %blend_four.2.refs_0_, bf16[4,384,1536]{2,1,0:T(8,128)(2,1)} %collective-permute-done.73.refs_1_), custom_call_target="tpu_custom_call" | custom-call | flops 300000000 | bytes 1000 | tf_op jit(solution)/shard_map/place_pair/pallas_call | solution.py:1363
  748.7 11.6 %place_pair.3 = f32[4,1536,1536]{2,1,0:T(8,128)} custom-call(s32[2]{0:T(128)S(1)} %pad_add_fusion.meta.meta_ref, f32[4,1536,1536]{2,1,0:T(8,128)} %place_pair.2.refs_0_, bf16[4,480,1536]{2,1,0:T(8,128)(2,1)S(1)} %bitcast.107, bf16[4,480,1536]{2,1,0:T(8,128)(2,1)} %collective-permute-done.74.refs_2_), custom_call_target="tpu_custom_call", output_to_operand_aliasing={{}: (1, {})} | custom-call | flops 300000000 | bytes 1000 | tf_op jit(solution)/shard_map/place_pair/pallas_call | solution.py:1363
  763.9 5.0 collective-permute-done.53
  781.8 8.2 %place_shared.1 = f32[384,3072]{1,0:T(8,128)} custom-call(s32[2]{0:T(128)S(1)} %pad_add_fusion.meta.meta_ref, bf16[4,96,1536]{2,1,0:T(8,128)(2,1)S(1)} %pad_maximum_fusion.4.mine_low.mine_high, bf16[4,96,1536]{2,1,0:T(8,128)(2,1)S(1)} %pad_maximum_fusion.4.mine_low.mine_high, bf16[4,96,1536]{2,1,0:T(8,128)(2,1)} %collective-permute-done.80.other_low.other_high, ...), custom_call_target="tpu_custom_call" | custom-call | flops 300000000 | bytes 1000 | tf_op jit(solution)/shard_map/place_shared/pallas_call | solution.py:585
  (570 shorter events, 297.8 us)
Async XLA Ops:
  9.8 42.8 %all-to-all-start.1 = ((bf16[4,256,1536]{2,1,0:T(8,128)(2,1)}), bf16[4,256,1536]{2,1,0:T(8,128)(2,1)}, u32[]{:S(2)}, u32[]{:S(2)}) async-start(bf16[4,256,1536]{2,1,0:T(8,128)(2,1)} %broadcast_in_dim.55), calls=%async_computation.1 | async-start | bytes 6291456 | tf_op jit(solution)/shard_map/all_to_all | solution.py:516
  20.5 29.5 %collective-permute-start.5 = (bf16[2,192,640]{2,1,0:T(8,128)(2,1)S(1)}, bf16[2,192,640]{2,1,0:T(8,128)(2,1)S(1)}, u32[]{:S(2)}, u32[]{:S(2)}) collective-permute-start(bf16[2,192,640]{2,1,0:T(8,128)(2,1)S(1)} %pad_maximum_fusion.9), channel_id=1, source_target_pairs={{0,2},{1,3},{2,0},{3,1},{4,6},{5,7},{6,4},{7,5},{8,10},{9,11},{10,... | collective-permute-start | bytes 1474568 | tf_op jit(solution)/shard_map/ppermute | solution.py:474
  23.2 28.0 %collective-permute-start.4 = (f32[2,32,256]{2,1,0:T(8,128)S(1)}, f32[2,32,256]{2,1,0:T(8,128)S(1)}, u32[]{:S(2)}, u32[]{:S(2)}) collective-permute-start(f32[2,32,256]{2,1,0:T(8,128)S(1)} %pad_maximum_fusion.16), channel_id=1, source_target_pairs={{0,2},{1,3},{2,0},{3,1},{4,6},{5,7},{6,4},{7,5},{8,10},{9,11},{10,... | collective-permute-start | bytes 196616 | tf_op jit(solution)/shard_map/ppermute | solution.py:474
  24.7 27.7 %collective-permute-start.3 = (bf16[2,48,768]{2,1,0:T(8,128)(2,1)S(1)}, bf16[2,48,768]{2,1,0:T(8,128)(2,1)S(1)}, u32[]{:S(2)}, u32[]{:S(2)}) collective-permute-start(bf16[2,48,768]{2,1,0:T(8,128)(2,1)S(1)} %pad_maximum_fusion.14), channel_id=1, source_target_pairs={{0,2},{1,3},{2,0},{3,1},{4,6},{5,7},{6,4},{7,5},{8,10},{9,11},{10,... | collective-permute-start | bytes 442376 | tf_op jit(solution)/shard_map/ppermute | solution.py:474
  54.2 57.0 %all-to-all-start = ((bf16[4,192,1536]{2,1,0:T(8,128)(2,1)}), bf16[4,192,1536]{2,1,0:T(8,128)(2,1)}, u32[]{:S(2)}, u32[]{:S(2)}) async-start(bf16[4,192,1536]{2,1,0:T(8,128)(2,1)} %broadcast_in_dim.54), calls=%async_computation | async-start | bytes 4718592 | tf_op jit(solution)/shard_map/all_to_all | solution.py:527
  111.2 26.1 %collective-permute-start.14 = (bf16[4,4,48,768]{3,2,1,0:T(8,128)(2,1)}, bf16[4,4,48,768]{3,2,1,0:T(8,128)(2,1)}, u32[]{:S(2)}, u32[]{:S(2)}) collective-permute-start(bf16[4,4,48,768]{3,2,1,0:T(8,128)(2,1)} %pad_maximum_fusion.3.mine), channel_id=1, source_target_pairs={{0,4},{4,0},{8,12},{12,8},{16,20},{20,16},{24,28},{28,24},{1,5},{5... | collective-permute-start | bytes 3538952 | tf_op jit(solution)/shard_map/ppermute | solution.py:470
  133.7 22.0 %collective-permute-start.15 = (bf16[256,1536]{1,0:T(8,128)(2,1)S(1)}, bf16[256,1536]{1,0:T(8,128)(2,1)}, u32[]{:S(2)}, u32[]{:S(2)}) collective-permute-start(bf16[256,1536]{1,0:T(8,128)(2,1)S(1)} %get-tuple-element.211.rows_ref.refs_0_), channel_id=1, source_target_pairs={{0,1},{1,0},{2,3},{3,2},{4,5},{5,4},{6,7},{7,6},{8,9},{9,8},{10,11... | collective-permute-start | bytes 2359304 | tf_op jit(solution)/shard_map/ppermute | solution.py:474
  133.7 22.0 %collective-permute-start.16 = (bf16[256,1536]{1,0:T(8,128)(2,1)S(1)}, bf16[256,1536]{1,0:T(8,128)(2,1)}, u32[]{:S(2)}, u32[]{:S(2)}) collective-permute-start(bf16[256,1536]{1,0:T(8,128)(2,1)S(1)} %get-tuple-element.211.rows_ref.refs_0_), channel_id=1, source_target_pairs={{1,2},{2,1},{5,6},{6,5},{9,10},{10,9},{13,14},{14,13},{17,18},{18,... | collective-permute-start | bytes 2359304 | tf_op jit(solution)/shard_map/ppermute | solution.py:478
  155.7 20.1 %collective-permute-start.17 = (bf16[256,1536]{1,0:T(8,128)(2,1)}, bf16[256,1536]{1,0:T(8,128)(2,1)}, u32[]{:S(2)}, u32[]{:S(2)}) collective-permute-start(bf16[256,1536]{1,0:T(8,128)(2,1)} %collective-permute-done.15.rows_ref.refs_1_), channel_id=1, source_target_pairs={{1,2},{2,1},{5,6},{6,5},{9,10},{10,9},{13,14},{14,13},{17,18},{18,... | collective-permute-start | bytes 2359304 | tf_op jit(solution)/shard_map/ppermute | solution.py:478
  157.3 22.1 %collective-permute-start.18 = (bf16[256,1536]{1,0:T(8,128)(2,1)}, bf16[256,1536]{1,0:T(8,128)(2,1)}, u32[]{:S(2)}, u32[]{:S(2)}) collective-permute-start(bf16[256,1536]{1,0:T(8,128)(2,1)} %collective-permute-done.16), channel_id=1, source_target_pairs={{1,0},{2,3},{5,4},{6,7},{9,8},{10,11},{13,12},{14,15},{17,16},{18,... | collective-permute-start | bytes 2359304 | tf_op jit(solution)/shard_map/ppermute | solution.py:482
  182.1 38.7 %collective-permute-start.22 = (bf16[768,640]{1,0:T(8,128)(2,1)S(1)}, bf16[768,640]{1,0:T(8,128)(2,1)S(1)}, u32[]{:S(2)}, u32[]{:S(2)}) collective-permute-start(bf16[768,640]{1,0:T(8,128)(2,1)S(1)} %constant_dynamic-slice_fusion.1), channel_id=1, source_target_pairs={{0,8},{4,12},{8,0},{12,4},{16,24},{20,28},{24,16},{28,20},{1,9},{5... | collective-permute-start | bytes 2949128 | tf_op jit(solution)/shard_map/ppermute | solution.py:470
  212.2 22.3 %collective-permute-start.21 = (bf16[256,1536]{1,0:T(8,128)(2,1)S(1)}, bf16[256,1536]{1,0:T(8,128)(2,1)S(1)}, u32[]{:S(2)}, u32[]{:S(2)}) collective-permute-start(bf16[256,1536]{1,0:T(8,128)(2,1)S(1)} %get-tuple-element.227), channel_id=1, source_target_pairs={{0,1},{3,2},{4,5},{7,6},{8,9},{11,10},{12,13},{15,14},{16,17},{19,... | collective-permute-start | bytes 2359304 | tf_op jit(solution)/shard_map/ppermute | solution.py:486
  234.7 21.1 %collective-permute-start.24 = (bf16[256,1536]{1,0:T(8,128)(2,1)S(1)}, bf16[256,1536]{1,0:T(8,128)(2,1)S(1)}, u32[]{:S(2)}, u32[]{:S(2)}) collective-permute-start(bf16[256,1536]{1,0:T(8,128)(2,1)S(1)} %add.250), channel_id=1, source_target_pairs={{0,1},{3,2},{4,5},{7,6},{8,9},{11,10},{12,13},{15,14},{16,17},{19,... | collective-permute-start | bytes 2359304 | tf_op jit(solution)/shard_map/ppermute | solution.py:486
  256.2 20.4 %collective-permute-start.27 = (bf16[256,1536]{1,0:T(8,128)(2,1)S(1)}, bf16[256,1536]{1,0:T(8,128)(2,1)S(1)}, u32[]{:S(2)}, u32[]{:S(2)}) collective-permute-start(bf16[256,1536]{1,0:T(8,128)(2,1)S(1)} %add.252), channel_id=1, source_target_pairs={{0,1},{1,0},{2,3},{3,2},{4,5},{5,4},{6,7},{7,6},{8,9},{9,8},{10,11... | collective-permute-start | bytes 2359304 | tf_op jit(solution)/shard_map/ppermute | solution.py:474
  260.7 55.6 %collective-permute-start.33 = (bf16[2,768,640]{2,1,0:T(8,128)(2,1)S(1)}, bf16[2,768,640]{2,1,0:T(8,128)(2,1)}, u32[]{:S(2)}, u32[]{:S(2)}) collective-permute-start(bf16[2,768,640]{2,1,0:T(8,128)(2,1)S(1)} %pad_maximum_fusion.1), channel_id=1, source_target_pairs={{0,16},{4,20},{8,24},{12,28},{16,0},{20,4},{24,8},{28,12},{1,17},{... | collective-permute-start | bytes 5898248 | tf_op jit(solution)/shard_map/ppermute | solution.py:470
  279.6 20.8 %collective-permute-start.29 = (bf16[256,1536]{1,0:T(8,128)(2,1)S(1)}, bf16[256,1536]{1,0:T(8,128)(2,1)S(1)}, u32[]{:S(2)}, u32[]{:S(2)}) collective-permute-start(bf16[256,1536]{1,0:T(8,128)(2,1)S(1)} %get-tuple-element.375.grad_ref.refs_4_), channel_id=1, source_target_pairs={{0,1},{1,0},{2,3},{3,2},{4,5},{5,4},{6,7},{7,6},{8,9},{9,8},{10,11... | collective-permute-start | bytes 2359304 | tf_op jit(solution)/shard_map/ppermute | solution.py:474
  300.4 20.5 %collective-permute-start.31 = (bf16[256,1536]{1,0:T(8,128)(2,1)S(1)}, bf16[256,1536]{1,0:T(8,128)(2,1)}, u32[]{:S(2)}, u32[]{:S(2)}) collective-permute-start(bf16[256,1536]{1,0:T(8,128)(2,1)S(1)} %collective-permute-done.29.grad_ref.refs_5_), channel_id=1, source_target_pairs={{1,2},{2,1},{5,6},{6,5},{9,10},{10,9},{13,14},{14,13},{17,18},{18,... | collective-permute-start | bytes 2359304 | tf_op jit(solution)/shard_map/ppermute | solution.py:478
  301.9 20.0 %collective-permute-start.32 = (bf16[256,1536]{1,0:T(8,128)(2,1)S(1)}, bf16[256,1536]{1,0:T(8,128)(2,1)S(1)}, u32[]{:S(2)}, u32[]{:S(2)}) collective-permute-start(bf16[256,1536]{1,0:T(8,128)(2,1)S(1)} %collective-permute-done.30), channel_id=1, source_target_pairs={{1,0},{2,3},{5,4},{6,7},{9,8},{10,11},{13,12},{14,15},{17,16},{18,... | collective-permute-start | bytes 2359304 | tf_op jit(solution)/shard_map/ppermute | solution.py:482
  373.5 40.1 %collective-permute-start.36 = (bf16[4,480,1536]{2,1,0:T(8,128)(2,1)}, bf16[4,480,1536]{2,1,0:T(8,128)(2,1)}, u32[]{:S(2)}, u32[]{:S(2)}) collective-permute-start(bf16[4,480,1536]{2,1,0:T(8,128)(2,1)} %expert_grad.4), channel_id=1, source_target_pairs={{0,4},{4,0},{8,12},{12,8},{16,20},{20,16},{24,28},{28,24},{1,5},{5... | collective-permute-start | bytes 17694728 | tf_op jit(solution)/shard_map/ppermute | solution.py:470
  386.2 56.2 %collective-permute-start.39 = (bf16[4,384,1536]{2,1,0:T(8,128)(2,1)}, bf16[4,384,1536]{2,1,0:T(8,128)(2,1)}, u32[]{:S(2)}, u32[]{:S(2)}) collective-permute-start(bf16[4,384,1536]{2,1,0:T(8,128)(2,1)} %expert_grad.5), channel_id=1, source_target_pairs={{0,4},{4,0},{8,12},{12,8},{16,20},{20,16},{24,28},{28,24},{1,5},{5... | collective-permute-start | bytes 14155784 | tf_op jit(solution)/shard_map/ppermute | solution.py:470
  386.7 36.9 %collective-permute-start.35 = (bf16[256,1536]{1,0:T(8,128)(2,1)}, bf16[256,1536]{1,0:T(8,128)(2,1)}, u32[]{:S(2)}, u32[]{:S(2)}) collective-permute-start(bf16[256,1536]{1,0:T(8,128)(2,1)} %get-tuple-element.261), channel_id=1, source_target_pairs={{0,1},{3,2},{4,5},{7,6},{8,9},{11,10},{12,13},{15,14},{16,17},{19,... | collective-permute-start | bytes 2359304 | tf_op jit(solution)/shard_map/ppermute | solution.py:486
  423.0 66.8 %collective-permute-start.42 = (bf16[2,480,1536]{2,1,0:T(8,128)(2,1)}, bf16[2,480,1536]{2,1,0:T(8,128)(2,1)}, u32[]{:S(2)}, u32[]{:S(2)}) collective-permute-start(bf16[2,480,1536]{2,1,0:T(8,128)(2,1)} %get-tuple-element.282), channel_id=1, source_target_pairs={{0,8},{4,12},{8,0},{12,4},{16,24},{20,28},{24,16},{28,20},{1,9},{5... | collective-permute-start | bytes 8847368 | tf_op jit(solution)/shard_map/ppermute | solution.py:470
  425.8 22.7 %collective-permute-start.37 = (bf16[256,1536]{1,0:T(8,128)(2,1)}, bf16[256,1536]{1,0:T(8,128)(2,1)}, u32[]{:S(2)}, u32[]{:S(2)}) collective-permute-start(bf16[256,1536]{1,0:T(8,128)(2,1)} %add.257), channel_id=1, source_target_pairs={{0,1},{3,2},{4,5},{7,6},{8,9},{11,10},{12,13},{15,14},{16,17},{19,... | collective-permute-start | bytes 2359304 | tf_op jit(solution)/shard_map/ppermute | solution.py:486
  427.9 20.6 %collective-permute-start.38 = (bf16[256,1536]{1,0:T(8,128)(2,1)}, bf16[256,1536]{1,0:T(8,128)(2,1)}, u32[]{:S(2)}, u32[]{:S(2)}) collective-permute-start(bf16[256,1536]{1,0:T(8,128)(2,1)} %add.257), channel_id=1, source_target_pairs={{1,2},{2,1},{5,6},{6,5},{9,10},{10,9},{13,14},{14,13},{17,18},{18,... | collective-permute-start | bytes 2359304 | tf_op jit(solution)/shard_map/ppermute | solution.py:478
  453.2 89.6 %collective-permute-start.44 = (bf16[2,384,1536]{2,1,0:T(8,128)(2,1)}, bf16[2,384,1536]{2,1,0:T(8,128)(2,1)}, u32[]{:S(2)}, u32[]{:S(2)}) collective-permute-start(bf16[2,384,1536]{2,1,0:T(8,128)(2,1)} %get-tuple-element.286), channel_id=1, source_target_pairs={{0,16},{4,20},{8,24},{12,28},{16,0},{20,4},{24,8},{28,12},{1,17},{... | collective-permute-start | bytes 7077896 | tf_op jit(solution)/shard_map/ppermute | solution.py:470
  454.7 128.8 %collective-permute-start.47 = (bf16[4,768,640]{2,1,0:T(8,128)(2,1)}, bf16[4,768,640]{2,1,0:T(8,128)(2,1)}, u32[]{:S(2)}, u32[]{:S(2)}) collective-permute-start(bf16[4,768,640]{2,1,0:T(8,128)(2,1)} %pad_maximum_fusion.refs_1_), channel_id=1, source_target_pairs={{0,4},{4,0},{8,12},{12,8},{16,20},{20,16},{24,28},{28,24},{1,5},{5... | collective-permute-start | bytes 11796488 | tf_op jit(solution)/shard_map/ppermute | solution.py:470
  482.6 32.1 %all-to-all-start.2 = ((bf16[4,256,384]{2,1,0:T(8,128)(2,1)}), bf16[4,256,384]{2,1,0:T(8,128)(2,1)S(1)}, u32[]{:S(2)}, u32[]{:S(2)}) async-start(bf16[4,256,384]{2,1,0:T(8,128)(2,1)} %get-tuple-element.297), calls=%async_computation.2 | async-start | bytes 1572864 | tf_op jit(solution)/shard_map/all_to_all | solution.py:516
  536.8 35.4 %collective-permute-start.45 = (bf16[480,1536]{1,0:T(8,128)(2,1)}, bf16[480,1536]{1,0:T(8,128)(2,1)}, u32[]{:S(2)}, u32[]{:S(2)}) collective-permute-start(bf16[480,1536]{1,0:T(8,128)(2,1)} %copy-done.120), channel_id=1, source_target_pairs={{0,16},{4,20},{8,24},{12,28},{16,0},{20,4},{24,8},{28,12},{1,17},{... | collective-permute-start | bytes 4423688 | tf_op jit(solution)/shard_map/ppermute | solution.py:470
  548.2 29.8 %collective-permute-start.46 = (bf16[384,1536]{1,0:T(8,128)(2,1)}, bf16[384,1536]{1,0:T(8,128)(2,1)}, u32[]{:S(2)}, u32[]{:S(2)}) collective-permute-start(bf16[384,1536]{1,0:T(8,128)(2,1)} %get-tuple-element.309), channel_id=1, source_target_pairs={{0,8},{4,12},{8,0},{12,4},{16,24},{20,28},{24,16},{28,20},{1,9},{5... | collective-permute-start | bytes 3538952 | tf_op jit(solution)/shard_map/ppermute | solution.py:470
  555.0 69.3 %collective-permute-start.50 = (bf16[4,192,1536]{2,1,0:T(8,128)(2,1)}, bf16[4,192,1536]{2,1,0:T(8,128)(2,1)}, u32[]{:S(2)}, u32[]{:S(2)}) collective-permute-start(bf16[4,192,1536]{2,1,0:T(8,128)(2,1)} %get-tuple-element.324), channel_id=1, source_target_pairs={{0,4},{4,0},{8,12},{12,8},{16,20},{20,16},{24,28},{28,24},{1,5},{5... | collective-permute-start | bytes 7077896 | tf_op jit(solution)/shard_map/ppermute | solution.py:470
  555.0 36.5 %all-to-all-start.3 = ((bf16[4,256,640]{2,1,0:T(8,128)(2,1)}), bf16[4,256,640]{2,1,0:T(8,128)(2,1)}, u32[]{:S(2)}, u32[]{:S(2)}) async-start(bf16[4,256,640]{2,1,0:T(8,128)(2,1)} %pad_maximum_fusion.2), calls=%async_computation.3 | async-start | bytes 2621440 | tf_op jit(solution)/shard_map/all_to_all | solution.py:516
  576.8 42.3 %collective-permute-start.52 = (bf16[480,1536]{1,0:T(8,128)(2,1)}, bf16[480,1536]{1,0:T(8,128)(2,1)}, u32[]{:S(2)}, u32[]{:S(2)}) collective-permute-start(bf16[480,1536]{1,0:T(8,128)(2,1)} %blend_sum.2.refs_0_), channel_id=1, source_target_pairs={{0,16},{4,20},{8,24},{12,28},{16,0},{20,4},{24,8},{28,12},{1,17},{... | collective-permute-start | bytes 4423688 | tf_op jit(solution)/shard_map/ppermute | solution.py:470
  582.1 34.0 %collective-permute-start.51 = (bf16[384,1536]{1,0:T(8,128)(2,1)}, bf16[384,1536]{1,0:T(8,128)(2,1)}, u32[]{:S(2)}, u32[]{:S(2)}) collective-permute-start(bf16[384,1536]{1,0:T(8,128)(2,1)} %blend_sum.3.refs_0_), channel_id=1, source_target_pairs={{0,8},{4,12},{8,0},{12,4},{16,24},{20,28},{24,16},{28,20},{1,9},{5... | collective-permute-start | bytes 3538952 | tf_op jit(solution)/shard_map/ppermute | solution.py:470
  608.1 22.7 %collective-permute-start.49 = (bf16[4,192,640]{2,1,0:T(8,128)(2,1)}, bf16[4,192,640]{2,1,0:T(8,128)(2,1)}, u32[]{:S(2)}, u32[]{:S(2)}) collective-permute-start(bf16[4,192,640]{2,1,0:T(8,128)(2,1)} %get-tuple-element.323), channel_id=1, source_target_pairs={{0,4},{4,0},{8,12},{12,8},{16,20},{20,16},{24,28},{28,24},{1,5},{5... | collective-permute-start | bytes 2949128 | tf_op jit(solution)/shard_map/ppermute | solution.py:470
  608.2 23.6 %collective-permute-start.48 = (f32[8,1536]{1,0:T(8,128)S(1)}, f32[8,1536]{1,0:T(8,128)S(1)}, u32[]{:S(2)}, u32[]{:S(2)}) collective-permute-start(f32[8,1536]{1,0:T(8,128)S(1)} %maximum_maximum_fusion), channel_id=1, source_target_pairs={{0,1},{1,0},{2,3},{3,2},{4,5},{5,4},{6,7},{7,6},{8,9},{9,8},{10,11... | collective-permute-start | bytes 147464 | tf_op jit(solution)/shard_map/ppermute | solution.py:474
  623.3 83.5 %collective-permute-start.65 = (bf16[2,480,1536]{2,1,0:T(8,128)(2,1)S(1)}, bf16[2,480,1536]{2,1,0:T(8,128)(2,1)S(1)}, u32[]{:S(2)}, u32[]{:S(2)}) collective-permute-start(bf16[2,480,1536]{2,1,0:T(8,128)(2,1)S(1)} %blend_stack.3.refs_0_), channel_id=1, source_target_pairs={{0,8},{4,12},{8,0},{12,4},{16,24},{20,28},{24,16},{28,20},{1,9},{5... | collective-permute-start | bytes 8847368 | tf_op jit(solution)/shard_map/ppermute | solution.py:470
  643.7 25.9 %collective-permute-start.58 = (bf16[192,1536]{1,0:T(8,128)(2,1)S(1)}, bf16[192,1536]{1,0:T(8,128)(2,1)S(1)}, u32[]{:S(2)}, u32[]{:S(2)}) collective-permute-start(bf16[192,1536]{1,0:T(8,128)(2,1)S(1)} %bitcast_add_fusion.1), channel_id=1, source_target_pairs={{0,1},{3,2},{4,5},{7,6},{8,9},{11,10},{12,13},{15,14},{16,17},{19,... | collective-permute-start | bytes 1769480 | tf_op jit(solution)/shard_map/ppermute | solution.py:486
  648.1 21.5 %collective-permute-start.59 = (bf16[192,1536]{1,0:T(8,128)(2,1)S(1)}, bf16[192,1536]{1,0:T(8,128)(2,1)S(1)}, u32[]{:S(2)}, u32[]{:S(2)}) collective-permute-start(bf16[192,1536]{1,0:T(8,128)(2,1)S(1)} %bitcast_add_fusion.1), channel_id=1, source_target_pairs={{1,2},{2,1},{5,6},{6,5},{9,10},{10,9},{13,14},{14,13},{17,18},{18,... | collective-permute-start | bytes 1769480 | tf_op jit(solution)/shard_map/ppermute | solution.py:478
  652.4 50.8 %collective-permute-start.64 = (bf16[2,384,1536]{2,1,0:T(8,128)(2,1)S(1)}, bf16[2,384,1536]{2,1,0:T(8,128)(2,1)S(1)}, u32[]{:S(2)}, u32[]{:S(2)}) collective-permute-start(bf16[2,384,1536]{2,1,0:T(8,128)(2,1)S(1)} %blend_stack.2.refs_0_), channel_id=1, source_target_pairs={{0,16},{4,20},{8,24},{12,28},{16,0},{20,4},{24,8},{28,12},{1,17},{... | collective-permute-start | bytes 7077896 | tf_op jit(solution)/shard_map/ppermute | solution.py:470
  670.9 22.2 %collective-permute-start.62 = (bf16[192,1536]{1,0:T(8,128)(2,1)S(1)}, bf16[192,1536]{1,0:T(8,128)(2,1)S(1)}, u32[]{:S(2)}, u32[]{:S(2)}) collective-permute-start(bf16[192,1536]{1,0:T(8,128)(2,1)S(1)} %bitcast_add_fusion), channel_id=1, source_target_pairs={{0,1},{1,0},{2,3},{3,2},{4,5},{5,4},{6,7},{7,6},{8,9},{9,8},{10,11... | collective-permute-start | bytes 1769480 | tf_op jit(solution)/shard_map/ppermute | solution.py:474
  671.0 22.8 %collective-permute-start.63 = (bf16[192,1536]{1,0:T(8,128)(2,1)S(1)}, bf16[192,1536]{1,0:T(8,128)(2,1)S(1)}, u32[]{:S(2)}, u32[]{:S(2)}) collective-permute-start(bf16[192,1536]{1,0:T(8,128)(2,1)S(1)} %add.281), channel_id=1, source_target_pairs={{1,2},{2,1},{5,6},{6,5},{9,10},{10,9},{13,14},{14,13},{17,18},{18,... | collective-permute-start | bytes 1769480 | tf_op jit(solution)/shard_map/ppermute | solution.py:478
  711.1 24.2 %collective-permute-start.74 = (bf16[4,480,1536]{2,1,0:T(8,128)(2,1)}, bf16[4,480,1536]{2,1,0:T(8,128)(2,1)}, u32[]{:S(2)}, u32[]{:S(2)}) collective-permute-start(bf16[4,480,1536]{2,1,0:T(8,128)(2,1)} %blend_four.3.refs_1_), channel_id=1, source_target_pairs={{0,4},{4,0},{8,12},{12,8},{16,20},{20,16},{24,28},{28,24},{1,5},{5... | collective-permute-start | bytes 17694728 | tf_op jit(solution)/shard_map/ppermute | solution.py:470
  711.1 22.8 %collective-permute-start.73 = (bf16[4,384,1536]{2,1,0:T(8,128)(2,1)}, bf16[4,384,1536]{2,1,0:T(8,128)(2,1)}, u32[]{:S(2)}, u32[]{:S(2)}) collective-permute-start(bf16[4,384,1536]{2,1,0:T(8,128)(2,1)} %blend_four.2.refs_0_), channel_id=1, source_target_pairs={{0,4},{4,0},{8,12},{12,8},{16,20},{20,16},{24,28},{28,24},{1,5},{5... | collective-permute-start | bytes 14155784 | tf_op jit(solution)/shard_map/ppermute | solution.py:470
  715.1 45.2 %collective-permute-start.70 = (bf16[96,1536]{1,0:T(8,128)(2,1)S(1)}, bf16[96,1536]{1,0:T(8,128)(2,1)S(1)}, u32[]{:S(2)}, u32[]{:S(2)}) collective-permute-start(bf16[96,1536]{1,0:T(8,128)(2,1)S(1)} %get-tuple-element.352), channel_id=1, source_target_pairs={{0,1},{1,0},{2,3},{3,2},{4,5},{5,4},{6,7},{7,6},{8,9},{9,8},{10,11... | collective-permute-start | bytes 884744 | tf_op jit(solution)/shard_map/ppermute | solution.py:474
  727.8 32.6 %collective-permute-start.71 = (bf16[96,1536]{1,0:T(8,128)(2,1)S(1)}, bf16[96,1536]{1,0:T(8,128)(2,1)S(1)}, u32[]{:S(2)}, u32[]{:S(2)}) collective-permute-start(bf16[96,1536]{1,0:T(8,128)(2,1)S(1)} %get-tuple-element.353), channel_id=1, source_target_pairs={{0,2},{1,3},{2,0},{3,1},{4,6},{5,7},{6,4},{7,5},{8,10},{9,11},{10,... | collective-permute-start | bytes 884744 | tf_op jit(solution)/shard_map/ppermute | solution.py:474
  732.1 28.3 %collective-permute-start.72 = (bf16[96,1536]{1,0:T(8,128)(2,1)S(1)}, bf16[96,1536]{1,0:T(8,128)(2,1)S(1)}, u32[]{:S(2)}, u32[]{:S(2)}) collective-permute-start(bf16[96,1536]{1,0:T(8,128)(2,1)S(1)} %get-tuple-element.354), channel_id=1, source_target_pairs={{0,3},{1,2},{2,1},{3,0},{4,7},{5,6},{6,5},{7,4},{8,11},{9,10},{10,... | collective-permute-start | bytes 884744 | tf_op jit(solution)/shard_map/ppermute | solution.py:474
  733.9 26.6 %collective-permute-start.69 = (bf16[192,1536]{1,0:T(8,128)(2,1)S(1)}, bf16[192,1536]{1,0:T(8,128)(2,1)S(1)}, u32[]{:S(2)}, u32[]{:S(2)}) collective-permute-start(bf16[192,1536]{1,0:T(8,128)(2,1)S(1)} %add.293), channel_id=1, source_target_pairs={{0,16},{4,20},{8,24},{12,28},{16,0},{20,4},{24,8},{28,12},{1,17},{... | collective-permute-start | bytes 1769480 | tf_op jit(solution)/shard_map/ppermute | solution.py:470
  735.3 26.2 %collective-permute-start.68 = (bf16[2,192,640]{2,1,0:T(8,128)(2,1)S(1)}, bf16[2,192,640]{2,1,0:T(8,128)(2,1)S(1)}, u32[]{:S(2)}, u32[]{:S(2)}) collective-permute-start(bf16[2,192,640]{2,1,0:T(8,128)(2,1)S(1)} %pad_maximum_fusion.10), channel_id=1, source_target_pairs={{0,16},{4,20},{8,24},{12,28},{16,0},{20,4},{24,8},{28,12},{1,17},{... | collective-permute-start | bytes 1474568 | tf_op jit(solution)/shard_map/ppermute | solution.py:470
  (186 other events, 1645.1 us)

commit v7 on v6

--- a/solution.py
+++ b/solution.py
@@ -1497,9 +1497,9 @@
     "M", "K", "R", "M", "K", "M", "M", "M", "M", "R", "M", "M",
 )
 LATE = (
-    "L", "0", "1", "0", "0", "L", "1", "1", "L", "L", "0", "L", "L", "1", "O", "0", "1", "L", "Q", "1", "0", "O", "Q", "L",
-    "O", "Q", "O", "Q", "O", "Q", "1", "0", "O", "Q", "S", "O", "Q", "1", "0", "S", "O", "Q", "L", "L", "L", "Q", "O", "S",
-    "L",
+    "L", "0", "1", "0", "0", "L", "1", "1", "L", "L", "O", "0", "L", "1", "L", "1", "0", "O", "Q", "1", "O", "L", "Q", "0",
+    "O", "L", "Q", "Q", "O", "Q", "L", "1", "0", "O", "Q", "S", "L", "O", "Q", "1", "S", "L", "0", "O", "Q", "L", "Q", "O",
+    "S",
 )
 
 

time: 801 us -> 783 us (0.978)
    ppermute x40, waiting for transfers between devices: 67.9 us -> 94.5 us  [flip(): lax.ppermute(value, 'ctx', [(index, index ^ bit) for index in range(8)])]
    ppermute x8, waiting for transfers between devices: 50.5 us -> 30.6 us  [line_inward(): return lax.ppermute(value, 'wt', [(0, 1), (3, 2)])]
    all_to_all x3, waiting for transfers between devices: 24.5 us -> 13.9 us  [chips_exchange(): lax.all_to_all(blocks, 'ctx', split_axis=0, concat_axis=0, tiled=True, ax...]
    unnamed x303 -> x297, local copies, waits for them, and re-layouts: 59.4 us -> 55 us
  transfers between devices with their start and end apart: 85 -> 85, of which waited for: 34 -> 35; matrix products, arithmetic and copies ran while one was open for 7% -> 8% of each run, Pallas kernels for 34% -> 33%
where the time goes in v7:
time: 783 us; the launch traced here: 776 us
  Pallas kernels  295 us (38%)
  waiting for transfers between devices  218 us (28%)
  starting transfers between devices  131 us (17%)
  local copies, waits for them, and re-layouts  75.1 us (10%)
  other arithmetic  50.2 us (6%)
    pallas_call x33, Pallas kernels, call(): pl.pallas_call(kernel, grid_spec=pltpu.PrefetchScalarGridSpec(num_scalar_...  272 us
    ppermute x40, waiting for transfers between devices, flip(): lax.ppermute(value, 'ctx', [(index, index ^ bit) for index in range(8)])  94.5 us
    ppermute x17, waiting for transfers between devices, line_swap(): lax.ppermute(value, 'wt', [(index, index ^ offset) for index in range(4)])  61 us
    unnamed x297, local copies, waits for them, and re-layouts  55 us
    ppermute x17, starting transfers between devices, line_swap(): lax.ppermute(value, 'wt', [(index, index ^ offset) for index in range(4)])  32.9 us
    ppermute x8, starting transfers between devices, line_inward(): return lax.ppermute(value, 'wt', [(0, 1), (3, 2)])  32.2 us
    ppermute x8, waiting for transfers between devices, line_inward(): return lax.ppermute(value, 'wt', [(0, 1), (3, 2)])  30.6 us
    ppermute x40, starting transfers between devices, flip(): lax.ppermute(value, 'ctx', [(index, index ^ bit) for index in range(8)])  29.3 us
  transfers between devices with their start and end apart: 85, of which 35 were waited for; matrix products, arithmetic and copies ran while one was open for 8% of the time, Pallas kernels for 33%

profile of v7, /device:TPU:0, one launch (start us, length us, event | category | flops | bytes accessed | tf_op | source)
XLA Modules:
  0.0 775.5 jit_solution(5571252253285429472)
XLA Ops:
  9.8 4.8 all-to-all-start.1
  27.0 22.9 %collective-permute-done.5 = bf16[2,192,640]{2,1,0:T(8,128)(2,1)S(1)} collective-permute-done((bf16[2,192,640]{2,1,0:T(8,128)(2,1)S(1)}, bf16[2,192,640]{2,1,0:T(8,128)(2,1)S(1)}, u32[]{:S(2)}, u32[]{:S(2)}) %collective-permute-start.5) | collective-permute-done | bytes 491552 | tf_op jit(solution)/shard_map/ppermute | solution.py:474
  54.1 4.7 all-to-all-start
  61.7 6.9 collective-permute-done.6
  71.7 6.8 project.1
  84.2 11.5 %attend.1 = (bf16[4,256,384]{2,1,0:T(8,128)(2,1)S(1)}, f32[8,1,384]{2,1,0:T(1,128)S(1)}) custom-call(s32[2]{0:T(128)S(1)} %pad_add_fusion.meta.meta_ref, bf16[4,256,384]{2,1,0:T(8,128)(2,1)S(1)} %copy-done.49, bf16[4,256,256]{2,1,0:T(8,128)(2,1)} %get-tuple-element.198.mine_ref, bf16[4,256,256]{2,1,0:T(8,128)(2,1)S(1)} %collective-permute-done.9.other_ref), custom_call_target="tpu_custom_call" | custom-call | flops 300000000 | bytes 1000 | tf_op jit(solution)/shard_map/attend/pallas_call | solution.py:585
  99.1 12.0 %all-to-all-done.refs_4_ = bf16[4,192,1536]{2,1,0:T(8,128)(2,1)} async-done(((bf16[4,192,1536]{2,1,0:T(8,128)(2,1)}), bf16[4,192,1536]{2,1,0:T(8,128)(2,1)}, u32[]{:S(2)}, u32[]{:S(2)}) %all-to-all-start) | async-done | bytes 2359328 | tf_op jit(solution)/shard_map/all_to_all | solution.py:527
  119.7 5.0 collective-permute-done.11.refs_2_
  126.2 6.2 leave.1
  141.6 11.7 %experts.4 = (bf16[4,256,1024]{2,1,0:T(8,128)(2,1)S(1)}, bf16[256,512]{1,0:T(8,128)(2,1)S(1)}, bf16[256,1536]{1,0:T(8,128)(2,1)S(1)}) custom-call(s32[2]{0:T(128)S(1)} %pad_add_fusion.meta.meta_ref, bf16[256,1536]{1,0:T(8,128)(2,1)S(1)} %get-tuple-element.211.rows_ref.refs_0_, f32[4,256,1]{2,1,0:T(8,128)S(1)} %copy-done.42, ...), custom_call_target="tpu_custom_call" | custom-call | flops 300000000 | bytes 1000 | tf_op jit(solution)/shard_map/experts/pallas_call | solution.py:585
  162.4 12.0 %experts.5 = (bf16[4,256,1024]{2,1,0:T(8,128)(2,1)S(1)}, bf16[256,512]{1,0:T(8,128)(2,1)S(1)}, bf16[256,1536]{1,0:T(8,128)(2,1)S(1)}) custom-call(s32[2]{0:T(128)S(1)} %pad_add_fusion.meta.meta_ref, bf16[256,1536]{1,0:T(8,128)(2,1)} %collective-permute-done.15.rows_ref.refs_1_, f32[4,256,1]{2,1,0:T(8,128)S(1)} %copy.40.gates_ref, ...), custom_call_target="tpu_custom_call" | custom-call | flops 300000000 | bytes 1000 | tf_op jit(solution)/shard_map/experts/pallas_call | solution.py:585
  185.5 11.7 %experts.6 = (bf16[4,256,1024]{2,1,0:T(8,128)(2,1)S(1)}, bf16[256,512]{1,0:T(8,128)(2,1)S(1)}, bf16[256,1536]{1,0:T(8,128)(2,1)S(1)}) custom-call(s32[2]{0:T(128)S(1)} %pad_add_fusion.meta.meta_ref, bf16[256,1536]{1,0:T(8,128)(2,1)S(1)} %broadcast_select_fusion.3.rows_ref.refs_2_, f32[4,256,1]{2,1,0:T(8,128)S(1)} %copy-done.40, ...), custom_call_target="tpu_custom_call" | custom-call | flops 300000000 | bytes 1000 | tf_op jit(solution)/shard_map/experts/pallas_call | solution.py:585
  200.4 11.7 %experts.7 = (bf16[4,256,1024]{2,1,0:T(8,128)(2,1)S(1)}, bf16[256,512]{1,0:T(8,128)(2,1)S(1)}, bf16[256,1536]{1,0:T(8,128)(2,1)S(1)}) custom-call(s32[2]{0:T(128)S(1)} %pad_add_fusion.meta.meta_ref, bf16[256,1536]{1,0:T(8,128)(2,1)S(1)} %broadcast_select_fusion.2.rows_ref.refs_3_, f32[4,256,1]{2,1,0:T(8,128)S(1)} %copy-done.38, ...), custom_call_target="tpu_custom_call" | custom-call | flops 300000000 | bytes 1000 | tf_op jit(solution)/shard_map/experts/pallas_call | solution.py:585
  212.2 4.9 collective-permute-start.21
  221.0 13.5 %collective-permute-done.21 = bf16[256,1536]{1,0:T(8,128)(2,1)S(1)} collective-permute-done((bf16[256,1536]{1,0:T(8,128)(2,1)S(1)}, bf16[256,1536]{1,0:T(8,128)(2,1)S(1)}, u32[]{:S(2)}, u32[]{:S(2)}) %collective-permute-start.21) | collective-permute-done | bytes 786464 | tf_op jit(solution)/shard_map/ppermute | solution.py:486
  243.6 12.2 %collective-permute-done.24 = bf16[256,1536]{1,0:T(8,128)(2,1)S(1)} collective-permute-done((bf16[256,1536]{1,0:T(8,128)(2,1)S(1)}, bf16[256,1536]{1,0:T(8,128)(2,1)S(1)}, u32[]{:S(2)}, u32[]{:S(2)}) %collective-permute-start.24) | collective-permute-done | bytes 786464 | tf_op jit(solution)/shard_map/ppermute | solution.py:486
  262.6 13.9 %collective-permute-done.27 = bf16[256,1536]{1,0:T(8,128)(2,1)S(1)} collective-permute-done((bf16[256,1536]{1,0:T(8,128)(2,1)S(1)}, bf16[256,1536]{1,0:T(8,128)(2,1)S(1)}, u32[]{:S(2)}, u32[]{:S(2)}) %collective-permute-start.27) | collective-permute-done | bytes 786464 | tf_op jit(solution)/shard_map/ppermute | solution.py:474
  284.1 13.0 %experts_back.4 = (bf16[4,256,1024]{2,1,0:T(8,128)(2,1)S(1)}, bf16[4,256,512]{2,1,0:T(8,128)(2,1)S(1)}, bf16[1,256,512]{2,1,0:T(8,128)(2,1)S(1)}, bf16[1,256,256]{2,1,0:T(8,128)(2,1)S(1)}, bf16[256,1536]{1,0:T(8,128)(2,1)S(1)}) custom-call(s32[2]{0:T(128)S(1)} %pad_add_fusion.meta.meta_ref, bf16[256,1536]{1,0:T(8,128)(2,1)S(1)} %get-tuple-element.375.grad_ref.refs_4_, ...), custom_call_target="tpu_custom_call" | custom-call | flops 300000000 | bytes 1000 | tf_op jit(solution)/shard_map/experts_back/pallas_call | solution.py:585
  303.2 13.0 %experts_back.5 = (bf16[4,256,1024]{2,1,0:T(8,128)(2,1)S(1)}, bf16[4,256,512]{2,1,0:T(8,128)(2,1)S(1)}, bf16[1,256,512]{2,1,0:T(8,128)(2,1)S(1)}, bf16[1,256,256]{2,1,0:T(8,128)(2,1)S(1)}, bf16[256,1536]{1,0:T(8,128)(2,1)S(1)}) custom-call(s32[2]{0:T(128)S(1)} %pad_add_fusion.meta.meta_ref, bf16[256,1536]{1,0:T(8,128)(2,1)S(1)} %collective-permute-done.29.grad_ref.refs_5_, ...), custom_call_target="tpu_custom_call" | custom-call | flops 300000000 | bytes 1000 | tf_op jit(solution)/shard_map/experts_back/pallas_call | solution.py:585
  326.7 13.0 %experts_back.6 = (bf16[4,256,1024]{2,1,0:T(8,128)(2,1)S(1)}, bf16[4,256,512]{2,1,0:T(8,128)(2,1)S(1)}, bf16[1,256,512]{2,1,0:T(8,128)(2,1)S(1)}, bf16[1,256,256]{2,1,0:T(8,128)(2,1)S(1)}, bf16[256,1536]{1,0:T(8,128)(2,1)S(1)}) custom-call(s32[2]{0:T(128)S(1)} %pad_add_fusion.meta.meta_ref, bf16[256,1536]{1,0:T(8,128)(2,1)S(1)} %broadcast_select_fusion.1.grad_ref.refs_6_, ...), custom_call_target="tpu_custom_call" | custom-call | flops 300000000 | bytes 1000 | tf_op jit(solution)/shard_map/experts_back/pallas_call | solution.py:585
  343.5 14.4 %experts_back.7 = (bf16[4,256,1024]{2,1,0:T(8,128)(2,1)S(1)}, bf16[4,256,512]{2,1,0:T(8,128)(2,1)S(1)}, bf16[1,256,512]{2,1,0:T(8,128)(2,1)S(1)}, bf16[1,256,256]{2,1,0:T(8,128)(2,1)S(1)}, bf16[256,1536]{1,0:T(8,128)(2,1)}) custom-call(s32[2]{0:T(128)S(1)} %pad_add_fusion.meta.meta_ref, bf16[256,1536]{1,0:T(8,128)(2,1)S(1)} %broadcast_select_fusion.grad_ref.refs_7_, ...), custom_call_target="tpu_custom_call" | custom-call | flops 300000000 | bytes 1000 | tf_op jit(solution)/shard_map/experts_back/pallas_call | solution.py:585
  360.5 13.0 %expert_grad.4 = bf16[4,480,1536]{2,1,0:T(8,128)(2,1)} custom-call(s32[3]{0:T(128)S(1)} %add_add_fusion.meta, bf16[256,1536]{1,0:T(8,128)(2,1)S(1)} %copy-done.20, bf16[256,1536]{1,0:T(8,128)(2,1)} %collective-permute-done.15.rows_ref.refs_1_, bf16[256,1536]{1,0:T(8,128)(2,1)S(1)} %broadcast_select_fusion.3.rows_ref.refs_2_, ...), custom_call_target="tpu_custom_call" | custom-call | flops 300000000 | bytes 1000 | tf_op jit(solution)/shard_map/expert_grad/pallas_call | solution.py:585
  376.0 10.2 %expert_grad.5 = bf16[4,384,1536]{2,1,0:T(8,128)(2,1)} custom-call(s32[3]{0:T(128)S(1)} %add_add_fusion.1.meta, bf16[256,1536]{1,0:T(8,128)(2,1)S(1)} %copy-done.21, bf16[256,1536]{1,0:T(8,128)(2,1)} %collective-permute-done.15.rows_ref.refs_1_, bf16[256,1536]{1,0:T(8,128)(2,1)S(1)} %broadcast_select_fusion.3.rows_ref.refs_2_, ...), custom_call_target="tpu_custom_call" | custom-call | flops 300000000 | bytes 1000 | tf_op jit(solution)/shard_map/expert_grad/pallas_call | solution.py:585
  386.6 5.4 collective-permute-start.35
  400.6 12.9 %expert_grad.6.refs_0_ = bf16[4,480,1536]{2,1,0:T(8,128)(2,1)} custom-call(s32[3]{0:T(128)S(1)} %add_add_fusion.2.meta, bf16[256,1536]{1,0:T(8,128)(2,1)S(1)} %copy-done.21, bf16[256,1536]{1,0:T(8,128)(2,1)} %collective-permute-done.15.rows_ref.refs_1_, bf16[256,1536]{1,0:T(8,128)(2,1)S(1)} %broadcast_select_fusion.3.rows_ref.refs_2_, ...), custom_call_target="tpu_custom_call" | custom-call | flops 300000000 | bytes 1000 | tf_op jit(solution)/shard_map/expert_grad/pallas_call | solution.py:585
  413.6 7.8 %blend_split.2 = (bf16[2,480,1536]{2,1,0:T(8,128)(2,1)}, bf16[2,480,1536]{2,1,0:T(8,128)(2,1)S(1)}) custom-call(s32[2]{0:T(128)S(1)} %pad_add_fusion.meta.meta_ref, bf16[4,480,1536]{2,1,0:T(8,128)(2,1)} %expert_grad.6.refs_0_, bf16[4,480,1536]{2,1,0:T(8,128)(2,1)} %collective-permute-done.36.refs_1_), custom_call_target="tpu_custom_call" | custom-call | flops 300000000 | bytes 1000 | tf_op jit(solution)/shard_map/blend_split/pallas_call | solution.py:585
  432.4 10.1 %expert_grad.7.refs_0_ = bf16[4,384,1536]{2,1,0:T(8,128)(2,1)} custom-call(s32[3]{0:T(128)S(1)} %add_add_fusion.3.meta, bf16[256,1536]{1,0:T(8,128)(2,1)S(1)} %copy-done.22, bf16[256,1536]{1,0:T(8,128)(2,1)} %collective-permute-done.15.rows_ref.refs_1_, bf16[256,1536]{1,0:T(8,128)(2,1)S(1)} %broadcast_select_fusion.3.rows_ref.refs_2_, ...), custom_call_target="tpu_custom_call" | custom-call | flops 300000000 | bytes 1000 | tf_op jit(solution)/shard_map/expert_grad/pallas_call | solution.py:585
  442.6 6.1 blend_split.3
  456.5 16.2 %collective-permute-done.40 = bf16[256,1536]{1,0:T(8,128)(2,1)} collective-permute-done((bf16[256,1536]{1,0:T(8,128)(2,1)}, bf16[256,1536]{1,0:T(8,128)(2,1)}, u32[]{:S(2)}, u32[]{:S(2)}) %collective-permute-start.40) | collective-permute-done | bytes 786464 | tf_op jit(solution)/shard_map/ppermute | solution.py:474
  475.5 7.2 enter_back.1
  497.1 5.1 blend_pair.2
  504.0 13.9 %all-to-all-done.2.refs_1_ = bf16[4,256,384]{2,1,0:T(8,128)(2,1)S(1)} async-done(((bf16[4,256,384]{2,1,0:T(8,128)(2,1)}), bf16[4,256,384]{2,1,0:T(8,128)(2,1)S(1)}, u32[]{:S(2)}, u32[]{:S(2)}) %all-to-all-start.2) | async-done | bytes 786464 | tf_op jit(solution)/shard_map/all_to_all | solution.py:516
  522.1 15.4 %attend_back.1 = (bf16[4,256,384]{2,1,0:T(8,128)(2,1)S(1)}, f32[4,256,256]{2,1,0:T(8,128)S(1)}, bf16[4,256,256]{2,1,0:T(8,128)(2,1)S(1)}) custom-call(s32[2]{0:T(128)S(1)} %pad_add_fusion.meta.meta_ref, bf16[4,256,384]{2,1,0:T(8,128)(2,1)S(1)} %copy-done.50, bf16[4,256,256]{2,1,0:T(8,128)(2,1)} %get-tuple-element.198.mine_ref, ...), custom_call_target="tpu_custom_call" | custom-call | flops 300000000 | bytes 1000 | tf_op jit(solution)/shard_map/attend_back/pallas_call | solution.py:585
  545.6 20.6 %collective-permute-done.46.refs_1_ = bf16[384,1536]{1,0:T(8,128)(2,1)S(1)} collective-permute-done((bf16[384,1536]{1,0:T(8,128)(2,1)S(1)}, bf16[384,1536]{1,0:T(8,128)(2,1)S(1)}, u32[]{:S(2)}, u32[]{:S(2)}) %collective-permute-start.46) | collective-permute-done | bytes 1179680 | tf_op jit(solution)/shard_map/ppermute | solution.py:470
  575.4 6.1 collective-permute-start.48
  588.7 6.3 weight_grad.3
  602.0 5.3 collective-permute-start.52
  610.2 8.9 %finish.1 = (f32[1,256,1536]{2,1,0:T(8,128)}, f32[1,1536]{1,0:T(1,128)S(1)}) custom-call(s32[2]{0:T(128)S(1)} %pad_add_fusion.meta.meta_ref, bf16[4,256,640]{2,1,0:T(8,128)(2,1)} %all-to-all-done.3.refs_0_, bf16[4,768,640]{2,1,0:T(8,128)(2,1)} %pad_maximum_fusion.refs_1_, bf16[4,768,640]{2,1,0:T(8,128)(2,1)} %collective-permute-done.50.refs_2_, ...), custom_call_target="tpu_custom_call" | custom-call | flops 300000000 | bytes 1000 | tf_op jit(solution)/shard_map/finish/pallas_call | solution.py:585
  621.2 12.9 %collective-permute-done.55.refs_1_ = bf16[480,1536]{1,0:T(8,128)(2,1)} collective-permute-done((bf16[480,1536]{1,0:T(8,128)(2,1)}, bf16[480,1536]{1,0:T(8,128)(2,1)}, u32[]{:S(2)}, u32[]{:S(2)}) %collective-permute-start.55) | collective-permute-done | bytes 1474592 | tf_op jit(solution)/shard_map/ppermute | solution.py:470
  648.5 4.9 collective-permute-done.58
  654.1 11.7 %collective-permute-start.56 = (f32[8,1536]{1,0:T(8,128)S(1)}, f32[8,1536]{1,0:T(8,128)S(1)}, u32[]{:S(2)}, u32[]{:S(2)}) collective-permute-start(f32[8,1536]{1,0:T(8,128)S(1)} %fusion.12), channel_id=1, source_target_pairs={{0,2},{1,3},{2,0},{3,1},{4,6},{5,7},{6,4},{7,5},{8,10},{9,11},{10,... | collective-permute-start | bytes 147464 | tf_op jit(solution)/shard_map/ppermute | solution.py:474
  677.9 5.5 blend_four.2.refs_0_
  683.4 8.2 %collective-permute-done.66.refs_1_ = bf16[2,480,1536]{2,1,0:T(8,128)(2,1)S(1)} collective-permute-done((bf16[2,480,1536]{2,1,0:T(8,128)(2,1)S(1)}, bf16[2,480,1536]{2,1,0:T(8,128)(2,1)S(1)}, u32[]{:S(2)}, u32[]{:S(2)}) %collective-permute-start.66) | collective-permute-done | bytes 2949152 | tf_op jit(solution)/shard_map/ppermute | solution.py:470
  698.1 6.9 collective-permute-done.64
  705.8 6.7 collective-permute-done.72
  721.1 12.3 %place_pair.2.refs_0_ = f32[4,1536,1536]{2,1,0:T(8,128)} custom-call(s32[2]{0:T(128)S(1)} %pad_add_fusion.meta.meta_ref, bf16[4,384,1536]{2,1,0:T(8,128)(2,1)} %blend_four.2.refs_0_, bf16[4,384,1536]{2,1,0:T(8,128)(2,1)} %collective-permute-done.73.refs_1_), custom_call_target="tpu_custom_call" | custom-call | flops 300000000 | bytes 1000 | tf_op jit(solution)/shard_map/place_pair/pallas_call | solution.py:1363
  737.6 11.6 %place_pair.3 = f32[4,1536,1536]{2,1,0:T(8,128)} custom-call(s32[2]{0:T(128)S(1)} %pad_add_fusion.meta.meta_ref, f32[4,1536,1536]{2,1,0:T(8,128)} %place_pair.2.refs_0_, bf16[4,480,1536]{2,1,0:T(8,128)(2,1)S(1)} %bitcast.107, bf16[4,480,1536]{2,1,0:T(8,128)(2,1)} %collective-permute-done.77.refs_2_), custom_call_target="tpu_custom_call", output_to_operand_aliasing={{}: (1, {})} | custom-call | flops 300000000 | bytes 1000 | tf_op jit(solution)/shard_map/place_pair/pallas_call | solution.py:1363
  766.0 8.2 %place_shared.1 = f32[384,3072]{1,0:T(8,128)} custom-call(s32[2]{0:T(128)S(1)} %pad_add_fusion.meta.meta_ref, bf16[4,96,1536]{2,1,0:T(8,128)(2,1)S(1)} %pad_maximum_fusion.4.mine_low.mine_high, bf16[4,96,1536]{2,1,0:T(8,128)(2,1)S(1)} %pad_maximum_fusion.4.mine_low.mine_high, bf16[4,96,1536]{2,1,0:T(8,128)(2,1)} %collective-permute-done.80.other_low.other_high, ...), custom_call_target="tpu_custom_call" | custom-call | flops 300000000 | bytes 1000 | tf_op jit(solution)/shard_map/place_shared/pallas_call | solution.py:585
  (564 shorter events, 284.0 us)
Async XLA Ops:
  9.8 42.7 %all-to-all-start.1 = ((bf16[4,256,1536]{2,1,0:T(8,128)(2,1)}), bf16[4,256,1536]{2,1,0:T(8,128)(2,1)}, u32[]{:S(2)}, u32[]{:S(2)}) async-start(bf16[4,256,1536]{2,1,0:T(8,128)(2,1)} %broadcast_in_dim.55), calls=%async_computation.1 | async-start | bytes 6291456 | tf_op jit(solution)/shard_map/all_to_all | solution.py:516
  20.5 29.5 %collective-permute-start.5 = (bf16[2,192,640]{2,1,0:T(8,128)(2,1)S(1)}, bf16[2,192,640]{2,1,0:T(8,128)(2,1)S(1)}, u32[]{:S(2)}, u32[]{:S(2)}) collective-permute-start(bf16[2,192,640]{2,1,0:T(8,128)(2,1)S(1)} %pad_maximum_fusion.9), channel_id=1, source_target_pairs={{0,2},{1,3},{2,0},{3,1},{4,6},{5,7},{6,4},{7,5},{8,10},{9,11},{10,... | collective-permute-start | bytes 1474568 | tf_op jit(solution)/shard_map/ppermute | solution.py:474
  23.1 28.0 %collective-permute-start.4 = (f32[2,32,256]{2,1,0:T(8,128)S(1)}, f32[2,32,256]{2,1,0:T(8,128)S(1)}, u32[]{:S(2)}, u32[]{:S(2)}) collective-permute-start(f32[2,32,256]{2,1,0:T(8,128)S(1)} %pad_maximum_fusion.16), channel_id=1, source_target_pairs={{0,2},{1,3},{2,0},{3,1},{4,6},{5,7},{6,4},{7,5},{8,10},{9,11},{10,... | collective-permute-start | bytes 196616 | tf_op jit(solution)/shard_map/ppermute | solution.py:474
  24.7 27.7 %collective-permute-start.3 = (bf16[2,48,768]{2,1,0:T(8,128)(2,1)S(1)}, bf16[2,48,768]{2,1,0:T(8,128)(2,1)S(1)}, u32[]{:S(2)}, u32[]{:S(2)}) collective-permute-start(bf16[2,48,768]{2,1,0:T(8,128)(2,1)S(1)} %pad_maximum_fusion.14), channel_id=1, source_target_pairs={{0,2},{1,3},{2,0},{3,1},{4,6},{5,7},{6,4},{7,5},{8,10},{9,11},{10,... | collective-permute-start | bytes 442376 | tf_op jit(solution)/shard_map/ppermute | solution.py:474
  54.1 57.0 %all-to-all-start = ((bf16[4,192,1536]{2,1,0:T(8,128)(2,1)}), bf16[4,192,1536]{2,1,0:T(8,128)(2,1)}, u32[]{:S(2)}, u32[]{:S(2)}) async-start(bf16[4,192,1536]{2,1,0:T(8,128)(2,1)} %broadcast_in_dim.54), calls=%async_computation | async-start | bytes 4718592 | tf_op jit(solution)/shard_map/all_to_all | solution.py:527
  111.1 26.1 %collective-permute-start.14 = (bf16[4,4,48,768]{3,2,1,0:T(8,128)(2,1)}, bf16[4,4,48,768]{3,2,1,0:T(8,128)(2,1)}, u32[]{:S(2)}, u32[]{:S(2)}) collective-permute-start(bf16[4,4,48,768]{3,2,1,0:T(8,128)(2,1)} %pad_maximum_fusion.3.mine), channel_id=1, source_target_pairs={{0,4},{4,0},{8,12},{12,8},{16,20},{20,16},{24,28},{28,24},{1,5},{5... | collective-permute-start | bytes 3538952 | tf_op jit(solution)/shard_map/ppermute | solution.py:470
  133.6 22.0 %collective-permute-start.15 = (bf16[256,1536]{1,0:T(8,128)(2,1)S(1)}, bf16[256,1536]{1,0:T(8,128)(2,1)}, u32[]{:S(2)}, u32[]{:S(2)}) collective-permute-start(bf16[256,1536]{1,0:T(8,128)(2,1)S(1)} %get-tuple-element.211.rows_ref.refs_0_), channel_id=1, source_target_pairs={{0,1},{1,0},{2,3},{3,2},{4,5},{5,4},{6,7},{7,6},{8,9},{9,8},{10,11... | collective-permute-start | bytes 2359304 | tf_op jit(solution)/shard_map/ppermute | solution.py:474
  133.6 22.0 %collective-permute-start.16 = (bf16[256,1536]{1,0:T(8,128)(2,1)S(1)}, bf16[256,1536]{1,0:T(8,128)(2,1)}, u32[]{:S(2)}, u32[]{:S(2)}) collective-permute-start(bf16[256,1536]{1,0:T(8,128)(2,1)S(1)} %get-tuple-element.211.rows_ref.refs_0_), channel_id=1, source_target_pairs={{1,2},{2,1},{5,6},{6,5},{9,10},{10,9},{13,14},{14,13},{17,18},{18,... | collective-permute-start | bytes 2359304 | tf_op jit(solution)/shard_map/ppermute | solution.py:478
  155.6 20.1 %collective-permute-start.17 = (bf16[256,1536]{1,0:T(8,128)(2,1)}, bf16[256,1536]{1,0:T(8,128)(2,1)}, u32[]{:S(2)}, u32[]{:S(2)}) collective-permute-start(bf16[256,1536]{1,0:T(8,128)(2,1)} %collective-permute-done.15.rows_ref.refs_1_), channel_id=1, source_target_pairs={{1,2},{2,1},{5,6},{6,5},{9,10},{10,9},{13,14},{14,13},{17,18},{18,... | collective-permute-start | bytes 2359304 | tf_op jit(solution)/shard_map/ppermute | solution.py:478
  157.2 22.1 %collective-permute-start.18 = (bf16[256,1536]{1,0:T(8,128)(2,1)}, bf16[256,1536]{1,0:T(8,128)(2,1)}, u32[]{:S(2)}, u32[]{:S(2)}) collective-permute-start(bf16[256,1536]{1,0:T(8,128)(2,1)} %collective-permute-done.16), channel_id=1, source_target_pairs={{1,0},{2,3},{5,4},{6,7},{9,8},{10,11},{13,12},{14,15},{17,16},{18,... | collective-permute-start | bytes 2359304 | tf_op jit(solution)/shard_map/ppermute | solution.py:482
  179.3 20.1 %collective-permute-start.19 = (bf16[256,1536]{1,0:T(8,128)(2,1)}, bf16[256,1536]{1,0:T(8,128)(2,1)S(1)}, u32[]{:S(2)}, u32[]{:S(2)}) collective-permute-start(bf16[256,1536]{1,0:T(8,128)(2,1)} %collective-permute-done.17), channel_id=1, source_target_pairs={{1,0},{2,3},{5,4},{6,7},{9,8},{10,11},{13,12},{14,15},{17,16},{18,... | collective-permute-start | bytes 2359304 | tf_op jit(solution)/shard_map/ppermute | solution.py:482
  182.0 38.8 %collective-permute-start.22 = (bf16[768,640]{1,0:T(8,128)(2,1)S(1)}, bf16[768,640]{1,0:T(8,128)(2,1)S(1)}, u32[]{:S(2)}, u32[]{:S(2)}) collective-permute-start(bf16[768,640]{1,0:T(8,128)(2,1)S(1)} %constant_dynamic-slice_fusion.1), channel_id=1, source_target_pairs={{0,8},{4,12},{8,0},{12,4},{16,24},{20,28},{24,16},{28,20},{1,9},{5... | collective-permute-start | bytes 2949128 | tf_op jit(solution)/shard_map/ppermute | solution.py:470
  212.2 22.3 %collective-permute-start.21 = (bf16[256,1536]{1,0:T(8,128)(2,1)S(1)}, bf16[256,1536]{1,0:T(8,128)(2,1)S(1)}, u32[]{:S(2)}, u32[]{:S(2)}) collective-permute-start(bf16[256,1536]{1,0:T(8,128)(2,1)S(1)} %get-tuple-element.227), channel_id=1, source_target_pairs={{0,1},{3,2},{4,5},{7,6},{8,9},{11,10},{12,13},{15,14},{16,17},{19,... | collective-permute-start | bytes 2359304 | tf_op jit(solution)/shard_map/ppermute | solution.py:486
  234.7 21.1 %collective-permute-start.24 = (bf16[256,1536]{1,0:T(8,128)(2,1)S(1)}, bf16[256,1536]{1,0:T(8,128)(2,1)S(1)}, u32[]{:S(2)}, u32[]{:S(2)}) collective-permute-start(bf16[256,1536]{1,0:T(8,128)(2,1)S(1)} %add.250), channel_id=1, source_target_pairs={{0,1},{3,2},{4,5},{7,6},{8,9},{11,10},{12,13},{15,14},{16,17},{19,... | collective-permute-start | bytes 2359304 | tf_op jit(solution)/shard_map/ppermute | solution.py:486
  256.2 20.4 %collective-permute-start.27 = (bf16[256,1536]{1,0:T(8,128)(2,1)S(1)}, bf16[256,1536]{1,0:T(8,128)(2,1)S(1)}, u32[]{:S(2)}, u32[]{:S(2)}) collective-permute-start(bf16[256,1536]{1,0:T(8,128)(2,1)S(1)} %add.252), channel_id=1, source_target_pairs={{0,1},{1,0},{2,3},{3,2},{4,5},{5,4},{6,7},{7,6},{8,9},{9,8},{10,11... | collective-permute-start | bytes 2359304 | tf_op jit(solution)/shard_map/ppermute | solution.py:474
  260.7 55.6 %collective-permute-start.33 = (bf16[2,768,640]{2,1,0:T(8,128)(2,1)S(1)}, bf16[2,768,640]{2,1,0:T(8,128)(2,1)}, u32[]{:S(2)}, u32[]{:S(2)}) collective-permute-start(bf16[2,768,640]{2,1,0:T(8,128)(2,1)S(1)} %pad_maximum_fusion.1), channel_id=1, source_target_pairs={{0,16},{4,20},{8,24},{12,28},{16,0},{20,4},{24,8},{28,12},{1,17},{... | collective-permute-start | bytes 5898248 | tf_op jit(solution)/shard_map/ppermute | solution.py:470
  279.6 20.8 %collective-permute-start.29 = (bf16[256,1536]{1,0:T(8,128)(2,1)S(1)}, bf16[256,1536]{1,0:T(8,128)(2,1)S(1)}, u32[]{:S(2)}, u32[]{:S(2)}) collective-permute-start(bf16[256,1536]{1,0:T(8,128)(2,1)S(1)} %get-tuple-element.375.grad_ref.refs_4_), channel_id=1, source_target_pairs={{0,1},{1,0},{2,3},{3,2},{4,5},{5,4},{6,7},{7,6},{8,9},{9,8},{10,11... | collective-permute-start | bytes 2359304 | tf_op jit(solution)/shard_map/ppermute | solution.py:474
  300.4 20.5 %collective-permute-start.31 = (bf16[256,1536]{1,0:T(8,128)(2,1)S(1)}, bf16[256,1536]{1,0:T(8,128)(2,1)}, u32[]{:S(2)}, u32[]{:S(2)}) collective-permute-start(bf16[256,1536]{1,0:T(8,128)(2,1)S(1)} %collective-permute-done.29.grad_ref.refs_5_), channel_id=1, source_target_pairs={{1,2},{2,1},{5,6},{6,5},{9,10},{10,9},{13,14},{14,13},{17,18},{18,... | collective-permute-start | bytes 2359304 | tf_op jit(solution)/shard_map/ppermute | solution.py:478
  301.9 20.0 %collective-permute-start.32 = (bf16[256,1536]{1,0:T(8,128)(2,1)S(1)}, bf16[256,1536]{1,0:T(8,128)(2,1)S(1)}, u32[]{:S(2)}, u32[]{:S(2)}) collective-permute-start(bf16[256,1536]{1,0:T(8,128)(2,1)S(1)} %collective-permute-done.30), channel_id=1, source_target_pairs={{1,0},{2,3},{5,4},{6,7},{9,8},{10,11},{13,12},{14,15},{17,16},{18,... | collective-permute-start | bytes 2359304 | tf_op jit(solution)/shard_map/ppermute | solution.py:482
  373.5 40.1 %collective-permute-start.36 = (bf16[4,480,1536]{2,1,0:T(8,128)(2,1)}, bf16[4,480,1536]{2,1,0:T(8,128)(2,1)}, u32[]{:S(2)}, u32[]{:S(2)}) collective-permute-start(bf16[4,480,1536]{2,1,0:T(8,128)(2,1)} %expert_grad.4), channel_id=1, source_target_pairs={{0,4},{4,0},{8,12},{12,8},{16,20},{20,16},{24,28},{28,24},{1,5},{5... | collective-permute-start | bytes 17694728 | tf_op jit(solution)/shard_map/ppermute | solution.py:470
  386.1 56.4 %collective-permute-start.39 = (bf16[4,384,1536]{2,1,0:T(8,128)(2,1)}, bf16[4,384,1536]{2,1,0:T(8,128)(2,1)}, u32[]{:S(2)}, u32[]{:S(2)}) collective-permute-start(bf16[4,384,1536]{2,1,0:T(8,128)(2,1)} %expert_grad.5), channel_id=1, source_target_pairs={{0,4},{4,0},{8,12},{12,8},{16,20},{20,16},{24,28},{28,24},{1,5},{5... | collective-permute-start | bytes 14155784 | tf_op jit(solution)/shard_map/ppermute | solution.py:470
  386.6 36.3 %collective-permute-start.35 = (bf16[256,1536]{1,0:T(8,128)(2,1)}, bf16[256,1536]{1,0:T(8,128)(2,1)}, u32[]{:S(2)}, u32[]{:S(2)}) collective-permute-start(bf16[256,1536]{1,0:T(8,128)(2,1)} %get-tuple-element.261), channel_id=1, source_target_pairs={{0,1},{3,2},{4,5},{7,6},{8,9},{11,10},{12,13},{15,14},{16,17},{19,... | collective-permute-start | bytes 2359304 | tf_op jit(solution)/shard_map/ppermute | solution.py:486
  425.3 23.4 %collective-permute-start.37 = (bf16[256,1536]{1,0:T(8,128)(2,1)}, bf16[256,1536]{1,0:T(8,128)(2,1)}, u32[]{:S(2)}, u32[]{:S(2)}) collective-permute-start(bf16[256,1536]{1,0:T(8,128)(2,1)} %add.257), channel_id=1, source_target_pairs={{0,1},{3,2},{4,5},{7,6},{8,9},{11,10},{12,13},{15,14},{16,17},{19,... | collective-permute-start | bytes 2359304 | tf_op jit(solution)/shard_map/ppermute | solution.py:486
  427.4 21.2 %collective-permute-start.38 = (bf16[256,1536]{1,0:T(8,128)(2,1)}, bf16[256,1536]{1,0:T(8,128)(2,1)}, u32[]{:S(2)}, u32[]{:S(2)}) collective-permute-start(bf16[256,1536]{1,0:T(8,128)(2,1)} %add.257), channel_id=1, source_target_pairs={{1,2},{2,1},{5,6},{6,5},{9,10},{10,9},{13,14},{14,13},{17,18},{18,... | collective-permute-start | bytes 2359304 | tf_op jit(solution)/shard_map/ppermute | solution.py:478
  429.4 65.9 %collective-permute-start.43 = (bf16[2,480,1536]{2,1,0:T(8,128)(2,1)}, bf16[2,480,1536]{2,1,0:T(8,128)(2,1)}, u32[]{:S(2)}, u32[]{:S(2)}) collective-permute-start(bf16[2,480,1536]{2,1,0:T(8,128)(2,1)} %get-tuple-element.282), channel_id=1, source_target_pairs={{0,8},{4,12},{8,0},{12,4},{16,24},{20,28},{24,16},{28,20},{1,9},{5... | collective-permute-start | bytes 8847368 | tf_op jit(solution)/shard_map/ppermute | solution.py:470
  455.0 82.5 %collective-permute-start.45 = (bf16[2,384,1536]{2,1,0:T(8,128)(2,1)}, bf16[2,384,1536]{2,1,0:T(8,128)(2,1)}, u32[]{:S(2)}, u32[]{:S(2)}) collective-permute-start(bf16[2,384,1536]{2,1,0:T(8,128)(2,1)} %get-tuple-element.286), channel_id=1, source_target_pairs={{0,16},{4,20},{8,24},{12,28},{16,0},{20,4},{24,8},{28,12},{1,17},{... | collective-permute-start | bytes 7077896 | tf_op jit(solution)/shard_map/ppermute | solution.py:470
  489.5 83.8 %collective-permute-start.42 = (bf16[4,192,1536]{2,1,0:T(8,128)(2,1)}, bf16[4,192,1536]{2,1,0:T(8,128)(2,1)}, u32[]{:S(2)}, u32[]{:S(2)}) collective-permute-start(bf16[4,192,1536]{2,1,0:T(8,128)(2,1)} %get-tuple-element.300), channel_id=1, source_target_pairs={{0,4},{4,0},{8,12},{12,8},{16,20},{20,16},{24,28},{28,24},{1,5},{5... | collective-permute-start | bytes 7077896 | tf_op jit(solution)/shard_map/ppermute | solution.py:470
  489.5 119.3 %collective-permute-start.50 = (bf16[4,768,640]{2,1,0:T(8,128)(2,1)}, bf16[4,768,640]{2,1,0:T(8,128)(2,1)}, u32[]{:S(2)}, u32[]{:S(2)}) collective-permute-start(bf16[4,768,640]{2,1,0:T(8,128)(2,1)} %pad_maximum_fusion.refs_1_), channel_id=1, source_target_pairs={{0,4},{4,0},{8,12},{12,8},{16,20},{20,16},{24,28},{28,24},{1,5},{5... | collective-permute-start | bytes 11796488 | tf_op jit(solution)/shard_map/ppermute | solution.py:470
  490.0 27.9 %all-to-all-start.2 = ((bf16[4,256,384]{2,1,0:T(8,128)(2,1)}), bf16[4,256,384]{2,1,0:T(8,128)(2,1)S(1)}, u32[]{:S(2)}, u32[]{:S(2)}) async-start(bf16[4,256,384]{2,1,0:T(8,128)(2,1)} %get-tuple-element.297), calls=%async_computation.2 | async-start | bytes 1572864 | tf_op jit(solution)/shard_map/all_to_all | solution.py:516
  503.4 65.1 %collective-permute-start.47 = (bf16[480,1536]{1,0:T(8,128)(2,1)}, bf16[480,1536]{1,0:T(8,128)(2,1)}, u32[]{:S(2)}, u32[]{:S(2)}) collective-permute-start(bf16[480,1536]{1,0:T(8,128)(2,1)} %get-tuple-element.303), channel_id=1, source_target_pairs={{0,16},{4,20},{8,24},{12,28},{16,0},{20,4},{24,8},{28,12},{1,17},{... | collective-permute-start | bytes 4423688 | tf_op jit(solution)/shard_map/ppermute | solution.py:470
  540.9 25.4 %collective-permute-start.46 = (bf16[384,1536]{1,0:T(8,128)(2,1)S(1)}, bf16[384,1536]{1,0:T(8,128)(2,1)S(1)}, u32[]{:S(2)}, u32[]{:S(2)}) collective-permute-start(bf16[384,1536]{1,0:T(8,128)(2,1)S(1)} %get-tuple-element.310), channel_id=1, source_target_pairs={{0,8},{4,12},{8,0},{12,4},{16,24},{20,28},{24,16},{28,20},{1,9},{5... | collective-permute-start | bytes 3538952 | tf_op jit(solution)/shard_map/ppermute | solution.py:470
  567.0 29.1 %collective-permute-start.49 = (bf16[384,1536]{1,0:T(8,128)(2,1)S(1)}, bf16[384,1536]{1,0:T(8,128)(2,1)}, u32[]{:S(2)}, u32[]{:S(2)}) collective-permute-start(bf16[384,1536]{1,0:T(8,128)(2,1)S(1)} %blend_sum.2.refs_0_), channel_id=1, source_target_pairs={{0,8},{4,12},{8,0},{12,4},{16,24},{20,28},{24,16},{28,20},{1,9},{5... | collective-permute-start | bytes 3538952 | tf_op jit(solution)/shard_map/ppermute | solution.py:470
  575.4 24.8 %collective-permute-start.48 = (bf16[192,1536]{1,0:T(8,128)(2,1)}, bf16[192,1536]{1,0:T(8,128)(2,1)}, u32[]{:S(2)}, u32[]{:S(2)}) collective-permute-start(bf16[192,1536]{1,0:T(8,128)(2,1)} %add_bitcast_fusion), channel_id=1, source_target_pairs={{0,1},{3,2},{4,5},{7,6},{8,9},{11,10},{12,13},{15,14},{16,17},{19,... | collective-permute-start | bytes 1769480 | tf_op jit(solution)/shard_map/ppermute | solution.py:486
  581.6 28.6 %all-to-all-start.3 = ((bf16[4,256,640]{2,1,0:T(8,128)(2,1)}), bf16[4,256,640]{2,1,0:T(8,128)(2,1)}, u32[]{:S(2)}, u32[]{:S(2)}) async-start(bf16[4,256,640]{2,1,0:T(8,128)(2,1)} %pad_maximum_fusion.2), calls=%async_computation.3 | async-start | bytes 2621440 | tf_op jit(solution)/shard_map/all_to_all | solution.py:516
  585.9 48.2 %collective-permute-start.55 = (bf16[480,1536]{1,0:T(8,128)(2,1)}, bf16[480,1536]{1,0:T(8,128)(2,1)}, u32[]{:S(2)}, u32[]{:S(2)}) collective-permute-start(bf16[480,1536]{1,0:T(8,128)(2,1)} %copy-done.36), channel_id=1, source_target_pairs={{0,16},{4,20},{8,24},{12,28},{16,0},{20,4},{24,8},{28,12},{1,17},{... | collective-permute-start | bytes 4423688 | tf_op jit(solution)/shard_map/ppermute | solution.py:470
  596.0 23.2 %collective-permute-start.54 = (bf16[4,192,640]{2,1,0:T(8,128)(2,1)}, bf16[4,192,640]{2,1,0:T(8,128)(2,1)}, u32[]{:S(2)}, u32[]{:S(2)}) collective-permute-start(bf16[4,192,640]{2,1,0:T(8,128)(2,1)} %get-tuple-element.327), channel_id=1, source_target_pairs={{0,4},{4,0},{8,12},{12,8},{16,20},{20,16},{24,28},{28,24},{1,5},{5... | collective-permute-start | bytes 2949128 | tf_op jit(solution)/shard_map/ppermute | solution.py:470
  602.0 37.6 %collective-permute-start.52 = (bf16[192,1536]{1,0:T(8,128)(2,1)S(1)}, bf16[192,1536]{1,0:T(8,128)(2,1)S(1)}, u32[]{:S(2)}, u32[]{:S(2)}) collective-permute-start(bf16[192,1536]{1,0:T(8,128)(2,1)S(1)} %bitcast_add_fusion.1), channel_id=1, source_target_pairs={{0,1},{3,2},{4,5},{7,6},{8,9},{11,10},{12,13},{15,14},{16,17},{19,... | collective-permute-start | bytes 1769480 | tf_op jit(solution)/shard_map/ppermute | solution.py:486
  607.3 34.7 %collective-permute-start.53 = (bf16[192,1536]{1,0:T(8,128)(2,1)S(1)}, bf16[192,1536]{1,0:T(8,128)(2,1)}, u32[]{:S(2)}, u32[]{:S(2)}) collective-permute-start(bf16[192,1536]{1,0:T(8,128)(2,1)S(1)} %bitcast_add_fusion.1), channel_id=1, source_target_pairs={{1,2},{2,1},{5,6},{6,5},{9,10},{10,9},{13,14},{14,13},{17,18},{18,... | collective-permute-start | bytes 1769480 | tf_op jit(solution)/shard_map/ppermute | solution.py:478
  608.8 69.1 %collective-permute-start.65 = (bf16[2,384,1536]{2,1,0:T(8,128)(2,1)}, bf16[2,384,1536]{2,1,0:T(8,128)(2,1)}, u32[]{:S(2)}, u32[]{:S(2)}) collective-permute-start(bf16[2,384,1536]{2,1,0:T(8,128)(2,1)} %blend_stack.2.refs_0_), channel_id=1, source_target_pairs={{0,16},{4,20},{8,24},{12,28},{16,0},{20,4},{24,8},{28,12},{1,17},{... | collective-permute-start | bytes 7077896 | tf_op jit(solution)/shard_map/ppermute | solution.py:470
  619.2 25.3 %collective-permute-start.51 = (f32[8,1536]{1,0:T(8,128)S(1)}, f32[8,1536]{1,0:T(8,128)S(1)}, u32[]{:S(2)}, u32[]{:S(2)}) collective-permute-start(f32[8,1536]{1,0:T(8,128)S(1)} %maximum_maximum_fusion), channel_id=1, source_target_pairs={{0,1},{1,0},{2,3},{3,2},{4,5},{5,4},{6,7},{7,6},{8,9},{9,8},{10,11... | collective-permute-start | bytes 147464 | tf_op jit(solution)/shard_map/ppermute | solution.py:474
  639.6 52.0 %collective-permute-start.66 = (bf16[2,480,1536]{2,1,0:T(8,128)(2,1)S(1)}, bf16[2,480,1536]{2,1,0:T(8,128)(2,1)S(1)}, u32[]{:S(2)}, u32[]{:S(2)}) collective-permute-start(bf16[2,480,1536]{2,1,0:T(8,128)(2,1)S(1)} %blend_stack.3.refs_0_), channel_id=1, source_target_pairs={{0,8},{4,12},{8,0},{12,4},{16,24},{20,28},{24,16},{28,20},{1,9},{5... | collective-permute-start | bytes 8847368 | tf_op jit(solution)/shard_map/ppermute | solution.py:470
  654.1 20.2 %collective-permute-start.56 = (f32[8,1536]{1,0:T(8,128)S(1)}, f32[8,1536]{1,0:T(8,128)S(1)}, u32[]{:S(2)}, u32[]{:S(2)}) collective-permute-start(f32[8,1536]{1,0:T(8,128)S(1)} %fusion.12), channel_id=1, source_target_pairs={{0,2},{1,3},{2,0},{3,1},{4,6},{5,7},{6,4},{7,5},{8,10},{9,11},{10,... | collective-permute-start | bytes 147464 | tf_op jit(solution)/shard_map/ppermute | solution.py:474
  695.8 41.8 %collective-permute-start.77 = (bf16[4,480,1536]{2,1,0:T(8,128)(2,1)}, bf16[4,480,1536]{2,1,0:T(8,128)(2,1)}, u32[]{:S(2)}, u32[]{:S(2)}) collective-permute-start(bf16[4,480,1536]{2,1,0:T(8,128)(2,1)} %blend_four.3.refs_1_), channel_id=1, source_target_pairs={{0,4},{4,0},{8,12},{12,8},{16,20},{20,16},{24,28},{28,24},{1,5},{5... | collective-permute-start | bytes 17694728 | tf_op jit(solution)/shard_map/ppermute | solution.py:470
  695.8 23.5 %collective-permute-start.73 = (bf16[4,384,1536]{2,1,0:T(8,128)(2,1)}, bf16[4,384,1536]{2,1,0:T(8,128)(2,1)}, u32[]{:S(2)}, u32[]{:S(2)}) collective-permute-start(bf16[4,384,1536]{2,1,0:T(8,128)(2,1)} %blend_four.2.refs_0_), channel_id=1, source_target_pairs={{0,4},{4,0},{8,12},{12,8},{16,20},{20,16},{24,28},{28,24},{1,5},{5... | collective-permute-start | bytes 14155784 | tf_op jit(solution)/shard_map/ppermute | solution.py:470
  698.1 20.8 %collective-permute-start.68 = (bf16[96,1536]{1,0:T(8,128)(2,1)S(1)}, bf16[96,1536]{1,0:T(8,128)(2,1)S(1)}, u32[]{:S(2)}, u32[]{:S(2)}) collective-permute-start(bf16[96,1536]{1,0:T(8,128)(2,1)S(1)} %get-tuple-element.352), channel_id=1, source_target_pairs={{0,1},{1,0},{2,3},{3,2},{4,5},{5,4},{6,7},{7,6},{8,9},{9,8},{10,11... | collective-permute-start | bytes 884744 | tf_op jit(solution)/shard_map/ppermute | solution.py:474
  713.3 20.2 %collective-permute-start.69 = (bf16[96,1536]{1,0:T(8,128)(2,1)S(1)}, bf16[96,1536]{1,0:T(8,128)(2,1)S(1)}, u32[]{:S(2)}, u32[]{:S(2)}) collective-permute-start(bf16[96,1536]{1,0:T(8,128)(2,1)S(1)} %get-tuple-element.353), channel_id=1, source_target_pairs={{0,2},{1,3},{2,0},{3,1},{4,6},{5,7},{6,4},{7,5},{8,10},{9,11},{10,... | collective-permute-start | bytes 884744 | tf_op jit(solution)/shard_map/ppermute | solution.py:474
  718.9 30.4 %collective-permute-start.76 = (bf16[192,1536]{1,0:T(8,128)(2,1)S(1)}, bf16[192,1536]{1,0:T(8,128)(2,1)S(1)}, u32[]{:S(2)}, u32[]{:S(2)}) collective-permute-start(bf16[192,1536]{1,0:T(8,128)(2,1)S(1)} %add.295), channel_id=1, source_target_pairs={{0,16},{4,20},{8,24},{12,28},{16,0},{20,4},{24,8},{28,12},{1,17},{... | collective-permute-start | bytes 1769480 | tf_op jit(solution)/shard_map/ppermute | solution.py:470
  719.3 30.9 %collective-permute-start.75 = (bf16[2,192,640]{2,1,0:T(8,128)(2,1)S(1)}, bf16[2,192,640]{2,1,0:T(8,128)(2,1)S(1)}, u32[]{:S(2)}, u32[]{:S(2)}) collective-permute-start(bf16[2,192,640]{2,1,0:T(8,128)(2,1)S(1)} %pad_maximum_fusion.10), channel_id=1, source_target_pairs={{0,16},{4,20},{8,24},{12,28},{16,0},{20,4},{24,8},{28,12},{1,17},{... | collective-permute-start | bytes 1474568 | tf_op jit(solution)/shard_map/ppermute | solution.py:470
  (183 other events, 1724.0 us)

commit v8 on v7

--- a/solution.py
+++ b/solution.py
@@ -1497,7 +1497,7 @@
     "M", "K", "R", "M", "K", "M", "M", "M", "M", "R", "M", "M",
 )
 LATE = (
-    "L", "0", "1", "0", "0", "L", "1", "1", "L", "L", "O", "0", "L", "1", "L", "1", "0", "O", "Q", "1", "O", "L", "Q", "0",
+    "L", "0", "1", "0", "0", "L", "1", "1", "L", "L", "O", "0", "1", "L", "L", "1", "0", "O", "Q", "1", "O", "0", "L", "Q",
     "O", "L", "Q", "Q", "O", "Q", "L", "1", "0", "O", "Q", "S", "L", "O", "Q", "1", "S", "L", "0", "O", "Q", "L", "Q", "O",
     "S",
 )

time: 783 us -> 764 us (0.976)
  waiting for transfers between devices: 218 us -> 174 us
  starting transfers between devices: 131 us -> 146 us
  Pallas kernels: 295 us -> 305 us
    ppermute x40, waiting for transfers between devices: 94.5 us -> 61.6 us  [flip(): lax.ppermute(value, 'ctx', [(index, index ^ bit) for index in range(8)])]
    all_to_all x3, waiting for transfers between devices: 13.9 us -> 0.01 us  [chips_exchange(): lax.all_to_all(blocks, 'ctx', split_axis=0, concat_axis=0, tiled=True, ax...]
    ppermute x17, starting transfers between devices: 32.9 us -> 43.8 us  [line_swap(): lax.ppermute(value, 'wt', [(index, index ^ offset) for index in range(4)])]
    pallas_call x33, Pallas kernels: 272 us -> 281 us  [call(): pl.pallas_call(kernel, grid_spec=pltpu.PrefetchScalarGridSpec(num_scalar_...]
    unnamed x297 -> x293, local copies, waits for them, and re-layouts: 55 us -> 53 us
  transfers between devices with their start and end apart: 85 -> 85, of which waited for: 35 -> 33; matrix products, arithmetic and copies ran while one was open for 8% -> 8% of each run, Pallas kernels for 33% -> 35%
where the time goes in v8:
time: 764 us; the launch traced here: 756 us
  Pallas kernels  305 us (40%)
  waiting for transfers between devices  174 us (23%)
  starting transfers between devices  146 us (19%)
  local copies, waits for them, and re-layouts  73.1 us (10%)
  other arithmetic  50.5 us (7%)
    pallas_call x33, Pallas kernels, call(): pl.pallas_call(kernel, grid_spec=pltpu.PrefetchScalarGridSpec(num_scalar_...  281 us
    ppermute x17, waiting for transfers between devices, line_swap(): lax.ppermute(value, 'wt', [(index, index ^ offset) for index in range(4)])  65.6 us
    ppermute x40, waiting for transfers between devices, flip(): lax.ppermute(value, 'ctx', [(index, index ^ bit) for index in range(8)])  61.6 us
    unnamed x293, local copies, waits for them, and re-layouts  53 us
    ppermute x17, starting transfers between devices, line_swap(): lax.ppermute(value, 'wt', [(index, index ^ offset) for index in range(4)])  43.8 us
    ppermute x8, starting transfers between devices, line_inward(): return lax.ppermute(value, 'wt', [(0, 1), (3, 2)])  35.3 us
    ppermute x40, starting transfers between devices, flip(): lax.ppermute(value, 'ctx', [(index, index ^ bit) for index in range(8)])  30.4 us
    ppermute x8, waiting for transfers between devices, line_inward(): return lax.ppermute(value, 'wt', [(0, 1), (3, 2)])  29.5 us
  transfers between devices with their start and end apart: 85, of which 33 were waited for; matrix products, arithmetic and copies ran while one was open for 8% of the time, Pallas kernels for 35%

profile of v8, /device:TPU:0, one launch (start us, length us, event | category | flops | bytes accessed | tf_op | source)
XLA Modules:
  0.0 755.7 jit_solution(10156778822224404330)
XLA Ops:
  9.8 4.8 all-to-all-start.1
  27.0 22.9 %collective-permute-done.5 = bf16[2,192,640]{2,1,0:T(8,128)(2,1)S(1)} collective-permute-done((bf16[2,192,640]{2,1,0:T(8,128)(2,1)S(1)}, bf16[2,192,640]{2,1,0:T(8,128)(2,1)S(1)}, u32[]{:S(2)}, u32[]{:S(2)}) %collective-permute-start.5) | collective-permute-done | bytes 491552 | tf_op jit(solution)/shard_map/ppermute | solution.py:474
  54.1 4.7 all-to-all-start
  61.7 6.9 collective-permute-done.6
  71.7 6.8 project.1
  84.2 11.5 %attend.1 = (bf16[4,256,384]{2,1,0:T(8,128)(2,1)S(1)}, f32[8,1,384]{2,1,0:T(1,128)S(1)}) custom-call(s32[2]{0:T(128)S(1)} %pad_add_fusion.meta.meta_ref, bf16[4,256,384]{2,1,0:T(8,128)(2,1)S(1)} %copy-done.47, bf16[4,256,256]{2,1,0:T(8,128)(2,1)} %get-tuple-element.198.mine_ref, bf16[4,256,256]{2,1,0:T(8,128)(2,1)S(1)} %collective-permute-done.9.other_ref), custom_call_target="tpu_custom_call" | custom-call | flops 300000000 | bytes 1000 | tf_op jit(solution)/shard_map/attend/pallas_call | solution.py:585
  99.1 12.0 %all-to-all-done.refs_4_ = bf16[4,192,1536]{2,1,0:T(8,128)(2,1)} async-done(((bf16[4,192,1536]{2,1,0:T(8,128)(2,1)}), bf16[4,192,1536]{2,1,0:T(8,128)(2,1)}, u32[]{:S(2)}, u32[]{:S(2)}) %all-to-all-start) | async-done | bytes 2359328 | tf_op jit(solution)/shard_map/all_to_all | solution.py:527
  119.7 5.0 collective-permute-done.11.refs_2_
  126.2 6.2 leave.1
  141.6 11.7 %experts.4 = (bf16[4,256,1024]{2,1,0:T(8,128)(2,1)S(1)}, bf16[256,512]{1,0:T(8,128)(2,1)S(1)}, bf16[256,1536]{1,0:T(8,128)(2,1)S(1)}) custom-call(s32[2]{0:T(128)S(1)} %pad_add_fusion.meta.meta_ref, bf16[256,1536]{1,0:T(8,128)(2,1)S(1)} %get-tuple-element.211.rows_ref.refs_0_, f32[4,256,1]{2,1,0:T(8,128)S(1)} %copy-done.40, ...), custom_call_target="tpu_custom_call" | custom-call | flops 300000000 | bytes 1000 | tf_op jit(solution)/shard_map/experts/pallas_call | solution.py:585
  162.3 12.0 %experts.5 = (bf16[4,256,1024]{2,1,0:T(8,128)(2,1)S(1)}, bf16[256,512]{1,0:T(8,128)(2,1)S(1)}, bf16[256,1536]{1,0:T(8,128)(2,1)S(1)}) custom-call(s32[2]{0:T(128)S(1)} %pad_add_fusion.meta.meta_ref, bf16[256,1536]{1,0:T(8,128)(2,1)} %collective-permute-done.15.rows_ref.refs_1_, f32[4,256,1]{2,1,0:T(8,128)S(1)} %copy.40.gates_ref, ...), custom_call_target="tpu_custom_call" | custom-call | flops 300000000 | bytes 1000 | tf_op jit(solution)/shard_map/experts/pallas_call | solution.py:585
  185.5 11.7 %experts.6 = (bf16[4,256,1024]{2,1,0:T(8,128)(2,1)S(1)}, bf16[256,512]{1,0:T(8,128)(2,1)S(1)}, bf16[256,1536]{1,0:T(8,128)(2,1)S(1)}) custom-call(s32[2]{0:T(128)S(1)} %pad_add_fusion.meta.meta_ref, bf16[256,1536]{1,0:T(8,128)(2,1)S(1)} %broadcast_select_fusion.3.rows_ref.refs_2_, f32[4,256,1]{2,1,0:T(8,128)S(1)} %copy-done.38, ...), custom_call_target="tpu_custom_call" | custom-call | flops 300000000 | bytes 1000 | tf_op jit(solution)/shard_map/experts/pallas_call | solution.py:585
  200.4 11.7 %experts.7 = (bf16[4,256,1024]{2,1,0:T(8,128)(2,1)S(1)}, bf16[256,512]{1,0:T(8,128)(2,1)S(1)}, bf16[256,1536]{1,0:T(8,128)(2,1)S(1)}) custom-call(s32[2]{0:T(128)S(1)} %pad_add_fusion.meta.meta_ref, bf16[256,1536]{1,0:T(8,128)(2,1)S(1)} %broadcast_select_fusion.2.rows_ref.refs_3_, f32[4,256,1]{2,1,0:T(8,128)S(1)} %copy-done.36, ...), custom_call_target="tpu_custom_call" | custom-call | flops 300000000 | bytes 1000 | tf_op jit(solution)/shard_map/experts/pallas_call | solution.py:585
  212.2 4.9 collective-permute-start.21
  221.0 13.5 %collective-permute-done.21 = bf16[256,1536]{1,0:T(8,128)(2,1)S(1)} collective-permute-done((bf16[256,1536]{1,0:T(8,128)(2,1)S(1)}, bf16[256,1536]{1,0:T(8,128)(2,1)S(1)}, u32[]{:S(2)}, u32[]{:S(2)}) %collective-permute-start.21) | collective-permute-done | bytes 786464 | tf_op jit(solution)/shard_map/ppermute | solution.py:486
  234.7 4.4 collective-permute-start.24
  243.6 12.2 %collective-permute-done.24 = bf16[256,1536]{1,0:T(8,128)(2,1)S(1)} collective-permute-done((bf16[256,1536]{1,0:T(8,128)(2,1)S(1)}, bf16[256,1536]{1,0:T(8,128)(2,1)S(1)}, u32[]{:S(2)}, u32[]{:S(2)}) %collective-permute-start.24) | collective-permute-done | bytes 786464 | tf_op jit(solution)/shard_map/ppermute | solution.py:486
  262.7 13.8 %collective-permute-done.27 = bf16[256,1536]{1,0:T(8,128)(2,1)S(1)} collective-permute-done((bf16[256,1536]{1,0:T(8,128)(2,1)S(1)}, bf16[256,1536]{1,0:T(8,128)(2,1)S(1)}, u32[]{:S(2)}, u32[]{:S(2)}) %collective-permute-start.27) | collective-permute-done | bytes 786464 | tf_op jit(solution)/shard_map/ppermute | solution.py:474
  284.1 13.0 %experts_back.4 = (bf16[4,256,1024]{2,1,0:T(8,128)(2,1)S(1)}, bf16[4,256,512]{2,1,0:T(8,128)(2,1)S(1)}, bf16[1,256,512]{2,1,0:T(8,128)(2,1)S(1)}, bf16[1,256,256]{2,1,0:T(8,128)(2,1)S(1)}, bf16[256,1536]{1,0:T(8,128)(2,1)S(1)}) custom-call(s32[2]{0:T(128)S(1)} %pad_add_fusion.meta.meta_ref, bf16[256,1536]{1,0:T(8,128)(2,1)S(1)} %get-tuple-element.375.grad_ref.refs_4_, ...), custom_call_target="tpu_custom_call" | custom-call | flops 300000000 | bytes 1000 | tf_op jit(solution)/shard_map/experts_back/pallas_call | solution.py:585
  303.2 13.0 %experts_back.5 = (bf16[4,256,1024]{2,1,0:T(8,128)(2,1)S(1)}, bf16[4,256,512]{2,1,0:T(8,128)(2,1)S(1)}, bf16[1,256,512]{2,1,0:T(8,128)(2,1)S(1)}, bf16[1,256,256]{2,1,0:T(8,128)(2,1)S(1)}, bf16[256,1536]{1,0:T(8,128)(2,1)S(1)}) custom-call(s32[2]{0:T(128)S(1)} %pad_add_fusion.meta.meta_ref, bf16[256,1536]{1,0:T(8,128)(2,1)S(1)} %collective-permute-done.29.grad_ref.refs_5_, ...), custom_call_target="tpu_custom_call" | custom-call | flops 300000000 | bytes 1000 | tf_op jit(solution)/shard_map/experts_back/pallas_call | solution.py:585
  316.3 4.5 pad_maximum_fusion.refs_1_
  326.7 13.0 %experts_back.6 = (bf16[4,256,1024]{2,1,0:T(8,128)(2,1)S(1)}, bf16[4,256,512]{2,1,0:T(8,128)(2,1)S(1)}, bf16[1,256,512]{2,1,0:T(8,128)(2,1)S(1)}, bf16[1,256,256]{2,1,0:T(8,128)(2,1)S(1)}, bf16[256,1536]{1,0:T(8,128)(2,1)S(1)}) custom-call(s32[2]{0:T(128)S(1)} %pad_add_fusion.meta.meta_ref, bf16[256,1536]{1,0:T(8,128)(2,1)S(1)} %broadcast_select_fusion.1.grad_ref.refs_6_, ...), custom_call_target="tpu_custom_call" | custom-call | flops 300000000 | bytes 1000 | tf_op jit(solution)/shard_map/experts_back/pallas_call | solution.py:585
  343.5 14.4 %experts_back.7 = (bf16[4,256,1024]{2,1,0:T(8,128)(2,1)S(1)}, bf16[4,256,512]{2,1,0:T(8,128)(2,1)S(1)}, bf16[1,256,512]{2,1,0:T(8,128)(2,1)S(1)}, bf16[1,256,256]{2,1,0:T(8,128)(2,1)S(1)}, bf16[256,1536]{1,0:T(8,128)(2,1)}) custom-call(s32[2]{0:T(128)S(1)} %pad_add_fusion.meta.meta_ref, bf16[256,1536]{1,0:T(8,128)(2,1)S(1)} %broadcast_select_fusion.grad_ref.refs_7_, ...), custom_call_target="tpu_custom_call" | custom-call | flops 300000000 | bytes 1000 | tf_op jit(solution)/shard_map/experts_back/pallas_call | solution.py:585
  360.4 13.0 %expert_grad.4 = bf16[4,480,1536]{2,1,0:T(8,128)(2,1)} custom-call(s32[3]{0:T(128)S(1)} %add_add_fusion.meta, bf16[256,1536]{1,0:T(8,128)(2,1)S(1)} %copy-done.20, bf16[256,1536]{1,0:T(8,128)(2,1)} %collective-permute-done.15.rows_ref.refs_1_, bf16[256,1536]{1,0:T(8,128)(2,1)S(1)} %broadcast_select_fusion.3.rows_ref.refs_2_, ...), custom_call_target="tpu_custom_call" | custom-call | flops 300000000 | bytes 1000 | tf_op jit(solution)/shard_map/expert_grad/pallas_call | solution.py:585
  375.9 10.1 %expert_grad.5 = bf16[4,384,1536]{2,1,0:T(8,128)(2,1)} custom-call(s32[3]{0:T(128)S(1)} %add_add_fusion.1.meta, bf16[256,1536]{1,0:T(8,128)(2,1)S(1)} %copy-done.21, bf16[256,1536]{1,0:T(8,128)(2,1)} %collective-permute-done.15.rows_ref.refs_1_, bf16[256,1536]{1,0:T(8,128)(2,1)S(1)} %broadcast_select_fusion.3.rows_ref.refs_2_, ...), custom_call_target="tpu_custom_call" | custom-call | flops 300000000 | bytes 1000 | tf_op jit(solution)/shard_map/expert_grad/pallas_call | solution.py:585
  386.6 5.3 collective-permute-start.35
  400.6 12.9 %expert_grad.6.refs_0_ = bf16[4,480,1536]{2,1,0:T(8,128)(2,1)} custom-call(s32[3]{0:T(128)S(1)} %add_add_fusion.2.meta, bf16[256,1536]{1,0:T(8,128)(2,1)S(1)} %copy-done.21, bf16[256,1536]{1,0:T(8,128)(2,1)} %collective-permute-done.15.rows_ref.refs_1_, bf16[256,1536]{1,0:T(8,128)(2,1)S(1)} %broadcast_select_fusion.3.rows_ref.refs_2_, ...), custom_call_target="tpu_custom_call" | custom-call | flops 300000000 | bytes 1000 | tf_op jit(solution)/shard_map/expert_grad/pallas_call | solution.py:585
  413.5 7.8 %blend_split.2 = (bf16[2,480,1536]{2,1,0:T(8,128)(2,1)}, bf16[2,480,1536]{2,1,0:T(8,128)(2,1)S(1)}) custom-call(s32[2]{0:T(128)S(1)} %pad_add_fusion.meta.meta_ref, bf16[4,480,1536]{2,1,0:T(8,128)(2,1)} %expert_grad.6.refs_0_, bf16[4,480,1536]{2,1,0:T(8,128)(2,1)} %collective-permute-done.36.refs_1_), custom_call_target="tpu_custom_call" | custom-call | flops 300000000 | bytes 1000 | tf_op jit(solution)/shard_map/blend_split/pallas_call | solution.py:585
  432.4 10.1 %expert_grad.7.refs_0_ = bf16[4,384,1536]{2,1,0:T(8,128)(2,1)} custom-call(s32[3]{0:T(128)S(1)} %add_add_fusion.3.meta, bf16[256,1536]{1,0:T(8,128)(2,1)S(1)} %copy-done.22, bf16[256,1536]{1,0:T(8,128)(2,1)} %collective-permute-done.15.rows_ref.refs_1_, bf16[256,1536]{1,0:T(8,128)(2,1)S(1)} %broadcast_select_fusion.3.rows_ref.refs_2_, ...), custom_call_target="tpu_custom_call" | custom-call | flops 300000000 | bytes 1000 | tf_op jit(solution)/shard_map/expert_grad/pallas_call | solution.py:585
  442.5 6.1 blend_split.3
  456.4 16.2 %collective-permute-done.40 = bf16[256,1536]{1,0:T(8,128)(2,1)} collective-permute-done((bf16[256,1536]{1,0:T(8,128)(2,1)}, bf16[256,1536]{1,0:T(8,128)(2,1)}, u32[]{:S(2)}, u32[]{:S(2)}) %collective-permute-start.40) | collective-permute-done | bytes 786464 | tf_op jit(solution)/shard_map/ppermute | solution.py:474
  475.4 7.2 enter_back.1
  497.1 5.2 blend_pair.2
  503.1 10.6 %collective-permute-done.44.refs_1_ = bf16[2,384,1536]{2,1,0:T(8,128)(2,1)} collective-permute-done((bf16[2,384,1536]{2,1,0:T(8,128)(2,1)}, bf16[2,384,1536]{2,1,0:T(8,128)(2,1)}, u32[]{:S(2)}, u32[]{:S(2)}) %collective-permute-start.44) | collective-permute-done | bytes 2359328 | tf_op jit(solution)/shard_map/ppermute | solution.py:470
  522.6 15.8 %attend_back.1 = (bf16[4,256,384]{2,1,0:T(8,128)(2,1)S(1)}, f32[4,256,256]{2,1,0:T(8,128)S(1)}, bf16[4,256,256]{2,1,0:T(8,128)(2,1)S(1)}) custom-call(s32[2]{0:T(128)S(1)} %pad_add_fusion.meta.meta_ref, bf16[4,256,384]{2,1,0:T(8,128)(2,1)S(1)} %copy-done.48, bf16[4,256,256]{2,1,0:T(8,128)(2,1)} %get-tuple-element.198.mine_ref, ...), custom_call_target="tpu_custom_call" | custom-call | flops 300000000 | bytes 1000 | tf_op jit(solution)/shard_map/attend_back/pallas_call | solution.py:585
  548.3 4.6 blend_sum.3.refs_0_
  556.1 5.5 collective-permute-start.48
  566.0 6.3 weight_grad.3
  588.1 7.5 collective-permute-done.50.refs_1_
  596.5 5.4 blend_stack.3.refs_0_
  604.3 9.0 %finish.1 = (f32[1,256,1536]{2,1,0:T(8,128)}, f32[1,1536]{1,0:T(1,128)S(1)}) custom-call(s32[2]{0:T(128)S(1)} %pad_add_fusion.meta.meta_ref, bf16[4,256,640]{2,1,0:T(8,128)(2,1)} %all-to-all-done.3.refs_0_, bf16[4,768,640]{2,1,0:T(8,128)(2,1)} %pad_maximum_fusion.refs_1_, bf16[4,768,640]{2,1,0:T(8,128)(2,1)} %collective-permute-done.51.refs_2_, ...), custom_call_target="tpu_custom_call" | custom-call | flops 300000000 | bytes 1000 | tf_op jit(solution)/shard_map/finish/pallas_call | solution.py:585
  635.1 15.4 %collective-permute-start.56 = (f32[8,1536]{1,0:T(8,128)S(1)}, f32[8,1536]{1,0:T(8,128)S(1)}, u32[]{:S(2)}, u32[]{:S(2)}) collective-permute-start(f32[8,1536]{1,0:T(8,128)S(1)} %fusion.12), channel_id=1, source_target_pairs={{0,2},{1,3},{2,0},{3,1},{4,6},{5,7},{6,4},{7,5},{8,10},{9,11},{10,... | collective-permute-start | bytes 147464 | tf_op jit(solution)/shard_map/ppermute | solution.py:474
  659.1 5.5 blend_four.2.refs_0_
  664.6 7.5 blend_four.3.refs_1_
  683.2 5.6 collective-permute-done.72
  699.3 12.8 %place_pair.2.refs_0_ = f32[4,1536,1536]{2,1,0:T(8,128)} custom-call(s32[2]{0:T(128)S(1)} %pad_add_fusion.meta.meta_ref, bf16[4,384,1536]{2,1,0:T(8,128)(2,1)} %blend_four.2.refs_0_, bf16[4,384,1536]{2,1,0:T(8,128)(2,1)} %collective-permute-done.73.refs_1_), custom_call_target="tpu_custom_call" | custom-call | flops 300000000 | bytes 1000 | tf_op jit(solution)/shard_map/place_pair/pallas_call | solution.py:1363
  717.9 11.6 %place_pair.3 = f32[4,1536,1536]{2,1,0:T(8,128)} custom-call(s32[2]{0:T(128)S(1)} %pad_add_fusion.meta.meta_ref, f32[4,1536,1536]{2,1,0:T(8,128)} %place_pair.2.refs_0_, bf16[4,480,1536]{2,1,0:T(8,128)(2,1)S(1)} %bitcast.107, bf16[4,480,1536]{2,1,0:T(8,128)(2,1)} %collective-permute-done.77.refs_2_), custom_call_target="tpu_custom_call", output_to_operand_aliasing={{}: (1, {})} | custom-call | flops 300000000 | bytes 1000 | tf_op jit(solution)/shard_map/place_pair/pallas_call | solution.py:1363
  746.2 8.2 %place_shared.1 = f32[384,3072]{1,0:T(8,128)} custom-call(s32[2]{0:T(128)S(1)} %pad_add_fusion.meta.meta_ref, bf16[4,96,1536]{2,1,0:T(8,128)(2,1)S(1)} %pad_maximum_fusion.4.mine_low.mine_high, bf16[4,96,1536]{2,1,0:T(8,128)(2,1)S(1)} %pad_maximum_fusion.4.mine_low.mine_high, bf16[4,96,1536]{2,1,0:T(8,128)(2,1)} %collective-permute-done.80.other_low.other_high, ...), custom_call_target="tpu_custom_call" | custom-call | flops 300000000 | bytes 1000 | tf_op jit(solution)/shard_map/place_shared/pallas_call | solution.py:585
  (560 shorter events, 289.6 us)
Async XLA Ops:
  9.8 42.7 %all-to-all-start.1 = ((bf16[4,256,1536]{2,1,0:T(8,128)(2,1)}), bf16[4,256,1536]{2,1,0:T(8,128)(2,1)}, u32[]{:S(2)}, u32[]{:S(2)}) async-start(bf16[4,256,1536]{2,1,0:T(8,128)(2,1)} %broadcast_in_dim.55), calls=%async_computation.1 | async-start | bytes 6291456 | tf_op jit(solution)/shard_map/all_to_all | solution.py:516
  20.4 29.5 %collective-permute-start.5 = (bf16[2,192,640]{2,1,0:T(8,128)(2,1)S(1)}, bf16[2,192,640]{2,1,0:T(8,128)(2,1)S(1)}, u32[]{:S(2)}, u32[]{:S(2)}) collective-permute-start(bf16[2,192,640]{2,1,0:T(8,128)(2,1)S(1)} %pad_maximum_fusion.9), channel_id=1, source_target_pairs={{0,2},{1,3},{2,0},{3,1},{4,6},{5,7},{6,4},{7,5},{8,10},{9,11},{10,... | collective-permute-start | bytes 1474568 | tf_op jit(solution)/shard_map/ppermute | solution.py:474
  23.1 28.0 %collective-permute-start.4 = (f32[2,32,256]{2,1,0:T(8,128)S(1)}, f32[2,32,256]{2,1,0:T(8,128)S(1)}, u32[]{:S(2)}, u32[]{:S(2)}) collective-permute-start(f32[2,32,256]{2,1,0:T(8,128)S(1)} %pad_maximum_fusion.16), channel_id=1, source_target_pairs={{0,2},{1,3},{2,0},{3,1},{4,6},{5,7},{6,4},{7,5},{8,10},{9,11},{10,... | collective-permute-start | bytes 196616 | tf_op jit(solution)/shard_map/ppermute | solution.py:474
  24.7 27.7 %collective-permute-start.3 = (bf16[2,48,768]{2,1,0:T(8,128)(2,1)S(1)}, bf16[2,48,768]{2,1,0:T(8,128)(2,1)S(1)}, u32[]{:S(2)}, u32[]{:S(2)}) collective-permute-start(bf16[2,48,768]{2,1,0:T(8,128)(2,1)S(1)} %pad_maximum_fusion.14), channel_id=1, source_target_pairs={{0,2},{1,3},{2,0},{3,1},{4,6},{5,7},{6,4},{7,5},{8,10},{9,11},{10,... | collective-permute-start | bytes 442376 | tf_op jit(solution)/shard_map/ppermute | solution.py:474
  54.1 57.0 %all-to-all-start = ((bf16[4,192,1536]{2,1,0:T(8,128)(2,1)}), bf16[4,192,1536]{2,1,0:T(8,128)(2,1)}, u32[]{:S(2)}, u32[]{:S(2)}) async-start(bf16[4,192,1536]{2,1,0:T(8,128)(2,1)} %broadcast_in_dim.54), calls=%async_computation | async-start | bytes 4718592 | tf_op jit(solution)/shard_map/all_to_all | solution.py:527
  111.1 26.1 %collective-permute-start.14 = (bf16[4,4,48,768]{3,2,1,0:T(8,128)(2,1)}, bf16[4,4,48,768]{3,2,1,0:T(8,128)(2,1)}, u32[]{:S(2)}, u32[]{:S(2)}) collective-permute-start(bf16[4,4,48,768]{3,2,1,0:T(8,128)(2,1)} %pad_maximum_fusion.3.mine), channel_id=1, source_target_pairs={{0,4},{4,0},{8,12},{12,8},{16,20},{20,16},{24,28},{28,24},{1,5},{5... | collective-permute-start | bytes 3538952 | tf_op jit(solution)/shard_map/ppermute | solution.py:470
  133.5 22.1 %collective-permute-start.15 = (bf16[256,1536]{1,0:T(8,128)(2,1)S(1)}, bf16[256,1536]{1,0:T(8,128)(2,1)}, u32[]{:S(2)}, u32[]{:S(2)}) collective-permute-start(bf16[256,1536]{1,0:T(8,128)(2,1)S(1)} %get-tuple-element.211.rows_ref.refs_0_), channel_id=1, source_target_pairs={{0,1},{1,0},{2,3},{3,2},{4,5},{5,4},{6,7},{7,6},{8,9},{9,8},{10,11... | collective-permute-start | bytes 2359304 | tf_op jit(solution)/shard_map/ppermute | solution.py:474
  133.6 22.1 %collective-permute-start.16 = (bf16[256,1536]{1,0:T(8,128)(2,1)S(1)}, bf16[256,1536]{1,0:T(8,128)(2,1)}, u32[]{:S(2)}, u32[]{:S(2)}) collective-permute-start(bf16[256,1536]{1,0:T(8,128)(2,1)S(1)} %get-tuple-element.211.rows_ref.refs_0_), channel_id=1, source_target_pairs={{1,2},{2,1},{5,6},{6,5},{9,10},{10,9},{13,14},{14,13},{17,18},{18,... | collective-permute-start | bytes 2359304 | tf_op jit(solution)/shard_map/ppermute | solution.py:478
  155.6 20.1 %collective-permute-start.17 = (bf16[256,1536]{1,0:T(8,128)(2,1)}, bf16[256,1536]{1,0:T(8,128)(2,1)}, u32[]{:S(2)}, u32[]{:S(2)}) collective-permute-start(bf16[256,1536]{1,0:T(8,128)(2,1)} %collective-permute-done.15.rows_ref.refs_1_), channel_id=1, source_target_pairs={{1,2},{2,1},{5,6},{6,5},{9,10},{10,9},{13,14},{14,13},{17,18},{18,... | collective-permute-start | bytes 2359304 | tf_op jit(solution)/shard_map/ppermute | solution.py:478
  157.2 22.2 %collective-permute-start.18 = (bf16[256,1536]{1,0:T(8,128)(2,1)}, bf16[256,1536]{1,0:T(8,128)(2,1)}, u32[]{:S(2)}, u32[]{:S(2)}) collective-permute-start(bf16[256,1536]{1,0:T(8,128)(2,1)} %collective-permute-done.16), channel_id=1, source_target_pairs={{1,0},{2,3},{5,4},{6,7},{9,8},{10,11},{13,12},{14,15},{17,16},{18,... | collective-permute-start | bytes 2359304 | tf_op jit(solution)/shard_map/ppermute | solution.py:482
  179.3 20.1 %collective-permute-start.19 = (bf16[256,1536]{1,0:T(8,128)(2,1)}, bf16[256,1536]{1,0:T(8,128)(2,1)S(1)}, u32[]{:S(2)}, u32[]{:S(2)}) collective-permute-start(bf16[256,1536]{1,0:T(8,128)(2,1)} %collective-permute-done.17), channel_id=1, source_target_pairs={{1,0},{2,3},{5,4},{6,7},{9,8},{10,11},{13,12},{14,15},{17,16},{18,... | collective-permute-start | bytes 2359304 | tf_op jit(solution)/shard_map/ppermute | solution.py:482
  182.0 38.8 %collective-permute-start.22 = (bf16[768,640]{1,0:T(8,128)(2,1)S(1)}, bf16[768,640]{1,0:T(8,128)(2,1)S(1)}, u32[]{:S(2)}, u32[]{:S(2)}) collective-permute-start(bf16[768,640]{1,0:T(8,128)(2,1)S(1)} %constant_dynamic-slice_fusion.1), channel_id=1, source_target_pairs={{0,8},{4,12},{8,0},{12,4},{16,24},{20,28},{24,16},{28,20},{1,9},{5... | collective-permute-start | bytes 2949128 | tf_op jit(solution)/shard_map/ppermute | solution.py:470
  212.2 22.3 %collective-permute-start.21 = (bf16[256,1536]{1,0:T(8,128)(2,1)S(1)}, bf16[256,1536]{1,0:T(8,128)(2,1)S(1)}, u32[]{:S(2)}, u32[]{:S(2)}) collective-permute-start(bf16[256,1536]{1,0:T(8,128)(2,1)S(1)} %get-tuple-element.227), channel_id=1, source_target_pairs={{0,1},{3,2},{4,5},{7,6},{8,9},{11,10},{12,13},{15,14},{16,17},{19,... | collective-permute-start | bytes 2359304 | tf_op jit(solution)/shard_map/ppermute | solution.py:486
  234.7 21.1 %collective-permute-start.24 = (bf16[256,1536]{1,0:T(8,128)(2,1)S(1)}, bf16[256,1536]{1,0:T(8,128)(2,1)S(1)}, u32[]{:S(2)}, u32[]{:S(2)}) collective-permute-start(bf16[256,1536]{1,0:T(8,128)(2,1)S(1)} %add.250), channel_id=1, source_target_pairs={{0,1},{3,2},{4,5},{7,6},{8,9},{11,10},{12,13},{15,14},{16,17},{19,... | collective-permute-start | bytes 2359304 | tf_op jit(solution)/shard_map/ppermute | solution.py:486
  256.1 20.4 %collective-permute-start.27 = (bf16[256,1536]{1,0:T(8,128)(2,1)S(1)}, bf16[256,1536]{1,0:T(8,128)(2,1)S(1)}, u32[]{:S(2)}, u32[]{:S(2)}) collective-permute-start(bf16[256,1536]{1,0:T(8,128)(2,1)S(1)} %add.252), channel_id=1, source_target_pairs={{0,1},{1,0},{2,3},{3,2},{4,5},{5,4},{6,7},{7,6},{8,9},{9,8},{10,11... | collective-permute-start | bytes 2359304 | tf_op jit(solution)/shard_map/ppermute | solution.py:474
  260.7 55.6 %collective-permute-start.33 = (bf16[2,768,640]{2,1,0:T(8,128)(2,1)S(1)}, bf16[2,768,640]{2,1,0:T(8,128)(2,1)}, u32[]{:S(2)}, u32[]{:S(2)}) collective-permute-start(bf16[2,768,640]{2,1,0:T(8,128)(2,1)S(1)} %pad_maximum_fusion.1), channel_id=1, source_target_pairs={{0,16},{4,20},{8,24},{12,28},{16,0},{20,4},{24,8},{28,12},{1,17},{... | collective-permute-start | bytes 5898248 | tf_op jit(solution)/shard_map/ppermute | solution.py:470
  279.6 20.8 %collective-permute-start.29 = (bf16[256,1536]{1,0:T(8,128)(2,1)S(1)}, bf16[256,1536]{1,0:T(8,128)(2,1)S(1)}, u32[]{:S(2)}, u32[]{:S(2)}) collective-permute-start(bf16[256,1536]{1,0:T(8,128)(2,1)S(1)} %get-tuple-element.375.grad_ref.refs_4_), channel_id=1, source_target_pairs={{0,1},{1,0},{2,3},{3,2},{4,5},{5,4},{6,7},{7,6},{8,9},{9,8},{10,11... | collective-permute-start | bytes 2359304 | tf_op jit(solution)/shard_map/ppermute | solution.py:474
  300.3 20.5 %collective-permute-start.31 = (bf16[256,1536]{1,0:T(8,128)(2,1)S(1)}, bf16[256,1536]{1,0:T(8,128)(2,1)}, u32[]{:S(2)}, u32[]{:S(2)}) collective-permute-start(bf16[256,1536]{1,0:T(8,128)(2,1)S(1)} %collective-permute-done.29.grad_ref.refs_5_), channel_id=1, source_target_pairs={{1,2},{2,1},{5,6},{6,5},{9,10},{10,9},{13,14},{14,13},{17,18},{18,... | collective-permute-start | bytes 2359304 | tf_op jit(solution)/shard_map/ppermute | solution.py:478
  373.4 40.1 %collective-permute-start.36 = (bf16[4,480,1536]{2,1,0:T(8,128)(2,1)}, bf16[4,480,1536]{2,1,0:T(8,128)(2,1)}, u32[]{:S(2)}, u32[]{:S(2)}) collective-permute-start(bf16[4,480,1536]{2,1,0:T(8,128)(2,1)} %expert_grad.4), channel_id=1, source_target_pairs={{0,4},{4,0},{8,12},{12,8},{16,20},{20,16},{24,28},{28,24},{1,5},{5... | collective-permute-start | bytes 17694728 | tf_op jit(solution)/shard_map/ppermute | solution.py:470
  386.1 56.4 %collective-permute-start.39 = (bf16[4,384,1536]{2,1,0:T(8,128)(2,1)}, bf16[4,384,1536]{2,1,0:T(8,128)(2,1)}, u32[]{:S(2)}, u32[]{:S(2)}) collective-permute-start(bf16[4,384,1536]{2,1,0:T(8,128)(2,1)} %expert_grad.5), channel_id=1, source_target_pairs={{0,4},{4,0},{8,12},{12,8},{16,20},{20,16},{24,28},{28,24},{1,5},{5... | collective-permute-start | bytes 14155784 | tf_op jit(solution)/shard_map/ppermute | solution.py:470
  386.6 36.3 %collective-permute-start.35 = (bf16[256,1536]{1,0:T(8,128)(2,1)}, bf16[256,1536]{1,0:T(8,128)(2,1)}, u32[]{:S(2)}, u32[]{:S(2)}) collective-permute-start(bf16[256,1536]{1,0:T(8,128)(2,1)} %get-tuple-element.261), channel_id=1, source_target_pairs={{0,1},{3,2},{4,5},{7,6},{8,9},{11,10},{12,13},{15,14},{16,17},{19,... | collective-permute-start | bytes 2359304 | tf_op jit(solution)/shard_map/ppermute | solution.py:486
  425.2 23.4 %collective-permute-start.37 = (bf16[256,1536]{1,0:T(8,128)(2,1)}, bf16[256,1536]{1,0:T(8,128)(2,1)}, u32[]{:S(2)}, u32[]{:S(2)}) collective-permute-start(bf16[256,1536]{1,0:T(8,128)(2,1)} %add.257), channel_id=1, source_target_pairs={{0,1},{3,2},{4,5},{7,6},{8,9},{11,10},{12,13},{15,14},{16,17},{19,... | collective-permute-start | bytes 2359304 | tf_op jit(solution)/shard_map/ppermute | solution.py:486
  427.4 21.2 %collective-permute-start.38 = (bf16[256,1536]{1,0:T(8,128)(2,1)}, bf16[256,1536]{1,0:T(8,128)(2,1)}, u32[]{:S(2)}, u32[]{:S(2)}) collective-permute-start(bf16[256,1536]{1,0:T(8,128)(2,1)} %add.257), channel_id=1, source_target_pairs={{1,2},{2,1},{5,6},{6,5},{9,10},{10,9},{13,14},{14,13},{17,18},{18,... | collective-permute-start | bytes 2359304 | tf_op jit(solution)/shard_map/ppermute | solution.py:478
  429.3 65.9 %collective-permute-start.43 = (bf16[2,480,1536]{2,1,0:T(8,128)(2,1)}, bf16[2,480,1536]{2,1,0:T(8,128)(2,1)}, u32[]{:S(2)}, u32[]{:S(2)}) collective-permute-start(bf16[2,480,1536]{2,1,0:T(8,128)(2,1)} %get-tuple-element.282), channel_id=1, source_target_pairs={{0,8},{4,12},{8,0},{12,4},{16,24},{20,28},{24,16},{28,20},{1,9},{5... | collective-permute-start | bytes 8847368 | tf_op jit(solution)/shard_map/ppermute | solution.py:470
  454.9 58.7 %collective-permute-start.44 = (bf16[2,384,1536]{2,1,0:T(8,128)(2,1)}, bf16[2,384,1536]{2,1,0:T(8,128)(2,1)}, u32[]{:S(2)}, u32[]{:S(2)}) collective-permute-start(bf16[2,384,1536]{2,1,0:T(8,128)(2,1)} %get-tuple-element.286), channel_id=1, source_target_pairs={{0,16},{4,20},{8,24},{12,28},{16,0},{20,4},{24,8},{28,12},{1,17},{... | collective-permute-start | bytes 7077896 | tf_op jit(solution)/shard_map/ppermute | solution.py:470
  489.3 64.6 %collective-permute-start.42 = (bf16[4,192,1536]{2,1,0:T(8,128)(2,1)}, bf16[4,192,1536]{2,1,0:T(8,128)(2,1)}, u32[]{:S(2)}, u32[]{:S(2)}) collective-permute-start(bf16[4,192,1536]{2,1,0:T(8,128)(2,1)} %get-tuple-element.300), channel_id=1, source_target_pairs={{0,4},{4,0},{8,12},{12,8},{16,20},{20,16},{24,28},{28,24},{1,5},{5... | collective-permute-start | bytes 7077896 | tf_op jit(solution)/shard_map/ppermute | solution.py:470
  489.4 112.5 %collective-permute-start.51 = (bf16[4,768,640]{2,1,0:T(8,128)(2,1)}, bf16[4,768,640]{2,1,0:T(8,128)(2,1)}, u32[]{:S(2)}, u32[]{:S(2)}) collective-permute-start(bf16[4,768,640]{2,1,0:T(8,128)(2,1)} %pad_maximum_fusion.refs_1_), channel_id=1, source_target_pairs={{0,4},{4,0},{8,12},{12,8},{16,20},{20,16},{24,28},{28,24},{1,5},{5... | collective-permute-start | bytes 11796488 | tf_op jit(solution)/shard_map/ppermute | solution.py:470
  489.9 30.6 %all-to-all-start.2 = ((bf16[4,256,384]{2,1,0:T(8,128)(2,1)}), bf16[4,256,384]{2,1,0:T(8,128)(2,1)}, u32[]{:S(2)}, u32[]{:S(2)}) async-start(bf16[4,256,384]{2,1,0:T(8,128)(2,1)} %get-tuple-element.297), calls=%async_computation.2 | async-start | bytes 1572864 | tf_op jit(solution)/shard_map/all_to_all | solution.py:516
  502.3 46.1 %collective-permute-start.47 = (bf16[480,1536]{1,0:T(8,128)(2,1)}, bf16[480,1536]{1,0:T(8,128)(2,1)}, u32[]{:S(2)}, u32[]{:S(2)}) collective-permute-start(bf16[480,1536]{1,0:T(8,128)(2,1)} %get-tuple-element.303), channel_id=1, source_target_pairs={{0,16},{4,20},{8,24},{12,28},{16,0},{20,4},{24,8},{28,12},{1,17},{... | collective-permute-start | bytes 4423688 | tf_op jit(solution)/shard_map/ppermute | solution.py:470
  519.0 25.1 %collective-permute-start.46 = (bf16[384,1536]{1,0:T(8,128)(2,1)}, bf16[384,1536]{1,0:T(8,128)(2,1)}, u32[]{:S(2)}, u32[]{:S(2)}) collective-permute-start(bf16[384,1536]{1,0:T(8,128)(2,1)} %get-tuple-element.306), channel_id=1, source_target_pairs={{0,8},{4,12},{8,0},{12,4},{16,24},{20,28},{24,16},{28,20},{1,9},{5... | collective-permute-start | bytes 3538952 | tf_op jit(solution)/shard_map/ppermute | solution.py:470
  546.8 29.1 %collective-permute-start.49 = (bf16[384,1536]{1,0:T(8,128)(2,1)S(1)}, bf16[384,1536]{1,0:T(8,128)(2,1)}, u32[]{:S(2)}, u32[]{:S(2)}) collective-permute-start(bf16[384,1536]{1,0:T(8,128)(2,1)S(1)} %blend_sum.2.refs_0_), channel_id=1, source_target_pairs={{0,8},{4,12},{8,0},{12,4},{16,24},{20,28},{24,16},{28,20},{1,9},{5... | collective-permute-start | bytes 3538952 | tf_op jit(solution)/shard_map/ppermute | solution.py:470
  553.0 42.6 %collective-permute-start.50 = (bf16[480,1536]{1,0:T(8,128)(2,1)}, bf16[480,1536]{1,0:T(8,128)(2,1)}, u32[]{:S(2)}, u32[]{:S(2)}) collective-permute-start(bf16[480,1536]{1,0:T(8,128)(2,1)} %blend_sum.3.refs_0_), channel_id=1, source_target_pairs={{0,16},{4,20},{8,24},{12,28},{16,0},{20,4},{24,8},{28,12},{1,17},{... | collective-permute-start | bytes 4423688 | tf_op jit(solution)/shard_map/ppermute | solution.py:470
  556.1 24.1 %collective-permute-start.48 = (bf16[192,1536]{1,0:T(8,128)(2,1)}, bf16[192,1536]{1,0:T(8,128)(2,1)}, u32[]{:S(2)}, u32[]{:S(2)}) collective-permute-start(bf16[192,1536]{1,0:T(8,128)(2,1)} %add_bitcast_fusion), channel_id=1, source_target_pairs={{0,1},{3,2},{4,5},{7,6},{8,9},{11,10},{12,13},{15,14},{16,17},{19,... | collective-permute-start | bytes 1769480 | tf_op jit(solution)/shard_map/ppermute | solution.py:486
  561.6 41.3 %all-to-all-start.3 = ((bf16[4,256,640]{2,1,0:T(8,128)(2,1)}), bf16[4,256,640]{2,1,0:T(8,128)(2,1)}, u32[]{:S(2)}, u32[]{:S(2)}) async-start(bf16[4,256,640]{2,1,0:T(8,128)(2,1)} %pad_maximum_fusion.2), calls=%async_computation.3 | async-start | bytes 2621440 | tf_op jit(solution)/shard_map/all_to_all | solution.py:516
  573.3 40.1 %collective-permute-start.55 = (bf16[4,192,640]{2,1,0:T(8,128)(2,1)}, bf16[4,192,640]{2,1,0:T(8,128)(2,1)}, u32[]{:S(2)}, u32[]{:S(2)}) collective-permute-start(bf16[4,192,640]{2,1,0:T(8,128)(2,1)} %get-tuple-element.328), channel_id=1, source_target_pairs={{0,4},{4,0},{8,12},{12,8},{16,20},{20,16},{24,28},{28,24},{1,5},{5... | collective-permute-start | bytes 2949128 | tf_op jit(solution)/shard_map/ppermute | solution.py:470
  582.4 36.2 %collective-permute-start.53 = (bf16[192,1536]{1,0:T(8,128)(2,1)}, bf16[192,1536]{1,0:T(8,128)(2,1)S(1)}, u32[]{:S(2)}, u32[]{:S(2)}) collective-permute-start(bf16[192,1536]{1,0:T(8,128)(2,1)} %bitcast_add_fusion.1), channel_id=1, source_target_pairs={{0,1},{3,2},{4,5},{7,6},{8,9},{11,10},{12,13},{15,14},{16,17},{19,... | collective-permute-start | bytes 1769480 | tf_op jit(solution)/shard_map/ppermute | solution.py:486
  586.6 32.1 %collective-permute-start.54 = (bf16[192,1536]{1,0:T(8,128)(2,1)}, bf16[192,1536]{1,0:T(8,128)(2,1)S(1)}, u32[]{:S(2)}, u32[]{:S(2)}) collective-permute-start(bf16[192,1536]{1,0:T(8,128)(2,1)} %bitcast_add_fusion.1), channel_id=1, source_target_pairs={{1,2},{2,1},{5,6},{6,5},{9,10},{10,9},{13,14},{14,13},{17,18},{18,... | collective-permute-start | bytes 1769480 | tf_op jit(solution)/shard_map/ppermute | solution.py:478
  595.5 63.5 %collective-permute-start.65 = (bf16[2,384,1536]{2,1,0:T(8,128)(2,1)}, bf16[2,384,1536]{2,1,0:T(8,128)(2,1)}, u32[]{:S(2)}, u32[]{:S(2)}) collective-permute-start(bf16[2,384,1536]{2,1,0:T(8,128)(2,1)} %blend_stack.2.refs_0_), channel_id=1, source_target_pairs={{0,16},{4,20},{8,24},{12,28},{16,0},{20,4},{24,8},{28,12},{1,17},{... | collective-permute-start | bytes 7077896 | tf_op jit(solution)/shard_map/ppermute | solution.py:470
  601.9 62.8 %collective-permute-start.66 = (bf16[2,480,1536]{2,1,0:T(8,128)(2,1)}, bf16[2,480,1536]{2,1,0:T(8,128)(2,1)}, u32[]{:S(2)}, u32[]{:S(2)}) collective-permute-start(bf16[2,480,1536]{2,1,0:T(8,128)(2,1)} %blend_stack.3.refs_0_), channel_id=1, source_target_pairs={{0,8},{4,12},{8,0},{12,4},{16,24},{20,28},{24,16},{28,20},{1,9},{5... | collective-permute-start | bytes 8847368 | tf_op jit(solution)/shard_map/ppermute | solution.py:470
  629.8 21.8 %collective-permute-start.62 = (bf16[192,1536]{1,0:T(8,128)(2,1)S(1)}, bf16[192,1536]{1,0:T(8,128)(2,1)S(1)}, u32[]{:S(2)}, u32[]{:S(2)}) collective-permute-start(bf16[192,1536]{1,0:T(8,128)(2,1)S(1)} %bitcast_add_fusion), channel_id=1, source_target_pairs={{0,1},{1,0},{2,3},{3,2},{4,5},{5,4},{6,7},{7,6},{8,9},{9,8},{10,11... | collective-permute-start | bytes 1769480 | tf_op jit(solution)/shard_map/ppermute | solution.py:474
  629.9 21.8 %collective-permute-start.63 = (bf16[192,1536]{1,0:T(8,128)(2,1)S(1)}, bf16[192,1536]{1,0:T(8,128)(2,1)S(1)}, u32[]{:S(2)}, u32[]{:S(2)}) collective-permute-start(bf16[192,1536]{1,0:T(8,128)(2,1)S(1)} %add.274), channel_id=1, source_target_pairs={{1,2},{2,1},{5,6},{6,5},{9,10},{10,9},{13,14},{14,13},{17,18},{18,... | collective-permute-start | bytes 1769480 | tf_op jit(solution)/shard_map/ppermute | solution.py:478
  635.1 23.8 %collective-permute-start.56 = (f32[8,1536]{1,0:T(8,128)S(1)}, f32[8,1536]{1,0:T(8,128)S(1)}, u32[]{:S(2)}, u32[]{:S(2)}) collective-permute-start(f32[8,1536]{1,0:T(8,128)S(1)} %fusion.12), channel_id=1, source_target_pairs={{0,2},{1,3},{2,0},{3,1},{4,6},{5,7},{6,4},{7,5},{8,10},{9,11},{10,... | collective-permute-start | bytes 147464 | tf_op jit(solution)/shard_map/ppermute | solution.py:474
  672.1 45.8 %collective-permute-start.77 = (bf16[4,480,1536]{2,1,0:T(8,128)(2,1)}, bf16[4,480,1536]{2,1,0:T(8,128)(2,1)}, u32[]{:S(2)}, u32[]{:S(2)}) collective-permute-start(bf16[4,480,1536]{2,1,0:T(8,128)(2,1)} %blend_four.3.refs_1_), channel_id=1, source_target_pairs={{0,4},{4,0},{8,12},{12,8},{16,20},{20,16},{24,28},{28,24},{1,5},{5... | collective-permute-start | bytes 17694728 | tf_op jit(solution)/shard_map/ppermute | solution.py:470
  672.1 26.6 %collective-permute-start.73 = (bf16[4,384,1536]{2,1,0:T(8,128)(2,1)}, bf16[4,384,1536]{2,1,0:T(8,128)(2,1)}, u32[]{:S(2)}, u32[]{:S(2)}) collective-permute-start(bf16[4,384,1536]{2,1,0:T(8,128)(2,1)} %blend_four.2.refs_0_), channel_id=1, source_target_pairs={{0,4},{4,0},{8,12},{12,8},{16,20},{20,16},{24,28},{28,24},{1,5},{5... | collective-permute-start | bytes 14155784 | tf_op jit(solution)/shard_map/ppermute | solution.py:470
  675.4 21.7 %collective-permute-start.68 = (bf16[96,1536]{1,0:T(8,128)(2,1)S(1)}, bf16[96,1536]{1,0:T(8,128)(2,1)S(1)}, u32[]{:S(2)}, u32[]{:S(2)}) collective-permute-start(bf16[96,1536]{1,0:T(8,128)(2,1)S(1)} %get-tuple-element.352), channel_id=1, source_target_pairs={{0,1},{1,0},{2,3},{3,2},{4,5},{5,4},{6,7},{7,6},{8,9},{9,8},{10,11... | collective-permute-start | bytes 884744 | tf_op jit(solution)/shard_map/ppermute | solution.py:474
  689.6 24.1 %collective-permute-start.69 = (bf16[96,1536]{1,0:T(8,128)(2,1)S(1)}, bf16[96,1536]{1,0:T(8,128)(2,1)S(1)}, u32[]{:S(2)}, u32[]{:S(2)}) collective-permute-start(bf16[96,1536]{1,0:T(8,128)(2,1)S(1)} %get-tuple-element.353), channel_id=1, source_target_pairs={{0,2},{1,3},{2,0},{3,1},{4,6},{5,7},{6,4},{7,5},{8,10},{9,11},{10,... | collective-permute-start | bytes 884744 | tf_op jit(solution)/shard_map/ppermute | solution.py:474
  697.1 32.4 %collective-permute-start.76 = (bf16[192,1536]{1,0:T(8,128)(2,1)S(1)}, bf16[192,1536]{1,0:T(8,128)(2,1)S(1)}, u32[]{:S(2)}, u32[]{:S(2)}) collective-permute-start(bf16[192,1536]{1,0:T(8,128)(2,1)S(1)} %add.295), channel_id=1, source_target_pairs={{0,16},{4,20},{8,24},{12,28},{16,0},{20,4},{24,8},{28,12},{1,17},{... | collective-permute-start | bytes 1769480 | tf_op jit(solution)/shard_map/ppermute | solution.py:470
  698.7 31.8 %collective-permute-start.75 = (bf16[2,192,640]{2,1,0:T(8,128)(2,1)S(1)}, bf16[2,192,640]{2,1,0:T(8,128)(2,1)S(1)}, u32[]{:S(2)}, u32[]{:S(2)}) collective-permute-start(bf16[2,192,640]{2,1,0:T(8,128)(2,1)S(1)} %pad_maximum_fusion.10), channel_id=1, source_target_pairs={{0,16},{4,20},{8,24},{12,28},{16,0},{20,4},{24,8},{28,12},{1,17},{... | collective-permute-start | bytes 1474568 | tf_op jit(solution)/shard_map/ppermute | solution.py:470
  (181 other events, 1649.7 us)

commit v9 on v8

--- a/solution.py
+++ b/solution.py
@@ -1497,7 +1497,7 @@
     "M", "K", "R", "M", "K", "M", "M", "M", "M", "R", "M", "M",
 )
 LATE = (
-    "L", "0", "1", "0", "0", "L", "1", "1", "L", "L", "O", "0", "1", "L", "L", "1", "0", "O", "Q", "1", "O", "0", "L", "Q",
+    "L", "0", "1", "0", "L", "0", "1", "1", "L", "L", "O", "0", "1", "L", "0", "L", "1", "O", "Q", "O", "0", "1", "L", "Q",
     "O", "L", "Q", "Q", "O", "Q", "L", "1", "0", "O", "Q", "S", "L", "O", "Q", "1", "S", "L", "0", "O", "Q", "L", "Q", "O",
     "S",
 )

time: 764 us -> 789 us (1.033)
  waiting for transfers between devices: 174 us -> 201 us
    all_to_all x3, waiting for transfers between devices: 0.01 us -> 33.3 us  [chips_exchange(): lax.all_to_all(blocks, 'ctx', split_axis=0, concat_axis=0, tiled=True, ax...]
    unnamed x293 -> x291, local copies, waits for them, and re-layouts: 53 us -> 55.9 us
  transfers between devices with their start and end apart: 85 -> 85, of which waited for: 33 -> 34; matrix products, arithmetic and copies ran while one was open for 8% -> 8% of each run, Pallas kernels for 35% -> 34%
where the time goes in v9:
time: 789 us; the launch traced here: 781 us
  Pallas kernels  307 us (39%)
  waiting for transfers between devices  201 us (25%)
  starting transfers between devices  140 us (18%)
  local copies, waits for them, and re-layouts  75.9 us (10%)
  other arithmetic  50.9 us (6%)
    pallas_call x33, Pallas kernels, call(): pl.pallas_call(kernel, grid_spec=pltpu.PrefetchScalarGridSpec(num_scalar_...  283 us
    ppermute x17, waiting for transfers between devices, line_swap(): lax.ppermute(value, 'wt', [(index, index ^ offset) for index in range(4)])  63.1 us
    ppermute x40, waiting for transfers between devices, flip(): lax.ppermute(value, 'ctx', [(index, index ^ bit) for index in range(8)])  55.9 us
    unnamed x291, local copies, waits for them, and re-layouts  55.9 us
    ppermute x17, starting transfers between devices, line_swap(): lax.ppermute(value, 'wt', [(index, index ^ offset) for index in range(4)])  40.8 us
    all_to_all x3, waiting for transfers between devices, chips_exchange(): lax.all_to_all(blocks, 'ctx', split_axis=0, concat_axis=0, tiled=True, ax...  33.3 us
    ppermute x8, starting transfers between devices, line_inward(): return lax.ppermute(value, 'wt', [(0, 1), (3, 2)])  33.3 us
    ppermute x8, waiting for transfers between devices, line_inward(): return lax.ppermute(value, 'wt', [(0, 1), (3, 2)])  31.3 us
  transfers between devices with their start and end apart: 85, of which 34 were waited for; matrix products, arithmetic and copies ran while one was open for 8% of the time, Pallas kernels for 34%

profile of v9, /device:TPU:0, one launch (start us, length us, event | category | flops | bytes accessed | tf_op | source)
XLA Modules:
  0.0 780.7 jit_solution(11273385043696498947)
XLA Ops:
  9.8 4.9 all-to-all-start.1
  27.0 22.9 %collective-permute-done.5 = bf16[2,192,640]{2,1,0:T(8,128)(2,1)S(1)} collective-permute-done((bf16[2,192,640]{2,1,0:T(8,128)(2,1)S(1)}, bf16[2,192,640]{2,1,0:T(8,128)(2,1)S(1)}, u32[]{:S(2)}, u32[]{:S(2)}) %collective-permute-start.5) | collective-permute-done | bytes 491552 | tf_op jit(solution)/shard_map/ppermute | solution.py:474
  61.8 6.9 collective-permute-done.6
  71.8 6.8 project.1
  84.3 11.5 %attend.1 = (bf16[4,256,384]{2,1,0:T(8,128)(2,1)S(1)}, f32[8,1,384]{2,1,0:T(1,128)S(1)}) custom-call(s32[2]{0:T(128)S(1)} %pad_add_fusion.meta.meta_ref, bf16[4,256,384]{2,1,0:T(8,128)(2,1)S(1)} %copy-done.47, bf16[4,256,256]{2,1,0:T(8,128)(2,1)} %get-tuple-element.198.mine_ref, bf16[4,256,256]{2,1,0:T(8,128)(2,1)S(1)} %collective-permute-done.9.other_ref), custom_call_target="tpu_custom_call" | custom-call | flops 300000000 | bytes 1000 | tf_op jit(solution)/shard_map/attend/pallas_call | solution.py:585
  99.2 12.0 %all-to-all-done.refs_4_ = bf16[4,192,1536]{2,1,0:T(8,128)(2,1)} async-done(((bf16[4,192,1536]{2,1,0:T(8,128)(2,1)}), bf16[4,192,1536]{2,1,0:T(8,128)(2,1)}, u32[]{:S(2)}, u32[]{:S(2)}) %all-to-all-start) | async-done | bytes 2359328 | tf_op jit(solution)/shard_map/all_to_all | solution.py:527
  119.8 5.0 collective-permute-done.11.refs_2_
  126.3 6.2 leave.1
  141.8 11.7 %experts.4 = (bf16[4,256,1024]{2,1,0:T(8,128)(2,1)S(1)}, bf16[256,512]{1,0:T(8,128)(2,1)S(1)}, bf16[256,1536]{1,0:T(8,128)(2,1)S(1)}) custom-call(s32[2]{0:T(128)S(1)} %pad_add_fusion.meta.meta_ref, bf16[256,1536]{1,0:T(8,128)(2,1)S(1)} %get-tuple-element.211.rows_ref.refs_0_, f32[4,256,1]{2,1,0:T(8,128)S(1)} %copy-done.40, ...), custom_call_target="tpu_custom_call" | custom-call | flops 300000000 | bytes 1000 | tf_op jit(solution)/shard_map/experts/pallas_call | solution.py:585
  162.4 12.0 %experts.5 = (bf16[4,256,1024]{2,1,0:T(8,128)(2,1)S(1)}, bf16[256,512]{1,0:T(8,128)(2,1)S(1)}, bf16[256,1536]{1,0:T(8,128)(2,1)S(1)}) custom-call(s32[2]{0:T(128)S(1)} %pad_add_fusion.meta.meta_ref, bf16[256,1536]{1,0:T(8,128)(2,1)} %collective-permute-done.15.rows_ref.refs_1_, f32[4,256,1]{2,1,0:T(8,128)S(1)} %copy.40.gates_ref, ...), custom_call_target="tpu_custom_call" | custom-call | flops 300000000 | bytes 1000 | tf_op jit(solution)/shard_map/experts/pallas_call | solution.py:585
  185.6 11.7 %experts.6 = (bf16[4,256,1024]{2,1,0:T(8,128)(2,1)S(1)}, bf16[256,512]{1,0:T(8,128)(2,1)S(1)}, bf16[256,1536]{1,0:T(8,128)(2,1)S(1)}) custom-call(s32[2]{0:T(128)S(1)} %pad_add_fusion.meta.meta_ref, bf16[256,1536]{1,0:T(8,128)(2,1)S(1)} %broadcast_select_fusion.3.rows_ref.refs_2_, f32[4,256,1]{2,1,0:T(8,128)S(1)} %copy-done.38, ...), custom_call_target="tpu_custom_call" | custom-call | flops 300000000 | bytes 1000 | tf_op jit(solution)/shard_map/experts/pallas_call | solution.py:585
  200.5 11.7 %experts.7 = (bf16[4,256,1024]{2,1,0:T(8,128)(2,1)S(1)}, bf16[256,512]{1,0:T(8,128)(2,1)S(1)}, bf16[256,1536]{1,0:T(8,128)(2,1)S(1)}) custom-call(s32[2]{0:T(128)S(1)} %pad_add_fusion.meta.meta_ref, bf16[256,1536]{1,0:T(8,128)(2,1)S(1)} %broadcast_select_fusion.2.rows_ref.refs_3_, f32[4,256,1]{2,1,0:T(8,128)S(1)} %copy-done.36, ...), custom_call_target="tpu_custom_call" | custom-call | flops 300000000 | bytes 1000 | tf_op jit(solution)/shard_map/experts/pallas_call | solution.py:585
  212.2 4.9 collective-permute-start.21
  221.1 13.5 %collective-permute-done.21 = bf16[256,1536]{1,0:T(8,128)(2,1)S(1)} collective-permute-done((bf16[256,1536]{1,0:T(8,128)(2,1)S(1)}, bf16[256,1536]{1,0:T(8,128)(2,1)S(1)}, u32[]{:S(2)}, u32[]{:S(2)}) %collective-permute-start.21) | collective-permute-done | bytes 786464 | tf_op jit(solution)/shard_map/ppermute | solution.py:486
  243.6 12.2 %collective-permute-done.24 = bf16[256,1536]{1,0:T(8,128)(2,1)S(1)} collective-permute-done((bf16[256,1536]{1,0:T(8,128)(2,1)S(1)}, bf16[256,1536]{1,0:T(8,128)(2,1)S(1)}, u32[]{:S(2)}, u32[]{:S(2)}) %collective-permute-start.24) | collective-permute-done | bytes 786464 | tf_op jit(solution)/shard_map/ppermute | solution.py:486
  262.7 13.8 %collective-permute-done.27 = bf16[256,1536]{1,0:T(8,128)(2,1)S(1)} collective-permute-done((bf16[256,1536]{1,0:T(8,128)(2,1)S(1)}, bf16[256,1536]{1,0:T(8,128)(2,1)S(1)}, u32[]{:S(2)}, u32[]{:S(2)}) %collective-permute-start.27) | collective-permute-done | bytes 786464 | tf_op jit(solution)/shard_map/ppermute | solution.py:474
  284.1 13.0 %experts_back.4 = (bf16[4,256,1024]{2,1,0:T(8,128)(2,1)S(1)}, bf16[4,256,512]{2,1,0:T(8,128)(2,1)S(1)}, bf16[1,256,512]{2,1,0:T(8,128)(2,1)S(1)}, bf16[1,256,256]{2,1,0:T(8,128)(2,1)S(1)}, bf16[256,1536]{1,0:T(8,128)(2,1)S(1)}) custom-call(s32[2]{0:T(128)S(1)} %pad_add_fusion.meta.meta_ref, bf16[256,1536]{1,0:T(8,128)(2,1)S(1)} %get-tuple-element.375.grad_ref.refs_4_, ...), custom_call_target="tpu_custom_call" | custom-call | flops 300000000 | bytes 1000 | tf_op jit(solution)/shard_map/experts_back/pallas_call | solution.py:585
  303.2 13.0 %experts_back.5 = (bf16[4,256,1024]{2,1,0:T(8,128)(2,1)S(1)}, bf16[4,256,512]{2,1,0:T(8,128)(2,1)S(1)}, bf16[1,256,512]{2,1,0:T(8,128)(2,1)S(1)}, bf16[1,256,256]{2,1,0:T(8,128)(2,1)S(1)}, bf16[256,1536]{1,0:T(8,128)(2,1)S(1)}) custom-call(s32[2]{0:T(128)S(1)} %pad_add_fusion.meta.meta_ref, bf16[256,1536]{1,0:T(8,128)(2,1)S(1)} %collective-permute-done.29.grad_ref.refs_5_, ...), custom_call_target="tpu_custom_call" | custom-call | flops 300000000 | bytes 1000 | tf_op jit(solution)/shard_map/experts_back/pallas_call | solution.py:585
  326.7 13.0 %experts_back.6 = (bf16[4,256,1024]{2,1,0:T(8,128)(2,1)S(1)}, bf16[4,256,512]{2,1,0:T(8,128)(2,1)S(1)}, bf16[1,256,512]{2,1,0:T(8,128)(2,1)S(1)}, bf16[1,256,256]{2,1,0:T(8,128)(2,1)S(1)}, bf16[256,1536]{1,0:T(8,128)(2,1)S(1)}) custom-call(s32[2]{0:T(128)S(1)} %pad_add_fusion.meta.meta_ref, bf16[256,1536]{1,0:T(8,128)(2,1)S(1)} %broadcast_select_fusion.1.grad_ref.refs_6_, ...), custom_call_target="tpu_custom_call" | custom-call | flops 300000000 | bytes 1000 | tf_op jit(solution)/shard_map/experts_back/pallas_call | solution.py:585
  343.5 14.4 %experts_back.7 = (bf16[4,256,1024]{2,1,0:T(8,128)(2,1)S(1)}, bf16[4,256,512]{2,1,0:T(8,128)(2,1)S(1)}, bf16[1,256,512]{2,1,0:T(8,128)(2,1)S(1)}, bf16[1,256,256]{2,1,0:T(8,128)(2,1)S(1)}, bf16[256,1536]{1,0:T(8,128)(2,1)}) custom-call(s32[2]{0:T(128)S(1)} %pad_add_fusion.meta.meta_ref, bf16[256,1536]{1,0:T(8,128)(2,1)S(1)} %broadcast_select_fusion.grad_ref.refs_7_, ...), custom_call_target="tpu_custom_call" | custom-call | flops 300000000 | bytes 1000 | tf_op jit(solution)/shard_map/experts_back/pallas_call | solution.py:585
  360.5 13.1 %expert_grad.4 = bf16[4,480,1536]{2,1,0:T(8,128)(2,1)} custom-call(s32[3]{0:T(128)S(1)} %add_add_fusion.meta, bf16[256,1536]{1,0:T(8,128)(2,1)S(1)} %copy-done.20, bf16[256,1536]{1,0:T(8,128)(2,1)} %collective-permute-done.15.rows_ref.refs_1_, bf16[256,1536]{1,0:T(8,128)(2,1)S(1)} %broadcast_select_fusion.3.rows_ref.refs_2_, ...), custom_call_target="tpu_custom_call" | custom-call | flops 300000000 | bytes 1000 | tf_op jit(solution)/shard_map/expert_grad/pallas_call | solution.py:585
  376.0 10.1 %expert_grad.5 = bf16[4,384,1536]{2,1,0:T(8,128)(2,1)} custom-call(s32[3]{0:T(128)S(1)} %add_add_fusion.1.meta, bf16[256,1536]{1,0:T(8,128)(2,1)S(1)} %copy-done.21, bf16[256,1536]{1,0:T(8,128)(2,1)} %collective-permute-done.15.rows_ref.refs_1_, bf16[256,1536]{1,0:T(8,128)(2,1)S(1)} %broadcast_select_fusion.3.rows_ref.refs_2_, ...), custom_call_target="tpu_custom_call" | custom-call | flops 300000000 | bytes 1000 | tf_op jit(solution)/shard_map/expert_grad/pallas_call | solution.py:585
  386.6 5.4 collective-permute-start.35
  400.7 12.9 %expert_grad.6.refs_0_ = bf16[4,480,1536]{2,1,0:T(8,128)(2,1)} custom-call(s32[3]{0:T(128)S(1)} %add_add_fusion.2.meta, bf16[256,1536]{1,0:T(8,128)(2,1)S(1)} %copy-done.21, bf16[256,1536]{1,0:T(8,128)(2,1)} %collective-permute-done.15.rows_ref.refs_1_, bf16[256,1536]{1,0:T(8,128)(2,1)S(1)} %broadcast_select_fusion.3.rows_ref.refs_2_, ...), custom_call_target="tpu_custom_call" | custom-call | flops 300000000 | bytes 1000 | tf_op jit(solution)/shard_map/expert_grad/pallas_call | solution.py:585
  415.9 7.7 blend_split.2
  433.4 10.1 %expert_grad.7.refs_0_ = bf16[4,384,1536]{2,1,0:T(8,128)(2,1)} custom-call(s32[3]{0:T(128)S(1)} %add_add_fusion.3.meta, bf16[256,1536]{1,0:T(8,128)(2,1)S(1)} %copy-done.22, bf16[256,1536]{1,0:T(8,128)(2,1)} %collective-permute-done.15.rows_ref.refs_1_, bf16[256,1536]{1,0:T(8,128)(2,1)S(1)} %broadcast_select_fusion.3.rows_ref.refs_2_, ...), custom_call_target="tpu_custom_call" | custom-call | flops 300000000 | bytes 1000 | tf_op jit(solution)/shard_map/expert_grad/pallas_call | solution.py:585
  443.5 6.1 blend_split.3
  457.5 16.1 %collective-permute-done.40 = bf16[256,1536]{1,0:T(8,128)(2,1)} collective-permute-done((bf16[256,1536]{1,0:T(8,128)(2,1)}, bf16[256,1536]{1,0:T(8,128)(2,1)}, u32[]{:S(2)}, u32[]{:S(2)}) %collective-permute-start.40) | collective-permute-done | bytes 786464 | tf_op jit(solution)/shard_map/ppermute | solution.py:474
  476.5 7.4 enter_back.1
  491.2 5.1 blend_pair.2
  503.1 11.6 %collective-permute-done.44.refs_1_ = bf16[2,384,1536]{2,1,0:T(8,128)(2,1)} collective-permute-done((bf16[2,384,1536]{2,1,0:T(8,128)(2,1)}, bf16[2,384,1536]{2,1,0:T(8,128)(2,1)}, u32[]{:S(2)}, u32[]{:S(2)}) %collective-permute-start.44) | collective-permute-done | bytes 2359328 | tf_op jit(solution)/shard_map/ppermute | solution.py:470
  523.3 25.7 %all-to-all-done.2.refs_1_ = bf16[4,256,384]{2,1,0:T(8,128)(2,1)} async-done(((bf16[4,256,384]{2,1,0:T(8,128)(2,1)}), bf16[4,256,384]{2,1,0:T(8,128)(2,1)}, u32[]{:S(2)}, u32[]{:S(2)}) %all-to-all-start.2) | async-done | bytes 786464 | tf_op jit(solution)/shard_map/all_to_all | solution.py:516
  551.1 15.6 %attend_back.1 = (bf16[4,256,384]{2,1,0:T(8,128)(2,1)S(1)}, f32[4,256,256]{2,1,0:T(8,128)S(1)}, bf16[4,256,256]{2,1,0:T(8,128)(2,1)S(1)}) custom-call(s32[2]{0:T(128)S(1)} %pad_add_fusion.meta.meta_ref, bf16[4,256,384]{2,1,0:T(8,128)(2,1)S(1)} %copy-done.48, bf16[4,256,256]{2,1,0:T(8,128)(2,1)} %get-tuple-element.198.mine_ref, ...), custom_call_target="tpu_custom_call" | custom-call | flops 300000000 | bytes 1000 | tf_op jit(solution)/shard_map/attend_back/pallas_call | solution.py:585
  568.2 4.8 blend_sum.2.refs_0_
  581.4 5.7 collective-permute-start.48
  592.1 6.3 weight_grad.3
  601.7 5.0 collective-permute-start.53
  610.7 5.4 blend_stack.2.refs_0_
  622.6 7.7 all-to-all-done.3.refs_0_
  631.7 9.0 %finish.1 = (f32[1,256,1536]{2,1,0:T(8,128)}, f32[1,1536]{1,0:T(1,128)S(1)}) custom-call(s32[2]{0:T(128)S(1)} %pad_add_fusion.meta.meta_ref, bf16[4,256,640]{2,1,0:T(8,128)(2,1)} %all-to-all-done.3.refs_0_, bf16[4,768,640]{2,1,0:T(8,128)(2,1)} %pad_maximum_fusion.refs_1_, bf16[4,768,640]{2,1,0:T(8,128)(2,1)} %collective-permute-done.51.refs_2_, ...), custom_call_target="tpu_custom_call" | custom-call | flops 300000000 | bytes 1000 | tf_op jit(solution)/shard_map/finish/pallas_call | solution.py:585
  654.0 5.6 collective-permute-done.58
  660.3 15.9 %collective-permute-start.56 = (f32[8,1536]{1,0:T(8,128)S(1)}, f32[8,1536]{1,0:T(8,128)S(1)}, u32[]{:S(2)}, u32[]{:S(2)}) collective-permute-start(f32[8,1536]{1,0:T(8,128)S(1)} %fusion.12), channel_id=1, source_target_pairs={{0,2},{1,3},{2,0},{3,1},{4,6},{5,7},{6,4},{7,5},{8,10},{9,11},{10,... | collective-permute-start | bytes 147464 | tf_op jit(solution)/shard_map/ppermute | solution.py:474
  684.7 5.5 blend_four.2.refs_0_
  692.4 7.4 blend_four.3.refs_1_
  710.2 6.5 collective-permute-done.72
  725.2 12.3 %place_pair.2.refs_0_ = f32[4,1536,1536]{2,1,0:T(8,128)} custom-call(s32[2]{0:T(128)S(1)} %pad_add_fusion.meta.meta_ref, bf16[4,384,1536]{2,1,0:T(8,128)(2,1)} %blend_four.2.refs_0_, bf16[4,384,1536]{2,1,0:T(8,128)(2,1)} %collective-permute-done.73.refs_1_), custom_call_target="tpu_custom_call" | custom-call | flops 300000000 | bytes 1000 | tf_op jit(solution)/shard_map/place_pair/pallas_call | solution.py:1363
  742.9 11.6 %place_pair.3 = f32[4,1536,1536]{2,1,0:T(8,128)} custom-call(s32[2]{0:T(128)S(1)} %pad_add_fusion.meta.meta_ref, f32[4,1536,1536]{2,1,0:T(8,128)} %place_pair.2.refs_0_, bf16[4,480,1536]{2,1,0:T(8,128)(2,1)S(1)} %bitcast.107, bf16[4,480,1536]{2,1,0:T(8,128)(2,1)} %collective-permute-done.77.refs_2_), custom_call_target="tpu_custom_call", output_to_operand_aliasing={{}: (1, {})} | custom-call | flops 300000000 | bytes 1000 | tf_op jit(solution)/shard_map/place_pair/pallas_call | solution.py:1363
  771.2 8.2 %place_shared.1 = f32[384,3072]{1,0:T(8,128)} custom-call(s32[2]{0:T(128)S(1)} %pad_add_fusion.meta.meta_ref, bf16[4,96,1536]{2,1,0:T(8,128)(2,1)S(1)} %pad_maximum_fusion.4.mine_low.mine_high, bf16[4,96,1536]{2,1,0:T(8,128)(2,1)S(1)} %pad_maximum_fusion.4.mine_low.mine_high, bf16[4,96,1536]{2,1,0:T(8,128)(2,1)} %collective-permute-done.80.other_low.other_high, ...), custom_call_target="tpu_custom_call" | custom-call | flops 300000000 | bytes 1000 | tf_op jit(solution)/shard_map/place_shared/pallas_call | solution.py:585
  (558 shorter events, 289.5 us)
Async XLA Ops:
  9.8 42.8 %all-to-all-start.1 = ((bf16[4,256,1536]{2,1,0:T(8,128)(2,1)}), bf16[4,256,1536]{2,1,0:T(8,128)(2,1)}, u32[]{:S(2)}, u32[]{:S(2)}) async-start(bf16[4,256,1536]{2,1,0:T(8,128)(2,1)} %broadcast_in_dim.55), calls=%async_computation.1 | async-start | bytes 6291456 | tf_op jit(solution)/shard_map/all_to_all | solution.py:516
  20.5 29.5 %collective-permute-start.5 = (bf16[2,192,640]{2,1,0:T(8,128)(2,1)S(1)}, bf16[2,192,640]{2,1,0:T(8,128)(2,1)S(1)}, u32[]{:S(2)}, u32[]{:S(2)}) collective-permute-start(bf16[2,192,640]{2,1,0:T(8,128)(2,1)S(1)} %pad_maximum_fusion.9), channel_id=1, source_target_pairs={{0,2},{1,3},{2,0},{3,1},{4,6},{5,7},{6,4},{7,5},{8,10},{9,11},{10,... | collective-permute-start | bytes 1474568 | tf_op jit(solution)/shard_map/ppermute | solution.py:474
  23.2 28.0 %collective-permute-start.4 = (f32[2,32,256]{2,1,0:T(8,128)S(1)}, f32[2,32,256]{2,1,0:T(8,128)S(1)}, u32[]{:S(2)}, u32[]{:S(2)}) collective-permute-start(f32[2,32,256]{2,1,0:T(8,128)S(1)} %pad_maximum_fusion.16), channel_id=1, source_target_pairs={{0,2},{1,3},{2,0},{3,1},{4,6},{5,7},{6,4},{7,5},{8,10},{9,11},{10,... | collective-permute-start | bytes 196616 | tf_op jit(solution)/shard_map/ppermute | solution.py:474
  24.7 27.7 %collective-permute-start.3 = (bf16[2,48,768]{2,1,0:T(8,128)(2,1)S(1)}, bf16[2,48,768]{2,1,0:T(8,128)(2,1)S(1)}, u32[]{:S(2)}, u32[]{:S(2)}) collective-permute-start(bf16[2,48,768]{2,1,0:T(8,128)(2,1)S(1)} %pad_maximum_fusion.14), channel_id=1, source_target_pairs={{0,2},{1,3},{2,0},{3,1},{4,6},{5,7},{6,4},{7,5},{8,10},{9,11},{10,... | collective-permute-start | bytes 442376 | tf_op jit(solution)/shard_map/ppermute | solution.py:474
  54.2 57.0 %all-to-all-start = ((bf16[4,192,1536]{2,1,0:T(8,128)(2,1)}), bf16[4,192,1536]{2,1,0:T(8,128)(2,1)}, u32[]{:S(2)}, u32[]{:S(2)}) async-start(bf16[4,192,1536]{2,1,0:T(8,128)(2,1)} %broadcast_in_dim.54), calls=%async_computation | async-start | bytes 4718592 | tf_op jit(solution)/shard_map/all_to_all | solution.py:527
  111.2 26.1 %collective-permute-start.14 = (bf16[4,4,48,768]{3,2,1,0:T(8,128)(2,1)}, bf16[4,4,48,768]{3,2,1,0:T(8,128)(2,1)}, u32[]{:S(2)}, u32[]{:S(2)}) collective-permute-start(bf16[4,4,48,768]{3,2,1,0:T(8,128)(2,1)} %pad_maximum_fusion.3.mine), channel_id=1, source_target_pairs={{0,4},{4,0},{8,12},{12,8},{16,20},{20,16},{24,28},{28,24},{1,5},{5... | collective-permute-start | bytes 3538952 | tf_op jit(solution)/shard_map/ppermute | solution.py:470
  133.7 22.1 %collective-permute-start.15 = (bf16[256,1536]{1,0:T(8,128)(2,1)S(1)}, bf16[256,1536]{1,0:T(8,128)(2,1)}, u32[]{:S(2)}, u32[]{:S(2)}) collective-permute-start(bf16[256,1536]{1,0:T(8,128)(2,1)S(1)} %get-tuple-element.211.rows_ref.refs_0_), channel_id=1, source_target_pairs={{0,1},{1,0},{2,3},{3,2},{4,5},{5,4},{6,7},{7,6},{8,9},{9,8},{10,11... | collective-permute-start | bytes 2359304 | tf_op jit(solution)/shard_map/ppermute | solution.py:474
  133.7 22.1 %collective-permute-start.16 = (bf16[256,1536]{1,0:T(8,128)(2,1)S(1)}, bf16[256,1536]{1,0:T(8,128)(2,1)}, u32[]{:S(2)}, u32[]{:S(2)}) collective-permute-start(bf16[256,1536]{1,0:T(8,128)(2,1)S(1)} %get-tuple-element.211.rows_ref.refs_0_), channel_id=1, source_target_pairs={{1,2},{2,1},{5,6},{6,5},{9,10},{10,9},{13,14},{14,13},{17,18},{18,... | collective-permute-start | bytes 2359304 | tf_op jit(solution)/shard_map/ppermute | solution.py:478
  155.7 20.0 %collective-permute-start.17 = (bf16[256,1536]{1,0:T(8,128)(2,1)}, bf16[256,1536]{1,0:T(8,128)(2,1)}, u32[]{:S(2)}, u32[]{:S(2)}) collective-permute-start(bf16[256,1536]{1,0:T(8,128)(2,1)} %collective-permute-done.15.rows_ref.refs_1_), channel_id=1, source_target_pairs={{1,2},{2,1},{5,6},{6,5},{9,10},{10,9},{13,14},{14,13},{17,18},{18,... | collective-permute-start | bytes 2359304 | tf_op jit(solution)/shard_map/ppermute | solution.py:478
  157.3 22.1 %collective-permute-start.18 = (bf16[256,1536]{1,0:T(8,128)(2,1)}, bf16[256,1536]{1,0:T(8,128)(2,1)}, u32[]{:S(2)}, u32[]{:S(2)}) collective-permute-start(bf16[256,1536]{1,0:T(8,128)(2,1)} %collective-permute-done.16), channel_id=1, source_target_pairs={{1,0},{2,3},{5,4},{6,7},{9,8},{10,11},{13,12},{14,15},{17,16},{18,... | collective-permute-start | bytes 2359304 | tf_op jit(solution)/shard_map/ppermute | solution.py:482
  179.4 20.1 %collective-permute-start.19 = (bf16[256,1536]{1,0:T(8,128)(2,1)}, bf16[256,1536]{1,0:T(8,128)(2,1)S(1)}, u32[]{:S(2)}, u32[]{:S(2)}) collective-permute-start(bf16[256,1536]{1,0:T(8,128)(2,1)} %collective-permute-done.17), channel_id=1, source_target_pairs={{1,0},{2,3},{5,4},{6,7},{9,8},{10,11},{13,12},{14,15},{17,16},{18,... | collective-permute-start | bytes 2359304 | tf_op jit(solution)/shard_map/ppermute | solution.py:482
  182.1 38.8 %collective-permute-start.22 = (bf16[768,640]{1,0:T(8,128)(2,1)S(1)}, bf16[768,640]{1,0:T(8,128)(2,1)S(1)}, u32[]{:S(2)}, u32[]{:S(2)}) collective-permute-start(bf16[768,640]{1,0:T(8,128)(2,1)S(1)} %constant_dynamic-slice_fusion.1), channel_id=1, source_target_pairs={{0,8},{4,12},{8,0},{12,4},{16,24},{20,28},{24,16},{28,20},{1,9},{5... | collective-permute-start | bytes 2949128 | tf_op jit(solution)/shard_map/ppermute | solution.py:470
  212.2 22.3 %collective-permute-start.21 = (bf16[256,1536]{1,0:T(8,128)(2,1)S(1)}, bf16[256,1536]{1,0:T(8,128)(2,1)S(1)}, u32[]{:S(2)}, u32[]{:S(2)}) collective-permute-start(bf16[256,1536]{1,0:T(8,128)(2,1)S(1)} %get-tuple-element.227), channel_id=1, source_target_pairs={{0,1},{3,2},{4,5},{7,6},{8,9},{11,10},{12,13},{15,14},{16,17},{19,... | collective-permute-start | bytes 2359304 | tf_op jit(solution)/shard_map/ppermute | solution.py:486
  234.7 21.0 %collective-permute-start.24 = (bf16[256,1536]{1,0:T(8,128)(2,1)S(1)}, bf16[256,1536]{1,0:T(8,128)(2,1)S(1)}, u32[]{:S(2)}, u32[]{:S(2)}) collective-permute-start(bf16[256,1536]{1,0:T(8,128)(2,1)S(1)} %add.250), channel_id=1, source_target_pairs={{0,1},{3,2},{4,5},{7,6},{8,9},{11,10},{12,13},{15,14},{16,17},{19,... | collective-permute-start | bytes 2359304 | tf_op jit(solution)/shard_map/ppermute | solution.py:486
  256.2 20.3 %collective-permute-start.27 = (bf16[256,1536]{1,0:T(8,128)(2,1)S(1)}, bf16[256,1536]{1,0:T(8,128)(2,1)S(1)}, u32[]{:S(2)}, u32[]{:S(2)}) collective-permute-start(bf16[256,1536]{1,0:T(8,128)(2,1)S(1)} %add.252), channel_id=1, source_target_pairs={{0,1},{1,0},{2,3},{3,2},{4,5},{5,4},{6,7},{7,6},{8,9},{9,8},{10,11... | collective-permute-start | bytes 2359304 | tf_op jit(solution)/shard_map/ppermute | solution.py:474
  260.7 55.6 %collective-permute-start.33 = (bf16[2,768,640]{2,1,0:T(8,128)(2,1)S(1)}, bf16[2,768,640]{2,1,0:T(8,128)(2,1)}, u32[]{:S(2)}, u32[]{:S(2)}) collective-permute-start(bf16[2,768,640]{2,1,0:T(8,128)(2,1)S(1)} %pad_maximum_fusion.1), channel_id=1, source_target_pairs={{0,16},{4,20},{8,24},{12,28},{16,0},{20,4},{24,8},{28,12},{1,17},{... | collective-permute-start | bytes 5898248 | tf_op jit(solution)/shard_map/ppermute | solution.py:470
  279.6 20.8 %collective-permute-start.29 = (bf16[256,1536]{1,0:T(8,128)(2,1)S(1)}, bf16[256,1536]{1,0:T(8,128)(2,1)S(1)}, u32[]{:S(2)}, u32[]{:S(2)}) collective-permute-start(bf16[256,1536]{1,0:T(8,128)(2,1)S(1)} %get-tuple-element.375.grad_ref.refs_4_), channel_id=1, source_target_pairs={{0,1},{1,0},{2,3},{3,2},{4,5},{5,4},{6,7},{7,6},{8,9},{9,8},{10,11... | collective-permute-start | bytes 2359304 | tf_op jit(solution)/shard_map/ppermute | solution.py:474
  300.4 20.5 %collective-permute-start.31 = (bf16[256,1536]{1,0:T(8,128)(2,1)S(1)}, bf16[256,1536]{1,0:T(8,128)(2,1)}, u32[]{:S(2)}, u32[]{:S(2)}) collective-permute-start(bf16[256,1536]{1,0:T(8,128)(2,1)S(1)} %collective-permute-done.29.grad_ref.refs_5_), channel_id=1, source_target_pairs={{1,2},{2,1},{5,6},{6,5},{9,10},{10,9},{13,14},{14,13},{17,18},{18,... | collective-permute-start | bytes 2359304 | tf_op jit(solution)/shard_map/ppermute | solution.py:478
  301.9 20.0 %collective-permute-start.32 = (bf16[256,1536]{1,0:T(8,128)(2,1)S(1)}, bf16[256,1536]{1,0:T(8,128)(2,1)S(1)}, u32[]{:S(2)}, u32[]{:S(2)}) collective-permute-start(bf16[256,1536]{1,0:T(8,128)(2,1)S(1)} %collective-permute-done.30), channel_id=1, source_target_pairs={{1,0},{2,3},{5,4},{6,7},{9,8},{10,11},{13,12},{14,15},{17,16},{18,... | collective-permute-start | bytes 2359304 | tf_op jit(solution)/shard_map/ppermute | solution.py:482
  373.6 42.3 %collective-permute-start.38 = (bf16[4,480,1536]{2,1,0:T(8,128)(2,1)}, bf16[4,480,1536]{2,1,0:T(8,128)(2,1)}, u32[]{:S(2)}, u32[]{:S(2)}) collective-permute-start(bf16[4,480,1536]{2,1,0:T(8,128)(2,1)} %expert_grad.4), channel_id=1, source_target_pairs={{0,4},{4,0},{8,12},{12,8},{16,20},{20,16},{24,28},{28,24},{1,5},{5... | collective-permute-start | bytes 17694728 | tf_op jit(solution)/shard_map/ppermute | solution.py:470
  386.1 57.4 %collective-permute-start.39 = (bf16[4,384,1536]{2,1,0:T(8,128)(2,1)}, bf16[4,384,1536]{2,1,0:T(8,128)(2,1)}, u32[]{:S(2)}, u32[]{:S(2)}) collective-permute-start(bf16[4,384,1536]{2,1,0:T(8,128)(2,1)} %expert_grad.5), channel_id=1, source_target_pairs={{0,4},{4,0},{8,12},{12,8},{16,20},{20,16},{24,28},{28,24},{1,5},{5... | collective-permute-start | bytes 14155784 | tf_op jit(solution)/shard_map/ppermute | solution.py:470
  386.6 27.0 %collective-permute-start.35 = (bf16[256,1536]{1,0:T(8,128)(2,1)}, bf16[256,1536]{1,0:T(8,128)(2,1)}, u32[]{:S(2)}, u32[]{:S(2)}) collective-permute-start(bf16[256,1536]{1,0:T(8,128)(2,1)} %get-tuple-element.261), channel_id=1, source_target_pairs={{0,1},{3,2},{4,5},{7,6},{8,9},{11,10},{12,13},{15,14},{16,17},{19,... | collective-permute-start | bytes 2359304 | tf_op jit(solution)/shard_map/ppermute | solution.py:486
  425.2 66.0 %collective-permute-start.43 = (bf16[2,480,1536]{2,1,0:T(8,128)(2,1)}, bf16[2,480,1536]{2,1,0:T(8,128)(2,1)}, u32[]{:S(2)}, u32[]{:S(2)}) collective-permute-start(bf16[2,480,1536]{2,1,0:T(8,128)(2,1)} %get-tuple-element.283), channel_id=1, source_target_pairs={{0,8},{4,12},{8,0},{12,4},{16,24},{20,28},{24,16},{28,20},{1,9},{5... | collective-permute-start | bytes 8847368 | tf_op jit(solution)/shard_map/ppermute | solution.py:470
  425.8 23.9 %collective-permute-start.36 = (bf16[256,1536]{1,0:T(8,128)(2,1)}, bf16[256,1536]{1,0:T(8,128)(2,1)}, u32[]{:S(2)}, u32[]{:S(2)}) collective-permute-start(bf16[256,1536]{1,0:T(8,128)(2,1)} %add.257), channel_id=1, source_target_pairs={{0,1},{3,2},{4,5},{7,6},{8,9},{11,10},{12,13},{15,14},{16,17},{19,... | collective-permute-start | bytes 2359304 | tf_op jit(solution)/shard_map/ppermute | solution.py:486
  427.9 21.7 %collective-permute-start.37 = (bf16[256,1536]{1,0:T(8,128)(2,1)}, bf16[256,1536]{1,0:T(8,128)(2,1)}, u32[]{:S(2)}, u32[]{:S(2)}) collective-permute-start(bf16[256,1536]{1,0:T(8,128)(2,1)} %add.257), channel_id=1, source_target_pairs={{1,2},{2,1},{5,6},{6,5},{9,10},{10,9},{13,14},{14,13},{17,18},{18,... | collective-permute-start | bytes 2359304 | tf_op jit(solution)/shard_map/ppermute | solution.py:478
  456.0 58.7 %collective-permute-start.44 = (bf16[2,384,1536]{2,1,0:T(8,128)(2,1)}, bf16[2,384,1536]{2,1,0:T(8,128)(2,1)}, u32[]{:S(2)}, u32[]{:S(2)}) collective-permute-start(bf16[2,384,1536]{2,1,0:T(8,128)(2,1)} %get-tuple-element.286), channel_id=1, source_target_pairs={{0,16},{4,20},{8,24},{12,28},{16,0},{20,4},{24,8},{28,12},{1,17},{... | collective-permute-start | bytes 7077896 | tf_op jit(solution)/shard_map/ppermute | solution.py:470
  490.7 89.3 %collective-permute-start.42 = (bf16[4,192,1536]{2,1,0:T(8,128)(2,1)}, bf16[4,192,1536]{2,1,0:T(8,128)(2,1)}, u32[]{:S(2)}, u32[]{:S(2)}) collective-permute-start(bf16[4,192,1536]{2,1,0:T(8,128)(2,1)} %get-tuple-element.300), channel_id=1, source_target_pairs={{0,4},{4,0},{8,12},{12,8},{16,20},{20,16},{24,28},{28,24},{1,5},{5... | collective-permute-start | bytes 7077896 | tf_op jit(solution)/shard_map/ppermute | solution.py:470
  490.7 131.2 %collective-permute-start.51 = (bf16[4,768,640]{2,1,0:T(8,128)(2,1)}, bf16[4,768,640]{2,1,0:T(8,128)(2,1)}, u32[]{:S(2)}, u32[]{:S(2)}) collective-permute-start(bf16[4,768,640]{2,1,0:T(8,128)(2,1)} %pad_maximum_fusion.refs_1_), channel_id=1, source_target_pairs={{0,4},{4,0},{8,12},{12,8},{16,20},{20,16},{24,28},{28,24},{1,5},{5... | collective-permute-start | bytes 11796488 | tf_op jit(solution)/shard_map/ppermute | solution.py:470
  497.4 69.4 %collective-permute-start.46 = (bf16[480,1536]{1,0:T(8,128)(2,1)}, bf16[480,1536]{1,0:T(8,128)(2,1)}, u32[]{:S(2)}, u32[]{:S(2)}) collective-permute-start(bf16[480,1536]{1,0:T(8,128)(2,1)} %get-tuple-element.303), channel_id=1, source_target_pairs={{0,16},{4,20},{8,24},{12,28},{16,0},{20,4},{24,8},{28,12},{1,17},{... | collective-permute-start | bytes 4423688 | tf_op jit(solution)/shard_map/ppermute | solution.py:470
  498.9 50.1 %all-to-all-start.2 = ((bf16[4,256,384]{2,1,0:T(8,128)(2,1)}), bf16[4,256,384]{2,1,0:T(8,128)(2,1)}, u32[]{:S(2)}, u32[]{:S(2)}) async-start(bf16[4,256,384]{2,1,0:T(8,128)(2,1)} %get-tuple-element.297), calls=%async_computation.2 | async-start | bytes 1572864 | tf_op jit(solution)/shard_map/all_to_all | solution.py:516
  521.9 54.1 %collective-permute-start.47 = (bf16[384,1536]{1,0:T(8,128)(2,1)}, bf16[384,1536]{1,0:T(8,128)(2,1)}, u32[]{:S(2)}, u32[]{:S(2)}) collective-permute-start(bf16[384,1536]{1,0:T(8,128)(2,1)} %get-tuple-element.306), channel_id=1, source_target_pairs={{0,8},{4,12},{8,0},{12,4},{16,24},{20,28},{24,16},{28,20},{1,9},{5... | collective-permute-start | bytes 3538952 | tf_op jit(solution)/shard_map/ppermute | solution.py:470
  573.0 35.5 %collective-permute-start.49 = (bf16[480,1536]{1,0:T(8,128)(2,1)}, bf16[480,1536]{1,0:T(8,128)(2,1)}, u32[]{:S(2)}, u32[]{:S(2)}) collective-permute-start(bf16[480,1536]{1,0:T(8,128)(2,1)} %blend_sum.2.refs_0_), channel_id=1, source_target_pairs={{0,16},{4,20},{8,24},{12,28},{16,0},{20,4},{24,8},{28,12},{1,17},{... | collective-permute-start | bytes 4423688 | tf_op jit(solution)/shard_map/ppermute | solution.py:470
  587.0 29.2 %collective-permute-start.50 = (bf16[384,1536]{1,0:T(8,128)(2,1)}, bf16[384,1536]{1,0:T(8,128)(2,1)}, u32[]{:S(2)}, u32[]{:S(2)}) collective-permute-start(bf16[384,1536]{1,0:T(8,128)(2,1)} %blend_sum.3.refs_0_), channel_id=1, source_target_pairs={{0,8},{4,12},{8,0},{12,4},{16,24},{20,28},{24,16},{28,20},{1,9},{5... | collective-permute-start | bytes 3538952 | tf_op jit(solution)/shard_map/ppermute | solution.py:470
  587.6 42.6 %all-to-all-start.3 = ((bf16[4,256,640]{2,1,0:T(8,128)(2,1)}), bf16[4,256,640]{2,1,0:T(8,128)(2,1)}, u32[]{:S(2)}, u32[]{:S(2)}) async-start(bf16[4,256,640]{2,1,0:T(8,128)(2,1)} %pad_maximum_fusion.2), calls=%async_computation.3 | async-start | bytes 2621440 | tf_op jit(solution)/shard_map/all_to_all | solution.py:516
  599.4 41.3 %collective-permute-start.55 = (bf16[4,192,640]{2,1,0:T(8,128)(2,1)}, bf16[4,192,640]{2,1,0:T(8,128)(2,1)}, u32[]{:S(2)}, u32[]{:S(2)}) collective-permute-start(bf16[4,192,640]{2,1,0:T(8,128)(2,1)} %get-tuple-element.328), channel_id=1, source_target_pairs={{0,4},{4,0},{8,12},{12,8},{16,20},{20,16},{24,28},{28,24},{1,5},{5... | collective-permute-start | bytes 2949128 | tf_op jit(solution)/shard_map/ppermute | solution.py:470
  601.7 41.3 %collective-permute-start.53 = (bf16[192,1536]{1,0:T(8,128)(2,1)}, bf16[192,1536]{1,0:T(8,128)(2,1)}, u32[]{:S(2)}, u32[]{:S(2)}) collective-permute-start(bf16[192,1536]{1,0:T(8,128)(2,1)} %bitcast_add_fusion.1), channel_id=1, source_target_pairs={{0,1},{3,2},{4,5},{7,6},{8,9},{11,10},{12,13},{15,14},{16,17},{19,... | collective-permute-start | bytes 1769480 | tf_op jit(solution)/shard_map/ppermute | solution.py:486
  608.5 34.6 %collective-permute-start.54 = (bf16[192,1536]{1,0:T(8,128)(2,1)}, bf16[192,1536]{1,0:T(8,128)(2,1)}, u32[]{:S(2)}, u32[]{:S(2)}) collective-permute-start(bf16[192,1536]{1,0:T(8,128)(2,1)} %bitcast_add_fusion.1), channel_id=1, source_target_pairs={{1,2},{2,1},{5,6},{6,5},{9,10},{10,9},{13,14},{14,13},{17,18},{18,... | collective-permute-start | bytes 1769480 | tf_op jit(solution)/shard_map/ppermute | solution.py:478
  620.6 64.1 %collective-permute-start.65 = (bf16[2,384,1536]{2,1,0:T(8,128)(2,1)}, bf16[2,384,1536]{2,1,0:T(8,128)(2,1)}, u32[]{:S(2)}, u32[]{:S(2)}) collective-permute-start(bf16[2,384,1536]{2,1,0:T(8,128)(2,1)} %blend_stack.3.refs_0_), channel_id=1, source_target_pairs={{0,16},{4,20},{8,24},{12,28},{16,0},{20,4},{24,8},{28,12},{1,17},{... | collective-permute-start | bytes 7077896 | tf_op jit(solution)/shard_map/ppermute | solution.py:470
  621.9 70.5 %collective-permute-start.66 = (bf16[2,480,1536]{2,1,0:T(8,128)(2,1)}, bf16[2,480,1536]{2,1,0:T(8,128)(2,1)}, u32[]{:S(2)}, u32[]{:S(2)}) collective-permute-start(bf16[2,480,1536]{2,1,0:T(8,128)(2,1)} %blend_stack.2.refs_0_), channel_id=1, source_target_pairs={{0,8},{4,12},{8,0},{12,4},{16,24},{20,28},{24,16},{28,20},{1,9},{5... | collective-permute-start | bytes 8847368 | tf_op jit(solution)/shard_map/ppermute | solution.py:470
  653.2 24.0 %collective-permute-start.62 = (bf16[192,1536]{1,0:T(8,128)(2,1)S(1)}, bf16[192,1536]{1,0:T(8,128)(2,1)S(1)}, u32[]{:S(2)}, u32[]{:S(2)}) collective-permute-start(bf16[192,1536]{1,0:T(8,128)(2,1)S(1)} %bitcast_add_fusion), channel_id=1, source_target_pairs={{0,1},{1,0},{2,3},{3,2},{4,5},{5,4},{6,7},{7,6},{8,9},{9,8},{10,11... | collective-permute-start | bytes 1769480 | tf_op jit(solution)/shard_map/ppermute | solution.py:474
  653.3 24.1 %collective-permute-start.63 = (bf16[192,1536]{1,0:T(8,128)(2,1)S(1)}, bf16[192,1536]{1,0:T(8,128)(2,1)S(1)}, u32[]{:S(2)}, u32[]{:S(2)}) collective-permute-start(bf16[192,1536]{1,0:T(8,128)(2,1)S(1)} %add.274), channel_id=1, source_target_pairs={{1,2},{2,1},{5,6},{6,5},{9,10},{10,9},{13,14},{14,13},{17,18},{18,... | collective-permute-start | bytes 1769480 | tf_op jit(solution)/shard_map/ppermute | solution.py:478
  660.3 24.3 %collective-permute-start.56 = (f32[8,1536]{1,0:T(8,128)S(1)}, f32[8,1536]{1,0:T(8,128)S(1)}, u32[]{:S(2)}, u32[]{:S(2)}) collective-permute-start(f32[8,1536]{1,0:T(8,128)S(1)} %fusion.12), channel_id=1, source_target_pairs={{0,2},{1,3},{2,0},{3,1},{4,6},{5,7},{6,4},{7,5},{8,10},{9,11},{10,... | collective-permute-start | bytes 147464 | tf_op jit(solution)/shard_map/ppermute | solution.py:474
  699.8 43.0 %collective-permute-start.77 = (bf16[4,480,1536]{2,1,0:T(8,128)(2,1)}, bf16[4,480,1536]{2,1,0:T(8,128)(2,1)}, u32[]{:S(2)}, u32[]{:S(2)}) collective-permute-start(bf16[4,480,1536]{2,1,0:T(8,128)(2,1)} %blend_four.3.refs_1_), channel_id=1, source_target_pairs={{0,4},{4,0},{8,12},{12,8},{16,20},{20,16},{24,28},{28,24},{1,5},{5... | collective-permute-start | bytes 17694728 | tf_op jit(solution)/shard_map/ppermute | solution.py:470
  699.8 23.9 %collective-permute-start.73 = (bf16[4,384,1536]{2,1,0:T(8,128)(2,1)}, bf16[4,384,1536]{2,1,0:T(8,128)(2,1)}, u32[]{:S(2)}, u32[]{:S(2)}) collective-permute-start(bf16[4,384,1536]{2,1,0:T(8,128)(2,1)} %blend_four.2.refs_0_), channel_id=1, source_target_pairs={{0,4},{4,0},{8,12},{12,8},{16,20},{20,16},{24,28},{28,24},{1,5},{5... | collective-permute-start | bytes 14155784 | tf_op jit(solution)/shard_map/ppermute | solution.py:470
  702.4 20.6 %collective-permute-start.68 = (bf16[96,1536]{1,0:T(8,128)(2,1)S(1)}, bf16[96,1536]{1,0:T(8,128)(2,1)S(1)}, u32[]{:S(2)}, u32[]{:S(2)}) collective-permute-start(bf16[96,1536]{1,0:T(8,128)(2,1)S(1)} %get-tuple-element.352), channel_id=1, source_target_pairs={{0,1},{1,0},{2,3},{3,2},{4,5},{5,4},{6,7},{7,6},{8,9},{9,8},{10,11... | collective-permute-start | bytes 884744 | tf_op jit(solution)/shard_map/ppermute | solution.py:474
  716.7 22.0 %collective-permute-start.69 = (bf16[96,1536]{1,0:T(8,128)(2,1)S(1)}, bf16[96,1536]{1,0:T(8,128)(2,1)S(1)}, u32[]{:S(2)}, u32[]{:S(2)}) collective-permute-start(bf16[96,1536]{1,0:T(8,128)(2,1)S(1)} %get-tuple-element.353), channel_id=1, source_target_pairs={{0,2},{1,3},{2,0},{3,1},{4,6},{5,7},{6,4},{7,5},{8,10},{9,11},{10,... | collective-permute-start | bytes 884744 | tf_op jit(solution)/shard_map/ppermute | solution.py:474
  723.0 31.5 %collective-permute-start.76 = (bf16[192,1536]{1,0:T(8,128)(2,1)S(1)}, bf16[192,1536]{1,0:T(8,128)(2,1)S(1)}, u32[]{:S(2)}, u32[]{:S(2)}) collective-permute-start(bf16[192,1536]{1,0:T(8,128)(2,1)S(1)} %add.295), channel_id=1, source_target_pairs={{0,16},{4,20},{8,24},{12,28},{16,0},{20,4},{24,8},{28,12},{1,17},{... | collective-permute-start | bytes 1769480 | tf_op jit(solution)/shard_map/ppermute | solution.py:470
  723.7 31.8 %collective-permute-start.75 = (bf16[2,192,640]{2,1,0:T(8,128)(2,1)S(1)}, bf16[2,192,640]{2,1,0:T(8,128)(2,1)S(1)}, u32[]{:S(2)}, u32[]{:S(2)}) collective-permute-start(bf16[2,192,640]{2,1,0:T(8,128)(2,1)S(1)} %pad_maximum_fusion.10), channel_id=1, source_target_pairs={{0,16},{4,20},{8,24},{12,28},{16,0},{20,4},{24,8},{28,12},{1,17},{... | collective-permute-start | bytes 1474568 | tf_op jit(solution)/shard_map/ppermute | solution.py:470
  (180 other events, 1678.0 us)

commit v10 on v9

--- a/solution.py
+++ b/solution.py
@@ -460,7 +460,7 @@
     "blend_sum": 0.3,
     "blend_stack": 0.3,
     "blend_four": 0.3,
-    "place_pair": 0.3,
+    "place_sum": 0.3,
     "place_shared": 0.3,
     "place_heads": 0.3,
 }
@@ -1335,49 +1335,38 @@
     )
 
 
-def place_pair_kernel(meta, *refs):
-    mine, other, out_ref = refs[-3:]
-    rows = out_ref.shape[1]
-
-    @pl.when(pl.program_id(0) == 0)
-    def _():
-        out_ref[0] = mine[0, :rows].astype(jnp.float32)
-
-    @pl.when(pl.program_id(0) == 1)
-    def _():
-        out_ref[0] = other[0, :rows].astype(jnp.float32)
-
-
-def place_pair(meta, total, index, shape, mine, other):
-    _, rows, columns = mine.shape
-    arrays = [mine, other]
-    in_specs = [
-        pl.BlockSpec((1, rows, columns), lambda k, r, m: ((1 - k) * r + 3 * k, 0, 0)),
-        pl.BlockSpec((1, rows, columns), lambda k, r, m: (k * r, 0, 0)),
-    ]
+def place_sum_kernel(meta, *refs):
+    rows = refs[-1].shape[1]
+    refs[-1][0] = refs[-2][0, :rows].astype(jnp.float32)
+
+
+def place_sum(meta, total, index, of_other, shape, value):
+    _, rows, columns = value.shape
+    arrays = [value]
+    in_specs = [pl.BlockSpec((1, rows, columns), lambda r, m: (r, 0, 0))]
     aliases = {}
     if total is not None:
         arrays = [total] + arrays
         in_specs = [pl.BlockSpec(memory_space=pl.ANY)] + in_specs
         aliases = {1: 0}
     return pl.pallas_call(
-        place_pair_kernel,
+        place_sum_kernel,
         grid_spec=pltpu.PrefetchScalarGridSpec(
             num_scalar_prefetch=1,
-            grid=(2, 4),
+            grid=(4,),
             in_specs=in_specs,
             out_specs=pl.BlockSpec(
                 (1, shape[1] // 4, shape[2]),
-                lambda k, r, m: (2 * ((m[0] & 1) ^ k) + index, (m[0] >> 1) ^ r, 0),
+                lambda r, m: (2 * ((m[0] & 1) ^ of_other) + index, (m[0] >> 1) ^ r, 0),
             ),
         ),
         out_shape=shape_of(shape, jnp.float32),
         input_output_aliases=aliases,
         compiler_params=pltpu.CompilerParams(vmem_limit_bytes=48 * 1024 * 1024),
         cost_estimate=pl.CostEstimate(
-            flops=int(COSTS.get("place_pair", 1.0) * 1e9), bytes_accessed=1000, transcendentals=0
+            flops=int(COSTS.get("place_sum", 1.0) * 1e9), bytes_accessed=1000, transcendentals=0
         ),
-        name="place_pair",
+        name="place_sum",
     )(meta, *arrays)
 
 
@@ -1497,9 +1486,9 @@
     "M", "K", "R", "M", "K", "M", "M", "M", "M", "R", "M", "M",
 )
 LATE = (
-    "L", "0", "1", "0", "L", "0", "1", "1", "L", "L", "O", "0", "1", "L", "0", "L", "1", "O", "Q", "O", "0", "1", "L", "Q",
-    "O", "L", "Q", "Q", "O", "Q", "L", "1", "0", "O", "Q", "S", "L", "O", "Q", "1", "S", "L", "0", "O", "Q", "L", "Q", "O",
-    "S",
+    "L", "0", "1", "0", "0", "L", "1", "1", "L", "L", "O", "0", "1", "L", "0", "L", "1", "O", "Q", "1", "O", "0", "L", "Q",
+    "O", "L", "Q", "Q", "O", "Q", "L", "1", "0", "O", "Q", "S", "1", "0", "L", "O", "Q", "1", "S", "L", "0", "O", "Q", "L",
+    "Q", "O", "S",
 )
 
 
@@ -1899,11 +1888,12 @@
         if index == 0:
             have["shared_sum"] = stacked[:, shard_rows:]
         yield
-        have["grad_experts"] = place_pair(
-            meta(), have.get("grad_experts"), index, expert_weight.shape, stacked, other
-        )
-        clock.mark(have["grad_experts"])
-        yield
+        for of_other, value in ((0, stacked), (1, other)):
+            have["grad_experts"] = place_sum(
+                meta(), have.get("grad_experts"), index, of_other, expert_weight.shape, value
+            )
+            clock.mark(have["grad_experts"])
+            yield
 
     def shared_grad_chain():
         total = now(have["shared_sum"])

time: 789 us -> 791 us (level)
    pallas_call x2 -> x4, Pallas kernels: 23.9 us -> 25.8 us  [place_sum(): pl.pallas_call(place_sum_kernel, grid_spec=pltpu.PrefetchScalarGridSpec(n...]
    unnamed x291 -> x293, local copies, waits for them, and re-layouts: 55.9 us -> 55.6 us
  transfers between devices with their start and end apart: 85 -> 85, of which waited for: 34 -> 31; matrix products, arithmetic and copies ran while one was open for 8% -> 8% of each run, Pallas kernels for 34% -> 34%
where the time goes in v10:
time: 791 us; the launch traced here: 783 us
  Pallas kernels  307 us (39%)
  waiting for transfers between devices  198 us (25%)
  starting transfers between devices  147 us (19%)
  local copies, waits for them, and re-layouts  75.6 us (10%)
  other arithmetic  49.8 us (6%)
    pallas_call x33, Pallas kernels, call(): pl.pallas_call(kernel, grid_spec=pltpu.PrefetchScalarGridSpec(num_scalar_...  281 us
    ppermute x17, waiting for transfers between devices, line_swap(): lax.ppermute(value, 'wt', [(index, index ^ offset) for index in range(4)])  69 us
    unnamed x293, local copies, waits for them, and re-layouts  55.6 us
    ppermute x40, waiting for transfers between devices, flip(): lax.ppermute(value, 'ctx', [(index, index ^ bit) for index in range(8)])  52.5 us
    ppermute x17, starting transfers between devices, line_swap(): lax.ppermute(value, 'wt', [(index, index ^ offset) for index in range(4)])  47.4 us
    ppermute x8, starting transfers between devices, line_inward(): return lax.ppermute(value, 'wt', [(0, 1), (3, 2)])  33.6 us
    ppermute x8, waiting for transfers between devices, line_inward(): return lax.ppermute(value, 'wt', [(0, 1), (3, 2)])  32.6 us
    ppermute x40, starting transfers between devices, flip(): lax.ppermute(value, 'ctx', [(index, index ^ bit) for index in range(8)])  28.3 us
  transfers between devices with their start and end apart: 85, of which 31 were waited for; matrix products, arithmetic and copies ran while one was open for 8% of the time, Pallas kernels for 34%

profile of v10, /device:TPU:0, one launch (start us, length us, event | category | flops | bytes accessed | tf_op | source)
XLA Modules:
  0.0 782.9 jit_solution(17571232017761098006)
XLA Ops:
  27.0 22.9 %collective-permute-done.5 = bf16[2,192,640]{2,1,0:T(8,128)(2,1)S(1)} collective-permute-done((bf16[2,192,640]{2,1,0:T(8,128)(2,1)S(1)}, bf16[2,192,640]{2,1,0:T(8,128)(2,1)S(1)}, u32[]{:S(2)}, u32[]{:S(2)}) %collective-permute-start.5) | collective-permute-done | bytes 491552 | tf_op jit(solution)/shard_map/ppermute | solution.py:474
  61.7 6.9 collective-permute-done.6
  71.7 6.8 project.1
  84.2 11.5 %attend.1 = (bf16[4,256,384]{2,1,0:T(8,128)(2,1)S(1)}, f32[8,1,384]{2,1,0:T(1,128)S(1)}) custom-call(s32[2]{0:T(128)S(1)} %pad_add_fusion.meta.meta_ref, bf16[4,256,384]{2,1,0:T(8,128)(2,1)S(1)} %copy-done.47, bf16[4,256,256]{2,1,0:T(8,128)(2,1)} %get-tuple-element.200.mine_ref, bf16[4,256,256]{2,1,0:T(8,128)(2,1)S(1)} %collective-permute-done.9.other_ref), custom_call_target="tpu_custom_call" | custom-call | flops 300000000 | bytes 1000 | tf_op jit(solution)/shard_map/attend/pallas_call | solution.py:585
  99.1 12.0 %all-to-all-done.refs_4_ = bf16[4,192,1536]{2,1,0:T(8,128)(2,1)} async-done(((bf16[4,192,1536]{2,1,0:T(8,128)(2,1)}), bf16[4,192,1536]{2,1,0:T(8,128)(2,1)}, u32[]{:S(2)}, u32[]{:S(2)}) %all-to-all-start) | async-done | bytes 2359328 | tf_op jit(solution)/shard_map/all_to_all | solution.py:527
  119.7 5.0 collective-permute-done.11.refs_2_
  126.2 6.2 leave.1
  141.6 11.7 %experts.4 = (bf16[4,256,1024]{2,1,0:T(8,128)(2,1)S(1)}, bf16[256,512]{1,0:T(8,128)(2,1)S(1)}, bf16[256,1536]{1,0:T(8,128)(2,1)S(1)}) custom-call(s32[2]{0:T(128)S(1)} %pad_add_fusion.meta.meta_ref, bf16[256,1536]{1,0:T(8,128)(2,1)S(1)} %get-tuple-element.213.rows_ref.refs_0_, f32[4,256,1]{2,1,0:T(8,128)S(1)} %copy-done.40, ...), custom_call_target="tpu_custom_call" | custom-call | flops 300000000 | bytes 1000 | tf_op jit(solution)/shard_map/experts/pallas_call | solution.py:585
  162.3 12.0 %experts.5 = (bf16[4,256,1024]{2,1,0:T(8,128)(2,1)S(1)}, bf16[256,512]{1,0:T(8,128)(2,1)S(1)}, bf16[256,1536]{1,0:T(8,128)(2,1)S(1)}) custom-call(s32[2]{0:T(128)S(1)} %pad_add_fusion.meta.meta_ref, bf16[256,1536]{1,0:T(8,128)(2,1)} %collective-permute-done.15.rows_ref.refs_1_, f32[4,256,1]{2,1,0:T(8,128)S(1)} %copy.42.gates_ref, ...), custom_call_target="tpu_custom_call" | custom-call | flops 300000000 | bytes 1000 | tf_op jit(solution)/shard_map/experts/pallas_call | solution.py:585
  185.5 11.7 %experts.6 = (bf16[4,256,1024]{2,1,0:T(8,128)(2,1)S(1)}, bf16[256,512]{1,0:T(8,128)(2,1)S(1)}, bf16[256,1536]{1,0:T(8,128)(2,1)S(1)}) custom-call(s32[2]{0:T(128)S(1)} %pad_add_fusion.meta.meta_ref, bf16[256,1536]{1,0:T(8,128)(2,1)S(1)} %broadcast_select_fusion.3.rows_ref.refs_2_, f32[4,256,1]{2,1,0:T(8,128)S(1)} %copy-done.38, ...), custom_call_target="tpu_custom_call" | custom-call | flops 300000000 | bytes 1000 | tf_op jit(solution)/shard_map/experts/pallas_call | solution.py:585
  200.4 11.7 %experts.7 = (bf16[4,256,1024]{2,1,0:T(8,128)(2,1)S(1)}, bf16[256,512]{1,0:T(8,128)(2,1)S(1)}, bf16[256,1536]{1,0:T(8,128)(2,1)S(1)}) custom-call(s32[2]{0:T(128)S(1)} %pad_add_fusion.meta.meta_ref, bf16[256,1536]{1,0:T(8,128)(2,1)S(1)} %broadcast_select_fusion.2.rows_ref.refs_3_, f32[4,256,1]{2,1,0:T(8,128)S(1)} %copy-done.36, ...), custom_call_target="tpu_custom_call" | custom-call | flops 300000000 | bytes 1000 | tf_op jit(solution)/shard_map/experts/pallas_call | solution.py:585
  212.2 4.9 collective-permute-start.21
  221.1 13.5 %collective-permute-done.21 = bf16[256,1536]{1,0:T(8,128)(2,1)S(1)} collective-permute-done((bf16[256,1536]{1,0:T(8,128)(2,1)S(1)}, bf16[256,1536]{1,0:T(8,128)(2,1)S(1)}, u32[]{:S(2)}, u32[]{:S(2)}) %collective-permute-start.21) | collective-permute-done | bytes 786464 | tf_op jit(solution)/shard_map/ppermute | solution.py:486
  243.6 12.2 %collective-permute-done.24 = bf16[256,1536]{1,0:T(8,128)(2,1)S(1)} collective-permute-done((bf16[256,1536]{1,0:T(8,128)(2,1)S(1)}, bf16[256,1536]{1,0:T(8,128)(2,1)S(1)}, u32[]{:S(2)}, u32[]{:S(2)}) %collective-permute-start.24) | collective-permute-done | bytes 786464 | tf_op jit(solution)/shard_map/ppermute | solution.py:486
  262.6 13.9 %collective-permute-done.27 = bf16[256,1536]{1,0:T(8,128)(2,1)S(1)} collective-permute-done((bf16[256,1536]{1,0:T(8,128)(2,1)S(1)}, bf16[256,1536]{1,0:T(8,128)(2,1)S(1)}, u32[]{:S(2)}, u32[]{:S(2)}) %collective-permute-start.27) | collective-permute-done | bytes 786464 | tf_op jit(solution)/shard_map/ppermute | solution.py:474
  284.1 13.0 %experts_back.4 = (bf16[4,256,1024]{2,1,0:T(8,128)(2,1)S(1)}, bf16[4,256,512]{2,1,0:T(8,128)(2,1)S(1)}, bf16[1,256,512]{2,1,0:T(8,128)(2,1)S(1)}, bf16[1,256,256]{2,1,0:T(8,128)(2,1)S(1)}, bf16[256,1536]{1,0:T(8,128)(2,1)S(1)}) custom-call(s32[2]{0:T(128)S(1)} %pad_add_fusion.meta.meta_ref, bf16[256,1536]{1,0:T(8,128)(2,1)S(1)} %get-tuple-element.379.grad_ref.refs_4_, ...), custom_call_target="tpu_custom_call" | custom-call | flops 300000000 | bytes 1000 | tf_op jit(solution)/shard_map/experts_back/pallas_call | solution.py:585
  303.2 13.0 %experts_back.5 = (bf16[4,256,1024]{2,1,0:T(8,128)(2,1)S(1)}, bf16[4,256,512]{2,1,0:T(8,128)(2,1)S(1)}, bf16[1,256,512]{2,1,0:T(8,128)(2,1)S(1)}, bf16[1,256,256]{2,1,0:T(8,128)(2,1)S(1)}, bf16[256,1536]{1,0:T(8,128)(2,1)S(1)}) custom-call(s32[2]{0:T(128)S(1)} %pad_add_fusion.meta.meta_ref, bf16[256,1536]{1,0:T(8,128)(2,1)S(1)} %collective-permute-done.29.grad_ref.refs_5_, ...), custom_call_target="tpu_custom_call" | custom-call | flops 300000000 | bytes 1000 | tf_op jit(solution)/shard_map/experts_back/pallas_call | solution.py:585
  326.7 13.0 %experts_back.6 = (bf16[4,256,1024]{2,1,0:T(8,128)(2,1)S(1)}, bf16[4,256,512]{2,1,0:T(8,128)(2,1)S(1)}, bf16[1,256,512]{2,1,0:T(8,128)(2,1)S(1)}, bf16[1,256,256]{2,1,0:T(8,128)(2,1)S(1)}, bf16[256,1536]{1,0:T(8,128)(2,1)S(1)}) custom-call(s32[2]{0:T(128)S(1)} %pad_add_fusion.meta.meta_ref, bf16[256,1536]{1,0:T(8,128)(2,1)S(1)} %broadcast_select_fusion.1.grad_ref.refs_6_, ...), custom_call_target="tpu_custom_call" | custom-call | flops 300000000 | bytes 1000 | tf_op jit(solution)/shard_map/experts_back/pallas_call | solution.py:585
  343.5 14.4 %experts_back.7 = (bf16[4,256,1024]{2,1,0:T(8,128)(2,1)S(1)}, bf16[4,256,512]{2,1,0:T(8,128)(2,1)S(1)}, bf16[1,256,512]{2,1,0:T(8,128)(2,1)S(1)}, bf16[1,256,256]{2,1,0:T(8,128)(2,1)S(1)}, bf16[256,1536]{1,0:T(8,128)(2,1)}) custom-call(s32[2]{0:T(128)S(1)} %pad_add_fusion.meta.meta_ref, bf16[256,1536]{1,0:T(8,128)(2,1)S(1)} %broadcast_select_fusion.grad_ref.refs_7_, ...), custom_call_target="tpu_custom_call" | custom-call | flops 300000000 | bytes 1000 | tf_op jit(solution)/shard_map/experts_back/pallas_call | solution.py:585
  360.4 13.0 %expert_grad.4 = bf16[4,480,1536]{2,1,0:T(8,128)(2,1)} custom-call(s32[3]{0:T(128)S(1)} %add_add_fusion.meta, bf16[256,1536]{1,0:T(8,128)(2,1)S(1)} %copy-done.20, bf16[256,1536]{1,0:T(8,128)(2,1)} %collective-permute-done.15.rows_ref.refs_1_, bf16[256,1536]{1,0:T(8,128)(2,1)S(1)} %broadcast_select_fusion.3.rows_ref.refs_2_, ...), custom_call_target="tpu_custom_call" | custom-call | flops 300000000 | bytes 1000 | tf_op jit(solution)/shard_map/expert_grad/pallas_call | solution.py:585
  375.9 10.1 %expert_grad.5 = bf16[4,384,1536]{2,1,0:T(8,128)(2,1)} custom-call(s32[3]{0:T(128)S(1)} %add_add_fusion.1.meta, bf16[256,1536]{1,0:T(8,128)(2,1)S(1)} %copy-done.21, bf16[256,1536]{1,0:T(8,128)(2,1)} %collective-permute-done.15.rows_ref.refs_1_, bf16[256,1536]{1,0:T(8,128)(2,1)S(1)} %broadcast_select_fusion.3.rows_ref.refs_2_, ...), custom_call_target="tpu_custom_call" | custom-call | flops 300000000 | bytes 1000 | tf_op jit(solution)/shard_map/expert_grad/pallas_call | solution.py:585
  386.5 5.3 collective-permute-start.35
  400.5 12.9 %expert_grad.6.refs_0_ = bf16[4,480,1536]{2,1,0:T(8,128)(2,1)} custom-call(s32[3]{0:T(128)S(1)} %add_add_fusion.2.meta, bf16[256,1536]{1,0:T(8,128)(2,1)S(1)} %copy-done.21, bf16[256,1536]{1,0:T(8,128)(2,1)} %collective-permute-done.15.rows_ref.refs_1_, bf16[256,1536]{1,0:T(8,128)(2,1)S(1)} %broadcast_select_fusion.3.rows_ref.refs_2_, ...), custom_call_target="tpu_custom_call" | custom-call | flops 300000000 | bytes 1000 | tf_op jit(solution)/shard_map/expert_grad/pallas_call | solution.py:585
  413.5 7.8 blend_split.2
  432.3 10.1 %expert_grad.7.refs_0_ = bf16[4,384,1536]{2,1,0:T(8,128)(2,1)} custom-call(s32[3]{0:T(128)S(1)} %add_add_fusion.3.meta, bf16[256,1536]{1,0:T(8,128)(2,1)S(1)} %copy-done.22, bf16[256,1536]{1,0:T(8,128)(2,1)} %collective-permute-done.15.rows_ref.refs_1_, bf16[256,1536]{1,0:T(8,128)(2,1)S(1)} %broadcast_select_fusion.3.rows_ref.refs_2_, ...), custom_call_target="tpu_custom_call" | custom-call | flops 300000000 | bytes 1000 | tf_op jit(solution)/shard_map/expert_grad/pallas_call | solution.py:585
  442.4 6.1 blend_split.3
  456.3 16.3 %collective-permute-done.40 = bf16[256,1536]{1,0:T(8,128)(2,1)} collective-permute-done((bf16[256,1536]{1,0:T(8,128)(2,1)}, bf16[256,1536]{1,0:T(8,128)(2,1)}, u32[]{:S(2)}, u32[]{:S(2)}) %collective-permute-start.40) | collective-permute-done | bytes 786464 | tf_op jit(solution)/shard_map/ppermute | solution.py:474
  475.4 7.4 enter_back.1
  490.2 5.1 blend_pair.2
  501.9 11.6 %collective-permute-done.44.refs_1_ = bf16[2,384,1536]{2,1,0:T(8,128)(2,1)} collective-permute-done((bf16[2,384,1536]{2,1,0:T(8,128)(2,1)}, bf16[2,384,1536]{2,1,0:T(8,128)(2,1)}, u32[]{:S(2)}, u32[]{:S(2)}) %collective-permute-start.44) | collective-permute-done | bytes 2359328 | tf_op jit(solution)/shard_map/ppermute | solution.py:470
  522.0 25.9 %all-to-all-done.2.refs_1_ = bf16[4,256,384]{2,1,0:T(8,128)(2,1)} async-done(((bf16[4,256,384]{2,1,0:T(8,128)(2,1)}), bf16[4,256,384]{2,1,0:T(8,128)(2,1)}, u32[]{:S(2)}, u32[]{:S(2)}) %all-to-all-start.2) | async-done | bytes 786464 | tf_op jit(solution)/shard_map/all_to_all | solution.py:516
  550.1 15.6 %attend_back.1 = (bf16[4,256,384]{2,1,0:T(8,128)(2,1)S(1)}, f32[4,256,256]{2,1,0:T(8,128)S(1)}, bf16[4,256,256]{2,1,0:T(8,128)(2,1)S(1)}) custom-call(s32[2]{0:T(128)S(1)} %pad_add_fusion.meta.meta_ref, bf16[4,256,384]{2,1,0:T(8,128)(2,1)S(1)} %copy-done.48, bf16[4,256,256]{2,1,0:T(8,128)(2,1)} %get-tuple-element.200.mine_ref, ...), custom_call_target="tpu_custom_call" | custom-call | flops 300000000 | bytes 1000 | tf_op jit(solution)/shard_map/attend_back/pallas_call | solution.py:585
  567.2 4.8 blend_sum.2.refs_0_
  580.3 5.5 collective-permute-start.48
  590.3 6.3 weight_grad.3
  598.3 6.8 collective-permute-done.49.refs_1_
  610.8 4.9 collective-permute-start.53
  620.7 5.4 blend_stack.3.refs_0_
  628.7 9.0 %finish.1 = (f32[1,256,1536]{2,1,0:T(8,128)}, f32[1,1536]{1,0:T(1,128)S(1)}) custom-call(s32[2]{0:T(128)S(1)} %pad_add_fusion.meta.meta_ref, bf16[4,256,640]{2,1,0:T(8,128)(2,1)} %all-to-all-done.3.refs_0_, bf16[4,768,640]{2,1,0:T(8,128)(2,1)} %pad_maximum_fusion.refs_1_, bf16[4,768,640]{2,1,0:T(8,128)(2,1)} %collective-permute-done.51.refs_2_, ...), custom_call_target="tpu_custom_call" | custom-call | flops 300000000 | bytes 1000 | tf_op jit(solution)/shard_map/finish/pallas_call | solution.py:585
  653.7 5.6 collective-permute-done.58
  660.0 16.2 %collective-permute-start.56 = (f32[8,1536]{1,0:T(8,128)S(1)}, f32[8,1536]{1,0:T(8,128)S(1)}, u32[]{:S(2)}, u32[]{:S(2)}) collective-permute-start(f32[8,1536]{1,0:T(8,128)S(1)} %fusion.12), channel_id=1, source_target_pairs={{0,2},{1,3},{2,0},{3,1},{4,6},{5,7},{6,4},{7,5},{8,10},{9,11},{10,... | collective-permute-start | bytes 147464 | tf_op jit(solution)/shard_map/ppermute | solution.py:474
  684.7 5.5 blend_four.2.refs_0_
  690.5 7.5 blend_four.3.refs_1_
  708.2 7.0 place_sum.4.refs_0_
  730.3 7.0 place_sum.6.refs_0_
  737.3 8.0 %collective-permute-done.69 = bf16[96,1536]{1,0:T(8,128)(2,1)S(1)} collective-permute-done((bf16[96,1536]{1,0:T(8,128)(2,1)S(1)}, bf16[96,1536]{1,0:T(8,128)(2,1)S(1)}, u32[]{:S(2)}, u32[]{:S(2)}) %collective-permute-start.69) | collective-permute-done | bytes 294944 | tf_op jit(solution)/shard_map/ppermute | solution.py:474
  749.4 7.2 place_sum.7
  773.3 8.2 %place_shared.1 = f32[384,3072]{1,0:T(8,128)} custom-call(s32[2]{0:T(128)S(1)} %pad_add_fusion.meta.meta_ref, bf16[4,96,1536]{2,1,0:T(8,128)(2,1)S(1)} %pad_maximum_fusion.4.mine_low.mine_high, bf16[4,96,1536]{2,1,0:T(8,128)(2,1)S(1)} %pad_maximum_fusion.4.mine_low.mine_high, bf16[4,96,1536]{2,1,0:T(8,128)(2,1)} %collective-permute-done.80.other_low.other_high, ...), custom_call_target="tpu_custom_call" | custom-call | flops 300000000 | bytes 1000 | tf_op jit(solution)/shard_map/place_shared/pallas_call | solution.py:585
  (562 shorter events, 298.0 us)
Async XLA Ops:
  9.8 42.7 %all-to-all-start.1 = ((bf16[4,256,1536]{2,1,0:T(8,128)(2,1)}), bf16[4,256,1536]{2,1,0:T(8,128)(2,1)}, u32[]{:S(2)}, u32[]{:S(2)}) async-start(bf16[4,256,1536]{2,1,0:T(8,128)(2,1)} %broadcast_in_dim.55), calls=%async_computation.1 | async-start | bytes 6291456 | tf_op jit(solution)/shard_map/all_to_all | solution.py:516
  20.4 29.5 %collective-permute-start.5 = (bf16[2,192,640]{2,1,0:T(8,128)(2,1)S(1)}, bf16[2,192,640]{2,1,0:T(8,128)(2,1)S(1)}, u32[]{:S(2)}, u32[]{:S(2)}) collective-permute-start(bf16[2,192,640]{2,1,0:T(8,128)(2,1)S(1)} %pad_maximum_fusion.9), channel_id=1, source_target_pairs={{0,2},{1,3},{2,0},{3,1},{4,6},{5,7},{6,4},{7,5},{8,10},{9,11},{10,... | collective-permute-start | bytes 1474568 | tf_op jit(solution)/shard_map/ppermute | solution.py:474
  23.1 28.0 %collective-permute-start.4 = (f32[2,32,256]{2,1,0:T(8,128)S(1)}, f32[2,32,256]{2,1,0:T(8,128)S(1)}, u32[]{:S(2)}, u32[]{:S(2)}) collective-permute-start(f32[2,32,256]{2,1,0:T(8,128)S(1)} %pad_maximum_fusion.16), channel_id=1, source_target_pairs={{0,2},{1,3},{2,0},{3,1},{4,6},{5,7},{6,4},{7,5},{8,10},{9,11},{10,... | collective-permute-start | bytes 196616 | tf_op jit(solution)/shard_map/ppermute | solution.py:474
  24.7 27.7 %collective-permute-start.3 = (bf16[2,48,768]{2,1,0:T(8,128)(2,1)S(1)}, bf16[2,48,768]{2,1,0:T(8,128)(2,1)S(1)}, u32[]{:S(2)}, u32[]{:S(2)}) collective-permute-start(bf16[2,48,768]{2,1,0:T(8,128)(2,1)S(1)} %pad_maximum_fusion.14), channel_id=1, source_target_pairs={{0,2},{1,3},{2,0},{3,1},{4,6},{5,7},{6,4},{7,5},{8,10},{9,11},{10,... | collective-permute-start | bytes 442376 | tf_op jit(solution)/shard_map/ppermute | solution.py:474
  54.1 57.0 %all-to-all-start = ((bf16[4,192,1536]{2,1,0:T(8,128)(2,1)}), bf16[4,192,1536]{2,1,0:T(8,128)(2,1)}, u32[]{:S(2)}, u32[]{:S(2)}) async-start(bf16[4,192,1536]{2,1,0:T(8,128)(2,1)} %broadcast_in_dim.54), calls=%async_computation | async-start | bytes 4718592 | tf_op jit(solution)/shard_map/all_to_all | solution.py:527
  111.1 26.1 %collective-permute-start.14 = (bf16[4,4,48,768]{3,2,1,0:T(8,128)(2,1)}, bf16[4,4,48,768]{3,2,1,0:T(8,128)(2,1)}, u32[]{:S(2)}, u32[]{:S(2)}) collective-permute-start(bf16[4,4,48,768]{3,2,1,0:T(8,128)(2,1)} %pad_maximum_fusion.3.mine), channel_id=1, source_target_pairs={{0,4},{4,0},{8,12},{12,8},{16,20},{20,16},{24,28},{28,24},{1,5},{5... | collective-permute-start | bytes 3538952 | tf_op jit(solution)/shard_map/ppermute | solution.py:470
  133.5 22.1 %collective-permute-start.15 = (bf16[256,1536]{1,0:T(8,128)(2,1)S(1)}, bf16[256,1536]{1,0:T(8,128)(2,1)}, u32[]{:S(2)}, u32[]{:S(2)}) collective-permute-start(bf16[256,1536]{1,0:T(8,128)(2,1)S(1)} %get-tuple-element.213.rows_ref.refs_0_), channel_id=1, source_target_pairs={{0,1},{1,0},{2,3},{3,2},{4,5},{5,4},{6,7},{7,6},{8,9},{9,8},{10,11... | collective-permute-start | bytes 2359304 | tf_op jit(solution)/shard_map/ppermute | solution.py:474
  133.6 22.1 %collective-permute-start.16 = (bf16[256,1536]{1,0:T(8,128)(2,1)S(1)}, bf16[256,1536]{1,0:T(8,128)(2,1)}, u32[]{:S(2)}, u32[]{:S(2)}) collective-permute-start(bf16[256,1536]{1,0:T(8,128)(2,1)S(1)} %get-tuple-element.213.rows_ref.refs_0_), channel_id=1, source_target_pairs={{1,2},{2,1},{5,6},{6,5},{9,10},{10,9},{13,14},{14,13},{17,18},{18,... | collective-permute-start | bytes 2359304 | tf_op jit(solution)/shard_map/ppermute | solution.py:478
  157.2 22.2 %collective-permute-start.18 = (bf16[256,1536]{1,0:T(8,128)(2,1)}, bf16[256,1536]{1,0:T(8,128)(2,1)}, u32[]{:S(2)}, u32[]{:S(2)}) collective-permute-start(bf16[256,1536]{1,0:T(8,128)(2,1)} %collective-permute-done.16), channel_id=1, source_target_pairs={{1,0},{2,3},{5,4},{6,7},{9,8},{10,11},{13,12},{14,15},{17,16},{18,... | collective-permute-start | bytes 2359304 | tf_op jit(solution)/shard_map/ppermute | solution.py:482
  182.0 38.8 %collective-permute-start.22 = (bf16[768,640]{1,0:T(8,128)(2,1)S(1)}, bf16[768,640]{1,0:T(8,128)(2,1)S(1)}, u32[]{:S(2)}, u32[]{:S(2)}) collective-permute-start(bf16[768,640]{1,0:T(8,128)(2,1)S(1)} %constant_dynamic-slice_fusion.1), channel_id=1, source_target_pairs={{0,8},{4,12},{8,0},{12,4},{16,24},{20,28},{24,16},{28,20},{1,9},{5... | collective-permute-start | bytes 2949128 | tf_op jit(solution)/shard_map/ppermute | solution.py:470
  212.2 22.3 %collective-permute-start.21 = (bf16[256,1536]{1,0:T(8,128)(2,1)S(1)}, bf16[256,1536]{1,0:T(8,128)(2,1)S(1)}, u32[]{:S(2)}, u32[]{:S(2)}) collective-permute-start(bf16[256,1536]{1,0:T(8,128)(2,1)S(1)} %get-tuple-element.229), channel_id=1, source_target_pairs={{0,1},{3,2},{4,5},{7,6},{8,9},{11,10},{12,13},{15,14},{16,17},{19,... | collective-permute-start | bytes 2359304 | tf_op jit(solution)/shard_map/ppermute | solution.py:486
  234.7 21.1 %collective-permute-start.24 = (bf16[256,1536]{1,0:T(8,128)(2,1)S(1)}, bf16[256,1536]{1,0:T(8,128)(2,1)S(1)}, u32[]{:S(2)}, u32[]{:S(2)}) collective-permute-start(bf16[256,1536]{1,0:T(8,128)(2,1)S(1)} %add.250), channel_id=1, source_target_pairs={{0,1},{3,2},{4,5},{7,6},{8,9},{11,10},{12,13},{15,14},{16,17},{19,... | collective-permute-start | bytes 2359304 | tf_op jit(solution)/shard_map/ppermute | solution.py:486
  256.2 20.4 %collective-permute-start.27 = (bf16[256,1536]{1,0:T(8,128)(2,1)S(1)}, bf16[256,1536]{1,0:T(8,128)(2,1)S(1)}, u32[]{:S(2)}, u32[]{:S(2)}) collective-permute-start(bf16[256,1536]{1,0:T(8,128)(2,1)S(1)} %add.252), channel_id=1, source_target_pairs={{0,1},{1,0},{2,3},{3,2},{4,5},{5,4},{6,7},{7,6},{8,9},{9,8},{10,11... | collective-permute-start | bytes 2359304 | tf_op jit(solution)/shard_map/ppermute | solution.py:474
  260.7 55.6 %collective-permute-start.33 = (bf16[2,768,640]{2,1,0:T(8,128)(2,1)S(1)}, bf16[2,768,640]{2,1,0:T(8,128)(2,1)}, u32[]{:S(2)}, u32[]{:S(2)}) collective-permute-start(bf16[2,768,640]{2,1,0:T(8,128)(2,1)S(1)} %pad_maximum_fusion.1), channel_id=1, source_target_pairs={{0,16},{4,20},{8,24},{12,28},{16,0},{20,4},{24,8},{28,12},{1,17},{... | collective-permute-start | bytes 5898248 | tf_op jit(solution)/shard_map/ppermute | solution.py:470
  279.6 20.8 %collective-permute-start.29 = (bf16[256,1536]{1,0:T(8,128)(2,1)S(1)}, bf16[256,1536]{1,0:T(8,128)(2,1)S(1)}, u32[]{:S(2)}, u32[]{:S(2)}) collective-permute-start(bf16[256,1536]{1,0:T(8,128)(2,1)S(1)} %get-tuple-element.379.grad_ref.refs_4_), channel_id=1, source_target_pairs={{0,1},{1,0},{2,3},{3,2},{4,5},{5,4},{6,7},{7,6},{8,9},{9,8},{10,11... | collective-permute-start | bytes 2359304 | tf_op jit(solution)/shard_map/ppermute | solution.py:474
  300.4 20.5 %collective-permute-start.31 = (bf16[256,1536]{1,0:T(8,128)(2,1)S(1)}, bf16[256,1536]{1,0:T(8,128)(2,1)}, u32[]{:S(2)}, u32[]{:S(2)}) collective-permute-start(bf16[256,1536]{1,0:T(8,128)(2,1)S(1)} %collective-permute-done.29.grad_ref.refs_5_), channel_id=1, source_target_pairs={{1,2},{2,1},{5,6},{6,5},{9,10},{10,9},{13,14},{14,13},{17,18},{18,... | collective-permute-start | bytes 2359304 | tf_op jit(solution)/shard_map/ppermute | solution.py:478
  373.4 40.0 %collective-permute-start.36 = (bf16[4,480,1536]{2,1,0:T(8,128)(2,1)}, bf16[4,480,1536]{2,1,0:T(8,128)(2,1)}, u32[]{:S(2)}, u32[]{:S(2)}) collective-permute-start(bf16[4,480,1536]{2,1,0:T(8,128)(2,1)} %expert_grad.4), channel_id=1, source_target_pairs={{0,4},{4,0},{8,12},{12,8},{16,20},{20,16},{24,28},{28,24},{1,5},{5... | collective-permute-start | bytes 17694728 | tf_op jit(solution)/shard_map/ppermute | solution.py:470
  386.0 56.3 %collective-permute-start.39 = (bf16[4,384,1536]{2,1,0:T(8,128)(2,1)}, bf16[4,384,1536]{2,1,0:T(8,128)(2,1)}, u32[]{:S(2)}, u32[]{:S(2)}) collective-permute-start(bf16[4,384,1536]{2,1,0:T(8,128)(2,1)} %expert_grad.5), channel_id=1, source_target_pairs={{0,4},{4,0},{8,12},{12,8},{16,20},{20,16},{24,28},{28,24},{1,5},{5... | collective-permute-start | bytes 14155784 | tf_op jit(solution)/shard_map/ppermute | solution.py:470
  386.5 37.0 %collective-permute-start.35 = (bf16[256,1536]{1,0:T(8,128)(2,1)}, bf16[256,1536]{1,0:T(8,128)(2,1)}, u32[]{:S(2)}, u32[]{:S(2)}) collective-permute-start(bf16[256,1536]{1,0:T(8,128)(2,1)} %get-tuple-element.263), channel_id=1, source_target_pairs={{0,1},{3,2},{4,5},{7,6},{8,9},{11,10},{12,13},{15,14},{16,17},{19,... | collective-permute-start | bytes 2359304 | tf_op jit(solution)/shard_map/ppermute | solution.py:486
  422.9 67.2 %collective-permute-start.43 = (bf16[2,480,1536]{2,1,0:T(8,128)(2,1)}, bf16[2,480,1536]{2,1,0:T(8,128)(2,1)}, u32[]{:S(2)}, u32[]{:S(2)}) collective-permute-start(bf16[2,480,1536]{2,1,0:T(8,128)(2,1)} %get-tuple-element.284), channel_id=1, source_target_pairs={{0,8},{4,12},{8,0},{12,4},{16,24},{20,28},{24,16},{28,20},{1,9},{5... | collective-permute-start | bytes 8847368 | tf_op jit(solution)/shard_map/ppermute | solution.py:470
  425.8 22.7 %collective-permute-start.37 = (bf16[256,1536]{1,0:T(8,128)(2,1)}, bf16[256,1536]{1,0:T(8,128)(2,1)}, u32[]{:S(2)}, u32[]{:S(2)}) collective-permute-start(bf16[256,1536]{1,0:T(8,128)(2,1)} %add.257), channel_id=1, source_target_pairs={{0,1},{3,2},{4,5},{7,6},{8,9},{11,10},{12,13},{15,14},{16,17},{19,... | collective-permute-start | bytes 2359304 | tf_op jit(solution)/shard_map/ppermute | solution.py:486
  427.9 20.5 %collective-permute-start.38 = (bf16[256,1536]{1,0:T(8,128)(2,1)}, bf16[256,1536]{1,0:T(8,128)(2,1)}, u32[]{:S(2)}, u32[]{:S(2)}) collective-permute-start(bf16[256,1536]{1,0:T(8,128)(2,1)} %add.257), channel_id=1, source_target_pairs={{1,2},{2,1},{5,6},{6,5},{9,10},{10,9},{13,14},{14,13},{17,18},{18,... | collective-permute-start | bytes 2359304 | tf_op jit(solution)/shard_map/ppermute | solution.py:478
  454.8 58.7 %collective-permute-start.44 = (bf16[2,384,1536]{2,1,0:T(8,128)(2,1)}, bf16[2,384,1536]{2,1,0:T(8,128)(2,1)}, u32[]{:S(2)}, u32[]{:S(2)}) collective-permute-start(bf16[2,384,1536]{2,1,0:T(8,128)(2,1)} %get-tuple-element.288), channel_id=1, source_target_pairs={{0,16},{4,20},{8,24},{12,28},{16,0},{20,4},{24,8},{28,12},{1,17},{... | collective-permute-start | bytes 7077896 | tf_op jit(solution)/shard_map/ppermute | solution.py:470
  489.6 88.5 %collective-permute-start.42 = (bf16[4,192,1536]{2,1,0:T(8,128)(2,1)}, bf16[4,192,1536]{2,1,0:T(8,128)(2,1)}, u32[]{:S(2)}, u32[]{:S(2)}) collective-permute-start(bf16[4,192,1536]{2,1,0:T(8,128)(2,1)} %get-tuple-element.302), channel_id=1, source_target_pairs={{0,4},{4,0},{8,12},{12,8},{16,20},{20,16},{24,28},{28,24},{1,5},{5... | collective-permute-start | bytes 7077896 | tf_op jit(solution)/shard_map/ppermute | solution.py:470
  489.7 136.4 %collective-permute-start.51 = (bf16[4,768,640]{2,1,0:T(8,128)(2,1)}, bf16[4,768,640]{2,1,0:T(8,128)(2,1)}, u32[]{:S(2)}, u32[]{:S(2)}) collective-permute-start(bf16[4,768,640]{2,1,0:T(8,128)(2,1)} %pad_maximum_fusion.refs_1_), channel_id=1, source_target_pairs={{0,4},{4,0},{8,12},{12,8},{16,20},{20,16},{24,28},{28,24},{1,5},{5... | collective-permute-start | bytes 11796488 | tf_op jit(solution)/shard_map/ppermute | solution.py:470
  496.5 69.3 %collective-permute-start.46 = (bf16[480,1536]{1,0:T(8,128)(2,1)}, bf16[480,1536]{1,0:T(8,128)(2,1)}, u32[]{:S(2)}, u32[]{:S(2)}) collective-permute-start(bf16[480,1536]{1,0:T(8,128)(2,1)} %get-tuple-element.305), channel_id=1, source_target_pairs={{0,16},{4,20},{8,24},{12,28},{16,0},{20,4},{24,8},{28,12},{1,17},{... | collective-permute-start | bytes 4423688 | tf_op jit(solution)/shard_map/ppermute | solution.py:470
  497.7 50.2 %all-to-all-start.2 = ((bf16[4,256,384]{2,1,0:T(8,128)(2,1)}), bf16[4,256,384]{2,1,0:T(8,128)(2,1)}, u32[]{:S(2)}, u32[]{:S(2)}) async-start(bf16[4,256,384]{2,1,0:T(8,128)(2,1)} %get-tuple-element.299), calls=%async_computation.2 | async-start | bytes 1572864 | tf_op jit(solution)/shard_map/all_to_all | solution.py:516
  520.5 52.8 %collective-permute-start.47 = (bf16[384,1536]{1,0:T(8,128)(2,1)}, bf16[384,1536]{1,0:T(8,128)(2,1)}, u32[]{:S(2)}, u32[]{:S(2)}) collective-permute-start(bf16[384,1536]{1,0:T(8,128)(2,1)} %get-tuple-element.308), channel_id=1, source_target_pairs={{0,8},{4,12},{8,0},{12,4},{16,24},{20,28},{24,16},{28,20},{1,9},{5... | collective-permute-start | bytes 3538952 | tf_op jit(solution)/shard_map/ppermute | solution.py:470
  576.1 28.9 %collective-permute-start.49 = (bf16[384,1536]{1,0:T(8,128)(2,1)S(1)}, bf16[384,1536]{1,0:T(8,128)(2,1)}, u32[]{:S(2)}, u32[]{:S(2)}) collective-permute-start(bf16[384,1536]{1,0:T(8,128)(2,1)S(1)} %blend_sum.3.refs_0_), channel_id=1, source_target_pairs={{0,8},{4,12},{8,0},{12,4},{16,24},{20,28},{24,16},{28,20},{1,9},{5... | collective-permute-start | bytes 3538952 | tf_op jit(solution)/shard_map/ppermute | solution.py:470
  577.5 42.5 %collective-permute-start.50 = (bf16[480,1536]{1,0:T(8,128)(2,1)}, bf16[480,1536]{1,0:T(8,128)(2,1)}, u32[]{:S(2)}, u32[]{:S(2)}) collective-permute-start(bf16[480,1536]{1,0:T(8,128)(2,1)} %blend_sum.2.refs_0_), channel_id=1, source_target_pairs={{0,16},{4,20},{8,24},{12,28},{16,0},{20,4},{24,8},{28,12},{1,17},{... | collective-permute-start | bytes 4423688 | tf_op jit(solution)/shard_map/ppermute | solution.py:470
  580.3 28.9 %collective-permute-start.48 = (bf16[192,1536]{1,0:T(8,128)(2,1)}, bf16[192,1536]{1,0:T(8,128)(2,1)}, u32[]{:S(2)}, u32[]{:S(2)}) collective-permute-start(bf16[192,1536]{1,0:T(8,128)(2,1)} %add_bitcast_fusion), channel_id=1, source_target_pairs={{0,1},{3,2},{4,5},{7,6},{8,9},{11,10},{12,13},{15,14},{16,17},{19,... | collective-permute-start | bytes 1769480 | tf_op jit(solution)/shard_map/ppermute | solution.py:486
  585.9 41.5 %all-to-all-start.3 = ((bf16[4,256,640]{2,1,0:T(8,128)(2,1)}), bf16[4,256,640]{2,1,0:T(8,128)(2,1)}, u32[]{:S(2)}, u32[]{:S(2)}) async-start(bf16[4,256,640]{2,1,0:T(8,128)(2,1)} %pad_maximum_fusion.2), calls=%async_computation.3 | async-start | bytes 2621440 | tf_op jit(solution)/shard_map/all_to_all | solution.py:516
  597.6 40.2 %collective-permute-start.55 = (bf16[4,192,640]{2,1,0:T(8,128)(2,1)}, bf16[4,192,640]{2,1,0:T(8,128)(2,1)}, u32[]{:S(2)}, u32[]{:S(2)}) collective-permute-start(bf16[4,192,640]{2,1,0:T(8,128)(2,1)} %get-tuple-element.330), channel_id=1, source_target_pairs={{0,4},{4,0},{8,12},{12,8},{16,20},{20,16},{24,28},{28,24},{1,5},{5... | collective-permute-start | bytes 2949128 | tf_op jit(solution)/shard_map/ppermute | solution.py:470
  610.8 30.9 %collective-permute-start.53 = (bf16[192,1536]{1,0:T(8,128)(2,1)S(1)}, bf16[192,1536]{1,0:T(8,128)(2,1)S(1)}, u32[]{:S(2)}, u32[]{:S(2)}) collective-permute-start(bf16[192,1536]{1,0:T(8,128)(2,1)S(1)} %bitcast_add_fusion.1), channel_id=1, source_target_pairs={{0,1},{3,2},{4,5},{7,6},{8,9},{11,10},{12,13},{15,14},{16,17},{19,... | collective-permute-start | bytes 1769480 | tf_op jit(solution)/shard_map/ppermute | solution.py:486
  615.7 27.9 %collective-permute-start.54 = (bf16[192,1536]{1,0:T(8,128)(2,1)S(1)}, bf16[192,1536]{1,0:T(8,128)(2,1)}, u32[]{:S(2)}, u32[]{:S(2)}) collective-permute-start(bf16[192,1536]{1,0:T(8,128)(2,1)S(1)} %bitcast_add_fusion.1), channel_id=1, source_target_pairs={{1,2},{2,1},{5,6},{6,5},{9,10},{10,9},{13,14},{14,13},{17,18},{18,... | collective-permute-start | bytes 1769480 | tf_op jit(solution)/shard_map/ppermute | solution.py:478
  619.9 64.8 %collective-permute-start.65 = (bf16[2,384,1536]{2,1,0:T(8,128)(2,1)}, bf16[2,384,1536]{2,1,0:T(8,128)(2,1)}, u32[]{:S(2)}, u32[]{:S(2)}) collective-permute-start(bf16[2,384,1536]{2,1,0:T(8,128)(2,1)} %blend_stack.2.refs_0_), channel_id=1, source_target_pairs={{0,16},{4,20},{8,24},{12,28},{16,0},{20,4},{24,8},{28,12},{1,17},{... | collective-permute-start | bytes 7077896 | tf_op jit(solution)/shard_map/ppermute | solution.py:470
  626.0 64.5 %collective-permute-start.66 = (bf16[2,480,1536]{2,1,0:T(8,128)(2,1)}, bf16[2,480,1536]{2,1,0:T(8,128)(2,1)}, u32[]{:S(2)}, u32[]{:S(2)}) collective-permute-start(bf16[2,480,1536]{2,1,0:T(8,128)(2,1)} %blend_stack.3.refs_0_), channel_id=1, source_target_pairs={{0,8},{4,12},{8,0},{12,4},{16,24},{20,28},{24,16},{28,20},{1,9},{5... | collective-permute-start | bytes 8847368 | tf_op jit(solution)/shard_map/ppermute | solution.py:470
  652.9 24.3 %collective-permute-start.62 = (bf16[192,1536]{1,0:T(8,128)(2,1)S(1)}, bf16[192,1536]{1,0:T(8,128)(2,1)S(1)}, u32[]{:S(2)}, u32[]{:S(2)}) collective-permute-start(bf16[192,1536]{1,0:T(8,128)(2,1)S(1)} %bitcast_add_fusion), channel_id=1, source_target_pairs={{0,1},{1,0},{2,3},{3,2},{4,5},{5,4},{6,7},{7,6},{8,9},{9,8},{10,11... | collective-permute-start | bytes 1769480 | tf_op jit(solution)/shard_map/ppermute | solution.py:474
  653.0 24.3 %collective-permute-start.63 = (bf16[192,1536]{1,0:T(8,128)(2,1)S(1)}, bf16[192,1536]{1,0:T(8,128)(2,1)S(1)}, u32[]{:S(2)}, u32[]{:S(2)}) collective-permute-start(bf16[192,1536]{1,0:T(8,128)(2,1)S(1)} %add.274), channel_id=1, source_target_pairs={{1,2},{2,1},{5,6},{6,5},{9,10},{10,9},{13,14},{14,13},{17,18},{18,... | collective-permute-start | bytes 1769480 | tf_op jit(solution)/shard_map/ppermute | solution.py:478
  660.0 24.6 %collective-permute-start.56 = (f32[8,1536]{1,0:T(8,128)S(1)}, f32[8,1536]{1,0:T(8,128)S(1)}, u32[]{:S(2)}, u32[]{:S(2)}) collective-permute-start(f32[8,1536]{1,0:T(8,128)S(1)} %fusion.12), channel_id=1, source_target_pairs={{0,2},{1,3},{2,0},{3,1},{4,6},{5,7},{6,4},{7,5},{8,10},{9,11},{10,... | collective-permute-start | bytes 147464 | tf_op jit(solution)/shard_map/ppermute | solution.py:474
  698.0 51.4 %collective-permute-start.77 = (bf16[4,480,1536]{2,1,0:T(8,128)(2,1)}, bf16[4,480,1536]{2,1,0:T(8,128)(2,1)}, u32[]{:S(2)}, u32[]{:S(2)}) collective-permute-start(bf16[4,480,1536]{2,1,0:T(8,128)(2,1)} %blend_four.3.refs_1_), channel_id=1, source_target_pairs={{0,4},{4,0},{8,12},{12,8},{16,20},{20,16},{24,28},{28,24},{1,5},{5... | collective-permute-start | bytes 17694728 | tf_op jit(solution)/shard_map/ppermute | solution.py:470
  698.0 31.5 %collective-permute-start.73 = (bf16[4,384,1536]{2,1,0:T(8,128)(2,1)}, bf16[4,384,1536]{2,1,0:T(8,128)(2,1)}, u32[]{:S(2)}, u32[]{:S(2)}) collective-permute-start(bf16[4,384,1536]{2,1,0:T(8,128)(2,1)} %blend_four.2.refs_0_), channel_id=1, source_target_pairs={{0,4},{4,0},{8,12},{12,8},{16,20},{20,16},{24,28},{28,24},{1,5},{5... | collective-permute-start | bytes 14155784 | tf_op jit(solution)/shard_map/ppermute | solution.py:470
  698.5 21.2 %collective-permute-start.72 = (bf16[192,1536]{1,0:T(8,128)(2,1)S(1)}, bf16[192,1536]{1,0:T(8,128)(2,1)S(1)}, u32[]{:S(2)}, u32[]{:S(2)}) collective-permute-start(bf16[192,1536]{1,0:T(8,128)(2,1)S(1)} %fusion.3), channel_id=1, source_target_pairs={{0,8},{4,12},{8,0},{12,4},{16,24},{20,28},{24,16},{28,20},{1,9},{5... | collective-permute-start | bytes 1769480 | tf_op jit(solution)/shard_map/ppermute | solution.py:470
  700.5 27.6 %collective-permute-start.68 = (bf16[96,1536]{1,0:T(8,128)(2,1)S(1)}, bf16[96,1536]{1,0:T(8,128)(2,1)S(1)}, u32[]{:S(2)}, u32[]{:S(2)}) collective-permute-start(bf16[96,1536]{1,0:T(8,128)(2,1)S(1)} %get-tuple-element.356), channel_id=1, source_target_pairs={{0,1},{1,0},{2,3},{3,2},{4,5},{5,4},{6,7},{7,6},{8,9},{9,8},{10,11... | collective-permute-start | bytes 884744 | tf_op jit(solution)/shard_map/ppermute | solution.py:474
  720.5 24.7 %collective-permute-start.69 = (bf16[96,1536]{1,0:T(8,128)(2,1)S(1)}, bf16[96,1536]{1,0:T(8,128)(2,1)S(1)}, u32[]{:S(2)}, u32[]{:S(2)}) collective-permute-start(bf16[96,1536]{1,0:T(8,128)(2,1)S(1)} %get-tuple-element.357), channel_id=1, source_target_pairs={{0,2},{1,3},{2,0},{3,1},{4,6},{5,7},{6,4},{7,5},{8,10},{9,11},{10,... | collective-permute-start | bytes 884744 | tf_op jit(solution)/shard_map/ppermute | solution.py:474
  726.0 20.5 %collective-permute-start.70 = (bf16[96,1536]{1,0:T(8,128)(2,1)S(1)}, bf16[96,1536]{1,0:T(8,128)(2,1)S(1)}, u32[]{:S(2)}, u32[]{:S(2)}) collective-permute-start(bf16[96,1536]{1,0:T(8,128)(2,1)S(1)} %get-tuple-element.358), channel_id=1, source_target_pairs={{0,3},{1,2},{2,1},{3,0},{4,7},{5,6},{6,5},{7,4},{8,11},{9,10},{10,... | collective-permute-start | bytes 884744 | tf_op jit(solution)/shard_map/ppermute | solution.py:474
  728.1 28.5 %collective-permute-start.76 = (bf16[192,1536]{1,0:T(8,128)(2,1)S(1)}, bf16[192,1536]{1,0:T(8,128)(2,1)S(1)}, u32[]{:S(2)}, u32[]{:S(2)}) collective-permute-start(bf16[192,1536]{1,0:T(8,128)(2,1)S(1)} %add.295), channel_id=1, source_target_pairs={{0,16},{4,20},{8,24},{12,28},{16,0},{20,4},{24,8},{28,12},{1,17},{... | collective-permute-start | bytes 1769480 | tf_op jit(solution)/shard_map/ppermute | solution.py:470
  729.5 28.1 %collective-permute-start.75 = (bf16[2,192,640]{2,1,0:T(8,128)(2,1)S(1)}, bf16[2,192,640]{2,1,0:T(8,128)(2,1)S(1)}, u32[]{:S(2)}, u32[]{:S(2)}) collective-permute-start(bf16[2,192,640]{2,1,0:T(8,128)(2,1)S(1)} %pad_maximum_fusion.10), channel_id=1, source_target_pairs={{0,16},{4,20},{8,24},{12,28},{16,0},{20,4},{24,8},{28,12},{1,17},{... | collective-permute-start | bytes 1474568 | tf_op jit(solution)/shard_map/ppermute | solution.py:470
  (181 other events, 1692.7 us)

commit v11 on v10

--- a/solution.py
+++ b/solution.py
@@ -459,7 +459,6 @@
     "blend_pair": 0.3,
     "blend_sum": 0.3,
     "blend_stack": 0.3,
-    "blend_four": 0.3,
     "place_sum": 0.3,
     "place_shared": 0.3,
     "place_heads": 0.3,
@@ -1340,7 +1339,7 @@
     refs[-1][0] = refs[-2][0, :rows].astype(jnp.float32)
 
 
-def place_sum(meta, total, index, of_other, shape, value):
+def place_sum(meta, total, index, of_other, shape, value, stride, offset):
     _, rows, columns = value.shape
     arrays = [value]
     in_specs = [pl.BlockSpec((1, rows, columns), lambda r, m: (r, 0, 0))]
@@ -1353,11 +1352,11 @@
         place_sum_kernel,
         grid_spec=pltpu.PrefetchScalarGridSpec(
             num_scalar_prefetch=1,
-            grid=(4,),
+            grid=(2,),
             in_specs=in_specs,
             out_specs=pl.BlockSpec(
                 (1, shape[1] // 4, shape[2]),
-                lambda r, m: (2 * ((m[0] & 1) ^ of_other) + index, (m[0] >> 1) ^ r, 0),
+                lambda r, m: (2 * ((m[0] & 1) ^ of_other) + index, (m[0] >> 1) ^ (stride * r + offset), 0),
             ),
         ),
         out_shape=shape_of(shape, jnp.float32),
@@ -1486,9 +1485,9 @@
     "M", "K", "R", "M", "K", "M", "M", "M", "M", "R", "M", "M",
 )
 LATE = (
-    "L", "0", "1", "0", "0", "L", "1", "1", "L", "L", "O", "0", "1", "L", "0", "L", "1", "O", "Q", "1", "O", "0", "L", "Q",
-    "O", "L", "Q", "Q", "O", "Q", "L", "1", "0", "O", "Q", "S", "1", "0", "L", "O", "Q", "1", "S", "L", "0", "O", "Q", "L",
-    "Q", "O", "S",
+    "L", "0", "1", "0", "0", "L", "1", "1", "L", "L", "O", "0", "1", "L", "L", "1", "0", "O", "Q", "1", "O", "0", "L", "Q",
+    "O", "L", "1", "Q", "1", "Q", "0", "O", "0", "Q", "L", "1", "0", "O", "Q", "S", "1", "0", "L", "O", "Q", "1", "S", "L",
+    "0", "O", "Q", "L", "Q", "O", "S",
 )
 
 
@@ -1876,24 +1875,36 @@
             blend(meta(), "blend_stack", lambda a, b: jnp.stack([a, b]), [own, came], pieces)
         )
         came = flip(pair, first)
-        yield
-
-        def stack_four(near, far):
-            if x_first:
-                return jnp.stack([near[0], far[0], near[1], far[1]])
-            return jnp.stack([near[0], near[1], far[0], far[1]])
-
-        stacked = clock.mark(blend(meta(), "blend_four", stack_four, [pair, came], pieces))
-        other = flip(stacked, 1)
-        if index == 0:
-            have["shared_sum"] = stacked[:, shard_rows:]
-        yield
-        for of_other, value in ((0, stacked), (1, other)):
+        pair_other = flip(pair, 1)
+        yield
+
+        def place(of_other, value, far):
+            stride, offset = (2, far) if x_first else (1, 2 * far)
             have["grad_experts"] = place_sum(
-                meta(), have.get("grad_experts"), index, of_other, expert_weight.shape, value
+                meta(),
+                have.get("grad_experts"),
+                index,
+                of_other,
+                expert_weight.shape,
+                value,
+                stride,
+                offset,
             )
             clock.mark(have["grad_experts"])
-            yield
+
+        place(0, pair, 0)
+        yield
+        place(1, pair_other, 0)
+        yield
+        came = now(came)
+        came_other = flip(came, 1)
+        if index == 0:
+            have["shared_sum"] = jnp.stack([pair[0], came[0], pair[1], came[1]])[:, shard_rows:]
+        yield
+        place(0, came, 1)
+        yield
+        place(1, came_other, 1)
+        yield
 
     def shared_grad_chain():
         total = now(have["shared_sum"])

time: 791 us -> 768 us (0.971)
  Pallas kernels: 307 us -> 295 us
  starting transfers between devices: 147 us -> 137 us
    ppermute x40 -> x42, waiting for transfers between devices: 52.5 us -> 81.3 us  [flip(): lax.ppermute(value, 'ctx', [(index, index ^ bit) for index in range(8)])]
    all_to_all x3, waiting for transfers between devices: 25.9 us -> 0.01 us  [chips_exchange(): lax.all_to_all(blocks, 'ctx', split_axis=0, concat_axis=0, tiled=True, ax...]
    pallas_call x33 -> x31, Pallas kernels: 281 us -> 262 us  [call(): pl.pallas_call(kernel, grid_spec=pltpu.PrefetchScalarGridSpec(num_scalar_...]
    ppermute x17, starting transfers between devices: 47.4 us -> 38.4 us  [line_swap(): lax.ppermute(value, 'wt', [(index, index ^ offset) for index in range(4)])]
    pallas_call x4 -> x8, Pallas kernels: 25.8 us -> 32.3 us  [place_sum(): pl.pallas_call(place_sum_kernel, grid_spec=pltpu.PrefetchScalarGridSpec(n...]
    unnamed x293 -> x289, local copies, waits for them, and re-layouts: 55.6 us -> 50.9 us
    ppermute x40 -> x42, starting transfers between devices: 28.3 us -> 27.7 us  [flip(): lax.ppermute(value, 'ctx', [(index, index ^ bit) for index in range(8)])]
  transfers between devices with their start and end apart: 85 -> 87, of which waited for: 31 -> 35; matrix products, arithmetic and copies ran while one was open for 8% -> 8% of each run, Pallas kernels for 34% -> 34%
where the time goes in v11:
time: 768 us; the launch traced here: 761 us
  Pallas kernels  295 us (38%)
  waiting for transfers between devices  202 us (26%)
  starting transfers between devices  137 us (18%)
  local copies, waits for them, and re-layouts  69.2 us (9%)
  other arithmetic  51.8 us (7%)
    pallas_call x31, Pallas kernels, call(): pl.pallas_call(kernel, grid_spec=pltpu.PrefetchScalarGridSpec(num_scalar_...  262 us
    ppermute x42, waiting for transfers between devices, flip(): lax.ppermute(value, 'ctx', [(index, index ^ bit) for index in range(8)])  81.3 us
    ppermute x17, waiting for transfers between devices, line_swap(): lax.ppermute(value, 'wt', [(index, index ^ offset) for index in range(4)])  68.7 us
    unnamed x289, local copies, waits for them, and re-layouts  50.9 us
    ppermute x17, starting transfers between devices, line_swap(): lax.ppermute(value, 'wt', [(index, index ^ offset) for index in range(4)])  38.4 us
    ppermute x8, starting transfers between devices, line_inward(): return lax.ppermute(value, 'wt', [(0, 1), (3, 2)])  34.5 us
    pallas_call x8, Pallas kernels, place_sum(): pl.pallas_call(place_sum_kernel, grid_spec=pltpu.PrefetchScalarGridSpec(n...  32.3 us
    ppermute x8, waiting for transfers between devices, line_inward(): return lax.ppermute(value, 'wt', [(0, 1), (3, 2)])  27.9 us
  transfers between devices with their start and end apart: 87, of which 35 were waited for; matrix products, arithmetic and copies ran while one was open for 8% of the time, Pallas kernels for 34%

profile of v11, /device:TPU:0, one launch (start us, length us, event | category | flops | bytes accessed | tf_op | source)
XLA Modules:
  0.0 761.3 jit_solution(11585755445574482090)
XLA Ops:
  8.7 4.8 all-to-all-start.1
  27.6 22.4 %collective-permute-done.5 = bf16[2,192,640]{2,1,0:T(8,128)(2,1)S(1)} collective-permute-done((bf16[2,192,640]{2,1,0:T(8,128)(2,1)S(1)}, bf16[2,192,640]{2,1,0:T(8,128)(2,1)S(1)}, u32[]{:S(2)}, u32[]{:S(2)}) %collective-permute-start.5) | collective-permute-done | bytes 491552 | tf_op jit(solution)/shard_map/ppermute | solution.py:473
  55.8 4.7 all-to-all-start
  62.5 7.8 %collective-permute-done.6 = bf16[4,48,768]{2,1,0:T(8,128)(2,1)S(1)} collective-permute-done((bf16[4,48,768]{2,1,0:T(8,128)(2,1)}, bf16[4,48,768]{2,1,0:T(8,128)(2,1)S(1)}, u32[]{:S(2)}, u32[]{:S(2)}) %collective-permute-start.6) | collective-permute-done | bytes 294944 | tf_op jit(solution)/shard_map/ppermute | solution.py:469
  73.4 6.8 project.1
  83.4 10.4 %attend.1 = (bf16[4,256,384]{2,1,0:T(8,128)(2,1)S(1)}, f32[8,1,384]{2,1,0:T(1,128)S(1)}) custom-call(s32[2]{0:T(128)S(1)} %pad_add_fusion.meta.meta_ref, bf16[4,256,384]{2,1,0:T(8,128)(2,1)S(1)} %get-tuple-element.206.query_ref, bf16[4,256,256]{2,1,0:T(8,128)(2,1)S(1)} %get-tuple-element.204.mine_ref, bf16[4,256,256]{2,1,0:T(8,128)(2,1)S(1)} %collective-permute-done.9.other_ref), custom_call_target="tpu_custom_call" | custom-call | flops 300000000 | bytes 1000 | tf_op jit(solution)/shard_map/attend/pallas_call | solution.py:584
  99.7 14.1 %all-to-all-done.refs_4_ = bf16[4,192,1536]{2,1,0:T(8,128)(2,1)} async-done(((bf16[4,192,1536]{2,1,0:T(8,128)(2,1)}), bf16[4,192,1536]{2,1,0:T(8,128)(2,1)}, u32[]{:S(2)}, u32[]{:S(2)}) %all-to-all-start) | async-done | bytes 2359328 | tf_op jit(solution)/shard_map/all_to_all | solution.py:526
  122.1 4.6 collective-permute-done.11.refs_2_
  128.2 6.2 leave.1
  142.9 11.7 %experts.4 = (bf16[4,256,1024]{2,1,0:T(8,128)(2,1)S(1)}, bf16[256,512]{1,0:T(8,128)(2,1)S(1)}, bf16[256,1536]{1,0:T(8,128)(2,1)S(1)}) custom-call(s32[2]{0:T(128)S(1)} %pad_add_fusion.meta.meta_ref, bf16[256,1536]{1,0:T(8,128)(2,1)S(1)} %get-tuple-element.217.rows_ref.refs_0_, f32[4,256,1]{2,1,0:T(8,128)S(1)} %copy.45.gates_ref, ...), custom_call_target="tpu_custom_call" | custom-call | flops 300000000 | bytes 1000 | tf_op jit(solution)/shard_map/experts/pallas_call | solution.py:584
  160.5 11.9 %experts.5 = (bf16[4,256,1024]{2,1,0:T(8,128)(2,1)S(1)}, bf16[256,512]{1,0:T(8,128)(2,1)S(1)}, bf16[256,1536]{1,0:T(8,128)(2,1)S(1)}) custom-call(s32[2]{0:T(128)S(1)} %pad_add_fusion.meta.meta_ref, bf16[256,1536]{1,0:T(8,128)(2,1)S(1)} %collective-permute-done.15.rows_ref.refs_1_, f32[4,256,1]{2,1,0:T(8,128)S(1)} %copy.46.gates_ref, ...), custom_call_target="tpu_custom_call" | custom-call | flops 300000000 | bytes 1000 | tf_op jit(solution)/shard_map/experts/pallas_call | solution.py:584
  173.8 6.7 collective-permute-done.18
  186.7 11.7 %experts.6 = (bf16[4,256,1024]{2,1,0:T(8,128)(2,1)S(1)}, bf16[256,512]{1,0:T(8,128)(2,1)S(1)}, bf16[256,1536]{1,0:T(8,128)(2,1)S(1)}) custom-call(s32[2]{0:T(128)S(1)} %pad_add_fusion.meta.meta_ref, bf16[256,1536]{1,0:T(8,128)(2,1)S(1)} %broadcast_select_fusion.3.rows_ref.refs_2_, f32[4,256,1]{2,1,0:T(8,128)S(1)} %copy.47.gates_ref, ...), custom_call_target="tpu_custom_call" | custom-call | flops 300000000 | bytes 1000 | tf_op jit(solution)/shard_map/experts/pallas_call | solution.py:584
  200.7 11.7 %experts.7 = (bf16[4,256,1024]{2,1,0:T(8,128)(2,1)S(1)}, bf16[256,512]{1,0:T(8,128)(2,1)S(1)}, bf16[256,1536]{1,0:T(8,128)(2,1)S(1)}) custom-call(s32[2]{0:T(128)S(1)} %pad_add_fusion.meta.meta_ref, bf16[256,1536]{1,0:T(8,128)(2,1)S(1)} %broadcast_select_fusion.2.rows_ref.refs_3_, f32[4,256,1]{2,1,0:T(8,128)S(1)} %copy.48.gates_ref, ...), custom_call_target="tpu_custom_call" | custom-call | flops 300000000 | bytes 1000 | tf_op jit(solution)/shard_map/experts/pallas_call | solution.py:584
  212.5 5.8 collective-permute-start.21
  223.4 12.2 %collective-permute-done.21 = bf16[256,1536]{1,0:T(8,128)(2,1)S(1)} collective-permute-done((bf16[256,1536]{1,0:T(8,128)(2,1)S(1)}, bf16[256,1536]{1,0:T(8,128)(2,1)S(1)}, u32[]{:S(2)}, u32[]{:S(2)}) %collective-permute-start.21) | collective-permute-done | bytes 786464 | tf_op jit(solution)/shard_map/ppermute | solution.py:485
  235.8 4.4 collective-permute-start.24
  244.7 12.2 %collective-permute-done.24 = bf16[256,1536]{1,0:T(8,128)(2,1)S(1)} collective-permute-done((bf16[256,1536]{1,0:T(8,128)(2,1)S(1)}, bf16[256,1536]{1,0:T(8,128)(2,1)S(1)}, u32[]{:S(2)}, u32[]{:S(2)}) %collective-permute-start.24) | collective-permute-done | bytes 786464 | tf_op jit(solution)/shard_map/ppermute | solution.py:485
  263.7 13.9 %collective-permute-done.27 = bf16[256,1536]{1,0:T(8,128)(2,1)S(1)} collective-permute-done((bf16[256,1536]{1,0:T(8,128)(2,1)S(1)}, bf16[256,1536]{1,0:T(8,128)(2,1)S(1)}, u32[]{:S(2)}, u32[]{:S(2)}) %collective-permute-start.27) | collective-permute-done | bytes 786464 | tf_op jit(solution)/shard_map/ppermute | solution.py:473
  285.3 13.0 %experts_back.4 = (bf16[4,256,1024]{2,1,0:T(8,128)(2,1)S(1)}, bf16[4,256,512]{2,1,0:T(8,128)(2,1)S(1)}, bf16[1,256,512]{2,1,0:T(8,128)(2,1)S(1)}, bf16[1,256,256]{2,1,0:T(8,128)(2,1)S(1)}, bf16[256,1536]{1,0:T(8,128)(2,1)S(1)}) custom-call(s32[2]{0:T(128)S(1)} %pad_add_fusion.meta.meta_ref, bf16[256,1536]{1,0:T(8,128)(2,1)S(1)} %get-tuple-element.387.grad_ref.refs_4_, ...), custom_call_target="tpu_custom_call" | custom-call | flops 300000000 | bytes 1000 | tf_op jit(solution)/shard_map/experts_back/pallas_call | solution.py:584
  305.2 13.0 %experts_back.5 = (bf16[4,256,1024]{2,1,0:T(8,128)(2,1)S(1)}, bf16[4,256,512]{2,1,0:T(8,128)(2,1)S(1)}, bf16[1,256,512]{2,1,0:T(8,128)(2,1)S(1)}, bf16[1,256,256]{2,1,0:T(8,128)(2,1)S(1)}, bf16[256,1536]{1,0:T(8,128)(2,1)S(1)}) custom-call(s32[2]{0:T(128)S(1)} %pad_add_fusion.meta.meta_ref, bf16[256,1536]{1,0:T(8,128)(2,1)S(1)} %collective-permute-done.29.grad_ref.refs_5_, ...), custom_call_target="tpu_custom_call" | custom-call | flops 300000000 | bytes 1000 | tf_op jit(solution)/shard_map/experts_back/pallas_call | solution.py:584
  318.2 4.5 pad_maximum_fusion.refs_1_
  327.3 13.0 %experts_back.6 = (bf16[4,256,1024]{2,1,0:T(8,128)(2,1)S(1)}, bf16[4,256,512]{2,1,0:T(8,128)(2,1)S(1)}, bf16[1,256,512]{2,1,0:T(8,128)(2,1)S(1)}, bf16[1,256,256]{2,1,0:T(8,128)(2,1)S(1)}, bf16[256,1536]{1,0:T(8,128)(2,1)S(1)}) custom-call(s32[2]{0:T(128)S(1)} %pad_add_fusion.meta.meta_ref, bf16[256,1536]{1,0:T(8,128)(2,1)S(1)} %broadcast_select_fusion.1.grad_ref.refs_6_, ...), custom_call_target="tpu_custom_call" | custom-call | flops 300000000 | bytes 1000 | tf_op jit(solution)/shard_map/experts_back/pallas_call | solution.py:584
  345.5 14.4 %experts_back.7 = (bf16[4,256,1024]{2,1,0:T(8,128)(2,1)S(1)}, bf16[4,256,512]{2,1,0:T(8,128)(2,1)S(1)}, bf16[1,256,512]{2,1,0:T(8,128)(2,1)S(1)}, bf16[1,256,256]{2,1,0:T(8,128)(2,1)S(1)}, bf16[256,1536]{1,0:T(8,128)(2,1)}) custom-call(s32[2]{0:T(128)S(1)} %pad_add_fusion.meta.meta_ref, bf16[256,1536]{1,0:T(8,128)(2,1)S(1)} %broadcast_select_fusion.grad_ref.refs_7_, ...), custom_call_target="tpu_custom_call" | custom-call | flops 300000000 | bytes 1000 | tf_op jit(solution)/shard_map/experts_back/pallas_call | solution.py:584
  362.3 13.1 %expert_grad.4 = bf16[4,480,1536]{2,1,0:T(8,128)(2,1)} custom-call(s32[3]{0:T(128)S(1)} %add_add_fusion.meta, bf16[256,1536]{1,0:T(8,128)(2,1)S(1)} %copy-done.15, bf16[256,1536]{1,0:T(8,128)(2,1)S(1)} %copy-done.20, bf16[256,1536]{1,0:T(8,128)(2,1)S(1)} %broadcast_select_fusion.3.rows_ref.refs_2_, ...), custom_call_target="tpu_custom_call" | custom-call | flops 300000000 | bytes 1000 | tf_op jit(solution)/shard_map/expert_grad/pallas_call | solution.py:584
  379.0 10.2 %expert_grad.5 = bf16[4,384,1536]{2,1,0:T(8,128)(2,1)} custom-call(s32[3]{0:T(128)S(1)} %add_add_fusion.1.meta, bf16[256,1536]{1,0:T(8,128)(2,1)S(1)} %copy-done.16, bf16[256,1536]{1,0:T(8,128)(2,1)S(1)} %copy-done.21, bf16[256,1536]{1,0:T(8,128)(2,1)S(1)} %broadcast_select_fusion.3.rows_ref.refs_2_, ...), custom_call_target="tpu_custom_call" | custom-call | flops 300000000 | bytes 1000 | tf_op jit(solution)/shard_map/expert_grad/pallas_call | solution.py:584
  401.7 13.0 %expert_grad.6.refs_0_ = bf16[4,480,1536]{2,1,0:T(8,128)(2,1)} custom-call(s32[3]{0:T(128)S(1)} %add_add_fusion.2.meta, bf16[256,1536]{1,0:T(8,128)(2,1)S(1)} %copy-done.17, bf16[256,1536]{1,0:T(8,128)(2,1)S(1)} %copy-done.22, bf16[256,1536]{1,0:T(8,128)(2,1)S(1)} %broadcast_select_fusion.3.rows_ref.refs_2_, ...), custom_call_target="tpu_custom_call" | custom-call | flops 300000000 | bytes 1000 | tf_op jit(solution)/shard_map/expert_grad/pallas_call | solution.py:584
  414.6 7.8 %blend_split.2 = (bf16[2,480,1536]{2,1,0:T(8,128)(2,1)}, bf16[2,480,1536]{2,1,0:T(8,128)(2,1)S(1)}) custom-call(s32[2]{0:T(128)S(1)} %pad_add_fusion.meta.meta_ref, bf16[4,480,1536]{2,1,0:T(8,128)(2,1)} %expert_grad.6.refs_0_, bf16[4,480,1536]{2,1,0:T(8,128)(2,1)} %collective-permute-done.36.refs_1_), custom_call_target="tpu_custom_call" | custom-call | flops 300000000 | bytes 1000 | tf_op jit(solution)/shard_map/blend_split/pallas_call | solution.py:584
  434.6 10.1 %expert_grad.7.refs_0_ = bf16[4,384,1536]{2,1,0:T(8,128)(2,1)} custom-call(s32[3]{0:T(128)S(1)} %add_add_fusion.3.meta, bf16[256,1536]{1,0:T(8,128)(2,1)S(1)} %copy-done.18, bf16[256,1536]{1,0:T(8,128)(2,1)S(1)} %copy-done.23, bf16[256,1536]{1,0:T(8,128)(2,1)S(1)} %broadcast_select_fusion.3.rows_ref.refs_2_, ...), custom_call_target="tpu_custom_call" | custom-call | flops 300000000 | bytes 1000 | tf_op jit(solution)/shard_map/expert_grad/pallas_call | solution.py:584
  444.7 6.1 blend_split.3
  458.0 15.9 %collective-permute-done.40 = bf16[256,1536]{1,0:T(8,128)(2,1)} collective-permute-done((bf16[256,1536]{1,0:T(8,128)(2,1)S(1)}, bf16[256,1536]{1,0:T(8,128)(2,1)}, u32[]{:S(2)}, u32[]{:S(2)}) %collective-permute-start.40) | collective-permute-done | bytes 786464 | tf_op jit(solution)/shard_map/ppermute | solution.py:473
  476.7 7.3 enter_back.1
  498.1 5.2 blend_pair.2
  505.1 10.0 %collective-permute-done.44.refs_1_ = bf16[2,384,1536]{2,1,0:T(8,128)(2,1)} collective-permute-done((bf16[2,384,1536]{2,1,0:T(8,128)(2,1)}, bf16[2,384,1536]{2,1,0:T(8,128)(2,1)}, u32[]{:S(2)}, u32[]{:S(2)}) %collective-permute-start.44) | collective-permute-done | bytes 2359328 | tf_op jit(solution)/shard_map/ppermute | solution.py:469
  515.2 4.5 blend_pair.3
  522.2 14.3 %attend_back.1 = (bf16[4,256,384]{2,1,0:T(8,128)(2,1)S(1)}, f32[4,256,256]{2,1,0:T(8,128)S(1)}, bf16[4,256,256]{2,1,0:T(8,128)(2,1)S(1)}) custom-call(s32[2]{0:T(128)S(1)} %pad_add_fusion.meta.meta_ref, bf16[4,256,384]{2,1,0:T(8,128)(2,1)S(1)} %copy-done.47, bf16[4,256,256]{2,1,0:T(8,128)(2,1)S(1)} %copy-done.57, bf16[4,256,256]{2,1,0:T(8,128)(2,1)S(1)} %copy-done.59, ...), custom_call_target="tpu_custom_call" | custom-call | flops 300000000 | bytes 1000 | tf_op jit(solution)/shard_map/attend_back/pallas_call | solution.py:584
  539.8 6.1 collective-permute-done.46.refs_1_
  555.8 5.1 collective-permute-start.48
  560.9 4.3 all-to-all-start.3
  565.4 6.8 weight_grad.3
  584.5 4.5 collective-permute-start.53
  590.5 5.8 collective-permute-done.50.refs_1_
  603.1 9.1 %finish.1 = (f32[1,256,1536]{2,1,0:T(8,128)}, f32[1,1536]{1,0:T(1,128)S(1)}) custom-call(s32[2]{0:T(128)S(1)} %pad_add_fusion.meta.meta_ref, bf16[4,256,640]{2,1,0:T(8,128)(2,1)} %all-to-all-done.3.refs_0_, bf16[4,768,640]{2,1,0:T(8,128)(2,1)} %pad_maximum_fusion.refs_1_, bf16[4,768,640]{2,1,0:T(8,128)(2,1)} %collective-permute-done.51.refs_2_, ...), custom_call_target="tpu_custom_call" | custom-call | flops 300000000 | bytes 1000 | tf_op jit(solution)/shard_map/finish/pallas_call | solution.py:584
  629.6 4.4 collective-permute-start.58
  639.0 9.9 %collective-permute-start.63 = (bf16[192,1536]{1,0:T(8,128)(2,1)S(1)}, bf16[192,1536]{1,0:T(8,128)(2,1)S(1)}, u32[]{:S(2)}, u32[]{:S(2)}) collective-permute-start(bf16[192,1536]{1,0:T(8,128)(2,1)S(1)} %bitcast_add_fusion), channel_id=1, source_target_pairs={{0,1},{1,0},{2,3},{3,2},{4,5},{5,4},{6,7},{7,6},{8,9},{9,8},{10,11... | collective-permute-start | bytes 1769480 | tf_op jit(solution)/shard_map/ppermute | solution.py:473
  678.1 8.1 %collective-permute-done.68.refs_1_ = bf16[2,384,1536]{2,1,0:T(8,128)(2,1)} collective-permute-done((bf16[2,384,1536]{2,1,0:T(8,128)(2,1)}, bf16[2,384,1536]{2,1,0:T(8,128)(2,1)}, u32[]{:S(2)}, u32[]{:S(2)}) %collective-permute-start.68) | collective-permute-done | bytes 2359328 | tf_op jit(solution)/shard_map/ppermute | solution.py:469
  717.0 8.0 %collective-permute-done.71 = bf16[96,1536]{1,0:T(8,128)(2,1)S(1)} collective-permute-done((bf16[96,1536]{1,0:T(8,128)(2,1)S(1)}, bf16[96,1536]{1,0:T(8,128)(2,1)S(1)}, u32[]{:S(2)}, u32[]{:S(2)}) %collective-permute-start.71) | collective-permute-done | bytes 294944 | tf_op jit(solution)/shard_map/ppermute | solution.py:473
  754.4 5.5 place_shared.1
  (565 shorter events, 318.1 us)
Async XLA Ops:
  8.7 45.5 %all-to-all-start.1 = ((bf16[4,256,1536]{2,1,0:T(8,128)(2,1)}), bf16[4,256,1536]{2,1,0:T(8,128)(2,1)}, u32[]{:S(2)}, u32[]{:S(2)}) async-start(bf16[4,256,1536]{2,1,0:T(8,128)(2,1)} %broadcast_in_dim.55), calls=%async_computation.1 | async-start | bytes 6291456 | tf_op jit(solution)/shard_map/all_to_all | solution.py:515
  20.7 29.3 %collective-permute-start.5 = (bf16[2,192,640]{2,1,0:T(8,128)(2,1)S(1)}, bf16[2,192,640]{2,1,0:T(8,128)(2,1)S(1)}, u32[]{:S(2)}, u32[]{:S(2)}) collective-permute-start(bf16[2,192,640]{2,1,0:T(8,128)(2,1)S(1)} %pad_maximum_fusion.12), channel_id=1, source_target_pairs={{0,2},{1,3},{2,0},{3,1},{4,6},{5,7},{6,4},{7,5},{8,10},{9,11},{10,... | collective-permute-start | bytes 1474568 | tf_op jit(solution)/shard_map/ppermute | solution.py:473
  23.3 28.0 %collective-permute-start.4 = (f32[2,32,256]{2,1,0:T(8,128)S(1)}, f32[2,32,256]{2,1,0:T(8,128)S(1)}, u32[]{:S(2)}, u32[]{:S(2)}) collective-permute-start(f32[2,32,256]{2,1,0:T(8,128)S(1)} %pad_maximum_fusion.19), channel_id=1, source_target_pairs={{0,2},{1,3},{2,0},{3,1},{4,6},{5,7},{6,4},{7,5},{8,10},{9,11},{10,... | collective-permute-start | bytes 196616 | tf_op jit(solution)/shard_map/ppermute | solution.py:473
  23.7 29.7 %collective-permute-start.3 = (bf16[2,48,768]{2,1,0:T(8,128)(2,1)S(1)}, bf16[2,48,768]{2,1,0:T(8,128)(2,1)S(1)}, u32[]{:S(2)}, u32[]{:S(2)}) collective-permute-start(bf16[2,48,768]{2,1,0:T(8,128)(2,1)S(1)} %pad_maximum_fusion.17), channel_id=1, source_target_pairs={{0,2},{1,3},{2,0},{3,1},{4,6},{5,7},{6,4},{7,5},{8,10},{9,11},{10,... | collective-permute-start | bytes 442376 | tf_op jit(solution)/shard_map/ppermute | solution.py:473
  55.8 58.0 %all-to-all-start = ((bf16[4,192,1536]{2,1,0:T(8,128)(2,1)}), bf16[4,192,1536]{2,1,0:T(8,128)(2,1)}, u32[]{:S(2)}, u32[]{:S(2)}) async-start(bf16[4,192,1536]{2,1,0:T(8,128)(2,1)} %broadcast_in_dim.54), calls=%async_computation | async-start | bytes 4718592 | tf_op jit(solution)/shard_map/all_to_all | solution.py:526
  113.8 24.7 %collective-permute-start.14 = (bf16[4,4,48,768]{3,2,1,0:T(8,128)(2,1)}, bf16[4,4,48,768]{3,2,1,0:T(8,128)(2,1)}, u32[]{:S(2)}, u32[]{:S(2)}) collective-permute-start(bf16[4,4,48,768]{3,2,1,0:T(8,128)(2,1)} %pad_maximum_fusion.6.mine), channel_id=1, source_target_pairs={{0,4},{4,0},{8,12},{12,8},{16,20},{20,16},{24,28},{28,24},{1,5},{5... | collective-permute-start | bytes 3538952 | tf_op jit(solution)/shard_map/ppermute | solution.py:469
  135.6 21.3 %collective-permute-start.15 = (bf16[256,1536]{1,0:T(8,128)(2,1)S(1)}, bf16[256,1536]{1,0:T(8,128)(2,1)S(1)}, u32[]{:S(2)}, u32[]{:S(2)}) collective-permute-start(bf16[256,1536]{1,0:T(8,128)(2,1)S(1)} %get-tuple-element.217.rows_ref.refs_0_), channel_id=1, source_target_pairs={{0,1},{1,0},{2,3},{3,2},{4,5},{5,4},{6,7},{7,6},{8,9},{9,8},{10,11... | collective-permute-start | bytes 2359304 | tf_op jit(solution)/shard_map/ppermute | solution.py:473
  135.6 21.3 %collective-permute-start.16 = (bf16[256,1536]{1,0:T(8,128)(2,1)S(1)}, bf16[256,1536]{1,0:T(8,128)(2,1)}, u32[]{:S(2)}, u32[]{:S(2)}) collective-permute-start(bf16[256,1536]{1,0:T(8,128)(2,1)S(1)} %get-tuple-element.217.rows_ref.refs_0_), channel_id=1, source_target_pairs={{1,2},{2,1},{5,6},{6,5},{9,10},{10,9},{13,14},{14,13},{17,18},{18,... | collective-permute-start | bytes 2359304 | tf_op jit(solution)/shard_map/ppermute | solution.py:477
  158.4 22.1 %collective-permute-start.18 = (bf16[256,1536]{1,0:T(8,128)(2,1)}, bf16[256,1536]{1,0:T(8,128)(2,1)}, u32[]{:S(2)}, u32[]{:S(2)}) collective-permute-start(bf16[256,1536]{1,0:T(8,128)(2,1)} %collective-permute-done.16), channel_id=1, source_target_pairs={{1,0},{2,3},{5,4},{6,7},{9,8},{10,11},{13,12},{14,15},{17,16},{18,... | collective-permute-start | bytes 2359304 | tf_op jit(solution)/shard_map/ppermute | solution.py:481
  180.5 20.1 %collective-permute-start.19 = (bf16[256,1536]{1,0:T(8,128)(2,1)}, bf16[256,1536]{1,0:T(8,128)(2,1)S(1)}, u32[]{:S(2)}, u32[]{:S(2)}) collective-permute-start(bf16[256,1536]{1,0:T(8,128)(2,1)} %collective-permute-done.17), channel_id=1, source_target_pairs={{1,0},{2,3},{5,4},{6,7},{9,8},{10,11},{13,12},{14,15},{17,16},{18,... | collective-permute-start | bytes 2359304 | tf_op jit(solution)/shard_map/ppermute | solution.py:481
  183.2 38.7 %collective-permute-start.22 = (bf16[768,640]{1,0:T(8,128)(2,1)S(1)}, bf16[768,640]{1,0:T(8,128)(2,1)S(1)}, u32[]{:S(2)}, u32[]{:S(2)}) collective-permute-start(bf16[768,640]{1,0:T(8,128)(2,1)S(1)} %constant_dynamic-slice_fusion.1), channel_id=1, source_target_pairs={{0,8},{4,12},{8,0},{12,4},{16,24},{20,28},{24,16},{28,20},{1,9},{5... | collective-permute-start | bytes 2949128 | tf_op jit(solution)/shard_map/ppermute | solution.py:469
  212.5 23.2 %collective-permute-start.21 = (bf16[256,1536]{1,0:T(8,128)(2,1)S(1)}, bf16[256,1536]{1,0:T(8,128)(2,1)S(1)}, u32[]{:S(2)}, u32[]{:S(2)}) collective-permute-start(bf16[256,1536]{1,0:T(8,128)(2,1)S(1)} %get-tuple-element.233), channel_id=1, source_target_pairs={{0,1},{3,2},{4,5},{7,6},{8,9},{11,10},{12,13},{15,14},{16,17},{19,... | collective-permute-start | bytes 2359304 | tf_op jit(solution)/shard_map/ppermute | solution.py:485
  235.8 21.0 %collective-permute-start.24 = (bf16[256,1536]{1,0:T(8,128)(2,1)S(1)}, bf16[256,1536]{1,0:T(8,128)(2,1)S(1)}, u32[]{:S(2)}, u32[]{:S(2)}) collective-permute-start(bf16[256,1536]{1,0:T(8,128)(2,1)S(1)} %add.250), channel_id=1, source_target_pairs={{0,1},{3,2},{4,5},{7,6},{8,9},{11,10},{12,13},{15,14},{16,17},{19,... | collective-permute-start | bytes 2359304 | tf_op jit(solution)/shard_map/ppermute | solution.py:485
  257.3 20.4 %collective-permute-start.27 = (bf16[256,1536]{1,0:T(8,128)(2,1)S(1)}, bf16[256,1536]{1,0:T(8,128)(2,1)S(1)}, u32[]{:S(2)}, u32[]{:S(2)}) collective-permute-start(bf16[256,1536]{1,0:T(8,128)(2,1)S(1)} %add.252), channel_id=1, source_target_pairs={{0,1},{1,0},{2,3},{3,2},{4,5},{5,4},{6,7},{7,6},{8,9},{9,8},{10,11... | collective-permute-start | bytes 2359304 | tf_op jit(solution)/shard_map/ppermute | solution.py:473
  261.9 56.4 %collective-permute-start.33 = (bf16[2,768,640]{2,1,0:T(8,128)(2,1)}, bf16[2,768,640]{2,1,0:T(8,128)(2,1)}, u32[]{:S(2)}, u32[]{:S(2)}) collective-permute-start(bf16[2,768,640]{2,1,0:T(8,128)(2,1)} %pad_maximum_fusion.1), channel_id=1, source_target_pairs={{0,16},{4,20},{8,24},{12,28},{16,0},{20,4},{24,8},{28,12},{1,17},{... | collective-permute-start | bytes 5898248 | tf_op jit(solution)/shard_map/ppermute | solution.py:469
  280.7 21.6 %collective-permute-start.29 = (bf16[256,1536]{1,0:T(8,128)(2,1)S(1)}, bf16[256,1536]{1,0:T(8,128)(2,1)S(1)}, u32[]{:S(2)}, u32[]{:S(2)}) collective-permute-start(bf16[256,1536]{1,0:T(8,128)(2,1)S(1)} %get-tuple-element.387.grad_ref.refs_4_), channel_id=1, source_target_pairs={{0,1},{1,0},{2,3},{3,2},{4,5},{5,4},{6,7},{7,6},{8,9},{9,8},{10,11... | collective-permute-start | bytes 2359304 | tf_op jit(solution)/shard_map/ppermute | solution.py:473
  302.3 20.5 %collective-permute-start.31 = (bf16[256,1536]{1,0:T(8,128)(2,1)S(1)}, bf16[256,1536]{1,0:T(8,128)(2,1)}, u32[]{:S(2)}, u32[]{:S(2)}) collective-permute-start(bf16[256,1536]{1,0:T(8,128)(2,1)S(1)} %collective-permute-done.29.grad_ref.refs_5_), channel_id=1, source_target_pairs={{1,2},{2,1},{5,6},{6,5},{9,10},{10,9},{13,14},{14,13},{17,18},{18,... | collective-permute-start | bytes 2359304 | tf_op jit(solution)/shard_map/ppermute | solution.py:477
  303.9 20.0 %collective-permute-start.32 = (bf16[256,1536]{1,0:T(8,128)(2,1)S(1)}, bf16[256,1536]{1,0:T(8,128)(2,1)S(1)}, u32[]{:S(2)}, u32[]{:S(2)}) collective-permute-start(bf16[256,1536]{1,0:T(8,128)(2,1)S(1)} %collective-permute-done.30), channel_id=1, source_target_pairs={{1,0},{2,3},{5,4},{6,7},{9,8},{10,11},{13,12},{14,15},{17,16},{18,... | collective-permute-start | bytes 2359304 | tf_op jit(solution)/shard_map/ppermute | solution.py:481
  375.4 39.2 %collective-permute-start.36 = (bf16[4,480,1536]{2,1,0:T(8,128)(2,1)}, bf16[4,480,1536]{2,1,0:T(8,128)(2,1)}, u32[]{:S(2)}, u32[]{:S(2)}) collective-permute-start(bf16[4,480,1536]{2,1,0:T(8,128)(2,1)} %expert_grad.4), channel_id=1, source_target_pairs={{0,4},{4,0},{8,12},{12,8},{16,20},{20,16},{24,28},{28,24},{1,5},{5... | collective-permute-start | bytes 17694728 | tf_op jit(solution)/shard_map/ppermute | solution.py:469
  389.2 55.5 %collective-permute-start.39 = (bf16[4,384,1536]{2,1,0:T(8,128)(2,1)}, bf16[4,384,1536]{2,1,0:T(8,128)(2,1)}, u32[]{:S(2)}, u32[]{:S(2)}) collective-permute-start(bf16[4,384,1536]{2,1,0:T(8,128)(2,1)} %expert_grad.5), channel_id=1, source_target_pairs={{0,4},{4,0},{8,12},{12,8},{16,20},{20,16},{24,28},{28,24},{1,5},{5... | collective-permute-start | bytes 14155784 | tf_op jit(solution)/shard_map/ppermute | solution.py:469
  389.7 34.3 %collective-permute-start.35 = (bf16[256,1536]{1,0:T(8,128)(2,1)}, bf16[256,1536]{1,0:T(8,128)(2,1)}, u32[]{:S(2)}, u32[]{:S(2)}) collective-permute-start(bf16[256,1536]{1,0:T(8,128)(2,1)} %get-tuple-element.267), channel_id=1, source_target_pairs={{0,1},{3,2},{4,5},{7,6},{8,9},{11,10},{12,13},{15,14},{16,17},{19,... | collective-permute-start | bytes 2359304 | tf_op jit(solution)/shard_map/ppermute | solution.py:485
  426.3 24.5 %collective-permute-start.37 = (bf16[256,1536]{1,0:T(8,128)(2,1)}, bf16[256,1536]{1,0:T(8,128)(2,1)}, u32[]{:S(2)}, u32[]{:S(2)}) collective-permute-start(bf16[256,1536]{1,0:T(8,128)(2,1)} %add.257), channel_id=1, source_target_pairs={{0,1},{3,2},{4,5},{7,6},{8,9},{11,10},{12,13},{15,14},{16,17},{19,... | collective-permute-start | bytes 2359304 | tf_op jit(solution)/shard_map/ppermute | solution.py:485
  428.5 22.4 %collective-permute-start.38 = (bf16[256,1536]{1,0:T(8,128)(2,1)}, bf16[256,1536]{1,0:T(8,128)(2,1)}, u32[]{:S(2)}, u32[]{:S(2)}) collective-permute-start(bf16[256,1536]{1,0:T(8,128)(2,1)} %add.257), channel_id=1, source_target_pairs={{1,2},{2,1},{5,6},{6,5},{9,10},{10,9},{13,14},{14,13},{17,18},{18,... | collective-permute-start | bytes 2359304 | tf_op jit(solution)/shard_map/ppermute | solution.py:477
  430.4 65.9 %collective-permute-start.43 = (bf16[2,480,1536]{2,1,0:T(8,128)(2,1)}, bf16[2,480,1536]{2,1,0:T(8,128)(2,1)}, u32[]{:S(2)}, u32[]{:S(2)}) collective-permute-start(bf16[2,480,1536]{2,1,0:T(8,128)(2,1)} %get-tuple-element.288), channel_id=1, source_target_pairs={{0,8},{4,12},{8,0},{12,4},{16,24},{20,28},{24,16},{28,20},{1,9},{5... | collective-permute-start | bytes 8847368 | tf_op jit(solution)/shard_map/ppermute | solution.py:469
  456.5 58.7 %collective-permute-start.44 = (bf16[2,384,1536]{2,1,0:T(8,128)(2,1)}, bf16[2,384,1536]{2,1,0:T(8,128)(2,1)}, u32[]{:S(2)}, u32[]{:S(2)}) collective-permute-start(bf16[2,384,1536]{2,1,0:T(8,128)(2,1)} %get-tuple-element.292), channel_id=1, source_target_pairs={{0,16},{4,20},{8,24},{12,28},{16,0},{20,4},{24,8},{28,12},{1,17},{... | collective-permute-start | bytes 7077896 | tf_op jit(solution)/shard_map/ppermute | solution.py:469
  490.7 63.8 %collective-permute-start.42 = (bf16[4,192,1536]{2,1,0:T(8,128)(2,1)}, bf16[4,192,1536]{2,1,0:T(8,128)(2,1)}, u32[]{:S(2)}, u32[]{:S(2)}) collective-permute-start(bf16[4,192,1536]{2,1,0:T(8,128)(2,1)} %get-tuple-element.306), channel_id=1, source_target_pairs={{0,4},{4,0},{8,12},{12,8},{16,20},{20,16},{24,28},{28,24},{1,5},{5... | collective-permute-start | bytes 7077896 | tf_op jit(solution)/shard_map/ppermute | solution.py:469
  490.8 109.2 %collective-permute-start.51 = (bf16[4,768,640]{2,1,0:T(8,128)(2,1)}, bf16[4,768,640]{2,1,0:T(8,128)(2,1)}, u32[]{:S(2)}, u32[]{:S(2)}) collective-permute-start(bf16[4,768,640]{2,1,0:T(8,128)(2,1)} %pad_maximum_fusion.refs_1_), channel_id=1, source_target_pairs={{0,4},{4,0},{8,12},{12,8},{16,20},{20,16},{24,28},{28,24},{1,5},{5... | collective-permute-start | bytes 11796488 | tf_op jit(solution)/shard_map/ppermute | solution.py:469
  491.3 30.9 %all-to-all-start.2 = ((bf16[4,256,384]{2,1,0:T(8,128)(2,1)}), bf16[4,256,384]{2,1,0:T(8,128)(2,1)S(1)}, u32[]{:S(2)}, u32[]{:S(2)}) async-start(bf16[4,256,384]{2,1,0:T(8,128)(2,1)} %get-tuple-element.303), calls=%async_computation.2 | async-start | bytes 1572864 | tf_op jit(solution)/shard_map/all_to_all | solution.py:515
  504.5 45.7 %collective-permute-start.47 = (bf16[480,1536]{1,0:T(8,128)(2,1)}, bf16[480,1536]{1,0:T(8,128)(2,1)}, u32[]{:S(2)}, u32[]{:S(2)}) collective-permute-start(bf16[480,1536]{1,0:T(8,128)(2,1)} %get-tuple-element.309), channel_id=1, source_target_pairs={{0,16},{4,20},{8,24},{12,28},{16,0},{20,4},{24,8},{28,12},{1,17},{... | collective-permute-start | bytes 4423688 | tf_op jit(solution)/shard_map/ppermute | solution.py:469
  520.7 25.1 %collective-permute-start.46 = (bf16[384,1536]{1,0:T(8,128)(2,1)}, bf16[384,1536]{1,0:T(8,128)(2,1)}, u32[]{:S(2)}, u32[]{:S(2)}) collective-permute-start(bf16[384,1536]{1,0:T(8,128)(2,1)} %get-tuple-element.312), channel_id=1, source_target_pairs={{0,8},{4,12},{8,0},{12,4},{16,24},{20,28},{24,16},{28,20},{1,9},{5... | collective-permute-start | bytes 3538952 | tf_op jit(solution)/shard_map/ppermute | solution.py:469
  548.7 29.1 %collective-permute-start.49 = (bf16[384,1536]{1,0:T(8,128)(2,1)S(1)}, bf16[384,1536]{1,0:T(8,128)(2,1)}, u32[]{:S(2)}, u32[]{:S(2)}) collective-permute-start(bf16[384,1536]{1,0:T(8,128)(2,1)S(1)} %blend_sum.2.refs_0_), channel_id=1, source_target_pairs={{0,8},{4,12},{8,0},{12,4},{16,24},{20,28},{24,16},{28,20},{1,9},{5... | collective-permute-start | bytes 3538952 | tf_op jit(solution)/shard_map/ppermute | solution.py:469
  553.8 42.4 %collective-permute-start.50 = (bf16[480,1536]{1,0:T(8,128)(2,1)S(1)}, bf16[480,1536]{1,0:T(8,128)(2,1)}, u32[]{:S(2)}, u32[]{:S(2)}) collective-permute-start(bf16[480,1536]{1,0:T(8,128)(2,1)S(1)} %blend_sum.3.refs_0_), channel_id=1, source_target_pairs={{0,16},{4,20},{8,24},{12,28},{16,0},{20,4},{24,8},{28,12},{1,17},{... | collective-permute-start | bytes 4423688 | tf_op jit(solution)/shard_map/ppermute | solution.py:469
  555.8 26.2 %collective-permute-start.48 = (bf16[192,1536]{1,0:T(8,128)(2,1)S(1)}, bf16[192,1536]{1,0:T(8,128)(2,1)}, u32[]{:S(2)}, u32[]{:S(2)}) collective-permute-start(bf16[192,1536]{1,0:T(8,128)(2,1)S(1)} %add_bitcast_fusion), channel_id=1, source_target_pairs={{0,1},{3,2},{4,5},{7,6},{8,9},{11,10},{12,13},{15,14},{16,17},{19,... | collective-permute-start | bytes 1769480 | tf_op jit(solution)/shard_map/ppermute | solution.py:485
  560.9 39.6 %all-to-all-start.3 = ((bf16[4,256,640]{2,1,0:T(8,128)(2,1)}), bf16[4,256,640]{2,1,0:T(8,128)(2,1)}, u32[]{:S(2)}, u32[]{:S(2)}) async-start(bf16[4,256,640]{2,1,0:T(8,128)(2,1)} %pad_maximum_fusion.2), calls=%async_computation.3 | async-start | bytes 2621440 | tf_op jit(solution)/shard_map/all_to_all | solution.py:515
  573.1 39.1 %collective-permute-start.55 = (bf16[4,192,640]{2,1,0:T(8,128)(2,1)}, bf16[4,192,640]{2,1,0:T(8,128)(2,1)}, u32[]{:S(2)}, u32[]{:S(2)}) collective-permute-start(bf16[4,192,640]{2,1,0:T(8,128)(2,1)} %get-tuple-element.334), channel_id=1, source_target_pairs={{0,4},{4,0},{8,12},{12,8},{16,20},{20,16},{24,28},{28,24},{1,5},{5... | collective-permute-start | bytes 2949128 | tf_op jit(solution)/shard_map/ppermute | solution.py:469
  584.5 29.7 %collective-permute-start.53 = (bf16[192,1536]{1,0:T(8,128)(2,1)}, bf16[192,1536]{1,0:T(8,128)(2,1)}, u32[]{:S(2)}, u32[]{:S(2)}) collective-permute-start(bf16[192,1536]{1,0:T(8,128)(2,1)} %bitcast_add_fusion.1), channel_id=1, source_target_pairs={{0,1},{3,2},{4,5},{7,6},{8,9},{11,10},{12,13},{15,14},{16,17},{19,... | collective-permute-start | bytes 1769480 | tf_op jit(solution)/shard_map/ppermute | solution.py:485
  589.0 29.3 %collective-permute-start.54 = (bf16[192,1536]{1,0:T(8,128)(2,1)}, bf16[192,1536]{1,0:T(8,128)(2,1)}, u32[]{:S(2)}, u32[]{:S(2)}) collective-permute-start(bf16[192,1536]{1,0:T(8,128)(2,1)} %bitcast_add_fusion.1), channel_id=1, source_target_pairs={{1,2},{2,1},{5,6},{6,5},{9,10},{10,9},{13,14},{14,13},{17,18},{18,... | collective-permute-start | bytes 1769480 | tf_op jit(solution)/shard_map/ppermute | solution.py:477
  596.2 52.6 %collective-permute-start.60 = (bf16[2,384,1536]{2,1,0:T(8,128)(2,1)}, bf16[2,384,1536]{2,1,0:T(8,128)(2,1)}, u32[]{:S(2)}, u32[]{:S(2)}) collective-permute-start(bf16[2,384,1536]{2,1,0:T(8,128)(2,1)} %blend_stack.2.refs_0_), channel_id=1, source_target_pairs={{0,4},{4,0},{8,12},{12,8},{16,20},{20,16},{24,28},{28,24},{1,5},{5... | collective-permute-start | bytes 7077896 | tf_op jit(solution)/shard_map/ppermute | solution.py:469
  600.0 65.1 %collective-permute-start.65 = (bf16[2,480,1536]{2,1,0:T(8,128)(2,1)S(1)}, bf16[2,480,1536]{2,1,0:T(8,128)(2,1)}, u32[]{:S(2)}, u32[]{:S(2)}) collective-permute-start(bf16[2,480,1536]{2,1,0:T(8,128)(2,1)S(1)} %blend_stack.3.refs_1_), channel_id=1, source_target_pairs={{0,4},{4,0},{8,12},{12,8},{16,20},{20,16},{24,28},{28,24},{1,5},{5... | collective-permute-start | bytes 8847368 | tf_op jit(solution)/shard_map/ppermute | solution.py:469
  612.2 65.9 %collective-permute-start.67 = (bf16[2,480,1536]{2,1,0:T(8,128)(2,1)S(1)}, bf16[2,480,1536]{2,1,0:T(8,128)(2,1)}, u32[]{:S(2)}, u32[]{:S(2)}) collective-permute-start(bf16[2,480,1536]{2,1,0:T(8,128)(2,1)S(1)} %blend_stack.3.refs_1_), channel_id=1, source_target_pairs={{0,8},{4,12},{8,0},{12,4},{16,24},{20,28},{24,16},{28,20},{1,9},{5... | collective-permute-start | bytes 8847368 | tf_op jit(solution)/shard_map/ppermute | solution.py:469
  634.0 52.2 %collective-permute-start.68 = (bf16[2,384,1536]{2,1,0:T(8,128)(2,1)}, bf16[2,384,1536]{2,1,0:T(8,128)(2,1)}, u32[]{:S(2)}, u32[]{:S(2)}) collective-permute-start(bf16[2,384,1536]{2,1,0:T(8,128)(2,1)} %blend_stack.2.refs_0_), channel_id=1, source_target_pairs={{0,16},{4,20},{8,24},{12,28},{16,0},{20,4},{24,8},{28,12},{1,17},{... | collective-permute-start | bytes 7077896 | tf_op jit(solution)/shard_map/ppermute | solution.py:469
  639.0 21.2 %collective-permute-start.63 = (bf16[192,1536]{1,0:T(8,128)(2,1)S(1)}, bf16[192,1536]{1,0:T(8,128)(2,1)S(1)}, u32[]{:S(2)}, u32[]{:S(2)}) collective-permute-start(bf16[192,1536]{1,0:T(8,128)(2,1)S(1)} %bitcast_add_fusion), channel_id=1, source_target_pairs={{0,1},{1,0},{2,3},{3,2},{4,5},{5,4},{6,7},{7,6},{8,9},{9,8},{10,11... | collective-permute-start | bytes 1769480 | tf_op jit(solution)/shard_map/ppermute | solution.py:473
  678.1 51.0 %collective-permute-start.79 = (bf16[2,480,1536]{2,1,0:T(8,128)(2,1)}, bf16[2,480,1536]{2,1,0:T(8,128)(2,1)}, u32[]{:S(2)}, u32[]{:S(2)}) collective-permute-start(bf16[2,480,1536]{2,1,0:T(8,128)(2,1)} %collective-permute-done.67.refs_1_), channel_id=1, source_target_pairs={{0,4},{4,0},{8,12},{12,8},{16,20},{20,16},{24,28},{28,24},{1,5},{5... | collective-permute-start | bytes 8847368 | tf_op jit(solution)/shard_map/ppermute | solution.py:469
  686.2 25.4 %collective-permute-start.75 = (bf16[2,384,1536]{2,1,0:T(8,128)(2,1)}, bf16[2,384,1536]{2,1,0:T(8,128)(2,1)}, u32[]{:S(2)}, u32[]{:S(2)}) collective-permute-start(bf16[2,384,1536]{2,1,0:T(8,128)(2,1)} %collective-permute-done.68.refs_1_), channel_id=1, source_target_pairs={{0,4},{4,0},{8,12},{12,8},{16,20},{20,16},{24,28},{28,24},{1,5},{5... | collective-permute-start | bytes 7077896 | tf_op jit(solution)/shard_map/ppermute | solution.py:469
  690.4 20.3 %collective-permute-start.70 = (bf16[96,1536]{1,0:T(8,128)(2,1)S(1)}, bf16[96,1536]{1,0:T(8,128)(2,1)S(1)}, u32[]{:S(2)}, u32[]{:S(2)}) collective-permute-start(bf16[96,1536]{1,0:T(8,128)(2,1)S(1)} %get-tuple-element.364), channel_id=1, source_target_pairs={{0,1},{1,0},{2,3},{3,2},{4,5},{5,4},{6,7},{7,6},{8,9},{9,8},{10,11... | collective-permute-start | bytes 884744 | tf_op jit(solution)/shard_map/ppermute | solution.py:473
  703.4 21.6 %collective-permute-start.71 = (bf16[96,1536]{1,0:T(8,128)(2,1)S(1)}, bf16[96,1536]{1,0:T(8,128)(2,1)S(1)}, u32[]{:S(2)}, u32[]{:S(2)}) collective-permute-start(bf16[96,1536]{1,0:T(8,128)(2,1)S(1)} %get-tuple-element.365), channel_id=1, source_target_pairs={{0,2},{1,3},{2,0},{3,1},{4,6},{5,7},{6,4},{7,5},{8,10},{9,11},{10,... | collective-permute-start | bytes 884744 | tf_op jit(solution)/shard_map/ppermute | solution.py:473
  710.7 22.7 %collective-permute-start.78 = (bf16[192,1536]{1,0:T(8,128)(2,1)S(1)}, bf16[192,1536]{1,0:T(8,128)(2,1)S(1)}, u32[]{:S(2)}, u32[]{:S(2)}) collective-permute-start(bf16[192,1536]{1,0:T(8,128)(2,1)S(1)} %add.295), channel_id=1, source_target_pairs={{0,16},{4,20},{8,24},{12,28},{16,0},{20,4},{24,8},{28,12},{1,17},{... | collective-permute-start | bytes 1769480 | tf_op jit(solution)/shard_map/ppermute | solution.py:469
  711.6 24.3 %collective-permute-start.77 = (bf16[2,192,640]{2,1,0:T(8,128)(2,1)S(1)}, bf16[2,192,640]{2,1,0:T(8,128)(2,1)S(1)}, u32[]{:S(2)}, u32[]{:S(2)}) collective-permute-start(bf16[2,192,640]{2,1,0:T(8,128)(2,1)S(1)} %pad_maximum_fusion.13), channel_id=1, source_target_pairs={{0,16},{4,20},{8,24},{12,28},{16,0},{20,4},{24,8},{28,12},{1,17},{... | collective-permute-start | bytes 1474568 | tf_op jit(solution)/shard_map/ppermute | solution.py:469
  (181 other events, 1634.4 us)

commit v12 on v11

--- a/solution.py
+++ b/solution.py
@@ -1486,8 +1486,8 @@
 )
 LATE = (
     "L", "0", "1", "0", "0", "L", "1", "1", "L", "L", "O", "0", "1", "L", "L", "1", "0", "O", "Q", "1", "O", "0", "L", "Q",
-    "O", "L", "1", "Q", "1", "Q", "0", "O", "0", "Q", "L", "1", "0", "O", "Q", "S", "1", "0", "L", "O", "Q", "1", "S", "L",
-    "0", "O", "Q", "L", "Q", "O", "S",
+    "O", "L", "1", "Q", "0", "Q", "O", "O", "Q", "L", "1", "0", "1", "0", "O", "Q", "S", "1", "0", "L", "O", "Q", "1", "S",
+    "L", "0", "O", "Q", "L", "Q", "O", "S",
 )
 
 
@@ -1875,7 +1875,6 @@
             blend(meta(), "blend_stack", lambda a, b: jnp.stack([a, b]), [own, came], pieces)
         )
         came = flip(pair, first)
-        pair_other = flip(pair, 1)
         yield
 
         def place(of_other, value, far):
@@ -1893,6 +1892,7 @@
             clock.mark(have["grad_experts"])
 
         place(0, pair, 0)
+        pair_other = flip(now(pair), 1)
         yield
         place(1, pair_other, 0)
         yield

time: 768 us -> 802 us (1.044)
  waiting for transfers between devices: 202 us -> 226 us
  starting transfers between devices: 137 us -> 149 us
    ppermute x17, starting transfers between devices: 38.4 us -> 53.7 us  [line_swap(): lax.ppermute(value, 'wt', [(index, index ^ offset) for index in range(4)])]
    ppermute x8, waiting for transfers between devices: 27.9 us -> 40.1 us  [line_inward(): return lax.ppermute(value, 'wt', [(0, 1), (3, 2)])]
    ppermute x17, waiting for transfers between devices: 68.7 us -> 78.9 us  [line_swap(): lax.ppermute(value, 'wt', [(index, index ^ offset) for index in range(4)])]
    unnamed x289 -> x295, local copies, waits for them, and re-layouts: 50.9 us -> 51.5 us
  transfers between devices with their start and end apart: 87 -> 87, of which waited for: 35 -> 35; matrix products, arithmetic and copies ran while one was open for 8% -> 8% of each run, Pallas kernels for 34% -> 32%
where the time goes in v12:
time: 802 us; the launch traced here: 793 us
  Pallas kernels  289 us (36%)
  waiting for transfers between devices  226 us (28%)
  starting transfers between devices  149 us (19%)
  local copies, waits for them, and re-layouts  70.6 us (9%)
  other arithmetic  52.2 us (7%)
    pallas_call x31, Pallas kernels, call(): pl.pallas_call(kernel, grid_spec=pltpu.PrefetchScalarGridSpec(num_scalar_...  261 us
    ppermute x42, waiting for transfers between devices, flip(): lax.ppermute(value, 'ctx', [(index, index ^ bit) for index in range(8)])  82.4 us
    ppermute x17, waiting for transfers between devices, line_swap(): lax.ppermute(value, 'wt', [(index, index ^ offset) for index in range(4)])  78.9 us
    ppermute x17, starting transfers between devices, line_swap(): lax.ppermute(value, 'wt', [(index, index ^ offset) for index in range(4)])  53.7 us
    unnamed x295, local copies, waits for them, and re-layouts  51.5 us
    ppermute x8, waiting for transfers between devices, line_inward(): return lax.ppermute(value, 'wt', [(0, 1), (3, 2)])  40.1 us
    ppermute x8, starting transfers between devices, line_inward(): return lax.ppermute(value, 'wt', [(0, 1), (3, 2)])  32 us
    pallas_call x8, Pallas kernels, place_sum(): pl.pallas_call(place_sum_kernel, grid_spec=pltpu.PrefetchScalarGridSpec(n...  28.5 us
  transfers between devices with their start and end apart: 87, of which 35 were waited for; matrix products, arithmetic and copies ran while one was open for 8% of the time, Pallas kernels for 32%

profile of v12, /device:TPU:0, one launch (start us, length us, event | category | flops | bytes accessed | tf_op | source)
XLA Modules:
  0.0 792.8 jit_solution(16708066016661381794)
XLA Ops:
  8.7 4.8 all-to-all-start.1
  27.6 22.4 %collective-permute-done.5 = bf16[2,192,640]{2,1,0:T(8,128)(2,1)S(1)} collective-permute-done((bf16[2,192,640]{2,1,0:T(8,128)(2,1)S(1)}, bf16[2,192,640]{2,1,0:T(8,128)(2,1)S(1)}, u32[]{:S(2)}, u32[]{:S(2)}) %collective-permute-start.5) | collective-permute-done | bytes 491552 | tf_op jit(solution)/shard_map/ppermute | solution.py:473
  55.8 4.7 all-to-all-start
  62.5 7.8 collective-permute-done.6
  73.4 6.8 project.1
  83.4 10.4 %attend.1 = (bf16[4,256,384]{2,1,0:T(8,128)(2,1)S(1)}, f32[8,1,384]{2,1,0:T(1,128)S(1)}) custom-call(s32[2]{0:T(128)S(1)} %pad_add_fusion.meta.meta_ref, bf16[4,256,384]{2,1,0:T(8,128)(2,1)S(1)} %get-tuple-element.207.query_ref, bf16[4,256,256]{2,1,0:T(8,128)(2,1)S(1)} %get-tuple-element.205.mine_ref, bf16[4,256,256]{2,1,0:T(8,128)(2,1)S(1)} %collective-permute-done.9.other_ref), custom_call_target="tpu_custom_call" | custom-call | flops 300000000 | bytes 1000 | tf_op jit(solution)/shard_map/attend/pallas_call | solution.py:584
  99.7 14.1 %all-to-all-done.refs_4_ = bf16[4,192,1536]{2,1,0:T(8,128)(2,1)} async-done(((bf16[4,192,1536]{2,1,0:T(8,128)(2,1)}), bf16[4,192,1536]{2,1,0:T(8,128)(2,1)}, u32[]{:S(2)}, u32[]{:S(2)}) %all-to-all-start) | async-done | bytes 2359328 | tf_op jit(solution)/shard_map/all_to_all | solution.py:526
  122.1 4.6 collective-permute-done.11.refs_2_
  128.2 6.2 leave.1
  142.9 11.7 %experts.4 = (bf16[4,256,1024]{2,1,0:T(8,128)(2,1)S(1)}, bf16[256,512]{1,0:T(8,128)(2,1)S(1)}, bf16[256,1536]{1,0:T(8,128)(2,1)S(1)}) custom-call(s32[2]{0:T(128)S(1)} %pad_add_fusion.meta.meta_ref, bf16[256,1536]{1,0:T(8,128)(2,1)S(1)} %get-tuple-element.218.rows_ref.refs_0_, f32[4,256,1]{2,1,0:T(8,128)S(1)} %copy.45.gates_ref, ...), custom_call_target="tpu_custom_call" | custom-call | flops 300000000 | bytes 1000 | tf_op jit(solution)/shard_map/experts/pallas_call | solution.py:584
  160.5 11.9 %experts.5 = (bf16[4,256,1024]{2,1,0:T(8,128)(2,1)S(1)}, bf16[256,512]{1,0:T(8,128)(2,1)S(1)}, bf16[256,1536]{1,0:T(8,128)(2,1)S(1)}) custom-call(s32[2]{0:T(128)S(1)} %pad_add_fusion.meta.meta_ref, bf16[256,1536]{1,0:T(8,128)(2,1)S(1)} %collective-permute-done.15.rows_ref.refs_1_, f32[4,256,1]{2,1,0:T(8,128)S(1)} %copy.46.gates_ref, ...), custom_call_target="tpu_custom_call" | custom-call | flops 300000000 | bytes 1000 | tf_op jit(solution)/shard_map/experts/pallas_call | solution.py:584
  173.8 6.7 collective-permute-done.18
  186.7 11.7 %experts.6 = (bf16[4,256,1024]{2,1,0:T(8,128)(2,1)S(1)}, bf16[256,512]{1,0:T(8,128)(2,1)S(1)}, bf16[256,1536]{1,0:T(8,128)(2,1)S(1)}) custom-call(s32[2]{0:T(128)S(1)} %pad_add_fusion.meta.meta_ref, bf16[256,1536]{1,0:T(8,128)(2,1)S(1)} %broadcast_select_fusion.3.rows_ref.refs_2_, f32[4,256,1]{2,1,0:T(8,128)S(1)} %copy.47.gates_ref, ...), custom_call_target="tpu_custom_call" | custom-call | flops 300000000 | bytes 1000 | tf_op jit(solution)/shard_map/experts/pallas_call | solution.py:584
  200.7 11.7 %experts.7 = (bf16[4,256,1024]{2,1,0:T(8,128)(2,1)S(1)}, bf16[256,512]{1,0:T(8,128)(2,1)S(1)}, bf16[256,1536]{1,0:T(8,128)(2,1)S(1)}) custom-call(s32[2]{0:T(128)S(1)} %pad_add_fusion.meta.meta_ref, bf16[256,1536]{1,0:T(8,128)(2,1)S(1)} %broadcast_select_fusion.2.rows_ref.refs_3_, f32[4,256,1]{2,1,0:T(8,128)S(1)} %copy.48.gates_ref, ...), custom_call_target="tpu_custom_call" | custom-call | flops 300000000 | bytes 1000 | tf_op jit(solution)/shard_map/experts/pallas_call | solution.py:584
  212.5 5.8 collective-permute-start.21
  223.5 12.2 %collective-permute-done.21 = bf16[256,1536]{1,0:T(8,128)(2,1)S(1)} collective-permute-done((bf16[256,1536]{1,0:T(8,128)(2,1)S(1)}, bf16[256,1536]{1,0:T(8,128)(2,1)S(1)}, u32[]{:S(2)}, u32[]{:S(2)}) %collective-permute-start.21) | collective-permute-done | bytes 786464 | tf_op jit(solution)/shard_map/ppermute | solution.py:485
  244.7 12.2 %collective-permute-done.24 = bf16[256,1536]{1,0:T(8,128)(2,1)S(1)} collective-permute-done((bf16[256,1536]{1,0:T(8,128)(2,1)S(1)}, bf16[256,1536]{1,0:T(8,128)(2,1)S(1)}, u32[]{:S(2)}, u32[]{:S(2)}) %collective-permute-start.24) | collective-permute-done | bytes 786464 | tf_op jit(solution)/shard_map/ppermute | solution.py:485
  263.7 13.9 %collective-permute-done.27 = bf16[256,1536]{1,0:T(8,128)(2,1)S(1)} collective-permute-done((bf16[256,1536]{1,0:T(8,128)(2,1)S(1)}, bf16[256,1536]{1,0:T(8,128)(2,1)S(1)}, u32[]{:S(2)}, u32[]{:S(2)}) %collective-permute-start.27) | collective-permute-done | bytes 786464 | tf_op jit(solution)/shard_map/ppermute | solution.py:473
  285.3 13.0 %experts_back.4 = (bf16[4,256,1024]{2,1,0:T(8,128)(2,1)S(1)}, bf16[4,256,512]{2,1,0:T(8,128)(2,1)S(1)}, bf16[1,256,512]{2,1,0:T(8,128)(2,1)S(1)}, bf16[1,256,256]{2,1,0:T(8,128)(2,1)S(1)}, bf16[256,1536]{1,0:T(8,128)(2,1)S(1)}) custom-call(s32[2]{0:T(128)S(1)} %pad_add_fusion.meta.meta_ref, bf16[256,1536]{1,0:T(8,128)(2,1)S(1)} %get-tuple-element.389.grad_ref.refs_4_, ...), custom_call_target="tpu_custom_call" | custom-call | flops 300000000 | bytes 1000 | tf_op jit(solution)/shard_map/experts_back/pallas_call | solution.py:584
  305.1 13.0 %experts_back.5 = (bf16[4,256,1024]{2,1,0:T(8,128)(2,1)S(1)}, bf16[4,256,512]{2,1,0:T(8,128)(2,1)S(1)}, bf16[1,256,512]{2,1,0:T(8,128)(2,1)S(1)}, bf16[1,256,256]{2,1,0:T(8,128)(2,1)S(1)}, bf16[256,1536]{1,0:T(8,128)(2,1)S(1)}) custom-call(s32[2]{0:T(128)S(1)} %pad_add_fusion.meta.meta_ref, bf16[256,1536]{1,0:T(8,128)(2,1)S(1)} %collective-permute-done.29.grad_ref.refs_5_, ...), custom_call_target="tpu_custom_call" | custom-call | flops 300000000 | bytes 1000 | tf_op jit(solution)/shard_map/experts_back/pallas_call | solution.py:584
  327.3 13.0 %experts_back.6 = (bf16[4,256,1024]{2,1,0:T(8,128)(2,1)S(1)}, bf16[4,256,512]{2,1,0:T(8,128)(2,1)S(1)}, bf16[1,256,512]{2,1,0:T(8,128)(2,1)S(1)}, bf16[1,256,256]{2,1,0:T(8,128)(2,1)S(1)}, bf16[256,1536]{1,0:T(8,128)(2,1)S(1)}) custom-call(s32[2]{0:T(128)S(1)} %pad_add_fusion.meta.meta_ref, bf16[256,1536]{1,0:T(8,128)(2,1)S(1)} %broadcast_select_fusion.1.grad_ref.refs_6_, ...), custom_call_target="tpu_custom_call" | custom-call | flops 300000000 | bytes 1000 | tf_op jit(solution)/shard_map/experts_back/pallas_call | solution.py:584
  345.4 14.4 %experts_back.7 = (bf16[4,256,1024]{2,1,0:T(8,128)(2,1)S(1)}, bf16[4,256,512]{2,1,0:T(8,128)(2,1)S(1)}, bf16[1,256,512]{2,1,0:T(8,128)(2,1)S(1)}, bf16[1,256,256]{2,1,0:T(8,128)(2,1)S(1)}, bf16[256,1536]{1,0:T(8,128)(2,1)}) custom-call(s32[2]{0:T(128)S(1)} %pad_add_fusion.meta.meta_ref, bf16[256,1536]{1,0:T(8,128)(2,1)S(1)} %broadcast_select_fusion.grad_ref.refs_7_, ...), custom_call_target="tpu_custom_call" | custom-call | flops 300000000 | bytes 1000 | tf_op jit(solution)/shard_map/experts_back/pallas_call | solution.py:584
  362.3 13.1 %expert_grad.4 = bf16[4,480,1536]{2,1,0:T(8,128)(2,1)} custom-call(s32[3]{0:T(128)S(1)} %add_add_fusion.meta, bf16[256,1536]{1,0:T(8,128)(2,1)S(1)} %copy-done.15, bf16[256,1536]{1,0:T(8,128)(2,1)S(1)} %copy-done.20, bf16[256,1536]{1,0:T(8,128)(2,1)S(1)} %broadcast_select_fusion.3.rows_ref.refs_2_, ...), custom_call_target="tpu_custom_call" | custom-call | flops 300000000 | bytes 1000 | tf_op jit(solution)/shard_map/expert_grad/pallas_call | solution.py:584
  379.0 10.2 %expert_grad.5 = bf16[4,384,1536]{2,1,0:T(8,128)(2,1)} custom-call(s32[3]{0:T(128)S(1)} %add_add_fusion.1.meta, bf16[256,1536]{1,0:T(8,128)(2,1)S(1)} %copy-done.16, bf16[256,1536]{1,0:T(8,128)(2,1)S(1)} %copy-done.21, bf16[256,1536]{1,0:T(8,128)(2,1)S(1)} %broadcast_select_fusion.3.rows_ref.refs_2_, ...), custom_call_target="tpu_custom_call" | custom-call | flops 300000000 | bytes 1000 | tf_op jit(solution)/shard_map/expert_grad/pallas_call | solution.py:584
  401.8 13.0 %expert_grad.6.refs_0_ = bf16[4,480,1536]{2,1,0:T(8,128)(2,1)} custom-call(s32[3]{0:T(128)S(1)} %add_add_fusion.2.meta, bf16[256,1536]{1,0:T(8,128)(2,1)S(1)} %copy-done.17, bf16[256,1536]{1,0:T(8,128)(2,1)S(1)} %copy-done.22, bf16[256,1536]{1,0:T(8,128)(2,1)S(1)} %broadcast_select_fusion.3.rows_ref.refs_2_, ...), custom_call_target="tpu_custom_call" | custom-call | flops 300000000 | bytes 1000 | tf_op jit(solution)/shard_map/expert_grad/pallas_call | solution.py:584
  414.7 7.8 blend_split.2
  434.7 10.1 %expert_grad.7.refs_0_ = bf16[4,384,1536]{2,1,0:T(8,128)(2,1)} custom-call(s32[3]{0:T(128)S(1)} %add_add_fusion.3.meta, bf16[256,1536]{1,0:T(8,128)(2,1)S(1)} %copy-done.18, bf16[256,1536]{1,0:T(8,128)(2,1)S(1)} %copy-done.23, bf16[256,1536]{1,0:T(8,128)(2,1)S(1)} %broadcast_select_fusion.3.rows_ref.refs_2_, ...), custom_call_target="tpu_custom_call" | custom-call | flops 300000000 | bytes 1000 | tf_op jit(solution)/shard_map/expert_grad/pallas_call | solution.py:584
  444.8 6.1 blend_split.3
  458.1 15.9 %collective-permute-done.40 = bf16[256,1536]{1,0:T(8,128)(2,1)} collective-permute-done((bf16[256,1536]{1,0:T(8,128)(2,1)S(1)}, bf16[256,1536]{1,0:T(8,128)(2,1)}, u32[]{:S(2)}, u32[]{:S(2)}) %collective-permute-start.40) | collective-permute-done | bytes 786464 | tf_op jit(solution)/shard_map/ppermute | solution.py:473
  476.8 7.3 enter_back.1
  498.2 5.2 blend_pair.2
  505.3 10.0 %collective-permute-done.44.refs_1_ = bf16[2,384,1536]{2,1,0:T(8,128)(2,1)} collective-permute-done((bf16[2,384,1536]{2,1,0:T(8,128)(2,1)}, bf16[2,384,1536]{2,1,0:T(8,128)(2,1)}, u32[]{:S(2)}, u32[]{:S(2)}) %collective-permute-start.44) | collective-permute-done | bytes 2359328 | tf_op jit(solution)/shard_map/ppermute | solution.py:469
  522.3 14.3 %attend_back.1 = (bf16[4,256,384]{2,1,0:T(8,128)(2,1)S(1)}, f32[4,256,256]{2,1,0:T(8,128)S(1)}, bf16[4,256,256]{2,1,0:T(8,128)(2,1)S(1)}) custom-call(s32[2]{0:T(128)S(1)} %pad_add_fusion.meta.meta_ref, bf16[4,256,384]{2,1,0:T(8,128)(2,1)S(1)} %copy-done.49, bf16[4,256,256]{2,1,0:T(8,128)(2,1)S(1)} %copy-done.59, bf16[4,256,256]{2,1,0:T(8,128)(2,1)S(1)} %copy-done.61, ...), custom_call_target="tpu_custom_call" | custom-call | flops 300000000 | bytes 1000 | tf_op jit(solution)/shard_map/attend_back/pallas_call | solution.py:584
  539.9 6.1 collective-permute-done.46.refs_1_
  555.9 5.2 collective-permute-start.48
  565.5 6.8 weight_grad.3
  573.2 4.7 collective-permute-done.49.refs_1_
  590.8 5.6 collective-permute-done.50.refs_1_
  602.6 9.1 %finish.1 = (f32[1,256,1536]{2,1,0:T(8,128)}, f32[1,1536]{1,0:T(1,128)S(1)}) custom-call(s32[2]{0:T(128)S(1)} %pad_add_fusion.meta.meta_ref, bf16[4,256,640]{2,1,0:T(8,128)(2,1)} %all-to-all-done.3.refs_0_, bf16[4,768,640]{2,1,0:T(8,128)(2,1)} %pad_maximum_fusion.refs_1_, bf16[4,768,640]{2,1,0:T(8,128)(2,1)} %collective-permute-done.51.refs_2_, ...), custom_call_target="tpu_custom_call" | custom-call | flops 300000000 | bytes 1000 | tf_op jit(solution)/shard_map/finish/pallas_call | solution.py:584
  634.8 15.7 %collective-permute-done.58 = bf16[192,640]{1,0:T(8,128)(2,1)S(1)} collective-permute-done((bf16[192,640]{1,0:T(8,128)(2,1)}, bf16[192,640]{1,0:T(8,128)(2,1)S(1)}, u32[]{:S(2)}, u32[]{:S(2)}) %collective-permute-start.58) | collective-permute-done | bytes 245792 | tf_op jit(solution)/shard_map/ppermute | solution.py:485
  653.0 17.9 %collective-permute-start.60 = (bf16[192,640]{1,0:T(8,128)(2,1)S(1)}, bf16[192,640]{1,0:T(8,128)(2,1)S(1)}, u32[]{:S(2)}, u32[]{:S(2)}) collective-permute-start(bf16[192,640]{1,0:T(8,128)(2,1)S(1)} %bitcast_add_fusion.3), channel_id=1, source_target_pairs={{0,1},{1,0},{2,3},{3,2},{4,5},{5,4},{6,7},{7,6},{8,9},{9,8},{10,11... | collective-permute-start | bytes 737288 | tf_op jit(solution)/shard_map/ppermute | solution.py:473
  671.0 5.6 collective-permute-done.60
  679.4 8.7 %collective-permute-start.56 = (f32[8,1536]{1,0:T(8,128)S(1)}, f32[8,1536]{1,0:T(8,128)S(1)}, u32[]{:S(2)}, u32[]{:S(2)}) collective-permute-start(f32[8,1536]{1,0:T(8,128)S(1)} %fusion.12), channel_id=1, source_target_pairs={{0,2},{1,3},{2,0},{3,1},{4,6},{5,7},{6,4},{7,5},{8,10},{9,11},{10,... | collective-permute-start | bytes 147464 | tf_op jit(solution)/shard_map/ppermute | solution.py:473
  696.1 8.2 %collective-permute-done.69.refs_1_ = bf16[2,384,1536]{2,1,0:T(8,128)(2,1)} collective-permute-done((bf16[2,384,1536]{2,1,0:T(8,128)(2,1)S(1)}, bf16[2,384,1536]{2,1,0:T(8,128)(2,1)}, u32[]{:S(2)}, u32[]{:S(2)}) %collective-permute-start.69) | collective-permute-done | bytes 2359328 | tf_op jit(solution)/shard_map/ppermute | solution.py:469
  705.5 14.8 %collective-permute-done.68 = bf16[192,1536]{1,0:T(8,128)(2,1)S(1)} collective-permute-done((bf16[192,1536]{1,0:T(8,128)(2,1)}, bf16[192,1536]{1,0:T(8,128)(2,1)S(1)}, u32[]{:S(2)}, u32[]{:S(2)}) %collective-permute-start.68) | collective-permute-done | bytes 589856 | tf_op jit(solution)/shard_map/ppermute | solution.py:469
  744.8 7.0 collective-permute-done.71
  752.4 9.4 %collective-permute-done.72 = bf16[96,1536]{1,0:T(8,128)(2,1)S(1)} collective-permute-done((bf16[96,1536]{1,0:T(8,128)(2,1)}, bf16[96,1536]{1,0:T(8,128)(2,1)S(1)}, u32[]{:S(2)}, u32[]{:S(2)}) %collective-permute-start.72) | collective-permute-done | bytes 294944 | tf_op jit(solution)/shard_map/ppermute | solution.py:473
  785.9 5.5 place_shared.1
  (571 shorter events, 310.4 us)
Async XLA Ops:
  8.7 45.5 %all-to-all-start.1 = ((bf16[4,256,1536]{2,1,0:T(8,128)(2,1)}), bf16[4,256,1536]{2,1,0:T(8,128)(2,1)}, u32[]{:S(2)}, u32[]{:S(2)}) async-start(bf16[4,256,1536]{2,1,0:T(8,128)(2,1)} %broadcast_in_dim.55), calls=%async_computation.1 | async-start | bytes 6291456 | tf_op jit(solution)/shard_map/all_to_all | solution.py:515
  20.7 29.3 %collective-permute-start.5 = (bf16[2,192,640]{2,1,0:T(8,128)(2,1)S(1)}, bf16[2,192,640]{2,1,0:T(8,128)(2,1)S(1)}, u32[]{:S(2)}, u32[]{:S(2)}) collective-permute-start(bf16[2,192,640]{2,1,0:T(8,128)(2,1)S(1)} %pad_maximum_fusion.12), channel_id=1, source_target_pairs={{0,2},{1,3},{2,0},{3,1},{4,6},{5,7},{6,4},{7,5},{8,10},{9,11},{10,... | collective-permute-start | bytes 1474568 | tf_op jit(solution)/shard_map/ppermute | solution.py:473
  23.4 28.0 %collective-permute-start.4 = (f32[2,32,256]{2,1,0:T(8,128)S(1)}, f32[2,32,256]{2,1,0:T(8,128)S(1)}, u32[]{:S(2)}, u32[]{:S(2)}) collective-permute-start(f32[2,32,256]{2,1,0:T(8,128)S(1)} %pad_maximum_fusion.19), channel_id=1, source_target_pairs={{0,2},{1,3},{2,0},{3,1},{4,6},{5,7},{6,4},{7,5},{8,10},{9,11},{10,... | collective-permute-start | bytes 196616 | tf_op jit(solution)/shard_map/ppermute | solution.py:473
  23.7 29.7 %collective-permute-start.3 = (bf16[2,48,768]{2,1,0:T(8,128)(2,1)S(1)}, bf16[2,48,768]{2,1,0:T(8,128)(2,1)S(1)}, u32[]{:S(2)}, u32[]{:S(2)}) collective-permute-start(bf16[2,48,768]{2,1,0:T(8,128)(2,1)S(1)} %pad_maximum_fusion.17), channel_id=1, source_target_pairs={{0,2},{1,3},{2,0},{3,1},{4,6},{5,7},{6,4},{7,5},{8,10},{9,11},{10,... | collective-permute-start | bytes 442376 | tf_op jit(solution)/shard_map/ppermute | solution.py:473
  55.8 58.0 %all-to-all-start = ((bf16[4,192,1536]{2,1,0:T(8,128)(2,1)}), bf16[4,192,1536]{2,1,0:T(8,128)(2,1)}, u32[]{:S(2)}, u32[]{:S(2)}) async-start(bf16[4,192,1536]{2,1,0:T(8,128)(2,1)} %broadcast_in_dim.54), calls=%async_computation | async-start | bytes 4718592 | tf_op jit(solution)/shard_map/all_to_all | solution.py:526
  113.8 24.7 %collective-permute-start.14 = (bf16[4,4,48,768]{3,2,1,0:T(8,128)(2,1)}, bf16[4,4,48,768]{3,2,1,0:T(8,128)(2,1)}, u32[]{:S(2)}, u32[]{:S(2)}) collective-permute-start(bf16[4,4,48,768]{3,2,1,0:T(8,128)(2,1)} %pad_maximum_fusion.6.mine), channel_id=1, source_target_pairs={{0,4},{4,0},{8,12},{12,8},{16,20},{20,16},{24,28},{28,24},{1,5},{5... | collective-permute-start | bytes 3538952 | tf_op jit(solution)/shard_map/ppermute | solution.py:469
  135.6 21.3 %collective-permute-start.15 = (bf16[256,1536]{1,0:T(8,128)(2,1)S(1)}, bf16[256,1536]{1,0:T(8,128)(2,1)S(1)}, u32[]{:S(2)}, u32[]{:S(2)}) collective-permute-start(bf16[256,1536]{1,0:T(8,128)(2,1)S(1)} %get-tuple-element.218.rows_ref.refs_0_), channel_id=1, source_target_pairs={{0,1},{1,0},{2,3},{3,2},{4,5},{5,4},{6,7},{7,6},{8,9},{9,8},{10,11... | collective-permute-start | bytes 2359304 | tf_op jit(solution)/shard_map/ppermute | solution.py:473
  135.6 21.3 %collective-permute-start.16 = (bf16[256,1536]{1,0:T(8,128)(2,1)S(1)}, bf16[256,1536]{1,0:T(8,128)(2,1)}, u32[]{:S(2)}, u32[]{:S(2)}) collective-permute-start(bf16[256,1536]{1,0:T(8,128)(2,1)S(1)} %get-tuple-element.218.rows_ref.refs_0_), channel_id=1, source_target_pairs={{1,2},{2,1},{5,6},{6,5},{9,10},{10,9},{13,14},{14,13},{17,18},{18,... | collective-permute-start | bytes 2359304 | tf_op jit(solution)/shard_map/ppermute | solution.py:477
  158.4 22.1 %collective-permute-start.18 = (bf16[256,1536]{1,0:T(8,128)(2,1)}, bf16[256,1536]{1,0:T(8,128)(2,1)}, u32[]{:S(2)}, u32[]{:S(2)}) collective-permute-start(bf16[256,1536]{1,0:T(8,128)(2,1)} %collective-permute-done.16), channel_id=1, source_target_pairs={{1,0},{2,3},{5,4},{6,7},{9,8},{10,11},{13,12},{14,15},{17,16},{18,... | collective-permute-start | bytes 2359304 | tf_op jit(solution)/shard_map/ppermute | solution.py:481
  183.2 38.7 %collective-permute-start.22 = (bf16[768,640]{1,0:T(8,128)(2,1)S(1)}, bf16[768,640]{1,0:T(8,128)(2,1)S(1)}, u32[]{:S(2)}, u32[]{:S(2)}) collective-permute-start(bf16[768,640]{1,0:T(8,128)(2,1)S(1)} %constant_dynamic-slice_fusion.1), channel_id=1, source_target_pairs={{0,8},{4,12},{8,0},{12,4},{16,24},{20,28},{24,16},{28,20},{1,9},{5... | collective-permute-start | bytes 2949128 | tf_op jit(solution)/shard_map/ppermute | solution.py:469
  212.5 23.1 %collective-permute-start.21 = (bf16[256,1536]{1,0:T(8,128)(2,1)S(1)}, bf16[256,1536]{1,0:T(8,128)(2,1)S(1)}, u32[]{:S(2)}, u32[]{:S(2)}) collective-permute-start(bf16[256,1536]{1,0:T(8,128)(2,1)S(1)} %get-tuple-element.234), channel_id=1, source_target_pairs={{0,1},{3,2},{4,5},{7,6},{8,9},{11,10},{12,13},{15,14},{16,17},{19,... | collective-permute-start | bytes 2359304 | tf_op jit(solution)/shard_map/ppermute | solution.py:485
  235.8 21.0 %collective-permute-start.24 = (bf16[256,1536]{1,0:T(8,128)(2,1)S(1)}, bf16[256,1536]{1,0:T(8,128)(2,1)S(1)}, u32[]{:S(2)}, u32[]{:S(2)}) collective-permute-start(bf16[256,1536]{1,0:T(8,128)(2,1)S(1)} %add.250), channel_id=1, source_target_pairs={{0,1},{3,2},{4,5},{7,6},{8,9},{11,10},{12,13},{15,14},{16,17},{19,... | collective-permute-start | bytes 2359304 | tf_op jit(solution)/shard_map/ppermute | solution.py:485
  257.3 20.3 %collective-permute-start.27 = (bf16[256,1536]{1,0:T(8,128)(2,1)S(1)}, bf16[256,1536]{1,0:T(8,128)(2,1)S(1)}, u32[]{:S(2)}, u32[]{:S(2)}) collective-permute-start(bf16[256,1536]{1,0:T(8,128)(2,1)S(1)} %add.252), channel_id=1, source_target_pairs={{0,1},{1,0},{2,3},{3,2},{4,5},{5,4},{6,7},{7,6},{8,9},{9,8},{10,11... | collective-permute-start | bytes 2359304 | tf_op jit(solution)/shard_map/ppermute | solution.py:473
  261.9 56.3 %collective-permute-start.33 = (bf16[2,768,640]{2,1,0:T(8,128)(2,1)}, bf16[2,768,640]{2,1,0:T(8,128)(2,1)}, u32[]{:S(2)}, u32[]{:S(2)}) collective-permute-start(bf16[2,768,640]{2,1,0:T(8,128)(2,1)} %pad_maximum_fusion.1), channel_id=1, source_target_pairs={{0,16},{4,20},{8,24},{12,28},{16,0},{20,4},{24,8},{28,12},{1,17},{... | collective-permute-start | bytes 5898248 | tf_op jit(solution)/shard_map/ppermute | solution.py:469
  280.6 21.6 %collective-permute-start.29 = (bf16[256,1536]{1,0:T(8,128)(2,1)S(1)}, bf16[256,1536]{1,0:T(8,128)(2,1)S(1)}, u32[]{:S(2)}, u32[]{:S(2)}) collective-permute-start(bf16[256,1536]{1,0:T(8,128)(2,1)S(1)} %get-tuple-element.389.grad_ref.refs_4_), channel_id=1, source_target_pairs={{0,1},{1,0},{2,3},{3,2},{4,5},{5,4},{6,7},{7,6},{8,9},{9,8},{10,11... | collective-permute-start | bytes 2359304 | tf_op jit(solution)/shard_map/ppermute | solution.py:473
  302.3 20.5 %collective-permute-start.31 = (bf16[256,1536]{1,0:T(8,128)(2,1)S(1)}, bf16[256,1536]{1,0:T(8,128)(2,1)}, u32[]{:S(2)}, u32[]{:S(2)}) collective-permute-start(bf16[256,1536]{1,0:T(8,128)(2,1)S(1)} %collective-permute-done.29.grad_ref.refs_5_), channel_id=1, source_target_pairs={{1,2},{2,1},{5,6},{6,5},{9,10},{10,9},{13,14},{14,13},{17,18},{18,... | collective-permute-start | bytes 2359304 | tf_op jit(solution)/shard_map/ppermute | solution.py:477
  375.4 39.3 %collective-permute-start.36 = (bf16[4,480,1536]{2,1,0:T(8,128)(2,1)}, bf16[4,480,1536]{2,1,0:T(8,128)(2,1)}, u32[]{:S(2)}, u32[]{:S(2)}) collective-permute-start(bf16[4,480,1536]{2,1,0:T(8,128)(2,1)} %expert_grad.4), channel_id=1, source_target_pairs={{0,4},{4,0},{8,12},{12,8},{16,20},{20,16},{24,28},{28,24},{1,5},{5... | collective-permute-start | bytes 17694728 | tf_op jit(solution)/shard_map/ppermute | solution.py:469
  389.2 55.6 %collective-permute-start.39 = (bf16[4,384,1536]{2,1,0:T(8,128)(2,1)}, bf16[4,384,1536]{2,1,0:T(8,128)(2,1)}, u32[]{:S(2)}, u32[]{:S(2)}) collective-permute-start(bf16[4,384,1536]{2,1,0:T(8,128)(2,1)} %expert_grad.5), channel_id=1, source_target_pairs={{0,4},{4,0},{8,12},{12,8},{16,20},{20,16},{24,28},{28,24},{1,5},{5... | collective-permute-start | bytes 14155784 | tf_op jit(solution)/shard_map/ppermute | solution.py:469
  389.7 34.4 %collective-permute-start.35 = (bf16[256,1536]{1,0:T(8,128)(2,1)}, bf16[256,1536]{1,0:T(8,128)(2,1)}, u32[]{:S(2)}, u32[]{:S(2)}) collective-permute-start(bf16[256,1536]{1,0:T(8,128)(2,1)} %get-tuple-element.268), channel_id=1, source_target_pairs={{0,1},{3,2},{4,5},{7,6},{8,9},{11,10},{12,13},{15,14},{16,17},{19,... | collective-permute-start | bytes 2359304 | tf_op jit(solution)/shard_map/ppermute | solution.py:485
  426.4 24.6 %collective-permute-start.37 = (bf16[256,1536]{1,0:T(8,128)(2,1)}, bf16[256,1536]{1,0:T(8,128)(2,1)}, u32[]{:S(2)}, u32[]{:S(2)}) collective-permute-start(bf16[256,1536]{1,0:T(8,128)(2,1)} %add.257), channel_id=1, source_target_pairs={{0,1},{3,2},{4,5},{7,6},{8,9},{11,10},{12,13},{15,14},{16,17},{19,... | collective-permute-start | bytes 2359304 | tf_op jit(solution)/shard_map/ppermute | solution.py:485
  428.6 22.4 %collective-permute-start.38 = (bf16[256,1536]{1,0:T(8,128)(2,1)}, bf16[256,1536]{1,0:T(8,128)(2,1)}, u32[]{:S(2)}, u32[]{:S(2)}) collective-permute-start(bf16[256,1536]{1,0:T(8,128)(2,1)} %add.257), channel_id=1, source_target_pairs={{1,2},{2,1},{5,6},{6,5},{9,10},{10,9},{13,14},{14,13},{17,18},{18,... | collective-permute-start | bytes 2359304 | tf_op jit(solution)/shard_map/ppermute | solution.py:477
  430.5 65.9 %collective-permute-start.43 = (bf16[2,480,1536]{2,1,0:T(8,128)(2,1)}, bf16[2,480,1536]{2,1,0:T(8,128)(2,1)}, u32[]{:S(2)}, u32[]{:S(2)}) collective-permute-start(bf16[2,480,1536]{2,1,0:T(8,128)(2,1)} %get-tuple-element.289), channel_id=1, source_target_pairs={{0,8},{4,12},{8,0},{12,4},{16,24},{20,28},{24,16},{28,20},{1,9},{5... | collective-permute-start | bytes 8847368 | tf_op jit(solution)/shard_map/ppermute | solution.py:469
  456.6 58.7 %collective-permute-start.44 = (bf16[2,384,1536]{2,1,0:T(8,128)(2,1)}, bf16[2,384,1536]{2,1,0:T(8,128)(2,1)}, u32[]{:S(2)}, u32[]{:S(2)}) collective-permute-start(bf16[2,384,1536]{2,1,0:T(8,128)(2,1)} %get-tuple-element.293), channel_id=1, source_target_pairs={{0,16},{4,20},{8,24},{12,28},{16,0},{20,4},{24,8},{28,12},{1,17},{... | collective-permute-start | bytes 7077896 | tf_op jit(solution)/shard_map/ppermute | solution.py:469
  490.9 63.7 %collective-permute-start.42 = (bf16[4,192,1536]{2,1,0:T(8,128)(2,1)}, bf16[4,192,1536]{2,1,0:T(8,128)(2,1)}, u32[]{:S(2)}, u32[]{:S(2)}) collective-permute-start(bf16[4,192,1536]{2,1,0:T(8,128)(2,1)} %get-tuple-element.307), channel_id=1, source_target_pairs={{0,4},{4,0},{8,12},{12,8},{16,20},{20,16},{24,28},{28,24},{1,5},{5... | collective-permute-start | bytes 7077896 | tf_op jit(solution)/shard_map/ppermute | solution.py:469
  490.9 109.2 %collective-permute-start.51 = (bf16[4,768,640]{2,1,0:T(8,128)(2,1)}, bf16[4,768,640]{2,1,0:T(8,128)(2,1)}, u32[]{:S(2)}, u32[]{:S(2)}) collective-permute-start(bf16[4,768,640]{2,1,0:T(8,128)(2,1)} %pad_maximum_fusion.refs_1_), channel_id=1, source_target_pairs={{0,4},{4,0},{8,12},{12,8},{16,20},{20,16},{24,28},{28,24},{1,5},{5... | collective-permute-start | bytes 11796488 | tf_op jit(solution)/shard_map/ppermute | solution.py:469
  491.4 30.9 %all-to-all-start.2 = ((bf16[4,256,384]{2,1,0:T(8,128)(2,1)}), bf16[4,256,384]{2,1,0:T(8,128)(2,1)S(1)}, u32[]{:S(2)}, u32[]{:S(2)}) async-start(bf16[4,256,384]{2,1,0:T(8,128)(2,1)} %get-tuple-element.304), calls=%async_computation.2 | async-start | bytes 1572864 | tf_op jit(solution)/shard_map/all_to_all | solution.py:515
  504.7 45.7 %collective-permute-start.47 = (bf16[480,1536]{1,0:T(8,128)(2,1)}, bf16[480,1536]{1,0:T(8,128)(2,1)}, u32[]{:S(2)}, u32[]{:S(2)}) collective-permute-start(bf16[480,1536]{1,0:T(8,128)(2,1)} %get-tuple-element.310), channel_id=1, source_target_pairs={{0,16},{4,20},{8,24},{12,28},{16,0},{20,4},{24,8},{28,12},{1,17},{... | collective-permute-start | bytes 4423688 | tf_op jit(solution)/shard_map/ppermute | solution.py:469
  520.8 25.1 %collective-permute-start.46 = (bf16[384,1536]{1,0:T(8,128)(2,1)}, bf16[384,1536]{1,0:T(8,128)(2,1)}, u32[]{:S(2)}, u32[]{:S(2)}) collective-permute-start(bf16[384,1536]{1,0:T(8,128)(2,1)} %get-tuple-element.313), channel_id=1, source_target_pairs={{0,8},{4,12},{8,0},{12,4},{16,24},{20,28},{24,16},{28,20},{1,9},{5... | collective-permute-start | bytes 3538952 | tf_op jit(solution)/shard_map/ppermute | solution.py:469
  548.8 29.1 %collective-permute-start.49 = (bf16[384,1536]{1,0:T(8,128)(2,1)S(1)}, bf16[384,1536]{1,0:T(8,128)(2,1)}, u32[]{:S(2)}, u32[]{:S(2)}) collective-permute-start(bf16[384,1536]{1,0:T(8,128)(2,1)S(1)} %blend_sum.2.refs_0_), channel_id=1, source_target_pairs={{0,8},{4,12},{8,0},{12,4},{16,24},{20,28},{24,16},{28,20},{1,9},{5... | collective-permute-start | bytes 3538952 | tf_op jit(solution)/shard_map/ppermute | solution.py:469
  553.9 42.4 %collective-permute-start.50 = (bf16[480,1536]{1,0:T(8,128)(2,1)S(1)}, bf16[480,1536]{1,0:T(8,128)(2,1)}, u32[]{:S(2)}, u32[]{:S(2)}) collective-permute-start(bf16[480,1536]{1,0:T(8,128)(2,1)S(1)} %blend_sum.3.refs_0_), channel_id=1, source_target_pairs={{0,16},{4,20},{8,24},{12,28},{16,0},{20,4},{24,8},{28,12},{1,17},{... | collective-permute-start | bytes 4423688 | tf_op jit(solution)/shard_map/ppermute | solution.py:469
  555.9 24.8 %collective-permute-start.48 = (bf16[192,1536]{1,0:T(8,128)(2,1)S(1)}, bf16[192,1536]{1,0:T(8,128)(2,1)}, u32[]{:S(2)}, u32[]{:S(2)}) collective-permute-start(bf16[192,1536]{1,0:T(8,128)(2,1)S(1)} %add_bitcast_fusion), channel_id=1, source_target_pairs={{0,1},{3,2},{4,5},{7,6},{8,9},{11,10},{12,13},{15,14},{16,17},{19,... | collective-permute-start | bytes 1769480 | tf_op jit(solution)/shard_map/ppermute | solution.py:485
  561.1 39.0 %all-to-all-start.3 = ((bf16[4,256,640]{2,1,0:T(8,128)(2,1)}), bf16[4,256,640]{2,1,0:T(8,128)(2,1)}, u32[]{:S(2)}, u32[]{:S(2)}) async-start(bf16[4,256,640]{2,1,0:T(8,128)(2,1)} %pad_maximum_fusion.2), calls=%async_computation.3 | async-start | bytes 2621440 | tf_op jit(solution)/shard_map/all_to_all | solution.py:515
  573.2 38.5 %collective-permute-start.55 = (bf16[4,192,640]{2,1,0:T(8,128)(2,1)}, bf16[4,192,640]{2,1,0:T(8,128)(2,1)}, u32[]{:S(2)}, u32[]{:S(2)}) collective-permute-start(bf16[4,192,640]{2,1,0:T(8,128)(2,1)} %get-tuple-element.335), channel_id=1, source_target_pairs={{0,4},{4,0},{8,12},{12,8},{16,20},{20,16},{24,28},{28,24},{1,5},{5... | collective-permute-start | bytes 2949128 | tf_op jit(solution)/shard_map/ppermute | solution.py:469
  583.9 32.6 %collective-permute-start.53 = (bf16[192,1536]{1,0:T(8,128)(2,1)}, bf16[192,1536]{1,0:T(8,128)(2,1)}, u32[]{:S(2)}, u32[]{:S(2)}) collective-permute-start(bf16[192,1536]{1,0:T(8,128)(2,1)} %bitcast_add_fusion.1), channel_id=1, source_target_pairs={{0,1},{3,2},{4,5},{7,6},{8,9},{11,10},{12,13},{15,14},{16,17},{19,... | collective-permute-start | bytes 1769480 | tf_op jit(solution)/shard_map/ppermute | solution.py:485
  588.6 28.0 %collective-permute-start.54 = (bf16[192,1536]{1,0:T(8,128)(2,1)}, bf16[192,1536]{1,0:T(8,128)(2,1)}, u32[]{:S(2)}, u32[]{:S(2)}) collective-permute-start(bf16[192,1536]{1,0:T(8,128)(2,1)} %bitcast_add_fusion.1), channel_id=1, source_target_pairs={{1,2},{2,1},{5,6},{6,5},{9,10},{10,9},{13,14},{14,13},{17,18},{18,... | collective-permute-start | bytes 1769480 | tf_op jit(solution)/shard_map/ppermute | solution.py:477
  628.4 64.9 %collective-permute-start.67 = (bf16[2,480,1536]{2,1,0:T(8,128)(2,1)S(1)}, bf16[2,480,1536]{2,1,0:T(8,128)(2,1)S(1)}, u32[]{:S(2)}, u32[]{:S(2)}) collective-permute-start(bf16[2,480,1536]{2,1,0:T(8,128)(2,1)S(1)} %blend_stack.3.refs_1_), channel_id=1, source_target_pairs={{0,4},{4,0},{8,12},{12,8},{16,20},{20,16},{24,28},{28,24},{1,5},{5... | collective-permute-start | bytes 8847368 | tf_op jit(solution)/shard_map/ppermute | solution.py:469
  628.4 67.8 %collective-permute-start.65 = (bf16[2,480,1536]{2,1,0:T(8,128)(2,1)S(1)}, bf16[2,480,1536]{2,1,0:T(8,128)(2,1)}, u32[]{:S(2)}, u32[]{:S(2)}) collective-permute-start(bf16[2,480,1536]{2,1,0:T(8,128)(2,1)S(1)} %blend_stack.3.refs_1_), channel_id=1, source_target_pairs={{0,8},{4,12},{8,0},{12,4},{16,24},{20,28},{24,16},{28,20},{1,9},{5... | collective-permute-start | bytes 8847368 | tf_op jit(solution)/shard_map/ppermute | solution.py:469
  629.7 21.5 %collective-permute-start.62 = (bf16[192,1536]{1,0:T(8,128)(2,1)S(1)}, bf16[192,1536]{1,0:T(8,128)(2,1)S(1)}, u32[]{:S(2)}, u32[]{:S(2)}) collective-permute-start(bf16[192,1536]{1,0:T(8,128)(2,1)S(1)} %bitcast_add_fusion), channel_id=1, source_target_pairs={{0,1},{1,0},{2,3},{3,2},{4,5},{5,4},{6,7},{7,6},{8,9},{9,8},{10,11... | collective-permute-start | bytes 1769480 | tf_op jit(solution)/shard_map/ppermute | solution.py:473
  650.5 39.8 %collective-permute-start.66 = (bf16[2,384,1536]{2,1,0:T(8,128)(2,1)S(1)}, bf16[2,384,1536]{2,1,0:T(8,128)(2,1)S(1)}, u32[]{:S(2)}, u32[]{:S(2)}) collective-permute-start(bf16[2,384,1536]{2,1,0:T(8,128)(2,1)S(1)} %copy-done.32), channel_id=1, source_target_pairs={{0,4},{4,0},{8,12},{12,8},{16,20},{20,16},{24,28},{28,24},{1,5},{5... | collective-permute-start | bytes 7077896 | tf_op jit(solution)/shard_map/ppermute | solution.py:469
  650.6 53.8 %collective-permute-start.69 = (bf16[2,384,1536]{2,1,0:T(8,128)(2,1)S(1)}, bf16[2,384,1536]{2,1,0:T(8,128)(2,1)}, u32[]{:S(2)}, u32[]{:S(2)}) collective-permute-start(bf16[2,384,1536]{2,1,0:T(8,128)(2,1)S(1)} %copy-done.32), channel_id=1, source_target_pairs={{0,16},{4,20},{8,24},{12,28},{16,0},{20,4},{24,8},{28,12},{1,17},{... | collective-permute-start | bytes 7077896 | tf_op jit(solution)/shard_map/ppermute | solution.py:469
  653.0 23.6 %collective-permute-start.60 = (bf16[192,640]{1,0:T(8,128)(2,1)S(1)}, bf16[192,640]{1,0:T(8,128)(2,1)S(1)}, u32[]{:S(2)}, u32[]{:S(2)}) collective-permute-start(bf16[192,640]{1,0:T(8,128)(2,1)S(1)} %bitcast_add_fusion.3), channel_id=1, source_target_pairs={{0,1},{1,0},{2,3},{3,2},{4,5},{5,4},{6,7},{7,6},{8,9},{9,8},{10,11... | collective-permute-start | bytes 737288 | tf_op jit(solution)/shard_map/ppermute | solution.py:473
  696.1 66.6 %collective-permute-start.80 = (bf16[2,480,1536]{2,1,0:T(8,128)(2,1)}, bf16[2,480,1536]{2,1,0:T(8,128)(2,1)}, u32[]{:S(2)}, u32[]{:S(2)}) collective-permute-start(bf16[2,480,1536]{2,1,0:T(8,128)(2,1)} %collective-permute-done.65.refs_1_), channel_id=1, source_target_pairs={{0,4},{4,0},{8,12},{12,8},{16,20},{20,16},{24,28},{28,24},{1,5},{5... | collective-permute-start | bytes 8847368 | tf_op jit(solution)/shard_map/ppermute | solution.py:469
  704.3 34.8 %collective-permute-start.76 = (bf16[2,384,1536]{2,1,0:T(8,128)(2,1)}, bf16[2,384,1536]{2,1,0:T(8,128)(2,1)}, u32[]{:S(2)}, u32[]{:S(2)}) collective-permute-start(bf16[2,384,1536]{2,1,0:T(8,128)(2,1)} %collective-permute-done.69.refs_1_), channel_id=1, source_target_pairs={{0,4},{4,0},{8,12},{12,8},{16,20},{20,16},{24,28},{28,24},{1,5},{5... | collective-permute-start | bytes 7077896 | tf_op jit(solution)/shard_map/ppermute | solution.py:469
  705.2 28.9 %collective-permute-start.64 = (f32[8,1536]{1,0:T(8,128)S(1)}, f32[8,1536]{1,0:T(8,128)S(1)}, u32[]{:S(2)}, u32[]{:S(2)}) collective-permute-start(f32[8,1536]{1,0:T(8,128)S(1)} %fusion.23), channel_id=1, source_target_pairs={{0,4},{4,0},{8,12},{12,8},{16,20},{20,16},{24,28},{28,24},{1,5},{5... | collective-permute-start | bytes 147464 | tf_op jit(solution)/shard_map/ppermute | solution.py:469
  735.6 31.4 %collective-permute-start.79 = (bf16[192,1536]{1,0:T(8,128)(2,1)S(1)}, bf16[192,1536]{1,0:T(8,128)(2,1)}, u32[]{:S(2)}, u32[]{:S(2)}) collective-permute-start(bf16[192,1536]{1,0:T(8,128)(2,1)S(1)} %add.296), channel_id=1, source_target_pairs={{0,4},{4,0},{8,12},{12,8},{16,20},{20,16},{24,28},{28,24},{1,5},{5... | collective-permute-start | bytes 1769480 | tf_op jit(solution)/shard_map/ppermute | solution.py:469
  738.1 23.6 %collective-permute-start.72 = (bf16[96,1536]{1,0:T(8,128)(2,1)}, bf16[96,1536]{1,0:T(8,128)(2,1)S(1)}, u32[]{:S(2)}, u32[]{:S(2)}) collective-permute-start(bf16[96,1536]{1,0:T(8,128)(2,1)} %get-tuple-element.368), channel_id=1, source_target_pairs={{0,2},{1,3},{2,0},{3,1},{4,6},{5,7},{6,4},{7,5},{8,10},{9,11},{10,... | collective-permute-start | bytes 884744 | tf_op jit(solution)/shard_map/ppermute | solution.py:473
  739.1 23.3 %collective-permute-start.73 = (bf16[96,1536]{1,0:T(8,128)(2,1)S(1)}, bf16[96,1536]{1,0:T(8,128)(2,1)S(1)}, u32[]{:S(2)}, u32[]{:S(2)}) collective-permute-start(bf16[96,1536]{1,0:T(8,128)(2,1)S(1)} %get-tuple-element.369), channel_id=1, source_target_pairs={{0,3},{1,2},{2,1},{3,0},{4,7},{5,6},{6,5},{7,4},{8,11},{9,10},{10,... | collective-permute-start | bytes 884744 | tf_op jit(solution)/shard_map/ppermute | solution.py:473
  762.6 21.0 %collective-permute-start.82 = (bf16[4,96,1536]{2,1,0:T(8,128)(2,1)S(1)}, bf16[4,96,1536]{2,1,0:T(8,128)(2,1)S(1)}, u32[]{:S(2)}, u32[]{:S(2)}) collective-permute-start(bf16[4,96,1536]{2,1,0:T(8,128)(2,1)S(1)} %pad_maximum_fusion.7.mine_low.mine_high), channel_id=1, source_target_pairs={{0,4},{4,0},{8,12},{12,8},{16,20},{20,16},{24,28},{28,24},{1,5},{5... | collective-permute-start | bytes 3538952 | tf_op jit(solution)/shard_map/ppermute | solution.py:469
  (184 other events, 1729.3 us)
